TPU v7x, 32 devices: a whole 2x2x4 slice. The times are simulated.
32 devices in a mesh: groups: 2 (over x), dp: 8 (over z, y), tensor: 2 (over core).
Axes of the slice: x: 2, y: 2, z: 4, core: 2. Of those that a mesh axis runs over, the one named last changes fastest.
Arguments:
- tokens: bfloat16 [6144, 8192], P(('groups', 'dp'), 'tensor'), parts along dimension 0, may hold values from -6 to 6
- base_key: bfloat16 [8192, 1024], P('tensor'), may hold values from -0.0625 to 0.0625
- adapter_down: bfloat16 [16, 8192, 64], P('dp', 'tensor'), may hold values from -0.0625 to 0.0625
- adapter_up: bfloat16 [16, 64, 1024], P('dp', None, 'tensor'), may hold values from -0.75 to 0.75
- adapter_ids: int32 [48, 1], P(('groups', 'dp')), parts along dimension 0, may hold values from 0 to 15
- owner_slot: int32 [16], replicated, may hold values from 0 to 15, each once
- lengths: int32 [48], P(('groups', 'dp')), parts along dimension 0, may hold values from 1 to 128, 2304 in all
Outputs:
- keys: bfloat16 [6144, 1024], P(('groups', 'dp'), 'tensor'), parts along dimension 0
There are 2 independent parts, one for each index of `groups`. A program takes and returns all parts, laid end to end along the dimension named above; an argument that names none is the same for every part. Nothing has to cross between parts.
Inputs may be any that keep to these rules, and one draw needn't show every extreme that they name: `adapter_ids`: every adapter is named by some block. `owner_slot`: each slot holds exactly one adapter. `lengths`: some block is full.
All inputs are finite; a program needn't handle non-finite values.
Results may differ from a plain program's by a relative error of at most 0.0039.
Values may be sent and summed in bfloat16 or wider, within the bound.
No kernel may reach another device: no remote copies, remote signals or barrier semaphores. Data moves between devices by JAX's collectives and lax.ppermute only.
A program may use at most 128 MiB of HBM per device.

v0:
```python
import jax
import jax.numpy as jnp
from jax import lax
from jax.sharding import PartitionSpec as P


def body(tokens, base_key, adapter_down, adapter_up, adapter_ids, owner_slot, lengths):
    tok_rows = tokens.shape[0]
    blocks_here = lengths.shape[0]
    block = tok_rows // blocks_here
    rank = adapter_down.shape[2]
    partial_base = jnp.dot(tokens, base_key, preferred_element_type=jnp.float32)
    base_part = lax.psum_scatter(partial_base, "tensor", scatter_dimension=1, tiled=True)
    spread = lax.all_to_all(tokens, "dp", split_axis=1, concat_axis=0, tiled=True)
    down_cols = lax.all_to_all(adapter_down, "dp", split_axis=1, concat_axis=0, tiled=True)
    all_ids = lax.all_gather(adapter_ids, "dp", axis=0, tiled=True)
    all_slots = owner_slot[all_ids[:, 0]]
    local_slots = owner_slot[adapter_ids[:, 0]]
    count = all_ids.shape[0]
    grouped = spread.reshape(count, block, spread.shape[1])
    picked = down_cols[all_slots]
    partial_value = jnp.einsum("bnf,bfr->bnr", grouped, picked, preferred_element_type=jnp.float32)
    partial_value = partial_value.reshape(-1, 128)
    summed = lax.psum_scatter(partial_value, "dp", scatter_dimension=0, tiled=True)
    summed = lax.psum(summed, "tensor")
    shrunk = summed.reshape(blocks_here, block, rank).astype(jnp.bfloat16)
    up_all = lax.all_gather(adapter_up, "dp", axis=0, tiled=True)
    delta = jnp.einsum(
        "bnr,brk->bnk", shrunk, up_all[local_slots], preferred_element_type=jnp.float32
    )
    positions = lax.broadcasted_iota(jnp.int32, (blocks_here, block), 1)
    inside = positions < lengths[:, None]
    total = base_part.reshape(blocks_here, block, -1) + delta
    keys = jnp.where(inside[:, :, None], total, jnp.zeros_like(total))
    return keys.reshape(tok_rows, -1).astype(jnp.bfloat16)


def solution(mesh):
    placed = (
        P(("groups", "dp"), "tensor"),
        P("tensor", None),
        P("dp", "tensor", None),
        P("dp", None, "tensor"),
        P(("groups", "dp"), None),
        P(),
        P(("groups", "dp")),
    )
    return jax.shard_map(
        body, mesh=mesh, in_specs=placed, out_specs=P(("groups", "dp"), "tensor"), check_vma=False
    )
```

profile of v0, /device:TPU:0, one launch (start us, length us, event | category | flops | bytes accessed | tf_op | source)
XLA Modules:
  0.0 224.6 jit_solution(641701928465077871)
XLA Ops:
  6.5 0.0 copy-start
  6.5 5.0 %copy.16 = bf16[2,4096,64]{2,0,1:T(2,128)(2,1)S(1)} copy(bf16[2,4096,64]{1,2,0:T(8,128)(2,1)} %param.9) | data formatting | bytes 2097152 | tf_op args[2]
  11.6 2.7 %reshape.102 = bf16[8,2,32768]{2,1,0:T(2,128)(2,1)} reshape(bf16[4096,2,64]{2,1,0:T(2,128)(2,1)S(1)} %bitcast.43) | data formatting | bytes 2097152
  14.3 7.3 %all-to-all-start = ((bf16[8,2,32768]{2,1,0:T(2,128)(2,1)}), bf16[8,2,32768]{2,1,0:T(2,128)(2,1)S(1)}, u32[]{:S(2)}, u32[]{:S(2)}) async-start(bf16[8,2,32768]{2,1,0:T(2,128)(2,1)} %reshape.102), calls=%async_computation.1 | async-start | bytes 2097152 | tf_op jit(solution)/shard_map/all_to_all | solution.py:15
  21.5 3.8 %copy.27 = bf16[48,8,8,512]{3,2,0,1:T(8,128)(2,1)} copy(bf16[48,8,8,512]{3,2,1,0:T(8,128)(2,1)} %bitcast.44) | data formatting | bytes 6291456 | tf_op jit(solution)/shard_map/all_to_all | solution.py:14
  25.4 21.9 %all-to-all-done = bf16[8,2,32768]{2,1,0:T(2,128)(2,1)S(1)} async-done(((bf16[8,2,32768]{2,1,0:T(2,128)(2,1)}), bf16[8,2,32768]{2,1,0:T(2,128)(2,1)S(1)}, u32[]{:S(2)}, u32[]{:S(2)}) %all-to-all-start) | async-done | bytes 1048608 | tf_op jit(solution)/shard_map/all_to_all | solution.py:15
  47.3 0.0 copy-start.3
  47.3 0.0 copy-start.1
  47.3 4.6 %all-to-all-start.1 = ((bf16[384,8,512]{2,0,1:T(8,128)(2,1)}), bf16[384,8,512]{2,0,1:T(8,128)(2,1)}, u32[]{:S(2)}, u32[]{:S(2)}) async-start(bf16[384,8,512]{2,0,1:T(8,128)(2,1)} %bitcast.40), calls=%async_computation.2 | async-start | bytes 6291456 | tf_op jit(solution)/shard_map/all_to_all | solution.py:14
  51.9 0.0 all-gather.2.cloned.1.call-start
  51.9 0.7 all-gather.2.cloned.1.call-update
  52.6 0.0 reduce-scatter.5.cloned.1.call-start
  52.7 0.0 copy-done.3
  52.7 0.6 dynamic-slice
  53.9 0.0 copy-done.1
  53.9 0.1 bitcast_dynamic-update-slice_fusion
  54.0 80.8 %all-reduce = s32[24]{0:T(128)S(1)} all-reduce(s32[24]{0:T(128)S(1)} %bitcast_dynamic-update-slice_fusion), channel_id=1, replica_groups=mesh['groups'=2,'dp'=8,'tensor'=2] {'dp'}, use_global_device_ids=true, to_apply=%add | all-reduce | flops 24 | bytes 192
  134.8 0.0 copy-done
  134.8 0.7 gather_fusion
  135.6 1.4 reshape.103
  137.0 1.4 copy.24
  138.5 0.6 gather_fusion.1
  139.1 0.0 all-to-all-done.1
  139.1 3.1 %convolution_bitcast_fusion = f32[24,128,64]{1,2,0:T(8,128)S(1)} fusion(bf16[24,512,64]{1,2,0:T(8,128)(2,1)S(1)} %gather_fusion.1, bf16[24,128,512]{2,1,0:T(8,128)(2,1)} %bitcast.12), kind=kOutput, calls=%fused_computation.5 | convolution fusion | flops 201326592 | bytes 5505024 | tf_op jit(solution)/shard_map/bnf,bfr->bnr/dot_general | solution.py:22
  142.2 0.5 copy.20
  142.7 1.2 reshape.64
  143.8 0.0 reduce-scatter.5.cloned.1.call-update
  143.9 0.0 copy-start.2
  143.9 0.0 reduce-scatter.3.cloned.1.call-start
  143.9 8.9 %fusion.6 = f32[384,1024]{1,0:T(8,128)} fusion(bf16[384,4096]{1,0:T(8,128)(2,1)} %param.7, bf16[4096,1024]{1,0:T(8,128)(2,1)} %param.8), kind=kOutput, calls=%fused_computation.23 | convolution fusion | flops 3221225472 | bytes 13107200 | tf_op jit(solution)/shard_map/dot_general | solution.py:12
  152.8 0.0 reduce-scatter.3.cloned.1.call-update
  152.9 0.6 gather_fusion.2
  153.5 0.0 copy-done.2
  153.5 0.1 iota_compare_fusion
  153.6 0.0 all-gather.2.cloned.1.call-done
  153.6 1.8 gather_fusion.3
  155.4 50.1 %reduce-scatter.5.cloned.1.call-done = f32[192,128]{1,0:T(8,128)} async-done(((f32[1536,128]{1,0:T(8,128)}), f32[192,128]{1,0:T(8,128)}) %reduce-scatter.5.cloned.1.call-update) | async-done | bytes 98320 | tf_op jit(solution)/shard_map/reduce_scatter | solution.py:24
  205.5 4.4 %psum.7 = bf16[192,128]{1,0:T(8,128)(2,1)S(1)} all-reduce(f32[192,128]{1,0:T(8,128)} %reduce-scatter.5.cloned.1.call-done), channel_id=1, replica_groups=mesh['groups'=2,'dp'=8,'tensor'=2] {'tensor'}, use_global_device_ids=true, to_apply=%region_2.0 | all-reduce | flops 24576 | bytes 147456 | tf_op jit(solution)/shard_map/psum | solution.py:25
  209.9 0.1 convert_element_type.13
  210.0 6.0 %reduce-scatter.3.cloned.1.call-done = f32[384,512]{1,0:T(8,128)} async-done(((f32[384,1024]{1,0:T(8,128)}), f32[384,512]{1,0:T(8,128)}) %reduce-scatter.3.cloned.1.call-update) | async-done | bytes 786448 | tf_op jit(solution)/shard_map/reduce_scatter | solution.py:13
  215.9 2.1 fusion.1
  (9 shorter events, 0.1 us)
Async XLA Ops:
  6.5 128.3 %copy-start = (s32[16]{0:T(128)S(1)}, s32[16]{0:T(128)}, u32[]{:S(2)}) copy-start(s32[16]{0:T(128)} %param.12) | copy-start | bytes 196
  14.3 33.0 %all-to-all-start = ((bf16[8,2,32768]{2,1,0:T(2,128)(2,1)}), bf16[8,2,32768]{2,1,0:T(2,128)(2,1)S(1)}, u32[]{:S(2)}, u32[]{:S(2)}) async-start(bf16[8,2,32768]{2,1,0:T(2,128)(2,1)} %reshape.102), calls=%async_computation.1 | async-start | bytes 2097152 | tf_op jit(solution)/shard_map/all_to_all | solution.py:15
  47.3 5.4 %copy-start.3 = (u32[32]{0:T(128)S(1)}, u32[32]{0:T(128)}, u32[]{:S(2)}) copy-start(u32[32]{0:T(128)} %constant.14) | copy-start | bytes 388
  47.3 6.6 %copy-start.1 = (s32[3,1]{0,1:T(1,128)S(1)}, s32[3,1]{0,1:T(1,128)}, u32[]{:S(2)}) copy-start(s32[3,1]{0,1:T(1,128)} %param.11) | copy-start | bytes 40
  47.3 91.8 %all-to-all-start.1 = ((bf16[384,8,512]{2,0,1:T(8,128)(2,1)}), bf16[384,8,512]{2,0,1:T(8,128)(2,1)}, u32[]{:S(2)}, u32[]{:S(2)}) async-start(bf16[384,8,512]{2,0,1:T(8,128)(2,1)} %bitcast.40), calls=%async_computation.2 | async-start | bytes 6291456 | tf_op jit(solution)/shard_map/all_to_all | solution.py:14
  51.9 101.7 %all-gather.2.cloned.1.call-start = ((), (), s32[]{:S(2)}) async-start(), calls=%async_computation.6 | async-start | bytes 1179648 | tf_op jit(solution)/shard_map/all_gather | solution.py:27
  52.6 152.9 %reduce-scatter.5.cloned.1.call-start = ((), (), s32[]{:S(2)}) async-start(), calls=%async_computation.5 | async-start | bytes 884736 | tf_op jit(solution)/shard_map/reduce_scatter | solution.py:24
  143.9 9.7 %copy-start.2 = (s32[3]{0:T(128)S(1)}, s32[3]{0:T(128)}, u32[]{:S(2)}) copy-start(s32[3]{0:T(128)} %param.13) | copy-start | bytes 40
  143.9 72.1 %reduce-scatter.3.cloned.1.call-start = ((), (), s32[]{:S(2)}) async-start(), calls=%async_computation.4 | async-start | bytes 2359296 | tf_op jit(solution)/shard_map/reduce_scatter | solution.py:13
Sparse Core Ops, SparseCore 0:
  54.9 68.8 all-gather.1
  144.0 61.4 reduce-scatter.4
  207.9 8.0 reduce-scatter.2
where the time goes:
time: 225 us
  blocking collectives  85.1 us (38%)
  waiting for transfers between devices  78.7 us (35%)
  local copies, waits for them, and re-layouts  20.6 us (9%)
  matrix products  14.1 us (6%)
  between operations  13.9 us (6%)
  starting transfers between devices  12 us (5%)
    unnamed x1, blocking collectives  80.8 us
    reduce_scatter x1, waiting for transfers between devices, body(): lax.psum_scatter(partial_value, 'dp', scatter_dimension=0, tiled=True)  50.1 us
    all_to_all x1, waiting for transfers between devices, body(): lax.all_to_all(adapter_down, 'dp', split_axis=1, concat_axis=0, tiled=True)  21.9 us
    unnamed x14, local copies, waits for them, and re-layouts  9.86 us
    dot_general x1, matrix products, body(): partial_base = jnp.dot(tokens, base_key, preferred_element_type=jnp.float32)  8.91 us
    all_to_all x1, starting transfers between devices, body(): lax.all_to_all(adapter_down, 'dp', split_axis=1, concat_axis=0, tiled=True)  7.28 us
    reduce_scatter x1, waiting for transfers between devices, body(): lax.psum_scatter(partial_base, 'tensor', scatter_dimension=1, tiled=True)  5.95 us
    all_to_all x1, starting transfers between devices, body(): lax.all_to_all(tokens, 'dp', split_axis=1, concat_axis=0, tiled=True)  4.57 us
  transfers between devices with their start and end apart: 5, of which 3 were waited for; matrix products, arithmetic and copies ran while one was open for 11% of the time, Pallas kernels for 0%

commit v1 on v0

v1 whole, which is shorter than its diff:
```python
import functools

import jax
import jax.numpy as jnp
from jax import lax
from jax.experimental import pallas as pl
from jax.experimental.pallas import tpu as pltpu
from jax.sharding import PartitionSpec as P

LANES = 128
ANY = pl.BlockSpec(memory_space=pl.ANY)
SMEM = pl.BlockSpec(memory_space=pltpu.SMEM)
BIG = pltpu.CompilerParams(vmem_limit_bytes=32 * 1024 * 1024)


def pack_kernel(where, *refs):
    ways = (len(refs) - 1) // 2
    downs, up_ref, outs = refs[:ways], refs[ways], refs[ways + 1 :]
    for way in range(ways):
        down_ref, out_ref = downs[way], outs[way]
        share = where[way]
        adapters, feats, rank = down_ref.shape
        half = feats // 2
        wide = up_ref.shape[2] // LANES
        up_rows = (out_ref.shape[1] - half) // wide
        for a in range(adapters):
            out_ref[a, :half, :] = jnp.concatenate([down_ref[a, :half, :], down_ref[a, half:, :]], axis=1)
            row = pl.multiple_of(share * up_rows, up_rows)
            part = up_ref[a, pl.ds(row, up_rows), :]
            part = jnp.concatenate([part[:, c * LANES : (c + 1) * LANES] for c in range(wide)], axis=0)
            out_ref[a, half:, :] = part.astype(out_ref.dtype)


def pack(down, up, shares, share_of):
    adapters, feats, rank = down.shape
    step = feats // shares
    ways = len(share_of)
    rows = step // 2 + rank * up.shape[2] // shares // LANES

    def at(way):
        return lambda i, s: (0, s[way], 0)

    return pl.pallas_call(
        pack_kernel,
        grid_spec=pltpu.PrefetchScalarGridSpec(
            num_scalar_prefetch=1,
            grid=(1,),
            in_specs=[pl.BlockSpec((adapters, step, rank), at(w)) for w in range(ways)]
            + [pl.BlockSpec(up.shape, lambda i, s: (0, 0, 0))],
            out_specs=[pl.BlockSpec((adapters, rows, LANES), lambda i, s: (0, 0, 0)) for _ in range(ways)],
        ),
        out_shape=[jax.ShapeDtypeStruct((adapters, rows, LANES), down.dtype) for _ in range(ways)],
        compiler_params=BIG,
        name="pack",
    )(jnp.stack(share_of).astype(jnp.int32), *([down] * ways), up.astype(jnp.float32))


def pick_kernel(targets, ring, pair, *refs):
    here, owner = refs[0], refs[1]
    ids = refs[2 : 2 + targets]
    pieces = refs[2 + targets : 2 + targets + ring * pair]
    outs = refs[2 + targets + ring * pair : -1]
    sems = refs[-1]
    blocks = outs[0].shape[0]
    per = pieces[0].shape[0]
    for k in range(targets):
        for b in range(blocks):
            slot = owner[ids[k][b, 0]]
            chip = slot // per
            local = slot - chip * per
            dz = lax.rem(chip // pair - here[0] + ring, ring)
            dy = lax.rem(lax.rem(chip, pair) - here[1] + pair, pair)
            piece = dz * pair + dy
            for j in range(ring * pair):

                @pl.when(piece == j)
                def _():
                    pltpu.make_async_copy(pieces[j].at[local], outs[k].at[b], sems.at[k, b]).start()

    for k in range(targets):
        for b in range(blocks):
            pltpu.make_async_copy(pieces[0].at[0], outs[k].at[b], sems.at[k, b]).wait()


def pick(here, owner, ids, pieces, ring, pair):
    targets = len(ids)
    blocks = ids[0].shape[0]
    shape = (blocks,) + pieces[0].shape[1:]
    return pl.pallas_call(
        functools.partial(pick_kernel, targets, ring, pair),
        in_specs=[SMEM] * (2 + targets) + [ANY] * len(pieces),
        out_specs=[ANY] * targets,
        out_shape=[jax.ShapeDtypeStruct(shape, pieces[0].dtype)] * targets,
        scratch_shapes=[pltpu.SemaphoreType.DMA((targets, blocks))],
        name="pick",
    )(here, owner, *ids, *pieces)


def base_kernel(side, tok_ref, key_ref, out_ref):
    part = jnp.dot(tok_ref[...], key_ref[...], preferred_element_type=jnp.float32)

    @pl.when(pl.program_id(0) == 0)
    def _():
        out_ref[...] = part

    @pl.when(pl.program_id(0) > 0)
    def _():
        out_ref[...] += part


def base_half(tokens, base_key, side, sides):
    rows, depth = tokens.shape
    wide = base_key.shape[1] // sides
    step = 1024
    return pl.pallas_call(
        base_kernel,
        grid_spec=pltpu.PrefetchScalarGridSpec(
            num_scalar_prefetch=1,
            grid=(depth // step,),
            in_specs=[
                pl.BlockSpec((rows, step), lambda i, s: (0, i)),
                pl.BlockSpec((step, wide), lambda i, s: (i, s[0])),
            ],
            out_specs=pl.BlockSpec((rows, wide), lambda i, s: (0, 0)),
        ),
        out_shape=jax.ShapeDtypeStruct((rows, wide), jnp.float32),
        compiler_params=BIG,
        cost_estimate=pl.CostEstimate(
            flops=2 * rows * depth * wide, bytes_accessed=2 * depth * (rows + wide) + 4 * rows * wide, transcendentals=0
        ),
        name="base",
    )(side.reshape(1), tokens, base_key)


def rank_kernel(where, tok_ref, *refs):
    parts, (sum_ref, up_ref, up_acc) = refs[:-3], refs[-3:]
    shares = len(parts)
    step = tok_ref.shape[1] // shares
    half = step // 2
    rank = sum_ref.shape[1]
    wide = up_ref.shape[2] // LANES
    up_rows = rank // shares
    low = high = None
    for k in range(shares):
        start = where[k] * step
        one = tok_ref[:, pl.ds(pl.multiple_of(start, LANES), half)]
        two = tok_ref[:, pl.ds(pl.multiple_of(start + half, LANES), half)]
        down = parts[k][0, :half, :]
        first = jnp.dot(one, down, preferred_element_type=jnp.float32)
        second = jnp.dot(two, down, preferred_element_type=jnp.float32)
        low = first if low is None else low + first
        high = second if high is None else high + second
        up = parts[k][0, half:, :].astype(jnp.float32)
        for c in range(wide):
            row = pl.multiple_of(where[k] * up_rows, up_rows)
            up_acc[pl.ds(row, up_rows), c * LANES : (c + 1) * LANES] = up[c * up_rows : (c + 1) * up_rows, :]
    sum_ref[...] = low[:, :rank] + high[:, rank:]
    up_ref[0] = up_acc[...].astype(up_ref.dtype)


def rank_sums(tokens, parts, share_of, rank, up_wide):
    rows, feats = tokens.shape
    blocks = parts[0].shape[0]
    block = rows // blocks
    return pl.pallas_call(
        rank_kernel,
        grid_spec=pltpu.PrefetchScalarGridSpec(
            num_scalar_prefetch=1,
            grid=(blocks,),
            in_specs=[pl.BlockSpec((block, feats), lambda i, s: (i, 0))]
            + [pl.BlockSpec((1,) + p.shape[1:], lambda i, s: (i, 0, 0)) for p in parts],
            out_specs=[
                pl.BlockSpec((block, rank), lambda i, s: (i, 0)),
                pl.BlockSpec((1, rank, up_wide), lambda i, s: (i, 0, 0)),
            ],
            scratch_shapes=[pltpu.VMEM((rank, up_wide), jnp.float32)],
        ),
        out_shape=[
            jax.ShapeDtypeStruct((rows, rank), jnp.float32),
            jax.ShapeDtypeStruct((blocks, rank, up_wide), tokens.dtype),
        ],
        compiler_params=BIG,
        cost_estimate=pl.CostEstimate(
            flops=4 * rows * feats * rank, bytes_accessed=2 * rows * feats + 2 * len(parts) * parts[0].size, transcendentals=0
        ),
        name="rank",
    )(jnp.stack(share_of).astype(jnp.int32), tokens, *parts)


def final_kernel(lengths, mine, theirs, up_ref, base_a, base_b, out_ref):
    shrunk = (mine[...] + theirs[...]).astype(jnp.bfloat16)
    delta = jnp.dot(shrunk, up_ref[0], preferred_element_type=jnp.float32)
    total = base_a[...] + base_b[...] + delta
    rows = lax.broadcasted_iota(jnp.int32, total.shape, 0)
    out_ref[...] = jnp.where(rows < lengths[pl.program_id(0)], total, 0.0).astype(out_ref.dtype)


def final(lengths, mine, theirs, up, base_a, base_b, dtype):
    blocks, rank, wide = up.shape
    block = mine.shape[0] // blocks
    row = lambda i, s: (i, 0)
    return pl.pallas_call(
        final_kernel,
        grid_spec=pltpu.PrefetchScalarGridSpec(
            num_scalar_prefetch=1,
            grid=(blocks,),
            in_specs=[
                pl.BlockSpec((block, rank), row),
                pl.BlockSpec((block, rank), row),
                pl.BlockSpec((1, rank, wide), lambda i, s: (i, 0, 0)),
                pl.BlockSpec((block, wide), row),
                pl.BlockSpec((block, wide), row),
            ],
            out_specs=pl.BlockSpec((block, wide), row),
        ),
        out_shape=jax.ShapeDtypeStruct((blocks * block, wide), dtype),
        name="final",
    )(lengths, mine, theirs, up, base_a, base_b)


def body(tokens, base_key, adapter_down, adapter_up, adapter_ids, owner_slot, lengths):
    groups, dp, sides = lax.axis_size("groups"), lax.axis_size("dp"), lax.axis_size("tensor")
    pair = 2 if dp % 2 == 0 else 1
    ring = dp // pair
    shares = groups * pair
    g, d, t = lax.axis_index("groups"), lax.axis_index("dp"), lax.axis_index("tensor")
    z, y = d // pair, d % pair
    rank, up_wide = adapter_up.shape[1:]

    def along_ring(x, step):
        return lax.ppermute(
            x, "dp", [(a * pair + b, (a + step) % ring * pair + b) for a in range(ring) for b in range(pair)]
        )

    def in_plane(x, kg, ky):
        pairs = []
        for a in range(groups):
            for c in range(ring):
                for b in range(pair):
                    to = (a + kg) % groups * dp + c * pair + (b + ky) % pair
                    pairs.append((a * dp + c * pair + b, to))
        return lax.ppermute(x, ("groups", "dp"), pairs)

    def across(x):
        return lax.ppermute(x, "tensor", [(i, (i + 1) % sides) for i in range(sides)])

    offsets = [(k // pair, k % pair) for k in range(shares)]
    ids = [adapter_ids] + [in_plane(adapter_ids, -kg, -ky) for kg, ky in offsets[1:]]

    packed = pack(adapter_down, adapter_up, shares, [g * pair + (y + w) % pair for w in range(pair)])
    pieces = {(0, 0): packed[0]}
    for w in range(1, pair):
        pieces[0, pair - w] = in_plane(packed[w], 0, w)
    for k in range(1, ring // 2 + 1):
        last = 2 * k == ring
        for w in range(pair):
            if not last or w == 0:
                pieces[ring - k, w] = along_ring(pieces[(ring - k + 1) % ring, w], 1)
            if not last or w > 0:
                pieces[k, w] = along_ring(pieces[k - 1, w], -1)
    pieces = [pieces[a, w] for a in range(ring) for w in range(pair)]

    base_out = base_half(tokens, base_key, (t + 1) % sides, sides)
    base_in = across(base_out)
    base_mine = base_half(tokens, base_key, t, sides)

    here = jnp.stack([z, y]).astype(jnp.int32)
    picked = pick(here, owner_slot, ids, pieces, ring, pair)
    parts = [picked[0]] + [in_plane(picked[k], *offsets[k]) for k in range(1, shares)]
    share_of = [(g - kg) % groups * pair + (y - ky) % pair for kg, ky in offsets]
    mine, up = rank_sums(tokens, parts, share_of, rank, up_wide)
    theirs = across(mine)
    return final(lengths, mine, theirs, up, base_mine, base_in, tokens.dtype)


def solution(mesh):
    placed = (
        P(("groups", "dp"), "tensor"),
        P("tensor", None),
        P("dp", "tensor", None),
        P("dp", None, "tensor"),
        P(("groups", "dp"), None),
        P(),
        P(("groups", "dp")),
    )
    return jax.shard_map(
        body, mesh=mesh, in_specs=placed, out_specs=P(("groups", "dp"), "tensor"), check_vma=False
    )
```

time: 225 us -> 147 us (0.65)
  blocking collectives: 85.1 us -> 0 us
  Pallas kernels: 0 us -> 71.2 us
  waiting for transfers between devices: 78.7 us -> 35.6 us
  matrix products: 14.1 us -> 0 us
  between operations: 13.9 us -> 0.11 us
  starting transfers between devices: 12 us -> 23.9 us
  local copies, waits for them, and re-layouts: 20.6 us -> 14.7 us
    unnamed x1 -> x0, blocking collectives: 80.8 us -> none
    pallas_call x0 -> x6, Pallas kernels: none -> 71.2 us  [the longest x1 55.7 us: pick(): pl.pallas_call(functools.partial(pick_kernel, targets, ring, pair), in_sp...]
    reduce_scatter x2 -> x0, waiting for transfers between devices: 56.1 us -> none  [the longest x1 50.1 us: body(): lax.psum_scatter(partial_value, 'dp', scatter_dimension=0, tiled=True)]
    ppermute x0 -> x15, waiting for transfers between devices: none -> 35.6 us  [the longest x7 28.7 us: in_plane(): return lax.ppermute(x, ('groups', 'dp'), pairs)]
    ppermute x0 -> x15, starting transfers between devices: none -> 23.9 us  [the longest x7 12.1 us: in_plane(): return lax.ppermute(x, ('groups', 'dp'), pairs)]
    all_to_all x2 -> x0, waiting for transfers between devices: 21.9 us -> none  [the longest x1 21.9 us: body(): lax.all_to_all(adapter_down, 'dp', split_axis=1, concat_axis=0, tiled=True)]
    dot_general x3 -> x0, matrix products: 14.1 us -> none  [the longest x1 8.91 us: body(): partial_base = jnp.dot(tokens, base_key, preferred_element_type=jnp.float32)]
    all_to_all x2 -> x0, starting transfers between devices: 11.9 us -> none  [the longest x1 7.28 us: body(): lax.all_to_all(adapter_down, 'dp', split_axis=1, concat_axis=0, tiled=True)]
  transfers between devices with their start and end apart: 5 -> 15, of which waited for: 3 -> 8; matrix products, arithmetic and copies ran while one was open for 11% -> 1% of each run, Pallas kernels for 0% -> 45%
where the time goes in v1:
time: 147 us; the launch traced here: 146 us
  Pallas kernels  71.2 us (48%)
  waiting for transfers between devices  35.6 us (24%)
  starting transfers between devices  23.9 us (16%)
  local copies, waits for them, and re-layouts  14.7 us (10%)
    pallas_call x1, Pallas kernels, pick(): pl.pallas_call(functools.partial(pick_kernel, targets, ring, pair), in_sp...  55.7 us
    ppermute x7, waiting for transfers between devices, in_plane(): return lax.ppermute(x, ('groups', 'dp'), pairs)  28.7 us
    unnamed x34, local copies, waits for them, and re-layouts  14.7 us
    ppermute x7, starting transfers between devices, in_plane(): return lax.ppermute(x, ('groups', 'dp'), pairs)  12.1 us
    ppermute x6, starting transfers between devices, along_ring(): lax.ppermute(x, 'dp', [(a * pair + b, (a + step) % ring * pair + b) for a...  11.8 us
    pallas_call x2, Pallas kernels, base_half(): pl.pallas_call(base_kernel, grid_spec=pltpu.PrefetchScalarGridSpec(num_sc...  7.1 us
    ppermute x6, waiting for transfers between devices, along_ring(): lax.ppermute(x, 'dp', [(a * pair + b, (a + step) % ring * pair + b) for a...  6.92 us
    pallas_call x1, Pallas kernels, final(): pl.pallas_call(final_kernel, grid_spec=pltpu.PrefetchScalarGridSpec(num_s...  4.01 us
  transfers between devices with their start and end apart: 15, of which 8 were waited for; matrix products, arithmetic and copies ran while one was open for 1% of the time, Pallas kernels for 45%

profile of v1, /device:TPU:0, one launch (start us, length us, event | category | flops | bytes accessed | tf_op | source)
XLA Modules:
  0.0 146.3 jit_solution(1230121276649347388)
XLA Ops:
  0.0 2.8 %copy.11.refs_0_.refs_1_ = bf16[2,4096,64]{2,1,0:T(8,128)(2,1)} copy(bf16[2,4096,64]{1,2,0:T(8,128)(2,1)} %param.9) | data formatting | bytes 2097152 | tf_op args[2]
  2.8 0.1 pad_add_fusion.2.where
  2.9 1.7 %copy-done.3 = bf16[2,4096,64]{2,1,0:T(8,128)(2,1)S(1)} copy-done((bf16[2,4096,64]{2,1,0:T(8,128)(2,1)S(1)}, bf16[2,4096,64]{2,1,0:T(8,128)(2,1)}, u32[]{:S(2)}) %copy-start.3) | copy-done | bytes 1048600
  4.6 0.8 pack.1
  5.4 0.0 copy-start.6
  5.4 3.0 %collective-permute-start.3 = (bf16[2,576,128]{2,1,0:T(8,128)(2,1)S(1)}, bf16[2,576,128]{2,1,0:T(8,128)(2,1)}, u32[]{:S(2)}, u32[]{:S(2)}) collective-permute-start(bf16[2,576,128]{2,1,0:T(8,128)(2,1)S(1)} %get-tuple-element.14), channel_id=1, source_target_pairs={{0,2},{2,0},{4,6},{6,4},{8,10},{10,8},{12,14},{14,12},{16,18},{18,... | collective-permute-start | bytes 884744 | tf_op jit(solution)/shard_map/ppermute | solution.py:242
  8.5 1.6 %collective-permute-start.6 = (bf16[2,576,128]{2,1,0:T(8,128)(2,1)S(1)}, bf16[2,576,128]{2,1,0:T(8,128)(2,1)}, u32[]{:S(2)}, u32[]{:S(2)}) collective-permute-start(bf16[2,576,128]{2,1,0:T(8,128)(2,1)S(1)} %get-tuple-element.13.refs_6_), channel_id=1, source_target_pairs={{0,4},{2,6},{4,8},{6,10},{8,12},{10,14},{12,0},{14,2},{1,5},{3,7},... | collective-permute-start | bytes 884744 | tf_op jit(solution)/shard_map/ppermute | solution.py:231
  10.0 5.5 %collective-permute-done.3.refs_7_ = bf16[2,576,128]{2,1,0:T(8,128)(2,1)} collective-permute-done((bf16[2,576,128]{2,1,0:T(8,128)(2,1)S(1)}, bf16[2,576,128]{2,1,0:T(8,128)(2,1)}, u32[]{:S(2)}, u32[]{:S(2)}) %collective-permute-start.3) | collective-permute-done | bytes 294944 | tf_op jit(solution)/shard_map/ppermute | solution.py:242
  15.6 3.8 %collective-permute-start.5 = (bf16[2,576,128]{2,1,0:T(8,128)(2,1)}, bf16[2,576,128]{2,1,0:T(8,128)(2,1)}, u32[]{:S(2)}, u32[]{:S(2)}) collective-permute-start(bf16[2,576,128]{2,1,0:T(8,128)(2,1)} %collective-permute-done.3.refs_7_), channel_id=1, source_target_pairs={{0,12},{2,14},{4,0},{6,2},{8,4},{10,6},{12,8},{14,10},{1,13},{3,15... | collective-permute-start | bytes 884744 | tf_op jit(solution)/shard_map/ppermute | solution.py:231
  19.4 0.4 collective-permute-start.4
  19.8 0.1 copy.13.refs_2_
  19.9 1.5 %collective-permute-start = (s32[3,1]{1,0:T(4,128)S(1)}, s32[3,1]{1,0:T(4,128)S(1)}, u32[]{:S(2)}, u32[]{:S(2)}) collective-permute-start(s32[3,1]{1,0:T(4,128)S(1)} %copy.13.refs_2_), channel_id=1, source_target_pairs={{0,2},{2,0},{4,6},{6,4},{8,10},{10,8},{12,14},{14,12},{16,18},{18,... | collective-permute-start | bytes 44 | tf_op jit(solution)/shard_map/ppermute | solution.py:242
  21.5 1.6 %collective-permute-start.9 = (bf16[2,576,128]{2,1,0:T(8,128)(2,1)}, bf16[2,576,128]{2,1,0:T(8,128)(2,1)}, u32[]{:S(2)}, u32[]{:S(2)}) collective-permute-start(bf16[2,576,128]{2,1,0:T(8,128)(2,1)} %collective-permute-done.3.refs_7_), channel_id=1, source_target_pairs={{0,4},{2,6},{4,8},{6,10},{8,12},{10,14},{12,0},{14,2},{1,5},{3,7},... | collective-permute-start | bytes 884744 | tf_op jit(solution)/shard_map/ppermute | solution.py:231
  23.0 0.0 collective-permute-done.6.refs_12_
  23.0 0.0 collective-permute-start.7
  23.1 4.2 %collective-permute-done.5.refs_9_ = bf16[2,576,128]{2,1,0:T(8,128)(2,1)} collective-permute-done((bf16[2,576,128]{2,1,0:T(8,128)(2,1)}, bf16[2,576,128]{2,1,0:T(8,128)(2,1)}, u32[]{:S(2)}, u32[]{:S(2)}) %collective-permute-start.5) | collective-permute-done | bytes 294944 | tf_op jit(solution)/shard_map/ppermute | solution.py:231
  27.3 4.4 %collective-permute-start.8 = (bf16[2,576,128]{2,1,0:T(8,128)(2,1)}, bf16[2,576,128]{2,1,0:T(8,128)(2,1)}, u32[]{:S(2)}, u32[]{:S(2)}) collective-permute-start(bf16[2,576,128]{2,1,0:T(8,128)(2,1)} %collective-permute-done.5.refs_9_), channel_id=1, source_target_pairs={{0,12},{2,14},{4,0},{6,2},{8,4},{10,6},{12,8},{14,10},{1,13},{3,15... | collective-permute-start | bytes 884744 | tf_op jit(solution)/shard_map/ppermute | solution.py:231
  31.6 3.4 %copy-done = bf16[4096,1024]{1,0:T(8,128)(2,1)S(1)} copy-done((bf16[4096,1024]{1,0:T(8,128)(2,1)S(1)}, bf16[4096,1024]{1,0:T(8,128)(2,1)}, u32[]{:S(2)}) %copy-start) | copy-done | bytes 8388632
  35.0 4.0 %base.3 = f32[384,512]{1,0:T(8,128)} custom-call(s32[1]{0:T(128)} %bitcast.9.side, bf16[384,4096]{1,0:T(8,128)(2,1)S(1)} %copy-done.2, bf16[4096,1024]{1,0:T(8,128)(2,1)S(1)} %copy-done), custom_call_target="tpu_custom_call" | custom-call | flops 1610612736 | bytes 8126464 | tf_op jit(solution)/shard_map/base/pallas_call | solution.py:115
  39.0 0.0 collective-permute-done.refs_3_
  39.0 1.6 %collective-permute-start.1 = (s32[3,1]{1,0:T(4,128)S(1)}, s32[3,1]{1,0:T(4,128)S(1)}, u32[]{:S(2)}, u32[]{:S(2)}) collective-permute-start(s32[3,1]{1,0:T(4,128)S(1)} %copy.13.refs_2_), channel_id=1, source_target_pairs={{0,16},{2,18},{4,20},{6,22},{8,24},{10,26},{12,28},{14,30},{16,0},... | collective-permute-start | bytes 44 | tf_op jit(solution)/shard_map/ppermute | solution.py:242
  40.6 2.1 %collective-permute-done.1.refs_4_ = s32[3,1]{1,0:T(4,128)S(1)} collective-permute-done((s32[3,1]{1,0:T(4,128)S(1)}, s32[3,1]{1,0:T(4,128)S(1)}, u32[]{:S(2)}, u32[]{:S(2)}) %collective-permute-start.1) | collective-permute-done | bytes 44 | tf_op jit(solution)/shard_map/ppermute | solution.py:242
  42.7 2.4 %collective-permute-start.2 = (s32[3,1]{1,0:T(4,128)S(1)}, s32[3,1]{1,0:T(4,128)S(1)}, u32[]{:S(2)}, u32[]{:S(2)}) collective-permute-start(s32[3,1]{1,0:T(4,128)S(1)} %copy.13.refs_2_), channel_id=1, source_target_pairs={{0,18},{2,16},{4,22},{6,20},{8,26},{10,24},{12,30},{14,28},{16,2},... | collective-permute-start | bytes 44 | tf_op jit(solution)/shard_map/ppermute | solution.py:242
  45.1 2.1 %collective-permute-done.2.refs_5_ = s32[3,1]{1,0:T(4,128)S(1)} collective-permute-done((s32[3,1]{1,0:T(4,128)S(1)}, s32[3,1]{1,0:T(4,128)S(1)}, u32[]{:S(2)}, u32[]{:S(2)}) %collective-permute-start.2) | collective-permute-done | bytes 44 | tf_op jit(solution)/shard_map/ppermute | solution.py:242
  47.2 0.0 collective-permute-start.14
  47.2 0.6 pad_add_fusion.1.refs_0_
  47.8 0.0 collective-permute-done.4.refs_8_
  47.8 0.0 collective-permute-done.7.refs_10_
  47.8 0.0 collective-permute-done.9.refs_13_
  47.8 2.7 %collective-permute-done.8.refs_11_ = bf16[2,576,128]{2,1,0:T(8,128)(2,1)} collective-permute-done((bf16[2,576,128]{2,1,0:T(8,128)(2,1)}, bf16[2,576,128]{2,1,0:T(8,128)(2,1)}, u32[]{:S(2)}, u32[]{:S(2)}) %collective-permute-start.8) | collective-permute-done | bytes 294944 | tf_op jit(solution)/shard_map/ppermute | solution.py:231
  50.5 55.7 %pick.1 = (bf16[3,576,128]{2,1,0:T(8,128)(2,1)}, bf16[3,576,128]{2,1,0:T(8,128)(2,1)}, bf16[3,576,128]{2,1,0:T(8,128)(2,1)}, bf16[3,576,128]{2,1,0:T(8,128)(2,1)}) custom-call(s32[2]{0:T(128)} %pad_add_fusion.1.refs_0_, s32[16]{0:T(128)} %refs_1_.2, s32[3,1]{1,0:T(4,128)} %copy-done.11, s32[3,1]{1,0:T(4,128)} %copy-done.12, s32[3,1]{1,0:T(4,128)} %copy-done.13, ...), custom_call_target="tpu_custom_call" | custom-call | tf_op jit(solution)/shard_map/pick/pallas_call | solution.py:89
  106.2 1.5 %collective-permute-start.10 = (bf16[3,576,128]{2,1,0:T(8,128)(2,1)}, bf16[3,576,128]{2,1,0:T(8,128)(2,1)}, u32[]{:S(2)}, u32[]{:S(2)}) collective-permute-start(bf16[3,576,128]{2,1,0:T(8,128)(2,1)} %get-tuple-element.16), channel_id=1, source_target_pairs={{0,2},{2,0},{4,6},{6,4},{8,10},{10,8},{12,14},{14,12},{16,18},{18,... | collective-permute-start | bytes 1327112 | tf_op jit(solution)/shard_map/ppermute | solution.py:242
  107.7 1.5 %collective-permute-start.11 = (bf16[3,576,128]{2,1,0:T(8,128)(2,1)}, bf16[3,576,128]{2,1,0:T(8,128)(2,1)}, u32[]{:S(2)}, u32[]{:S(2)}) collective-permute-start(bf16[3,576,128]{2,1,0:T(8,128)(2,1)} %get-tuple-element.17), channel_id=1, source_target_pairs={{0,16},{2,18},{4,20},{6,22},{8,24},{10,26},{12,28},{14,30},{16,0},... | collective-permute-start | bytes 1327112 | tf_op jit(solution)/shard_map/ppermute | solution.py:242
  109.2 0.6 collective-permute-start.12
  109.7 0.1 pad_add_fusion.where
  109.8 8.9 %collective-permute-done.10.refs_1_ = bf16[3,576,128]{2,1,0:T(8,128)(2,1)} collective-permute-done((bf16[3,576,128]{2,1,0:T(8,128)(2,1)}, bf16[3,576,128]{2,1,0:T(8,128)(2,1)}, u32[]{:S(2)}, u32[]{:S(2)}) %collective-permute-start.10) | collective-permute-done | bytes 442400 | tf_op jit(solution)/shard_map/ppermute | solution.py:242
  118.7 2.4 %collective-permute-done.11.refs_2_ = bf16[3,576,128]{2,1,0:T(8,128)(2,1)} collective-permute-done((bf16[3,576,128]{2,1,0:T(8,128)(2,1)}, bf16[3,576,128]{2,1,0:T(8,128)(2,1)}, u32[]{:S(2)}, u32[]{:S(2)}) %collective-permute-start.11) | collective-permute-done | bytes 442400 | tf_op jit(solution)/shard_map/ppermute | solution.py:242
  121.1 7.7 %collective-permute-done.12.refs_3_ = bf16[3,576,128]{2,1,0:T(8,128)(2,1)} collective-permute-done((bf16[3,576,128]{2,1,0:T(8,128)(2,1)}, bf16[3,576,128]{2,1,0:T(8,128)(2,1)}, u32[]{:S(2)}, u32[]{:S(2)}) %collective-permute-start.12) | collective-permute-done | bytes 442400 | tf_op jit(solution)/shard_map/ppermute | solution.py:242
  128.8 1.0 copy-done.5
  129.8 3.7 %rank.1 = (f32[384,64]{1,0:T(8,128)S(1)}, bf16[3,64,512]{2,1,0:T(8,128)(2,1)S(1)}) custom-call(s32[4]{0:T(128)S(1)} %pad_add_fusion.where, bf16[384,4096]{1,0:T(8,128)(2,1)S(1)} %copy-done.2, bf16[3,576,128]{2,1,0:T(8,128)(2,1)S(1)} %copy-done.5, bf16[3,576,128]{2,1,0:T(8,128)(2,1)} %collective-permute-done.10.refs_1_, ...), custom_call_target="tpu_custom_call" | custom-call | flops 402653184 | bytes 4915200 | tf_op jit(solution)/shard_map/rank/pallas_call | solution.py:165
  133.5 0.7 copy-done.8
  134.2 3.5 %copy-done.1 = bf16[4096,1024]{1,0:T(8,128)(2,1)S(1)} copy-done((bf16[4096,1024]{1,0:T(8,128)(2,1)S(1)}, bf16[4096,1024]{1,0:T(8,128)(2,1)}, u32[]{:S(2)}) %copy-start.1) | copy-done | bytes 8388632
  137.6 3.1 %base.2.base_a = f32[384,512]{1,0:T(8,128)S(1)} custom-call(s32[1]{0:T(128)} %bitcast.8.side, bf16[384,4096]{1,0:T(8,128)(2,1)S(1)} %copy-done.2, bf16[4096,1024]{1,0:T(8,128)(2,1)S(1)} %copy-done.1), custom_call_target="tpu_custom_call" | custom-call | flops 1610612736 | bytes 8126464 | tf_op jit(solution)/shard_map/base/pallas_call | solution.py:115
  140.7 0.9 copy-done.4
  141.6 0.0 collective-permute-done.14.base_b
  141.6 0.0 collective-permute-done.13.theirs
  141.6 0.7 copy-done.9
  142.3 4.0 %final.1 = bf16[384,512]{1,0:T(8,128)(2,1)} custom-call(s32[3]{0:T(128)} %lengths.1, f32[384,64]{1,0:T(8,128)} %copy-done.7, f32[384,64]{1,0:T(8,128)} %copy-done.9, bf16[3,64,512]{2,1,0:T(8,128)(2,1)} %copy-done.8, f32[384,512]{1,0:T(8,128)} %copy-done.4, f32[384,512]{1,0:T(8,128)} %collective-permute-done.14.base_b), custom_call_target="tpu_custom_call" | custom-call | tf_op jit(solution)/shard_map/final/pallas_call | solution.py:202
  (26 shorter events, 0.1 us)
Async XLA Ops:
  0.0 2.8 %copy-start.10 = (bf16[2,64,512]{2,1,0:T(8,128)(2,1)S(1)}, bf16[2,64,512]{2,1,0:T(8,128)(2,1)}, u32[]{:S(2)}) copy-start(bf16[2,64,512]{2,1,0:T(8,128)(2,1)} %param.10) | copy-start | bytes 393220
  0.0 19.8 %copy-start.15 = (s32[3,1]{0,1:T(1,128)S(1)}, s32[3,1]{0,1:T(1,128)}, u32[]{:S(2)}) copy-start(s32[3,1]{0,1:T(1,128)} %param.11) | copy-start | bytes 40
  2.8 28.9 %copy-start.2 = (bf16[384,4096]{1,0:T(8,128)(2,1)S(1)}, bf16[384,4096]{1,0:T(8,128)(2,1)}, u32[]{:S(2)}) copy-start(bf16[384,4096]{1,0:T(8,128)(2,1)} %tok_ref.5) | copy-start | bytes 9437188
  2.9 1.7 %copy-start.3 = (bf16[2,4096,64]{2,1,0:T(8,128)(2,1)S(1)}, bf16[2,4096,64]{2,1,0:T(8,128)(2,1)}, u32[]{:S(2)}) copy-start(bf16[2,4096,64]{2,1,0:T(8,128)(2,1)} %copy.11.refs_0_.refs_1_) | copy-start | bytes 3145732
  5.4 33.6 %copy-start.6 = (bf16[2,576,128]{2,1,0:T(8,128)(2,1)}, bf16[2,576,128]{2,1,0:T(8,128)(2,1)S(1)}, u32[]{:S(2)}) copy-start(bf16[2,576,128]{2,1,0:T(8,128)(2,1)S(1)} %get-tuple-element.13.refs_6_) | copy-start | bytes 884740
  5.4 10.1 %collective-permute-start.3 = (bf16[2,576,128]{2,1,0:T(8,128)(2,1)S(1)}, bf16[2,576,128]{2,1,0:T(8,128)(2,1)}, u32[]{:S(2)}, u32[]{:S(2)}) collective-permute-start(bf16[2,576,128]{2,1,0:T(8,128)(2,1)S(1)} %get-tuple-element.14), channel_id=1, source_target_pairs={{0,2},{2,0},{4,6},{6,4},{8,10},{10,8},{12,14},{14,12},{16,18},{18,... | collective-permute-start | bytes 884744 | tf_op jit(solution)/shard_map/ppermute | solution.py:242
  8.5 14.6 %collective-permute-start.6 = (bf16[2,576,128]{2,1,0:T(8,128)(2,1)S(1)}, bf16[2,576,128]{2,1,0:T(8,128)(2,1)}, u32[]{:S(2)}, u32[]{:S(2)}) collective-permute-start(bf16[2,576,128]{2,1,0:T(8,128)(2,1)S(1)} %get-tuple-element.13.refs_6_), channel_id=1, source_target_pairs={{0,4},{2,6},{4,8},{6,10},{8,12},{10,14},{12,0},{14,2},{1,5},{3,7},... | collective-permute-start | bytes 884744 | tf_op jit(solution)/shard_map/ppermute | solution.py:231
  15.6 11.7 %collective-permute-start.5 = (bf16[2,576,128]{2,1,0:T(8,128)(2,1)}, bf16[2,576,128]{2,1,0:T(8,128)(2,1)}, u32[]{:S(2)}, u32[]{:S(2)}) collective-permute-start(bf16[2,576,128]{2,1,0:T(8,128)(2,1)} %collective-permute-done.3.refs_7_), channel_id=1, source_target_pairs={{0,12},{2,14},{4,0},{6,2},{8,4},{10,6},{12,8},{14,10},{1,13},{3,15... | collective-permute-start | bytes 884744 | tf_op jit(solution)/shard_map/ppermute | solution.py:231
  19.4 28.4 %collective-permute-start.4 = (bf16[2,576,128]{2,1,0:T(8,128)(2,1)S(1)}, bf16[2,576,128]{2,1,0:T(8,128)(2,1)}, u32[]{:S(2)}, u32[]{:S(2)}) collective-permute-start(bf16[2,576,128]{2,1,0:T(8,128)(2,1)S(1)} %get-tuple-element.13.refs_6_), channel_id=1, source_target_pairs={{0,12},{2,14},{4,0},{6,2},{8,4},{10,6},{12,8},{14,10},{1,13},{3,15... | collective-permute-start | bytes 884744 | tf_op jit(solution)/shard_map/ppermute | solution.py:231
  19.9 22.7 %copy-start.11 = (s32[3,1]{1,0:T(4,128)}, s32[3,1]{1,0:T(4,128)S(1)}, u32[]{:S(2)}) copy-start(s32[3,1]{1,0:T(4,128)S(1)} %copy.13.refs_2_) | copy-start | bytes 40
  19.9 19.1 %collective-permute-start = (s32[3,1]{1,0:T(4,128)S(1)}, s32[3,1]{1,0:T(4,128)S(1)}, u32[]{:S(2)}, u32[]{:S(2)}) collective-permute-start(s32[3,1]{1,0:T(4,128)S(1)} %copy.13.refs_2_), channel_id=1, source_target_pairs={{0,2},{2,0},{4,6},{6,4},{8,10},{10,8},{12,14},{14,12},{16,18},{18,... | collective-permute-start | bytes 44 | tf_op jit(solution)/shard_map/ppermute | solution.py:242
  21.5 26.3 %collective-permute-start.9 = (bf16[2,576,128]{2,1,0:T(8,128)(2,1)}, bf16[2,576,128]{2,1,0:T(8,128)(2,1)}, u32[]{:S(2)}, u32[]{:S(2)}) collective-permute-start(bf16[2,576,128]{2,1,0:T(8,128)(2,1)} %collective-permute-done.3.refs_7_), channel_id=1, source_target_pairs={{0,4},{2,6},{4,8},{6,10},{8,12},{10,14},{12,0},{14,2},{1,5},{3,7},... | collective-permute-start | bytes 884744 | tf_op jit(solution)/shard_map/ppermute | solution.py:231
  23.0 24.7 %collective-permute-start.7 = (bf16[2,576,128]{2,1,0:T(8,128)(2,1)}, bf16[2,576,128]{2,1,0:T(8,128)(2,1)}, u32[]{:S(2)}, u32[]{:S(2)}) collective-permute-start(bf16[2,576,128]{2,1,0:T(8,128)(2,1)} %collective-permute-done.6.refs_12_), channel_id=1, source_target_pairs={{0,4},{2,6},{4,8},{6,10},{8,12},{10,14},{12,0},{14,2},{1,5},{3,7},... | collective-permute-start | bytes 884744 | tf_op jit(solution)/shard_map/ppermute | solution.py:231
  27.3 23.2 %collective-permute-start.8 = (bf16[2,576,128]{2,1,0:T(8,128)(2,1)}, bf16[2,576,128]{2,1,0:T(8,128)(2,1)}, u32[]{:S(2)}, u32[]{:S(2)}) collective-permute-start(bf16[2,576,128]{2,1,0:T(8,128)(2,1)} %collective-permute-done.5.refs_9_), channel_id=1, source_target_pairs={{0,12},{2,14},{4,0},{6,2},{8,4},{10,6},{12,8},{14,10},{1,13},{3,15... | collective-permute-start | bytes 884744 | tf_op jit(solution)/shard_map/ppermute | solution.py:231
  31.6 3.4 %copy-start = (bf16[4096,1024]{1,0:T(8,128)(2,1)S(1)}, bf16[4096,1024]{1,0:T(8,128)(2,1)}, u32[]{:S(2)}) copy-start(bf16[4096,1024]{1,0:T(8,128)(2,1)} %key_ref.3) | copy-start | bytes 25165828
  39.0 11.5 %copy-start.12 = (s32[3,1]{1,0:T(4,128)}, s32[3,1]{1,0:T(4,128)S(1)}, u32[]{:S(2)}) copy-start(s32[3,1]{1,0:T(4,128)S(1)} %collective-permute-done.refs_3_) | copy-start | bytes 40
  39.0 3.6 %collective-permute-start.1 = (s32[3,1]{1,0:T(4,128)S(1)}, s32[3,1]{1,0:T(4,128)S(1)}, u32[]{:S(2)}, u32[]{:S(2)}) collective-permute-start(s32[3,1]{1,0:T(4,128)S(1)} %copy.13.refs_2_), channel_id=1, source_target_pairs={{0,16},{2,18},{4,20},{6,22},{8,24},{10,26},{12,28},{14,30},{16,0},... | collective-permute-start | bytes 44 | tf_op jit(solution)/shard_map/ppermute | solution.py:242
  42.7 7.8 %copy-start.13 = (s32[3,1]{1,0:T(4,128)}, s32[3,1]{1,0:T(4,128)S(1)}, u32[]{:S(2)}) copy-start(s32[3,1]{1,0:T(4,128)S(1)} %collective-permute-done.1.refs_4_) | copy-start | bytes 40
  42.7 4.5 %collective-permute-start.2 = (s32[3,1]{1,0:T(4,128)S(1)}, s32[3,1]{1,0:T(4,128)S(1)}, u32[]{:S(2)}, u32[]{:S(2)}) collective-permute-start(s32[3,1]{1,0:T(4,128)S(1)} %copy.13.refs_2_), channel_id=1, source_target_pairs={{0,18},{2,16},{4,22},{6,20},{8,26},{10,24},{12,30},{14,28},{16,2},... | collective-permute-start | bytes 44 | tf_op jit(solution)/shard_map/ppermute | solution.py:242
  47.2 3.3 %copy-start.14 = (s32[3,1]{1,0:T(4,128)}, s32[3,1]{1,0:T(4,128)S(1)}, u32[]{:S(2)}) copy-start(s32[3,1]{1,0:T(4,128)S(1)} %collective-permute-done.2.refs_5_) | copy-start | bytes 40
  47.2 94.5 %collective-permute-start.14 = (f32[384,512]{1,0:T(8,128)}, f32[384,512]{1,0:T(8,128)}, u32[]{:S(2)}, u32[]{:S(2)}) collective-permute-start(f32[384,512]{1,0:T(8,128)} %base.3), channel_id=1, source_target_pairs={{0,1},{1,0},{2,3},{3,2},{4,5},{5,4},{6,7},{7,6},{8,9},{9,8},{10,11... | collective-permute-start | bytes 2359304 | tf_op jit(solution)/shard_map/ppermute | solution.py:245
  106.2 12.6 %collective-permute-start.10 = (bf16[3,576,128]{2,1,0:T(8,128)(2,1)}, bf16[3,576,128]{2,1,0:T(8,128)(2,1)}, u32[]{:S(2)}, u32[]{:S(2)}) collective-permute-start(bf16[3,576,128]{2,1,0:T(8,128)(2,1)} %get-tuple-element.16), channel_id=1, source_target_pairs={{0,2},{2,0},{4,6},{6,4},{8,10},{10,8},{12,14},{14,12},{16,18},{18,... | collective-permute-start | bytes 1327112 | tf_op jit(solution)/shard_map/ppermute | solution.py:242
  107.7 13.4 %collective-permute-start.11 = (bf16[3,576,128]{2,1,0:T(8,128)(2,1)}, bf16[3,576,128]{2,1,0:T(8,128)(2,1)}, u32[]{:S(2)}, u32[]{:S(2)}) collective-permute-start(bf16[3,576,128]{2,1,0:T(8,128)(2,1)} %get-tuple-element.17), channel_id=1, source_target_pairs={{0,16},{2,18},{4,20},{6,22},{8,24},{10,26},{12,28},{14,30},{16,0},... | collective-permute-start | bytes 1327112 | tf_op jit(solution)/shard_map/ppermute | solution.py:242
  109.2 19.6 %collective-permute-start.12 = (bf16[3,576,128]{2,1,0:T(8,128)(2,1)}, bf16[3,576,128]{2,1,0:T(8,128)(2,1)}, u32[]{:S(2)}, u32[]{:S(2)}) collective-permute-start(bf16[3,576,128]{2,1,0:T(8,128)(2,1)} %get-tuple-element.18), channel_id=1, source_target_pairs={{0,18},{2,16},{4,22},{6,20},{8,26},{10,24},{12,30},{14,28},{16,2},... | collective-permute-start | bytes 1327112 | tf_op jit(solution)/shard_map/ppermute | solution.py:242
  128.8 1.0 copy-start.5
  133.5 0.7 copy-start.8
  134.2 6.6 %copy-start.7 = (f32[384,64]{1,0:T(8,128)}, f32[384,64]{1,0:T(8,128)S(1)}, u32[]{:S(2)}) copy-start(f32[384,64]{1,0:T(8,128)S(1)} %get-tuple-element.19.mine) | copy-start | bytes 294916
  134.2 7.5 %collective-permute-start.13 = (f32[384,64]{1,0:T(8,128)S(1)}, f32[384,64]{1,0:T(8,128)S(1)}, u32[]{:S(2)}, u32[]{:S(2)}) collective-permute-start(f32[384,64]{1,0:T(8,128)S(1)} %get-tuple-element.19.mine), channel_id=1, source_target_pairs={{0,1},{1,0},{2,3},{3,2},{4,5},{5,4},{6,7},{7,6},{8,9},{9,8},{10,11... | collective-permute-start | bytes 294920 | tf_op jit(solution)/shard_map/ppermute | solution.py:245
  134.2 3.5 %copy-start.1 = (bf16[4096,1024]{1,0:T(8,128)(2,1)S(1)}, bf16[4096,1024]{1,0:T(8,128)(2,1)}, u32[]{:S(2)}) copy-start(bf16[4096,1024]{1,0:T(8,128)(2,1)} %key_ref.3) | copy-start | bytes 25165828
  140.7 0.9 copy-start.4
  141.6 0.7 copy-start.9

commit v2 on v0

v2 whole, which is shorter than its diff:
```python
import functools

import jax
import jax.numpy as jnp
from jax import lax
from jax.experimental import pallas as pl
from jax.experimental.pallas import tpu as pltpu
from jax.sharding import Mesh
from jax.sharding import PartitionSpec as P

LANES = 128
ANY = pl.BlockSpec(memory_space=pl.ANY)
SMEM = pl.BlockSpec(memory_space=pltpu.SMEM)
VMEM = pl.BlockSpec(memory_space=pltpu.VMEM)
BIG = pltpu.CompilerParams(vmem_limit_bytes=32 * 1024 * 1024)
PLANE = ("groups", "pair")
WHOLE = ("groups", "ring", "pair")


def pack_kernel(where, *refs):
    ways = (len(refs)) // 3
    for way in range(ways):
        down_ref, up_ref, out_ref = refs[way], refs[ways + way], refs[2 * ways + way]
        feats = down_ref.shape[2]
        out_ref[:, :, :feats] = down_ref[...]
        out_ref[:, :, feats:] = up_ref[...]


def pack(down, up, shares, share_of):
    adapters, rank, feats = down.shape
    step = feats // shares
    tiles = up.shape[2] // LANES
    ways = len(share_of)

    def down_at(way):
        return lambda i, s: (0, 0, s[way])

    def up_at(way):
        return lambda i, s: (0, 0, s[way] % tiles)

    shape = (adapters, rank, step + LANES)
    return pl.pallas_call(
        pack_kernel,
        grid_spec=pltpu.PrefetchScalarGridSpec(
            num_scalar_prefetch=1,
            grid=(1,),
            in_specs=[pl.BlockSpec((adapters, rank, step), down_at(w)) for w in range(ways)]
            + [pl.BlockSpec((adapters, rank, LANES), up_at(w)) for w in range(ways)],
            out_specs=[pl.BlockSpec(shape, lambda i, s: (0, 0, 0)) for _ in range(ways)],
        ),
        out_shape=[jax.ShapeDtypeStruct(shape, down.dtype) for _ in range(ways)],
        compiler_params=BIG,
        name="pack",
    )(jnp.stack(share_of).astype(jnp.int32), *([down] * ways), *([up] * ways))


def spread_kernel(in_ref, out_ref):
    out_ref[0] = in_ref[...]


def spread(tokens, shares):
    rows, feats = tokens.shape
    step = feats // shares
    return pl.pallas_call(
        spread_kernel,
        grid=(shares,),
        in_specs=[pl.BlockSpec((rows, step), lambda i: (0, i))],
        out_specs=pl.BlockSpec((1, rows, step), lambda i: (i, 0, 0)),
        out_shape=jax.ShapeDtypeStruct((shares, rows, step), tokens.dtype),
        compiler_params=BIG,
        name="spread",
    )(tokens)


def base_kernel(side, tok_ref, key_ref, after, out_ref):
    part = jnp.dot(tok_ref[...], key_ref[...], preferred_element_type=jnp.float32)

    @pl.when(pl.program_id(0) == 0)
    def _():
        out_ref[...] = part

    @pl.when(pl.program_id(0) > 0)
    def _():
        out_ref[...] += part


def base_half(tokens, base_key, side, sides, after):
    rows, depth = tokens.shape
    wide = base_key.shape[1] // sides
    step = 1024
    return pl.pallas_call(
        base_kernel,
        grid_spec=pltpu.PrefetchScalarGridSpec(
            num_scalar_prefetch=1,
            grid=(depth // step,),
            in_specs=[
                pl.BlockSpec((rows, step), lambda i, s: (0, i)),
                pl.BlockSpec((step, wide), lambda i, s: (i, s[0])),
                ANY,
            ],
            out_specs=pl.BlockSpec((rows, wide), lambda i, s: (0, 0)),
        ),
        out_shape=jax.ShapeDtypeStruct((rows, wide), jnp.float32),
        compiler_params=BIG,
        cost_estimate=pl.CostEstimate(
            flops=2 * rows * depth * wide, bytes_accessed=2 * depth * (rows + wide) + 4 * rows * wide, transcendentals=0
        ),
        name="base",
    )(side.reshape(1), tokens, base_key, after)


def rank_kernel(place, pair, ids, owner, here, tok_ref, *refs):
    pieces = refs[:-4]
    after, out_ref, held, sems = refs[-4:]
    per, rank = pieces[0].shape[:2]
    blocks = out_ref.shape[1]
    feats = tok_ref.shape[2]
    block = tok_ref.shape[1] // blocks
    mate = pl.program_id(0)

    @pl.when(mate == 0)
    def _():
        copies = [
            pltpu.make_async_copy(piece, held.at[pl.ds(j * per, per)], sems.at[j]) for j, piece in enumerate(pieces)
        ]
        for copy in copies:
            copy.start()
        for copy in copies:
            copy.wait()

    for b in range(blocks):
        slot = owner[ids[mate * blocks + b]]
        chip = slot // per
        at = place(chip // pair, chip % pair, here[0], here[1]) * per + slot % per
        tok = tok_ref[0, b * block : (b + 1) * block, :]
        part = lax.dot_general(
            tok, held[at, :, :feats], (((1,), (1,)), ((), ())), preferred_element_type=jnp.float32
        )
        half = block // 2
        part = jnp.concatenate([part[:half], part[half:]], axis=1)
        out_ref[0, b, :half, :] = part.astype(out_ref.dtype)
        out_ref[0, b, half:, :] = held[at, :, feats:]


def rank_parts(ids, owner, here, tok, pieces, place, pair, blocks, after):
    shares, rows, feats = tok.shape
    per, rank, wide = pieces[0].shape
    tall = rows // blocks // 2 + rank
    return pl.pallas_call(
        functools.partial(rank_kernel, place, pair),
        grid=(shares,),
        in_specs=[SMEM, SMEM, SMEM, pl.BlockSpec((1, rows, feats), lambda i: (i, 0, 0))] + [ANY] * (len(pieces) + 1),
        out_specs=pl.BlockSpec((1, blocks, tall, LANES), lambda i: (i, 0, 0, 0)),
        out_shape=jax.ShapeDtypeStruct((shares, blocks, tall, LANES), tok.dtype),
        scratch_shapes=[
            pltpu.VMEM((len(pieces) * per, rank, wide), tok.dtype),
            pltpu.SemaphoreType.DMA((len(pieces),)),
        ],
        compiler_params=BIG,
        cost_estimate=pl.CostEstimate(
            flops=2 * shares * rows * feats * rank, bytes_accessed=2 * tok.size, transcendentals=0
        ),
        name="rank",
    )(ids, owner, here, tok, *pieces, after)


def sum_kernel(in_ref, out_ref):
    shares, blocks = in_ref.shape[:2]
    block, rank = out_ref.shape[0] // blocks, out_ref.shape[1]
    half = block // 2
    for b in range(blocks):
        total = in_ref[0, b, :half, :].astype(jnp.float32)
        for s in range(1, shares):
            total += in_ref[s, b, :half, :].astype(jnp.float32)
        out_ref[b * block : b * block + half, :] = total[:, :rank]
        out_ref[b * block + half : (b + 1) * block, :] = total[:, rank:]


def rank_sums(parts, rows, rank):
    return pl.pallas_call(
        sum_kernel,
        in_specs=[VMEM],
        out_specs=VMEM,
        out_shape=jax.ShapeDtypeStruct((rows, rank), jnp.float32),
        name="sums",
    )(parts)


def final_kernel(lengths, mine, theirs, parts, base, out_ref):
    shares, blocks = parts.shape[:2]
    block = out_ref.shape[0] // blocks
    rank = mine.shape[1]
    wide = out_ref.shape[1]
    shrunk = (mine[...] + theirs[...]).astype(jnp.bfloat16)
    rows = lax.broadcasted_iota(jnp.int32, (block, wide), 0)
    for b in range(blocks):
        here = slice(b * block, (b + 1) * block)
        up = jnp.concatenate([parts[s, b, block // 2 :, :] for s in range(wide // LANES)], axis=1)
        delta = jnp.dot(shrunk[here], up, preferred_element_type=jnp.float32)
        out_ref[here, :] = jnp.where(rows < lengths[b], base[here, :] + delta, 0.0).astype(out_ref.dtype)


def final(lengths, mine, theirs, parts, base, dtype):
    return pl.pallas_call(
        final_kernel,
        in_specs=[SMEM, VMEM, VMEM, VMEM, VMEM],
        out_specs=VMEM,
        out_shape=jax.ShapeDtypeStruct(base.shape, dtype),
        compiler_params=BIG,
        name="final",
    )(lengths, mine, theirs, parts, base)


def line_of_four(x):
    two = lax.ppermute(x, "ring", [(0, 2), (1, 3), (2, 0), (3, 1)])
    up = lax.ppermute(x, "ring", [(0, 1), (1, 2), (2, 3)])
    down = lax.ppermute(x, "ring", [(1, 0), (2, 1), (3, 2)])
    three = lax.ppermute(two, "ring", [(1, 0), (2, 3)])
    return [x, up, down, two, three]


def place_in_four(z_from, z):
    away = jnp.abs(z_from - z)
    near = jnp.where(z_from < z, 1, 2)
    return jnp.where(away == 0, 0, jnp.where(away == 1, near, jnp.where(away == 2, 3, 4)))


def any_ring(x, ring):
    held = {0: x}
    for k in range(1, ring // 2 + 1):
        held[ring - k] = lax.ppermute(held[(ring - k + 1) % ring], "ring", [(a, (a + 1) % ring) for a in range(ring)])
        if 2 * k < ring:
            held[k] = lax.ppermute(held[k - 1], "ring", [(a, (a - 1) % ring) for a in range(ring)])
    return [held[k] for k in range(ring)]


def body(tokens, base_key, adapter_down, adapter_up, adapter_ids, owner_slot, lengths):
    groups, ring, pair = lax.axis_size("groups"), lax.axis_size("ring"), lax.axis_size("pair")
    sides = lax.axis_size("tensor")
    shares = groups * pair
    g, z, y, t = (lax.axis_index(name) for name in ("groups", "ring", "pair", "tensor"))
    rows = tokens.shape[0]
    blocks = lengths.shape[0]
    rank = adapter_up.shape[1]

    def across(x):
        return lax.ppermute(x, "tensor", [(i, (i + 1) % sides) for i in range(sides)])

    def to_plane(x):
        return lax.all_to_all(x, PLANE, split_axis=0, concat_axis=0, tiled=True)

    gather = line_of_four if ring == 4 else functools.partial(any_ring, ring=ring)
    each = 5 if ring == 4 else ring

    def place(z_from, y_from, z_here, y_here):
        at = place_in_four(z_from, z_here) if ring == 4 else lax.rem(z_from - z_here + ring, ring)
        return lax.rem(y_from - y_here + pair, pair) * each + at

    packed = pack(jnp.swapaxes(adapter_down, 1, 2), adapter_up, shares, [g * pair + (y + w) % pair for w in range(pair)])
    swapped = [
        lax.ppermute(packed[w], "pair", [(a, (a + w) % pair) for a in range(pair)]) for w in range(1, pair)
    ]
    pieces = gather(packed[0])
    for w in range(1, pair):
        pieces = pieces + gather(swapped[pair - 1 - w])

    tok = to_plane(spread(tokens, shares))
    ids = to_plane(jnp.broadcast_to(adapter_ids[:, 0], (shares, blocks))).reshape(-1)

    base_out = base_half(tokens, base_key, (t + 1) % sides, sides, pieces[-4])
    base_in = across(base_out)
    base_mine = base_half(tokens, base_key, t, sides, base_out)
    base = base_mine + base_in

    here = jnp.stack([z, y]).astype(jnp.int32)
    parts = to_plane(rank_parts(ids, owner_slot, here, tok, pieces, place, pair, blocks, base))
    mine = rank_sums(parts, rows, rank)
    return final(lengths, mine, across(mine), parts, base, tokens.dtype)


def solution(mesh):
    groups, dp, sides = (mesh.shape[name] for name in ("groups", "dp", "tensor"))
    pair = 2 if dp % 2 == 0 else 1
    cut = Mesh(mesh.devices.reshape(groups, dp // pair, pair, sides), ("groups", "ring", "pair", "tensor"))
    stored = ("ring", "pair")
    placed = (
        P(WHOLE, "tensor"),
        P("tensor", None),
        P(stored, "tensor", None),
        P(stored, None, "tensor"),
        P(WHOLE, None),
        P(),
        P(WHOLE),
    )
    return jax.shard_map(body, mesh=cut, in_specs=placed, out_specs=P(WHOLE, "tensor"), check_vma=False)
```

time: 225 us -> 150 us (0.67)
  blocking collectives: 85.1 us -> 10.8 us
  Pallas kernels: 0 us -> 16.9 us
  starting transfers between devices: 12 us -> 28.5 us
  matrix products: 14.1 us -> 0 us
  between operations: 13.9 us -> 0.21 us
  waiting for transfers between devices: 78.7 us -> 70.7 us
    unnamed x1 -> x0, blocking collectives: 80.8 us -> none
    ppermute x0 -> x11, waiting for transfers between devices: none -> 70.3 us  [the longest x1 37.5 us: body(): lax.ppermute(packed[w], 'pair', [(a, (a + w) % pair) for a in range(pair)])]
    reduce_scatter x2 -> x0, waiting for transfers between devices: 56.1 us -> none  [the longest x1 50.1 us: body(): lax.psum_scatter(partial_value, 'dp', scatter_dimension=0, tiled=True)]
    all_to_all x2, waiting for transfers between devices: 21.9 us -> 0.49 us  [to_plane(): return lax.all_to_all(x, PLANE, split_axis=0, concat_axis=0, tiled=True)]
    ppermute x0 -> x11, starting transfers between devices: none -> 18.6 us  [the longest x2 7.99 us: line_of_four(): up = lax.ppermute(x, 'ring', [(0, 1), (1, 2), (2, 3)])]
    pallas_call x0 -> x7, Pallas kernels: none -> 16.9 us  [the longest x2 6.2 us: base_half(): pl.pallas_call(base_kernel, grid_spec=pltpu.PrefetchScalarGridSpec(num_sc...]
    dot_general x3 -> x0, matrix products: 14.1 us -> none  [the longest x1 8.91 us: body(): partial_base = jnp.dot(tokens, base_key, preferred_element_type=jnp.float32)]
    all_to_all x0 -> x1, blocking collectives: none -> 10.8 us  [to_plane(): return lax.all_to_all(x, PLANE, split_axis=0, concat_axis=0, tiled=True)]
  transfers between devices with their start and end apart: 5 -> 13, of which waited for: 3 -> 7; matrix products, arithmetic and copies ran while one was open for 11% -> 2% of each run, Pallas kernels for 0% -> 5%
where the time goes in v2:
time: 150 us; the launch traced here: 149 us
  waiting for transfers between devices  70.7 us (47%)
  starting transfers between devices  28.5 us (19%)
  local copies, waits for them, and re-layouts  20.5 us (14%)
  Pallas kernels  16.9 us (11%)
  blocking collectives  10.8 us (7%)
  other arithmetic  1.83 us (1%)
    ppermute x1, waiting for transfers between devices, body(): lax.ppermute(packed[w], 'pair', [(a, (a + w) % pair) for a in range(pair)])  37.5 us
    ppermute x2, waiting for transfers between devices, line_of_four(): two = lax.ppermute(x, 'ring', [(0, 2), (1, 3), (2, 0), (3, 1)])  20 us
    unnamed x34, local copies, waits for them, and re-layouts  18.6 us
    all_to_all x1, blocking collectives, to_plane(): return lax.all_to_all(x, PLANE, split_axis=0, concat_axis=0, tiled=True)  10.8 us
    all_to_all x2, starting transfers between devices, to_plane(): return lax.all_to_all(x, PLANE, split_axis=0, concat_axis=0, tiled=True)  9.96 us
    ppermute x2, starting transfers between devices, line_of_four(): up = lax.ppermute(x, 'ring', [(0, 1), (1, 2), (2, 3)])  7.99 us
    pallas_call x2, Pallas kernels, base_half(): pl.pallas_call(base_kernel, grid_spec=pltpu.PrefetchScalarGridSpec(num_sc...  6.2 us
    ppermute x2, waiting for transfers between devices, line_of_four(): up = lax.ppermute(x, 'ring', [(0, 1), (1, 2), (2, 3)])  5.8 us
  transfers between devices with their start and end apart: 13, of which 7 were waited for; matrix products, arithmetic and copies ran while one was open for 2% of the time, Pallas kernels for 5%

profile of v2, /device:TPU:0, one launch (start us, length us, event | category | flops | bytes accessed | tf_op | source)
XLA Modules:
  0.0 149.5 jit_solution(14811232383522688505)
XLA Ops:
  0.0 1.2 broadcast_in_dim.6
  1.2 5.2 %all-to-all-start = ((s32[4,1,3]{2,1,0:T(1,128)}), s32[4,1,3]{2,1,0:T(1,128)S(1)}, u32[]{:S(2)}, u32[]{:S(2)}) async-start(s32[4,1,3]{2,1,0:T(1,128)} %broadcast_in_dim.6), calls=%async_computation | async-start | bytes 4096 | tf_op jit(solution)/shard_map/all_to_all | solution.py:250
  6.4 1.9 %copy-done.2 = bf16[384,4096]{1,0:T(8,128)(2,1)S(1)} copy-done((bf16[384,4096]{1,0:T(8,128)(2,1)S(1)}, bf16[384,4096]{1,0:T(8,128)(2,1)}, u32[]{:S(2)}) %copy-start.2) | copy-done | bytes 3145752
  8.3 0.5 spread.1
  8.8 1.7 %copy-done.4 = bf16[4,384,1024]{2,1,0:T(8,128)(2,1)} copy-done((bf16[4,384,1024]{2,1,0:T(8,128)(2,1)}, bf16[4,384,1024]{2,1,0:T(8,128)(2,1)S(1)}, u32[]{:S(2)}) %copy-start.4) | copy-done | bytes 3145752
  10.5 0.5 all-to-all-done
  11.0 4.8 %all-to-all-start.1 = ((bf16[4,384,1024]{2,1,0:T(8,128)(2,1)}), bf16[4,384,1024]{2,1,0:T(8,128)(2,1)}, u32[]{:S(2)}, u32[]{:S(2)}) async-start(bf16[4,384,1024]{2,1,0:T(8,128)(2,1)} %copy-done.4), calls=%async_computation.1 | async-start | bytes 6291456 | tf_op jit(solution)/shard_map/all_to_all | solution.py:250
  15.8 0.1 pad_add_fusion.1.where
  15.9 1.2 copy-done.7
  17.1 1.3 pack.1
  18.4 2.0 %collective-permute-start.4 = (bf16[2,64,1152]{2,1,0:T(8,128)(2,1)S(1)}, bf16[2,64,1152]{2,1,0:T(8,128)(2,1)}, u32[]{:S(2)}, u32[]{:S(2)}) collective-permute-start(bf16[2,64,1152]{2,1,0:T(8,128)(2,1)S(1)} %get-tuple-element.8), channel_id=1, source_target_pairs={{0,2},{2,0},{1,3},{3,1},{4,6},{6,4},{5,7},{7,5},{8,10},{10,8},{9,1... | collective-permute-start | bytes 884744 | tf_op jit(solution)/shard_map/ppermute | solution.py:261
  20.4 37.5 %collective-permute-done.4.refs_5_ = bf16[2,64,1152]{2,1,0:T(8,128)(2,1)} collective-permute-done((bf16[2,64,1152]{2,1,0:T(8,128)(2,1)S(1)}, bf16[2,64,1152]{2,1,0:T(8,128)(2,1)}, u32[]{:S(2)}, u32[]{:S(2)}) %collective-permute-start.4) | collective-permute-done | bytes 294944 | tf_op jit(solution)/shard_map/ppermute | solution.py:261
  57.9 3.5 %collective-permute-start.5 = (bf16[2,64,1152]{2,1,0:T(8,128)(2,1)}, bf16[2,64,1152]{2,1,0:T(8,128)(2,1)S(1)}, u32[]{:S(2)}, u32[]{:S(2)}) collective-permute-start(bf16[2,64,1152]{2,1,0:T(8,128)(2,1)} %collective-permute-done.4.refs_5_), channel_id=1, source_target_pairs={{0,4},{4,8},{8,12},{1,5},{5,9},{9,13},{2,6},{6,10},{10,14},{3,7},{... | collective-permute-start | bytes 884744 | tf_op jit(solution)/shard_map/ppermute | solution.py:216
  61.4 5.8 %collective-permute-done.5.after.refs_6_ = bf16[2,64,1152]{2,1,0:T(8,128)(2,1)S(1)} collective-permute-done((bf16[2,64,1152]{2,1,0:T(8,128)(2,1)}, bf16[2,64,1152]{2,1,0:T(8,128)(2,1)S(1)}, u32[]{:S(2)}, u32[]{:S(2)}) %collective-permute-start.5) | collective-permute-done | bytes 294944 | tf_op jit(solution)/shard_map/ppermute | solution.py:216
  67.2 3.4 %copy-done = bf16[4096,1024]{1,0:T(8,128)(2,1)S(1)} copy-done((bf16[4096,1024]{1,0:T(8,128)(2,1)S(1)}, bf16[4096,1024]{1,0:T(8,128)(2,1)}, u32[]{:S(2)}) %copy-start) | copy-done | bytes 8388632
  70.6 3.1 %base.2.after = f32[384,512]{1,0:T(8,128)S(1)} custom-call(s32[1]{0:T(128)} %bitcast.7.side, bf16[384,4096]{1,0:T(8,128)(2,1)S(1)} %copy-done.3, bf16[4096,1024]{1,0:T(8,128)(2,1)S(1)} %copy-done, bf16[2,64,1152]{2,1,0:T(8,128)(2,1)S(1)} %collective-permute-done.5.after.refs_6_), custom_call_target="tpu_custom_call" | custom-call | flops 1610612736 | bytes 8126464 | tf_op jit(solution)/shard_map/base/pallas_call | solution.py:91
  73.7 0.1 collective-permute-start.9
  73.8 0.9 copy-done.9
  74.7 3.4 %collective-permute-start.2 = (bf16[2,64,1152]{2,1,0:T(8,128)(2,1)}, bf16[2,64,1152]{2,1,0:T(8,128)(2,1)}, u32[]{:S(2)}, u32[]{:S(2)}) collective-permute-start(bf16[2,64,1152]{2,1,0:T(8,128)(2,1)} %get-tuple-element.7.refs_0_), channel_id=1, source_target_pairs={{0,8},{4,12},{8,0},{12,4},{1,9},{5,13},{9,1},{13,5},{2,10},{6,14},... | collective-permute-start | bytes 884744 | tf_op jit(solution)/shard_map/ppermute | solution.py:215
  78.1 0.0 collective-permute-start.7
  78.1 4.5 %collective-permute-start = (bf16[2,64,1152]{2,1,0:T(8,128)(2,1)}, bf16[2,64,1152]{2,1,0:T(8,128)(2,1)}, u32[]{:S(2)}, u32[]{:S(2)}) collective-permute-start(bf16[2,64,1152]{2,1,0:T(8,128)(2,1)} %get-tuple-element.7.refs_0_), channel_id=1, source_target_pairs={{0,4},{4,8},{8,12},{1,5},{5,9},{9,13},{2,6},{6,10},{10,14},{3,7},{... | collective-permute-start | bytes 884744 | tf_op jit(solution)/shard_map/ppermute | solution.py:216
  82.6 1.3 collective-permute-start.1
  83.9 15.0 %collective-permute-done.2.refs_3_ = bf16[2,64,1152]{2,1,0:T(8,128)(2,1)} collective-permute-done((bf16[2,64,1152]{2,1,0:T(8,128)(2,1)}, bf16[2,64,1152]{2,1,0:T(8,128)(2,1)}, u32[]{:S(2)}, u32[]{:S(2)}) %collective-permute-start.2) | collective-permute-done | bytes 294944 | tf_op jit(solution)/shard_map/ppermute | solution.py:215
  98.9 1.3 collective-permute-start.6
  100.2 5.0 %collective-permute-done.7.refs_8_ = bf16[2,64,1152]{2,1,0:T(8,128)(2,1)} collective-permute-done((bf16[2,64,1152]{2,1,0:T(8,128)(2,1)}, bf16[2,64,1152]{2,1,0:T(8,128)(2,1)}, u32[]{:S(2)}, u32[]{:S(2)}) %collective-permute-start.7) | collective-permute-done | bytes 294944 | tf_op jit(solution)/shard_map/ppermute | solution.py:215
  105.2 1.3 collective-permute-start.3
  106.5 0.0 collective-permute-done.9
  106.5 0.9 copy-done.15
  107.4 1.3 collective-permute-start.8
  108.7 0.1 pad_add_fusion.here
  108.8 0.5 broadcast.9
  109.3 0.6 reduce.3
  110.0 0.1 reshape.17.ids
  110.0 3.4 %copy-done.1 = bf16[4096,1024]{1,0:T(8,128)(2,1)S(1)} copy-done((bf16[4096,1024]{1,0:T(8,128)(2,1)S(1)}, bf16[4096,1024]{1,0:T(8,128)(2,1)}, u32[]{:S(2)}) %copy-start.1) | copy-done | bytes 8388632
  113.4 1.1 copy-done.10
  114.6 3.1 %base.3 = f32[384,512]{1,0:T(8,128)S(1)} custom-call(s32[1]{0:T(128)} %bitcast.6.side, bf16[384,4096]{1,0:T(8,128)(2,1)S(1)} %copy-done.3, bf16[4096,1024]{1,0:T(8,128)(2,1)S(1)} %copy-done.1, f32[384,512]{1,0:T(8,128)S(1)} %copy-done.10), custom_call_target="tpu_custom_call" | custom-call | flops 1610612736 | bytes 8126464 | tf_op jit(solution)/shard_map/base/pallas_call | solution.py:91
  117.7 0.0 copy-start.14
  117.7 1.0 add.32.refs_10_.base
  118.7 5.2 %collective-permute-done.8.refs_9_ = bf16[2,64,1152]{2,1,0:T(8,128)(2,1)} collective-permute-done((bf16[2,64,1152]{2,1,0:T(8,128)(2,1)}, bf16[2,64,1152]{2,1,0:T(8,128)(2,1)}, u32[]{:S(2)}, u32[]{:S(2)}) %collective-permute-start.8) | collective-permute-done | bytes 294944 | tf_op jit(solution)/shard_map/ppermute | solution.py:218
  124.0 1.1 copy-done.5
  125.1 5.6 %rank.1 = bf16[4,3,128,128]{3,2,1,0:T(8,128)(2,1)S(1)} custom-call(s32[12]{0:T(128)S(1)} %reshape.17.ids, s32[16]{0:T(128)S(1)} %copy-done.13, s32[2]{0:T(128)S(1)} %pad_add_fusion.here, bf16[4,384,1024]{2,1,0:T(8,128)(2,1)} %all-to-all-done.1.tok_ref, bf16[2,64,1152]{2,1,0:T(8,128)(2,1)} %get-tuple-element.7.refs_0_, ...), custom_call_target="tpu_custom_call" | custom-call | flops 201326592 | bytes 3145728 | tf_op jit(solution)/shard_map/rank/pallas_call | solution.py:149
  130.7 10.8 %all_to_all.16.in_ref.parts = bf16[4,3,128,128]{3,2,1,0:T(8,128)(2,1)} all-to-all(bf16[4,3,128,128]{3,2,1,0:T(8,128)(2,1)S(1)} %rank.1), channel_id=1, replica_groups=mesh['groups'=2,'ring'=4,'pair'=2,'tensor'=2] {'groups','pair'}, dimensions={0} | all-to-all | bytes 786432 | tf_op jit(solution)/shard_map/all_to_all | solution.py:250
  141.4 1.8 %sums.1.mine = f32[384,64]{1,0:T(8,128)} custom-call(bf16[4,3,128,128]{3,2,1,0:T(8,128)(2,1)} %all_to_all.16.in_ref.parts), custom_call_target="tpu_custom_call" | custom-call | tf_op jit(solution)/shard_map/sums/pallas_call | solution.py:180
  143.2 1.6 %collective-permute-done.10.theirs = f32[384,64]{1,0:T(8,128)S(1)} collective-permute-done((f32[384,64]{1,0:T(8,128)}, f32[384,64]{1,0:T(8,128)S(1)}, u32[]{:S(2)}, u32[]{:S(2)}) %collective-permute-start.10) | collective-permute-done | bytes 98336 | tf_op jit(solution)/shard_map/ppermute | solution.py:247
  144.9 1.1 copy-done.6
  146.0 1.0 copy-done.8
  147.0 0.9 copy-done.11
  147.9 1.5 %final.1 = bf16[384,512]{1,0:T(8,128)(2,1)} custom-call(s32[3]{0:T(128)S(1)} %copy-done.14, f32[384,64]{1,0:T(8,128)S(1)} %copy-done.11, f32[384,64]{1,0:T(8,128)S(1)} %collective-permute-done.10.theirs, bf16[4,3,128,128]{3,2,1,0:T(8,128)(2,1)S(1)} %copy-done.8, f32[384,512]{1,0:T(8,128)S(1)} %copy-done.6), custom_call_target="tpu_custom_call" | custom-call | tf_op jit(solution)/shard_map/final/pallas_call | solution.py:204
  (27 shorter events, 0.1 us)
Async XLA Ops:
  1.2 9.7 %all-to-all-start = ((s32[4,1,3]{2,1,0:T(1,128)}), s32[4,1,3]{2,1,0:T(1,128)S(1)}, u32[]{:S(2)}, u32[]{:S(2)}) async-start(s32[4,1,3]{2,1,0:T(1,128)} %broadcast_in_dim.6), calls=%async_computation | async-start | bytes 4096 | tf_op jit(solution)/shard_map/all_to_all | solution.py:250
  6.4 1.9 %copy-start.2 = (bf16[384,4096]{1,0:T(8,128)(2,1)S(1)}, bf16[384,4096]{1,0:T(8,128)(2,1)}, u32[]{:S(2)}) copy-start(bf16[384,4096]{1,0:T(8,128)(2,1)} %tok_ref.3) | copy-start | bytes 9437188
  8.8 1.7 %copy-start.4 = (bf16[4,384,1024]{2,1,0:T(8,128)(2,1)}, bf16[4,384,1024]{2,1,0:T(8,128)(2,1)S(1)}, u32[]{:S(2)}) copy-start(bf16[4,384,1024]{2,1,0:T(8,128)(2,1)S(1)} %spread.1) | copy-start | bytes 9437188
  10.5 5.4 %copy-start.12 = (bf16[2,64,512]{2,1,0:T(8,128)(2,1)S(1)}, bf16[2,64,512]{2,1,0:T(8,128)(2,1)}, u32[]{:S(2)}) copy-start(bf16[2,64,512]{2,1,0:T(8,128)(2,1)} %refs_3_.1) | copy-start | bytes 393220
  10.5 56.7 %copy-start.3 = (bf16[384,4096]{1,0:T(8,128)(2,1)S(1)}, bf16[384,4096]{1,0:T(8,128)(2,1)}, u32[]{:S(2)}) copy-start(bf16[384,4096]{1,0:T(8,128)(2,1)} %tok_ref.3) | copy-start | bytes 9437188
  11.0 113.0 %all-to-all-start.1 = ((bf16[4,384,1024]{2,1,0:T(8,128)(2,1)}), bf16[4,384,1024]{2,1,0:T(8,128)(2,1)}, u32[]{:S(2)}, u32[]{:S(2)}) async-start(bf16[4,384,1024]{2,1,0:T(8,128)(2,1)} %copy-done.4), calls=%async_computation.1 | async-start | bytes 6291456 | tf_op jit(solution)/shard_map/all_to_all | solution.py:250
  15.9 1.2 copy-start.7
  18.4 39.5 %collective-permute-start.4 = (bf16[2,64,1152]{2,1,0:T(8,128)(2,1)S(1)}, bf16[2,64,1152]{2,1,0:T(8,128)(2,1)}, u32[]{:S(2)}, u32[]{:S(2)}) collective-permute-start(bf16[2,64,1152]{2,1,0:T(8,128)(2,1)S(1)} %get-tuple-element.8), channel_id=1, source_target_pairs={{0,2},{2,0},{1,3},{3,1},{4,6},{6,4},{5,7},{7,5},{8,10},{10,8},{9,1... | collective-permute-start | bytes 884744 | tf_op jit(solution)/shard_map/ppermute | solution.py:261
  57.9 9.3 %collective-permute-start.5 = (bf16[2,64,1152]{2,1,0:T(8,128)(2,1)}, bf16[2,64,1152]{2,1,0:T(8,128)(2,1)S(1)}, u32[]{:S(2)}, u32[]{:S(2)}) collective-permute-start(bf16[2,64,1152]{2,1,0:T(8,128)(2,1)} %collective-permute-done.4.refs_5_), channel_id=1, source_target_pairs={{0,4},{4,8},{8,12},{1,5},{5,9},{9,13},{2,6},{6,10},{10,14},{3,7},{... | collective-permute-start | bytes 884744 | tf_op jit(solution)/shard_map/ppermute | solution.py:216
  67.2 3.4 %copy-start = (bf16[4096,1024]{1,0:T(8,128)(2,1)S(1)}, bf16[4096,1024]{1,0:T(8,128)(2,1)}, u32[]{:S(2)}) copy-start(bf16[4096,1024]{1,0:T(8,128)(2,1)} %key_ref.3) | copy-start | bytes 25165828
  73.7 32.8 %collective-permute-start.9 = (f32[384,512]{1,0:T(8,128)S(1)}, f32[384,512]{1,0:T(8,128)S(1)}, u32[]{:S(2)}, u32[]{:S(2)}) collective-permute-start(f32[384,512]{1,0:T(8,128)S(1)} %base.2.after), channel_id=1, source_target_pairs={{0,1},{1,0},{2,3},{3,2},{4,5},{5,4},{6,7},{7,6},{8,9},{9,8},{10,11... | collective-permute-start | bytes 2359304 | tf_op jit(solution)/shard_map/ppermute | solution.py:247
  73.8 0.9 copy-start.9
  74.7 24.2 %collective-permute-start.2 = (bf16[2,64,1152]{2,1,0:T(8,128)(2,1)}, bf16[2,64,1152]{2,1,0:T(8,128)(2,1)}, u32[]{:S(2)}, u32[]{:S(2)}) collective-permute-start(bf16[2,64,1152]{2,1,0:T(8,128)(2,1)} %get-tuple-element.7.refs_0_), channel_id=1, source_target_pairs={{0,8},{4,12},{8,0},{12,4},{1,9},{5,13},{9,1},{13,5},{2,10},{6,14},... | collective-permute-start | bytes 884744 | tf_op jit(solution)/shard_map/ppermute | solution.py:215
  78.1 27.1 %collective-permute-start.7 = (bf16[2,64,1152]{2,1,0:T(8,128)(2,1)}, bf16[2,64,1152]{2,1,0:T(8,128)(2,1)}, u32[]{:S(2)}, u32[]{:S(2)}) collective-permute-start(bf16[2,64,1152]{2,1,0:T(8,128)(2,1)} %collective-permute-done.4.refs_5_), channel_id=1, source_target_pairs={{0,8},{4,12},{8,0},{12,4},{1,9},{5,13},{9,1},{13,5},{2,10},{6,14},... | collective-permute-start | bytes 884744 | tf_op jit(solution)/shard_map/ppermute | solution.py:215
  78.1 40.6 %collective-permute-start = (bf16[2,64,1152]{2,1,0:T(8,128)(2,1)}, bf16[2,64,1152]{2,1,0:T(8,128)(2,1)}, u32[]{:S(2)}, u32[]{:S(2)}) collective-permute-start(bf16[2,64,1152]{2,1,0:T(8,128)(2,1)} %get-tuple-element.7.refs_0_), channel_id=1, source_target_pairs={{0,4},{4,8},{8,12},{1,5},{5,9},{9,13},{2,6},{6,10},{10,14},{3,7},{... | collective-permute-start | bytes 884744 | tf_op jit(solution)/shard_map/ppermute | solution.py:216
  82.6 36.1 %collective-permute-start.1 = (bf16[2,64,1152]{2,1,0:T(8,128)(2,1)}, bf16[2,64,1152]{2,1,0:T(8,128)(2,1)}, u32[]{:S(2)}, u32[]{:S(2)}) collective-permute-start(bf16[2,64,1152]{2,1,0:T(8,128)(2,1)} %get-tuple-element.7.refs_0_), channel_id=1, source_target_pairs={{4,0},{8,4},{12,8},{5,1},{9,5},{13,9},{6,2},{10,6},{14,10},{7,3},{... | collective-permute-start | bytes 884744 | tf_op jit(solution)/shard_map/ppermute | solution.py:217
  98.9 19.9 %collective-permute-start.6 = (bf16[2,64,1152]{2,1,0:T(8,128)(2,1)}, bf16[2,64,1152]{2,1,0:T(8,128)(2,1)}, u32[]{:S(2)}, u32[]{:S(2)}) collective-permute-start(bf16[2,64,1152]{2,1,0:T(8,128)(2,1)} %collective-permute-done.4.refs_5_), channel_id=1, source_target_pairs={{4,0},{8,4},{12,8},{5,1},{9,5},{13,9},{6,2},{10,6},{14,10},{7,3},{... | collective-permute-start | bytes 884744 | tf_op jit(solution)/shard_map/ppermute | solution.py:217
  105.2 13.5 %collective-permute-start.3 = (bf16[2,64,1152]{2,1,0:T(8,128)(2,1)}, bf16[2,64,1152]{2,1,0:T(8,128)(2,1)}, u32[]{:S(2)}, u32[]{:S(2)}) collective-permute-start(bf16[2,64,1152]{2,1,0:T(8,128)(2,1)} %collective-permute-done.2.refs_3_), channel_id=1, source_target_pairs={{4,0},{8,12},{5,1},{9,13},{6,2},{10,14},{7,3},{11,15},{20,16},{24,... | collective-permute-start | bytes 884744 | tf_op jit(solution)/shard_map/ppermute | solution.py:218
  106.5 0.9 copy-start.15
  107.4 16.6 %collective-permute-start.8 = (bf16[2,64,1152]{2,1,0:T(8,128)(2,1)}, bf16[2,64,1152]{2,1,0:T(8,128)(2,1)}, u32[]{:S(2)}, u32[]{:S(2)}) collective-permute-start(bf16[2,64,1152]{2,1,0:T(8,128)(2,1)} %collective-permute-done.7.refs_8_), channel_id=1, source_target_pairs={{4,0},{8,12},{5,1},{9,13},{6,2},{10,14},{7,3},{11,15},{20,16},{24,... | collective-permute-start | bytes 884744 | tf_op jit(solution)/shard_map/ppermute | solution.py:218
  110.0 3.4 %copy-start.1 = (bf16[4096,1024]{1,0:T(8,128)(2,1)S(1)}, bf16[4096,1024]{1,0:T(8,128)(2,1)}, u32[]{:S(2)}) copy-start(bf16[4096,1024]{1,0:T(8,128)(2,1)} %key_ref.3) | copy-start | bytes 25165828
  113.4 1.1 copy-start.10
  114.6 3.1 %copy-start.16 = (f32[384,512]{1,0:T(8,128)S(1)}, f32[384,512]{1,0:T(8,128)}, u32[]{:S(2)}) copy-start(f32[384,512]{1,0:T(8,128)} %copy-done.15) | copy-start | bytes 2359300
  114.6 9.4 %copy-start.13 = (s32[16]{0:T(128)S(1)}, s32[16]{0:T(128)}, u32[]{:S(2)}) copy-start(s32[16]{0:T(128)} %owner.1) | copy-start | bytes 196
  117.7 27.2 %copy-start.14 = (s32[3]{0:T(128)S(1)}, s32[3]{0:T(128)}, u32[]{:S(2)}) copy-start(s32[3]{0:T(128)} %lengths.1) | copy-start | bytes 40
  124.0 1.1 copy-start.5
  143.2 1.7 %collective-permute-start.10 = (f32[384,64]{1,0:T(8,128)}, f32[384,64]{1,0:T(8,128)S(1)}, u32[]{:S(2)}, u32[]{:S(2)}) collective-permute-start(f32[384,64]{1,0:T(8,128)} %sums.1.mine), channel_id=1, source_target_pairs={{0,1},{1,0},{2,3},{3,2},{4,5},{5,4},{6,7},{7,6},{8,9},{9,8},{10,11... | collective-permute-start | bytes 294920 | tf_op jit(solution)/shard_map/ppermute | solution.py:247
  144.9 1.1 copy-start.6
  146.0 1.0 copy-start.8
  147.0 0.9 copy-start.11

commit v3 on v2

v3 whole, which is shorter than its diff:
```python
import functools

import jax
import jax.numpy as jnp
from jax import lax
from jax.experimental import pallas as pl
from jax.experimental.pallas import tpu as pltpu
from jax.sharding import Mesh
from jax.sharding import PartitionSpec as P

LANES = 128
ANY = pl.BlockSpec(memory_space=pl.ANY)
SMEM = pl.BlockSpec(memory_space=pltpu.SMEM)
VMEM = pl.BlockSpec(memory_space=pltpu.VMEM)
BIG = pltpu.CompilerParams(vmem_limit_bytes=32 * 1024 * 1024)
PLANE = ("groups", "pair")
WHOLE = ("groups", "ring", "pair")


def pack_kernel(where, *refs):
    ways = (len(refs)) // 3
    for way in range(ways):
        down_ref, up_ref, out_ref = refs[way], refs[ways + way], refs[2 * ways + way]
        feats = down_ref.shape[2]
        out_ref[:, :, :feats] = down_ref[...]
        out_ref[:, :, feats:] = up_ref[...]


def pack(down, up, shares, share_of):
    adapters, rank, feats = down.shape
    step = feats // shares
    tiles = up.shape[2] // LANES
    ways = len(share_of)

    def down_at(way):
        return lambda i, s: (0, 0, s[way])

    def up_at(way):
        return lambda i, s: (0, 0, s[way] % tiles)

    shape = (adapters, rank, step + LANES)
    return pl.pallas_call(
        pack_kernel,
        grid_spec=pltpu.PrefetchScalarGridSpec(
            num_scalar_prefetch=1,
            grid=(1,),
            in_specs=[pl.BlockSpec((adapters, rank, step), down_at(w)) for w in range(ways)]
            + [pl.BlockSpec((adapters, rank, LANES), up_at(w)) for w in range(ways)],
            out_specs=[pl.BlockSpec(shape, lambda i, s: (0, 0, 0)) for _ in range(ways)],
        ),
        out_shape=[jax.ShapeDtypeStruct(shape, down.dtype) for _ in range(ways)],
        compiler_params=BIG,
        name="pack",
    )(jnp.stack(share_of).astype(jnp.int32), *([down] * ways), *([up] * ways))


def spread_kernel(lengths, ids, in_ref, after, out_ref):
    blocks = lengths.shape[0]
    rows, step = in_ref.shape
    block = rows // blocks
    row = lax.broadcasted_iota(jnp.int32, (block, step), 0)
    for b in range(blocks):
        part = in_ref[b * block : (b + 1) * block, :]
        out_ref[0, b * block : (b + 1) * block, :] = jnp.where(row < lengths[b], part, jnp.zeros_like(part))
    extra = out_ref.shape[1] - rows
    lane = lax.broadcasted_iota(jnp.int32, (extra, step), 1)
    named = jnp.zeros((extra, step), jnp.float32)
    for b in range(blocks):
        named = jnp.where(lane == b, ids[b, 0].astype(jnp.float32), named)
    out_ref[0, rows:, :] = named.astype(out_ref.dtype)


def spread(tokens, lengths, ids, shares, after):
    rows, feats = tokens.shape
    step = feats // shares
    return pl.pallas_call(
        spread_kernel,
        grid=(shares,),
        in_specs=[SMEM, SMEM, pl.BlockSpec((rows, step), lambda i: (0, i)), ANY],
        out_specs=pl.BlockSpec((1, rows + 16, step), lambda i: (i, 0, 0)),
        out_shape=jax.ShapeDtypeStruct((shares, rows + 16, step), tokens.dtype),
        compiler_params=BIG,
        name="spread",
    )(lengths, ids, tokens, after)


def base_kernel(side, tok_ref, key_ref, after, out_ref):
    part = jnp.dot(tok_ref[0, : out_ref.shape[0], :], key_ref[...], preferred_element_type=jnp.float32)

    @pl.when(pl.program_id(0) == 0)
    def _():
        out_ref[...] = part

    @pl.when(pl.program_id(0) > 0)
    def _():
        out_ref[...] += part


def base_half(slabs, base_key, side, sides, rows, after):
    shares, tall, step = slabs.shape
    depth = shares * step
    wide = base_key.shape[1] // sides
    return pl.pallas_call(
        base_kernel,
        grid_spec=pltpu.PrefetchScalarGridSpec(
            num_scalar_prefetch=1,
            grid=(shares,),
            in_specs=[
                pl.BlockSpec((1, tall, step), lambda i, s: (i, 0, 0)),
                pl.BlockSpec((step, wide), lambda i, s: (i, s[0])),
                ANY,
            ],
            out_specs=pl.BlockSpec((rows, wide), lambda i, s: (0, 0)),
        ),
        out_shape=jax.ShapeDtypeStruct((rows, wide), jnp.float32),
        compiler_params=BIG,
        cost_estimate=pl.CostEstimate(
            flops=2 * rows * depth * wide, bytes_accessed=2 * depth * (rows + wide) + 4 * rows * wide, transcendentals=0
        ),
        name="base",
    )(side.reshape(1), slabs, base_key, after)


def rank_kernel(pair, per, ids, owner, here, tok_ref, *refs):
    pieces = refs[:-4]
    after, out_ref, held, sems = refs[-4:]
    count, rank = pieces[0].shape[:2]
    blocks = out_ref.shape[1]
    feats = tok_ref.shape[2]
    block = out_ref.shape[3]
    mate = pl.program_id(0)

    @pl.when(mate == 0)
    def _():
        copies = [
            pltpu.make_async_copy(piece, held.at[pl.ds(j * count, count)], sems.at[j])
            for j, piece in enumerate(pieces)
        ]
        for copy in copies:
            copy.start()
        for copy in copies:
            copy.wait()

    for b in range(blocks):
        slot = owner[ids[mate * blocks + b]]
        chip = slot // per
        way = lax.rem(lax.rem(chip, pair) - here[0] + pair, pair)
        at = way * count + chip // pair * per + lax.rem(slot, per)
        tok = tok_ref[0, b * block : (b + 1) * block, :]
        part = lax.dot_general(
            held[at, :, :feats], tok, (((1,), (1,)), ((), ())), preferred_element_type=jnp.float32
        )
        out_ref[0, b, :rank, :] = part.astype(out_ref.dtype)
        out_ref[0, b, rank:, :] = held[at, :, feats:]


def rank_parts(ids, owner, here, tok, pieces, pair, per, blocks, after):
    shares, tall, feats = tok.shape
    block = tall // blocks // LANES * LANES
    count, rank, wide = pieces[0].shape
    shape = (shares, blocks, 2 * rank, block)
    return pl.pallas_call(
        functools.partial(rank_kernel, pair, per),
        grid=(shares,),
        in_specs=[SMEM, SMEM, SMEM, pl.BlockSpec((1, tall, feats), lambda i: (i, 0, 0))] + [ANY] * (len(pieces) + 1),
        out_specs=pl.BlockSpec((1,) + shape[1:], lambda i: (i, 0, 0, 0)),
        out_shape=jax.ShapeDtypeStruct(shape, tok.dtype),
        scratch_shapes=[
            pltpu.VMEM((len(pieces) * count, rank, wide), tok.dtype),
            pltpu.SemaphoreType.DMA((len(pieces),)),
        ],
        compiler_params=BIG,
        cost_estimate=pl.CostEstimate(
            flops=2 * tok.size * rank, bytes_accessed=2 * tok.size, transcendentals=0
        ),
        name="rank",
    )(ids, owner, here, tok, *pieces, after)


def final_kernel(mine, theirs, base, out_ref):
    shares, blocks, tall, block = mine.shape
    rank = tall // 2
    wide = out_ref.shape[1]
    for b in range(blocks):
        here = slice(b * block, (b + 1) * block)
        total = mine[0, b, :rank, :].astype(jnp.float32) + theirs[0, b, :rank, :].astype(jnp.float32)
        for s in range(1, shares):
            total += mine[s, b, :rank, :].astype(jnp.float32) + theirs[s, b, :rank, :].astype(jnp.float32)
        up = jnp.concatenate([mine[s, b, rank:, :] for s in range(wide // LANES)], axis=1)
        delta = lax.dot_general(
            total.astype(jnp.bfloat16), up, (((0,), (0,)), ((), ())), preferred_element_type=jnp.float32
        )
        out_ref[here, :] = (base[here, :] + delta).astype(out_ref.dtype)


def final(mine, theirs, base, dtype):
    return pl.pallas_call(
        final_kernel,
        in_specs=[VMEM, VMEM, VMEM],
        out_specs=VMEM,
        out_shape=jax.ShapeDtypeStruct(base.shape, dtype),
        compiler_params=BIG,
        name="final",
    )(mine, theirs, base)


def body(tokens, base_key, adapter_down, adapter_up, adapter_ids, owner_slot, lengths):
    groups, pair = lax.axis_size("groups"), lax.axis_size("pair")
    sides = lax.axis_size("tensor")
    shares = groups * pair
    g, y, t = (lax.axis_index(name) for name in ("groups", "pair", "tensor"))
    rows = tokens.shape[0]
    blocks = lengths.shape[0]
    per = adapter_down.shape[0]

    def across(x):
        return lax.ppermute(x, "tensor", [(i, (i + 1) % sides) for i in range(sides)])

    def to_plane(x):
        return lax.all_to_all(x, PLANE, split_axis=0, concat_axis=0, tiled=True)

    packed = pack(jnp.swapaxes(adapter_down, 1, 2), adapter_up, shares, [g * pair + (y + w) % pair for w in range(pair)])
    slabs = spread(tokens, lengths, adapter_ids, shares, packed[0])
    pieces = [packed[0]]
    for w in range(1, pair):
        pieces.append(lax.ppermute(packed[pair - w], "pair", [(a, (a - w) % pair) for a in range(pair)]))
    swapped = pieces[-1]
    pieces = [lax.all_gather(piece, "ring", axis=0, tiled=True) for piece in pieces]

    tok = to_plane(slabs)
    ids = tok[:, rows, :blocks].astype(jnp.int32).reshape(-1)

    base_out = base_half(slabs, base_key, (t + 1) % sides, sides, rows, swapped)
    base_in = across(base_out)
    base_mine = base_half(slabs, base_key, t, sides, rows, base_out)
    base = base_mine + base_in

    mine = to_plane(rank_parts(ids, owner_slot, y.reshape(1), tok, pieces, pair, per, blocks, base))
    return final(mine, across(mine), base, tokens.dtype)


def solution(mesh):
    groups, dp, sides = (mesh.shape[name] for name in ("groups", "dp", "tensor"))
    pair = 2 if dp % 2 == 0 else 1
    cut = Mesh(mesh.devices.reshape(groups, dp // pair, pair, sides), ("groups", "ring", "pair", "tensor"))
    stored = ("ring", "pair")
    placed = (
        P(WHOLE, "tensor"),
        P("tensor", None),
        P(stored, "tensor", None),
        P(stored, None, "tensor"),
        P(WHOLE, None),
        P(),
        P(WHOLE),
    )
    return jax.shard_map(body, mesh=cut, in_specs=placed, out_specs=P(WHOLE, "tensor"), check_vma=False)
```

time: 150 us -> 124 us (0.83)
  starting transfers between devices: 28.5 us -> 7.26 us
  between operations: 0.21 us -> 13.5 us
  waiting for transfers between devices: 70.7 us -> 60.9 us
  local copies, waits for them, and re-layouts: 20.5 us -> 13.3 us
    ppermute x9 -> x1, waiting for transfers between devices: 68.6 us -> 41.9 us  [body(): lax.ppermute(packed[pair - w], 'pair', [(a, (a - w) % pair) for a in rang...]
    all_gather x0 -> x2, waiting for transfers between devices: none -> 17.2 us  [body(): lax.all_gather(piece, 'ring', axis=0, tiled=True)]
    ppermute x9 -> x1, starting transfers between devices: 18.5 us -> 2.02 us  [body(): lax.ppermute(packed[pair - w], 'pair', [(a, (a - w) % pair) for a in rang...]
    unnamed x34 -> x23, local copies, waits for them, and re-layouts: 18.6 us -> 13.2 us
    all_to_all x2 -> x1, starting transfers between devices: 9.96 us -> 5.16 us  [to_plane(): return lax.all_to_all(x, PLANE, split_axis=0, concat_axis=0, tiled=True)]
    pallas_call x2, Pallas kernels: 6.2 us -> 9.19 us  [base_half(): pl.pallas_call(base_kernel, grid_spec=pltpu.PrefetchScalarGridSpec(num_sc...]
    pallas_call x4 -> x3, Pallas kernels: 9.37 us -> 6.59 us  [the longest x1 2.9 us: spread(): pl.pallas_call(spread_kernel, grid=(shares,), in_specs=[SMEM, SMEM, pl.Bl...]
  transfers between devices with their start and end apart: 13 -> 6, of which waited for: 7 -> 3; matrix products, arithmetic and copies ran while one was open for 2% -> 2% of each run, Pallas kernels for 5% -> 10%
where the time goes in v3:
time: 124 us; the launch traced here: 123 us
  waiting for transfers between devices  60.9 us (49%)
  Pallas kernels  17.1 us (14%)
  between operations  13.5 us (11%)
  local copies, waits for them, and re-layouts  13.3 us (11%)
  blocking collectives  9.98 us (8%)
  starting transfers between devices  7.26 us (6%)
    ppermute x1, waiting for transfers between devices, body(): lax.ppermute(packed[pair - w], 'pair', [(a, (a - w) % pair) for a in rang...  41.9 us
    all_gather x2, waiting for transfers between devices, body(): lax.all_gather(piece, 'ring', axis=0, tiled=True)  17.2 us
    unnamed x23, local copies, waits for them, and re-layouts  13.2 us
    all_to_all x1, blocking collectives, to_plane(): return lax.all_to_all(x, PLANE, split_axis=0, concat_axis=0, tiled=True)  9.98 us
    pallas_call x2, Pallas kernels, base_half(): pl.pallas_call(base_kernel, grid_spec=pltpu.PrefetchScalarGridSpec(num_sc...  9.19 us
    all_to_all x1, starting transfers between devices, to_plane(): return lax.all_to_all(x, PLANE, split_axis=0, concat_axis=0, tiled=True)  5.16 us
    pallas_call x1, Pallas kernels, spread(): pl.pallas_call(spread_kernel, grid=(shares,), in_specs=[SMEM, SMEM, pl.Bl...  2.9 us
    pallas_call x1, Pallas kernels, rank_parts(): pl.pallas_call(functools.partial(rank_kernel, pair, per), grid=(shares,),...  2.65 us
  transfers between devices with their start and end apart: 6, of which 3 were waited for; matrix products, arithmetic and copies ran while one was open for 2% of the time, Pallas kernels for 10%

profile of v3, /device:TPU:0, one launch (start us, length us, event | category | flops | bytes accessed | tf_op | source)
XLA Modules:
  0.0 123.2 jit_solution(13631892889376560571)
XLA Ops:
  6.5 0.0 all-gather.3.cloned.1.call-start
  6.5 0.1 pad_add_fusion.where
  6.6 0.0 copy-start.3
  6.6 1.2 copy-done.3
  7.8 0.0 copy-start.7
  7.8 0.9 copy-done.7
  8.7 1.3 %pack.1 = (bf16[2,64,1152]{2,1,0:T(8,128)(2,1)}, bf16[2,64,1152]{2,1,0:T(8,128)(2,1)S(1)}) custom-call(s32[2]{0:T(128)S(1)} %pad_add_fusion.where, bf16[2,64,4096]{2,1,0:T(8,128)(2,1)S(1)} %bitcast.6, bf16[2,64,4096]{2,1,0:T(8,128)(2,1)S(1)} %bitcast.7, bf16[2,64,512]{2,1,0:T(8,128)(2,1)S(1)} %copy-done.7, bf16[2,64,512]{2,1,0:T(8,128)(2,1)S(1)} %copy-done.7), custom_call_target="tpu_custom_call" | custom-call | tf_op jit(solution)/shard_map/pack/pallas_call | solution.py:42
  10.1 0.0 copy-start.10
  10.1 0.7 copy-done.10
  10.8 0.0 all-gather.3.cloned.1.call-update
  10.8 0.7 copy.10.ids
  11.6 0.0 copy-start.4
  11.6 1.9 %copy-done.4 = bf16[384,4096]{1,0:T(8,128)(2,1)S(1)} copy-done((bf16[384,4096]{1,0:T(8,128)(2,1)S(1)}, bf16[384,4096]{1,0:T(8,128)(2,1)}, u32[]{:S(2)}) %copy-start.4) | copy-done | bytes 3145752
  13.5 0.0 copy-start.8
  13.5 0.7 copy-done.8
  14.1 2.9 %spread.1.tok_ref = bf16[4,400,1024]{2,1,0:T(8,128)(2,1)} custom-call(s32[3]{0:T(128)S(1)} %copy-done.8, s32[3,1]{1,0:T(4,128)S(1)} %copy.10.ids, bf16[384,4096]{1,0:T(8,128)(2,1)S(1)} %copy-done.4, bf16[2,64,1152]{2,1,0:T(8,128)(2,1)} %get-tuple-element.7.after), custom_call_target="tpu_custom_call" | custom-call | tf_op jit(solution)/shard_map/spread/pallas_call | solution.py:76
  17.0 5.2 %all-to-all-start = ((bf16[4,400,1024]{2,1,0:T(8,128)(2,1)}), bf16[4,400,1024]{2,1,0:T(8,128)(2,1)S(1)}, u32[]{:S(2)}, u32[]{:S(2)}) async-start(bf16[4,400,1024]{2,1,0:T(8,128)(2,1)} %spread.1.tok_ref), calls=%async_computation | async-start | bytes 6553600 | tf_op jit(solution)/shard_map/all_to_all | solution.py:220
  22.2 0.0 all-gather.5.cloned.1.call-start
  22.2 2.0 %collective-permute-start = (bf16[2,64,1152]{2,1,0:T(8,128)(2,1)}, bf16[2,64,1152]{2,1,0:T(8,128)(2,1)}, u32[]{:S(2)}, u32[]{:S(2)}) collective-permute-start(bf16[2,64,1152]{2,1,0:T(8,128)(2,1)} %copy-done.10), channel_id=1, source_target_pairs={{0,2},{2,0},{1,3},{3,1},{4,6},{6,4},{5,7},{7,5},{8,10},{10,8},{9,1... | collective-permute-start | bytes 884744 | tf_op jit(solution)/shard_map/ppermute | solution.py:226
  24.2 41.9 %collective-permute-done.after = bf16[2,64,1152]{2,1,0:T(8,128)(2,1)} collective-permute-done((bf16[2,64,1152]{2,1,0:T(8,128)(2,1)}, bf16[2,64,1152]{2,1,0:T(8,128)(2,1)}, u32[]{:S(2)}, u32[]{:S(2)}) %collective-permute-start) | collective-permute-done | bytes 294944 | tf_op jit(solution)/shard_map/ppermute | solution.py:226
  66.1 0.0 all-gather.5.cloned.1.call-update
  66.2 0.0 copy-start
  66.2 3.4 %copy-done = bf16[4096,1024]{1,0:T(8,128)(2,1)S(1)} copy-done((bf16[4096,1024]{1,0:T(8,128)(2,1)S(1)}, bf16[4096,1024]{1,0:T(8,128)(2,1)}, u32[]{:S(2)}) %copy-start) | copy-done | bytes 8388632
  69.5 0.0 copy-start.1
  69.5 4.7 %base.2.after = f32[384,512]{1,0:T(8,128)S(1)} custom-call(s32[1]{0:T(128)} %bitcast.5.side, bf16[4,400,1024]{2,1,0:T(8,128)(2,1)} %spread.1.tok_ref, bf16[4096,1024]{1,0:T(8,128)(2,1)S(1)} %copy-done, bf16[2,64,1152]{2,1,0:T(8,128)(2,1)} %collective-permute-done.after), custom_call_target="tpu_custom_call" | custom-call | flops 1610612736 | bytes 8126464 | tf_op jit(solution)/shard_map/base/pallas_call | solution.py:103
  74.3 0.1 collective-permute-start.1
  74.4 0.0 copy-done.1
  74.4 0.0 copy-start.9
  74.4 4.4 %base.3 = f32[384,512]{1,0:T(8,128)S(1)} custom-call(s32[1]{0:T(128)} %bitcast.4.side, bf16[4,400,1024]{2,1,0:T(8,128)(2,1)} %spread.1.tok_ref, bf16[4096,1024]{1,0:T(8,128)(2,1)S(1)} %copy-done.1, f32[384,512]{1,0:T(8,128)S(1)} %base.2.after), custom_call_target="tpu_custom_call" | custom-call | flops 1610612736 | bytes 8126464 | tf_op jit(solution)/shard_map/base/pallas_call | solution.py:103
  78.9 0.0 collective-permute-done.1
  78.9 1.0 add.32.refs_2_.base
  79.9 0.0 all-to-all-done.tok_ref
  79.9 0.1 reshape.16.ids
  80.0 0.0 all-gather.3.cloned.1.call-done.refs_0_
  80.0 17.2 %all-gather.5.cloned.1.call-done.refs_1_ = bf16[8,64,1152]{2,1,0:T(8,128)(2,1)} async-done(((bf16[2,64,1152]{2,1,0:T(8,128)(2,1)}), bf16[8,64,1152]{2,1,0:T(8,128)(2,1)}) %all-gather.5.cloned.1.call-update) | async-done | bytes 1179664 | tf_op jit(solution)/shard_map/all_gather | solution.py:228
  97.2 0.0 copy-done.9
  97.2 0.0 copy-start.2
  97.2 1.1 copy-done.2
  98.4 0.0 copy-start.5
  98.4 1.3 %copy-done.5 = bf16[8,64,1152]{2,1,0:T(8,128)(2,1)S(1)} copy-done((bf16[8,64,1152]{2,1,0:T(8,128)(2,1)S(1)}, bf16[8,64,1152]{2,1,0:T(8,128)(2,1)}, u32[]{:S(2)}) %copy-start.5) | copy-done | bytes 1179672
  99.6 0.0 copy-start.6
  99.6 1.3 %copy-done.6 = bf16[8,64,1152]{2,1,0:T(8,128)(2,1)S(1)} copy-done((bf16[8,64,1152]{2,1,0:T(8,128)(2,1)S(1)}, bf16[8,64,1152]{2,1,0:T(8,128)(2,1)}, u32[]{:S(2)}) %copy-start.6) | copy-done | bytes 1179672
  100.9 2.6 %rank.1 = bf16[4,3,128,128]{3,2,1,0:T(8,128)(2,1)S(1)} custom-call(s32[12]{0:T(128)S(1)} %reshape.16.ids, s32[16]{0:T(128)S(1)} %copy-done.9, s32[1]{0:T(128)} %bitcast.3.here, bf16[4,400,1024]{2,1,0:T(8,128)(2,1)S(1)} %all-to-all-done.tok_ref, bf16[8,64,1152]{2,1,0:T(8,128)(2,1)S(1)} %copy-done.5, bf16[8,64,1152]{2,1,0:T(8,128)(2,1)S(1)} %copy-done.6, ...), custom_call_target="tpu_custom_call" | custom-call | flops 209715200 | bytes 3276800 | tf_op jit(solution)/shard_map/rank/pallas_call | solution.py:162
  103.6 10.0 %all_to_all.10.mine = bf16[4,3,128,128]{3,2,1,0:T(8,128)(2,1)S(1)} all-to-all(bf16[4,3,128,128]{3,2,1,0:T(8,128)(2,1)S(1)} %rank.1), channel_id=1, replica_groups=mesh['groups'=2,'ring'=4,'pair'=2,'tensor'=2] {'groups','pair'}, dimensions={0} | all-to-all | bytes 786432 | tf_op jit(solution)/shard_map/all_to_all | solution.py:220
  113.5 0.0 collective-permute-start.2
  113.6 1.7 %collective-permute-done.2.theirs = bf16[4,3,128,128]{3,2,1,0:T(8,128)(2,1)S(1)} collective-permute-done((bf16[4,3,128,128]{3,2,1,0:T(8,128)(2,1)S(1)}, bf16[4,3,128,128]{3,2,1,0:T(8,128)(2,1)S(1)}, u32[]{:S(2)}, u32[]{:S(2)}) %collective-permute-start.2) | collective-permute-done | bytes 393248 | tf_op jit(solution)/shard_map/ppermute | solution.py:217
  115.3 1.0 final.1
  (1 shorter events, 0.0 us)
Async XLA Ops:
  6.5 73.5 %all-gather.3.cloned.1.call-start = ((), (), s32[]{:S(2)}) async-start(), calls=%async_computation.2 | async-start | bytes 1474560 | tf_op jit(solution)/shard_map/all_gather | solution.py:228
  6.6 1.2 copy-start.3
  7.8 0.9 copy-start.7
  10.1 0.7 copy-start.10
  11.6 1.9 %copy-start.4 = (bf16[384,4096]{1,0:T(8,128)(2,1)S(1)}, bf16[384,4096]{1,0:T(8,128)(2,1)}, u32[]{:S(2)}) copy-start(bf16[384,4096]{1,0:T(8,128)(2,1)} %in_ref.1) | copy-start | bytes 9437188
  13.5 0.7 copy-start.8
  17.0 62.9 %all-to-all-start = ((bf16[4,400,1024]{2,1,0:T(8,128)(2,1)}), bf16[4,400,1024]{2,1,0:T(8,128)(2,1)S(1)}, u32[]{:S(2)}, u32[]{:S(2)}) async-start(bf16[4,400,1024]{2,1,0:T(8,128)(2,1)} %spread.1.tok_ref), calls=%async_computation | async-start | bytes 6553600 | tf_op jit(solution)/shard_map/all_to_all | solution.py:220
  22.2 75.1 %all-gather.5.cloned.1.call-start = ((), (), s32[]{:S(2)}) async-start(), calls=%async_computation.3 | async-start | bytes 1474560 | tf_op jit(solution)/shard_map/all_gather | solution.py:228
  22.2 44.0 %collective-permute-start = (bf16[2,64,1152]{2,1,0:T(8,128)(2,1)}, bf16[2,64,1152]{2,1,0:T(8,128)(2,1)}, u32[]{:S(2)}, u32[]{:S(2)}) collective-permute-start(bf16[2,64,1152]{2,1,0:T(8,128)(2,1)} %copy-done.10), channel_id=1, source_target_pairs={{0,2},{2,0},{1,3},{3,1},{4,6},{6,4},{5,7},{7,5},{8,10},{10,8},{9,1... | collective-permute-start | bytes 884744 | tf_op jit(solution)/shard_map/ppermute | solution.py:226
  66.2 3.4 %copy-start = (bf16[4096,1024]{1,0:T(8,128)(2,1)S(1)}, bf16[4096,1024]{1,0:T(8,128)(2,1)}, u32[]{:S(2)}) copy-start(bf16[4096,1024]{1,0:T(8,128)(2,1)} %key_ref.3) | copy-start | bytes 25165828
  69.5 4.8 %copy-start.1 = (bf16[4096,1024]{1,0:T(8,128)(2,1)S(1)}, bf16[4096,1024]{1,0:T(8,128)(2,1)}, u32[]{:S(2)}) copy-start(bf16[4096,1024]{1,0:T(8,128)(2,1)} %key_ref.3) | copy-start | bytes 25165828
  74.3 4.6 %collective-permute-start.1 = (f32[384,512]{1,0:T(8,128)S(1)}, f32[384,512]{1,0:T(8,128)S(1)}, u32[]{:S(2)}, u32[]{:S(2)}) collective-permute-start(f32[384,512]{1,0:T(8,128)S(1)} %base.2.after), channel_id=1, source_target_pairs={{0,1},{1,0},{2,3},{3,2},{4,5},{5,4},{6,7},{7,6},{8,9},{9,8},{10,11... | collective-permute-start | bytes 2359304 | tf_op jit(solution)/shard_map/ppermute | solution.py:217
  74.4 22.8 %copy-start.9 = (s32[16]{0:T(128)S(1)}, s32[16]{0:T(128)}, u32[]{:S(2)}) copy-start(s32[16]{0:T(128)} %owner.1) | copy-start | bytes 196
  97.2 1.1 copy-start.2
  98.4 1.3 %copy-start.5 = (bf16[8,64,1152]{2,1,0:T(8,128)(2,1)S(1)}, bf16[8,64,1152]{2,1,0:T(8,128)(2,1)}, u32[]{:S(2)}) copy-start(bf16[8,64,1152]{2,1,0:T(8,128)(2,1)} %all-gather.3.cloned.1.call-done.refs_0_) | copy-start | bytes 3538948
  99.6 1.3 %copy-start.6 = (bf16[8,64,1152]{2,1,0:T(8,128)(2,1)S(1)}, bf16[8,64,1152]{2,1,0:T(8,128)(2,1)}, u32[]{:S(2)}) copy-start(bf16[8,64,1152]{2,1,0:T(8,128)(2,1)} %all-gather.5.cloned.1.call-done.refs_1_) | copy-start | bytes 3538948
  113.5 1.7 %collective-permute-start.2 = (bf16[4,3,128,128]{3,2,1,0:T(8,128)(2,1)S(1)}, bf16[4,3,128,128]{3,2,1,0:T(8,128)(2,1)S(1)}, u32[]{:S(2)}, u32[]{:S(2)}) collective-permute-start(bf16[4,3,128,128]{3,2,1,0:T(8,128)(2,1)S(1)} %all_to_all.10.mine), channel_id=1, source_target_pairs={{0,1},{1,0},{2,3},{3,2},{4,5},{5,4},{6,7},{7,6},{8,9},{9,8},{10,11... | collective-permute-start | bytes 1179656 | tf_op jit(solution)/shard_map/ppermute | solution.py:217
Sparse Core Ops, SparseCore 0:
  10.9 33.1 all-gather.2
  66.3 30.9 all-gather.4

commit v4 on v3

v4 whole, which is shorter than its diff:
```python
import functools

import jax
import jax.numpy as jnp
from jax import lax
from jax.experimental import pallas as pl
from jax.experimental.pallas import tpu as pltpu
from jax.sharding import Mesh
from jax.sharding import PartitionSpec as P

LANES = 128
ANY = pl.BlockSpec(memory_space=pl.ANY)
SMEM = pl.BlockSpec(memory_space=pltpu.SMEM)
VMEM = pl.BlockSpec(memory_space=pltpu.VMEM)
HBM = pl.BlockSpec(memory_space=pltpu.HBM)
BIG = pltpu.CompilerParams(vmem_limit_bytes=32 * 1024 * 1024)
PLANE = ("groups", "pair")
WHOLE = ("groups", "ring", "pair")


def hand_kernel(*refs):
    pass


def hand_on(x, *after):
    return pl.pallas_call(
        hand_kernel,
        in_specs=[ANY] * (1 + len(after)),
        out_specs=ANY,
        out_shape=jax.ShapeDtypeStruct(x.shape, x.dtype),
        input_output_aliases={0: 0},
        name="hand",
    )(x, *after)


def pack_kernel(where, down, up, *refs):
    outs, sems = refs[:-1], refs[-1]
    feats = outs[0].shape[2] - LANES
    copies = []
    for way, out in enumerate(outs):
        start = pl.multiple_of(where[way] * feats, LANES)
        tile = pl.multiple_of(lax.rem(where[way], up.shape[2] // LANES) * LANES, LANES)
        copies.append(pltpu.make_async_copy(down.at[:, :, pl.ds(start, feats)], out.at[:, :, :feats], sems.at[way, 0]))
        copies.append(pltpu.make_async_copy(up.at[:, :, pl.ds(tile, LANES)], out.at[:, :, feats:], sems.at[way, 1]))
    for copy in copies:
        copy.start()
    for copy in copies:
        copy.wait()


def pack(down, up, shares, share_of):
    adapters, rank, feats = down.shape
    ways = len(share_of)
    shape = jax.ShapeDtypeStruct((adapters, rank, feats // shares + LANES), down.dtype)
    return pl.pallas_call(
        pack_kernel,
        in_specs=[SMEM, HBM, HBM],
        out_specs=[VMEM] * ways,
        out_shape=[shape] * ways,
        scratch_shapes=[pltpu.SemaphoreType.DMA((ways, 2))],
        compiler_params=BIG,
        name="pack",
    )(jnp.stack(share_of).astype(jnp.int32), down, up)


def spread_kernel(lengths, ids, in_ref, out_ref):
    blocks = lengths.shape[0]
    rows, step = in_ref.shape
    block = rows // blocks
    row = lax.broadcasted_iota(jnp.int32, (block, step), 0)
    for b in range(blocks):
        part = in_ref[b * block : (b + 1) * block, :]
        out_ref[0, b * block : (b + 1) * block, :] = jnp.where(row < lengths[b], part, jnp.zeros_like(part))
    extra = out_ref.shape[1] - rows
    lane = lax.broadcasted_iota(jnp.int32, (extra, step), 1)
    named = jnp.zeros((extra, step), jnp.float32)
    for b in range(blocks):
        named = jnp.where(lane == b, ids[b, 0].astype(jnp.float32), named)
    out_ref[0, rows:, :] = named.astype(out_ref.dtype)


def spread(tokens, lengths, ids, shares):
    rows, feats = tokens.shape
    step = feats // shares
    return pl.pallas_call(
        spread_kernel,
        grid=(shares,),
        in_specs=[SMEM, SMEM, pl.BlockSpec((rows, step), lambda i: (0, i))],
        out_specs=pl.BlockSpec((1, rows + 16, step), lambda i: (i, 0, 0)),
        out_shape=jax.ShapeDtypeStruct((shares, rows + 16, step), tokens.dtype),
        compiler_params=BIG,
        name="spread",
    )(lengths, ids, tokens)


def base_kernel(side, lengths, tok_ref, key_ref, *refs):
    out_ref = refs[-1]
    part = jnp.dot(tok_ref[...], key_ref[...], preferred_element_type=jnp.float32)
    step = pl.program_id(0)

    @pl.when(step == 0)
    def _():
        out_ref[...] = part

    @pl.when(step > 0)
    def _():
        out_ref[...] += part

    @pl.when(step == pl.num_programs(0) - 1)
    def _():
        blocks = lengths.shape[0]
        block = out_ref.shape[0] // blocks
        row = lax.broadcasted_iota(jnp.int32, (block, out_ref.shape[1]), 0)
        for b in range(blocks):
            here = slice(b * block, (b + 1) * block)
            out_ref[here, :] = jnp.where(row < lengths[b], out_ref[here, :], 0.0)


def base_half(tokens, base_key, side, sides, lengths, *after):
    rows, depth = tokens.shape
    wide = base_key.shape[1] // sides
    step = 1024
    return pl.pallas_call(
        base_kernel,
        grid_spec=pltpu.PrefetchScalarGridSpec(
            num_scalar_prefetch=2,
            grid=(depth // step,),
            in_specs=[
                pl.BlockSpec((rows, step), lambda i, s, n: (0, i)),
                pl.BlockSpec((step, wide), lambda i, s, n: (i, s[0])),
            ]
            + [ANY] * len(after),
            out_specs=pl.BlockSpec((rows, wide), lambda i, s, n: (0, 0)),
        ),
        out_shape=jax.ShapeDtypeStruct((rows, wide), jnp.float32),
        compiler_params=BIG,
        cost_estimate=pl.CostEstimate(
            flops=2 * rows * depth * wide, bytes_accessed=2 * depth * (rows + wide) + 4 * rows * wide, transcendentals=0
        ),
        name="base",
    )(side.reshape(1), lengths, tokens, base_key, *after)


def rank_kernel(ring, pair, ids, owner, here, tok_ref, *refs):
    pieces = refs[:-4]
    after, out_ref, held, sems = refs[-4:]
    per, rank = pieces[0].shape[:2]
    blocks = out_ref.shape[1]
    feats = tok_ref.shape[2]
    block = out_ref.shape[3]
    mate = pl.program_id(0)

    @pl.when(mate == 0)
    def _():
        copies = [
            pltpu.make_async_copy(piece, held.at[pl.ds(j * per, per)], sems.at[j])
            for j, piece in enumerate(pieces)
        ]
        for copy in copies:
            copy.start()
        for copy in copies:
            copy.wait()

    for b in range(blocks):
        slot = owner[ids[mate * blocks + b]]
        chip = slot // per
        away = lax.rem(chip // pair - here[0] + ring, ring)
        way = lax.rem(lax.rem(chip, pair) - here[1] + pair, pair)
        at = (way * ring + away) * per + lax.rem(slot, per)
        tok = tok_ref[0, b * block : (b + 1) * block, :]
        part = lax.dot_general(
            held[at, :, :feats], tok, (((1,), (1,)), ((), ())), preferred_element_type=jnp.float32
        )
        out_ref[0, b, :rank, :] = part.astype(out_ref.dtype)
        out_ref[0, b, rank:, :] = held[at, :, feats:]


def rank_parts(ids, owner, here, tok, pieces, ring, pair, blocks, after):
    shares, tall, feats = tok.shape
    block = tall // blocks // LANES * LANES
    per, rank, wide = pieces[0].shape
    shape = (shares, blocks, 2 * rank, block)
    return pl.pallas_call(
        functools.partial(rank_kernel, ring, pair),
        grid=(shares,),
        in_specs=[SMEM, SMEM, SMEM, pl.BlockSpec((1, tall, feats), lambda i: (i, 0, 0))] + [ANY] * (len(pieces) + 1),
        out_specs=pl.BlockSpec((1,) + shape[1:], lambda i: (i, 0, 0, 0)),
        out_shape=jax.ShapeDtypeStruct(shape, tok.dtype),
        scratch_shapes=[
            pltpu.VMEM((len(pieces) * per, rank, wide), tok.dtype),
            pltpu.SemaphoreType.DMA((len(pieces),)),
        ],
        compiler_params=BIG,
        cost_estimate=pl.CostEstimate(
            flops=2 * tok.size * rank, bytes_accessed=2 * tok.size, transcendentals=0
        ),
        name="rank",
    )(ids, owner, here, tok, *pieces, after)


def final_kernel(mine, theirs, base, out_ref):
    shares, blocks, tall, block = mine.shape
    rank = tall // 2
    wide = out_ref.shape[1]
    for b in range(blocks):
        here = slice(b * block, (b + 1) * block)
        total = mine[0, b, :rank, :].astype(jnp.float32) + theirs[0, b, :rank, :].astype(jnp.float32)
        for s in range(1, shares):
            total += mine[s, b, :rank, :].astype(jnp.float32) + theirs[s, b, :rank, :].astype(jnp.float32)
        up = jnp.concatenate([mine[s, b, rank:, :] for s in range(wide // LANES)], axis=1)
        delta = lax.dot_general(
            total.astype(jnp.bfloat16), up, (((0,), (0,)), ((), ())), preferred_element_type=jnp.float32
        )
        out_ref[here, :] = (base[here, :] + delta).astype(out_ref.dtype)


def final(mine, theirs, base, dtype):
    return pl.pallas_call(
        final_kernel,
        in_specs=[VMEM, VMEM, VMEM],
        out_specs=VMEM,
        out_shape=jax.ShapeDtypeStruct(base.shape, dtype),
        compiler_params=BIG,
        name="final",
    )(mine, theirs, base)


def body(tokens, base_key, adapter_down, adapter_up, adapter_ids, owner_slot, lengths):
    groups, ring, pair = lax.axis_size("groups"), lax.axis_size("ring"), lax.axis_size("pair")
    sides = lax.axis_size("tensor")
    shares = groups * pair
    g, z, y, t = (lax.axis_index(name) for name in ("groups", "ring", "pair", "tensor"))
    rows = tokens.shape[0]
    blocks = lengths.shape[0]

    def across(x):
        return lax.ppermute(x, "tensor", [(i, (i + 1) % sides) for i in range(sides)])

    def to_plane(x):
        return lax.all_to_all(x, PLANE, split_axis=0, concat_axis=0, tiled=True)

    def along(x, step):
        return lax.ppermute(x, "ring", [(a, (a + step) % ring) for a in range(ring)])

    def first_hops(x):
        return {0: x, ring - 1: along(x, 1), **({1: along(x, -1)} if ring > 2 else {})}

    def more_hops(held, way):
        for k in range(2, ring // 2 + 1):
            if 2 * k < ring or way % 2 == 0:
                held[ring - k] = along(held[ring - k + 1], 1)
            if 2 * k < ring or way % 2 == 1:
                held[k] = along(held[k - 1], -1)
        return [held[k] for k in range(ring)]

    packed = pack(jnp.swapaxes(adapter_down, 1, 2), adapter_up, shares, [g * pair + (y + w) % pair for w in range(pair)])
    slabs = spread(tokens, lengths, adapter_ids, shares)
    swapped = [
        lax.ppermute(packed[pair - w], "pair", [(a, (a - w) % pair) for a in range(pair)]) for w in range(1, pair)
    ]
    own = first_hops(packed[0])
    near = [own[k] for k in own if k > 0]
    others = [first_hops(hand_on(piece, *near)) for piece in swapped]
    tok = to_plane(hand_on(slabs, *swapped))
    ids = tok[:, rows, :blocks].astype(jnp.int32).reshape(-1)

    next_near = [held[k] for held in others for k in held if k > 0]
    base_out = base_half(tokens, base_key, (t + 1) % sides, sides, lengths, *next_near)
    pieces = [more_hops(held, way) for way, held in enumerate([own] + others)]
    base_in = across(base_out)
    base_mine = base_half(tokens, base_key, t, sides, lengths, base_out, pieces[0][ring // 2])
    base = base_mine + base_in

    here = jnp.stack([z, y]).astype(jnp.int32)
    flat = [piece for way in pieces for piece in way]
    mine = to_plane(rank_parts(ids, owner_slot, here, tok, flat, ring, pair, blocks, base))
    return final(mine, across(mine), base, tokens.dtype)


def solution(mesh):
    groups, dp, sides = (mesh.shape[name] for name in ("groups", "dp", "tensor"))
    pair = 2 if dp % 2 == 0 else 1
    cut = Mesh(mesh.devices.reshape(groups, dp // pair, pair, sides), ("groups", "ring", "pair", "tensor"))
    stored = ("ring", "pair")
    placed = (
        P(WHOLE, "tensor"),
        P("tensor", None),
        P(stored, "tensor", None),
        P(stored, None, "tensor"),
        P(WHOLE, None),
        P(),
        P(WHOLE),
    )
    return jax.shard_map(body, mesh=cut, in_specs=placed, out_specs=P(WHOLE, "tensor"), check_vma=False)
```

time: 124 us -> 103 us (0.83)
  waiting for transfers between devices: 60.9 us -> 35.4 us
  between operations: 13.5 us -> 0.12 us
  starting transfers between devices: 7.26 us -> 17.6 us
  local copies, waits for them, and re-layouts: 13.3 us -> 21.1 us
    ppermute x1, waiting for transfers between devices: 41.9 us -> 0.87 us  [body(): lax.ppermute(packed[pair - w], 'pair', [(a, (a - w) % pair) for a in rang...]
    ppermute x0 -> x6, waiting for transfers between devices: none -> 32.8 us  [along(): lax.ppermute(x, 'ring', [(a, (a + step) % ring) for a in range(ring)])]
    all_gather x2 -> x0, waiting for transfers between devices: 17.2 us -> none  [body(): lax.all_gather(piece, 'ring', axis=0, tiled=True)]
    ppermute x0 -> x6, starting transfers between devices: none -> 9.73 us  [along(): lax.ppermute(x, 'ring', [(a, (a + step) % ring) for a in range(ring)])]
    unnamed x23 -> x43, local copies, waits for them, and re-layouts: 13.2 us -> 21 us
    pallas_call x1, Pallas kernels: 2.9 us -> 1.12 us  [spread(): pl.pallas_call(spread_kernel, grid=(shares,), in_specs=[SMEM, SMEM, pl.Bl...]
    pallas_call x2 -> x4, Pallas kernels: 3.96 us -> 5.64 us  [the longest x1 5 us: rank_parts(): pl.pallas_call(functools.partial(rank_kernel, ring, pair), grid=(shares,)...]
  transfers between devices with their start and end apart: 6 -> 10, of which waited for: 3 -> 7; matrix products, arithmetic and copies ran while one was open for 2% -> 3% of each run, Pallas kernels for 10% -> 9%
where the time goes in v4:
time: 103 us
  waiting for transfers between devices  35.4 us (34%)
  local copies, waits for them, and re-layouts  21.1 us (20%)
  starting transfers between devices  17.6 us (17%)
  Pallas kernels  16.1 us (16%)
  blocking collectives  10.2 us (10%)
  other arithmetic  2.14 us (2%)
    ppermute x6, waiting for transfers between devices, along(): lax.ppermute(x, 'ring', [(a, (a + step) % ring) for a in range(ring)])  32.8 us
    unnamed x43, local copies, waits for them, and re-layouts  21 us
    all_to_all x1, blocking collectives, to_plane(): return lax.all_to_all(x, PLANE, split_axis=0, concat_axis=0, tiled=True)  10.2 us
    ppermute x6, starting transfers between devices, along(): lax.ppermute(x, 'ring', [(a, (a + step) % ring) for a in range(ring)])  9.73 us
    pallas_call x2, Pallas kernels, base_half(): pl.pallas_call(base_kernel, grid_spec=pltpu.PrefetchScalarGridSpec(num_sc...  8.31 us
    pallas_call x1, Pallas kernels, rank_parts(): pl.pallas_call(functools.partial(rank_kernel, ring, pair), grid=(shares,)...  5 us
    all_to_all x1, starting transfers between devices, to_plane(): return lax.all_to_all(x, PLANE, split_axis=0, concat_axis=0, tiled=True)  4.94 us
    ppermute x1, starting transfers between devices, body(): lax.ppermute(packed[pair - w], 'pair', [(a, (a - w) % pair) for a in rang...  2.97 us
  transfers between devices with their start and end apart: 10, of which 7 were waited for; matrix products, arithmetic and copies ran while one was open for 3% of the time, Pallas kernels for 9%

profile of v4, /device:TPU:0, one launch (start us, length us, event | category | flops | bytes accessed | tf_op | source)
XLA Modules:
  0.0 102.7 jit_solution(1120561931418289663)
XLA Ops:
  0.0 0.1 pad_add_fusion.where
  0.1 1.2 %copy-done.14 = bf16[2,4096,64]{1,2,0:T(8,128)(2,1)S(1)} copy-done((bf16[2,4096,64]{1,2,0:T(8,128)(2,1)S(1)}, bf16[2,4096,64]{1,2,0:T(8,128)(2,1)}, u32[]{:S(2)}) %copy-start.14) | copy-done | bytes 1048600
  1.3 0.9 copy-done.17
  2.2 0.6 pack.1
  2.9 0.7 copy-done.15
  3.6 3.0 %collective-permute-start = (bf16[2,64,1152]{2,1,0:T(8,128)(2,1)S(1)}, bf16[2,64,1152]{2,1,0:T(8,128)(2,1)S(1)}, u32[]{:S(2)}, u32[]{:S(2)}) collective-permute-start(bf16[2,64,1152]{2,1,0:T(8,128)(2,1)S(1)} %get-tuple-element.7), channel_id=1, source_target_pairs={{0,2},{2,0},{1,3},{3,1},{4,6},{6,4},{5,7},{7,5},{8,10},{10,8},{9,1... | collective-permute-start | bytes 884744 | tf_op jit(solution)/shard_map/ppermute | solution.py:259
  6.5 0.7 copy.11.ids
  7.3 1.9 %copy-done.3 = bf16[384,4096]{1,0:T(8,128)(2,1)S(1)} copy-done((bf16[384,4096]{1,0:T(8,128)(2,1)S(1)}, bf16[384,4096]{1,0:T(8,128)(2,1)}, u32[]{:S(2)}) %copy-start.3) | copy-done | bytes 3145752
  9.2 0.7 copy-done.18
  9.8 1.1 %spread.1.refs_0_ = bf16[4,400,1024]{2,1,0:T(8,128)(2,1)S(1)} custom-call(s32[3]{0:T(128)S(1)} %copy-done.18, s32[3,1]{1,0:T(4,128)S(1)} %copy.11.ids, bf16[384,4096]{1,0:T(8,128)(2,1)S(1)} %copy-done.3), custom_call_target="tpu_custom_call" | custom-call | tf_op jit(solution)/shard_map/spread/pallas_call | solution.py:85
  11.0 1.7 %copy-done.2 = bf16[4,400,1024]{2,1,0:T(8,128)(2,1)} copy-done((bf16[4,400,1024]{2,1,0:T(8,128)(2,1)}, bf16[4,400,1024]{2,1,0:T(8,128)(2,1)S(1)}, u32[]{:S(2)}) %copy-start.2) | copy-done | bytes 3276824
  12.7 0.9 collective-permute-done.refs_1_.refs_0_
  13.6 0.7 copy-done.5
  14.3 4.9 %all-to-all-start = ((bf16[4,400,1024]{2,1,0:T(8,128)(2,1)}), bf16[4,400,1024]{2,1,0:T(8,128)(2,1)}, u32[]{:S(2)}, u32[]{:S(2)}) async-start(bf16[4,400,1024]{2,1,0:T(8,128)(2,1)} %hand.2), calls=%async_computation | async-start | bytes 6553600 | tf_op jit(solution)/shard_map/all_to_all | solution.py:240
  19.2 3.9 %collective-permute-start.1 = (bf16[2,64,1152]{2,1,0:T(8,128)(2,1)}, bf16[2,64,1152]{2,1,0:T(8,128)(2,1)S(1)}, u32[]{:S(2)}, u32[]{:S(2)}) collective-permute-start(bf16[2,64,1152]{2,1,0:T(8,128)(2,1)} %copy-done.15), channel_id=1, source_target_pairs={{0,12},{4,0},{8,4},{12,8},{1,13},{5,1},{9,5},{13,9},{2,14},{6,2},{... | collective-permute-start | bytes 884744 | tf_op jit(solution)/shard_map/ppermute | solution.py:243
  23.1 0.0 collective-permute-start.2
  23.1 7.8 %collective-permute-done.1.refs_2_.refs_1_ = bf16[2,64,1152]{2,1,0:T(8,128)(2,1)S(1)} collective-permute-done((bf16[2,64,1152]{2,1,0:T(8,128)(2,1)}, bf16[2,64,1152]{2,1,0:T(8,128)(2,1)S(1)}, u32[]{:S(2)}, u32[]{:S(2)}) %collective-permute-start.1) | collective-permute-done | bytes 294944 | tf_op jit(solution)/shard_map/ppermute | solution.py:243
  30.9 5.2 %collective-permute-done.2.refs_1_.refs_3_ = bf16[2,64,1152]{2,1,0:T(8,128)(2,1)} collective-permute-done((bf16[2,64,1152]{2,1,0:T(8,128)(2,1)}, bf16[2,64,1152]{2,1,0:T(8,128)(2,1)}, u32[]{:S(2)}, u32[]{:S(2)}) %collective-permute-start.2) | collective-permute-done | bytes 294944 | tf_op jit(solution)/shard_map/ppermute | solution.py:243
  36.0 1.7 %collective-permute-start.4 = (bf16[2,64,1152]{2,1,0:T(8,128)(2,1)}, bf16[2,64,1152]{2,1,0:T(8,128)(2,1)}, u32[]{:S(2)}, u32[]{:S(2)}) collective-permute-start(bf16[2,64,1152]{2,1,0:T(8,128)(2,1)} %hand.3.refs_4_), channel_id=1, source_target_pairs={{0,12},{4,0},{8,4},{12,8},{1,13},{5,1},{9,5},{13,9},{2,14},{6,2},{... | collective-permute-start | bytes 884744 | tf_op jit(solution)/shard_map/ppermute | solution.py:243
  37.8 0.3 collective-permute-start.6
  38.1 7.7 %collective-permute-done.4.refs_1_.refs_5_ = bf16[2,64,1152]{2,1,0:T(8,128)(2,1)} collective-permute-done((bf16[2,64,1152]{2,1,0:T(8,128)(2,1)}, bf16[2,64,1152]{2,1,0:T(8,128)(2,1)}, u32[]{:S(2)}, u32[]{:S(2)}) %collective-permute-start.4) | collective-permute-done | bytes 294944 | tf_op jit(solution)/shard_map/ppermute | solution.py:243
  45.8 4.2 %collective-permute-done.6.refs_0_.refs_7_ = bf16[2,64,1152]{2,1,0:T(8,128)(2,1)S(1)} collective-permute-done((bf16[2,64,1152]{2,1,0:T(8,128)(2,1)}, bf16[2,64,1152]{2,1,0:T(8,128)(2,1)S(1)}, u32[]{:S(2)}, u32[]{:S(2)}) %collective-permute-start.6) | collective-permute-done | bytes 294944 | tf_op jit(solution)/shard_map/ppermute | solution.py:243
  50.0 3.5 %copy-done = bf16[4096,1024]{1,0:T(8,128)(2,1)S(1)} copy-done((bf16[4096,1024]{1,0:T(8,128)(2,1)S(1)}, bf16[4096,1024]{1,0:T(8,128)(2,1)}, u32[]{:S(2)}) %copy-start) | copy-done | bytes 8388632
  53.5 4.6 %base.2.refs_0_ = f32[384,512]{1,0:T(8,128)} custom-call(s32[1]{0:T(128)} %bitcast.6.side, s32[3]{0:T(128)S(1)} %copy-done.19, bf16[384,4096]{1,0:T(8,128)(2,1)S(1)} %copy-done.4, bf16[4096,1024]{1,0:T(8,128)(2,1)S(1)} %copy-done, bf16[2,64,1152]{2,1,0:T(8,128)(2,1)S(1)} %collective-permute-done.6.refs_0_.refs_7_, ...), custom_call_target="tpu_custom_call" | custom-call | flops 1610612736 | bytes 8126464 | tf_op jit(solution)/shard_map/base/pallas_call | solution.py:123
  58.1 0.0 collective-permute-start.7
  58.1 1.6 %collective-permute-start.3 = (bf16[2,64,1152]{2,1,0:T(8,128)(2,1)}, bf16[2,64,1152]{2,1,0:T(8,128)(2,1)S(1)}, u32[]{:S(2)}, u32[]{:S(2)}) collective-permute-start(bf16[2,64,1152]{2,1,0:T(8,128)(2,1)} %collective-permute-done.2.refs_1_.refs_3_), channel_id=1, source_target_pairs={{0,4},{4,8},{8,12},{12,0},{1,5},{5,9},{9,13},{13,1},{2,6},{6,10},{... | collective-permute-start | bytes 884744 | tf_op jit(solution)/shard_map/ppermute | solution.py:243
  59.6 2.3 %collective-permute-start.5 = (bf16[2,64,1152]{2,1,0:T(8,128)(2,1)}, bf16[2,64,1152]{2,1,0:T(8,128)(2,1)}, u32[]{:S(2)}, u32[]{:S(2)}) collective-permute-start(bf16[2,64,1152]{2,1,0:T(8,128)(2,1)} %collective-permute-done.4.refs_1_.refs_5_), channel_id=1, source_target_pairs={{0,12},{4,0},{8,4},{12,8},{1,13},{5,1},{9,5},{13,9},{2,14},{6,2},{... | collective-permute-start | bytes 884744 | tf_op jit(solution)/shard_map/ppermute | solution.py:243
  61.9 0.1 pad_add_fusion.1.here
  62.0 8.0 %collective-permute-done.3.refs_1_.refs_2_ = bf16[2,64,1152]{2,1,0:T(8,128)(2,1)S(1)} collective-permute-done((bf16[2,64,1152]{2,1,0:T(8,128)(2,1)}, bf16[2,64,1152]{2,1,0:T(8,128)(2,1)S(1)}, u32[]{:S(2)}, u32[]{:S(2)}) %collective-permute-start.3) | collective-permute-done | bytes 294944 | tf_op jit(solution)/shard_map/ppermute | solution.py:243
  69.9 0.7 copy-done.9
  70.7 3.4 %copy-done.1 = bf16[4096,1024]{1,0:T(8,128)(2,1)S(1)} copy-done((bf16[4096,1024]{1,0:T(8,128)(2,1)S(1)}, bf16[4096,1024]{1,0:T(8,128)(2,1)}, u32[]{:S(2)}) %copy-start.1) | copy-done | bytes 8388632
  74.0 1.0 copy-done.10
  75.0 3.7 %base.3 = f32[384,512]{1,0:T(8,128)S(1)} custom-call(s32[1]{0:T(128)} %bitcast.5.side, s32[3]{0:T(128)S(1)} %copy-done.19, bf16[384,4096]{1,0:T(8,128)(2,1)S(1)} %copy-done.4, bf16[4096,1024]{1,0:T(8,128)(2,1)S(1)} %copy-done.1, f32[384,512]{1,0:T(8,128)} %base.2.refs_0_, bf16[2,64,1152]{2,1,0:T(8,128)(2,1)S(1)} %copy-done.10), custom_call_target="tpu_custom_call" | custom-call | flops 1610612736 | bytes 8126464 | tf_op jit(solution)/shard_map/base/pallas_call | solution.py:123
  78.7 0.0 collective-permute-done.7
  78.8 1.3 %add.32.refs_8_.base = f32[384,512]{1,0:T(8,128)S(1)} add(f32[384,512]{1,0:T(8,128)S(1)} %base.3, f32[384,512]{1,0:T(8,128)} %collective-permute-done.7) | non-fusion elementwise | flops 196608 | bytes 2359296 | tf_op jit(solution)/shard_map/add | solution.py:272
  80.0 0.0 all-to-all-done.tok_ref
  80.0 0.7 fusion
  80.8 0.1 reshape.12.ids
  80.8 0.0 collective-permute-done.5.refs_6_
  80.9 1.0 copy-done.8
  81.8 1.0 copy-done.11
  82.8 1.0 copy-done.13
  83.7 1.0 copy-done.16
  84.7 5.0 %rank.1 = bf16[4,3,128,128]{3,2,1,0:T(8,128)(2,1)S(1)} custom-call(s32[12]{0:T(128)S(1)} %reshape.12.ids, s32[16]{0:T(128)S(1)} %copy-done.20, s32[2]{0:T(128)S(1)} %pad_add_fusion.1.here, bf16[4,400,1024]{2,1,0:T(8,128)(2,1)} %all-to-all-done.tok_ref, bf16[2,64,1152]{2,1,0:T(8,128)(2,1)S(1)} %copy-done.16, bf16[2,64,1152]{2,1,0:T(8,128)(2,1)S(1)} %copy-done.13, ...), custom_call_target="tpu_custom_call" | custom-call | flops 209715200 | bytes 3276800 | tf_op jit(solution)/shard_map/rank/pallas_call | solution.py:183
  89.7 10.2 %all_to_all.10.mine = bf16[4,3,128,128]{3,2,1,0:T(8,128)(2,1)S(1)} all-to-all(bf16[4,3,128,128]{3,2,1,0:T(8,128)(2,1)S(1)} %rank.1), channel_id=1, replica_groups=mesh['groups'=2,'ring'=4,'pair'=2,'tensor'=2] {'groups','pair'}, dimensions={0} | all-to-all | bytes 786432 | tf_op jit(solution)/shard_map/all_to_all | solution.py:240
  99.9 0.0 collective-permute-start.8
  99.9 1.7 %collective-permute-done.8.theirs = bf16[4,3,128,128]{3,2,1,0:T(8,128)(2,1)S(1)} collective-permute-done((bf16[4,3,128,128]{3,2,1,0:T(8,128)(2,1)S(1)}, bf16[4,3,128,128]{3,2,1,0:T(8,128)(2,1)S(1)}, u32[]{:S(2)}, u32[]{:S(2)}) %collective-permute-start.8) | collective-permute-done | bytes 393248 | tf_op jit(solution)/shard_map/ppermute | solution.py:237
  101.7 1.0 %final.1 = bf16[384,512]{1,0:T(8,128)(2,1)} custom-call(bf16[4,3,128,128]{3,2,1,0:T(8,128)(2,1)S(1)} %all_to_all.10.mine, bf16[4,3,128,128]{3,2,1,0:T(8,128)(2,1)S(1)} %collective-permute-done.8.theirs, f32[384,512]{1,0:T(8,128)S(1)} %add.32.refs_8_.base), custom_call_target="tpu_custom_call" | custom-call | tf_op jit(solution)/shard_map/final/pallas_call | solution.py:218
  (29 shorter events, 0.0 us)
Async XLA Ops:
  0.1 1.2 %copy-start.14 = (bf16[2,4096,64]{1,2,0:T(8,128)(2,1)S(1)}, bf16[2,4096,64]{1,2,0:T(8,128)(2,1)}, u32[]{:S(2)}) copy-start(bf16[2,4096,64]{1,2,0:T(8,128)(2,1)} %param.9) | copy-start | bytes 3145732
  1.3 0.9 copy-start.17
  2.9 0.7 copy-start.15
  3.6 10.0 %collective-permute-start = (bf16[2,64,1152]{2,1,0:T(8,128)(2,1)S(1)}, bf16[2,64,1152]{2,1,0:T(8,128)(2,1)S(1)}, u32[]{:S(2)}, u32[]{:S(2)}) collective-permute-start(bf16[2,64,1152]{2,1,0:T(8,128)(2,1)S(1)} %get-tuple-element.7), channel_id=1, source_target_pairs={{0,2},{2,0},{1,3},{3,1},{4,6},{6,4},{5,7},{7,5},{8,10},{10,8},{9,1... | collective-permute-start | bytes 884744 | tf_op jit(solution)/shard_map/ppermute | solution.py:259
  7.3 1.9 %copy-start.3 = (bf16[384,4096]{1,0:T(8,128)(2,1)S(1)}, bf16[384,4096]{1,0:T(8,128)(2,1)}, u32[]{:S(2)}) copy-start(bf16[384,4096]{1,0:T(8,128)(2,1)} %tok_ref.3) | copy-start | bytes 9437188
  9.2 0.7 copy-start.18
  11.0 1.7 %copy-start.2 = (bf16[4,400,1024]{2,1,0:T(8,128)(2,1)}, bf16[4,400,1024]{2,1,0:T(8,128)(2,1)S(1)}, u32[]{:S(2)}) copy-start(bf16[4,400,1024]{2,1,0:T(8,128)(2,1)S(1)} %spread.1.refs_0_) | copy-start | bytes 9830404
  13.6 0.7 copy-start.5
  14.3 35.7 %copy-start.4 = (bf16[384,4096]{1,0:T(8,128)(2,1)S(1)}, bf16[384,4096]{1,0:T(8,128)(2,1)}, u32[]{:S(2)}) copy-start(bf16[384,4096]{1,0:T(8,128)(2,1)} %tok_ref.3) | copy-start | bytes 9437188
  14.3 35.7 %copy-start.19 = (s32[3]{0:T(128)S(1)}, s32[3]{0:T(128)}, u32[]{:S(2)}) copy-start(s32[3]{0:T(128)} %lengths.5) | copy-start | bytes 40
  14.3 65.8 %all-to-all-start = ((bf16[4,400,1024]{2,1,0:T(8,128)(2,1)}), bf16[4,400,1024]{2,1,0:T(8,128)(2,1)}, u32[]{:S(2)}, u32[]{:S(2)}) async-start(bf16[4,400,1024]{2,1,0:T(8,128)(2,1)} %hand.2), calls=%async_computation | async-start | bytes 6553600 | tf_op jit(solution)/shard_map/all_to_all | solution.py:240
  19.2 11.7 %collective-permute-start.1 = (bf16[2,64,1152]{2,1,0:T(8,128)(2,1)}, bf16[2,64,1152]{2,1,0:T(8,128)(2,1)S(1)}, u32[]{:S(2)}, u32[]{:S(2)}) collective-permute-start(bf16[2,64,1152]{2,1,0:T(8,128)(2,1)} %copy-done.15), channel_id=1, source_target_pairs={{0,12},{4,0},{8,4},{12,8},{1,13},{5,1},{9,5},{13,9},{2,14},{6,2},{... | collective-permute-start | bytes 884744 | tf_op jit(solution)/shard_map/ppermute | solution.py:243
  23.1 12.9 %collective-permute-start.2 = (bf16[2,64,1152]{2,1,0:T(8,128)(2,1)}, bf16[2,64,1152]{2,1,0:T(8,128)(2,1)}, u32[]{:S(2)}, u32[]{:S(2)}) collective-permute-start(bf16[2,64,1152]{2,1,0:T(8,128)(2,1)} %copy-done.15), channel_id=1, source_target_pairs={{0,4},{4,8},{8,12},{12,0},{1,5},{5,9},{9,13},{13,1},{2,6},{6,10},{... | collective-permute-start | bytes 884744 | tf_op jit(solution)/shard_map/ppermute | solution.py:243
  30.9 5.2 %copy-start.12 = (bf16[2,64,1152]{2,1,0:T(8,128)(2,1)}, bf16[2,64,1152]{2,1,0:T(8,128)(2,1)S(1)}, u32[]{:S(2)}) copy-start(bf16[2,64,1152]{2,1,0:T(8,128)(2,1)S(1)} %collective-permute-done.1.refs_2_.refs_1_) | copy-start | bytes 884740
  36.0 9.8 %collective-permute-start.4 = (bf16[2,64,1152]{2,1,0:T(8,128)(2,1)}, bf16[2,64,1152]{2,1,0:T(8,128)(2,1)}, u32[]{:S(2)}, u32[]{:S(2)}) collective-permute-start(bf16[2,64,1152]{2,1,0:T(8,128)(2,1)} %hand.3.refs_4_), channel_id=1, source_target_pairs={{0,12},{4,0},{8,4},{12,8},{1,13},{5,1},{9,5},{13,9},{2,14},{6,2},{... | collective-permute-start | bytes 884744 | tf_op jit(solution)/shard_map/ppermute | solution.py:243
  37.8 12.2 %collective-permute-start.6 = (bf16[2,64,1152]{2,1,0:T(8,128)(2,1)}, bf16[2,64,1152]{2,1,0:T(8,128)(2,1)S(1)}, u32[]{:S(2)}, u32[]{:S(2)}) collective-permute-start(bf16[2,64,1152]{2,1,0:T(8,128)(2,1)} %hand.3.refs_4_), channel_id=1, source_target_pairs={{0,4},{4,8},{8,12},{12,0},{1,5},{5,9},{9,13},{13,1},{2,6},{6,10},{... | collective-permute-start | bytes 884744 | tf_op jit(solution)/shard_map/ppermute | solution.py:243
  50.0 8.1 %copy-start.7 = (bf16[2,64,1152]{2,1,0:T(8,128)(2,1)}, bf16[2,64,1152]{2,1,0:T(8,128)(2,1)S(1)}, u32[]{:S(2)}) copy-start(bf16[2,64,1152]{2,1,0:T(8,128)(2,1)S(1)} %collective-permute-done.6.refs_0_.refs_7_) | copy-start | bytes 884740
  50.0 3.5 %copy-start = (bf16[4096,1024]{1,0:T(8,128)(2,1)S(1)}, bf16[4096,1024]{1,0:T(8,128)(2,1)}, u32[]{:S(2)}) copy-start(bf16[4096,1024]{1,0:T(8,128)(2,1)} %key_ref.3) | copy-start | bytes 25165828
  58.1 20.7 %collective-permute-start.7 = (f32[384,512]{1,0:T(8,128)}, f32[384,512]{1,0:T(8,128)}, u32[]{:S(2)}, u32[]{:S(2)}) collective-permute-start(f32[384,512]{1,0:T(8,128)} %base.2.refs_0_), channel_id=1, source_target_pairs={{0,1},{1,0},{2,3},{3,2},{4,5},{5,4},{6,7},{7,6},{8,9},{9,8},{10,11... | collective-permute-start | bytes 2359304 | tf_op jit(solution)/shard_map/ppermute | solution.py:237
  58.1 11.9 %collective-permute-start.3 = (bf16[2,64,1152]{2,1,0:T(8,128)(2,1)}, bf16[2,64,1152]{2,1,0:T(8,128)(2,1)S(1)}, u32[]{:S(2)}, u32[]{:S(2)}) collective-permute-start(bf16[2,64,1152]{2,1,0:T(8,128)(2,1)} %collective-permute-done.2.refs_1_.refs_3_), channel_id=1, source_target_pairs={{0,4},{4,8},{8,12},{12,0},{1,5},{5,9},{9,13},{13,1},{2,6},{6,10},{... | collective-permute-start | bytes 884744 | tf_op jit(solution)/shard_map/ppermute | solution.py:243
  59.6 21.2 %collective-permute-start.5 = (bf16[2,64,1152]{2,1,0:T(8,128)(2,1)}, bf16[2,64,1152]{2,1,0:T(8,128)(2,1)}, u32[]{:S(2)}, u32[]{:S(2)}) collective-permute-start(bf16[2,64,1152]{2,1,0:T(8,128)(2,1)} %collective-permute-done.4.refs_1_.refs_5_), channel_id=1, source_target_pairs={{0,12},{4,0},{8,4},{12,8},{1,13},{5,1},{9,5},{13,9},{2,14},{6,2},{... | collective-permute-start | bytes 884744 | tf_op jit(solution)/shard_map/ppermute | solution.py:243
  69.9 0.7 copy-start.9
  70.7 3.4 %copy-start.1 = (bf16[4096,1024]{1,0:T(8,128)(2,1)S(1)}, bf16[4096,1024]{1,0:T(8,128)(2,1)}, u32[]{:S(2)}) copy-start(bf16[4096,1024]{1,0:T(8,128)(2,1)} %key_ref.3) | copy-start | bytes 25165828
  74.0 1.0 copy-start.10
  75.0 5.8 %copy-start.6 = (bf16[2,64,1152]{2,1,0:T(8,128)(2,1)S(1)}, bf16[2,64,1152]{2,1,0:T(8,128)(2,1)}, u32[]{:S(2)}) copy-start(bf16[2,64,1152]{2,1,0:T(8,128)(2,1)} %hand.3.refs_4_) | copy-start | bytes 884740
  75.0 5.8 %copy-start.20 = (s32[16]{0:T(128)S(1)}, s32[16]{0:T(128)}, u32[]{:S(2)}) copy-start(s32[16]{0:T(128)} %owner.1) | copy-start | bytes 196
  80.9 1.0 copy-start.8
  81.8 1.0 copy-start.11
  82.8 1.0 copy-start.13
  83.7 1.0 copy-start.16
  99.9 1.7 %collective-permute-start.8 = (bf16[4,3,128,128]{3,2,1,0:T(8,128)(2,1)S(1)}, bf16[4,3,128,128]{3,2,1,0:T(8,128)(2,1)S(1)}, u32[]{:S(2)}, u32[]{:S(2)}) collective-permute-start(bf16[4,3,128,128]{3,2,1,0:T(8,128)(2,1)S(1)} %all_to_all.10.mine), channel_id=1, source_target_pairs={{0,1},{1,0},{2,3},{3,2},{4,5},{5,4},{6,7},{7,6},{8,9},{9,8},{10,11... | collective-permute-start | bytes 1179656 | tf_op jit(solution)/shard_map/ppermute | solution.py:237

commit v5 on v4

--- a/solution.py
+++ b/solution.py
@@ -58,7 +58,6 @@
         out_specs=[VMEM] * ways,
         out_shape=[shape] * ways,
         scratch_shapes=[pltpu.SemaphoreType.DMA((ways, 2))],
-        compiler_params=BIG,
         name="pack",
     )(jnp.stack(share_of).astype(jnp.int32), down, up)
 
@@ -88,7 +87,6 @@
         in_specs=[SMEM, SMEM, pl.BlockSpec((rows, step), lambda i: (0, i))],
         out_specs=pl.BlockSpec((1, rows + 16, step), lambda i: (i, 0, 0)),
         out_shape=jax.ShapeDtypeStruct((shares, rows + 16, step), tokens.dtype),
-        compiler_params=BIG,
         name="spread",
     )(lengths, ids, tokens)
 
@@ -133,7 +131,6 @@
             out_specs=pl.BlockSpec((rows, wide), lambda i, s, n: (0, 0)),
         ),
         out_shape=jax.ShapeDtypeStruct((rows, wide), jnp.float32),
-        compiler_params=BIG,
         cost_estimate=pl.CostEstimate(
             flops=2 * rows * depth * wide, bytes_accessed=2 * depth * (rows + wide) + 4 * rows * wide, transcendentals=0
         ),
@@ -190,7 +187,6 @@
             pltpu.VMEM((len(pieces) * per, rank, wide), tok.dtype),
             pltpu.SemaphoreType.DMA((len(pieces),)),
         ],
-        compiler_params=BIG,
         cost_estimate=pl.CostEstimate(
             flops=2 * tok.size * rank, bytes_accessed=2 * tok.size, transcendentals=0
         ),
@@ -245,11 +241,15 @@
     def first_hops(x):
         return {0: x, ring - 1: along(x, 1), **({1: along(x, -1)} if ring > 2 else {})}
 
-    def more_hops(held, way):
+    def more_hops(held, way, after):
         for k in range(2, ring // 2 + 1):
             if 2 * k < ring or way % 2 == 0:
+                if k == 2:
+                    held[ring - 1] = hand_on(held[ring - 1], after)
                 held[ring - k] = along(held[ring - k + 1], 1)
             if 2 * k < ring or way % 2 == 1:
+                if k == 2:
+                    held[1] = hand_on(held[1], after)
                 held[k] = along(held[k - 1], -1)
         return [held[k] for k in range(ring)]
 
@@ -258,18 +258,15 @@
     swapped = [
         lax.ppermute(packed[pair - w], "pair", [(a, (a - w) % pair) for a in range(pair)]) for w in range(1, pair)
     ]
-    own = first_hops(packed[0])
-    near = [own[k] for k in own if k > 0]
-    others = [first_hops(hand_on(piece, *near)) for piece in swapped]
+    firsts = [first_hops(piece) for piece in [packed[0]] + swapped]
     tok = to_plane(hand_on(slabs, *swapped))
     ids = tok[:, rows, :blocks].astype(jnp.int32).reshape(-1)
 
-    next_near = [held[k] for held in others for k in held if k > 0]
-    base_out = base_half(tokens, base_key, (t + 1) % sides, sides, lengths, *next_near)
-    pieces = [more_hops(held, way) for way, held in enumerate([own] + others)]
+    base_out = base_half(tokens, base_key, (t + 1) % sides, sides, lengths)
     base_in = across(base_out)
-    base_mine = base_half(tokens, base_key, t, sides, lengths, base_out, pieces[0][ring // 2])
+    base_mine = base_half(tokens, base_key, t, sides, lengths, base_out)
     base = base_mine + base_in
+    pieces = [more_hops(held, way, base_out if way == 0 else base_mine) for way, held in enumerate(firsts)]
 
     here = jnp.stack([z, y]).astype(jnp.int32)
     flat = [piece for way in pieces for piece in way]

time: 103 us -> 87.6 us (0.85)
  waiting for transfers between devices: 35.4 us -> 14.8 us
  local copies, waits for them, and re-layouts: 21.1 us -> 4.28 us
  Pallas kernels: 16.1 us -> 27.3 us
  starting transfers between devices: 17.6 us -> 26.2 us
  other arithmetic: 2.14 us -> 3.61 us
    ppermute x6, waiting for transfers between devices: 32.8 us -> 10 us  [along(): lax.ppermute(x, 'ring', [(a, (a + step) % ring) for a in range(ring)])]
    unnamed x43 -> x7, local copies, waits for them, and re-layouts: 21 us -> 3.72 us
    ppermute x6, starting transfers between devices: 9.73 us -> 19.2 us  [along(): lax.ppermute(x, 'ring', [(a, (a + step) % ring) for a in range(ring)])]
    pallas_call x2, Pallas kernels: 8.31 us -> 13.3 us  [base_half(): pl.pallas_call(base_kernel, grid_spec=pltpu.PrefetchScalarGridSpec(num_sc...]
    pallas_call x1, Pallas kernels: 1.12 us -> 4.3 us  [spread(): pl.pallas_call(spread_kernel, grid=(shares,), in_specs=[SMEM, SMEM, pl.Bl...]
    pallas_call x1, Pallas kernels: 0.64 us -> 2.56 us  [pack(): pl.pallas_call(pack_kernel, in_specs=[SMEM, HBM, HBM], out_specs=[VMEM] *...]
    all_to_all x1, waiting for transfers between devices: 0.01 us -> 1.48 us  [to_plane(): return lax.all_to_all(x, PLANE, split_axis=0, concat_axis=0, tiled=True)]
    pallas_call x1, Pallas kernels: 5 us -> 6.16 us  [rank_parts(): pl.pallas_call(functools.partial(rank_kernel, ring, pair), grid=(shares,)...]
  transfers between devices with their start and end apart: 10 -> 10, of which waited for: 7 -> 6; matrix products, arithmetic and copies ran while one was open for 3% -> 6% of each run, Pallas kernels for 9% -> 20%
where the time goes in v5:
time: 87.6 us; the launch traced here: 87 us
  Pallas kernels  27.3 us (31%)
  starting transfers between devices  26.2 us (30%)
  waiting for transfers between devices  14.8 us (17%)
  blocking collectives  10.8 us (12%)
  local copies, waits for them, and re-layouts  4.28 us (5%)
  other arithmetic  3.61 us (4%)
    ppermute x6, starting transfers between devices, along(): lax.ppermute(x, 'ring', [(a, (a + step) % ring) for a in range(ring)])  19.2 us
    pallas_call x2, Pallas kernels, base_half(): pl.pallas_call(base_kernel, grid_spec=pltpu.PrefetchScalarGridSpec(num_sc...  13.3 us
    all_to_all x1, blocking collectives, to_plane(): return lax.all_to_all(x, PLANE, split_axis=0, concat_axis=0, tiled=True)  10.8 us
    ppermute x6, waiting for transfers between devices, along(): lax.ppermute(x, 'ring', [(a, (a + step) % ring) for a in range(ring)])  10 us
    pallas_call x1, Pallas kernels, rank_parts(): pl.pallas_call(functools.partial(rank_kernel, ring, pair), grid=(shares,)...  6.16 us
    pallas_call x1, Pallas kernels, spread(): pl.pallas_call(spread_kernel, grid=(shares,), in_specs=[SMEM, SMEM, pl.Bl...  4.3 us
    all_to_all x1, starting transfers between devices, to_plane(): return lax.all_to_all(x, PLANE, split_axis=0, concat_axis=0, tiled=True)  3.94 us
    unnamed x7, local copies, waits for them, and re-layouts  3.72 us
  transfers between devices with their start and end apart: 10, of which 6 were waited for; matrix products, arithmetic and copies ran while one was open for 6% of the time, Pallas kernels for 20%

profile of v5, /device:TPU:0, one launch (start us, length us, event | category | flops | bytes accessed | tf_op | source)
XLA Modules:
  0.0 87.0 jit_solution(5392319012459270967)
XLA Ops:
  0.0 0.6 pad_add_fusion.where
  0.6 2.6 %pack.1 = (bf16[2,64,1152]{2,1,0:T(8,128)(2,1)}, bf16[2,64,1152]{2,1,0:T(8,128)(2,1)}) custom-call(s32[2]{0:T(128)} %pad_add_fusion.where, bf16[2,64,4096]{2,1,0:T(8,128)(2,1)} %bitcast.7, bf16[2,64,512]{2,1,0:T(8,128)(2,1)} %up.1), custom_call_target="tpu_custom_call" | custom-call | tf_op jit(solution)/shard_map/pack/pallas_call | solution.py:55
  3.2 3.0 %collective-permute-start = (bf16[2,64,1152]{2,1,0:T(8,128)(2,1)}, bf16[2,64,1152]{2,1,0:T(8,128)(2,1)S(1)}, u32[]{:S(2)}, u32[]{:S(2)}) collective-permute-start(bf16[2,64,1152]{2,1,0:T(8,128)(2,1)} %get-tuple-element.7), channel_id=1, source_target_pairs={{0,2},{2,0},{1,3},{3,1},{4,6},{6,4},{5,7},{7,5},{8,10},{10,8},{9,1... | collective-permute-start | bytes 884744 | tf_op jit(solution)/shard_map/ppermute | solution.py:259
  6.2 1.3 %copy.12.ids = s32[3,1]{1,0:T(4,128)} copy(s32[3,1]{0,1:T(1,128)} %param.11) | data formatting | bytes 24 | tf_op args[4]
  7.5 4.3 %spread.1.refs_0_ = bf16[4,400,1024]{2,1,0:T(8,128)(2,1)} custom-call(s32[3]{0:T(128)} %lengths.5, s32[3,1]{1,0:T(4,128)} %copy.12.ids, bf16[384,4096]{1,0:T(8,128)(2,1)} %tok_ref.3), custom_call_target="tpu_custom_call" | custom-call | tf_op jit(solution)/shard_map/spread/pallas_call | solution.py:84
  11.8 1.6 %collective-permute-done.refs_1_.refs_4_ = bf16[2,64,1152]{2,1,0:T(8,128)(2,1)S(1)} collective-permute-done((bf16[2,64,1152]{2,1,0:T(8,128)(2,1)}, bf16[2,64,1152]{2,1,0:T(8,128)(2,1)S(1)}, u32[]{:S(2)}, u32[]{:S(2)}) %collective-permute-start) | collective-permute-done | bytes 294944 | tf_op jit(solution)/shard_map/ppermute | solution.py:259
  13.4 0.0 copy-start.2
  13.4 0.7 copy-done.2
  14.1 3.9 %all-to-all-start = ((bf16[4,400,1024]{2,1,0:T(8,128)(2,1)}), bf16[4,400,1024]{2,1,0:T(8,128)(2,1)S(1)}, u32[]{:S(2)}, u32[]{:S(2)}) async-start(bf16[4,400,1024]{2,1,0:T(8,128)(2,1)} %hand.3), calls=%async_computation | async-start | bytes 6553600 | tf_op jit(solution)/shard_map/all_to_all | solution.py:236
  18.1 6.6 %base.2.refs_1_.refs_0_ = f32[384,512]{1,0:T(8,128)} custom-call(s32[1]{0:T(128)} %bitcast.5.side, s32[3]{0:T(128)} %lengths.5, bf16[384,4096]{1,0:T(8,128)(2,1)} %tok_ref.3, bf16[4096,1024]{1,0:T(8,128)(2,1)} %key_ref.3), custom_call_target="tpu_custom_call" | custom-call | flops 1610612736 | bytes 8126464 | tf_op jit(solution)/shard_map/base/pallas_call | solution.py:121
  24.7 0.0 collective-permute-start.7
  24.7 1.6 %collective-permute-start.2 = (bf16[2,64,1152]{2,1,0:T(8,128)(2,1)}, bf16[2,64,1152]{2,1,0:T(8,128)(2,1)}, u32[]{:S(2)}, u32[]{:S(2)}) collective-permute-start(bf16[2,64,1152]{2,1,0:T(8,128)(2,1)} %get-tuple-element.8.refs_0_), channel_id=1, source_target_pairs={{0,4},{4,8},{8,12},{12,0},{1,5},{5,9},{9,13},{13,1},{2,6},{6,10},{... | collective-permute-start | bytes 884744 | tf_op jit(solution)/shard_map/ppermute | solution.py:239
  26.3 2.2 %collective-permute-start.4 = (bf16[2,64,1152]{2,1,0:T(8,128)(2,1)}, bf16[2,64,1152]{2,1,0:T(8,128)(2,1)}, u32[]{:S(2)}, u32[]{:S(2)}) collective-permute-start(bf16[2,64,1152]{2,1,0:T(8,128)(2,1)} %copy-done.2), channel_id=1, source_target_pairs={{0,12},{4,0},{8,4},{12,8},{1,13},{5,1},{9,5},{13,9},{2,14},{6,2},{... | collective-permute-start | bytes 884744 | tf_op jit(solution)/shard_map/ppermute | solution.py:239
  28.5 1.8 %collective-permute-start.1 = (bf16[2,64,1152]{2,1,0:T(8,128)(2,1)}, bf16[2,64,1152]{2,1,0:T(8,128)(2,1)}, u32[]{:S(2)}, u32[]{:S(2)}) collective-permute-start(bf16[2,64,1152]{2,1,0:T(8,128)(2,1)} %get-tuple-element.8.refs_0_), channel_id=1, source_target_pairs={{0,12},{4,0},{8,4},{12,8},{1,13},{5,1},{9,5},{13,9},{2,14},{6,2},{... | collective-permute-start | bytes 884744 | tf_op jit(solution)/shard_map/ppermute | solution.py:239
  30.3 6.6 %base.3.refs_1_ = f32[384,512]{1,0:T(8,128)} custom-call(s32[1]{0:T(128)} %bitcast.6.side, s32[3]{0:T(128)} %lengths.5, bf16[384,4096]{1,0:T(8,128)(2,1)} %tok_ref.3, bf16[4096,1024]{1,0:T(8,128)(2,1)} %key_ref.3, f32[384,512]{1,0:T(8,128)} %base.2.refs_1_.refs_0_), custom_call_target="tpu_custom_call" | custom-call | flops 1610612736 | bytes 8126464 | tf_op jit(solution)/shard_map/base/pallas_call | solution.py:121
  37.0 0.0 collective-permute-done.2.refs_0_
  37.0 0.2 collective-permute-start.3
  37.2 12.7 %collective-permute-start.6 = (bf16[2,64,1152]{2,1,0:T(8,128)(2,1)}, bf16[2,64,1152]{2,1,0:T(8,128)(2,1)}, u32[]{:S(2)}, u32[]{:S(2)}) collective-permute-start(bf16[2,64,1152]{2,1,0:T(8,128)(2,1)} %copy-done.2), channel_id=1, source_target_pairs={{0,4},{4,8},{8,12},{12,0},{1,5},{5,9},{9,13},{13,1},{2,6},{6,10},{... | collective-permute-start | bytes 884744 | tf_op jit(solution)/shard_map/ppermute | solution.py:239
  49.9 0.0 collective-permute-done.4.refs_0_
  49.9 0.7 collective-permute-start.5
  50.6 0.6 pad_add_fusion.1.here
  51.1 0.0 collective-permute-done.7
  51.2 2.4 %add.32.refs_8_.base = f32[384,512]{1,0:T(8,128)} add(f32[384,512]{1,0:T(8,128)} %base.3.refs_1_, f32[384,512]{1,0:T(8,128)} %collective-permute-done.7) | non-fusion elementwise | flops 196608 | bytes 2359296 | tf_op jit(solution)/shard_map/add | solution.py:268
  53.6 1.5 %all-to-all-done.tok_ref = bf16[4,400,1024]{2,1,0:T(8,128)(2,1)S(1)} async-done(((bf16[4,400,1024]{2,1,0:T(8,128)(2,1)}), bf16[4,400,1024]{2,1,0:T(8,128)(2,1)S(1)}, u32[]{:S(2)}, u32[]{:S(2)}) %all-to-all-start) | async-done | bytes 3276832 | tf_op jit(solution)/shard_map/all_to_all | solution.py:236
  55.0 0.0 copy-start.1
  55.1 1.7 %copy-done.1 = bf16[4,400,1024]{2,1,0:T(8,128)(2,1)} copy-done((bf16[4,400,1024]{2,1,0:T(8,128)(2,1)}, bf16[4,400,1024]{2,1,0:T(8,128)(2,1)S(1)}, u32[]{:S(2)}) %copy-start.1) | copy-done | bytes 3276824
  56.7 0.6 reshape.12.ids
  57.3 0.0 copy-start
  57.3 0.0 collective-permute-done.1.refs_1_
  57.3 1.4 %collective-permute-done.3.refs_2_ = bf16[2,64,1152]{2,1,0:T(8,128)(2,1)} collective-permute-done((bf16[2,64,1152]{2,1,0:T(8,128)(2,1)}, bf16[2,64,1152]{2,1,0:T(8,128)(2,1)}, u32[]{:S(2)}, u32[]{:S(2)}) %collective-permute-start.3) | collective-permute-done | bytes 294944 | tf_op jit(solution)/shard_map/ppermute | solution.py:239
  58.7 6.1 %collective-permute-done.6.refs_7_ = bf16[2,64,1152]{2,1,0:T(8,128)(2,1)} collective-permute-done((bf16[2,64,1152]{2,1,0:T(8,128)(2,1)}, bf16[2,64,1152]{2,1,0:T(8,128)(2,1)}, u32[]{:S(2)}, u32[]{:S(2)}) %collective-permute-start.6) | collective-permute-done | bytes 294944 | tf_op jit(solution)/shard_map/ppermute | solution.py:239
  64.9 2.5 %collective-permute-done.5.refs_6_ = bf16[2,64,1152]{2,1,0:T(8,128)(2,1)} collective-permute-done((bf16[2,64,1152]{2,1,0:T(8,128)(2,1)}, bf16[2,64,1152]{2,1,0:T(8,128)(2,1)}, u32[]{:S(2)}, u32[]{:S(2)}) %collective-permute-start.5) | collective-permute-done | bytes 294944 | tf_op jit(solution)/shard_map/ppermute | solution.py:239
  67.3 6.2 %rank.1 = bf16[4,3,128,128]{3,2,1,0:T(8,128)(2,1)} custom-call(s32[12]{0:T(128)} %reshape.12.ids, s32[16]{0:T(128)} %owner.1, s32[2]{0:T(128)} %pad_add_fusion.1.here, bf16[4,400,1024]{2,1,0:T(8,128)(2,1)} %copy-done.1, bf16[2,64,1152]{2,1,0:T(8,128)(2,1)} %get-tuple-element.8.refs_0_, bf16[2,64,1152]{2,1,0:T(8,128)(2,1)} %collective-permute-done.1.refs_1_, ...), custom_call_target="tpu_custom_call" | custom-call | flops 209715200 | bytes 3276800 | tf_op jit(solution)/shard_map/rank/pallas_call | solution.py:180
  73.5 10.8 %all_to_all.10.mine = bf16[4,3,128,128]{3,2,1,0:T(8,128)(2,1)S(1)} all-to-all(bf16[4,3,128,128]{3,2,1,0:T(8,128)(2,1)} %rank.1), channel_id=1, replica_groups=mesh['groups'=2,'ring'=4,'pair'=2,'tensor'=2] {'groups','pair'}, dimensions={0} | all-to-all | bytes 786432 | tf_op jit(solution)/shard_map/all_to_all | solution.py:236
  84.3 0.0 collective-permute-start.8
  84.3 1.7 %collective-permute-done.8.theirs = bf16[4,3,128,128]{3,2,1,0:T(8,128)(2,1)S(1)} collective-permute-done((bf16[4,3,128,128]{3,2,1,0:T(8,128)(2,1)S(1)}, bf16[4,3,128,128]{3,2,1,0:T(8,128)(2,1)S(1)}, u32[]{:S(2)}, u32[]{:S(2)}) %collective-permute-start.8) | collective-permute-done | bytes 393248 | tf_op jit(solution)/shard_map/ppermute | solution.py:233
  86.0 0.0 copy-done
  86.0 1.0 %final.1 = bf16[384,512]{1,0:T(8,128)(2,1)} custom-call(bf16[4,3,128,128]{3,2,1,0:T(8,128)(2,1)S(1)} %all_to_all.10.mine, bf16[4,3,128,128]{3,2,1,0:T(8,128)(2,1)S(1)} %collective-permute-done.8.theirs, f32[384,512]{1,0:T(8,128)S(1)} %copy-done), custom_call_target="tpu_custom_call" | custom-call | tf_op jit(solution)/shard_map/final/pallas_call | solution.py:214
  (4 shorter events, 0.0 us)
Async XLA Ops:
  3.2 10.2 %collective-permute-start = (bf16[2,64,1152]{2,1,0:T(8,128)(2,1)}, bf16[2,64,1152]{2,1,0:T(8,128)(2,1)S(1)}, u32[]{:S(2)}, u32[]{:S(2)}) collective-permute-start(bf16[2,64,1152]{2,1,0:T(8,128)(2,1)} %get-tuple-element.7), channel_id=1, source_target_pairs={{0,2},{2,0},{1,3},{3,1},{4,6},{6,4},{5,7},{7,5},{8,10},{10,8},{9,1... | collective-permute-start | bytes 884744 | tf_op jit(solution)/shard_map/ppermute | solution.py:259
  13.4 0.7 copy-start.2
  14.1 40.9 %all-to-all-start = ((bf16[4,400,1024]{2,1,0:T(8,128)(2,1)}), bf16[4,400,1024]{2,1,0:T(8,128)(2,1)S(1)}, u32[]{:S(2)}, u32[]{:S(2)}) async-start(bf16[4,400,1024]{2,1,0:T(8,128)(2,1)} %hand.3), calls=%async_computation | async-start | bytes 6553600 | tf_op jit(solution)/shard_map/all_to_all | solution.py:236
  24.7 26.5 %collective-permute-start.7 = (f32[384,512]{1,0:T(8,128)}, f32[384,512]{1,0:T(8,128)}, u32[]{:S(2)}, u32[]{:S(2)}) collective-permute-start(f32[384,512]{1,0:T(8,128)} %base.2.refs_1_.refs_0_), channel_id=1, source_target_pairs={{0,1},{1,0},{2,3},{3,2},{4,5},{5,4},{6,7},{7,6},{8,9},{9,8},{10,11... | collective-permute-start | bytes 2359304 | tf_op jit(solution)/shard_map/ppermute | solution.py:233
  24.7 12.3 %collective-permute-start.2 = (bf16[2,64,1152]{2,1,0:T(8,128)(2,1)}, bf16[2,64,1152]{2,1,0:T(8,128)(2,1)}, u32[]{:S(2)}, u32[]{:S(2)}) collective-permute-start(bf16[2,64,1152]{2,1,0:T(8,128)(2,1)} %get-tuple-element.8.refs_0_), channel_id=1, source_target_pairs={{0,4},{4,8},{8,12},{12,0},{1,5},{5,9},{9,13},{13,1},{2,6},{6,10},{... | collective-permute-start | bytes 884744 | tf_op jit(solution)/shard_map/ppermute | solution.py:239
  26.3 23.6 %collective-permute-start.4 = (bf16[2,64,1152]{2,1,0:T(8,128)(2,1)}, bf16[2,64,1152]{2,1,0:T(8,128)(2,1)}, u32[]{:S(2)}, u32[]{:S(2)}) collective-permute-start(bf16[2,64,1152]{2,1,0:T(8,128)(2,1)} %copy-done.2), channel_id=1, source_target_pairs={{0,12},{4,0},{8,4},{12,8},{1,13},{5,1},{9,5},{13,9},{2,14},{6,2},{... | collective-permute-start | bytes 884744 | tf_op jit(solution)/shard_map/ppermute | solution.py:239
  28.5 28.8 %collective-permute-start.1 = (bf16[2,64,1152]{2,1,0:T(8,128)(2,1)}, bf16[2,64,1152]{2,1,0:T(8,128)(2,1)}, u32[]{:S(2)}, u32[]{:S(2)}) collective-permute-start(bf16[2,64,1152]{2,1,0:T(8,128)(2,1)} %get-tuple-element.8.refs_0_), channel_id=1, source_target_pairs={{0,12},{4,0},{8,4},{12,8},{1,13},{5,1},{9,5},{13,9},{2,14},{6,2},{... | collective-permute-start | bytes 884744 | tf_op jit(solution)/shard_map/ppermute | solution.py:239
  37.0 21.8 %collective-permute-start.3 = (bf16[2,64,1152]{2,1,0:T(8,128)(2,1)}, bf16[2,64,1152]{2,1,0:T(8,128)(2,1)}, u32[]{:S(2)}, u32[]{:S(2)}) collective-permute-start(bf16[2,64,1152]{2,1,0:T(8,128)(2,1)} %hand.4.refs_3_), channel_id=1, source_target_pairs={{0,4},{4,8},{8,12},{12,0},{1,5},{5,9},{9,13},{13,1},{2,6},{6,10},{... | collective-permute-start | bytes 884744 | tf_op jit(solution)/shard_map/ppermute | solution.py:239
  37.2 27.7 %collective-permute-start.6 = (bf16[2,64,1152]{2,1,0:T(8,128)(2,1)}, bf16[2,64,1152]{2,1,0:T(8,128)(2,1)}, u32[]{:S(2)}, u32[]{:S(2)}) collective-permute-start(bf16[2,64,1152]{2,1,0:T(8,128)(2,1)} %copy-done.2), channel_id=1, source_target_pairs={{0,4},{4,8},{8,12},{12,0},{1,5},{5,9},{9,13},{13,1},{2,6},{6,10},{... | collective-permute-start | bytes 884744 | tf_op jit(solution)/shard_map/ppermute | solution.py:239
  49.9 17.4 %collective-permute-start.5 = (bf16[2,64,1152]{2,1,0:T(8,128)(2,1)}, bf16[2,64,1152]{2,1,0:T(8,128)(2,1)}, u32[]{:S(2)}, u32[]{:S(2)}) collective-permute-start(bf16[2,64,1152]{2,1,0:T(8,128)(2,1)} %hand.5.refs_5_), channel_id=1, source_target_pairs={{0,12},{4,0},{8,4},{12,8},{1,13},{5,1},{9,5},{13,9},{2,14},{6,2},{... | collective-permute-start | bytes 884744 | tf_op jit(solution)/shard_map/ppermute | solution.py:239
  55.0 1.7 %copy-start.1 = (bf16[4,400,1024]{2,1,0:T(8,128)(2,1)}, bf16[4,400,1024]{2,1,0:T(8,128)(2,1)S(1)}, u32[]{:S(2)}) copy-start(bf16[4,400,1024]{2,1,0:T(8,128)(2,1)S(1)} %all-to-all-done.tok_ref) | copy-start | bytes 9830404
  57.3 28.7 %copy-start = (f32[384,512]{1,0:T(8,128)S(1)}, f32[384,512]{1,0:T(8,128)}, u32[]{:S(2)}) copy-start(f32[384,512]{1,0:T(8,128)} %add.32.refs_8_.base) | copy-start | bytes 2359300
  84.3 1.7 %collective-permute-start.8 = (bf16[4,3,128,128]{3,2,1,0:T(8,128)(2,1)S(1)}, bf16[4,3,128,128]{3,2,1,0:T(8,128)(2,1)S(1)}, u32[]{:S(2)}, u32[]{:S(2)}) collective-permute-start(bf16[4,3,128,128]{3,2,1,0:T(8,128)(2,1)S(1)} %all_to_all.10.mine), channel_id=1, source_target_pairs={{0,1},{1,0},{2,3},{3,2},{4,5},{5,4},{6,7},{7,6},{8,9},{9,8},{10,11... | collective-permute-start | bytes 1179656 | tf_op jit(solution)/shard_map/ppermute | solution.py:233

commit v6 on v5

--- a/solution.py
+++ b/solution.py
@@ -13,7 +13,7 @@
 SMEM = pl.BlockSpec(memory_space=pltpu.SMEM)
 VMEM = pl.BlockSpec(memory_space=pltpu.VMEM)
 HBM = pl.BlockSpec(memory_space=pltpu.HBM)
-BIG = pltpu.CompilerParams(vmem_limit_bytes=32 * 1024 * 1024)
+BIG = pltpu.CompilerParams(vmem_limit_bytes=55 * 1024 * 1024)
 PLANE = ("groups", "pair")
 WHOLE = ("groups", "ring", "pair")
 
@@ -29,6 +29,7 @@
         out_specs=ANY,
         out_shape=jax.ShapeDtypeStruct(x.shape, x.dtype),
         input_output_aliases={0: 0},
+        compiler_params=BIG,
         name="hand",
     )(x, *after)
 
@@ -58,6 +59,7 @@
         out_specs=[VMEM] * ways,
         out_shape=[shape] * ways,
         scratch_shapes=[pltpu.SemaphoreType.DMA((ways, 2))],
+        compiler_params=BIG,
         name="pack",
     )(jnp.stack(share_of).astype(jnp.int32), down, up)
 
@@ -87,6 +89,7 @@
         in_specs=[SMEM, SMEM, pl.BlockSpec((rows, step), lambda i: (0, i))],
         out_specs=pl.BlockSpec((1, rows + 16, step), lambda i: (i, 0, 0)),
         out_shape=jax.ShapeDtypeStruct((shares, rows + 16, step), tokens.dtype),
+        compiler_params=BIG,
         name="spread",
     )(lengths, ids, tokens)
 
@@ -132,8 +135,9 @@
         ),
         out_shape=jax.ShapeDtypeStruct((rows, wide), jnp.float32),
         cost_estimate=pl.CostEstimate(
-            flops=2 * rows * depth * wide, bytes_accessed=2 * depth * (rows + wide) + 4 * rows * wide, transcendentals=0
+            flops=0, bytes_accessed=0, transcendentals=0
         ),
+        compiler_params=BIG,
         name="base",
     )(side.reshape(1), lengths, tokens, base_key, *after)
 
@@ -190,6 +194,7 @@
         cost_estimate=pl.CostEstimate(
             flops=2 * tok.size * rank, bytes_accessed=2 * tok.size, transcendentals=0
         ),
+        compiler_params=BIG,
         name="rank",
     )(ids, owner, here, tok, *pieces, after)
 

time: 87.6 us -> 89.2 us (1.018)
  Pallas kernels: 27.3 us -> 28.7 us
    ppermute x6, waiting for transfers between devices: 10 us -> 11.6 us  [along(): lax.ppermute(x, 'ring', [(a, (a + step) % ring) for a in range(ring)])]
    pallas_call x1, Pallas kernels: 1.04 us -> 2.42 us  [final(): pl.pallas_call(final_kernel, in_specs=[VMEM, VMEM, VMEM], out_specs=VMEM,...]
    all_to_all x1, waiting for transfers between devices: 1.48 us -> 0.26 us  [to_plane(): return lax.all_to_all(x, PLANE, split_axis=0, concat_axis=0, tiled=True)]
    unnamed x7 -> x11, local copies, waits for them, and re-layouts: 3.72 us -> 3.49 us
where the time goes in v6:
time: 89.2 us; the launch traced here: 88.6 us
  Pallas kernels  28.7 us (32%)
  starting transfers between devices  26 us (29%)
  waiting for transfers between devices  15.3 us (17%)
  blocking collectives  10.8 us (12%)
  local copies, waits for them, and re-layouts  4.15 us (5%)
  other arithmetic  3.6 us (4%)
    ppermute x6, starting transfers between devices, along(): lax.ppermute(x, 'ring', [(a, (a + step) % ring) for a in range(ring)])  19.1 us
    pallas_call x2, Pallas kernels, base_half(): pl.pallas_call(base_kernel, grid_spec=pltpu.PrefetchScalarGridSpec(num_sc...  13.2 us
    ppermute x6, waiting for transfers between devices, along(): lax.ppermute(x, 'ring', [(a, (a + step) % ring) for a in range(ring)])  11.6 us
    all_to_all x1, blocking collectives, to_plane(): return lax.all_to_all(x, PLANE, split_axis=0, concat_axis=0, tiled=True)  10.8 us
    pallas_call x1, Pallas kernels, rank_parts(): pl.pallas_call(functools.partial(rank_kernel, ring, pair), grid=(shares,)...  6.15 us
    pallas_call x1, Pallas kernels, spread(): pl.pallas_call(spread_kernel, grid=(shares,), in_specs=[SMEM, SMEM, pl.Bl...  4.3 us
    all_to_all x1, starting transfers between devices, to_plane(): return lax.all_to_all(x, PLANE, split_axis=0, concat_axis=0, tiled=True)  3.94 us
    unnamed x11, local copies, waits for them, and re-layouts  3.49 us
  transfers between devices with their start and end apart: 10, of which 6 were waited for; matrix products, arithmetic and copies ran while one was open for 6% of the time, Pallas kernels for 20%

profile of v6, /device:TPU:0, one launch (start us, length us, event | category | flops | bytes accessed | tf_op | source)
XLA Modules:
  0.0 88.6 jit_solution(10602228681039082530)
XLA Ops:
  0.0 0.6 pad_add_fusion.where
  0.6 2.6 %pack.1 = (bf16[2,64,1152]{2,1,0:T(8,128)(2,1)}, bf16[2,64,1152]{2,1,0:T(8,128)(2,1)}) custom-call(s32[2]{0:T(128)} %pad_add_fusion.where, bf16[2,64,4096]{2,1,0:T(8,128)(2,1)} %bitcast.7, bf16[2,64,512]{2,1,0:T(8,128)(2,1)} %up.1), custom_call_target="tpu_custom_call" | custom-call | tf_op jit(solution)/shard_map/pack/pallas_call | solution.py:56
  3.2 3.0 %collective-permute-start = (bf16[2,64,1152]{2,1,0:T(8,128)(2,1)}, bf16[2,64,1152]{2,1,0:T(8,128)(2,1)}, u32[]{:S(2)}, u32[]{:S(2)}) collective-permute-start(bf16[2,64,1152]{2,1,0:T(8,128)(2,1)} %get-tuple-element.7), channel_id=1, source_target_pairs={{0,2},{2,0},{1,3},{3,1},{4,6},{6,4},{5,7},{7,5},{8,10},{10,8},{9,1... | collective-permute-start | bytes 884744 | tf_op jit(solution)/shard_map/ppermute | solution.py:264
  6.2 1.3 %copy.12.ids = s32[3,1]{1,0:T(4,128)} copy(s32[3,1]{0,1:T(1,128)} %param.11) | data formatting | bytes 24 | tf_op args[4]
  7.5 4.3 %spread.1.refs_0_ = bf16[4,400,1024]{2,1,0:T(8,128)(2,1)} custom-call(s32[3]{0:T(128)} %lengths.5, s32[3,1]{1,0:T(4,128)} %copy.12.ids, bf16[384,4096]{1,0:T(8,128)(2,1)} %tok_ref.3), custom_call_target="tpu_custom_call" | custom-call | tf_op jit(solution)/shard_map/spread/pallas_call | solution.py:86
  11.8 1.7 %collective-permute-done.refs_1_.refs_4_ = bf16[2,64,1152]{2,1,0:T(8,128)(2,1)} collective-permute-done((bf16[2,64,1152]{2,1,0:T(8,128)(2,1)}, bf16[2,64,1152]{2,1,0:T(8,128)(2,1)}, u32[]{:S(2)}, u32[]{:S(2)}) %collective-permute-start) | collective-permute-done | bytes 294944 | tf_op jit(solution)/shard_map/ppermute | solution.py:264
  13.5 3.9 %all-to-all-start = ((bf16[4,400,1024]{2,1,0:T(8,128)(2,1)}), bf16[4,400,1024]{2,1,0:T(8,128)(2,1)S(1)}, u32[]{:S(2)}, u32[]{:S(2)}) async-start(bf16[4,400,1024]{2,1,0:T(8,128)(2,1)} %hand.3), calls=%async_computation | async-start | bytes 6553600 | tf_op jit(solution)/shard_map/all_to_all | solution.py:241
  17.5 6.6 %base.2.refs_1_.refs_0_ = f32[384,512]{1,0:T(8,128)} custom-call(s32[1]{0:T(128)} %bitcast.5.side, s32[3]{0:T(128)} %lengths.5, bf16[384,4096]{1,0:T(8,128)(2,1)} %tok_ref.3, bf16[4096,1024]{1,0:T(8,128)(2,1)} %key_ref.3), custom_call_target="tpu_custom_call" | custom-call | tf_op jit(solution)/shard_map/base/pallas_call | solution.py:124
  24.1 0.0 collective-permute-start.7
  24.1 1.6 %collective-permute-start.2 = (bf16[2,64,1152]{2,1,0:T(8,128)(2,1)}, bf16[2,64,1152]{2,1,0:T(8,128)(2,1)S(1)}, u32[]{:S(2)}, u32[]{:S(2)}) collective-permute-start(bf16[2,64,1152]{2,1,0:T(8,128)(2,1)} %get-tuple-element.8.refs_0_), channel_id=1, source_target_pairs={{0,4},{4,8},{8,12},{12,0},{1,5},{5,9},{9,13},{13,1},{2,6},{6,10},{... | collective-permute-start | bytes 884744 | tf_op jit(solution)/shard_map/ppermute | solution.py:244
  25.7 2.2 %collective-permute-start.4 = (bf16[2,64,1152]{2,1,0:T(8,128)(2,1)}, bf16[2,64,1152]{2,1,0:T(8,128)(2,1)S(1)}, u32[]{:S(2)}, u32[]{:S(2)}) collective-permute-start(bf16[2,64,1152]{2,1,0:T(8,128)(2,1)} %collective-permute-done.refs_1_.refs_4_), channel_id=1, source_target_pairs={{0,12},{4,0},{8,4},{12,8},{1,13},{5,1},{9,5},{13,9},{2,14},{6,2},{... | collective-permute-start | bytes 884744 | tf_op jit(solution)/shard_map/ppermute | solution.py:244
  27.9 1.8 %collective-permute-start.1 = (bf16[2,64,1152]{2,1,0:T(8,128)(2,1)}, bf16[2,64,1152]{2,1,0:T(8,128)(2,1)}, u32[]{:S(2)}, u32[]{:S(2)}) collective-permute-start(bf16[2,64,1152]{2,1,0:T(8,128)(2,1)} %get-tuple-element.8.refs_0_), channel_id=1, source_target_pairs={{0,12},{4,0},{8,4},{12,8},{1,13},{5,1},{9,5},{13,9},{2,14},{6,2},{... | collective-permute-start | bytes 884744 | tf_op jit(solution)/shard_map/ppermute | solution.py:244
  29.7 6.6 %base.3.refs_1_ = f32[384,512]{1,0:T(8,128)} custom-call(s32[1]{0:T(128)} %bitcast.6.side, s32[3]{0:T(128)} %lengths.5, bf16[384,4096]{1,0:T(8,128)(2,1)} %tok_ref.3, bf16[4096,1024]{1,0:T(8,128)(2,1)} %key_ref.3, f32[384,512]{1,0:T(8,128)} %base.2.refs_1_.refs_0_), custom_call_target="tpu_custom_call" | custom-call | tf_op jit(solution)/shard_map/base/pallas_call | solution.py:124
  36.4 0.0 collective-permute-done.2.refs_0_
  36.4 0.0 copy-start.3
  36.4 0.7 copy-done.3
  37.1 0.2 collective-permute-start.3
  37.3 12.6 %collective-permute-start.6 = (bf16[2,64,1152]{2,1,0:T(8,128)(2,1)}, bf16[2,64,1152]{2,1,0:T(8,128)(2,1)}, u32[]{:S(2)}, u32[]{:S(2)}) collective-permute-start(bf16[2,64,1152]{2,1,0:T(8,128)(2,1)} %collective-permute-done.refs_1_.refs_4_), channel_id=1, source_target_pairs={{0,4},{4,8},{8,12},{12,0},{1,5},{5,9},{9,13},{13,1},{2,6},{6,10},{... | collective-permute-start | bytes 884744 | tf_op jit(solution)/shard_map/ppermute | solution.py:244
  49.9 0.0 collective-permute-done.4.refs_0_
  49.9 0.0 copy-start.2
  49.9 0.7 copy-done.2
  50.6 0.6 collective-permute-start.5
  51.2 0.6 pad_add_fusion.1.here
  51.8 0.0 collective-permute-done.7
  51.8 2.4 %add.32.refs_8_.base = f32[384,512]{1,0:T(8,128)} add(f32[384,512]{1,0:T(8,128)} %base.3.refs_1_, f32[384,512]{1,0:T(8,128)} %collective-permute-done.7) | non-fusion elementwise | flops 196608 | bytes 2359296 | tf_op jit(solution)/shard_map/add | solution.py:273
  54.2 0.3 all-to-all-done.tok_ref
  54.5 0.0 copy-start
  54.5 0.7 reshape.12.ids
  55.1 0.0 collective-permute-done.1.refs_1_
  55.1 3.6 %collective-permute-done.3.refs_2_ = bf16[2,64,1152]{2,1,0:T(8,128)(2,1)} collective-permute-done((bf16[2,64,1152]{2,1,0:T(8,128)(2,1)}, bf16[2,64,1152]{2,1,0:T(8,128)(2,1)}, u32[]{:S(2)}, u32[]{:S(2)}) %collective-permute-start.3) | collective-permute-done | bytes 294944 | tf_op jit(solution)/shard_map/ppermute | solution.py:244
  58.7 5.6 %collective-permute-done.6.refs_7_ = bf16[2,64,1152]{2,1,0:T(8,128)(2,1)} collective-permute-done((bf16[2,64,1152]{2,1,0:T(8,128)(2,1)}, bf16[2,64,1152]{2,1,0:T(8,128)(2,1)}, u32[]{:S(2)}, u32[]{:S(2)}) %collective-permute-start.6) | collective-permute-done | bytes 294944 | tf_op jit(solution)/shard_map/ppermute | solution.py:244
  64.3 2.4 %collective-permute-done.5.refs_6_ = bf16[2,64,1152]{2,1,0:T(8,128)(2,1)} collective-permute-done((bf16[2,64,1152]{2,1,0:T(8,128)(2,1)}, bf16[2,64,1152]{2,1,0:T(8,128)(2,1)}, u32[]{:S(2)}, u32[]{:S(2)}) %collective-permute-start.5) | collective-permute-done | bytes 294944 | tf_op jit(solution)/shard_map/ppermute | solution.py:244
  66.7 0.0 copy-done
  66.7 6.2 %rank.1 = bf16[4,3,128,128]{3,2,1,0:T(8,128)(2,1)} custom-call(s32[12]{0:T(128)} %reshape.12.ids, s32[16]{0:T(128)} %owner.1, s32[2]{0:T(128)} %pad_add_fusion.1.here, bf16[4,400,1024]{2,1,0:T(8,128)(2,1)} %copy-done, bf16[2,64,1152]{2,1,0:T(8,128)(2,1)} %get-tuple-element.8.refs_0_, bf16[2,64,1152]{2,1,0:T(8,128)(2,1)} %collective-permute-done.1.refs_1_, ...), custom_call_target="tpu_custom_call" | custom-call | flops 209715200 | bytes 3276800 | tf_op jit(solution)/shard_map/rank/pallas_call | solution.py:184
  72.9 10.8 %all_to_all.10.mine = bf16[4,3,128,128]{3,2,1,0:T(8,128)(2,1)S(1)} all-to-all(bf16[4,3,128,128]{3,2,1,0:T(8,128)(2,1)} %rank.1), channel_id=1, replica_groups=mesh['groups'=2,'ring'=4,'pair'=2,'tensor'=2] {'groups','pair'}, dimensions={0} | all-to-all | bytes 786432 | tf_op jit(solution)/shard_map/all_to_all | solution.py:241
  83.7 0.0 copy-start.1
  83.7 0.0 collective-permute-start.8
  83.7 1.7 %collective-permute-done.8.theirs = bf16[4,3,128,128]{3,2,1,0:T(8,128)(2,1)S(1)} collective-permute-done((bf16[4,3,128,128]{3,2,1,0:T(8,128)(2,1)S(1)}, bf16[4,3,128,128]{3,2,1,0:T(8,128)(2,1)S(1)}, u32[]{:S(2)}, u32[]{:S(2)}) %collective-permute-start.8) | collective-permute-done | bytes 393248 | tf_op jit(solution)/shard_map/ppermute | solution.py:238
  85.4 0.0 copy-done.1
  85.4 0.0 copy-start.4
  85.4 0.8 copy-done.4
  86.2 2.4 %final.1 = bf16[384,512]{1,0:T(8,128)(2,1)} custom-call(bf16[4,3,128,128]{3,2,1,0:T(8,128)(2,1)} %copy-done.1, bf16[4,3,128,128]{3,2,1,0:T(8,128)(2,1)} %copy-done.4, f32[384,512]{1,0:T(8,128)} %add.32.refs_8_.base), custom_call_target="tpu_custom_call" | custom-call | tf_op jit(solution)/shard_map/final/pallas_call | solution.py:219
  (4 shorter events, 0.0 us)
Async XLA Ops:
  3.2 10.4 %collective-permute-start = (bf16[2,64,1152]{2,1,0:T(8,128)(2,1)}, bf16[2,64,1152]{2,1,0:T(8,128)(2,1)}, u32[]{:S(2)}, u32[]{:S(2)}) collective-permute-start(bf16[2,64,1152]{2,1,0:T(8,128)(2,1)} %get-tuple-element.7), channel_id=1, source_target_pairs={{0,2},{2,0},{1,3},{3,1},{4,6},{6,4},{5,7},{7,5},{8,10},{10,8},{9,1... | collective-permute-start | bytes 884744 | tf_op jit(solution)/shard_map/ppermute | solution.py:264
  13.5 40.9 %all-to-all-start = ((bf16[4,400,1024]{2,1,0:T(8,128)(2,1)}), bf16[4,400,1024]{2,1,0:T(8,128)(2,1)S(1)}, u32[]{:S(2)}, u32[]{:S(2)}) async-start(bf16[4,400,1024]{2,1,0:T(8,128)(2,1)} %hand.3), calls=%async_computation | async-start | bytes 6553600 | tf_op jit(solution)/shard_map/all_to_all | solution.py:241
  24.1 27.7 %collective-permute-start.7 = (f32[384,512]{1,0:T(8,128)}, f32[384,512]{1,0:T(8,128)}, u32[]{:S(2)}, u32[]{:S(2)}) collective-permute-start(f32[384,512]{1,0:T(8,128)} %base.2.refs_1_.refs_0_), channel_id=1, source_target_pairs={{0,1},{1,0},{2,3},{3,2},{4,5},{5,4},{6,7},{7,6},{8,9},{9,8},{10,11... | collective-permute-start | bytes 2359304 | tf_op jit(solution)/shard_map/ppermute | solution.py:238
  24.1 12.3 %collective-permute-start.2 = (bf16[2,64,1152]{2,1,0:T(8,128)(2,1)}, bf16[2,64,1152]{2,1,0:T(8,128)(2,1)S(1)}, u32[]{:S(2)}, u32[]{:S(2)}) collective-permute-start(bf16[2,64,1152]{2,1,0:T(8,128)(2,1)} %get-tuple-element.8.refs_0_), channel_id=1, source_target_pairs={{0,4},{4,8},{8,12},{12,0},{1,5},{5,9},{9,13},{13,1},{2,6},{6,10},{... | collective-permute-start | bytes 884744 | tf_op jit(solution)/shard_map/ppermute | solution.py:244
  25.7 24.2 %collective-permute-start.4 = (bf16[2,64,1152]{2,1,0:T(8,128)(2,1)}, bf16[2,64,1152]{2,1,0:T(8,128)(2,1)S(1)}, u32[]{:S(2)}, u32[]{:S(2)}) collective-permute-start(bf16[2,64,1152]{2,1,0:T(8,128)(2,1)} %collective-permute-done.refs_1_.refs_4_), channel_id=1, source_target_pairs={{0,12},{4,0},{8,4},{12,8},{1,13},{5,1},{9,5},{13,9},{2,14},{6,2},{... | collective-permute-start | bytes 884744 | tf_op jit(solution)/shard_map/ppermute | solution.py:244
  27.9 27.2 %collective-permute-start.1 = (bf16[2,64,1152]{2,1,0:T(8,128)(2,1)}, bf16[2,64,1152]{2,1,0:T(8,128)(2,1)}, u32[]{:S(2)}, u32[]{:S(2)}) collective-permute-start(bf16[2,64,1152]{2,1,0:T(8,128)(2,1)} %get-tuple-element.8.refs_0_), channel_id=1, source_target_pairs={{0,12},{4,0},{8,4},{12,8},{1,13},{5,1},{9,5},{13,9},{2,14},{6,2},{... | collective-permute-start | bytes 884744 | tf_op jit(solution)/shard_map/ppermute | solution.py:244
  36.4 0.7 copy-start.3
  37.1 21.7 %collective-permute-start.3 = (bf16[2,64,1152]{2,1,0:T(8,128)(2,1)}, bf16[2,64,1152]{2,1,0:T(8,128)(2,1)}, u32[]{:S(2)}, u32[]{:S(2)}) collective-permute-start(bf16[2,64,1152]{2,1,0:T(8,128)(2,1)} %hand.4.refs_3_), channel_id=1, source_target_pairs={{0,4},{4,8},{8,12},{12,0},{1,5},{5,9},{9,13},{13,1},{2,6},{6,10},{... | collective-permute-start | bytes 884744 | tf_op jit(solution)/shard_map/ppermute | solution.py:244
  37.3 27.0 %collective-permute-start.6 = (bf16[2,64,1152]{2,1,0:T(8,128)(2,1)}, bf16[2,64,1152]{2,1,0:T(8,128)(2,1)}, u32[]{:S(2)}, u32[]{:S(2)}) collective-permute-start(bf16[2,64,1152]{2,1,0:T(8,128)(2,1)} %collective-permute-done.refs_1_.refs_4_), channel_id=1, source_target_pairs={{0,4},{4,8},{8,12},{12,0},{1,5},{5,9},{9,13},{13,1},{2,6},{6,10},{... | collective-permute-start | bytes 884744 | tf_op jit(solution)/shard_map/ppermute | solution.py:244
  49.9 0.7 copy-start.2
  50.6 16.1 %collective-permute-start.5 = (bf16[2,64,1152]{2,1,0:T(8,128)(2,1)}, bf16[2,64,1152]{2,1,0:T(8,128)(2,1)}, u32[]{:S(2)}, u32[]{:S(2)}) collective-permute-start(bf16[2,64,1152]{2,1,0:T(8,128)(2,1)} %hand.5.refs_5_), channel_id=1, source_target_pairs={{0,12},{4,0},{8,4},{12,8},{1,13},{5,1},{9,5},{13,9},{2,14},{6,2},{... | collective-permute-start | bytes 884744 | tf_op jit(solution)/shard_map/ppermute | solution.py:244
  54.5 12.3 %copy-start = (bf16[4,400,1024]{2,1,0:T(8,128)(2,1)}, bf16[4,400,1024]{2,1,0:T(8,128)(2,1)S(1)}, u32[]{:S(2)}) copy-start(bf16[4,400,1024]{2,1,0:T(8,128)(2,1)S(1)} %all-to-all-done.tok_ref) | copy-start | bytes 9830404
  83.7 1.7 %copy-start.1 = (bf16[4,3,128,128]{3,2,1,0:T(8,128)(2,1)}, bf16[4,3,128,128]{3,2,1,0:T(8,128)(2,1)S(1)}, u32[]{:S(2)}) copy-start(bf16[4,3,128,128]{3,2,1,0:T(8,128)(2,1)S(1)} %all_to_all.10.mine) | copy-start | bytes 1179652
  83.7 1.7 %collective-permute-start.8 = (bf16[4,3,128,128]{3,2,1,0:T(8,128)(2,1)S(1)}, bf16[4,3,128,128]{3,2,1,0:T(8,128)(2,1)S(1)}, u32[]{:S(2)}, u32[]{:S(2)}) collective-permute-start(bf16[4,3,128,128]{3,2,1,0:T(8,128)(2,1)S(1)} %all_to_all.10.mine), channel_id=1, source_target_pairs={{0,1},{1,0},{2,3},{3,2},{4,5},{5,4},{6,7},{7,6},{8,9},{9,8},{10,11... | collective-permute-start | bytes 1179656 | tf_op jit(solution)/shard_map/ppermute | solution.py:238
  85.4 0.8 copy-start.4

commit v7 on v5

--- a/solution.py
+++ b/solution.py
@@ -33,13 +33,14 @@
     )(x, *after)
 
 
-def pack_kernel(where, down, up, *refs):
+def pack_kernel(down, up, *refs):
     outs, sems = refs[:-1], refs[-1]
     feats = outs[0].shape[2] - LANES
     copies = []
     for way, out in enumerate(outs):
-        start = pl.multiple_of(where[way] * feats, LANES)
-        tile = pl.multiple_of(lax.rem(where[way], up.shape[2] // LANES) * LANES, LANES)
+        share = lax.axis_index("groups") * len(outs) + lax.rem(lax.axis_index("pair") + way, len(outs))
+        start = pl.multiple_of(share * feats, LANES)
+        tile = pl.multiple_of(lax.rem(share, up.shape[2] // LANES) * LANES, LANES)
         copies.append(pltpu.make_async_copy(down.at[:, :, pl.ds(start, feats)], out.at[:, :, :feats], sems.at[way, 0]))
         copies.append(pltpu.make_async_copy(up.at[:, :, pl.ds(tile, LANES)], out.at[:, :, feats:], sems.at[way, 1]))
     for copy in copies:
@@ -48,18 +49,17 @@
         copy.wait()
 
 
-def pack(down, up, shares, share_of):
+def pack(down, up, shares, ways):
     adapters, rank, feats = down.shape
-    ways = len(share_of)
     shape = jax.ShapeDtypeStruct((adapters, rank, feats // shares + LANES), down.dtype)
     return pl.pallas_call(
         pack_kernel,
-        in_specs=[SMEM, HBM, HBM],
+        in_specs=[HBM, HBM],
         out_specs=[VMEM] * ways,
         out_shape=[shape] * ways,
         scratch_shapes=[pltpu.SemaphoreType.DMA((ways, 2))],
         name="pack",
-    )(jnp.stack(share_of).astype(jnp.int32), down, up)
+    )(down, up)
 
 
 def spread_kernel(lengths, ids, in_ref, out_ref):
@@ -132,100 +132,115 @@
         ),
         out_shape=jax.ShapeDtypeStruct((rows, wide), jnp.float32),
         cost_estimate=pl.CostEstimate(
-            flops=2 * rows * depth * wide, bytes_accessed=2 * depth * (rows + wide) + 4 * rows * wide, transcendentals=0
+            flops=0, bytes_accessed=0, transcendentals=0
         ),
         name="base",
     )(side.reshape(1), lengths, tokens, base_key, *after)
 
 
-def rank_kernel(ring, pair, ids, owner, here, tok_ref, *refs):
-    pieces = refs[:-4]
-    after, out_ref, held, sems = refs[-4:]
+def mate_at(k, sign, groups, pair):
+    kg, ky = k // pair, k % pair
+    g = lax.rem(lax.axis_index("groups") + sign * kg + groups, groups)
+    y = lax.rem(lax.axis_index("pair") + sign * ky + pair, pair)
+    return g * pair + y
+
+
+def rank_kernel(groups, ring, pair, ids, owner, tok, *refs):
+    shares = groups * pair
+    tok_held, held, tok_sems, sems = refs[-4:]
+    outs = refs[-4 - shares : -4]
+    pieces = refs[: ring * pair]
     per, rank = pieces[0].shape[:2]
-    blocks = out_ref.shape[1]
-    feats = tok_ref.shape[2]
-    block = out_ref.shape[3]
-    mate = pl.program_id(0)
-
-    @pl.when(mate == 0)
-    def _():
-        copies = [
-            pltpu.make_async_copy(piece, held.at[pl.ds(j * per, per)], sems.at[j])
-            for j, piece in enumerate(pieces)
-        ]
-        for copy in copies:
-            copy.start()
-        for copy in copies:
-            copy.wait()
-
-    for b in range(blocks):
-        slot = owner[ids[mate * blocks + b]]
-        chip = slot // per
-        away = lax.rem(chip // pair - here[0] + ring, ring)
-        way = lax.rem(lax.rem(chip, pair) - here[1] + pair, pair)
-        at = (way * ring + away) * per + lax.rem(slot, per)
-        tok = tok_ref[0, b * block : (b + 1) * block, :]
-        part = lax.dot_general(
-            held[at, :, :feats], tok, (((1,), (1,)), ((), ())), preferred_element_type=jnp.float32
-        )
-        out_ref[0, b, :rank, :] = part.astype(out_ref.dtype)
-        out_ref[0, b, rank:, :] = held[at, :, feats:]
-
-
-def rank_parts(ids, owner, here, tok, pieces, ring, pair, blocks, after):
+    blocks, _, block = outs[0].shape
+    feats = tok.shape[2]
+    z, y = lax.axis_index("ring"), lax.axis_index("pair")
+    mates = [mate_at(k, 1, groups, pair) for k in range(shares)]
+    copies = [pltpu.make_async_copy(piece, held.at[pl.ds(j * per, per)], sems.at[j]) for j, piece in enumerate(pieces)]
+    tok_copies = [
+        pltpu.make_async_copy(tok.at[mates[k], : blocks * block, :], tok_held.at[k], tok_sems.at[k])
+        for k in range(shares)
+    ]
+    for copy in copies + tok_copies:
+        copy.start()
+    for copy in copies:
+        copy.wait()
+    for k in range(shares):
+        tok_copies[k].wait()
+        for b in range(blocks):
+            slot = owner[ids[mates[k] * blocks + b]]
+            chip = slot // per
+            away = lax.rem(chip // pair - z + ring, ring)
+            way = lax.rem(lax.rem(chip, pair) - y + pair, pair)
+            at = (way * ring + away) * per + lax.rem(slot, per)
+            part = lax.dot_general(
+                held[at, :, :feats],
+                tok_held[k, b * block : (b + 1) * block, :],
+                (((1,), (1,)), ((), ())),
+                preferred_element_type=jnp.float32,
+            )
+            outs[k][b, :rank, :] = part.astype(outs[k].dtype)
+            outs[k][b, rank:, :] = held[at, :, feats:]
+
+
+def rank_parts(ids, owner, tok, pieces, groups, ring, pair, blocks, after):
     shares, tall, feats = tok.shape
     block = tall // blocks // LANES * LANES
     per, rank, wide = pieces[0].shape
-    shape = (shares, blocks, 2 * rank, block)
-    return pl.pallas_call(
-        functools.partial(rank_kernel, ring, pair),
-        grid=(shares,),
-        in_specs=[SMEM, SMEM, SMEM, pl.BlockSpec((1, tall, feats), lambda i: (i, 0, 0))] + [ANY] * (len(pieces) + 1),
-        out_specs=pl.BlockSpec((1,) + shape[1:], lambda i: (i, 0, 0, 0)),
-        out_shape=jax.ShapeDtypeStruct(shape, tok.dtype),
+    return pl.pallas_call(
+        functools.partial(rank_kernel, groups, ring, pair),
+        in_specs=[SMEM, SMEM, ANY] + [ANY] * (len(pieces) + 1),
+        out_specs=[VMEM] * shares,
+        out_shape=[jax.ShapeDtypeStruct((blocks, 2 * rank, block), tok.dtype)] * shares,
         scratch_shapes=[
+            pltpu.VMEM((shares, blocks * block, feats), tok.dtype),
             pltpu.VMEM((len(pieces) * per, rank, wide), tok.dtype),
+            pltpu.SemaphoreType.DMA((shares,)),
             pltpu.SemaphoreType.DMA((len(pieces),)),
         ],
-        cost_estimate=pl.CostEstimate(
-            flops=2 * tok.size * rank, bytes_accessed=2 * tok.size, transcendentals=0
-        ),
+        compiler_params=BIG,
+        cost_estimate=pl.CostEstimate(flops=2 * tok.size * rank, bytes_accessed=2 * tok.size, transcendentals=0),
         name="rank",
-    )(ids, owner, here, tok, *pieces, after)
-
-
-def final_kernel(mine, theirs, base, out_ref):
-    shares, blocks, tall, block = mine.shape
+    )(ids, owner, tok, *pieces, after)
+
+
+def final_kernel(groups, pair, base, *refs):
+    shares = groups * pair
+    mine, theirs, out_ref, up = refs[:shares], refs[shares : 2 * shares], refs[-2], refs[-1]
+    blocks, tall, block = mine[0].shape
     rank = tall // 2
-    wide = out_ref.shape[1]
+    tiles = out_ref.shape[1] // LANES
     for b in range(blocks):
         here = slice(b * block, (b + 1) * block)
-        total = mine[0, b, :rank, :].astype(jnp.float32) + theirs[0, b, :rank, :].astype(jnp.float32)
-        for s in range(1, shares):
-            total += mine[s, b, :rank, :].astype(jnp.float32) + theirs[s, b, :rank, :].astype(jnp.float32)
-        up = jnp.concatenate([mine[s, b, rank:, :] for s in range(wide // LANES)], axis=1)
+        total = mine[0][b, :rank, :].astype(jnp.float32)
+        for part in mine[1:] + theirs:
+            total += part[b, :rank, :].astype(jnp.float32)
+        for k in range(shares):
+            tile = lax.rem(mate_at(k, -1, groups, pair), tiles)
+            up[b, :, pl.ds(pl.multiple_of(tile * LANES, LANES), LANES)] = mine[k][b, rank:, :]
         delta = lax.dot_general(
-            total.astype(jnp.bfloat16), up, (((0,), (0,)), ((), ())), preferred_element_type=jnp.float32
+            total.astype(jnp.bfloat16), up[b], (((0,), (0,)), ((), ())), preferred_element_type=jnp.float32
         )
         out_ref[here, :] = (base[here, :] + delta).astype(out_ref.dtype)
 
 
-def final(mine, theirs, base, dtype):
-    return pl.pallas_call(
-        final_kernel,
-        in_specs=[VMEM, VMEM, VMEM],
+def final(mine, theirs, base, groups, pair, dtype):
+    blocks, tall, _ = mine[0].shape
+    return pl.pallas_call(
+        functools.partial(final_kernel, groups, pair),
+        in_specs=[VMEM] * (1 + 2 * len(mine)),
         out_specs=VMEM,
         out_shape=jax.ShapeDtypeStruct(base.shape, dtype),
+        scratch_shapes=[pltpu.VMEM((blocks, tall // 2, base.shape[1]), mine[0].dtype)],
         compiler_params=BIG,
         name="final",
-    )(mine, theirs, base)
+    )(base, *mine, *theirs)
 
 
 def body(tokens, base_key, adapter_down, adapter_up, adapter_ids, owner_slot, lengths):
     groups, ring, pair = lax.axis_size("groups"), lax.axis_size("ring"), lax.axis_size("pair")
     sides = lax.axis_size("tensor")
     shares = groups * pair
-    g, z, y, t = (lax.axis_index(name) for name in ("groups", "ring", "pair", "tensor"))
+    t = lax.axis_index("tensor")
     rows = tokens.shape[0]
     blocks = lengths.shape[0]
 
@@ -241,19 +256,26 @@
     def first_hops(x):
         return {0: x, ring - 1: along(x, 1), **({1: along(x, -1)} if ring > 2 else {})}
 
-    def more_hops(held, way, after):
+    def in_plane(x, kg, ky):
+        pairs = []
+        for a in range(groups):
+            for b in range(pair):
+                pairs.append((a * pair + b, (a + kg) % groups * pair + (b + ky) % pair))
+        return lax.ppermute(x, PLANE, pairs)
+
+    def more_hops(held, way, *after):
         for k in range(2, ring // 2 + 1):
             if 2 * k < ring or way % 2 == 0:
                 if k == 2:
-                    held[ring - 1] = hand_on(held[ring - 1], after)
+                    held[ring - 1] = hand_on(held[ring - 1], *after)
                 held[ring - k] = along(held[ring - k + 1], 1)
             if 2 * k < ring or way % 2 == 1:
                 if k == 2:
-                    held[1] = hand_on(held[1], after)
+                    held[1] = hand_on(held[1], *after)
                 held[k] = along(held[k - 1], -1)
         return [held[k] for k in range(ring)]
 
-    packed = pack(jnp.swapaxes(adapter_down, 1, 2), adapter_up, shares, [g * pair + (y + w) % pair for w in range(pair)])
+    packed = pack(jnp.swapaxes(adapter_down, 1, 2), adapter_up, shares, pair)
     slabs = spread(tokens, lengths, adapter_ids, shares)
     swapped = [
         lax.ppermute(packed[pair - w], "pair", [(a, (a - w) % pair) for a in range(pair)]) for w in range(1, pair)
@@ -262,16 +284,20 @@
     tok = to_plane(hand_on(slabs, *swapped))
     ids = tok[:, rows, :blocks].astype(jnp.int32).reshape(-1)
 
-    base_out = base_half(tokens, base_key, (t + 1) % sides, sides, lengths)
+    near = [firsts[0][k] for k in firsts[0] if k > 0]
+    base_out = base_half(tokens, base_key, (t + 1) % sides, sides, lengths, *near)
     base_in = across(base_out)
-    base_mine = base_half(tokens, base_key, t, sides, lengths, base_out)
+    base_mine = base_half(tokens, base_key, t, sides, lengths)
     base = base_mine + base_in
-    pieces = [more_hops(held, way, base_out if way == 0 else base_mine) for way, held in enumerate(firsts)]
-
-    here = jnp.stack([z, y]).astype(jnp.int32)
+    pieces = [
+        more_hops(held, way, base_out, *([held[ring - 1]] if way % 2 and ring > 2 else [])) for way, held in enumerate(firsts)
+    ]
+
     flat = [piece for way in pieces for piece in way]
-    mine = to_plane(rank_parts(ids, owner_slot, here, tok, flat, ring, pair, blocks, base))
-    return final(mine, across(mine), base, tokens.dtype)
+    parts = rank_parts(ids, owner_slot, tok, flat, groups, ring, pair, blocks, base)
+    mine = [parts[0]] + [in_plane(parts[k], k // pair, k % pair) for k in range(1, shares)]
+    theirs = [across(part) for part in mine]
+    return final(mine, theirs, base, groups, pair, tokens.dtype)
 
 
 def solution(mesh):

time: 87.6 us -> 87.3 us (level)
  waiting for transfers between devices: 14.8 us -> 34.9 us
  blocking collectives: 10.8 us -> 0 us
  starting transfers between devices: 26.2 us -> 19.6 us
  Pallas kernels: 27.3 us -> 24.5 us
  other arithmetic: 3.61 us -> 2.45 us
  local copies, waits for them, and re-layouts: 4.28 us -> 5.16 us
    ppermute x6, waiting for transfers between devices: 10 us -> 26.9 us  [along(): lax.ppermute(x, 'ring', [(a, (a + step) % ring) for a in range(ring)])]
    all_to_all x1 -> x0, blocking collectives: 10.8 us -> none  [to_plane(): return lax.all_to_all(x, PLANE, split_axis=0, concat_axis=0, tiled=True)]
    ppermute x6, starting transfers between devices: 19.2 us -> 9.09 us  [along(): lax.ppermute(x, 'ring', [(a, (a + step) % ring) for a in range(ring)])]
    ppermute x0 -> x3, waiting for transfers between devices: none -> 5.14 us  [in_plane(): return lax.ppermute(x, PLANE, pairs)]
    ppermute x0 -> x3, starting transfers between devices: none -> 3.55 us  [in_plane(): return lax.ppermute(x, PLANE, pairs)]
    pallas_call x3, Pallas kernels: 9.76 us -> 6.8 us  [the longest x1 3.86 us: rank_parts(): pl.pallas_call(functools.partial(rank_kernel, groups, ring, pair), in_spe...]
    all_to_all x1, waiting for transfers between devices: 1.48 us -> 0.01 us  [to_plane(): return lax.all_to_all(x, PLANE, split_axis=0, concat_axis=0, tiled=True)]
    unnamed x7 -> x11, local copies, waits for them, and re-layouts: 3.72 us -> 5.08 us
  transfers between devices with their start and end apart: 10 -> 16, of which waited for: 6 -> 10; matrix products, arithmetic and copies ran while one was open for 6% -> 4% of each run, Pallas kernels for 20% -> 20%
where the time goes in v7:
time: 87.3 us; the launch traced here: 86.7 us
  waiting for transfers between devices  34.9 us (40%)
  Pallas kernels  24.5 us (28%)
  starting transfers between devices  19.6 us (22%)
  local copies, waits for them, and re-layouts  5.16 us (6%)
  other arithmetic  2.45 us (3%)
    ppermute x6, waiting for transfers between devices, along(): lax.ppermute(x, 'ring', [(a, (a + step) % ring) for a in range(ring)])  26.9 us
    pallas_call x2, Pallas kernels, base_half(): pl.pallas_call(base_kernel, grid_spec=pltpu.PrefetchScalarGridSpec(num_sc...  13.4 us
    ppermute x6, starting transfers between devices, along(): lax.ppermute(x, 'ring', [(a, (a + step) % ring) for a in range(ring)])  9.09 us
    ppermute x3, waiting for transfers between devices, in_plane(): return lax.ppermute(x, PLANE, pairs)  5.14 us
    unnamed x11, local copies, waits for them, and re-layouts  5.08 us
    pallas_call x1, Pallas kernels, spread(): pl.pallas_call(spread_kernel, grid=(shares,), in_specs=[SMEM, SMEM, pl.Bl...  4.28 us
    all_to_all x1, starting transfers between devices, to_plane(): return lax.all_to_all(x, PLANE, split_axis=0, concat_axis=0, tiled=True)  3.94 us
    pallas_call x1, Pallas kernels, rank_parts(): pl.pallas_call(functools.partial(rank_kernel, groups, ring, pair), in_spe...  3.86 us
  transfers between devices with their start and end apart: 16, of which 10 were waited for; matrix products, arithmetic and copies ran while one was open for 4% of the time, Pallas kernels for 20%

profile of v7, /device:TPU:0, one launch (start us, length us, event | category | flops | bytes accessed | tf_op | source)
XLA Modules:
  0.0 86.7 jit_solution(6643951644952939298)
XLA Ops:
  0.0 1.9 %pack.1 = (bf16[2,64,1152]{2,1,0:T(8,128)(2,1)}, bf16[2,64,1152]{2,1,0:T(8,128)(2,1)}) custom-call(bf16[2,64,4096]{2,1,0:T(8,128)(2,1)} %bitcast.3, bf16[2,64,512]{2,1,0:T(8,128)(2,1)} %up.1), custom_call_target="tpu_custom_call" | custom-call | tf_op jit(solution)/shard_map/pack/pallas_call | solution.py:55
  1.9 3.0 %collective-permute-start.3 = (bf16[2,64,1152]{2,1,0:T(8,128)(2,1)}, bf16[2,64,1152]{2,1,0:T(8,128)(2,1)S(1)}, u32[]{:S(2)}, u32[]{:S(2)}) collective-permute-start(bf16[2,64,1152]{2,1,0:T(8,128)(2,1)} %get-tuple-element.12), channel_id=1, source_target_pairs={{0,2},{2,0},{1,3},{3,1},{4,6},{6,4},{5,7},{7,5},{8,10},{10,8},{9,1... | collective-permute-start | bytes 884744 | tf_op jit(solution)/shard_map/ppermute | solution.py:281
  4.9 1.3 %copy.12.ids = s32[3,1]{1,0:T(4,128)} copy(s32[3,1]{0,1:T(1,128)} %param.11) | data formatting | bytes 24 | tf_op args[4]
  6.2 4.3 %spread.1.refs_0_ = bf16[4,400,1024]{2,1,0:T(8,128)(2,1)} custom-call(s32[3]{0:T(128)} %lengths.5, s32[3,1]{1,0:T(4,128)} %copy.12.ids, bf16[384,4096]{1,0:T(8,128)(2,1)} %in_ref.1), custom_call_target="tpu_custom_call" | custom-call | tf_op jit(solution)/shard_map/spread/pallas_call | solution.py:84
  10.5 1.6 %collective-permute-done.3.refs_1_.refs_4_ = bf16[2,64,1152]{2,1,0:T(8,128)(2,1)S(1)} collective-permute-done((bf16[2,64,1152]{2,1,0:T(8,128)(2,1)}, bf16[2,64,1152]{2,1,0:T(8,128)(2,1)S(1)}, u32[]{:S(2)}, u32[]{:S(2)}) %collective-permute-start.3) | collective-permute-done | bytes 294944 | tf_op jit(solution)/shard_map/ppermute | solution.py:281
  12.2 0.0 copy-start.1
  12.2 0.7 copy-done.1
  12.9 3.9 %all-to-all-start = ((bf16[4,400,1024]{2,1,0:T(8,128)(2,1)}), bf16[4,400,1024]{2,1,0:T(8,128)(2,1)S(1)}, u32[]{:S(2)}, u32[]{:S(2)}) async-start(bf16[4,400,1024]{2,1,0:T(8,128)(2,1)} %hand.3), calls=%async_computation | async-start | bytes 6553600 | tf_op jit(solution)/shard_map/all_to_all | solution.py:251
  16.8 1.6 %collective-permute-start = (bf16[2,64,1152]{2,1,0:T(8,128)(2,1)}, bf16[2,64,1152]{2,1,0:T(8,128)(2,1)}, u32[]{:S(2)}, u32[]{:S(2)}) collective-permute-start(bf16[2,64,1152]{2,1,0:T(8,128)(2,1)} %get-tuple-element.11.refs_0_), channel_id=1, source_target_pairs={{0,4},{4,8},{8,12},{12,0},{1,5},{5,9},{9,13},{13,1},{2,6},{6,10},{... | collective-permute-start | bytes 884744 | tf_op jit(solution)/shard_map/ppermute | solution.py:254
  18.4 2.2 %collective-permute-start.1 = (bf16[2,64,1152]{2,1,0:T(8,128)(2,1)}, bf16[2,64,1152]{2,1,0:T(8,128)(2,1)}, u32[]{:S(2)}, u32[]{:S(2)}) collective-permute-start(bf16[2,64,1152]{2,1,0:T(8,128)(2,1)} %get-tuple-element.11.refs_0_), channel_id=1, source_target_pairs={{0,12},{4,0},{8,4},{12,8},{1,13},{5,1},{9,5},{13,9},{2,14},{6,2},{... | collective-permute-start | bytes 884744 | tf_op jit(solution)/shard_map/ppermute | solution.py:254
  20.6 8.3 %collective-permute-done.refs_0_ = bf16[2,64,1152]{2,1,0:T(8,128)(2,1)} collective-permute-done((bf16[2,64,1152]{2,1,0:T(8,128)(2,1)}, bf16[2,64,1152]{2,1,0:T(8,128)(2,1)}, u32[]{:S(2)}, u32[]{:S(2)}) %collective-permute-start) | collective-permute-done | bytes 294944 | tf_op jit(solution)/shard_map/ppermute | solution.py:254
  28.9 3.8 %collective-permute-done.1.refs_1_ = bf16[2,64,1152]{2,1,0:T(8,128)(2,1)} collective-permute-done((bf16[2,64,1152]{2,1,0:T(8,128)(2,1)}, bf16[2,64,1152]{2,1,0:T(8,128)(2,1)}, u32[]{:S(2)}, u32[]{:S(2)}) %collective-permute-start.1) | collective-permute-done | bytes 294944 | tf_op jit(solution)/shard_map/ppermute | solution.py:254
  32.7 6.6 %base.3.refs_1_ = f32[384,512]{1,0:T(8,128)} custom-call(s32[1]{0:T(128)} %bitcast.1.side, s32[3]{0:T(128)} %lengths.5, bf16[384,4096]{1,0:T(8,128)(2,1)} %in_ref.1, bf16[4096,1024]{1,0:T(8,128)(2,1)} %key_ref.3, bf16[2,64,1152]{2,1,0:T(8,128)(2,1)} %collective-permute-done.refs_0_, bf16[2,64,1152]{2,1,0:T(8,128)(2,1)} %collective-permute-done.1.refs_1_), custom_call_target="tpu_custom_call" | custom-call | tf_op jit(solution)/shard_map/base/pallas_call | solution.py:121
  39.3 0.0 collective-permute-start.2
  39.3 2.3 %collective-permute-start.5 = (bf16[2,64,1152]{2,1,0:T(8,128)(2,1)}, bf16[2,64,1152]{2,1,0:T(8,128)(2,1)}, u32[]{:S(2)}, u32[]{:S(2)}) collective-permute-start(bf16[2,64,1152]{2,1,0:T(8,128)(2,1)} %copy-done.1), channel_id=1, source_target_pairs={{0,12},{4,0},{8,4},{12,8},{1,13},{5,1},{9,5},{13,9},{2,14},{6,2},{... | collective-permute-start | bytes 884744 | tf_op jit(solution)/shard_map/ppermute | solution.py:254
  41.6 0.0 collective-permute-start.6
  41.6 0.9 %collective-permute-start.4 = (bf16[2,64,1152]{2,1,0:T(8,128)(2,1)}, bf16[2,64,1152]{2,1,0:T(8,128)(2,1)}, u32[]{:S(2)}, u32[]{:S(2)}) collective-permute-start(bf16[2,64,1152]{2,1,0:T(8,128)(2,1)} %hand.4.refs_3_), channel_id=1, source_target_pairs={{0,4},{4,8},{8,12},{12,0},{1,5},{5,9},{9,13},{13,1},{2,6},{6,10},{... | collective-permute-start | bytes 884744 | tf_op jit(solution)/shard_map/ppermute | solution.py:254
  42.5 6.8 %collective-permute-done.5.refs_0_ = bf16[2,64,1152]{2,1,0:T(8,128)(2,1)} collective-permute-done((bf16[2,64,1152]{2,1,0:T(8,128)(2,1)}, bf16[2,64,1152]{2,1,0:T(8,128)(2,1)}, u32[]{:S(2)}, u32[]{:S(2)}) %collective-permute-start.5) | collective-permute-done | bytes 294944 | tf_op jit(solution)/shard_map/ppermute | solution.py:254
  49.3 7.2 %collective-permute-done.6.refs_2_.refs_7_ = bf16[2,64,1152]{2,1,0:T(8,128)(2,1)} collective-permute-done((bf16[2,64,1152]{2,1,0:T(8,128)(2,1)}, bf16[2,64,1152]{2,1,0:T(8,128)(2,1)}, u32[]{:S(2)}, u32[]{:S(2)}) %collective-permute-start.6) | collective-permute-done | bytes 294944 | tf_op jit(solution)/shard_map/ppermute | solution.py:254
  56.5 2.1 %collective-permute-start.7 = (bf16[2,64,1152]{2,1,0:T(8,128)(2,1)}, bf16[2,64,1152]{2,1,0:T(8,128)(2,1)}, u32[]{:S(2)}, u32[]{:S(2)}) collective-permute-start(bf16[2,64,1152]{2,1,0:T(8,128)(2,1)} %hand.5.refs_5_), channel_id=1, source_target_pairs={{0,12},{4,0},{8,4},{12,8},{1,13},{5,1},{9,5},{13,9},{2,14},{6,2},{... | collective-permute-start | bytes 884744 | tf_op jit(solution)/shard_map/ppermute | solution.py:254
  58.5 0.0 copy-start.4
  58.5 6.8 %base.2 = f32[384,512]{1,0:T(8,128)} custom-call(s32[1]{0:T(128)} %bitcast.side, s32[3]{0:T(128)} %lengths.5, bf16[384,4096]{1,0:T(8,128)(2,1)} %in_ref.1, bf16[4096,1024]{1,0:T(8,128)(2,1)} %key_ref.3), custom_call_target="tpu_custom_call" | custom-call | tf_op jit(solution)/shard_map/base/pallas_call | solution.py:121
  65.3 0.0 collective-permute-done.2
  65.3 2.4 %add.12.refs_8_.base = f32[384,512]{1,0:T(8,128)} add(f32[384,512]{1,0:T(8,128)} %base.2, f32[384,512]{1,0:T(8,128)} %collective-permute-done.2) | non-fusion elementwise | flops 196608 | bytes 2359296 | tf_op jit(solution)/shard_map/add | solution.py:291
  67.8 0.0 all-to-all-done.tok
  67.8 0.1 reshape.12.ids
  67.9 0.0 collective-permute-done.4.refs_2_
  67.9 0.9 collective-permute-done.7.refs_6_
  68.7 0.0 copy-done.4
  68.7 1.1 %copy-done = f32[384,512]{1,0:T(8,128)S(1)} copy-done((f32[384,512]{1,0:T(8,128)S(1)}, f32[384,512]{1,0:T(8,128)}, u32[]{:S(2)}) %copy-start) | copy-done | bytes 786456
  69.9 1.0 %copy-done.2 = bf16[2,64,1152]{2,1,0:T(8,128)(2,1)S(1)} copy-done((bf16[2,64,1152]{2,1,0:T(8,128)(2,1)S(1)}, bf16[2,64,1152]{2,1,0:T(8,128)(2,1)}, u32[]{:S(2)}) %copy-start.2) | copy-done | bytes 294936
  70.8 1.0 %copy-done.3 = bf16[2,64,1152]{2,1,0:T(8,128)(2,1)S(1)} copy-done((bf16[2,64,1152]{2,1,0:T(8,128)(2,1)S(1)}, bf16[2,64,1152]{2,1,0:T(8,128)(2,1)}, u32[]{:S(2)}) %copy-start.3) | copy-done | bytes 294936
  71.8 3.9 %rank.1 = (bf16[3,128,128]{2,1,0:T(8,128)(2,1)S(1)}, bf16[3,128,128]{2,1,0:T(8,128)(2,1)S(1)}, bf16[3,128,128]{2,1,0:T(8,128)(2,1)S(1)}, bf16[3,128,128]{2,1,0:T(8,128)(2,1)S(1)}) custom-call(s32[12]{0:T(128)S(1)} %reshape.12.ids, s32[16]{0:T(128)S(1)} %copy-done.4, bf16[4,400,1024]{2,1,0:T(8,128)(2,1)S(1)} %all-to-all-done.tok, ...), custom_call_target="tpu_custom_call" | custom-call | flops 209715200 | bytes 3276800 | tf_op jit(solution)/shard_map/rank/pallas_call | solution.py:189
  75.7 1.7 %collective-permute-start.8 = (bf16[3,128,128]{2,1,0:T(8,128)(2,1)S(1)}, bf16[3,128,128]{2,1,0:T(8,128)(2,1)S(1)}, u32[]{:S(2)}, u32[]{:S(2)}) collective-permute-start(bf16[3,128,128]{2,1,0:T(8,128)(2,1)S(1)} %get-tuple-element.14), channel_id=1, source_target_pairs={{0,2},{2,0},{16,18},{18,16},{1,3},{3,1},{17,19},{19,17},{4,6},{6,4... | collective-permute-start | bytes 294920 | tf_op jit(solution)/shard_map/ppermute | solution.py:264
  77.4 1.5 %collective-permute-start.9 = (bf16[3,128,128]{2,1,0:T(8,128)(2,1)S(1)}, bf16[3,128,128]{2,1,0:T(8,128)(2,1)S(1)}, u32[]{:S(2)}, u32[]{:S(2)}) collective-permute-start(bf16[3,128,128]{2,1,0:T(8,128)(2,1)S(1)} %get-tuple-element.15), channel_id=1, source_target_pairs={{0,16},{2,18},{16,0},{18,2},{1,17},{3,19},{17,1},{19,3},{4,20},{6,... | collective-permute-start | bytes 294920 | tf_op jit(solution)/shard_map/ppermute | solution.py:264
  78.8 0.4 collective-permute-start.10
  79.2 0.0 collective-permute-start.11
  79.2 1.2 %collective-permute-done.8.refs_1_ = bf16[3,128,128]{2,1,0:T(8,128)(2,1)S(1)} collective-permute-done((bf16[3,128,128]{2,1,0:T(8,128)(2,1)S(1)}, bf16[3,128,128]{2,1,0:T(8,128)(2,1)S(1)}, u32[]{:S(2)}, u32[]{:S(2)}) %collective-permute-start.8) | collective-permute-done | bytes 98336 | tf_op jit(solution)/shard_map/ppermute | solution.py:264
  80.4 0.0 collective-permute-start.12
  80.4 2.6 %collective-permute-done.9.refs_2_ = bf16[3,128,128]{2,1,0:T(8,128)(2,1)S(1)} collective-permute-done((bf16[3,128,128]{2,1,0:T(8,128)(2,1)S(1)}, bf16[3,128,128]{2,1,0:T(8,128)(2,1)S(1)}, u32[]{:S(2)}, u32[]{:S(2)}) %collective-permute-start.9) | collective-permute-done | bytes 98336 | tf_op jit(solution)/shard_map/ppermute | solution.py:264
  83.0 0.0 collective-permute-start.13
  83.0 1.4 %collective-permute-done.10.refs_3_ = bf16[3,128,128]{2,1,0:T(8,128)(2,1)S(1)} collective-permute-done((bf16[3,128,128]{2,1,0:T(8,128)(2,1)S(1)}, bf16[3,128,128]{2,1,0:T(8,128)(2,1)S(1)}, u32[]{:S(2)}, u32[]{:S(2)}) %collective-permute-start.10) | collective-permute-done | bytes 98336 | tf_op jit(solution)/shard_map/ppermute | solution.py:264
  84.4 0.0 collective-permute-start.14
  84.4 0.0 collective-permute-done.11.refs_4_
  84.4 0.0 collective-permute-done.12.refs_5_
  84.4 0.0 collective-permute-done.13.refs_6_
  84.4 1.3 %collective-permute-done.14.refs_7_ = bf16[3,128,128]{2,1,0:T(8,128)(2,1)S(1)} collective-permute-done((bf16[3,128,128]{2,1,0:T(8,128)(2,1)S(1)}, bf16[3,128,128]{2,1,0:T(8,128)(2,1)S(1)}, u32[]{:S(2)}, u32[]{:S(2)}) %collective-permute-start.14) | collective-permute-done | bytes 98336 | tf_op jit(solution)/shard_map/ppermute | solution.py:248
  85.7 1.0 %final.1 = bf16[384,512]{1,0:T(8,128)(2,1)} custom-call(f32[384,512]{1,0:T(8,128)S(1)} %copy-done, bf16[3,128,128]{2,1,0:T(8,128)(2,1)S(1)} %get-tuple-element.13.refs_0_, bf16[3,128,128]{2,1,0:T(8,128)(2,1)S(1)} %collective-permute-done.8.refs_1_, bf16[3,128,128]{2,1,0:T(8,128)(2,1)S(1)} %collective-permute-done.9.refs_2_, ...), custom_call_target="tpu_custom_call" | custom-call | tf_op jit(solution)/shard_map/final/pallas_call | solution.py:228
  (7 shorter events, 0.0 us)
Async XLA Ops:
  1.9 10.2 %collective-permute-start.3 = (bf16[2,64,1152]{2,1,0:T(8,128)(2,1)}, bf16[2,64,1152]{2,1,0:T(8,128)(2,1)S(1)}, u32[]{:S(2)}, u32[]{:S(2)}) collective-permute-start(bf16[2,64,1152]{2,1,0:T(8,128)(2,1)} %get-tuple-element.12), channel_id=1, source_target_pairs={{0,2},{2,0},{1,3},{3,1},{4,6},{6,4},{5,7},{7,5},{8,10},{10,8},{9,1... | collective-permute-start | bytes 884744 | tf_op jit(solution)/shard_map/ppermute | solution.py:281
  12.2 0.7 copy-start.1
  12.9 54.9 %all-to-all-start = ((bf16[4,400,1024]{2,1,0:T(8,128)(2,1)}), bf16[4,400,1024]{2,1,0:T(8,128)(2,1)S(1)}, u32[]{:S(2)}, u32[]{:S(2)}) async-start(bf16[4,400,1024]{2,1,0:T(8,128)(2,1)} %hand.3), calls=%async_computation | async-start | bytes 6553600 | tf_op jit(solution)/shard_map/all_to_all | solution.py:251
  16.8 12.1 %collective-permute-start = (bf16[2,64,1152]{2,1,0:T(8,128)(2,1)}, bf16[2,64,1152]{2,1,0:T(8,128)(2,1)}, u32[]{:S(2)}, u32[]{:S(2)}) collective-permute-start(bf16[2,64,1152]{2,1,0:T(8,128)(2,1)} %get-tuple-element.11.refs_0_), channel_id=1, source_target_pairs={{0,4},{4,8},{8,12},{12,0},{1,5},{5,9},{9,13},{13,1},{2,6},{6,10},{... | collective-permute-start | bytes 884744 | tf_op jit(solution)/shard_map/ppermute | solution.py:254
  18.4 14.2 %collective-permute-start.1 = (bf16[2,64,1152]{2,1,0:T(8,128)(2,1)}, bf16[2,64,1152]{2,1,0:T(8,128)(2,1)}, u32[]{:S(2)}, u32[]{:S(2)}) collective-permute-start(bf16[2,64,1152]{2,1,0:T(8,128)(2,1)} %get-tuple-element.11.refs_0_), channel_id=1, source_target_pairs={{0,12},{4,0},{8,4},{12,8},{1,13},{5,1},{9,5},{13,9},{2,14},{6,2},{... | collective-permute-start | bytes 884744 | tf_op jit(solution)/shard_map/ppermute | solution.py:254
  39.3 26.0 %collective-permute-start.2 = (f32[384,512]{1,0:T(8,128)}, f32[384,512]{1,0:T(8,128)}, u32[]{:S(2)}, u32[]{:S(2)}) collective-permute-start(f32[384,512]{1,0:T(8,128)} %base.3.refs_1_), channel_id=1, source_target_pairs={{0,1},{1,0},{2,3},{3,2},{4,5},{5,4},{6,7},{7,6},{8,9},{9,8},{10,11... | collective-permute-start | bytes 2359304 | tf_op jit(solution)/shard_map/ppermute | solution.py:248
  39.3 10.0 %collective-permute-start.5 = (bf16[2,64,1152]{2,1,0:T(8,128)(2,1)}, bf16[2,64,1152]{2,1,0:T(8,128)(2,1)}, u32[]{:S(2)}, u32[]{:S(2)}) collective-permute-start(bf16[2,64,1152]{2,1,0:T(8,128)(2,1)} %copy-done.1), channel_id=1, source_target_pairs={{0,12},{4,0},{8,4},{12,8},{1,13},{5,1},{9,5},{13,9},{2,14},{6,2},{... | collective-permute-start | bytes 884744 | tf_op jit(solution)/shard_map/ppermute | solution.py:254
  41.6 14.9 %collective-permute-start.6 = (bf16[2,64,1152]{2,1,0:T(8,128)(2,1)}, bf16[2,64,1152]{2,1,0:T(8,128)(2,1)}, u32[]{:S(2)}, u32[]{:S(2)}) collective-permute-start(bf16[2,64,1152]{2,1,0:T(8,128)(2,1)} %copy-done.1), channel_id=1, source_target_pairs={{0,4},{4,8},{8,12},{12,0},{1,5},{5,9},{9,13},{13,1},{2,6},{6,10},{... | collective-permute-start | bytes 884744 | tf_op jit(solution)/shard_map/ppermute | solution.py:254
  41.6 26.3 %collective-permute-start.4 = (bf16[2,64,1152]{2,1,0:T(8,128)(2,1)}, bf16[2,64,1152]{2,1,0:T(8,128)(2,1)}, u32[]{:S(2)}, u32[]{:S(2)}) collective-permute-start(bf16[2,64,1152]{2,1,0:T(8,128)(2,1)} %hand.4.refs_3_), channel_id=1, source_target_pairs={{0,4},{4,8},{8,12},{12,0},{1,5},{5,9},{9,13},{13,1},{2,6},{6,10},{... | collective-permute-start | bytes 884744 | tf_op jit(solution)/shard_map/ppermute | solution.py:254
  56.5 12.3 %collective-permute-start.7 = (bf16[2,64,1152]{2,1,0:T(8,128)(2,1)}, bf16[2,64,1152]{2,1,0:T(8,128)(2,1)}, u32[]{:S(2)}, u32[]{:S(2)}) collective-permute-start(bf16[2,64,1152]{2,1,0:T(8,128)(2,1)} %hand.5.refs_5_), channel_id=1, source_target_pairs={{0,12},{4,0},{8,4},{12,8},{1,13},{5,1},{9,5},{13,9},{2,14},{6,2},{... | collective-permute-start | bytes 884744 | tf_op jit(solution)/shard_map/ppermute | solution.py:254
  58.5 10.2 %copy-start.4 = (s32[16]{0:T(128)S(1)}, s32[16]{0:T(128)}, u32[]{:S(2)}) copy-start(s32[16]{0:T(128)} %owner.1) | copy-start | bytes 196
  68.7 1.1 %copy-start = (f32[384,512]{1,0:T(8,128)S(1)}, f32[384,512]{1,0:T(8,128)}, u32[]{:S(2)}) copy-start(f32[384,512]{1,0:T(8,128)} %add.12.refs_8_.base) | copy-start | bytes 2359300
  69.9 1.0 %copy-start.2 = (bf16[2,64,1152]{2,1,0:T(8,128)(2,1)S(1)}, bf16[2,64,1152]{2,1,0:T(8,128)(2,1)}, u32[]{:S(2)}) copy-start(bf16[2,64,1152]{2,1,0:T(8,128)(2,1)} %copy-done.1) | copy-start | bytes 884740
  70.8 1.0 %copy-start.3 = (bf16[2,64,1152]{2,1,0:T(8,128)(2,1)S(1)}, bf16[2,64,1152]{2,1,0:T(8,128)(2,1)}, u32[]{:S(2)}) copy-start(bf16[2,64,1152]{2,1,0:T(8,128)(2,1)} %get-tuple-element.11.refs_0_) | copy-start | bytes 884740
  75.7 4.8 %collective-permute-start.8 = (bf16[3,128,128]{2,1,0:T(8,128)(2,1)S(1)}, bf16[3,128,128]{2,1,0:T(8,128)(2,1)S(1)}, u32[]{:S(2)}, u32[]{:S(2)}) collective-permute-start(bf16[3,128,128]{2,1,0:T(8,128)(2,1)S(1)} %get-tuple-element.14), channel_id=1, source_target_pairs={{0,2},{2,0},{16,18},{18,16},{1,3},{3,1},{17,19},{19,17},{4,6},{6,4... | collective-permute-start | bytes 294920 | tf_op jit(solution)/shard_map/ppermute | solution.py:264
  77.4 5.6 %collective-permute-start.9 = (bf16[3,128,128]{2,1,0:T(8,128)(2,1)S(1)}, bf16[3,128,128]{2,1,0:T(8,128)(2,1)S(1)}, u32[]{:S(2)}, u32[]{:S(2)}) collective-permute-start(bf16[3,128,128]{2,1,0:T(8,128)(2,1)S(1)} %get-tuple-element.15), channel_id=1, source_target_pairs={{0,16},{2,18},{16,0},{18,2},{1,17},{3,19},{17,1},{19,3},{4,20},{6,... | collective-permute-start | bytes 294920 | tf_op jit(solution)/shard_map/ppermute | solution.py:264
  78.8 5.5 %collective-permute-start.10 = (bf16[3,128,128]{2,1,0:T(8,128)(2,1)S(1)}, bf16[3,128,128]{2,1,0:T(8,128)(2,1)S(1)}, u32[]{:S(2)}, u32[]{:S(2)}) collective-permute-start(bf16[3,128,128]{2,1,0:T(8,128)(2,1)S(1)} %get-tuple-element.16), channel_id=1, source_target_pairs={{0,18},{2,16},{16,2},{18,0},{1,19},{3,17},{17,3},{19,1},{4,22},{6,... | collective-permute-start | bytes 294920 | tf_op jit(solution)/shard_map/ppermute | solution.py:264
  79.2 5.2 %collective-permute-start.11 = (bf16[3,128,128]{2,1,0:T(8,128)(2,1)S(1)}, bf16[3,128,128]{2,1,0:T(8,128)(2,1)S(1)}, u32[]{:S(2)}, u32[]{:S(2)}) collective-permute-start(bf16[3,128,128]{2,1,0:T(8,128)(2,1)S(1)} %get-tuple-element.13.refs_0_), channel_id=1, source_target_pairs={{0,1},{1,0},{2,3},{3,2},{4,5},{5,4},{6,7},{7,6},{8,9},{9,8},{10,11... | collective-permute-start | bytes 294920 | tf_op jit(solution)/shard_map/ppermute | solution.py:248
  80.4 3.9 %collective-permute-start.12 = (bf16[3,128,128]{2,1,0:T(8,128)(2,1)S(1)}, bf16[3,128,128]{2,1,0:T(8,128)(2,1)S(1)}, u32[]{:S(2)}, u32[]{:S(2)}) collective-permute-start(bf16[3,128,128]{2,1,0:T(8,128)(2,1)S(1)} %collective-permute-done.8.refs_1_), channel_id=1, source_target_pairs={{0,1},{1,0},{2,3},{3,2},{4,5},{5,4},{6,7},{7,6},{8,9},{9,8},{10,11... | collective-permute-start | bytes 294920 | tf_op jit(solution)/shard_map/ppermute | solution.py:248
  83.0 1.4 %collective-permute-start.13 = (bf16[3,128,128]{2,1,0:T(8,128)(2,1)S(1)}, bf16[3,128,128]{2,1,0:T(8,128)(2,1)S(1)}, u32[]{:S(2)}, u32[]{:S(2)}) collective-permute-start(bf16[3,128,128]{2,1,0:T(8,128)(2,1)S(1)} %collective-permute-done.9.refs_2_), channel_id=1, source_target_pairs={{0,1},{1,0},{2,3},{3,2},{4,5},{5,4},{6,7},{7,6},{8,9},{9,8},{10,11... | collective-permute-start | bytes 294920 | tf_op jit(solution)/shard_map/ppermute | solution.py:248
  84.4 1.3 %collective-permute-start.14 = (bf16[3,128,128]{2,1,0:T(8,128)(2,1)S(1)}, bf16[3,128,128]{2,1,0:T(8,128)(2,1)S(1)}, u32[]{:S(2)}, u32[]{:S(2)}) collective-permute-start(bf16[3,128,128]{2,1,0:T(8,128)(2,1)S(1)} %collective-permute-done.10.refs_3_), channel_id=1, source_target_pairs={{0,1},{1,0},{2,3},{3,2},{4,5},{5,4},{6,7},{7,6},{8,9},{9,8},{10,11... | collective-permute-start | bytes 294920 | tf_op jit(solution)/shard_map/ppermute | solution.py:248

commit v8 on v7

--- a/solution.py
+++ b/solution.py
@@ -149,13 +149,16 @@
     shares = groups * pair
     tok_held, held, tok_sems, sems = refs[-4:]
     outs = refs[-4 - shares : -4]
-    pieces = refs[: ring * pair]
-    per, rank = pieces[0].shape[:2]
+    pieces = refs[: len(refs) - 5 - shares]
+    per, rank = owner.shape[0] // (ring * pair), pieces[0].shape[1]
     blocks, _, block = outs[0].shape
     feats = tok.shape[2]
     z, y = lax.axis_index("ring"), lax.axis_index("pair")
     mates = [mate_at(k, 1, groups, pair) for k in range(shares)]
-    copies = [pltpu.make_async_copy(piece, held.at[pl.ds(j * per, per)], sems.at[j]) for j, piece in enumerate(pieces)]
+    copies, start = [], 0
+    for j, piece in enumerate(pieces):
+        copies.append(pltpu.make_async_copy(piece, held.at[pl.ds(start, piece.shape[0])], sems.at[j]))
+        start += piece.shape[0]
     tok_copies = [
         pltpu.make_async_copy(tok.at[mates[k], : blocks * block, :], tok_held.at[k], tok_sems.at[k])
         for k in range(shares)
@@ -171,7 +174,7 @@
             chip = slot // per
             away = lax.rem(chip // pair - z + ring, ring)
             way = lax.rem(lax.rem(chip, pair) - y + pair, pair)
-            at = (way * ring + away) * per + lax.rem(slot, per)
+            at = (away * pair + way) * per + lax.rem(slot, per)
             part = lax.dot_general(
                 held[at, :, :feats],
                 tok_held[k, b * block : (b + 1) * block, :],
@@ -185,7 +188,7 @@
 def rank_parts(ids, owner, tok, pieces, groups, ring, pair, blocks, after):
     shares, tall, feats = tok.shape
     block = tall // blocks // LANES * LANES
-    per, rank, wide = pieces[0].shape
+    _, rank, wide = pieces[0].shape
     return pl.pallas_call(
         functools.partial(rank_kernel, groups, ring, pair),
         in_specs=[SMEM, SMEM, ANY] + [ANY] * (len(pieces) + 1),
@@ -193,11 +196,10 @@
         out_shape=[jax.ShapeDtypeStruct((blocks, 2 * rank, block), tok.dtype)] * shares,
         scratch_shapes=[
             pltpu.VMEM((shares, blocks * block, feats), tok.dtype),
-            pltpu.VMEM((len(pieces) * per, rank, wide), tok.dtype),
+            pltpu.VMEM((owner.shape[0], rank, wide), tok.dtype),
             pltpu.SemaphoreType.DMA((shares,)),
             pltpu.SemaphoreType.DMA((len(pieces),)),
         ],
-        compiler_params=BIG,
         cost_estimate=pl.CostEstimate(flops=2 * tok.size * rank, bytes_accessed=2 * tok.size, transcendentals=0),
         name="rank",
     )(ids, owner, tok, *pieces, after)
@@ -253,9 +255,6 @@
     def along(x, step):
         return lax.ppermute(x, "ring", [(a, (a + step) % ring) for a in range(ring)])
 
-    def first_hops(x):
-        return {0: x, ring - 1: along(x, 1), **({1: along(x, -1)} if ring > 2 else {})}
-
     def in_plane(x, kg, ky):
         pairs = []
         for a in range(groups):
@@ -263,38 +262,36 @@
                 pairs.append((a * pair + b, (a + kg) % groups * pair + (b + ky) % pair))
         return lax.ppermute(x, PLANE, pairs)
 
-    def more_hops(held, way, *after):
-        for k in range(2, ring // 2 + 1):
-            if 2 * k < ring or way % 2 == 0:
-                if k == 2:
-                    held[ring - 1] = hand_on(held[ring - 1], *after)
-                held[ring - k] = along(held[ring - k + 1], 1)
-            if 2 * k < ring or way % 2 == 1:
-                if k == 2:
-                    held[1] = hand_on(held[1], *after)
-                held[k] = along(held[k - 1], -1)
-        return [held[k] for k in range(ring)]
-
     packed = pack(jnp.swapaxes(adapter_down, 1, 2), adapter_up, shares, pair)
     slabs = spread(tokens, lengths, adapter_ids, shares)
     swapped = [
         lax.ppermute(packed[pair - w], "pair", [(a, (a - w) % pair) for a in range(pair)]) for w in range(1, pair)
     ]
-    firsts = [first_hops(piece) for piece in [packed[0]] + swapped]
+    held = {0: jnp.concatenate([packed[0]] + swapped)}
     tok = to_plane(hand_on(slabs, *swapped))
     ids = tok[:, rows, :blocks].astype(jnp.int32).reshape(-1)
-
-    near = [firsts[0][k] for k in firsts[0] if k > 0]
-    base_out = base_half(tokens, base_key, (t + 1) % sides, sides, lengths, *near)
+    held[ring - 1] = along(held[0], 1)
+    if ring > 2:
+        held[1] = along(held[0], -1)
+
+    base_out = base_half(tokens, base_key, (t + 1) % sides, sides, lengths, *swapped)
     base_in = across(base_out)
-    base_mine = base_half(tokens, base_key, t, sides, lengths)
+    base_mine = base_half(tokens, base_key, t, sides, lengths, *swapped)
     base = base_mine + base_in
-    pieces = [
-        more_hops(held, way, base_out, *([held[ring - 1]] if way % 2 and ring > 2 else [])) for way, held in enumerate(firsts)
-    ]
-
-    flat = [piece for way in pieces for piece in way]
-    parts = rank_parts(ids, owner_slot, tok, flat, groups, ring, pair, blocks, base)
+
+    for k in range(2, ring // 2 + 1):
+        if k == 2:
+            held[ring - 1] = hand_on(held[ring - 1], base_out, base_mine, held[1])
+            held[1] = hand_on(held[1], base_out, base_mine, held[ring - 1])
+        if 2 * k < ring:
+            held[ring - k] = along(held[ring - k + 1], 1)
+            held[k] = along(held[k - 1], -1)
+        else:
+            half = held[0].shape[0] // 2
+            one = along(lax.slice_in_dim(held[k + 1], 0, half), 1)
+            two = along(lax.slice_in_dim(held[k - 1], half, 2 * half), -1)
+    pieces = [held[k] for k in range(ring // 2)] + [one, two] + [held[k] for k in range(ring // 2 + 1, ring)]
+    parts = rank_parts(ids, owner_slot, tok, pieces, groups, ring, pair, blocks, base)
     mine = [parts[0]] + [in_plane(parts[k], k // pair, k % pair) for k in range(1, shares)]
     theirs = [across(part) for part in mine]
     return final(mine, theirs, base, groups, pair, tokens.dtype)

time: 87.3 us -> 92.8 us (1.063)
  waiting for transfers between devices: 34.9 us -> 38.2 us
  local copies, waits for them, and re-layouts: 5.16 us -> 7.08 us
  Pallas kernels: 24.5 us -> 25.8 us
    ppermute x6 -> x4, waiting for transfers between devices: 26.9 us -> 29.7 us  [along(): lax.ppermute(x, 'ring', [(a, (a + step) % ring) for a in range(ring)])]
    slice x0 -> x2, local copies, waits for them, and re-layouts: none -> 1.97 us  [the longest x1 0.98 us: body(): two = along(lax.slice_in_dim(held[k - 1], half, 2 * half), -1)]
    add x1, other arithmetic: 2.43 us -> 1.02 us  [body(): base = base_mine + base_in]
    pallas_call x1, Pallas kernels: 3.86 us -> 5.17 us  [rank_parts(): pl.pallas_call(functools.partial(rank_kernel, groups, ring, pair), in_spe...]
    ppermute x6 -> x4, starting transfers between devices: 9.09 us -> 7.81 us  [along(): lax.ppermute(x, 'ring', [(a, (a + step) % ring) for a in range(ring)])]
    unnamed x11 -> x24, local copies, waits for them, and re-layouts: 5.08 us -> 4.52 us
  transfers between devices with their start and end apart: 16 -> 14, of which waited for: 10 -> 9; matrix products, arithmetic and copies ran while one was open for 4% -> 6% of each run, Pallas kernels for 20% -> 19%
where the time goes in v8:
time: 92.8 us; the launch traced here: 92.2 us
  waiting for transfers between devices  38.2 us (41%)
  Pallas kernels  25.8 us (28%)
  starting transfers between devices  19.2 us (21%)
  local copies, waits for them, and re-layouts  7.08 us (8%)
  other arithmetic  1.81 us (2%)
    ppermute x4, waiting for transfers between devices, along(): lax.ppermute(x, 'ring', [(a, (a + step) % ring) for a in range(ring)])  29.7 us
    pallas_call x2, Pallas kernels, base_half(): pl.pallas_call(base_kernel, grid_spec=pltpu.PrefetchScalarGridSpec(num_sc...  13.4 us
    ppermute x4, starting transfers between devices, along(): lax.ppermute(x, 'ring', [(a, (a + step) % ring) for a in range(ring)])  7.81 us
    ppermute x3, waiting for transfers between devices, in_plane(): return lax.ppermute(x, PLANE, pairs)  5.64 us
    pallas_call x1, Pallas kernels, rank_parts(): pl.pallas_call(functools.partial(rank_kernel, groups, ring, pair), in_spe...  5.17 us
    all_to_all x1, starting transfers between devices, to_plane(): return lax.all_to_all(x, PLANE, split_axis=0, concat_axis=0, tiled=True)  4.8 us
    unnamed x24, local copies, waits for them, and re-layouts  4.52 us
    pallas_call x1, Pallas kernels, spread(): pl.pallas_call(spread_kernel, grid=(shares,), in_specs=[SMEM, SMEM, pl.Bl...  4.3 us
  transfers between devices with their start and end apart: 14, of which 9 were waited for; matrix products, arithmetic and copies ran while one was open for 6% of the time, Pallas kernels for 19%

profile of v8, /device:TPU:0, one launch (start us, length us, event | category | flops | bytes accessed | tf_op | source)
XLA Modules:
  0.0 92.2 jit_solution(654790648700881313)
XLA Ops:
  0.0 1.9 %pack.1 = (bf16[2,64,1152]{2,1,0:T(8,128)(2,1)}, bf16[2,64,1152]{2,1,0:T(8,128)(2,1)}) custom-call(bf16[2,64,4096]{2,1,0:T(8,128)(2,1)} %bitcast.3, bf16[2,64,512]{2,1,0:T(8,128)(2,1)} %up.1), custom_call_target="tpu_custom_call" | custom-call | tf_op jit(solution)/shard_map/pack/pallas_call | solution.py:55
  1.9 3.0 %collective-permute-start = (bf16[2,64,1152]{2,1,0:T(8,128)(2,1)}, bf16[2,64,1152]{2,1,0:T(8,128)(2,1)S(1)}, u32[]{:S(2)}, u32[]{:S(2)}) collective-permute-start(bf16[2,64,1152]{2,1,0:T(8,128)(2,1)} %get-tuple-element.11), channel_id=1, source_target_pairs={{0,2},{2,0},{1,3},{3,1},{4,6},{6,4},{5,7},{7,5},{8,10},{10,8},{9,1... | collective-permute-start | bytes 884744 | tf_op jit(solution)/shard_map/ppermute | solution.py:268
  4.9 1.3 %copy.12.ids = s32[3,1]{1,0:T(4,128)} copy(s32[3,1]{0,1:T(1,128)} %param.11) | data formatting | bytes 24 | tf_op args[4]
  6.2 4.3 %spread.1.refs_0_ = bf16[4,400,1024]{2,1,0:T(8,128)(2,1)} custom-call(s32[3]{0:T(128)} %lengths.5, s32[3,1]{1,0:T(4,128)} %copy.12.ids, bf16[384,4096]{1,0:T(8,128)(2,1)} %in_ref.1), custom_call_target="tpu_custom_call" | custom-call | tf_op jit(solution)/shard_map/spread/pallas_call | solution.py:84
  10.5 1.6 %collective-permute-done.refs_0_.refs_1_ = bf16[2,64,1152]{2,1,0:T(8,128)(2,1)S(1)} collective-permute-done((bf16[2,64,1152]{2,1,0:T(8,128)(2,1)}, bf16[2,64,1152]{2,1,0:T(8,128)(2,1)S(1)}, u32[]{:S(2)}, u32[]{:S(2)}) %collective-permute-start) | collective-permute-done | bytes 294944 | tf_op jit(solution)/shard_map/ppermute | solution.py:268
  12.1 0.7 copy-done.5
  12.9 4.8 %all-to-all-start = ((bf16[4,400,1024]{2,1,0:T(8,128)(2,1)}), bf16[4,400,1024]{2,1,0:T(8,128)(2,1)}, u32[]{:S(2)}, u32[]{:S(2)}) async-start(bf16[4,400,1024]{2,1,0:T(8,128)(2,1)} %hand.3), calls=%async_computation | async-start | bytes 6553600 | tf_op jit(solution)/shard_map/all_to_all | solution.py:253
  17.7 0.0 copy-done.8
  17.8 6.7 %base.3.refs_1_ = f32[384,512]{1,0:T(8,128)} custom-call(s32[1]{0:T(128)} %bitcast.2.side, s32[3]{0:T(128)} %lengths.5, bf16[384,4096]{1,0:T(8,128)(2,1)} %in_ref.1, bf16[4096,1024]{1,0:T(8,128)(2,1)} %key_ref.3, bf16[2,64,1152]{2,1,0:T(8,128)(2,1)} %copy-done.5), custom_call_target="tpu_custom_call" | custom-call | tf_op jit(solution)/shard_map/base/pallas_call | solution.py:121
  24.5 0.0 collective-permute-start.1
  24.5 0.0 copy-done.6
  24.6 3.9 %collective-permute-start.2 = (bf16[4,64,1152]{2,1,0:T(8,128)(2,1)S(1)}, bf16[4,64,1152]{2,1,0:T(8,128)(2,1)S(1)}, u32[]{:S(2)}, u32[]{:S(2)}) collective-permute-start(bf16[4,64,1152]{2,1,0:T(8,128)(2,1)S(1)} %constant_dynamic-update-slice_fusion.refs_0_), channel_id=1, source_target_pairs={{0,12},{4,0},{8,4},{12,8},{1,13},{5,1},{9,5},{13,9},{2,14},{6,2},{... | collective-permute-start | bytes 1769480 | tf_op jit(solution)/shard_map/ppermute | solution.py:256
  28.4 0.0 collective-permute-start.3
  28.4 6.7 %base.2.refs_2_ = f32[384,512]{1,0:T(8,128)} custom-call(s32[1]{0:T(128)} %bitcast.side, s32[3]{0:T(128)} %lengths.5, bf16[384,4096]{1,0:T(8,128)(2,1)} %in_ref.1, bf16[4096,1024]{1,0:T(8,128)(2,1)} %key_ref.3, bf16[2,64,1152]{2,1,0:T(8,128)(2,1)} %copy-done.5), custom_call_target="tpu_custom_call" | custom-call | tf_op jit(solution)/shard_map/base/pallas_call | solution.py:121
  35.1 0.0 copy-done.7
  35.1 7.0 %collective-permute-done.2.refs_3_.refs_0_ = bf16[4,64,1152]{2,1,0:T(8,128)(2,1)S(1)} collective-permute-done((bf16[4,64,1152]{2,1,0:T(8,128)(2,1)S(1)}, bf16[4,64,1152]{2,1,0:T(8,128)(2,1)S(1)}, u32[]{:S(2)}, u32[]{:S(2)}) %collective-permute-start.2) | collective-permute-done | bytes 589856 | tf_op jit(solution)/shard_map/ppermute | solution.py:256
  42.1 13.1 %collective-permute-done.3.refs_0_ = bf16[4,64,1152]{2,1,0:T(8,128)(2,1)S(1)} collective-permute-done((bf16[4,64,1152]{2,1,0:T(8,128)(2,1)S(1)}, bf16[4,64,1152]{2,1,0:T(8,128)(2,1)S(1)}, u32[]{:S(2)}, u32[]{:S(2)}) %collective-permute-start.3) | collective-permute-done | bytes 589856 | tf_op jit(solution)/shard_map/ppermute | solution.py:256
  55.2 0.0 copy-done.3
  55.2 0.8 copy-done.4
  56.1 1.0 %slice.13 = bf16[2,64,1152]{2,1,0:T(8,128)(2,1)S(1)} slice(bf16[4,64,1152]{2,1,0:T(8,128)(2,1)} %hand.4.refs_3_.refs_4_), slice={[0:2], [0:64], [0:1152]} | slice | bytes 589824 | tf_op jit(solution)/shard_map/slice | solution.py:291
  57.0 1.7 %collective-permute-start.4 = (bf16[2,64,1152]{2,1,0:T(8,128)(2,1)S(1)}, bf16[2,64,1152]{2,1,0:T(8,128)(2,1)S(1)}, u32[]{:S(2)}, u32[]{:S(2)}) collective-permute-start(bf16[2,64,1152]{2,1,0:T(8,128)(2,1)S(1)} %slice.13), channel_id=1, source_target_pairs={{0,4},{4,8},{8,12},{12,0},{1,5},{5,9},{9,13},{13,1},{2,6},{6,10},{... | collective-permute-start | bytes 884744 | tf_op jit(solution)/shard_map/ppermute | solution.py:256
  58.7 1.0 %slice.14 = bf16[2,64,1152]{2,1,0:T(8,128)(2,1)S(1)} slice(bf16[4,64,1152]{2,1,0:T(8,128)(2,1)} %hand.5.refs_1_), slice={[2:4], [0:64], [0:1152]} | slice | bytes 589824 | tf_op jit(solution)/shard_map/slice | solution.py:292
  59.7 2.3 %collective-permute-start.5 = (bf16[2,64,1152]{2,1,0:T(8,128)(2,1)S(1)}, bf16[2,64,1152]{2,1,0:T(8,128)(2,1)S(1)}, u32[]{:S(2)}, u32[]{:S(2)}) collective-permute-start(bf16[2,64,1152]{2,1,0:T(8,128)(2,1)S(1)} %slice.14), channel_id=1, source_target_pairs={{0,12},{4,0},{8,4},{12,8},{1,13},{5,1},{9,5},{13,9},{2,14},{6,2},{... | collective-permute-start | bytes 884744 | tf_op jit(solution)/shard_map/ppermute | solution.py:256
  62.0 0.0 collective-permute-done.1
  62.0 1.0 %add.12.refs_5_.base = f32[384,512]{1,0:T(8,128)} add(f32[384,512]{1,0:T(8,128)S(1)} %copy-done.2, f32[384,512]{1,0:T(8,128)S(1)} %collective-permute-done.1) | non-fusion elementwise | flops 196608 | bytes 2359296 | tf_op jit(solution)/shard_map/add | solution.py:280
  63.0 0.0 all-to-all-done.tok
  63.0 0.8 fusion
  63.8 0.6 reshape.12.ids
  64.3 4.5 %collective-permute-done.4.refs_2_ = bf16[2,64,1152]{2,1,0:T(8,128)(2,1)S(1)} collective-permute-done((bf16[2,64,1152]{2,1,0:T(8,128)(2,1)S(1)}, bf16[2,64,1152]{2,1,0:T(8,128)(2,1)S(1)}, u32[]{:S(2)}, u32[]{:S(2)}) %collective-permute-start.4) | collective-permute-done | bytes 294944 | tf_op jit(solution)/shard_map/ppermute | solution.py:256
  68.9 5.0 %collective-permute-done.5.refs_3_ = bf16[2,64,1152]{2,1,0:T(8,128)(2,1)S(1)} collective-permute-done((bf16[2,64,1152]{2,1,0:T(8,128)(2,1)S(1)}, bf16[2,64,1152]{2,1,0:T(8,128)(2,1)S(1)}, u32[]{:S(2)}, u32[]{:S(2)}) %collective-permute-start.5) | collective-permute-done | bytes 294944 | tf_op jit(solution)/shard_map/ppermute | solution.py:256
  73.9 0.7 copy-done.10
  74.6 5.2 %rank.1 = (bf16[3,128,128]{2,1,0:T(8,128)(2,1)}, bf16[3,128,128]{2,1,0:T(8,128)(2,1)}, bf16[3,128,128]{2,1,0:T(8,128)(2,1)}, bf16[3,128,128]{2,1,0:T(8,128)(2,1)}) custom-call(s32[12]{0:T(128)} %reshape.12.ids, s32[16]{0:T(128)} %owner.1, bf16[4,400,1024]{2,1,0:T(8,128)(2,1)} %all-to-all-done.tok, bf16[4,64,1152]{2,1,0:T(8,128)(2,1)} %copy-done.7, ...), custom_call_target="tpu_custom_call" | custom-call | flops 209715200 | bytes 3276800 | tf_op jit(solution)/shard_map/rank/pallas_call | solution.py:192
  79.8 2.0 %collective-permute-start.6 = (bf16[3,128,128]{2,1,0:T(8,128)(2,1)}, bf16[3,128,128]{2,1,0:T(8,128)(2,1)S(1)}, u32[]{:S(2)}, u32[]{:S(2)}) collective-permute-start(bf16[3,128,128]{2,1,0:T(8,128)(2,1)} %get-tuple-element.14), channel_id=1, source_target_pairs={{0,2},{2,0},{16,18},{18,16},{1,3},{3,1},{17,19},{19,17},{4,6},{6,4... | collective-permute-start | bytes 294920 | tf_op jit(solution)/shard_map/ppermute | solution.py:263
  81.8 1.5 %collective-permute-start.7 = (bf16[3,128,128]{2,1,0:T(8,128)(2,1)}, bf16[3,128,128]{2,1,0:T(8,128)(2,1)S(1)}, u32[]{:S(2)}, u32[]{:S(2)}) collective-permute-start(bf16[3,128,128]{2,1,0:T(8,128)(2,1)} %get-tuple-element.15), channel_id=1, source_target_pairs={{0,16},{2,18},{16,0},{18,2},{1,17},{3,19},{17,1},{19,3},{4,20},{6,... | collective-permute-start | bytes 294920 | tf_op jit(solution)/shard_map/ppermute | solution.py:263
  83.2 0.1 collective-permute-start.8
  83.3 0.0 collective-permute-start.9
  83.3 1.6 %collective-permute-done.6.refs_1_ = bf16[3,128,128]{2,1,0:T(8,128)(2,1)S(1)} collective-permute-done((bf16[3,128,128]{2,1,0:T(8,128)(2,1)}, bf16[3,128,128]{2,1,0:T(8,128)(2,1)S(1)}, u32[]{:S(2)}, u32[]{:S(2)}) %collective-permute-start.6) | collective-permute-done | bytes 98336 | tf_op jit(solution)/shard_map/ppermute | solution.py:263
  84.9 0.0 collective-permute-start.10
  84.9 2.6 %collective-permute-done.7.refs_2_ = bf16[3,128,128]{2,1,0:T(8,128)(2,1)S(1)} collective-permute-done((bf16[3,128,128]{2,1,0:T(8,128)(2,1)}, bf16[3,128,128]{2,1,0:T(8,128)(2,1)S(1)}, u32[]{:S(2)}, u32[]{:S(2)}) %collective-permute-start.7) | collective-permute-done | bytes 98336 | tf_op jit(solution)/shard_map/ppermute | solution.py:263
  87.6 0.0 collective-permute-start.11
  87.6 1.4 %collective-permute-done.8.refs_3_ = bf16[3,128,128]{2,1,0:T(8,128)(2,1)S(1)} collective-permute-done((bf16[3,128,128]{2,1,0:T(8,128)(2,1)}, bf16[3,128,128]{2,1,0:T(8,128)(2,1)S(1)}, u32[]{:S(2)}, u32[]{:S(2)}) %collective-permute-start.8) | collective-permute-done | bytes 98336 | tf_op jit(solution)/shard_map/ppermute | solution.py:263
  89.0 0.0 collective-permute-start.12
  89.0 0.0 collective-permute-done.9.refs_4_
  89.0 0.0 collective-permute-done.10.refs_5_
  89.0 0.0 collective-permute-done.11.refs_6_
  89.0 1.3 %collective-permute-done.12.refs_7_ = bf16[3,128,128]{2,1,0:T(8,128)(2,1)S(1)} collective-permute-done((bf16[3,128,128]{2,1,0:T(8,128)(2,1)S(1)}, bf16[3,128,128]{2,1,0:T(8,128)(2,1)S(1)}, u32[]{:S(2)}, u32[]{:S(2)}) %collective-permute-start.12) | collective-permute-done | bytes 98336 | tf_op jit(solution)/shard_map/ppermute | solution.py:250
  90.3 0.9 copy-done.1
  91.2 1.0 %final.1 = bf16[384,512]{1,0:T(8,128)(2,1)} custom-call(f32[384,512]{1,0:T(8,128)S(1)} %copy-done, bf16[3,128,128]{2,1,0:T(8,128)(2,1)S(1)} %copy-done.1, bf16[3,128,128]{2,1,0:T(8,128)(2,1)S(1)} %collective-permute-done.6.refs_1_, bf16[3,128,128]{2,1,0:T(8,128)(2,1)S(1)} %collective-permute-done.7.refs_2_, ...), custom_call_target="tpu_custom_call" | custom-call | tf_op jit(solution)/shard_map/final/pallas_call | solution.py:230
  (19 shorter events, 0.1 us)
Async XLA Ops:
  1.9 10.2 %collective-permute-start = (bf16[2,64,1152]{2,1,0:T(8,128)(2,1)}, bf16[2,64,1152]{2,1,0:T(8,128)(2,1)S(1)}, u32[]{:S(2)}, u32[]{:S(2)}) collective-permute-start(bf16[2,64,1152]{2,1,0:T(8,128)(2,1)} %get-tuple-element.11), channel_id=1, source_target_pairs={{0,2},{2,0},{1,3},{3,1},{4,6},{6,4},{5,7},{7,5},{8,10},{10,8},{9,1... | collective-permute-start | bytes 884744 | tf_op jit(solution)/shard_map/ppermute | solution.py:268
  12.1 0.7 copy-start.5
  12.9 4.8 %copy-start.8 = (bf16[2,64,1152]{2,1,0:T(8,128)(2,1)S(1)}, bf16[2,64,1152]{2,1,0:T(8,128)(2,1)}, u32[]{:S(2)}) copy-start(bf16[2,64,1152]{2,1,0:T(8,128)(2,1)} %get-tuple-element.12) | copy-start | bytes 884740
  12.9 50.1 %all-to-all-start = ((bf16[4,400,1024]{2,1,0:T(8,128)(2,1)}), bf16[4,400,1024]{2,1,0:T(8,128)(2,1)}, u32[]{:S(2)}, u32[]{:S(2)}) async-start(bf16[4,400,1024]{2,1,0:T(8,128)(2,1)} %hand.3), calls=%async_computation | async-start | bytes 6553600 | tf_op jit(solution)/shard_map/all_to_all | solution.py:253
  17.8 6.8 %copy-start.6 = (bf16[2,64,1152]{2,1,0:T(8,128)(2,1)S(1)}, bf16[2,64,1152]{2,1,0:T(8,128)(2,1)}, u32[]{:S(2)}) copy-start(bf16[2,64,1152]{2,1,0:T(8,128)(2,1)} %copy-done.5) | copy-start | bytes 884740
  24.5 37.5 %collective-permute-start.1 = (f32[384,512]{1,0:T(8,128)}, f32[384,512]{1,0:T(8,128)S(1)}, u32[]{:S(2)}, u32[]{:S(2)}) collective-permute-start(f32[384,512]{1,0:T(8,128)} %base.3.refs_1_), channel_id=1, source_target_pairs={{0,1},{1,0},{2,3},{3,2},{4,5},{5,4},{6,7},{7,6},{8,9},{9,8},{10,11... | collective-permute-start | bytes 2359304 | tf_op jit(solution)/shard_map/ppermute | solution.py:250
  24.6 10.6 %copy-start.7 = (bf16[4,64,1152]{2,1,0:T(8,128)(2,1)}, bf16[4,64,1152]{2,1,0:T(8,128)(2,1)S(1)}, u32[]{:S(2)}) copy-start(bf16[4,64,1152]{2,1,0:T(8,128)(2,1)S(1)} %constant_dynamic-update-slice_fusion.refs_0_) | copy-start | bytes 1769476
  24.6 17.6 %collective-permute-start.2 = (bf16[4,64,1152]{2,1,0:T(8,128)(2,1)S(1)}, bf16[4,64,1152]{2,1,0:T(8,128)(2,1)S(1)}, u32[]{:S(2)}, u32[]{:S(2)}) collective-permute-start(bf16[4,64,1152]{2,1,0:T(8,128)(2,1)S(1)} %constant_dynamic-update-slice_fusion.refs_0_), channel_id=1, source_target_pairs={{0,12},{4,0},{8,4},{12,8},{1,13},{5,1},{9,5},{13,9},{2,14},{6,2},{... | collective-permute-start | bytes 1769480 | tf_op jit(solution)/shard_map/ppermute | solution.py:256
  28.4 26.8 %collective-permute-start.3 = (bf16[4,64,1152]{2,1,0:T(8,128)(2,1)S(1)}, bf16[4,64,1152]{2,1,0:T(8,128)(2,1)S(1)}, u32[]{:S(2)}, u32[]{:S(2)}) collective-permute-start(bf16[4,64,1152]{2,1,0:T(8,128)(2,1)S(1)} %constant_dynamic-update-slice_fusion.refs_0_), channel_id=1, source_target_pairs={{0,4},{4,8},{8,12},{12,0},{1,5},{5,9},{9,13},{13,1},{2,6},{6,10},{... | collective-permute-start | bytes 1769480 | tf_op jit(solution)/shard_map/ppermute | solution.py:256
  35.1 26.9 %copy-start.2 = (f32[384,512]{1,0:T(8,128)S(1)}, f32[384,512]{1,0:T(8,128)}, u32[]{:S(2)}) copy-start(f32[384,512]{1,0:T(8,128)} %base.2.refs_2_) | copy-start | bytes 2359300
  42.1 13.1 %copy-start.3 = (bf16[4,64,1152]{2,1,0:T(8,128)(2,1)}, bf16[4,64,1152]{2,1,0:T(8,128)(2,1)S(1)}, u32[]{:S(2)}) copy-start(bf16[4,64,1152]{2,1,0:T(8,128)(2,1)S(1)} %collective-permute-done.2.refs_3_.refs_0_) | copy-start | bytes 1769476
  55.2 0.8 copy-start.4
  57.0 11.8 %collective-permute-start.4 = (bf16[2,64,1152]{2,1,0:T(8,128)(2,1)S(1)}, bf16[2,64,1152]{2,1,0:T(8,128)(2,1)S(1)}, u32[]{:S(2)}, u32[]{:S(2)}) collective-permute-start(bf16[2,64,1152]{2,1,0:T(8,128)(2,1)S(1)} %slice.13), channel_id=1, source_target_pairs={{0,4},{4,8},{8,12},{12,0},{1,5},{5,9},{9,13},{13,1},{2,6},{6,10},{... | collective-permute-start | bytes 884744 | tf_op jit(solution)/shard_map/ppermute | solution.py:256
  59.7 14.2 %collective-permute-start.5 = (bf16[2,64,1152]{2,1,0:T(8,128)(2,1)S(1)}, bf16[2,64,1152]{2,1,0:T(8,128)(2,1)S(1)}, u32[]{:S(2)}, u32[]{:S(2)}) collective-permute-start(bf16[2,64,1152]{2,1,0:T(8,128)(2,1)S(1)} %slice.14), channel_id=1, source_target_pairs={{0,12},{4,0},{8,4},{12,8},{1,13},{5,1},{9,5},{13,9},{2,14},{6,2},{... | collective-permute-start | bytes 884744 | tf_op jit(solution)/shard_map/ppermute | solution.py:256
  63.0 27.3 %copy-start = (f32[384,512]{1,0:T(8,128)S(1)}, f32[384,512]{1,0:T(8,128)}, u32[]{:S(2)}) copy-start(f32[384,512]{1,0:T(8,128)} %add.12.refs_5_.base) | copy-start | bytes 2359300
  68.8 5.0 %copy-start.9 = (bf16[2,64,1152]{2,1,0:T(8,128)(2,1)}, bf16[2,64,1152]{2,1,0:T(8,128)(2,1)S(1)}, u32[]{:S(2)}) copy-start(bf16[2,64,1152]{2,1,0:T(8,128)(2,1)S(1)} %collective-permute-done.4.refs_2_) | copy-start | bytes 884740
  73.9 0.7 copy-start.10
  79.8 5.2 %collective-permute-start.6 = (bf16[3,128,128]{2,1,0:T(8,128)(2,1)}, bf16[3,128,128]{2,1,0:T(8,128)(2,1)S(1)}, u32[]{:S(2)}, u32[]{:S(2)}) collective-permute-start(bf16[3,128,128]{2,1,0:T(8,128)(2,1)} %get-tuple-element.14), channel_id=1, source_target_pairs={{0,2},{2,0},{16,18},{18,16},{1,3},{3,1},{17,19},{19,17},{4,6},{6,4... | collective-permute-start | bytes 294920 | tf_op jit(solution)/shard_map/ppermute | solution.py:263
  81.8 5.8 %collective-permute-start.7 = (bf16[3,128,128]{2,1,0:T(8,128)(2,1)}, bf16[3,128,128]{2,1,0:T(8,128)(2,1)S(1)}, u32[]{:S(2)}, u32[]{:S(2)}) collective-permute-start(bf16[3,128,128]{2,1,0:T(8,128)(2,1)} %get-tuple-element.15), channel_id=1, source_target_pairs={{0,16},{2,18},{16,0},{18,2},{1,17},{3,19},{17,1},{19,3},{4,20},{6,... | collective-permute-start | bytes 294920 | tf_op jit(solution)/shard_map/ppermute | solution.py:263
  83.2 5.7 %collective-permute-start.8 = (bf16[3,128,128]{2,1,0:T(8,128)(2,1)}, bf16[3,128,128]{2,1,0:T(8,128)(2,1)S(1)}, u32[]{:S(2)}, u32[]{:S(2)}) collective-permute-start(bf16[3,128,128]{2,1,0:T(8,128)(2,1)} %get-tuple-element.16), channel_id=1, source_target_pairs={{0,18},{2,16},{16,2},{18,0},{1,19},{3,17},{17,3},{19,1},{4,22},{6,... | collective-permute-start | bytes 294920 | tf_op jit(solution)/shard_map/ppermute | solution.py:263
  83.3 5.7 %collective-permute-start.9 = (bf16[3,128,128]{2,1,0:T(8,128)(2,1)}, bf16[3,128,128]{2,1,0:T(8,128)(2,1)S(1)}, u32[]{:S(2)}, u32[]{:S(2)}) collective-permute-start(bf16[3,128,128]{2,1,0:T(8,128)(2,1)} %get-tuple-element.13.refs_0_), channel_id=1, source_target_pairs={{0,1},{1,0},{2,3},{3,2},{4,5},{5,4},{6,7},{7,6},{8,9},{9,8},{10,11... | collective-permute-start | bytes 294920 | tf_op jit(solution)/shard_map/ppermute | solution.py:250
  84.9 4.1 %collective-permute-start.10 = (bf16[3,128,128]{2,1,0:T(8,128)(2,1)S(1)}, bf16[3,128,128]{2,1,0:T(8,128)(2,1)S(1)}, u32[]{:S(2)}, u32[]{:S(2)}) collective-permute-start(bf16[3,128,128]{2,1,0:T(8,128)(2,1)S(1)} %collective-permute-done.6.refs_1_), channel_id=1, source_target_pairs={{0,1},{1,0},{2,3},{3,2},{4,5},{5,4},{6,7},{7,6},{8,9},{9,8},{10,11... | collective-permute-start | bytes 294920 | tf_op jit(solution)/shard_map/ppermute | solution.py:250
  87.6 1.4 %collective-permute-start.11 = (bf16[3,128,128]{2,1,0:T(8,128)(2,1)S(1)}, bf16[3,128,128]{2,1,0:T(8,128)(2,1)S(1)}, u32[]{:S(2)}, u32[]{:S(2)}) collective-permute-start(bf16[3,128,128]{2,1,0:T(8,128)(2,1)S(1)} %collective-permute-done.7.refs_2_), channel_id=1, source_target_pairs={{0,1},{1,0},{2,3},{3,2},{4,5},{5,4},{6,7},{7,6},{8,9},{9,8},{10,11... | collective-permute-start | bytes 294920 | tf_op jit(solution)/shard_map/ppermute | solution.py:250
  89.0 1.3 %collective-permute-start.12 = (bf16[3,128,128]{2,1,0:T(8,128)(2,1)S(1)}, bf16[3,128,128]{2,1,0:T(8,128)(2,1)S(1)}, u32[]{:S(2)}, u32[]{:S(2)}) collective-permute-start(bf16[3,128,128]{2,1,0:T(8,128)(2,1)S(1)} %collective-permute-done.8.refs_3_), channel_id=1, source_target_pairs={{0,1},{1,0},{2,3},{3,2},{4,5},{5,4},{6,7},{7,6},{8,9},{9,8},{10,11... | collective-permute-start | bytes 294920 | tf_op jit(solution)/shard_map/ppermute | solution.py:250
  90.3 0.9 copy-start.1

commit v9 on v7

--- a/solution.py
+++ b/solution.py
@@ -74,7 +74,7 @@
     lane = lax.broadcasted_iota(jnp.int32, (extra, step), 1)
     named = jnp.zeros((extra, step), jnp.float32)
     for b in range(blocks):
-        named = jnp.where(lane == b, ids[b, 0].astype(jnp.float32), named)
+        named = jnp.where(lane == b, ids[b].astype(jnp.float32), named)
     out_ref[0, rows:, :] = named.astype(out_ref.dtype)
 
 
@@ -182,13 +182,13 @@
             outs[k][b, rank:, :] = held[at, :, feats:]
 
 
-def rank_parts(ids, owner, tok, pieces, groups, ring, pair, blocks, after):
+def rank_parts(ids, owner, tok, pieces, groups, ring, pair, blocks):
     shares, tall, feats = tok.shape
     block = tall // blocks // LANES * LANES
     per, rank, wide = pieces[0].shape
     return pl.pallas_call(
         functools.partial(rank_kernel, groups, ring, pair),
-        in_specs=[SMEM, SMEM, ANY] + [ANY] * (len(pieces) + 1),
+        in_specs=[SMEM, SMEM, ANY] + [ANY] * len(pieces),
         out_specs=[VMEM] * shares,
         out_shape=[jax.ShapeDtypeStruct((blocks, 2 * rank, block), tok.dtype)] * shares,
         scratch_shapes=[
@@ -197,13 +197,12 @@
             pltpu.SemaphoreType.DMA((shares,)),
             pltpu.SemaphoreType.DMA((len(pieces),)),
         ],
-        compiler_params=BIG,
         cost_estimate=pl.CostEstimate(flops=2 * tok.size * rank, bytes_accessed=2 * tok.size, transcendentals=0),
         name="rank",
-    )(ids, owner, tok, *pieces, after)
-
-
-def final_kernel(groups, pair, base, *refs):
+    )(ids, owner, tok, *pieces)
+
+
+def final_kernel(groups, pair, base_a, base_b, *refs):
     shares = groups * pair
     mine, theirs, out_ref, up = refs[:shares], refs[shares : 2 * shares], refs[-2], refs[-1]
     blocks, tall, block = mine[0].shape
@@ -220,20 +219,20 @@
         delta = lax.dot_general(
             total.astype(jnp.bfloat16), up[b], (((0,), (0,)), ((), ())), preferred_element_type=jnp.float32
         )
-        out_ref[here, :] = (base[here, :] + delta).astype(out_ref.dtype)
+        out_ref[here, :] = (base_a[here, :] + base_b[here, :] + delta).astype(out_ref.dtype)
 
 
 def final(mine, theirs, base, groups, pair, dtype):
     blocks, tall, _ = mine[0].shape
     return pl.pallas_call(
         functools.partial(final_kernel, groups, pair),
-        in_specs=[VMEM] * (1 + 2 * len(mine)),
+        in_specs=[VMEM] * (2 + 2 * len(mine)),
         out_specs=VMEM,
-        out_shape=jax.ShapeDtypeStruct(base.shape, dtype),
-        scratch_shapes=[pltpu.VMEM((blocks, tall // 2, base.shape[1]), mine[0].dtype)],
+        out_shape=jax.ShapeDtypeStruct(base[0].shape, dtype),
+        scratch_shapes=[pltpu.VMEM((blocks, tall // 2, base[0].shape[1]), mine[0].dtype)],
         compiler_params=BIG,
         name="final",
-    )(base, *mine, *theirs)
+    )(*base, *mine, *theirs)
 
 
 def body(tokens, base_key, adapter_down, adapter_up, adapter_ids, owner_slot, lengths):
@@ -267,16 +266,16 @@
         for k in range(2, ring // 2 + 1):
             if 2 * k < ring or way % 2 == 0:
                 if k == 2:
-                    held[ring - 1] = hand_on(held[ring - 1], *after)
+                    held[ring - 1] = hand_on(held[ring - 1], held[1], *after)
                 held[ring - k] = along(held[ring - k + 1], 1)
             if 2 * k < ring or way % 2 == 1:
                 if k == 2:
-                    held[1] = hand_on(held[1], *after)
+                    held[1] = hand_on(held[1], held[ring - 1], *after)
                 held[k] = along(held[k - 1], -1)
         return [held[k] for k in range(ring)]
 
     packed = pack(jnp.swapaxes(adapter_down, 1, 2), adapter_up, shares, pair)
-    slabs = spread(tokens, lengths, adapter_ids, shares)
+    slabs = spread(tokens, lengths, adapter_ids.reshape(-1), shares)
     swapped = [
         lax.ppermute(packed[pair - w], "pair", [(a, (a - w) % pair) for a in range(pair)]) for w in range(1, pair)
     ]
@@ -284,20 +283,19 @@
     tok = to_plane(hand_on(slabs, *swapped))
     ids = tok[:, rows, :blocks].astype(jnp.int32).reshape(-1)
 
-    near = [firsts[0][k] for k in firsts[0] if k > 0]
-    base_out = base_half(tokens, base_key, (t + 1) % sides, sides, lengths, *near)
-    base_in = across(base_out)
-    base_mine = base_half(tokens, base_key, t, sides, lengths)
-    base = base_mine + base_in
+    base_out = base_half(tokens, base_key, (t + 1) % sides, sides, lengths, *swapped)
+    base_mine = base_half(tokens, base_key, t, sides, lengths, *swapped)
     pieces = [
-        more_hops(held, way, base_out, *([held[ring - 1]] if way % 2 and ring > 2 else [])) for way, held in enumerate(firsts)
+        more_hops(held, way, base_out, base_mine)
+        for way, held in enumerate(firsts)
     ]
 
     flat = [piece for way in pieces for piece in way]
-    parts = rank_parts(ids, owner_slot, tok, flat, groups, ring, pair, blocks, base)
+    parts = rank_parts(ids, owner_slot, tok, flat, groups, ring, pair, blocks)
     mine = [parts[0]] + [in_plane(parts[k], k // pair, k % pair) for k in range(1, shares)]
     theirs = [across(part) for part in mine]
-    return final(mine, theirs, base, groups, pair, tokens.dtype)
+    base_in = across(hand_on(base_out, parts[0]))
+    return final(mine, theirs, [base_mine, base_in], groups, pair, tokens.dtype)
 
 
 def solution(mesh):

time: 87.3 us -> 76.9 us (0.88)
  waiting for transfers between devices: 34.9 us -> 27 us
  other arithmetic: 2.45 us -> 0.02 us
  Pallas kernels: 24.5 us -> 25.9 us
  local copies, waits for them, and re-layouts: 5.16 us -> 3.87 us
    ppermute x6, waiting for transfers between devices: 26.9 us -> 13.3 us  [along(): lax.ppermute(x, 'ring', [(a, (a + step) % ring) for a in range(ring)])]
    all_to_all x1, waiting for transfers between devices: 0.01 us -> 4.16 us  [to_plane(): return lax.all_to_all(x, PLANE, split_axis=0, concat_axis=0, tiled=True)]
    add x1 -> x0, other arithmetic: 2.43 us -> none  [body(): base = base_mine + base_in]
    unnamed x11 -> x8, local copies, waits for them, and re-layouts: 5.08 us -> 3.27 us
    pallas_call x1, Pallas kernels: 3.86 us -> 5.43 us  [rank_parts(): pl.pallas_call(functools.partial(rank_kernel, groups, ring, pair), in_spe...]
    ppermute x1, waiting for transfers between devices: 1.64 us -> 2.93 us  [body(): lax.ppermute(packed[pair - w], 'pair', [(a, (a - w) % pair) for a in rang...]
  transfers between devices with their start and end apart: 16 -> 16, of which waited for: 10 -> 9; matrix products, arithmetic and copies ran while one was open for 4% -> 1% of each run, Pallas kernels for 20% -> 23%
where the time goes in v9:
time: 76.9 us; the launch traced here: 76.4 us
  waiting for transfers between devices  27 us (35%)
  Pallas kernels  25.9 us (34%)
  starting transfers between devices  19.5 us (25%)
  local copies, waits for them, and re-layouts  3.87 us (5%)
    ppermute x6, waiting for transfers between devices, along(): lax.ppermute(x, 'ring', [(a, (a + step) % ring) for a in range(ring)])  13.3 us
    pallas_call x2, Pallas kernels, base_half(): pl.pallas_call(base_kernel, grid_spec=pltpu.PrefetchScalarGridSpec(num_sc...  13.3 us
    ppermute x6, starting transfers between devices, along(): lax.ppermute(x, 'ring', [(a, (a + step) % ring) for a in range(ring)])  8.92 us
    pallas_call x1, Pallas kernels, rank_parts(): pl.pallas_call(functools.partial(rank_kernel, groups, ring, pair), in_spe...  5.43 us
    ppermute x3, waiting for transfers between devices, in_plane(): return lax.ppermute(x, PLANE, pairs)  5.35 us
    pallas_call x1, Pallas kernels, spread(): pl.pallas_call(spread_kernel, grid=(shares,), in_specs=[SMEM, SMEM, pl.Bl...  4.29 us
    all_to_all x1, waiting for transfers between devices, to_plane(): return lax.all_to_all(x, PLANE, split_axis=0, concat_axis=0, tiled=True)  4.16 us
    all_to_all x1, starting transfers between devices, to_plane(): return lax.all_to_all(x, PLANE, split_axis=0, concat_axis=0, tiled=True)  3.94 us
  transfers between devices with their start and end apart: 16, of which 9 were waited for; matrix products, arithmetic and copies ran while one was open for 1% of the time, Pallas kernels for 23%

profile of v9, /device:TPU:0, one launch (start us, length us, event | category | flops | bytes accessed | tf_op | source)
XLA Modules:
  0.0 76.4 jit_solution(3005124749875226288)
XLA Ops:
  0.0 1.9 %pack.1 = (bf16[2,64,1152]{2,1,0:T(8,128)(2,1)}, bf16[2,64,1152]{2,1,0:T(8,128)(2,1)}) custom-call(bf16[2,64,4096]{2,1,0:T(8,128)(2,1)} %bitcast.4, bf16[2,64,512]{2,1,0:T(8,128)(2,1)} %up.1), custom_call_target="tpu_custom_call" | custom-call | tf_op jit(solution)/shard_map/pack/pallas_call | solution.py:55
  1.9 3.0 %collective-permute-start = (bf16[2,64,1152]{2,1,0:T(8,128)(2,1)}, bf16[2,64,1152]{2,1,0:T(8,128)(2,1)S(1)}, u32[]{:S(2)}, u32[]{:S(2)}) collective-permute-start(bf16[2,64,1152]{2,1,0:T(8,128)(2,1)} %get-tuple-element.11), channel_id=1, source_target_pairs={{0,2},{2,0},{1,3},{3,1},{4,6},{6,4},{5,7},{7,5},{8,10},{10,8},{9,1... | collective-permute-start | bytes 884744 | tf_op jit(solution)/shard_map/ppermute | solution.py:280
  4.9 4.3 %spread.1.refs_0_ = bf16[4,400,1024]{2,1,0:T(8,128)(2,1)} custom-call(s32[3]{0:T(128)} %lengths.5, s32[3]{0:T(128)} %bitcast.5, bf16[384,4096]{1,0:T(8,128)(2,1)} %in_ref.1), custom_call_target="tpu_custom_call" | custom-call | tf_op jit(solution)/shard_map/spread/pallas_call | solution.py:84
  9.2 2.9 %collective-permute-done.refs_0_.refs_1_.refs_4_ = bf16[2,64,1152]{2,1,0:T(8,128)(2,1)S(1)} collective-permute-done((bf16[2,64,1152]{2,1,0:T(8,128)(2,1)}, bf16[2,64,1152]{2,1,0:T(8,128)(2,1)S(1)}, u32[]{:S(2)}, u32[]{:S(2)}) %collective-permute-start) | collective-permute-done | bytes 294944 | tf_op jit(solution)/shard_map/ppermute | solution.py:280
  12.1 0.0 copy-start.3
  12.2 0.7 copy-done.3
  12.9 3.9 %all-to-all-start = ((bf16[4,400,1024]{2,1,0:T(8,128)(2,1)}), bf16[4,400,1024]{2,1,0:T(8,128)(2,1)S(1)}, u32[]{:S(2)}, u32[]{:S(2)}) async-start(bf16[4,400,1024]{2,1,0:T(8,128)(2,1)} %hand.4), calls=%async_computation | async-start | bytes 6553600 | tf_op jit(solution)/shard_map/all_to_all | solution.py:250
  16.8 3.7 %collective-permute-start.1 = (bf16[2,64,1152]{2,1,0:T(8,128)(2,1)}, bf16[2,64,1152]{2,1,0:T(8,128)(2,1)}, u32[]{:S(2)}, u32[]{:S(2)}) collective-permute-start(bf16[2,64,1152]{2,1,0:T(8,128)(2,1)} %get-tuple-element.12.refs_0_), channel_id=1, source_target_pairs={{0,12},{4,0},{8,4},{12,8},{1,13},{5,1},{9,5},{13,9},{2,14},{6,2},{... | collective-permute-start | bytes 884744 | tf_op jit(solution)/shard_map/ppermute | solution.py:253
  20.5 0.0 collective-permute-start.2
  20.5 3.8 %collective-permute-start.4 = (bf16[2,64,1152]{2,1,0:T(8,128)(2,1)}, bf16[2,64,1152]{2,1,0:T(8,128)(2,1)}, u32[]{:S(2)}, u32[]{:S(2)}) collective-permute-start(bf16[2,64,1152]{2,1,0:T(8,128)(2,1)} %copy-done.3), channel_id=1, source_target_pairs={{0,12},{4,0},{8,4},{12,8},{1,13},{5,1},{9,5},{13,9},{2,14},{6,2},{... | collective-permute-start | bytes 884744 | tf_op jit(solution)/shard_map/ppermute | solution.py:253
  24.3 0.0 collective-permute-start.5
  24.3 6.6 %base.2.refs_3_.base_a = f32[384,512]{1,0:T(8,128)} custom-call(s32[1]{0:T(128)} %bitcast.side, s32[3]{0:T(128)} %lengths.5, bf16[384,4096]{1,0:T(8,128)(2,1)} %in_ref.1, bf16[4096,1024]{1,0:T(8,128)(2,1)} %key_ref.3, bf16[2,64,1152]{2,1,0:T(8,128)(2,1)} %copy-done.3), custom_call_target="tpu_custom_call" | custom-call | tf_op jit(solution)/shard_map/base/pallas_call | solution.py:121
  30.9 6.6 %base.3.refs_2_.refs_0_ = f32[384,512]{1,0:T(8,128)} custom-call(s32[1]{0:T(128)} %bitcast.2.side, s32[3]{0:T(128)} %lengths.5, bf16[384,4096]{1,0:T(8,128)(2,1)} %in_ref.1, bf16[4096,1024]{1,0:T(8,128)(2,1)} %key_ref.3, bf16[2,64,1152]{2,1,0:T(8,128)(2,1)} %copy-done.3), custom_call_target="tpu_custom_call" | custom-call | tf_op jit(solution)/shard_map/base/pallas_call | solution.py:121
  37.6 0.0 collective-permute-done.1.refs_1_
  37.6 0.0 collective-permute-done.2.refs_0_
  37.6 0.1 collective-permute-start.3
  37.6 3.3 %collective-permute-done.4.refs_0_ = bf16[2,64,1152]{2,1,0:T(8,128)(2,1)} collective-permute-done((bf16[2,64,1152]{2,1,0:T(8,128)(2,1)}, bf16[2,64,1152]{2,1,0:T(8,128)(2,1)}, u32[]{:S(2)}, u32[]{:S(2)}) %collective-permute-start.4) | collective-permute-done | bytes 294944 | tf_op jit(solution)/shard_map/ppermute | solution.py:253
  40.9 7.3 %collective-permute-done.5.refs_1_.refs_7_ = bf16[2,64,1152]{2,1,0:T(8,128)(2,1)} collective-permute-done((bf16[2,64,1152]{2,1,0:T(8,128)(2,1)}, bf16[2,64,1152]{2,1,0:T(8,128)(2,1)}, u32[]{:S(2)}, u32[]{:S(2)}) %collective-permute-start.5) | collective-permute-done | bytes 294944 | tf_op jit(solution)/shard_map/ppermute | solution.py:253
  48.3 1.4 %collective-permute-start.6 = (bf16[2,64,1152]{2,1,0:T(8,128)(2,1)}, bf16[2,64,1152]{2,1,0:T(8,128)(2,1)}, u32[]{:S(2)}, u32[]{:S(2)}) collective-permute-start(bf16[2,64,1152]{2,1,0:T(8,128)(2,1)} %hand.6.refs_5_), channel_id=1, source_target_pairs={{0,12},{4,0},{8,4},{12,8},{1,13},{5,1},{9,5},{13,9},{2,14},{6,2},{... | collective-permute-start | bytes 884744 | tf_op jit(solution)/shard_map/ppermute | solution.py:253
  49.6 4.2 %all-to-all-done.tok = bf16[4,400,1024]{2,1,0:T(8,128)(2,1)S(1)} async-done(((bf16[4,400,1024]{2,1,0:T(8,128)(2,1)}), bf16[4,400,1024]{2,1,0:T(8,128)(2,1)S(1)}, u32[]{:S(2)}, u32[]{:S(2)}) %all-to-all-start) | async-done | bytes 3276832 | tf_op jit(solution)/shard_map/all_to_all | solution.py:250
  53.8 0.0 copy-start.2
  53.8 1.6 %copy-done.2 = bf16[4,400,1024]{2,1,0:T(8,128)(2,1)} copy-done((bf16[4,400,1024]{2,1,0:T(8,128)(2,1)}, bf16[4,400,1024]{2,1,0:T(8,128)(2,1)S(1)}, u32[]{:S(2)}) %copy-start.2) | copy-done | bytes 3276824
  55.5 0.6 reshape.16.ids
  56.1 0.0 copy-start
  56.1 0.0 collective-permute-done.3.refs_2_
  56.1 2.7 %collective-permute-done.6.refs_6_ = bf16[2,64,1152]{2,1,0:T(8,128)(2,1)} collective-permute-done((bf16[2,64,1152]{2,1,0:T(8,128)(2,1)}, bf16[2,64,1152]{2,1,0:T(8,128)(2,1)}, u32[]{:S(2)}, u32[]{:S(2)}) %collective-permute-start.6) | collective-permute-done | bytes 294944 | tf_op jit(solution)/shard_map/ppermute | solution.py:253
  58.7 5.4 %rank.1 = (bf16[3,128,128]{2,1,0:T(8,128)(2,1)}, bf16[3,128,128]{2,1,0:T(8,128)(2,1)}, bf16[3,128,128]{2,1,0:T(8,128)(2,1)}, bf16[3,128,128]{2,1,0:T(8,128)(2,1)}) custom-call(s32[12]{0:T(128)} %reshape.16.ids, s32[16]{0:T(128)} %owner.1, bf16[4,400,1024]{2,1,0:T(8,128)(2,1)} %copy-done.2, bf16[2,64,1152]{2,1,0:T(8,128)(2,1)} %get-tuple-element.12.refs_0_, ...), custom_call_target="tpu_custom_call" | custom-call | flops 209715200 | bytes 3276800 | tf_op jit(solution)/shard_map/rank/pallas_call | solution.py:189
  64.2 0.1 collective-permute-start.7
  64.3 1.7 %collective-permute-start.8 = (bf16[3,128,128]{2,1,0:T(8,128)(2,1)}, bf16[3,128,128]{2,1,0:T(8,128)(2,1)S(1)}, u32[]{:S(2)}, u32[]{:S(2)}) collective-permute-start(bf16[3,128,128]{2,1,0:T(8,128)(2,1)} %get-tuple-element.14), channel_id=1, source_target_pairs={{0,2},{2,0},{16,18},{18,16},{1,3},{3,1},{17,19},{19,17},{4,6},{6,4... | collective-permute-start | bytes 294920 | tf_op jit(solution)/shard_map/ppermute | solution.py:263
  66.0 1.5 %collective-permute-start.9 = (bf16[3,128,128]{2,1,0:T(8,128)(2,1)}, bf16[3,128,128]{2,1,0:T(8,128)(2,1)S(1)}, u32[]{:S(2)}, u32[]{:S(2)}) collective-permute-start(bf16[3,128,128]{2,1,0:T(8,128)(2,1)} %get-tuple-element.15), channel_id=1, source_target_pairs={{0,16},{2,18},{16,0},{18,2},{1,17},{3,19},{17,1},{19,3},{4,20},{6,... | collective-permute-start | bytes 294920 | tf_op jit(solution)/shard_map/ppermute | solution.py:263
  67.4 0.4 collective-permute-start.10
  67.8 0.0 collective-permute-start.11
  67.8 1.9 %collective-permute-done.8.refs_1_ = bf16[3,128,128]{2,1,0:T(8,128)(2,1)S(1)} collective-permute-done((bf16[3,128,128]{2,1,0:T(8,128)(2,1)}, bf16[3,128,128]{2,1,0:T(8,128)(2,1)S(1)}, u32[]{:S(2)}, u32[]{:S(2)}) %collective-permute-start.8) | collective-permute-done | bytes 98336 | tf_op jit(solution)/shard_map/ppermute | solution.py:263
  69.7 0.0 collective-permute-start.12
  69.7 2.1 %collective-permute-done.9.refs_2_ = bf16[3,128,128]{2,1,0:T(8,128)(2,1)S(1)} collective-permute-done((bf16[3,128,128]{2,1,0:T(8,128)(2,1)}, bf16[3,128,128]{2,1,0:T(8,128)(2,1)S(1)}, u32[]{:S(2)}, u32[]{:S(2)}) %collective-permute-start.9) | collective-permute-done | bytes 98336 | tf_op jit(solution)/shard_map/ppermute | solution.py:263
  71.8 0.0 collective-permute-start.13
  71.8 1.3 %collective-permute-done.10.refs_3_ = bf16[3,128,128]{2,1,0:T(8,128)(2,1)S(1)} collective-permute-done((bf16[3,128,128]{2,1,0:T(8,128)(2,1)}, bf16[3,128,128]{2,1,0:T(8,128)(2,1)S(1)}, u32[]{:S(2)}, u32[]{:S(2)}) %collective-permute-start.10) | collective-permute-done | bytes 98336 | tf_op jit(solution)/shard_map/ppermute | solution.py:263
  73.2 0.0 collective-permute-start.14
  73.2 0.0 collective-permute-done.11.refs_4_
  73.2 0.0 collective-permute-done.12.refs_5_
  73.2 0.0 collective-permute-done.13.refs_6_
  73.2 1.3 %collective-permute-done.14.refs_7_ = bf16[3,128,128]{2,1,0:T(8,128)(2,1)S(1)} collective-permute-done((bf16[3,128,128]{2,1,0:T(8,128)(2,1)S(1)}, bf16[3,128,128]{2,1,0:T(8,128)(2,1)S(1)}, u32[]{:S(2)}, u32[]{:S(2)}) %collective-permute-start.14) | collective-permute-done | bytes 98336 | tf_op jit(solution)/shard_map/ppermute | solution.py:247
  74.5 0.0 collective-permute-done.7.base_b
  74.5 0.0 copy-done
  74.5 0.0 copy-start.1
  74.5 0.9 %copy-done.1 = bf16[3,128,128]{2,1,0:T(8,128)(2,1)S(1)} copy-done((bf16[3,128,128]{2,1,0:T(8,128)(2,1)S(1)}, bf16[3,128,128]{2,1,0:T(8,128)(2,1)}, u32[]{:S(2)}) %copy-start.1) | copy-done | bytes 98328
  75.4 1.1 %final.1 = bf16[384,512]{1,0:T(8,128)(2,1)} custom-call(f32[384,512]{1,0:T(8,128)S(1)} %copy-done, f32[384,512]{1,0:T(8,128)S(1)} %collective-permute-done.7.base_b, bf16[3,128,128]{2,1,0:T(8,128)(2,1)S(1)} %copy-done.1, bf16[3,128,128]{2,1,0:T(8,128)(2,1)S(1)} %collective-permute-done.8.refs_1_, bf16[3,128,128]{2,1,0:T(8,128)(2,1)S(1)} %collective-permute-done.9.refs_2_, ...), custom_call_target="tpu_custom_call" | custom-call | tf_op jit(solution)/shard_map/final/pallas_call | solution.py:227
  (5 shorter events, 0.0 us)
Async XLA Ops:
  1.9 10.2 %collective-permute-start = (bf16[2,64,1152]{2,1,0:T(8,128)(2,1)}, bf16[2,64,1152]{2,1,0:T(8,128)(2,1)S(1)}, u32[]{:S(2)}, u32[]{:S(2)}) collective-permute-start(bf16[2,64,1152]{2,1,0:T(8,128)(2,1)} %get-tuple-element.11), channel_id=1, source_target_pairs={{0,2},{2,0},{1,3},{3,1},{4,6},{6,4},{5,7},{7,5},{8,10},{10,8},{9,1... | collective-permute-start | bytes 884744 | tf_op jit(solution)/shard_map/ppermute | solution.py:280
  12.1 0.7 copy-start.3
  12.9 40.9 %all-to-all-start = ((bf16[4,400,1024]{2,1,0:T(8,128)(2,1)}), bf16[4,400,1024]{2,1,0:T(8,128)(2,1)S(1)}, u32[]{:S(2)}, u32[]{:S(2)}) async-start(bf16[4,400,1024]{2,1,0:T(8,128)(2,1)} %hand.4), calls=%async_computation | async-start | bytes 6553600 | tf_op jit(solution)/shard_map/all_to_all | solution.py:250
  16.8 20.7 %collective-permute-start.1 = (bf16[2,64,1152]{2,1,0:T(8,128)(2,1)}, bf16[2,64,1152]{2,1,0:T(8,128)(2,1)}, u32[]{:S(2)}, u32[]{:S(2)}) collective-permute-start(bf16[2,64,1152]{2,1,0:T(8,128)(2,1)} %get-tuple-element.12.refs_0_), channel_id=1, source_target_pairs={{0,12},{4,0},{8,4},{12,8},{1,13},{5,1},{9,5},{13,9},{2,14},{6,2},{... | collective-permute-start | bytes 884744 | tf_op jit(solution)/shard_map/ppermute | solution.py:253
  20.5 17.1 %collective-permute-start.2 = (bf16[2,64,1152]{2,1,0:T(8,128)(2,1)}, bf16[2,64,1152]{2,1,0:T(8,128)(2,1)}, u32[]{:S(2)}, u32[]{:S(2)}) collective-permute-start(bf16[2,64,1152]{2,1,0:T(8,128)(2,1)} %get-tuple-element.12.refs_0_), channel_id=1, source_target_pairs={{0,4},{4,8},{8,12},{12,0},{1,5},{5,9},{9,13},{13,1},{2,6},{6,10},{... | collective-permute-start | bytes 884744 | tf_op jit(solution)/shard_map/ppermute | solution.py:253
  20.5 20.5 %collective-permute-start.4 = (bf16[2,64,1152]{2,1,0:T(8,128)(2,1)}, bf16[2,64,1152]{2,1,0:T(8,128)(2,1)}, u32[]{:S(2)}, u32[]{:S(2)}) collective-permute-start(bf16[2,64,1152]{2,1,0:T(8,128)(2,1)} %copy-done.3), channel_id=1, source_target_pairs={{0,12},{4,0},{8,4},{12,8},{1,13},{5,1},{9,5},{13,9},{2,14},{6,2},{... | collective-permute-start | bytes 884744 | tf_op jit(solution)/shard_map/ppermute | solution.py:253
  24.3 24.0 %collective-permute-start.5 = (bf16[2,64,1152]{2,1,0:T(8,128)(2,1)}, bf16[2,64,1152]{2,1,0:T(8,128)(2,1)}, u32[]{:S(2)}, u32[]{:S(2)}) collective-permute-start(bf16[2,64,1152]{2,1,0:T(8,128)(2,1)} %copy-done.3), channel_id=1, source_target_pairs={{0,4},{4,8},{8,12},{12,0},{1,5},{5,9},{9,13},{13,1},{2,6},{6,10},{... | collective-permute-start | bytes 884744 | tf_op jit(solution)/shard_map/ppermute | solution.py:253
  37.6 18.5 %collective-permute-start.3 = (bf16[2,64,1152]{2,1,0:T(8,128)(2,1)}, bf16[2,64,1152]{2,1,0:T(8,128)(2,1)}, u32[]{:S(2)}, u32[]{:S(2)}) collective-permute-start(bf16[2,64,1152]{2,1,0:T(8,128)(2,1)} %hand.5.refs_3_), channel_id=1, source_target_pairs={{0,4},{4,8},{8,12},{12,0},{1,5},{5,9},{9,13},{13,1},{2,6},{6,10},{... | collective-permute-start | bytes 884744 | tf_op jit(solution)/shard_map/ppermute | solution.py:253
  48.3 10.5 %collective-permute-start.6 = (bf16[2,64,1152]{2,1,0:T(8,128)(2,1)}, bf16[2,64,1152]{2,1,0:T(8,128)(2,1)}, u32[]{:S(2)}, u32[]{:S(2)}) collective-permute-start(bf16[2,64,1152]{2,1,0:T(8,128)(2,1)} %hand.6.refs_5_), channel_id=1, source_target_pairs={{0,12},{4,0},{8,4},{12,8},{1,13},{5,1},{9,5},{13,9},{2,14},{6,2},{... | collective-permute-start | bytes 884744 | tf_op jit(solution)/shard_map/ppermute | solution.py:253
  53.8 1.7 %copy-start.2 = (bf16[4,400,1024]{2,1,0:T(8,128)(2,1)}, bf16[4,400,1024]{2,1,0:T(8,128)(2,1)S(1)}, u32[]{:S(2)}) copy-start(bf16[4,400,1024]{2,1,0:T(8,128)(2,1)S(1)} %all-to-all-done.tok) | copy-start | bytes 9830404
  56.1 18.4 %copy-start = (f32[384,512]{1,0:T(8,128)S(1)}, f32[384,512]{1,0:T(8,128)}, u32[]{:S(2)}) copy-start(f32[384,512]{1,0:T(8,128)} %base.2.refs_3_.base_a) | copy-start | bytes 2359300
  64.2 10.3 %collective-permute-start.7 = (f32[384,512]{1,0:T(8,128)}, f32[384,512]{1,0:T(8,128)S(1)}, u32[]{:S(2)}, u32[]{:S(2)}) collective-permute-start(f32[384,512]{1,0:T(8,128)} %hand.7), channel_id=1, source_target_pairs={{0,1},{1,0},{2,3},{3,2},{4,5},{5,4},{6,7},{7,6},{8,9},{9,8},{10,11... | collective-permute-start | bytes 2359304 | tf_op jit(solution)/shard_map/ppermute | solution.py:247
  64.3 5.4 %collective-permute-start.8 = (bf16[3,128,128]{2,1,0:T(8,128)(2,1)}, bf16[3,128,128]{2,1,0:T(8,128)(2,1)S(1)}, u32[]{:S(2)}, u32[]{:S(2)}) collective-permute-start(bf16[3,128,128]{2,1,0:T(8,128)(2,1)} %get-tuple-element.14), channel_id=1, source_target_pairs={{0,2},{2,0},{16,18},{18,16},{1,3},{3,1},{17,19},{19,17},{4,6},{6,4... | collective-permute-start | bytes 294920 | tf_op jit(solution)/shard_map/ppermute | solution.py:263
  66.0 5.9 %collective-permute-start.9 = (bf16[3,128,128]{2,1,0:T(8,128)(2,1)}, bf16[3,128,128]{2,1,0:T(8,128)(2,1)S(1)}, u32[]{:S(2)}, u32[]{:S(2)}) collective-permute-start(bf16[3,128,128]{2,1,0:T(8,128)(2,1)} %get-tuple-element.15), channel_id=1, source_target_pairs={{0,16},{2,18},{16,0},{18,2},{1,17},{3,19},{17,1},{19,3},{4,20},{6,... | collective-permute-start | bytes 294920 | tf_op jit(solution)/shard_map/ppermute | solution.py:263
  67.4 5.7 %collective-permute-start.10 = (bf16[3,128,128]{2,1,0:T(8,128)(2,1)}, bf16[3,128,128]{2,1,0:T(8,128)(2,1)S(1)}, u32[]{:S(2)}, u32[]{:S(2)}) collective-permute-start(bf16[3,128,128]{2,1,0:T(8,128)(2,1)} %get-tuple-element.16), channel_id=1, source_target_pairs={{0,18},{2,16},{16,2},{18,0},{1,19},{3,17},{17,3},{19,1},{4,22},{6,... | collective-permute-start | bytes 294920 | tf_op jit(solution)/shard_map/ppermute | solution.py:263
  67.8 5.4 %collective-permute-start.11 = (bf16[3,128,128]{2,1,0:T(8,128)(2,1)}, bf16[3,128,128]{2,1,0:T(8,128)(2,1)S(1)}, u32[]{:S(2)}, u32[]{:S(2)}) collective-permute-start(bf16[3,128,128]{2,1,0:T(8,128)(2,1)} %get-tuple-element.13.refs_1_.refs_0_), channel_id=1, source_target_pairs={{0,1},{1,0},{2,3},{3,2},{4,5},{5,4},{6,7},{7,6},{8,9},{9,8},{10,11... | collective-permute-start | bytes 294920 | tf_op jit(solution)/shard_map/ppermute | solution.py:247
  69.7 3.5 %collective-permute-start.12 = (bf16[3,128,128]{2,1,0:T(8,128)(2,1)S(1)}, bf16[3,128,128]{2,1,0:T(8,128)(2,1)S(1)}, u32[]{:S(2)}, u32[]{:S(2)}) collective-permute-start(bf16[3,128,128]{2,1,0:T(8,128)(2,1)S(1)} %collective-permute-done.8.refs_1_), channel_id=1, source_target_pairs={{0,1},{1,0},{2,3},{3,2},{4,5},{5,4},{6,7},{7,6},{8,9},{9,8},{10,11... | collective-permute-start | bytes 294920 | tf_op jit(solution)/shard_map/ppermute | solution.py:247
  71.8 1.4 %collective-permute-start.13 = (bf16[3,128,128]{2,1,0:T(8,128)(2,1)S(1)}, bf16[3,128,128]{2,1,0:T(8,128)(2,1)S(1)}, u32[]{:S(2)}, u32[]{:S(2)}) collective-permute-start(bf16[3,128,128]{2,1,0:T(8,128)(2,1)S(1)} %collective-permute-done.9.refs_2_), channel_id=1, source_target_pairs={{0,1},{1,0},{2,3},{3,2},{4,5},{5,4},{6,7},{7,6},{8,9},{9,8},{10,11... | collective-permute-start | bytes 294920 | tf_op jit(solution)/shard_map/ppermute | solution.py:247
  73.2 1.3 %collective-permute-start.14 = (bf16[3,128,128]{2,1,0:T(8,128)(2,1)S(1)}, bf16[3,128,128]{2,1,0:T(8,128)(2,1)S(1)}, u32[]{:S(2)}, u32[]{:S(2)}) collective-permute-start(bf16[3,128,128]{2,1,0:T(8,128)(2,1)S(1)} %collective-permute-done.10.refs_3_), channel_id=1, source_target_pairs={{0,1},{1,0},{2,3},{3,2},{4,5},{5,4},{6,7},{7,6},{8,9},{9,8},{10,11... | collective-permute-start | bytes 294920 | tf_op jit(solution)/shard_map/ppermute | solution.py:247
  74.5 0.9 %copy-start.1 = (bf16[3,128,128]{2,1,0:T(8,128)(2,1)S(1)}, bf16[3,128,128]{2,1,0:T(8,128)(2,1)}, u32[]{:S(2)}) copy-start(bf16[3,128,128]{2,1,0:T(8,128)(2,1)} %get-tuple-element.13.refs_1_.refs_0_) | copy-start | bytes 294916

commit v10 on v9

--- a/solution.py
+++ b/solution.py
@@ -33,16 +33,37 @@
     )(x, *after)
 
 
-def pack_kernel(down, up, *refs):
+def go_kernel(*refs):
+    refs[-1][...] = jnp.zeros(refs[-1].shape, refs[-1].dtype)
+
+
+def go_after(*arrays):
+    return pl.pallas_call(
+        go_kernel,
+        in_specs=[ANY] * len(arrays),
+        out_specs=VMEM,
+        out_shape=jax.ShapeDtypeStruct((16, LANES), jnp.bfloat16),
+        name="go",
+    )(*arrays)
+
+
+def pack_kernel(ways, down, up, *refs):
     outs, sems = refs[:-1], refs[-1]
     feats = outs[0].shape[2] - LANES
+    adapters = down.shape[0]
     copies = []
-    for way, out in enumerate(outs):
-        share = lax.axis_index("groups") * len(outs) + lax.rem(lax.axis_index("pair") + way, len(outs))
+    for way in range(ways):
+        share = lax.axis_index("groups") * ways + lax.rem(lax.axis_index("pair") + way, ways)
         start = pl.multiple_of(share * feats, LANES)
         tile = pl.multiple_of(lax.rem(share, up.shape[2] // LANES) * LANES, LANES)
-        copies.append(pltpu.make_async_copy(down.at[:, :, pl.ds(start, feats)], out.at[:, :, :feats], sems.at[way, 0]))
-        copies.append(pltpu.make_async_copy(up.at[:, :, pl.ds(tile, LANES)], out.at[:, :, feats:], sems.at[way, 1]))
+        for a in range(adapters):
+            if way == 0:
+                to = outs[0].at[a]
+            else:
+                to = outs[1 + (way - 1) * adapters + a].at[0]
+            sem = sems.at[way, a]
+            copies.append(pltpu.make_async_copy(down.at[a, :, pl.ds(start, feats)], to.at[:, :feats], sem.at[0]))
+            copies.append(pltpu.make_async_copy(up.at[a, :, pl.ds(tile, LANES)], to.at[:, feats:], sem.at[1]))
     for copy in copies:
         copy.start()
     for copy in copies:
@@ -51,15 +72,17 @@
 
 def pack(down, up, shares, ways):
     adapters, rank, feats = down.shape
-    shape = jax.ShapeDtypeStruct((adapters, rank, feats // shares + LANES), down.dtype)
-    return pl.pallas_call(
-        pack_kernel,
+    wide = feats // shares + LANES
+    shapes = [(adapters, rank, wide)] + [(1, rank, wide)] * (adapters * (ways - 1))
+    outs = pl.pallas_call(
+        functools.partial(pack_kernel, ways),
         in_specs=[HBM, HBM],
-        out_specs=[VMEM] * ways,
-        out_shape=[shape] * ways,
-        scratch_shapes=[pltpu.SemaphoreType.DMA((ways, 2))],
+        out_specs=[VMEM] * len(shapes),
+        out_shape=[jax.ShapeDtypeStruct(shape, down.dtype) for shape in shapes],
+        scratch_shapes=[pltpu.SemaphoreType.DMA((ways, adapters, 2))],
         name="pack",
     )(down, up)
+    return outs[0], [outs[1 + w * adapters : 1 + (w + 1) * adapters] for w in range(ways - 1)]
 
 
 def spread_kernel(lengths, ids, in_ref, out_ref):
@@ -274,19 +297,23 @@
                 held[k] = along(held[k - 1], -1)
         return [held[k] for k in range(ring)]
 
-    packed = pack(jnp.swapaxes(adapter_down, 1, 2), adapter_up, shares, pair)
+    own, others = pack(jnp.swapaxes(adapter_down, 1, 2), adapter_up, shares, pair)
     slabs = spread(tokens, lengths, adapter_ids.reshape(-1), shares)
-    swapped = [
-        lax.ppermute(packed[pair - w], "pair", [(a, (a - w) % pair) for a in range(pair)]) for w in range(1, pair)
-    ]
-    firsts = [first_hops(piece) for piece in [packed[0]] + swapped]
-    tok = to_plane(hand_on(slabs, *swapped))
+    swapped, first_in = [], []
+    for w in range(1, pair):
+        back = [(a, (a - w) % pair) for a in range(pair)]
+        halves = [lax.ppermute(piece, "pair", back) for piece in others[pair - w - 1]]
+        swapped.append(jnp.concatenate(halves))
+        first_in.append(halves[0])
+    firsts = [first_hops(piece) for piece in [own] + swapped]
+    go = across(go_after(*(firsts[0][k] for k in firsts[0] if k > 0)))
+    tok = to_plane(hand_on(slabs, *first_in))
     ids = tok[:, rows, :blocks].astype(jnp.int32).reshape(-1)
 
     base_out = base_half(tokens, base_key, (t + 1) % sides, sides, lengths, *swapped)
     base_mine = base_half(tokens, base_key, t, sides, lengths, *swapped)
     pieces = [
-        more_hops(held, way, base_out, base_mine)
+        more_hops(held, way, go, base_out, base_mine)
         for way, held in enumerate(firsts)
     ]
 

time: 76.9 us -> 107 us (1.39)
  waiting for transfers between devices: 27 us -> 50.2 us
  starting transfers between devices: 19.5 us -> 24.1 us
  local copies, waits for them, and re-layouts: 3.87 us -> 5.8 us
    ppermute x1 -> x2, waiting for transfers between devices: 2.93 us -> 34.3 us  [body(): lax.ppermute(piece, 'pair', back)]
    all_to_all x1, waiting for transfers between devices: 4.16 us -> 0.01 us  [to_plane(): return lax.all_to_all(x, PLANE, split_axis=0, concat_axis=0, tiled=True)]
    ppermute x6, waiting for transfers between devices: 13.3 us -> 9.91 us  [along(): lax.ppermute(x, 'ring', [(a, (a + step) % ring) for a in range(ring)])]
    ppermute x6, starting transfers between devices: 8.92 us -> 11.1 us  [along(): lax.ppermute(x, 'ring', [(a, (a + step) % ring) for a in range(ring)])]
    ppermute x1 -> x2, starting transfers between devices: 3.03 us -> 5 us  [body(): lax.ppermute(piece, 'pair', back)]
    unnamed x8 -> x13, local copies, waits for them, and re-layouts: 3.27 us -> 4.46 us
    pallas_call x1 -> x2, Pallas kernels: 1.89 us -> 2.62 us  [the longest x1 2.03 us: pack(): pl.pallas_call(functools.partial(pack_kernel, ways), in_specs=[HBM, HBM],...]
  transfers between devices with their start and end apart: 16 -> 18, of which waited for: 9 -> 6; matrix products, arithmetic and copies ran while one was open for 1% -> 2% of each run, Pallas kernels for 23% -> 17%
where the time goes in v10:
time: 107 us
  waiting for transfers between devices  50.2 us (47%)
  Pallas kernels  26.6 us (25%)
  starting transfers between devices  24.1 us (23%)
  local copies, waits for them, and re-layouts  5.8 us (5%)
    ppermute x2, waiting for transfers between devices, body(): lax.ppermute(piece, 'pair', back)  34.3 us
    pallas_call x2, Pallas kernels, base_half(): pl.pallas_call(base_kernel, grid_spec=pltpu.PrefetchScalarGridSpec(num_sc...  13.3 us
    ppermute x6, starting transfers between devices, along(): lax.ppermute(x, 'ring', [(a, (a + step) % ring) for a in range(ring)])  11.1 us
    ppermute x6, waiting for transfers between devices, along(): lax.ppermute(x, 'ring', [(a, (a + step) % ring) for a in range(ring)])  9.91 us
    pallas_call x1, Pallas kernels, rank_parts(): pl.pallas_call(functools.partial(rank_kernel, groups, ring, pair), in_spe...  5.44 us
    ppermute x2, starting transfers between devices, body(): lax.ppermute(piece, 'pair', back)  5 us
    ppermute x3, waiting for transfers between devices, in_plane(): return lax.ppermute(x, PLANE, pairs)  4.65 us
    unnamed x13, local copies, waits for them, and re-layouts  4.46 us
  transfers between devices with their start and end apart: 18, of which 6 were waited for; matrix products, arithmetic and copies ran while one was open for 2% of the time, Pallas kernels for 17%

profile of v10, /device:TPU:0, one launch (start us, length us, event | category | flops | bytes accessed | tf_op | source)
XLA Modules:
  0.0 106.8 jit_solution(2465226480684448817)
XLA Ops:
  0.0 2.0 %pack.1 = (bf16[2,64,1152]{2,1,0:T(8,128)(2,1)}, bf16[1,64,1152]{2,1,0:T(8,128)(2,1)}, bf16[1,64,1152]{2,1,0:T(8,128)(2,1)}) custom-call(bf16[2,64,4096]{2,1,0:T(8,128)(2,1)} %bitcast.4, bf16[2,64,512]{2,1,0:T(8,128)(2,1)} %up.1), custom_call_target="tpu_custom_call" | custom-call | tf_op jit(solution)/shard_map/pack/pallas_call | solution.py:77
  2.0 3.0 %collective-permute-start = (bf16[1,64,1152]{2,1,0:T(8,128)(2,1)}, bf16[1,64,1152]{2,1,0:T(8,128)(2,1)S(1)}, u32[]{:S(2)}, u32[]{:S(2)}) collective-permute-start(bf16[1,64,1152]{2,1,0:T(8,128)(2,1)} %get-tuple-element.12), channel_id=1, source_target_pairs={{0,2},{2,0},{1,3},{3,1},{4,6},{6,4},{5,7},{7,5},{8,10},{10,8},{9,1... | collective-permute-start | bytes 442376 | tf_op jit(solution)/shard_map/ppermute | solution.py:305
  5.1 4.3 %spread.1.refs_0_ = bf16[4,400,1024]{2,1,0:T(8,128)(2,1)} custom-call(s32[3]{0:T(128)} %lengths.5, s32[3]{0:T(128)} %bitcast.5, bf16[384,4096]{1,0:T(8,128)(2,1)} %in_ref.1), custom_call_target="tpu_custom_call" | custom-call | tf_op jit(solution)/shard_map/spread/pallas_call | solution.py:107
  9.3 0.0 collective-permute-done.refs_1_
  9.3 0.7 copy-done.3
  10.0 3.9 %all-to-all-start = ((bf16[4,400,1024]{2,1,0:T(8,128)(2,1)}), bf16[4,400,1024]{2,1,0:T(8,128)(2,1)S(1)}, u32[]{:S(2)}, u32[]{:S(2)}) async-start(bf16[4,400,1024]{2,1,0:T(8,128)(2,1)} %hand.4), calls=%async_computation | async-start | bytes 6553600 | tf_op jit(solution)/shard_map/all_to_all | solution.py:273
  13.9 3.7 %collective-permute-start.2 = (bf16[2,64,1152]{2,1,0:T(8,128)(2,1)}, bf16[2,64,1152]{2,1,0:T(8,128)(2,1)}, u32[]{:S(2)}, u32[]{:S(2)}) collective-permute-start(bf16[2,64,1152]{2,1,0:T(8,128)(2,1)} %get-tuple-element.14.refs_0_), channel_id=1, source_target_pairs={{0,12},{4,0},{8,4},{12,8},{1,13},{5,1},{9,5},{13,9},{2,14},{6,2},{... | collective-permute-start | bytes 884744 | tf_op jit(solution)/shard_map/ppermute | solution.py:276
  17.5 0.0 collective-permute-start.3
  17.5 2.0 %collective-permute-start.1 = (bf16[1,64,1152]{2,1,0:T(8,128)(2,1)}, bf16[1,64,1152]{2,1,0:T(8,128)(2,1)S(1)}, u32[]{:S(2)}, u32[]{:S(2)}) collective-permute-start(bf16[1,64,1152]{2,1,0:T(8,128)(2,1)} %get-tuple-element.13), channel_id=1, source_target_pairs={{0,2},{2,0},{1,3},{3,1},{4,6},{6,4},{5,7},{7,5},{8,10},{10,8},{9,1... | collective-permute-start | bytes 442376 | tf_op jit(solution)/shard_map/ppermute | solution.py:305
  19.5 0.7 constant_dynamic-update-slice_fusion.1
  20.2 34.3 %collective-permute-done.1 = bf16[1,64,1152]{2,1,0:T(8,128)(2,1)S(1)} collective-permute-done((bf16[1,64,1152]{2,1,0:T(8,128)(2,1)}, bf16[1,64,1152]{2,1,0:T(8,128)(2,1)S(1)}, u32[]{:S(2)}, u32[]{:S(2)}) %collective-permute-start.1) | collective-permute-done | bytes 147488 | tf_op jit(solution)/shard_map/ppermute | solution.py:305
  54.4 0.7 constant_dynamic-update-slice_fusion.refs_0_.refs_4_
  55.1 3.6 %collective-permute-start.6 = (bf16[2,64,1152]{2,1,0:T(8,128)(2,1)}, bf16[2,64,1152]{2,1,0:T(8,128)(2,1)}, u32[]{:S(2)}, u32[]{:S(2)}) collective-permute-start(bf16[2,64,1152]{2,1,0:T(8,128)(2,1)} %constant_dynamic-update-slice_fusion.refs_0_.refs_4_), channel_id=1, source_target_pairs={{0,12},{4,0},{8,4},{12,8},{1,13},{5,1},{9,5},{13,9},{2,14},{6,2},{... | collective-permute-start | bytes 884744 | tf_op jit(solution)/shard_map/ppermute | solution.py:276
  58.7 0.0 collective-permute-start.7
  58.7 0.0 collective-permute-done.2.refs_1_
  58.7 0.0 collective-permute-done.3.refs_0_
  58.7 0.6 go.1
  59.3 0.0 collective-permute-start.4
  59.3 6.6 %base.2.refs_4_.base_a = f32[384,512]{1,0:T(8,128)} custom-call(s32[1]{0:T(128)} %bitcast.side, s32[3]{0:T(128)} %lengths.5, bf16[384,4096]{1,0:T(8,128)(2,1)} %in_ref.1, bf16[4096,1024]{1,0:T(8,128)(2,1)} %key_ref.3, bf16[2,64,1152]{2,1,0:T(8,128)(2,1)} %constant_dynamic-update-slice_fusion.refs_0_.refs_4_), custom_call_target="tpu_custom_call" | custom-call | tf_op jit(solution)/shard_map/base/pallas_call | solution.py:144
  66.0 6.6 %base.3.refs_3_.refs_0_ = f32[384,512]{1,0:T(8,128)} custom-call(s32[1]{0:T(128)} %bitcast.2.side, s32[3]{0:T(128)} %lengths.5, bf16[384,4096]{1,0:T(8,128)(2,1)} %in_ref.1, bf16[4096,1024]{1,0:T(8,128)(2,1)} %key_ref.3, bf16[2,64,1152]{2,1,0:T(8,128)(2,1)} %constant_dynamic-update-slice_fusion.refs_0_.refs_4_), custom_call_target="tpu_custom_call" | custom-call | tf_op jit(solution)/shard_map/base/pallas_call | solution.py:144
  72.6 0.0 collective-permute-done.4.refs_2_
  72.6 0.6 copy-done.5
  73.2 0.0 collective-permute-start.5
  73.2 0.0 collective-permute-done.6.refs_0_
  73.2 0.0 collective-permute-done.7.refs_1_.refs_7_
  73.2 3.9 %collective-permute-start.8 = (bf16[2,64,1152]{2,1,0:T(8,128)(2,1)}, bf16[2,64,1152]{2,1,0:T(8,128)(2,1)}, u32[]{:S(2)}, u32[]{:S(2)}) collective-permute-start(bf16[2,64,1152]{2,1,0:T(8,128)(2,1)} %hand.6.refs_5_), channel_id=1, source_target_pairs={{0,12},{4,0},{8,4},{12,8},{1,13},{5,1},{9,5},{13,9},{2,14},{6,2},{... | collective-permute-start | bytes 884744 | tf_op jit(solution)/shard_map/ppermute | solution.py:276
  77.1 0.0 all-to-all-done.tok
  77.1 1.6 %copy-done.2 = bf16[4,400,1024]{2,1,0:T(8,128)(2,1)} copy-done((bf16[4,400,1024]{2,1,0:T(8,128)(2,1)}, bf16[4,400,1024]{2,1,0:T(8,128)(2,1)S(1)}, u32[]{:S(2)}) %copy-start.2) | copy-done | bytes 3276824
  78.8 0.7 reshape.16.ids
  79.4 5.8 %collective-permute-done.5.refs_2_ = bf16[2,64,1152]{2,1,0:T(8,128)(2,1)} collective-permute-done((bf16[2,64,1152]{2,1,0:T(8,128)(2,1)}, bf16[2,64,1152]{2,1,0:T(8,128)(2,1)}, u32[]{:S(2)}, u32[]{:S(2)}) %collective-permute-start.5) | collective-permute-done | bytes 294944 | tf_op jit(solution)/shard_map/ppermute | solution.py:276
  85.2 4.1 %collective-permute-done.8.refs_6_ = bf16[2,64,1152]{2,1,0:T(8,128)(2,1)} collective-permute-done((bf16[2,64,1152]{2,1,0:T(8,128)(2,1)}, bf16[2,64,1152]{2,1,0:T(8,128)(2,1)}, u32[]{:S(2)}, u32[]{:S(2)}) %collective-permute-start.8) | collective-permute-done | bytes 294944 | tf_op jit(solution)/shard_map/ppermute | solution.py:276
  89.3 5.4 %rank.1 = (bf16[3,128,128]{2,1,0:T(8,128)(2,1)}, bf16[3,128,128]{2,1,0:T(8,128)(2,1)}, bf16[3,128,128]{2,1,0:T(8,128)(2,1)}, bf16[3,128,128]{2,1,0:T(8,128)(2,1)}) custom-call(s32[12]{0:T(128)} %reshape.16.ids, s32[16]{0:T(128)} %owner.1, bf16[4,400,1024]{2,1,0:T(8,128)(2,1)} %copy-done.2, bf16[2,64,1152]{2,1,0:T(8,128)(2,1)} %get-tuple-element.14.refs_0_, ...), custom_call_target="tpu_custom_call" | custom-call | flops 209715200 | bytes 3276800 | tf_op jit(solution)/shard_map/rank/pallas_call | solution.py:212
  94.8 0.1 collective-permute-start.9
  94.9 0.4 collective-permute-start.10
  95.2 1.5 %collective-permute-start.11 = (bf16[3,128,128]{2,1,0:T(8,128)(2,1)}, bf16[3,128,128]{2,1,0:T(8,128)(2,1)S(1)}, u32[]{:S(2)}, u32[]{:S(2)}) collective-permute-start(bf16[3,128,128]{2,1,0:T(8,128)(2,1)} %get-tuple-element.17), channel_id=1, source_target_pairs={{0,16},{2,18},{16,0},{18,2},{1,17},{3,19},{17,1},{19,3},{4,20},{6,... | collective-permute-start | bytes 294920 | tf_op jit(solution)/shard_map/ppermute | solution.py:286
  96.7 1.7 %collective-permute-start.12 = (bf16[3,128,128]{2,1,0:T(8,128)(2,1)}, bf16[3,128,128]{2,1,0:T(8,128)(2,1)S(1)}, u32[]{:S(2)}, u32[]{:S(2)}) collective-permute-start(bf16[3,128,128]{2,1,0:T(8,128)(2,1)} %get-tuple-element.18), channel_id=1, source_target_pairs={{0,18},{2,16},{16,2},{18,0},{1,19},{3,17},{17,3},{19,1},{4,22},{6,... | collective-permute-start | bytes 294920 | tf_op jit(solution)/shard_map/ppermute | solution.py:286
  98.4 0.0 collective-permute-start.13
  98.4 1.9 %collective-permute-done.10.refs_1_ = bf16[3,128,128]{2,1,0:T(8,128)(2,1)S(1)} collective-permute-done((bf16[3,128,128]{2,1,0:T(8,128)(2,1)}, bf16[3,128,128]{2,1,0:T(8,128)(2,1)S(1)}, u32[]{:S(2)}, u32[]{:S(2)}) %collective-permute-start.10) | collective-permute-done | bytes 98336 | tf_op jit(solution)/shard_map/ppermute | solution.py:286
  100.3 0.0 collective-permute-start.14
  100.3 0.0 collective-permute-done.11.refs_2_
  100.3 0.5 collective-permute-start.15
  100.8 2.8 %collective-permute-done.12.refs_3_ = bf16[3,128,128]{2,1,0:T(8,128)(2,1)S(1)} collective-permute-done((bf16[3,128,128]{2,1,0:T(8,128)(2,1)}, bf16[3,128,128]{2,1,0:T(8,128)(2,1)S(1)}, u32[]{:S(2)}, u32[]{:S(2)}) %collective-permute-start.12) | collective-permute-done | bytes 98336 | tf_op jit(solution)/shard_map/ppermute | solution.py:286
  103.6 0.0 collective-permute-start.16
  103.6 0.0 collective-permute-done.13.refs_4_
  103.6 1.3 %collective-permute-done.16.refs_7_ = bf16[3,128,128]{2,1,0:T(8,128)(2,1)S(1)} collective-permute-done((bf16[3,128,128]{2,1,0:T(8,128)(2,1)S(1)}, bf16[3,128,128]{2,1,0:T(8,128)(2,1)S(1)}, u32[]{:S(2)}, u32[]{:S(2)}) %collective-permute-start.16) | collective-permute-done | bytes 98336 | tf_op jit(solution)/shard_map/ppermute | solution.py:270
  104.9 0.0 collective-permute-done.9.base_b
  104.9 0.9 copy-done.1
  105.8 1.0 final.1
  (15 shorter events, 0.0 us)
Async XLA Ops:
  2.0 7.3 %collective-permute-start = (bf16[1,64,1152]{2,1,0:T(8,128)(2,1)}, bf16[1,64,1152]{2,1,0:T(8,128)(2,1)S(1)}, u32[]{:S(2)}, u32[]{:S(2)}) collective-permute-start(bf16[1,64,1152]{2,1,0:T(8,128)(2,1)} %get-tuple-element.12), channel_id=1, source_target_pairs={{0,2},{2,0},{1,3},{3,1},{4,6},{6,4},{5,7},{7,5},{8,10},{10,8},{9,1... | collective-permute-start | bytes 442376 | tf_op jit(solution)/shard_map/ppermute | solution.py:305
  9.3 0.7 copy-start.3
  10.0 9.5 %copy-start.4 = (bf16[1,64,1152]{2,1,0:T(8,128)(2,1)S(1)}, bf16[1,64,1152]{2,1,0:T(8,128)(2,1)}, u32[]{:S(2)}) copy-start(bf16[1,64,1152]{2,1,0:T(8,128)(2,1)} %copy-done.3) | copy-start | bytes 442372
  10.0 67.1 %all-to-all-start = ((bf16[4,400,1024]{2,1,0:T(8,128)(2,1)}), bf16[4,400,1024]{2,1,0:T(8,128)(2,1)S(1)}, u32[]{:S(2)}, u32[]{:S(2)}) async-start(bf16[4,400,1024]{2,1,0:T(8,128)(2,1)} %hand.4), calls=%async_computation | async-start | bytes 6553600 | tf_op jit(solution)/shard_map/all_to_all | solution.py:273
  13.9 44.9 %collective-permute-start.2 = (bf16[2,64,1152]{2,1,0:T(8,128)(2,1)}, bf16[2,64,1152]{2,1,0:T(8,128)(2,1)}, u32[]{:S(2)}, u32[]{:S(2)}) collective-permute-start(bf16[2,64,1152]{2,1,0:T(8,128)(2,1)} %get-tuple-element.14.refs_0_), channel_id=1, source_target_pairs={{0,12},{4,0},{8,4},{12,8},{1,13},{5,1},{9,5},{13,9},{2,14},{6,2},{... | collective-permute-start | bytes 884744 | tf_op jit(solution)/shard_map/ppermute | solution.py:276
  17.5 41.2 %collective-permute-start.3 = (bf16[2,64,1152]{2,1,0:T(8,128)(2,1)}, bf16[2,64,1152]{2,1,0:T(8,128)(2,1)}, u32[]{:S(2)}, u32[]{:S(2)}) collective-permute-start(bf16[2,64,1152]{2,1,0:T(8,128)(2,1)} %get-tuple-element.14.refs_0_), channel_id=1, source_target_pairs={{0,4},{4,8},{8,12},{12,0},{1,5},{5,9},{9,13},{13,1},{2,6},{6,10},{... | collective-permute-start | bytes 884744 | tf_op jit(solution)/shard_map/ppermute | solution.py:276
  17.5 36.9 %collective-permute-start.1 = (bf16[1,64,1152]{2,1,0:T(8,128)(2,1)}, bf16[1,64,1152]{2,1,0:T(8,128)(2,1)S(1)}, u32[]{:S(2)}, u32[]{:S(2)}) collective-permute-start(bf16[1,64,1152]{2,1,0:T(8,128)(2,1)} %get-tuple-element.13), channel_id=1, source_target_pairs={{0,2},{2,0},{1,3},{3,1},{4,6},{6,4},{5,7},{7,5},{8,10},{10,8},{9,1... | collective-permute-start | bytes 442376 | tf_op jit(solution)/shard_map/ppermute | solution.py:305
  55.1 18.1 %collective-permute-start.6 = (bf16[2,64,1152]{2,1,0:T(8,128)(2,1)}, bf16[2,64,1152]{2,1,0:T(8,128)(2,1)}, u32[]{:S(2)}, u32[]{:S(2)}) collective-permute-start(bf16[2,64,1152]{2,1,0:T(8,128)(2,1)} %constant_dynamic-update-slice_fusion.refs_0_.refs_4_), channel_id=1, source_target_pairs={{0,12},{4,0},{8,4},{12,8},{1,13},{5,1},{9,5},{13,9},{2,14},{6,2},{... | collective-permute-start | bytes 884744 | tf_op jit(solution)/shard_map/ppermute | solution.py:276
  58.7 14.5 %collective-permute-start.7 = (bf16[2,64,1152]{2,1,0:T(8,128)(2,1)}, bf16[2,64,1152]{2,1,0:T(8,128)(2,1)}, u32[]{:S(2)}, u32[]{:S(2)}) collective-permute-start(bf16[2,64,1152]{2,1,0:T(8,128)(2,1)} %constant_dynamic-update-slice_fusion.refs_0_.refs_4_), channel_id=1, source_target_pairs={{0,4},{4,8},{8,12},{12,0},{1,5},{5,9},{9,13},{13,1},{2,6},{6,10},{... | collective-permute-start | bytes 884744 | tf_op jit(solution)/shard_map/ppermute | solution.py:276
  59.3 13.3 %collective-permute-start.4 = (bf16[16,128]{1,0:T(8,128)(2,1)}, bf16[16,128]{1,0:T(8,128)(2,1)S(1)}, u32[]{:S(2)}, u32[]{:S(2)}) collective-permute-start(bf16[16,128]{1,0:T(8,128)(2,1)} %go.1), channel_id=1, source_target_pairs={{0,1},{1,0},{2,3},{3,2},{4,5},{5,4},{6,7},{7,6},{8,9},{9,8},{10,11... | collective-permute-start | bytes 12296 | tf_op jit(solution)/shard_map/ppermute | solution.py:270
  72.6 0.6 copy-start.5
  73.2 12.0 %collective-permute-start.5 = (bf16[2,64,1152]{2,1,0:T(8,128)(2,1)}, bf16[2,64,1152]{2,1,0:T(8,128)(2,1)}, u32[]{:S(2)}, u32[]{:S(2)}) collective-permute-start(bf16[2,64,1152]{2,1,0:T(8,128)(2,1)} %hand.5.refs_3_), channel_id=1, source_target_pairs={{0,4},{4,8},{8,12},{12,0},{1,5},{5,9},{9,13},{13,1},{2,6},{6,10},{... | collective-permute-start | bytes 884744 | tf_op jit(solution)/shard_map/ppermute | solution.py:276
  73.2 16.1 %collective-permute-start.8 = (bf16[2,64,1152]{2,1,0:T(8,128)(2,1)}, bf16[2,64,1152]{2,1,0:T(8,128)(2,1)}, u32[]{:S(2)}, u32[]{:S(2)}) collective-permute-start(bf16[2,64,1152]{2,1,0:T(8,128)(2,1)} %hand.6.refs_5_), channel_id=1, source_target_pairs={{0,12},{4,0},{8,4},{12,8},{1,13},{5,1},{9,5},{13,9},{2,14},{6,2},{... | collective-permute-start | bytes 884744 | tf_op jit(solution)/shard_map/ppermute | solution.py:276
  77.1 1.7 %copy-start.2 = (bf16[4,400,1024]{2,1,0:T(8,128)(2,1)}, bf16[4,400,1024]{2,1,0:T(8,128)(2,1)S(1)}, u32[]{:S(2)}) copy-start(bf16[4,400,1024]{2,1,0:T(8,128)(2,1)S(1)} %all-to-all-done.tok) | copy-start | bytes 9830404
  79.4 25.5 %copy-start = (f32[384,512]{1,0:T(8,128)S(1)}, f32[384,512]{1,0:T(8,128)}, u32[]{:S(2)}) copy-start(f32[384,512]{1,0:T(8,128)} %base.2.refs_4_.base_a) | copy-start | bytes 2359300
  94.8 10.1 %collective-permute-start.9 = (f32[384,512]{1,0:T(8,128)}, f32[384,512]{1,0:T(8,128)S(1)}, u32[]{:S(2)}, u32[]{:S(2)}) collective-permute-start(f32[384,512]{1,0:T(8,128)} %hand.7), channel_id=1, source_target_pairs={{0,1},{1,0},{2,3},{3,2},{4,5},{5,4},{6,7},{7,6},{8,9},{9,8},{10,11... | collective-permute-start | bytes 2359304 | tf_op jit(solution)/shard_map/ppermute | solution.py:270
  94.9 5.4 %collective-permute-start.10 = (bf16[3,128,128]{2,1,0:T(8,128)(2,1)}, bf16[3,128,128]{2,1,0:T(8,128)(2,1)S(1)}, u32[]{:S(2)}, u32[]{:S(2)}) collective-permute-start(bf16[3,128,128]{2,1,0:T(8,128)(2,1)} %get-tuple-element.16), channel_id=1, source_target_pairs={{0,2},{2,0},{16,18},{18,16},{1,3},{3,1},{17,19},{19,17},{4,6},{6,4... | collective-permute-start | bytes 294920 | tf_op jit(solution)/shard_map/ppermute | solution.py:286
  95.2 5.1 %collective-permute-start.11 = (bf16[3,128,128]{2,1,0:T(8,128)(2,1)}, bf16[3,128,128]{2,1,0:T(8,128)(2,1)S(1)}, u32[]{:S(2)}, u32[]{:S(2)}) collective-permute-start(bf16[3,128,128]{2,1,0:T(8,128)(2,1)} %get-tuple-element.17), channel_id=1, source_target_pairs={{0,16},{2,18},{16,0},{18,2},{1,17},{3,19},{17,1},{19,3},{4,20},{6,... | collective-permute-start | bytes 294920 | tf_op jit(solution)/shard_map/ppermute | solution.py:286
  96.7 6.9 %collective-permute-start.12 = (bf16[3,128,128]{2,1,0:T(8,128)(2,1)}, bf16[3,128,128]{2,1,0:T(8,128)(2,1)S(1)}, u32[]{:S(2)}, u32[]{:S(2)}) collective-permute-start(bf16[3,128,128]{2,1,0:T(8,128)(2,1)} %get-tuple-element.18), channel_id=1, source_target_pairs={{0,18},{2,16},{16,2},{18,0},{1,19},{3,17},{17,3},{19,1},{4,22},{6,... | collective-permute-start | bytes 294920 | tf_op jit(solution)/shard_map/ppermute | solution.py:286
  98.4 5.2 %collective-permute-start.13 = (bf16[3,128,128]{2,1,0:T(8,128)(2,1)}, bf16[3,128,128]{2,1,0:T(8,128)(2,1)S(1)}, u32[]{:S(2)}, u32[]{:S(2)}) collective-permute-start(bf16[3,128,128]{2,1,0:T(8,128)(2,1)} %get-tuple-element.15.refs_1_.refs_0_), channel_id=1, source_target_pairs={{0,1},{1,0},{2,3},{3,2},{4,5},{5,4},{6,7},{7,6},{8,9},{9,8},{10,11... | collective-permute-start | bytes 294920 | tf_op jit(solution)/shard_map/ppermute | solution.py:270
  100.3 3.3 %collective-permute-start.14 = (bf16[3,128,128]{2,1,0:T(8,128)(2,1)S(1)}, bf16[3,128,128]{2,1,0:T(8,128)(2,1)S(1)}, u32[]{:S(2)}, u32[]{:S(2)}) collective-permute-start(bf16[3,128,128]{2,1,0:T(8,128)(2,1)S(1)} %collective-permute-done.10.refs_1_), channel_id=1, source_target_pairs={{0,1},{1,0},{2,3},{3,2},{4,5},{5,4},{6,7},{7,6},{8,9},{9,8},{10,11... | collective-permute-start | bytes 294920 | tf_op jit(solution)/shard_map/ppermute | solution.py:270
  100.3 3.3 %collective-permute-start.15 = (bf16[3,128,128]{2,1,0:T(8,128)(2,1)S(1)}, bf16[3,128,128]{2,1,0:T(8,128)(2,1)S(1)}, u32[]{:S(2)}, u32[]{:S(2)}) collective-permute-start(bf16[3,128,128]{2,1,0:T(8,128)(2,1)S(1)} %collective-permute-done.11.refs_2_), channel_id=1, source_target_pairs={{0,1},{1,0},{2,3},{3,2},{4,5},{5,4},{6,7},{7,6},{8,9},{9,8},{10,11... | collective-permute-start | bytes 294920 | tf_op jit(solution)/shard_map/ppermute | solution.py:270
  103.6 1.3 %collective-permute-start.16 = (bf16[3,128,128]{2,1,0:T(8,128)(2,1)S(1)}, bf16[3,128,128]{2,1,0:T(8,128)(2,1)S(1)}, u32[]{:S(2)}, u32[]{:S(2)}) collective-permute-start(bf16[3,128,128]{2,1,0:T(8,128)(2,1)S(1)} %collective-permute-done.12.refs_3_), channel_id=1, source_target_pairs={{0,1},{1,0},{2,3},{3,2},{4,5},{5,4},{6,7},{7,6},{8,9},{9,8},{10,11... | collective-permute-start | bytes 294920 | tf_op jit(solution)/shard_map/ppermute | solution.py:270
  104.9 0.9 copy-start.1

commit v11 on v10

--- a/solution.py
+++ b/solution.py
@@ -31,20 +31,6 @@
         input_output_aliases={0: 0},
         name="hand",
     )(x, *after)
-
-
-def go_kernel(*refs):
-    refs[-1][...] = jnp.zeros(refs[-1].shape, refs[-1].dtype)
-
-
-def go_after(*arrays):
-    return pl.pallas_call(
-        go_kernel,
-        in_specs=[ANY] * len(arrays),
-        out_specs=VMEM,
-        out_shape=jax.ShapeDtypeStruct((16, LANES), jnp.bfloat16),
-        name="go",
-    )(*arrays)
 
 
 def pack_kernel(ways, down, up, *refs):
@@ -57,10 +43,7 @@
         start = pl.multiple_of(share * feats, LANES)
         tile = pl.multiple_of(lax.rem(share, up.shape[2] // LANES) * LANES, LANES)
         for a in range(adapters):
-            if way == 0:
-                to = outs[0].at[a]
-            else:
-                to = outs[1 + (way - 1) * adapters + a].at[0]
+            to = outs[adapters + way - 1].at[a] if way else outs[a].at[0]
             sem = sems.at[way, a]
             copies.append(pltpu.make_async_copy(down.at[a, :, pl.ds(start, feats)], to.at[:, :feats], sem.at[0]))
             copies.append(pltpu.make_async_copy(up.at[a, :, pl.ds(tile, LANES)], to.at[:, feats:], sem.at[1]))
@@ -73,7 +56,7 @@
 def pack(down, up, shares, ways):
     adapters, rank, feats = down.shape
     wide = feats // shares + LANES
-    shapes = [(adapters, rank, wide)] + [(1, rank, wide)] * (adapters * (ways - 1))
+    shapes = [(1, rank, wide)] * adapters + [(adapters, rank, wide)] * (ways - 1)
     outs = pl.pallas_call(
         functools.partial(pack_kernel, ways),
         in_specs=[HBM, HBM],
@@ -82,7 +65,7 @@
         scratch_shapes=[pltpu.SemaphoreType.DMA((ways, adapters, 2))],
         name="pack",
     )(down, up)
-    return outs[0], [outs[1 + w * adapters : 1 + (w + 1) * adapters] for w in range(ways - 1)]
+    return outs[:adapters], outs[adapters:]
 
 
 def spread_kernel(lengths, ids, in_ref, out_ref):
@@ -172,13 +155,16 @@
     shares = groups * pair
     tok_held, held, tok_sems, sems = refs[-4:]
     outs = refs[-4 - shares : -4]
-    pieces = refs[: ring * pair]
-    per, rank = pieces[0].shape[:2]
+    pieces = refs[: len(refs) - 4 - shares]
+    per, rank = owner.shape[0] // (ring * pair), pieces[0].shape[1]
     blocks, _, block = outs[0].shape
     feats = tok.shape[2]
     z, y = lax.axis_index("ring"), lax.axis_index("pair")
     mates = [mate_at(k, 1, groups, pair) for k in range(shares)]
-    copies = [pltpu.make_async_copy(piece, held.at[pl.ds(j * per, per)], sems.at[j]) for j, piece in enumerate(pieces)]
+    copies, start = [], 0
+    for j, piece in enumerate(pieces):
+        copies.append(pltpu.make_async_copy(piece, held.at[pl.ds(start, piece.shape[0])], sems.at[j]))
+        start += piece.shape[0]
     tok_copies = [
         pltpu.make_async_copy(tok.at[mates[k], : blocks * block, :], tok_held.at[k], tok_sems.at[k])
         for k in range(shares)
@@ -208,7 +194,7 @@
 def rank_parts(ids, owner, tok, pieces, groups, ring, pair, blocks):
     shares, tall, feats = tok.shape
     block = tall // blocks // LANES * LANES
-    per, rank, wide = pieces[0].shape
+    _, rank, wide = pieces[0].shape
     return pl.pallas_call(
         functools.partial(rank_kernel, groups, ring, pair),
         in_specs=[SMEM, SMEM, ANY] + [ANY] * len(pieces),
@@ -216,7 +202,7 @@
         out_shape=[jax.ShapeDtypeStruct((blocks, 2 * rank, block), tok.dtype)] * shares,
         scratch_shapes=[
             pltpu.VMEM((shares, blocks * block, feats), tok.dtype),
-            pltpu.VMEM((len(pieces) * per, rank, wide), tok.dtype),
+            pltpu.VMEM((owner.shape[0], rank, wide), tok.dtype),
             pltpu.SemaphoreType.DMA((shares,)),
             pltpu.SemaphoreType.DMA((len(pieces),)),
         ],
@@ -299,25 +285,17 @@
 
     own, others = pack(jnp.swapaxes(adapter_down, 1, 2), adapter_up, shares, pair)
     slabs = spread(tokens, lengths, adapter_ids.reshape(-1), shares)
-    swapped, first_in = [], []
-    for w in range(1, pair):
-        back = [(a, (a - w) % pair) for a in range(pair)]
-        halves = [lax.ppermute(piece, "pair", back) for piece in others[pair - w - 1]]
-        swapped.append(jnp.concatenate(halves))
-        first_in.append(halves[0])
-    firsts = [first_hops(piece) for piece in [own] + swapped]
-    go = across(go_after(*(firsts[0][k] for k in firsts[0] if k > 0)))
-    tok = to_plane(hand_on(slabs, *first_in))
+    swapped = [lax.ppermute(others[pair - w - 1], "pair", [(a, (a - w) % pair) for a in range(pair)]) for w in range(1, pair)]
+    own_firsts = [first_hops(piece) for piece in own]
+    firsts = [first_hops(piece) for piece in swapped]
+    tok = to_plane(hand_on(slabs, *swapped, *(own_firsts[0][k] for k in own_firsts[0] if k > 0)))
     ids = tok[:, rows, :blocks].astype(jnp.int32).reshape(-1)
 
     base_out = base_half(tokens, base_key, (t + 1) % sides, sides, lengths, *swapped)
     base_mine = base_half(tokens, base_key, t, sides, lengths, *swapped)
-    pieces = [
-        more_hops(held, way, go, base_out, base_mine)
-        for way, held in enumerate(firsts)
-    ]
-
-    flat = [piece for way in pieces for piece in way]
+    own_pieces = [more_hops(held, 0, base_out, base_mine) for held in own_firsts]
+    pieces = [more_hops(held, 1 + way, base_out, base_mine) for way, held in enumerate(firsts)]
+    flat = [piece for same in zip(*own_pieces) for piece in same] + [piece for way in pieces for piece in way]
     parts = rank_parts(ids, owner_slot, tok, flat, groups, ring, pair, blocks)
     mine = [parts[0]] + [in_plane(parts[k], k // pair, k % pair) for k in range(1, shares)]
     theirs = [across(part) for part in mine]

time: 107 us -> 78.5 us (0.73)
  waiting for transfers between devices: 50.2 us -> 21.4 us
    ppermute x2 -> x1, waiting for transfers between devices: 34.3 us -> 0.01 us  [body(): lax.ppermute(others[pair - w - 1], 'pair', [(a, (a - w) % pair) for a in...]
    all_to_all x1, waiting for transfers between devices: 0.01 us -> 13.1 us  [to_plane(): return lax.all_to_all(x, PLANE, split_axis=0, concat_axis=0, tiled=True)]
    ppermute x6 -> x9, waiting for transfers between devices: 9.91 us -> 1.89 us  [along(): lax.ppermute(x, 'ring', [(a, (a + step) % ring) for a in range(ring)])]
    ppermute x6 -> x9, starting transfers between devices: 11.1 us -> 14.1 us  [along(): lax.ppermute(x, 'ring', [(a, (a + step) % ring) for a in range(ring)])]
    ppermute x2 -> x1, starting transfers between devices: 5 us -> 3.03 us  [body(): lax.ppermute(others[pair - w - 1], 'pair', [(a, (a - w) % pair) for a in...]
    unnamed x13 -> x16, local copies, waits for them, and re-layouts: 4.46 us -> 5.19 us
  transfers between devices with their start and end apart: 18 -> 19, of which waited for: 6 -> 7; matrix products, arithmetic and copies ran while one was open for 2% -> 1% of each run, Pallas kernels for 17% -> 22%
where the time goes in v11:
time: 78.5 us; the launch traced here: 78 us
  Pallas kernels  26.2 us (33%)
  starting transfers between devices  24.5 us (31%)
  waiting for transfers between devices  21.4 us (27%)
  local copies, waits for them, and re-layouts  5.81 us (7%)
    ppermute x9, starting transfers between devices, along(): lax.ppermute(x, 'ring', [(a, (a + step) % ring) for a in range(ring)])  14.1 us
    pallas_call x2, Pallas kernels, base_half(): pl.pallas_call(base_kernel, grid_spec=pltpu.PrefetchScalarGridSpec(num_sc...  13.2 us
    all_to_all x1, waiting for transfers between devices, to_plane(): return lax.all_to_all(x, PLANE, split_axis=0, concat_axis=0, tiled=True)  13.1 us
    pallas_call x1, Pallas kernels, rank_parts(): pl.pallas_call(functools.partial(rank_kernel, groups, ring, pair), in_spe...  5.58 us
    unnamed x16, local copies, waits for them, and re-layouts  5.19 us
    ppermute x3, waiting for transfers between devices, in_plane(): return lax.ppermute(x, PLANE, pairs)  5.15 us
    pallas_call x1, Pallas kernels, spread(): pl.pallas_call(spread_kernel, grid=(shares,), in_specs=[SMEM, SMEM, pl.Bl...  4.28 us
    all_to_all x1, starting transfers between devices, to_plane(): return lax.all_to_all(x, PLANE, split_axis=0, concat_axis=0, tiled=True)  3.71 us
  transfers between devices with their start and end apart: 19, of which 7 were waited for; matrix products, arithmetic and copies ran while one was open for 1% of the time, Pallas kernels for 22%

profile of v11, /device:TPU:0, one launch (start us, length us, event | category | flops | bytes accessed | tf_op | source)
XLA Modules:
  0.0 78.0 jit_solution(14358492565945012666)
XLA Ops:
  0.0 2.0 %pack.1 = (bf16[1,64,1152]{2,1,0:T(8,128)(2,1)}, bf16[1,64,1152]{2,1,0:T(8,128)(2,1)}, bf16[2,64,1152]{2,1,0:T(8,128)(2,1)}) custom-call(bf16[2,64,4096]{2,1,0:T(8,128)(2,1)} %bitcast.4, bf16[2,64,512]{2,1,0:T(8,128)(2,1)} %up.1), custom_call_target="tpu_custom_call" | custom-call | tf_op jit(solution)/shard_map/pack/pallas_call | solution.py:60
  2.0 3.0 %collective-permute-start = (bf16[2,64,1152]{2,1,0:T(8,128)(2,1)}, bf16[2,64,1152]{2,1,0:T(8,128)(2,1)S(1)}, u32[]{:S(2)}, u32[]{:S(2)}) collective-permute-start(bf16[2,64,1152]{2,1,0:T(8,128)(2,1)} %get-tuple-element.12), channel_id=1, source_target_pairs={{0,2},{2,0},{1,3},{3,1},{4,6},{6,4},{5,7},{7,5},{8,10},{10,8},{9,1... | collective-permute-start | bytes 884744 | tf_op jit(solution)/shard_map/ppermute | solution.py:288
  5.1 1.6 %collective-permute-start.1 = (bf16[1,64,1152]{2,1,0:T(8,128)(2,1)}, bf16[1,64,1152]{2,1,0:T(8,128)(2,1)S(1)}, u32[]{:S(2)}, u32[]{:S(2)}) collective-permute-start(bf16[1,64,1152]{2,1,0:T(8,128)(2,1)} %get-tuple-element.13.refs_0_), channel_id=1, source_target_pairs={{0,4},{4,8},{8,12},{12,0},{1,5},{5,9},{9,13},{13,1},{2,6},{6,10},{... | collective-permute-start | bytes 442376 | tf_op jit(solution)/shard_map/ppermute | solution.py:262
  6.6 2.2 %collective-permute-start.2 = (bf16[1,64,1152]{2,1,0:T(8,128)(2,1)}, bf16[1,64,1152]{2,1,0:T(8,128)(2,1)S(1)}, u32[]{:S(2)}, u32[]{:S(2)}) collective-permute-start(bf16[1,64,1152]{2,1,0:T(8,128)(2,1)} %get-tuple-element.13.refs_0_), channel_id=1, source_target_pairs={{0,12},{4,0},{8,4},{12,8},{1,13},{5,1},{9,5},{13,9},{2,14},{6,2},{... | collective-permute-start | bytes 442376 | tf_op jit(solution)/shard_map/ppermute | solution.py:262
  8.9 4.3 %spread.1.refs_0_ = bf16[4,400,1024]{2,1,0:T(8,128)(2,1)} custom-call(s32[3]{0:T(128)} %lengths.5, s32[3]{0:T(128)} %bitcast.5, bf16[384,4096]{1,0:T(8,128)(2,1)} %in_ref.1), custom_call_target="tpu_custom_call" | custom-call | tf_op jit(solution)/shard_map/spread/pallas_call | solution.py:90
  13.2 0.7 collective-permute-done.1.refs_2_.refs_0_
  13.8 1.2 %collective-permute-done.2.refs_3_.refs_1_.refs_2_ = bf16[1,64,1152]{2,1,0:T(8,128)(2,1)S(1)} collective-permute-done((bf16[1,64,1152]{2,1,0:T(8,128)(2,1)}, bf16[1,64,1152]{2,1,0:T(8,128)(2,1)S(1)}, u32[]{:S(2)}, u32[]{:S(2)}) %collective-permute-start.2) | collective-permute-done | bytes 147488 | tf_op jit(solution)/shard_map/ppermute | solution.py:262
  15.0 0.0 collective-permute-done.refs_0_.refs_1_.refs_8_
  15.1 0.6 copy-done.4
  15.7 0.7 copy-done.3
  16.4 3.7 %all-to-all-start = ((bf16[4,400,1024]{2,1,0:T(8,128)(2,1)}), bf16[4,400,1024]{2,1,0:T(8,128)(2,1)S(1)}, u32[]{:S(2)}, u32[]{:S(2)}) async-start(bf16[4,400,1024]{2,1,0:T(8,128)(2,1)} %hand.5), calls=%async_computation | async-start | bytes 6553600 | tf_op jit(solution)/shard_map/all_to_all | solution.py:259
  20.1 2.4 %collective-permute-start.7 = (bf16[2,64,1152]{2,1,0:T(8,128)(2,1)}, bf16[2,64,1152]{2,1,0:T(8,128)(2,1)}, u32[]{:S(2)}, u32[]{:S(2)}) collective-permute-start(bf16[2,64,1152]{2,1,0:T(8,128)(2,1)} %copy-done.3), channel_id=1, source_target_pairs={{0,12},{4,0},{8,4},{12,8},{1,13},{5,1},{9,5},{13,9},{2,14},{6,2},{... | collective-permute-start | bytes 884744 | tf_op jit(solution)/shard_map/ppermute | solution.py:262
  22.6 0.0 collective-permute-start.8
  22.6 3.8 %collective-permute-start.3 = (bf16[1,64,1152]{2,1,0:T(8,128)(2,1)}, bf16[1,64,1152]{2,1,0:T(8,128)(2,1)S(1)}, u32[]{:S(2)}, u32[]{:S(2)}) collective-permute-start(bf16[1,64,1152]{2,1,0:T(8,128)(2,1)} %get-tuple-element.14.refs_1_), channel_id=1, source_target_pairs={{0,12},{4,0},{8,4},{12,8},{1,13},{5,1},{9,5},{13,9},{2,14},{6,2},{... | collective-permute-start | bytes 442376 | tf_op jit(solution)/shard_map/ppermute | solution.py:262
  26.4 0.0 collective-permute-start.5
  26.4 6.6 %base.2.refs_3_.base_a = f32[384,512]{1,0:T(8,128)} custom-call(s32[1]{0:T(128)} %bitcast.side, s32[3]{0:T(128)} %lengths.5, bf16[384,4096]{1,0:T(8,128)(2,1)} %in_ref.1, bf16[4096,1024]{1,0:T(8,128)(2,1)} %key_ref.3, bf16[2,64,1152]{2,1,0:T(8,128)(2,1)} %copy-done.3), custom_call_target="tpu_custom_call" | custom-call | tf_op jit(solution)/shard_map/base/pallas_call | solution.py:127
  33.0 6.6 %base.3.refs_2_.refs_0_ = f32[384,512]{1,0:T(8,128)} custom-call(s32[1]{0:T(128)} %bitcast.2.side, s32[3]{0:T(128)} %lengths.5, bf16[384,4096]{1,0:T(8,128)(2,1)} %in_ref.1, bf16[4096,1024]{1,0:T(8,128)(2,1)} %key_ref.3, bf16[2,64,1152]{2,1,0:T(8,128)(2,1)} %copy-done.3), custom_call_target="tpu_custom_call" | custom-call | tf_op jit(solution)/shard_map/base/pallas_call | solution.py:127
  39.6 0.0 collective-permute-done.7.refs_0_
  39.6 0.0 collective-permute-done.8.refs_1_.refs_11_
  39.6 3.9 %collective-permute-start.9 = (bf16[2,64,1152]{2,1,0:T(8,128)(2,1)}, bf16[2,64,1152]{2,1,0:T(8,128)(2,1)}, u32[]{:S(2)}, u32[]{:S(2)}) collective-permute-start(bf16[2,64,1152]{2,1,0:T(8,128)(2,1)} %hand.8.refs_9_), channel_id=1, source_target_pairs={{0,12},{4,0},{8,4},{12,8},{1,13},{5,1},{9,5},{13,9},{2,14},{6,2},{... | collective-permute-start | bytes 884744 | tf_op jit(solution)/shard_map/ppermute | solution.py:262
  43.5 0.0 collective-permute-start.4
  43.5 0.0 collective-permute-done.3.refs_1_.refs_3_
  43.5 0.0 collective-permute-done.5.refs_0_
  43.5 0.6 copy-done.6
  44.2 0.2 collective-permute-start.6
  44.4 13.1 %all-to-all-done.tok = bf16[4,400,1024]{2,1,0:T(8,128)(2,1)S(1)} async-done(((bf16[4,400,1024]{2,1,0:T(8,128)(2,1)}), bf16[4,400,1024]{2,1,0:T(8,128)(2,1)S(1)}, u32[]{:S(2)}, u32[]{:S(2)}) %all-to-all-start) | async-done | bytes 3276832 | tf_op jit(solution)/shard_map/all_to_all | solution.py:259
  57.4 1.6 %copy-done.2 = bf16[4,400,1024]{2,1,0:T(8,128)(2,1)} copy-done((bf16[4,400,1024]{2,1,0:T(8,128)(2,1)}, bf16[4,400,1024]{2,1,0:T(8,128)(2,1)S(1)}, u32[]{:S(2)}) %copy-start.2) | copy-done | bytes 3276824
  59.1 0.6 reshape.16.ids
  59.7 0.0 collective-permute-done.4.refs_4_
  59.7 0.0 collective-permute-done.9.refs_10_
  59.7 0.6 copy-done.7
  60.4 5.6 %rank.1 = (bf16[3,128,128]{2,1,0:T(8,128)(2,1)}, bf16[3,128,128]{2,1,0:T(8,128)(2,1)}, bf16[3,128,128]{2,1,0:T(8,128)(2,1)}, bf16[3,128,128]{2,1,0:T(8,128)(2,1)}) custom-call(s32[12]{0:T(128)} %reshape.16.ids, s32[16]{0:T(128)} %owner.1, bf16[4,400,1024]{2,1,0:T(8,128)(2,1)} %copy-done.2, bf16[1,64,1152]{2,1,0:T(8,128)(2,1)} %get-tuple-element.13.refs_0_, ...), custom_call_target="tpu_custom_call" | custom-call | flops 209715200 | bytes 3276800 | tf_op jit(solution)/shard_map/rank/pallas_call | solution.py:198
  66.0 0.1 collective-permute-start.10
  66.1 1.5 %collective-permute-start.11 = (bf16[3,128,128]{2,1,0:T(8,128)(2,1)}, bf16[3,128,128]{2,1,0:T(8,128)(2,1)S(1)}, u32[]{:S(2)}, u32[]{:S(2)}) collective-permute-start(bf16[3,128,128]{2,1,0:T(8,128)(2,1)} %get-tuple-element.16), channel_id=1, source_target_pairs={{0,2},{2,0},{16,18},{18,16},{1,3},{3,1},{17,19},{19,17},{4,6},{6,4... | collective-permute-start | bytes 294920 | tf_op jit(solution)/shard_map/ppermute | solution.py:272
  67.6 0.6 collective-permute-start.12
  68.1 1.5 %collective-permute-start.13 = (bf16[3,128,128]{2,1,0:T(8,128)(2,1)}, bf16[3,128,128]{2,1,0:T(8,128)(2,1)S(1)}, u32[]{:S(2)}, u32[]{:S(2)}) collective-permute-start(bf16[3,128,128]{2,1,0:T(8,128)(2,1)} %get-tuple-element.18), channel_id=1, source_target_pairs={{0,18},{2,16},{16,2},{18,0},{1,19},{3,17},{17,3},{19,1},{4,22},{6,... | collective-permute-start | bytes 294920 | tf_op jit(solution)/shard_map/ppermute | solution.py:272
  69.6 0.0 collective-permute-start.14
  69.6 1.9 %collective-permute-done.11.refs_1_ = bf16[3,128,128]{2,1,0:T(8,128)(2,1)S(1)} collective-permute-done((bf16[3,128,128]{2,1,0:T(8,128)(2,1)}, bf16[3,128,128]{2,1,0:T(8,128)(2,1)S(1)}, u32[]{:S(2)}, u32[]{:S(2)}) %collective-permute-start.11) | collective-permute-done | bytes 98336 | tf_op jit(solution)/shard_map/ppermute | solution.py:272
  71.5 0.0 collective-permute-start.15
  71.5 1.9 %collective-permute-done.12.refs_2_ = bf16[3,128,128]{2,1,0:T(8,128)(2,1)S(1)} collective-permute-done((bf16[3,128,128]{2,1,0:T(8,128)(2,1)}, bf16[3,128,128]{2,1,0:T(8,128)(2,1)S(1)}, u32[]{:S(2)}, u32[]{:S(2)}) %collective-permute-start.12) | collective-permute-done | bytes 98336 | tf_op jit(solution)/shard_map/ppermute | solution.py:272
  73.4 0.0 collective-permute-start.16
  73.4 1.3 %collective-permute-done.13.refs_3_ = bf16[3,128,128]{2,1,0:T(8,128)(2,1)S(1)} collective-permute-done((bf16[3,128,128]{2,1,0:T(8,128)(2,1)}, bf16[3,128,128]{2,1,0:T(8,128)(2,1)S(1)}, u32[]{:S(2)}, u32[]{:S(2)}) %collective-permute-start.13) | collective-permute-done | bytes 98336 | tf_op jit(solution)/shard_map/ppermute | solution.py:272
  74.8 0.0 collective-permute-done.15.refs_5_
  74.8 0.0 collective-permute-done.16.refs_6_
  74.8 1.3 %collective-permute-done.17.refs_7_ = bf16[3,128,128]{2,1,0:T(8,128)(2,1)S(1)} collective-permute-done((bf16[3,128,128]{2,1,0:T(8,128)(2,1)S(1)}, bf16[3,128,128]{2,1,0:T(8,128)(2,1)S(1)}, u32[]{:S(2)}, u32[]{:S(2)}) %collective-permute-start.17) | collective-permute-done | bytes 98336 | tf_op jit(solution)/shard_map/ppermute | solution.py:256
  76.1 0.0 collective-permute-done.10.base_b
  76.1 0.9 %copy-done.1 = bf16[3,128,128]{2,1,0:T(8,128)(2,1)S(1)} copy-done((bf16[3,128,128]{2,1,0:T(8,128)(2,1)S(1)}, bf16[3,128,128]{2,1,0:T(8,128)(2,1)}, u32[]{:S(2)}) %copy-start.1) | copy-done | bytes 98328
  77.0 1.0 %final.1 = bf16[384,512]{1,0:T(8,128)(2,1)} custom-call(f32[384,512]{1,0:T(8,128)S(1)} %copy-done, f32[384,512]{1,0:T(8,128)S(1)} %collective-permute-done.10.base_b, bf16[3,128,128]{2,1,0:T(8,128)(2,1)S(1)} %copy-done.1, bf16[3,128,128]{2,1,0:T(8,128)(2,1)S(1)} %collective-permute-done.11.refs_1_, bf16[3,128,128]{2,1,0:T(8,128)(2,1)S(1)} %collective-permute-done.12.refs_2_, ...), custom_call_target="tpu_custom_call" | custom-call | tf_op jit(solution)/shard_map/final/pallas_call | solution.py:236
  (19 shorter events, 0.1 us)
Async XLA Ops:
  2.0 13.0 %collective-permute-start = (bf16[2,64,1152]{2,1,0:T(8,128)(2,1)}, bf16[2,64,1152]{2,1,0:T(8,128)(2,1)S(1)}, u32[]{:S(2)}, u32[]{:S(2)}) collective-permute-start(bf16[2,64,1152]{2,1,0:T(8,128)(2,1)} %get-tuple-element.12), channel_id=1, source_target_pairs={{0,2},{2,0},{1,3},{3,1},{4,6},{6,4},{5,7},{7,5},{8,10},{10,8},{9,1... | collective-permute-start | bytes 884744 | tf_op jit(solution)/shard_map/ppermute | solution.py:288
  5.1 8.8 %collective-permute-start.1 = (bf16[1,64,1152]{2,1,0:T(8,128)(2,1)}, bf16[1,64,1152]{2,1,0:T(8,128)(2,1)S(1)}, u32[]{:S(2)}, u32[]{:S(2)}) collective-permute-start(bf16[1,64,1152]{2,1,0:T(8,128)(2,1)} %get-tuple-element.13.refs_0_), channel_id=1, source_target_pairs={{0,4},{4,8},{8,12},{12,0},{1,5},{5,9},{9,13},{13,1},{2,6},{6,10},{... | collective-permute-start | bytes 442376 | tf_op jit(solution)/shard_map/ppermute | solution.py:262
  6.6 8.4 %collective-permute-start.2 = (bf16[1,64,1152]{2,1,0:T(8,128)(2,1)}, bf16[1,64,1152]{2,1,0:T(8,128)(2,1)S(1)}, u32[]{:S(2)}, u32[]{:S(2)}) collective-permute-start(bf16[1,64,1152]{2,1,0:T(8,128)(2,1)} %get-tuple-element.13.refs_0_), channel_id=1, source_target_pairs={{0,12},{4,0},{8,4},{12,8},{1,13},{5,1},{9,5},{13,9},{2,14},{6,2},{... | collective-permute-start | bytes 442376 | tf_op jit(solution)/shard_map/ppermute | solution.py:262
  13.8 1.2 %copy-start.5 = (bf16[1,64,1152]{2,1,0:T(8,128)(2,1)}, bf16[1,64,1152]{2,1,0:T(8,128)(2,1)S(1)}, u32[]{:S(2)}) copy-start(bf16[1,64,1152]{2,1,0:T(8,128)(2,1)S(1)} %collective-permute-done.1.refs_2_.refs_0_) | copy-start | bytes 442372
  15.0 0.7 copy-start.4
  15.7 0.7 copy-start.3
  16.4 41.0 %all-to-all-start = ((bf16[4,400,1024]{2,1,0:T(8,128)(2,1)}), bf16[4,400,1024]{2,1,0:T(8,128)(2,1)S(1)}, u32[]{:S(2)}, u32[]{:S(2)}) async-start(bf16[4,400,1024]{2,1,0:T(8,128)(2,1)} %hand.5), calls=%async_computation | async-start | bytes 6553600 | tf_op jit(solution)/shard_map/all_to_all | solution.py:259
  20.1 19.5 %collective-permute-start.7 = (bf16[2,64,1152]{2,1,0:T(8,128)(2,1)}, bf16[2,64,1152]{2,1,0:T(8,128)(2,1)}, u32[]{:S(2)}, u32[]{:S(2)}) collective-permute-start(bf16[2,64,1152]{2,1,0:T(8,128)(2,1)} %copy-done.3), channel_id=1, source_target_pairs={{0,12},{4,0},{8,4},{12,8},{1,13},{5,1},{9,5},{13,9},{2,14},{6,2},{... | collective-permute-start | bytes 884744 | tf_op jit(solution)/shard_map/ppermute | solution.py:262
  22.6 17.1 %collective-permute-start.8 = (bf16[2,64,1152]{2,1,0:T(8,128)(2,1)}, bf16[2,64,1152]{2,1,0:T(8,128)(2,1)}, u32[]{:S(2)}, u32[]{:S(2)}) collective-permute-start(bf16[2,64,1152]{2,1,0:T(8,128)(2,1)} %copy-done.3), channel_id=1, source_target_pairs={{0,4},{4,8},{8,12},{12,0},{1,5},{5,9},{9,13},{13,1},{2,6},{6,10},{... | collective-permute-start | bytes 884744 | tf_op jit(solution)/shard_map/ppermute | solution.py:262
  22.6 21.0 %collective-permute-start.3 = (bf16[1,64,1152]{2,1,0:T(8,128)(2,1)}, bf16[1,64,1152]{2,1,0:T(8,128)(2,1)S(1)}, u32[]{:S(2)}, u32[]{:S(2)}) collective-permute-start(bf16[1,64,1152]{2,1,0:T(8,128)(2,1)} %get-tuple-element.14.refs_1_), channel_id=1, source_target_pairs={{0,12},{4,0},{8,4},{12,8},{1,13},{5,1},{9,5},{13,9},{2,14},{6,2},{... | collective-permute-start | bytes 442376 | tf_op jit(solution)/shard_map/ppermute | solution.py:262
  26.4 17.2 %collective-permute-start.5 = (bf16[1,64,1152]{2,1,0:T(8,128)(2,1)}, bf16[1,64,1152]{2,1,0:T(8,128)(2,1)}, u32[]{:S(2)}, u32[]{:S(2)}) collective-permute-start(bf16[1,64,1152]{2,1,0:T(8,128)(2,1)} %get-tuple-element.14.refs_1_), channel_id=1, source_target_pairs={{0,4},{4,8},{8,12},{12,0},{1,5},{5,9},{9,13},{13,1},{2,6},{6,10},{... | collective-permute-start | bytes 442376 | tf_op jit(solution)/shard_map/ppermute | solution.py:262
  39.6 20.1 %collective-permute-start.9 = (bf16[2,64,1152]{2,1,0:T(8,128)(2,1)}, bf16[2,64,1152]{2,1,0:T(8,128)(2,1)}, u32[]{:S(2)}, u32[]{:S(2)}) collective-permute-start(bf16[2,64,1152]{2,1,0:T(8,128)(2,1)} %hand.8.refs_9_), channel_id=1, source_target_pairs={{0,12},{4,0},{8,4},{12,8},{1,13},{5,1},{9,5},{13,9},{2,14},{6,2},{... | collective-permute-start | bytes 884744 | tf_op jit(solution)/shard_map/ppermute | solution.py:262
  43.5 16.2 %collective-permute-start.4 = (bf16[1,64,1152]{2,1,0:T(8,128)(2,1)}, bf16[1,64,1152]{2,1,0:T(8,128)(2,1)}, u32[]{:S(2)}, u32[]{:S(2)}) collective-permute-start(bf16[1,64,1152]{2,1,0:T(8,128)(2,1)} %hand.6.refs_6_), channel_id=1, source_target_pairs={{0,4},{4,8},{8,12},{12,0},{1,5},{5,9},{9,13},{13,1},{2,6},{6,10},{... | collective-permute-start | bytes 442376 | tf_op jit(solution)/shard_map/ppermute | solution.py:262
  43.5 0.7 copy-start.6
  44.2 15.5 %collective-permute-start.6 = (bf16[1,64,1152]{2,1,0:T(8,128)(2,1)}, bf16[1,64,1152]{2,1,0:T(8,128)(2,1)S(1)}, u32[]{:S(2)}, u32[]{:S(2)}) collective-permute-start(bf16[1,64,1152]{2,1,0:T(8,128)(2,1)} %hand.7.refs_7_), channel_id=1, source_target_pairs={{0,4},{4,8},{8,12},{12,0},{1,5},{5,9},{9,13},{13,1},{2,6},{6,10},{... | collective-permute-start | bytes 442376 | tf_op jit(solution)/shard_map/ppermute | solution.py:262
  57.4 1.7 %copy-start.2 = (bf16[4,400,1024]{2,1,0:T(8,128)(2,1)}, bf16[4,400,1024]{2,1,0:T(8,128)(2,1)S(1)}, u32[]{:S(2)}) copy-start(bf16[4,400,1024]{2,1,0:T(8,128)(2,1)S(1)} %all-to-all-done.tok) | copy-start | bytes 9830404
  59.7 16.4 %copy-start = (f32[384,512]{1,0:T(8,128)S(1)}, f32[384,512]{1,0:T(8,128)}, u32[]{:S(2)}) copy-start(f32[384,512]{1,0:T(8,128)} %base.2.refs_3_.base_a) | copy-start | bytes 2359300
  59.7 0.7 copy-start.7
  66.0 10.1 %collective-permute-start.10 = (f32[384,512]{1,0:T(8,128)}, f32[384,512]{1,0:T(8,128)S(1)}, u32[]{:S(2)}, u32[]{:S(2)}) collective-permute-start(f32[384,512]{1,0:T(8,128)} %hand.9), channel_id=1, source_target_pairs={{0,1},{1,0},{2,3},{3,2},{4,5},{5,4},{6,7},{7,6},{8,9},{9,8},{10,11... | collective-permute-start | bytes 2359304 | tf_op jit(solution)/shard_map/ppermute | solution.py:256
  66.1 5.4 %collective-permute-start.11 = (bf16[3,128,128]{2,1,0:T(8,128)(2,1)}, bf16[3,128,128]{2,1,0:T(8,128)(2,1)S(1)}, u32[]{:S(2)}, u32[]{:S(2)}) collective-permute-start(bf16[3,128,128]{2,1,0:T(8,128)(2,1)} %get-tuple-element.16), channel_id=1, source_target_pairs={{0,2},{2,0},{16,18},{18,16},{1,3},{3,1},{17,19},{19,17},{4,6},{6,4... | collective-permute-start | bytes 294920 | tf_op jit(solution)/shard_map/ppermute | solution.py:272
  67.6 5.9 %collective-permute-start.12 = (bf16[3,128,128]{2,1,0:T(8,128)(2,1)}, bf16[3,128,128]{2,1,0:T(8,128)(2,1)S(1)}, u32[]{:S(2)}, u32[]{:S(2)}) collective-permute-start(bf16[3,128,128]{2,1,0:T(8,128)(2,1)} %get-tuple-element.17), channel_id=1, source_target_pairs={{0,16},{2,18},{16,0},{18,2},{1,17},{3,19},{17,1},{19,3},{4,20},{6,... | collective-permute-start | bytes 294920 | tf_op jit(solution)/shard_map/ppermute | solution.py:272
  68.1 6.6 %collective-permute-start.13 = (bf16[3,128,128]{2,1,0:T(8,128)(2,1)}, bf16[3,128,128]{2,1,0:T(8,128)(2,1)S(1)}, u32[]{:S(2)}, u32[]{:S(2)}) collective-permute-start(bf16[3,128,128]{2,1,0:T(8,128)(2,1)} %get-tuple-element.18), channel_id=1, source_target_pairs={{0,18},{2,16},{16,2},{18,0},{1,19},{3,17},{17,3},{19,1},{4,22},{6,... | collective-permute-start | bytes 294920 | tf_op jit(solution)/shard_map/ppermute | solution.py:272
  69.6 5.2 %collective-permute-start.14 = (bf16[3,128,128]{2,1,0:T(8,128)(2,1)}, bf16[3,128,128]{2,1,0:T(8,128)(2,1)S(1)}, u32[]{:S(2)}, u32[]{:S(2)}) collective-permute-start(bf16[3,128,128]{2,1,0:T(8,128)(2,1)} %get-tuple-element.15.refs_1_.refs_0_), channel_id=1, source_target_pairs={{0,1},{1,0},{2,3},{3,2},{4,5},{5,4},{6,7},{7,6},{8,9},{9,8},{10,11... | collective-permute-start | bytes 294920 | tf_op jit(solution)/shard_map/ppermute | solution.py:256
  71.5 3.3 %collective-permute-start.15 = (bf16[3,128,128]{2,1,0:T(8,128)(2,1)S(1)}, bf16[3,128,128]{2,1,0:T(8,128)(2,1)S(1)}, u32[]{:S(2)}, u32[]{:S(2)}) collective-permute-start(bf16[3,128,128]{2,1,0:T(8,128)(2,1)S(1)} %collective-permute-done.11.refs_1_), channel_id=1, source_target_pairs={{0,1},{1,0},{2,3},{3,2},{4,5},{5,4},{6,7},{7,6},{8,9},{9,8},{10,11... | collective-permute-start | bytes 294920 | tf_op jit(solution)/shard_map/ppermute | solution.py:256
  73.4 1.4 %collective-permute-start.16 = (bf16[3,128,128]{2,1,0:T(8,128)(2,1)S(1)}, bf16[3,128,128]{2,1,0:T(8,128)(2,1)S(1)}, u32[]{:S(2)}, u32[]{:S(2)}) collective-permute-start(bf16[3,128,128]{2,1,0:T(8,128)(2,1)S(1)} %collective-permute-done.12.refs_2_), channel_id=1, source_target_pairs={{0,1},{1,0},{2,3},{3,2},{4,5},{5,4},{6,7},{7,6},{8,9},{9,8},{10,11... | collective-permute-start | bytes 294920 | tf_op jit(solution)/shard_map/ppermute | solution.py:256
  74.8 1.3 %collective-permute-start.17 = (bf16[3,128,128]{2,1,0:T(8,128)(2,1)S(1)}, bf16[3,128,128]{2,1,0:T(8,128)(2,1)S(1)}, u32[]{:S(2)}, u32[]{:S(2)}) collective-permute-start(bf16[3,128,128]{2,1,0:T(8,128)(2,1)S(1)} %collective-permute-done.13.refs_3_), channel_id=1, source_target_pairs={{0,1},{1,0},{2,3},{3,2},{4,5},{5,4},{6,7},{7,6},{8,9},{9,8},{10,11... | collective-permute-start | bytes 294920 | tf_op jit(solution)/shard_map/ppermute | solution.py:256
  76.1 0.9 %copy-start.1 = (bf16[3,128,128]{2,1,0:T(8,128)(2,1)S(1)}, bf16[3,128,128]{2,1,0:T(8,128)(2,1)}, u32[]{:S(2)}) copy-start(bf16[3,128,128]{2,1,0:T(8,128)(2,1)} %get-tuple-element.15.refs_1_.refs_0_) | copy-start | bytes 294916

commit v12 on v11

--- a/solution.py
+++ b/solution.py
@@ -29,6 +29,7 @@
         out_specs=ANY,
         out_shape=jax.ShapeDtypeStruct(x.shape, x.dtype),
         input_output_aliases={0: 0},
+        compiler_params=BIG,
         name="hand",
     )(x, *after)
 
@@ -63,42 +64,66 @@
         out_specs=[VMEM] * len(shapes),
         out_shape=[jax.ShapeDtypeStruct(shape, down.dtype) for shape in shapes],
         scratch_shapes=[pltpu.SemaphoreType.DMA((ways, adapters, 2))],
+        compiler_params=BIG,
         name="pack",
     )(down, up)
     return outs[:adapters], outs[adapters:]
 
 
-def spread_kernel(lengths, ids, in_ref, out_ref):
+def spread_kernel(lengths, ids, tok, out, held, in_sems, out_sems):
     blocks = lengths.shape[0]
-    rows, step = in_ref.shape
+    shares, tall, step = held.shape
+    rows = tok.shape[0]
     block = rows // blocks
-    row = lax.broadcasted_iota(jnp.int32, (block, step), 0)
-    for b in range(blocks):
-        part = in_ref[b * block : (b + 1) * block, :]
-        out_ref[0, b * block : (b + 1) * block, :] = jnp.where(row < lengths[b], part, jnp.zeros_like(part))
-    extra = out_ref.shape[1] - rows
-    lane = lax.broadcasted_iota(jnp.int32, (extra, step), 1)
-    named = jnp.zeros((extra, step), jnp.float32)
+
+    def read(k, b):
+        here = pl.ds(b * block, block)
+        return pltpu.make_async_copy(tok.at[here, pl.ds(k * step, step)], held.at[k, here, :], in_sems.at[k, b])
+
+    for k in range(shares):
+        for b in range(blocks):
+            read(k, b).start()
+    lane = lax.broadcasted_iota(jnp.int32, (tall - rows, step), 1)
+    named = jnp.zeros((tall - rows, step), jnp.float32)
     for b in range(blocks):
         named = jnp.where(lane == b, ids[b].astype(jnp.float32), named)
-    out_ref[0, rows:, :] = named.astype(out_ref.dtype)
+    named = named.astype(held.dtype)
+    writes = [pltpu.make_async_copy(held.at[k], out.at[k], out_sems.at[k]) for k in range(shares)]
+    for k in range(shares):
+        held[k, rows:, :] = named
+        for b in range(blocks):
+            read(k, b).wait()
+
+            @pl.when(lengths[b] < block)
+            def _():
+                here = slice(b * block, (b + 1) * block)
+                row = lax.broadcasted_iota(jnp.int32, (block, step), 0)
+                part = held[k, here, :]
+                held[k, here, :] = jnp.where(row < lengths[b], part, jnp.zeros_like(part))
+
+        writes[k].start()
+    for write in writes:
+        write.wait()
 
 
 def spread(tokens, lengths, ids, shares):
     rows, feats = tokens.shape
-    step = feats // shares
+    shape = (shares, rows + 16, feats // shares)
     return pl.pallas_call(
         spread_kernel,
-        grid=(shares,),
-        in_specs=[SMEM, SMEM, pl.BlockSpec((rows, step), lambda i: (0, i))],
-        out_specs=pl.BlockSpec((1, rows + 16, step), lambda i: (i, 0, 0)),
-        out_shape=jax.ShapeDtypeStruct((shares, rows + 16, step), tokens.dtype),
+        in_specs=[SMEM, SMEM, ANY],
+        out_specs=ANY,
+        out_shape=jax.ShapeDtypeStruct(shape, tokens.dtype),
+        scratch_shapes=[
+            pltpu.VMEM(shape, tokens.dtype),
+            pltpu.SemaphoreType.DMA((shares, lengths.shape[0])),
+            pltpu.SemaphoreType.DMA((shares,)),
+        ],
         name="spread",
     )(lengths, ids, tokens)
 
 
-def base_kernel(side, lengths, tok_ref, key_ref, *refs):
-    out_ref = refs[-1]
+def base_kernel(side, lengths, tok_ref, key_ref, out_ref, flag_ref):
     part = jnp.dot(tok_ref[...], key_ref[...], preferred_element_type=jnp.float32)
     step = pl.program_id(0)
 
@@ -112,6 +137,7 @@
 
     @pl.when(step == pl.num_programs(0) - 1)
     def _():
+        flag_ref[...] = jnp.zeros_like(flag_ref)
         blocks = lengths.shape[0]
         block = out_ref.shape[0] // blocks
         row = lax.broadcasted_iota(jnp.int32, (block, out_ref.shape[1]), 0)
@@ -120,7 +146,7 @@
             out_ref[here, :] = jnp.where(row < lengths[b], out_ref[here, :], 0.0)
 
 
-def base_half(tokens, base_key, side, sides, lengths, *after):
+def base_half(tokens, base_key, side, sides, lengths):
     rows, depth = tokens.shape
     wide = base_key.shape[1] // sides
     step = 1024
@@ -132,16 +158,18 @@
             in_specs=[
                 pl.BlockSpec((rows, step), lambda i, s, n: (0, i)),
                 pl.BlockSpec((step, wide), lambda i, s, n: (i, s[0])),
-            ]
-            + [ANY] * len(after),
-            out_specs=pl.BlockSpec((rows, wide), lambda i, s, n: (0, 0)),
+            ],
+            out_specs=[
+                pl.BlockSpec((rows, wide), lambda i, s, n: (0, 0)),
+                pl.BlockSpec((8, LANES), lambda i, s, n: (0, 0)),
+            ],
         ),
-        out_shape=jax.ShapeDtypeStruct((rows, wide), jnp.float32),
+        out_shape=[jax.ShapeDtypeStruct((rows, wide), jnp.float32), jax.ShapeDtypeStruct((8, LANES), jnp.float32)],
         cost_estimate=pl.CostEstimate(
             flops=0, bytes_accessed=0, transcendentals=0
         ),
         name="base",
-    )(side.reshape(1), lengths, tokens, base_key, *after)
+    )(side.reshape(1), lengths, tokens, base_key)
 
 
 def mate_at(k, sign, groups, pair):
@@ -151,11 +179,11 @@
     return g * pair + y
 
 
-def rank_kernel(groups, ring, pair, ids, owner, tok, *refs):
+def rank_kernel(groups, ring, pair, rows, owner, tok, *refs):
     shares = groups * pair
-    tok_held, held, tok_sems, sems = refs[-4:]
-    outs = refs[-4 - shares : -4]
-    pieces = refs[: len(refs) - 4 - shares]
+    held, sems = refs[-2:]
+    outs = refs[-2 - shares : -2]
+    pieces = refs[: len(refs) - 2 - shares]
     per, rank = owner.shape[0] // (ring * pair), pieces[0].shape[1]
     blocks, _, block = outs[0].shape
     feats = tok.shape[2]
@@ -165,25 +193,27 @@
     for j, piece in enumerate(pieces):
         copies.append(pltpu.make_async_copy(piece, held.at[pl.ds(start, piece.shape[0])], sems.at[j]))
         start += piece.shape[0]
-    tok_copies = [
-        pltpu.make_async_copy(tok.at[mates[k], : blocks * block, :], tok_held.at[k], tok_sems.at[k])
-        for k in range(shares)
-    ]
-    for copy in copies + tok_copies:
+    for copy in copies:
         copy.start()
+    lane = lax.broadcasted_iota(jnp.int32, (16, LANES), 1)
+    row = lax.broadcasted_iota(jnp.int32, (16, LANES), 0)
+    slots = []
+    for k in range(shares):
+        named = tok[mates[k], rows:, :LANES].astype(jnp.float32)
+        ids = [jnp.sum(jnp.where((lane == b) & (row == 0), named, 0.0)).astype(jnp.int32) for b in range(blocks)]
+        slots.append([owner[i] for i in ids])
     for copy in copies:
         copy.wait()
     for k in range(shares):
-        tok_copies[k].wait()
         for b in range(blocks):
-            slot = owner[ids[mates[k] * blocks + b]]
+            slot = slots[k][b]
             chip = slot // per
             away = lax.rem(chip // pair - z + ring, ring)
             way = lax.rem(lax.rem(chip, pair) - y + pair, pair)
             at = (way * ring + away) * per + lax.rem(slot, per)
             part = lax.dot_general(
                 held[at, :, :feats],
-                tok_held[k, b * block : (b + 1) * block, :],
+                tok[mates[k], b * block : (b + 1) * block, :],
                 (((1,), (1,)), ((), ())),
                 preferred_element_type=jnp.float32,
             )
@@ -191,24 +221,23 @@
             outs[k][b, rank:, :] = held[at, :, feats:]
 
 
-def rank_parts(ids, owner, tok, pieces, groups, ring, pair, blocks):
+def rank_parts(owner, tok, pieces, groups, ring, pair, rows, blocks):
     shares, tall, feats = tok.shape
-    block = tall // blocks // LANES * LANES
+    block = rows // blocks
     _, rank, wide = pieces[0].shape
     return pl.pallas_call(
-        functools.partial(rank_kernel, groups, ring, pair),
-        in_specs=[SMEM, SMEM, ANY] + [ANY] * len(pieces),
+        functools.partial(rank_kernel, groups, ring, pair, rows),
+        in_specs=[SMEM, VMEM] + [ANY] * len(pieces),
         out_specs=[VMEM] * shares,
         out_shape=[jax.ShapeDtypeStruct((blocks, 2 * rank, block), tok.dtype)] * shares,
         scratch_shapes=[
-            pltpu.VMEM((shares, blocks * block, feats), tok.dtype),
             pltpu.VMEM((owner.shape[0], rank, wide), tok.dtype),
-            pltpu.SemaphoreType.DMA((shares,)),
             pltpu.SemaphoreType.DMA((len(pieces),)),
         ],
         cost_estimate=pl.CostEstimate(flops=2 * tok.size * rank, bytes_accessed=2 * tok.size, transcendentals=0),
+        compiler_params=BIG,
         name="rank",
-    )(ids, owner, tok, *pieces)
+    )(owner, tok, *pieces)
 
 
 def final_kernel(groups, pair, base_a, base_b, *refs):
@@ -289,14 +318,13 @@
     own_firsts = [first_hops(piece) for piece in own]
     firsts = [first_hops(piece) for piece in swapped]
     tok = to_plane(hand_on(slabs, *swapped, *(own_firsts[0][k] for k in own_firsts[0] if k > 0)))
-    ids = tok[:, rows, :blocks].astype(jnp.int32).reshape(-1)
-
-    base_out = base_half(tokens, base_key, (t + 1) % sides, sides, lengths, *swapped)
-    base_mine = base_half(tokens, base_key, t, sides, lengths, *swapped)
-    own_pieces = [more_hops(held, 0, base_out, base_mine) for held in own_firsts]
-    pieces = [more_hops(held, 1 + way, base_out, base_mine) for way, held in enumerate(firsts)]
+
+    base_out, flag_out = base_half(tokens, base_key, (t + 1) % sides, sides, lengths)
+    base_mine, flag_mine = base_half(tokens, base_key, t, sides, lengths)
+    own_pieces = [more_hops(held, 0, flag_out, flag_mine) for held in own_firsts]
+    pieces = [more_hops(held, 1 + way, flag_out, flag_mine) for way, held in enumerate(firsts)]
     flat = [piece for same in zip(*own_pieces) for piece in same] + [piece for way in pieces for piece in way]
-    parts = rank_parts(ids, owner_slot, tok, flat, groups, ring, pair, blocks)
+    parts = rank_parts(owner_slot, tok, flat, groups, ring, pair, rows, blocks)
     mine = [parts[0]] + [in_plane(parts[k], k // pair, k % pair) for k in range(1, shares)]
     theirs = [across(part) for part in mine]
     base_in = across(hand_on(base_out, parts[0]))

time: 78.5 us -> 83.4 us (1.062)
  local copies, waits for them, and re-layouts: 5.81 us -> 18.5 us
  waiting for transfers between devices: 21.4 us -> 17.2 us
  Pallas kernels: 26.2 us -> 22.5 us
    unnamed x16 -> x52, local copies, waits for them, and re-layouts: 5.19 us -> 18.5 us
    all_to_all x1, waiting for transfers between devices: 13.1 us -> 0.46 us  [to_plane(): return lax.all_to_all(x, PLANE, split_axis=0, concat_axis=0, tiled=True)]
    ppermute x9, waiting for transfers between devices: 1.89 us -> 10.5 us  [along(): lax.ppermute(x, 'ring', [(a, (a + step) % ring) for a in range(ring)])]
    pallas_call x2, Pallas kernels: 9.86 us -> 7.77 us  [the longest x1 4.16 us: rank_parts(): pl.pallas_call(functools.partial(rank_kernel, groups, ring, pair, rows),...]
    pallas_call x1, Pallas kernels: 2.02 us -> 0.18 us  [pack(): pl.pallas_call(functools.partial(pack_kernel, ways), in_specs=[HBM, HBM],...]
  transfers between devices with their start and end apart: 19 -> 19, of which waited for: 7 -> 9; matrix products, arithmetic and copies ran while one was open for 1% -> 0% of each run, Pallas kernels for 22% -> 21%
where the time goes in v12:
time: 83.4 us; the launch traced here: 82.6 us
  starting transfers between devices  24.4 us (29%)
  Pallas kernels  22.5 us (27%)
  local copies, waits for them, and re-layouts  18.5 us (22%)
  waiting for transfers between devices  17.2 us (21%)
    unnamed x52, local copies, waits for them, and re-layouts  18.5 us
    ppermute x9, starting transfers between devices, along(): lax.ppermute(x, 'ring', [(a, (a + step) % ring) for a in range(ring)])  14.1 us
    pallas_call x2, Pallas kernels, base_half(): pl.pallas_call(base_kernel, grid_spec=pltpu.PrefetchScalarGridSpec(num_sc...  13.5 us
    ppermute x9, waiting for transfers between devices, along(): lax.ppermute(x, 'ring', [(a, (a + step) % ring) for a in range(ring)])  10.5 us
    ppermute x3, waiting for transfers between devices, in_plane(): return lax.ppermute(x, PLANE, pairs)  4.94 us
    pallas_call x1, Pallas kernels, rank_parts(): pl.pallas_call(functools.partial(rank_kernel, groups, ring, pair, rows),...  4.16 us
    all_to_all x1, starting transfers between devices, to_plane(): return lax.all_to_all(x, PLANE, split_axis=0, concat_axis=0, tiled=True)  3.71 us
    pallas_call x1, Pallas kernels, spread(): pl.pallas_call(spread_kernel, in_specs=[SMEM, SMEM, ANY], out_specs=ANY,...  3.61 us
  transfers between devices with their start and end apart: 19, of which 9 were waited for; matrix products, arithmetic and copies ran while one was open for 0% of the time, Pallas kernels for 21%

profile of v12, /device:TPU:0, one launch (start us, length us, event | category | flops | bytes accessed | tf_op | source)
XLA Modules:
  0.0 82.6 jit_solution(9375665206984087788)
XLA Ops:
  0.0 1.2 %copy-done.8 = bf16[2,4096,64]{1,2,0:T(8,128)(2,1)S(1)} copy-done((bf16[2,4096,64]{1,2,0:T(8,128)(2,1)S(1)}, bf16[2,4096,64]{1,2,0:T(8,128)(2,1)}, u32[]{:S(2)}) %copy-start.8) | copy-done | bytes 1048600
  1.2 0.9 %copy-done.21 = bf16[2,64,512]{2,1,0:T(8,128)(2,1)S(1)} copy-done((bf16[2,64,512]{2,1,0:T(8,128)(2,1)S(1)}, bf16[2,64,512]{2,1,0:T(8,128)(2,1)}, u32[]{:S(2)}) %copy-start.21) | copy-done | bytes 131096
  2.1 0.2 pack.1
  2.3 0.6 copy-done.15
  3.0 3.0 %collective-permute-start = (bf16[2,64,1152]{2,1,0:T(8,128)(2,1)S(1)}, bf16[2,64,1152]{2,1,0:T(8,128)(2,1)S(1)}, u32[]{:S(2)}, u32[]{:S(2)}) collective-permute-start(bf16[2,64,1152]{2,1,0:T(8,128)(2,1)S(1)} %get-tuple-element.18), channel_id=1, source_target_pairs={{0,2},{2,0},{1,3},{3,1},{4,6},{6,4},{5,7},{7,5},{8,10},{10,8},{9,1... | collective-permute-start | bytes 884744 | tf_op jit(solution)/shard_map/ppermute | solution.py:317
  6.0 1.6 %collective-permute-start.1 = (bf16[1,64,1152]{2,1,0:T(8,128)(2,1)S(1)}, bf16[1,64,1152]{2,1,0:T(8,128)(2,1)S(1)}, u32[]{:S(2)}, u32[]{:S(2)}) collective-permute-start(bf16[1,64,1152]{2,1,0:T(8,128)(2,1)S(1)} %get-tuple-element.19.refs_0_), channel_id=1, source_target_pairs={{0,4},{4,8},{8,12},{12,0},{1,5},{5,9},{9,13},{13,1},{2,6},{6,10},{... | collective-permute-start | bytes 442376 | tf_op jit(solution)/shard_map/ppermute | solution.py:291
  7.5 2.2 %collective-permute-start.2 = (bf16[1,64,1152]{2,1,0:T(8,128)(2,1)S(1)}, bf16[1,64,1152]{2,1,0:T(8,128)(2,1)S(1)}, u32[]{:S(2)}, u32[]{:S(2)}) collective-permute-start(bf16[1,64,1152]{2,1,0:T(8,128)(2,1)S(1)} %get-tuple-element.19.refs_0_), channel_id=1, source_target_pairs={{0,12},{4,0},{8,4},{12,8},{1,13},{5,1},{9,5},{13,9},{2,14},{6,2},{... | collective-permute-start | bytes 442376 | tf_op jit(solution)/shard_map/ppermute | solution.py:291
  9.8 3.6 %spread.1.refs_0_ = bf16[4,400,1024]{2,1,0:T(8,128)(2,1)} custom-call(s32[3]{0:T(128)} %lengths.5, s32[3]{0:T(128)} %bitcast.5, bf16[384,4096]{1,0:T(8,128)(2,1)} %tok.1), custom_call_target="tpu_custom_call" | custom-call | tf_op jit(solution)/shard_map/spread/pallas_call | solution.py:112
  13.4 1.1 %collective-permute-done.1.refs_2_.refs_0_ = bf16[1,64,1152]{2,1,0:T(8,128)(2,1)S(1)} collective-permute-done((bf16[1,64,1152]{2,1,0:T(8,128)(2,1)S(1)}, bf16[1,64,1152]{2,1,0:T(8,128)(2,1)S(1)}, u32[]{:S(2)}, u32[]{:S(2)}) %collective-permute-start.1) | collective-permute-done | bytes 147488 | tf_op jit(solution)/shard_map/ppermute | solution.py:291
  14.5 1.2 %collective-permute-done.2.refs_3_.refs_1_.refs_2_ = bf16[1,64,1152]{2,1,0:T(8,128)(2,1)S(1)} collective-permute-done((bf16[1,64,1152]{2,1,0:T(8,128)(2,1)S(1)}, bf16[1,64,1152]{2,1,0:T(8,128)(2,1)S(1)}, u32[]{:S(2)}, u32[]{:S(2)}) %collective-permute-start.2) | collective-permute-done | bytes 147488 | tf_op jit(solution)/shard_map/ppermute | solution.py:291
  15.7 0.0 collective-permute-done.refs_1_.refs_8_
  15.7 1.9 %copy-done = bf16[4,400,1024]{2,1,0:T(8,128)(2,1)S(1)} copy-done((bf16[4,400,1024]{2,1,0:T(8,128)(2,1)S(1)}, bf16[4,400,1024]{2,1,0:T(8,128)(2,1)}, u32[]{:S(2)}) %copy-start) | copy-done | bytes 3276824
  17.7 0.7 copy-done.6
  18.4 1.7 %copy-done.1 = bf16[4,400,1024]{2,1,0:T(8,128)(2,1)} copy-done((bf16[4,400,1024]{2,1,0:T(8,128)(2,1)}, bf16[4,400,1024]{2,1,0:T(8,128)(2,1)S(1)}, u32[]{:S(2)}) %copy-start.1) | copy-done | bytes 3276824
  20.0 3.7 %all-to-all-start = ((bf16[4,400,1024]{2,1,0:T(8,128)(2,1)}), bf16[4,400,1024]{2,1,0:T(8,128)(2,1)S(1)}, u32[]{:S(2)}, u32[]{:S(2)}) async-start(bf16[4,400,1024]{2,1,0:T(8,128)(2,1)} %copy-done.1), calls=%async_computation | async-start | bytes 6553600 | tf_op jit(solution)/shard_map/all_to_all | solution.py:288
  23.7 2.4 %collective-permute-start.7 = (bf16[2,64,1152]{2,1,0:T(8,128)(2,1)}, bf16[2,64,1152]{2,1,0:T(8,128)(2,1)}, u32[]{:S(2)}, u32[]{:S(2)}) collective-permute-start(bf16[2,64,1152]{2,1,0:T(8,128)(2,1)} %copy-done.6), channel_id=1, source_target_pairs={{0,12},{4,0},{8,4},{12,8},{1,13},{5,1},{9,5},{13,9},{2,14},{6,2},{... | collective-permute-start | bytes 884744 | tf_op jit(solution)/shard_map/ppermute | solution.py:291
  26.2 3.8 %collective-permute-start.3 = (bf16[1,64,1152]{2,1,0:T(8,128)(2,1)}, bf16[1,64,1152]{2,1,0:T(8,128)(2,1)}, u32[]{:S(2)}, u32[]{:S(2)}) collective-permute-start(bf16[1,64,1152]{2,1,0:T(8,128)(2,1)} %copy-done.15), channel_id=1, source_target_pairs={{0,12},{4,0},{8,4},{12,8},{1,13},{5,1},{9,5},{13,9},{2,14},{6,2},{... | collective-permute-start | bytes 442376 | tf_op jit(solution)/shard_map/ppermute | solution.py:291
  30.0 6.6 %base.2 = (f32[384,512]{1,0:T(8,128)}, f32[8,128]{1,0:T(8,128)}) custom-call(s32[1]{0:T(128)} %bitcast.side, s32[3]{0:T(128)} %lengths.5, bf16[384,4096]{1,0:T(8,128)(2,1)} %tok.1, bf16[4096,1024]{1,0:T(8,128)(2,1)} %key_ref.3), custom_call_target="tpu_custom_call" | custom-call | tf_op jit(solution)/shard_map/base/pallas_call | solution.py:153
  36.6 6.8 %base.3 = (f32[384,512]{1,0:T(8,128)}, f32[8,128]{1,0:T(8,128)}) custom-call(s32[1]{0:T(128)} %bitcast.1.side, s32[3]{0:T(128)} %lengths.5, bf16[384,4096]{1,0:T(8,128)(2,1)} %tok.1, bf16[4096,1024]{1,0:T(8,128)(2,1)} %key_ref.3), custom_call_target="tpu_custom_call" | custom-call | tf_op jit(solution)/shard_map/base/pallas_call | solution.py:153
  43.5 0.7 copy-done.23
  44.1 3.8 %collective-permute-start.9 = (bf16[2,64,1152]{2,1,0:T(8,128)(2,1)}, bf16[2,64,1152]{2,1,0:T(8,128)(2,1)S(1)}, u32[]{:S(2)}, u32[]{:S(2)}) collective-permute-start(bf16[2,64,1152]{2,1,0:T(8,128)(2,1)} %hand.8.refs_9_), channel_id=1, source_target_pairs={{0,12},{4,0},{8,4},{12,8},{1,13},{5,1},{9,5},{13,9},{2,14},{6,2},{... | collective-permute-start | bytes 884744 | tf_op jit(solution)/shard_map/ppermute | solution.py:291
  48.0 0.9 %copy-done.3 = bf16[1,64,1152]{2,1,0:T(8,128)(2,1)S(1)} copy-done((bf16[1,64,1152]{2,1,0:T(8,128)(2,1)S(1)}, bf16[1,64,1152]{2,1,0:T(8,128)(2,1)}, u32[]{:S(2)}) %copy-start.3) | copy-done | bytes 147480
  48.9 0.7 copy-done.24
  49.5 0.2 collective-permute-start.4
  49.7 0.6 copy-done.4
  50.4 7.3 %collective-permute-done.6.refs_5_ = bf16[1,64,1152]{2,1,0:T(8,128)(2,1)S(1)} collective-permute-done((bf16[1,64,1152]{2,1,0:T(8,128)(2,1)}, bf16[1,64,1152]{2,1,0:T(8,128)(2,1)S(1)}, u32[]{:S(2)}, u32[]{:S(2)}) %collective-permute-start.6) | collective-permute-done | bytes 147488 | tf_op jit(solution)/shard_map/ppermute | solution.py:291
  57.6 0.7 copy-done.17
  58.3 0.9 %collective-permute-done.4.refs_4_ = bf16[1,64,1152]{2,1,0:T(8,128)(2,1)S(1)} collective-permute-done((bf16[1,64,1152]{2,1,0:T(8,128)(2,1)S(1)}, bf16[1,64,1152]{2,1,0:T(8,128)(2,1)S(1)}, u32[]{:S(2)}, u32[]{:S(2)}) %collective-permute-start.4) | collective-permute-done | bytes 147488 | tf_op jit(solution)/shard_map/ppermute | solution.py:291
  59.2 0.7 copy-done.19
  59.9 0.7 copy-done.11
  60.6 0.5 all-to-all-done.tok
  61.0 0.9 %copy-done.5 = bf16[1,64,1152]{2,1,0:T(8,128)(2,1)S(1)} copy-done((bf16[1,64,1152]{2,1,0:T(8,128)(2,1)S(1)}, bf16[1,64,1152]{2,1,0:T(8,128)(2,1)}, u32[]{:S(2)}) %copy-start.5) | copy-done | bytes 147480
  62.0 1.0 %copy-done.7 = bf16[2,64,1152]{2,1,0:T(8,128)(2,1)S(1)} copy-done((bf16[2,64,1152]{2,1,0:T(8,128)(2,1)S(1)}, bf16[2,64,1152]{2,1,0:T(8,128)(2,1)}, u32[]{:S(2)}) %copy-start.7) | copy-done | bytes 294936
  62.9 1.0 %copy-done.12 = bf16[2,64,1152]{2,1,0:T(8,128)(2,1)S(1)} copy-done((bf16[2,64,1152]{2,1,0:T(8,128)(2,1)S(1)}, bf16[2,64,1152]{2,1,0:T(8,128)(2,1)}, u32[]{:S(2)}) %copy-start.12) | copy-done | bytes 294936
  63.9 0.9 %copy-done.14 = bf16[1,64,1152]{2,1,0:T(8,128)(2,1)S(1)} copy-done((bf16[1,64,1152]{2,1,0:T(8,128)(2,1)S(1)}, bf16[1,64,1152]{2,1,0:T(8,128)(2,1)}, u32[]{:S(2)}) %copy-start.14) | copy-done | bytes 147480
  64.8 0.9 %copy-done.16 = bf16[1,64,1152]{2,1,0:T(8,128)(2,1)S(1)} copy-done((bf16[1,64,1152]{2,1,0:T(8,128)(2,1)S(1)}, bf16[1,64,1152]{2,1,0:T(8,128)(2,1)}, u32[]{:S(2)}) %copy-start.16) | copy-done | bytes 147480
  65.7 0.9 %copy-done.18 = bf16[1,64,1152]{2,1,0:T(8,128)(2,1)S(1)} copy-done((bf16[1,64,1152]{2,1,0:T(8,128)(2,1)S(1)}, bf16[1,64,1152]{2,1,0:T(8,128)(2,1)}, u32[]{:S(2)}) %copy-start.18) | copy-done | bytes 147480
  66.6 0.9 %copy-done.20 = bf16[1,64,1152]{2,1,0:T(8,128)(2,1)S(1)} copy-done((bf16[1,64,1152]{2,1,0:T(8,128)(2,1)S(1)}, bf16[1,64,1152]{2,1,0:T(8,128)(2,1)}, u32[]{:S(2)}) %copy-start.20) | copy-done | bytes 147480
  67.5 4.2 %rank.1 = (bf16[3,128,128]{2,1,0:T(8,128)(2,1)S(1)}, bf16[3,128,128]{2,1,0:T(8,128)(2,1)S(1)}, bf16[3,128,128]{2,1,0:T(8,128)(2,1)S(1)}, bf16[3,128,128]{2,1,0:T(8,128)(2,1)S(1)}) custom-call(s32[16]{0:T(128)S(1)} %copy-done.25, bf16[4,400,1024]{2,1,0:T(8,128)(2,1)S(1)} %all-to-all-done.tok, bf16[1,64,1152]{2,1,0:T(8,128)(2,1)S(1)} %copy-done.14, ...), custom_call_target="tpu_custom_call" | custom-call | flops 209715200 | bytes 3276800 | tf_op jit(solution)/shard_map/rank/pallas_call | solution.py:228
  71.7 0.1 collective-permute-start.10
  71.8 1.5 %collective-permute-start.11 = (bf16[3,128,128]{2,1,0:T(8,128)(2,1)S(1)}, bf16[3,128,128]{2,1,0:T(8,128)(2,1)S(1)}, u32[]{:S(2)}, u32[]{:S(2)}) collective-permute-start(bf16[3,128,128]{2,1,0:T(8,128)(2,1)S(1)} %get-tuple-element.24), channel_id=1, source_target_pairs={{0,2},{2,0},{16,18},{18,16},{1,3},{3,1},{17,19},{19,17},{4,6},{6,4... | collective-permute-start | bytes 294920 | tf_op jit(solution)/shard_map/ppermute | solution.py:301
  73.3 1.3 %collective-permute-start.12 = (bf16[3,128,128]{2,1,0:T(8,128)(2,1)S(1)}, bf16[3,128,128]{2,1,0:T(8,128)(2,1)S(1)}, u32[]{:S(2)}, u32[]{:S(2)}) collective-permute-start(bf16[3,128,128]{2,1,0:T(8,128)(2,1)S(1)} %get-tuple-element.25), channel_id=1, source_target_pairs={{0,16},{2,18},{16,0},{18,2},{1,17},{3,19},{17,1},{19,3},{4,20},{6,... | collective-permute-start | bytes 294920 | tf_op jit(solution)/shard_map/ppermute | solution.py:301
  74.6 0.7 collective-permute-start.13
  75.3 1.7 %collective-permute-done.11.refs_1_ = bf16[3,128,128]{2,1,0:T(8,128)(2,1)S(1)} collective-permute-done((bf16[3,128,128]{2,1,0:T(8,128)(2,1)S(1)}, bf16[3,128,128]{2,1,0:T(8,128)(2,1)S(1)}, u32[]{:S(2)}, u32[]{:S(2)}) %collective-permute-start.11) | collective-permute-done | bytes 98336 | tf_op jit(solution)/shard_map/ppermute | solution.py:301
  77.0 2.0 %collective-permute-done.12.refs_2_ = bf16[3,128,128]{2,1,0:T(8,128)(2,1)S(1)} collective-permute-done((bf16[3,128,128]{2,1,0:T(8,128)(2,1)S(1)}, bf16[3,128,128]{2,1,0:T(8,128)(2,1)S(1)}, u32[]{:S(2)}, u32[]{:S(2)}) %collective-permute-start.12) | collective-permute-done | bytes 98336 | tf_op jit(solution)/shard_map/ppermute | solution.py:301
  79.0 1.3 %collective-permute-done.13.refs_3_ = bf16[3,128,128]{2,1,0:T(8,128)(2,1)S(1)} collective-permute-done((bf16[3,128,128]{2,1,0:T(8,128)(2,1)S(1)}, bf16[3,128,128]{2,1,0:T(8,128)(2,1)S(1)}, u32[]{:S(2)}, u32[]{:S(2)}) %collective-permute-start.13) | collective-permute-done | bytes 98336 | tf_op jit(solution)/shard_map/ppermute | solution.py:301
  80.3 1.3 %collective-permute-done.17.refs_7_ = bf16[3,128,128]{2,1,0:T(8,128)(2,1)S(1)} collective-permute-done((bf16[3,128,128]{2,1,0:T(8,128)(2,1)S(1)}, bf16[3,128,128]{2,1,0:T(8,128)(2,1)S(1)}, u32[]{:S(2)}, u32[]{:S(2)}) %collective-permute-start.17) | collective-permute-done | bytes 98336 | tf_op jit(solution)/shard_map/ppermute | solution.py:285
  81.6 1.1 %final.1 = bf16[384,512]{1,0:T(8,128)(2,1)} custom-call(f32[384,512]{1,0:T(8,128)S(1)} %copy-done.10, f32[384,512]{1,0:T(8,128)S(1)} %collective-permute-done.10.base_b, bf16[3,128,128]{2,1,0:T(8,128)(2,1)S(1)} %get-tuple-element.23.refs_1_.refs_0_, bf16[3,128,128]{2,1,0:T(8,128)(2,1)S(1)} %collective-permute-done.11.refs_1_, ...), custom_call_target="tpu_custom_call" | custom-call | tf_op jit(solution)/shard_map/final/pallas_call | solution.py:265
  (53 shorter events, 0.1 us)
Async XLA Ops:
  0.0 1.2 %copy-start.8 = (bf16[2,4096,64]{1,2,0:T(8,128)(2,1)S(1)}, bf16[2,4096,64]{1,2,0:T(8,128)(2,1)}, u32[]{:S(2)}) copy-start(bf16[2,4096,64]{1,2,0:T(8,128)(2,1)} %param.9) | copy-start | bytes 3145732
  1.2 0.9 %copy-start.21 = (bf16[2,64,512]{2,1,0:T(8,128)(2,1)S(1)}, bf16[2,64,512]{2,1,0:T(8,128)(2,1)}, u32[]{:S(2)}) copy-start(bf16[2,64,512]{2,1,0:T(8,128)(2,1)} %up.1) | copy-start | bytes 393220
  2.3 0.7 copy-start.15
  3.0 14.7 %copy-start.13 = (bf16[1,64,1152]{2,1,0:T(8,128)(2,1)}, bf16[1,64,1152]{2,1,0:T(8,128)(2,1)S(1)}, u32[]{:S(2)}) copy-start(bf16[1,64,1152]{2,1,0:T(8,128)(2,1)S(1)} %get-tuple-element.19.refs_0_) | copy-start | bytes 442372
  3.0 12.7 %collective-permute-start = (bf16[2,64,1152]{2,1,0:T(8,128)(2,1)S(1)}, bf16[2,64,1152]{2,1,0:T(8,128)(2,1)S(1)}, u32[]{:S(2)}, u32[]{:S(2)}) collective-permute-start(bf16[2,64,1152]{2,1,0:T(8,128)(2,1)S(1)} %get-tuple-element.18), channel_id=1, source_target_pairs={{0,2},{2,0},{1,3},{3,1},{4,6},{6,4},{5,7},{7,5},{8,10},{10,8},{9,1... | collective-permute-start | bytes 884744 | tf_op jit(solution)/shard_map/ppermute | solution.py:317
  6.0 8.6 %collective-permute-start.1 = (bf16[1,64,1152]{2,1,0:T(8,128)(2,1)S(1)}, bf16[1,64,1152]{2,1,0:T(8,128)(2,1)S(1)}, u32[]{:S(2)}, u32[]{:S(2)}) collective-permute-start(bf16[1,64,1152]{2,1,0:T(8,128)(2,1)S(1)} %get-tuple-element.19.refs_0_), channel_id=1, source_target_pairs={{0,4},{4,8},{8,12},{12,0},{1,5},{5,9},{9,13},{13,1},{2,6},{6,10},{... | collective-permute-start | bytes 442376 | tf_op jit(solution)/shard_map/ppermute | solution.py:291
  7.5 8.2 %collective-permute-start.2 = (bf16[1,64,1152]{2,1,0:T(8,128)(2,1)S(1)}, bf16[1,64,1152]{2,1,0:T(8,128)(2,1)S(1)}, u32[]{:S(2)}, u32[]{:S(2)}) collective-permute-start(bf16[1,64,1152]{2,1,0:T(8,128)(2,1)S(1)} %get-tuple-element.19.refs_0_), channel_id=1, source_target_pairs={{0,12},{4,0},{8,4},{12,8},{1,13},{5,1},{9,5},{13,9},{2,14},{6,2},{... | collective-permute-start | bytes 442376 | tf_op jit(solution)/shard_map/ppermute | solution.py:291
  14.5 3.1 %copy-start.2 = (bf16[1,64,1152]{2,1,0:T(8,128)(2,1)}, bf16[1,64,1152]{2,1,0:T(8,128)(2,1)S(1)}, u32[]{:S(2)}) copy-start(bf16[1,64,1152]{2,1,0:T(8,128)(2,1)S(1)} %collective-permute-done.1.refs_2_.refs_0_) | copy-start | bytes 442372
  15.7 1.9 %copy-start = (bf16[4,400,1024]{2,1,0:T(8,128)(2,1)S(1)}, bf16[4,400,1024]{2,1,0:T(8,128)(2,1)}, u32[]{:S(2)}) copy-start(bf16[4,400,1024]{2,1,0:T(8,128)(2,1)} %spread.1.refs_0_) | copy-start | bytes 9830404
  17.6 0.7 copy-start.6
  18.4 1.7 %copy-start.1 = (bf16[4,400,1024]{2,1,0:T(8,128)(2,1)}, bf16[4,400,1024]{2,1,0:T(8,128)(2,1)S(1)}, u32[]{:S(2)}) copy-start(bf16[4,400,1024]{2,1,0:T(8,128)(2,1)S(1)} %hand.5) | copy-start | bytes 9830404
  20.0 41.0 %all-to-all-start = ((bf16[4,400,1024]{2,1,0:T(8,128)(2,1)}), bf16[4,400,1024]{2,1,0:T(8,128)(2,1)S(1)}, u32[]{:S(2)}, u32[]{:S(2)}) async-start(bf16[4,400,1024]{2,1,0:T(8,128)(2,1)} %copy-done.1), calls=%async_computation | async-start | bytes 6553600 | tf_op jit(solution)/shard_map/all_to_all | solution.py:288
  23.7 19.7 %collective-permute-start.7 = (bf16[2,64,1152]{2,1,0:T(8,128)(2,1)}, bf16[2,64,1152]{2,1,0:T(8,128)(2,1)}, u32[]{:S(2)}, u32[]{:S(2)}) collective-permute-start(bf16[2,64,1152]{2,1,0:T(8,128)(2,1)} %copy-done.6), channel_id=1, source_target_pairs={{0,12},{4,0},{8,4},{12,8},{1,13},{5,1},{9,5},{13,9},{2,14},{6,2},{... | collective-permute-start | bytes 884744 | tf_op jit(solution)/shard_map/ppermute | solution.py:291
  26.2 17.3 %collective-permute-start.8 = (bf16[2,64,1152]{2,1,0:T(8,128)(2,1)}, bf16[2,64,1152]{2,1,0:T(8,128)(2,1)}, u32[]{:S(2)}, u32[]{:S(2)}) collective-permute-start(bf16[2,64,1152]{2,1,0:T(8,128)(2,1)} %copy-done.6), channel_id=1, source_target_pairs={{0,4},{4,8},{8,12},{12,0},{1,5},{5,9},{9,13},{13,1},{2,6},{6,10},{... | collective-permute-start | bytes 884744 | tf_op jit(solution)/shard_map/ppermute | solution.py:291
  26.2 21.8 %collective-permute-start.3 = (bf16[1,64,1152]{2,1,0:T(8,128)(2,1)}, bf16[1,64,1152]{2,1,0:T(8,128)(2,1)}, u32[]{:S(2)}, u32[]{:S(2)}) collective-permute-start(bf16[1,64,1152]{2,1,0:T(8,128)(2,1)} %copy-done.15), channel_id=1, source_target_pairs={{0,12},{4,0},{8,4},{12,8},{1,13},{5,1},{9,5},{13,9},{2,14},{6,2},{... | collective-permute-start | bytes 442376 | tf_op jit(solution)/shard_map/ppermute | solution.py:291
  30.0 18.0 %collective-permute-start.5 = (bf16[1,64,1152]{2,1,0:T(8,128)(2,1)}, bf16[1,64,1152]{2,1,0:T(8,128)(2,1)}, u32[]{:S(2)}, u32[]{:S(2)}) collective-permute-start(bf16[1,64,1152]{2,1,0:T(8,128)(2,1)} %copy-done.15), channel_id=1, source_target_pairs={{0,4},{4,8},{8,12},{12,0},{1,5},{5,9},{9,13},{13,1},{2,6},{6,10},{... | collective-permute-start | bytes 442376 | tf_op jit(solution)/shard_map/ppermute | solution.py:291
  36.6 6.8 %copy-start.22 = (f32[8,128]{1,0:T(8,128)S(1)}, f32[8,128]{1,0:T(8,128)}, u32[]{:S(2)}) copy-start(f32[8,128]{1,0:T(8,128)} %get-tuple-element.22.refs_3_) | copy-start | bytes 12292
  36.6 24.4 %copy-start.25 = (s32[16]{0:T(128)S(1)}, s32[16]{0:T(128)}, u32[]{:S(2)}) copy-start(s32[16]{0:T(128)} %owner.1) | copy-start | bytes 196
  43.5 0.7 copy-start.23
  44.1 15.7 %collective-permute-start.9 = (bf16[2,64,1152]{2,1,0:T(8,128)(2,1)}, bf16[2,64,1152]{2,1,0:T(8,128)(2,1)S(1)}, u32[]{:S(2)}, u32[]{:S(2)}) collective-permute-start(bf16[2,64,1152]{2,1,0:T(8,128)(2,1)} %hand.8.refs_9_), channel_id=1, source_target_pairs={{0,12},{4,0},{8,4},{12,8},{1,13},{5,1},{9,5},{13,9},{2,14},{6,2},{... | collective-permute-start | bytes 884744 | tf_op jit(solution)/shard_map/ppermute | solution.py:291
  48.0 9.6 %collective-permute-start.6 = (bf16[1,64,1152]{2,1,0:T(8,128)(2,1)}, bf16[1,64,1152]{2,1,0:T(8,128)(2,1)S(1)}, u32[]{:S(2)}, u32[]{:S(2)}) collective-permute-start(bf16[1,64,1152]{2,1,0:T(8,128)(2,1)} %hand.7.refs_7_), channel_id=1, source_target_pairs={{0,4},{4,8},{8,12},{12,0},{1,5},{5,9},{9,13},{13,1},{2,6},{6,10},{... | collective-permute-start | bytes 442376 | tf_op jit(solution)/shard_map/ppermute | solution.py:291
  48.0 0.9 %copy-start.3 = (bf16[1,64,1152]{2,1,0:T(8,128)(2,1)S(1)}, bf16[1,64,1152]{2,1,0:T(8,128)(2,1)}, u32[]{:S(2)}) copy-start(bf16[1,64,1152]{2,1,0:T(8,128)(2,1)} %copy-done.2) | copy-start | bytes 442372
  48.9 0.7 copy-start.24
  49.5 9.6 %collective-permute-start.4 = (bf16[1,64,1152]{2,1,0:T(8,128)(2,1)S(1)}, bf16[1,64,1152]{2,1,0:T(8,128)(2,1)S(1)}, u32[]{:S(2)}, u32[]{:S(2)}) collective-permute-start(bf16[1,64,1152]{2,1,0:T(8,128)(2,1)S(1)} %hand.6.refs_6_), channel_id=1, source_target_pairs={{0,4},{4,8},{8,12},{12,0},{1,5},{5,9},{9,13},{13,1},{2,6},{6,10},{... | collective-permute-start | bytes 442376 | tf_op jit(solution)/shard_map/ppermute | solution.py:291
  49.7 0.6 copy-start.4
  57.6 0.7 copy-start.17
  59.2 0.7 copy-start.19
  59.9 0.7 copy-start.11
  61.0 0.9 %copy-start.5 = (bf16[1,64,1152]{2,1,0:T(8,128)(2,1)S(1)}, bf16[1,64,1152]{2,1,0:T(8,128)(2,1)}, u32[]{:S(2)}) copy-start(bf16[1,64,1152]{2,1,0:T(8,128)(2,1)} %copy-done.4) | copy-start | bytes 442372
  62.0 1.0 %copy-start.7 = (bf16[2,64,1152]{2,1,0:T(8,128)(2,1)S(1)}, bf16[2,64,1152]{2,1,0:T(8,128)(2,1)}, u32[]{:S(2)}) copy-start(bf16[2,64,1152]{2,1,0:T(8,128)(2,1)} %copy-done.6) | copy-start | bytes 884740
  62.9 1.0 %copy-start.12 = (bf16[2,64,1152]{2,1,0:T(8,128)(2,1)S(1)}, bf16[2,64,1152]{2,1,0:T(8,128)(2,1)}, u32[]{:S(2)}) copy-start(bf16[2,64,1152]{2,1,0:T(8,128)(2,1)} %copy-done.11) | copy-start | bytes 884740
  63.9 0.9 %copy-start.14 = (bf16[1,64,1152]{2,1,0:T(8,128)(2,1)S(1)}, bf16[1,64,1152]{2,1,0:T(8,128)(2,1)}, u32[]{:S(2)}) copy-start(bf16[1,64,1152]{2,1,0:T(8,128)(2,1)} %copy-done.13) | copy-start | bytes 442372
  64.8 0.9 %copy-start.16 = (bf16[1,64,1152]{2,1,0:T(8,128)(2,1)S(1)}, bf16[1,64,1152]{2,1,0:T(8,128)(2,1)}, u32[]{:S(2)}) copy-start(bf16[1,64,1152]{2,1,0:T(8,128)(2,1)} %copy-done.15) | copy-start | bytes 442372
  65.7 0.9 %copy-start.18 = (bf16[1,64,1152]{2,1,0:T(8,128)(2,1)S(1)}, bf16[1,64,1152]{2,1,0:T(8,128)(2,1)}, u32[]{:S(2)}) copy-start(bf16[1,64,1152]{2,1,0:T(8,128)(2,1)} %copy-done.17) | copy-start | bytes 442372
  66.6 0.9 %copy-start.20 = (bf16[1,64,1152]{2,1,0:T(8,128)(2,1)S(1)}, bf16[1,64,1152]{2,1,0:T(8,128)(2,1)}, u32[]{:S(2)}) copy-start(bf16[1,64,1152]{2,1,0:T(8,128)(2,1)} %copy-done.19) | copy-start | bytes 442372
  67.5 4.2 %copy-start.9 = (f32[384,512]{1,0:T(8,128)S(1)}, f32[384,512]{1,0:T(8,128)}, u32[]{:S(2)}) copy-start(f32[384,512]{1,0:T(8,128)} %get-tuple-element.17.refs_0_) | copy-start | bytes 2359300
  67.5 14.1 %copy-start.10 = (f32[384,512]{1,0:T(8,128)S(1)}, f32[384,512]{1,0:T(8,128)}, u32[]{:S(2)}) copy-start(f32[384,512]{1,0:T(8,128)} %get-tuple-element.16.base_a) | copy-start | bytes 2359300
  71.7 9.9 %collective-permute-start.10 = (f32[384,512]{1,0:T(8,128)S(1)}, f32[384,512]{1,0:T(8,128)S(1)}, u32[]{:S(2)}, u32[]{:S(2)}) collective-permute-start(f32[384,512]{1,0:T(8,128)S(1)} %hand.9), channel_id=1, source_target_pairs={{0,1},{1,0},{2,3},{3,2},{4,5},{5,4},{6,7},{7,6},{8,9},{9,8},{10,11... | collective-permute-start | bytes 2359304 | tf_op jit(solution)/shard_map/ppermute | solution.py:285
  71.8 5.2 %collective-permute-start.11 = (bf16[3,128,128]{2,1,0:T(8,128)(2,1)S(1)}, bf16[3,128,128]{2,1,0:T(8,128)(2,1)S(1)}, u32[]{:S(2)}, u32[]{:S(2)}) collective-permute-start(bf16[3,128,128]{2,1,0:T(8,128)(2,1)S(1)} %get-tuple-element.24), channel_id=1, source_target_pairs={{0,2},{2,0},{16,18},{18,16},{1,3},{3,1},{17,19},{19,17},{4,6},{6,4... | collective-permute-start | bytes 294920 | tf_op jit(solution)/shard_map/ppermute | solution.py:301
  73.3 5.6 %collective-permute-start.12 = (bf16[3,128,128]{2,1,0:T(8,128)(2,1)S(1)}, bf16[3,128,128]{2,1,0:T(8,128)(2,1)S(1)}, u32[]{:S(2)}, u32[]{:S(2)}) collective-permute-start(bf16[3,128,128]{2,1,0:T(8,128)(2,1)S(1)} %get-tuple-element.25), channel_id=1, source_target_pairs={{0,16},{2,18},{16,0},{18,2},{1,17},{3,19},{17,1},{19,3},{4,20},{6,... | collective-permute-start | bytes 294920 | tf_op jit(solution)/shard_map/ppermute | solution.py:301
  74.6 5.7 %collective-permute-start.13 = (bf16[3,128,128]{2,1,0:T(8,128)(2,1)S(1)}, bf16[3,128,128]{2,1,0:T(8,128)(2,1)S(1)}, u32[]{:S(2)}, u32[]{:S(2)}) collective-permute-start(bf16[3,128,128]{2,1,0:T(8,128)(2,1)S(1)} %get-tuple-element.26), channel_id=1, source_target_pairs={{0,18},{2,16},{16,2},{18,0},{1,19},{3,17},{17,3},{19,1},{4,22},{6,... | collective-permute-start | bytes 294920 | tf_op jit(solution)/shard_map/ppermute | solution.py:301
  75.3 5.0 %collective-permute-start.14 = (bf16[3,128,128]{2,1,0:T(8,128)(2,1)S(1)}, bf16[3,128,128]{2,1,0:T(8,128)(2,1)S(1)}, u32[]{:S(2)}, u32[]{:S(2)}) collective-permute-start(bf16[3,128,128]{2,1,0:T(8,128)(2,1)S(1)} %get-tuple-element.23.refs_1_.refs_0_), channel_id=1, source_target_pairs={{0,1},{1,0},{2,3},{3,2},{4,5},{5,4},{6,7},{7,6},{8,9},{9,8},{10,11... | collective-permute-start | bytes 294920 | tf_op jit(solution)/shard_map/ppermute | solution.py:285
  77.0 3.3 %collective-permute-start.15 = (bf16[3,128,128]{2,1,0:T(8,128)(2,1)S(1)}, bf16[3,128,128]{2,1,0:T(8,128)(2,1)S(1)}, u32[]{:S(2)}, u32[]{:S(2)}) collective-permute-start(bf16[3,128,128]{2,1,0:T(8,128)(2,1)S(1)} %collective-permute-done.11.refs_1_), channel_id=1, source_target_pairs={{0,1},{1,0},{2,3},{3,2},{4,5},{5,4},{6,7},{7,6},{8,9},{9,8},{10,11... | collective-permute-start | bytes 294920 | tf_op jit(solution)/shard_map/ppermute | solution.py:285
  79.0 1.3 %collective-permute-start.16 = (bf16[3,128,128]{2,1,0:T(8,128)(2,1)S(1)}, bf16[3,128,128]{2,1,0:T(8,128)(2,1)S(1)}, u32[]{:S(2)}, u32[]{:S(2)}) collective-permute-start(bf16[3,128,128]{2,1,0:T(8,128)(2,1)S(1)} %collective-permute-done.12.refs_2_), channel_id=1, source_target_pairs={{0,1},{1,0},{2,3},{3,2},{4,5},{5,4},{6,7},{7,6},{8,9},{9,8},{10,11... | collective-permute-start | bytes 294920 | tf_op jit(solution)/shard_map/ppermute | solution.py:285
  80.3 1.3 %collective-permute-start.17 = (bf16[3,128,128]{2,1,0:T(8,128)(2,1)S(1)}, bf16[3,128,128]{2,1,0:T(8,128)(2,1)S(1)}, u32[]{:S(2)}, u32[]{:S(2)}) collective-permute-start(bf16[3,128,128]{2,1,0:T(8,128)(2,1)S(1)} %collective-permute-done.13.refs_3_), channel_id=1, source_target_pairs={{0,1},{1,0},{2,3},{3,2},{4,5},{5,4},{6,7},{7,6},{8,9},{9,8},{10,11... | collective-permute-start | bytes 294920 | tf_op jit(solution)/shard_map/ppermute | solution.py:285

commit v13 on v9

--- a/solution.py
+++ b/solution.py
@@ -13,7 +13,8 @@
 SMEM = pl.BlockSpec(memory_space=pltpu.SMEM)
 VMEM = pl.BlockSpec(memory_space=pltpu.VMEM)
 HBM = pl.BlockSpec(memory_space=pltpu.HBM)
-BIG = pltpu.CompilerParams(vmem_limit_bytes=32 * 1024 * 1024)
+ROOM = pltpu.CompilerParams(vmem_limit_bytes=32 * 1024 * 1024)
+FULL = pltpu.CompilerParams(vmem_limit_bytes=60 * 1024 * 1024)
 PLANE = ("groups", "pair")
 WHOLE = ("groups", "ring", "pair")
 
@@ -29,6 +30,7 @@
         out_specs=ANY,
         out_shape=jax.ShapeDtypeStruct(x.shape, x.dtype),
         input_output_aliases={0: 0},
+        compiler_params=FULL,
         name="hand",
     )(x, *after)
 
@@ -58,35 +60,61 @@
         out_specs=[VMEM] * ways,
         out_shape=[shape] * ways,
         scratch_shapes=[pltpu.SemaphoreType.DMA((ways, 2))],
+        compiler_params=FULL,
         name="pack",
     )(down, up)
 
 
-def spread_kernel(lengths, ids, in_ref, out_ref):
+def spread_kernel(lengths, ids, tok, out, held, in_sems, out_sems):
     blocks = lengths.shape[0]
-    rows, step = in_ref.shape
+    shares, tall, step = held.shape
+    rows = tok.shape[0]
     block = rows // blocks
-    row = lax.broadcasted_iota(jnp.int32, (block, step), 0)
-    for b in range(blocks):
-        part = in_ref[b * block : (b + 1) * block, :]
-        out_ref[0, b * block : (b + 1) * block, :] = jnp.where(row < lengths[b], part, jnp.zeros_like(part))
-    extra = out_ref.shape[1] - rows
-    lane = lax.broadcasted_iota(jnp.int32, (extra, step), 1)
-    named = jnp.zeros((extra, step), jnp.float32)
+
+    def read(k, b):
+        here = pl.ds(b * block, block)
+        return pltpu.make_async_copy(tok.at[here, pl.ds(k * step, step)], held.at[k, here, :], in_sems.at[k, b])
+
+    for k in range(shares):
+        for b in range(blocks):
+            read(k, b).start()
+    lane = lax.broadcasted_iota(jnp.int32, (tall - rows, step), 1)
+    named = jnp.zeros((tall - rows, step), jnp.float32)
     for b in range(blocks):
         named = jnp.where(lane == b, ids[b].astype(jnp.float32), named)
-    out_ref[0, rows:, :] = named.astype(out_ref.dtype)
+    named = named.astype(held.dtype)
+    writes = [pltpu.make_async_copy(held.at[k], out.at[k], out_sems.at[k]) for k in range(shares)]
+    for k in range(shares):
+        held[k, rows:, :] = named
+        for b in range(blocks):
+            read(k, b).wait()
+
+            @pl.when(lengths[b] < block)
+            def _():
+                here = slice(b * block, (b + 1) * block)
+                row = lax.broadcasted_iota(jnp.int32, (block, step), 0)
+                part = held[k, here, :]
+                held[k, here, :] = jnp.where(row < lengths[b], part, jnp.zeros_like(part))
+
+        writes[k].start()
+    for write in writes:
+        write.wait()
 
 
 def spread(tokens, lengths, ids, shares):
     rows, feats = tokens.shape
-    step = feats // shares
+    shape = (shares, rows + 16, feats // shares)
     return pl.pallas_call(
         spread_kernel,
-        grid=(shares,),
-        in_specs=[SMEM, SMEM, pl.BlockSpec((rows, step), lambda i: (0, i))],
-        out_specs=pl.BlockSpec((1, rows + 16, step), lambda i: (i, 0, 0)),
-        out_shape=jax.ShapeDtypeStruct((shares, rows + 16, step), tokens.dtype),
+        in_specs=[SMEM, SMEM, ANY],
+        out_specs=ANY,
+        out_shape=jax.ShapeDtypeStruct(shape, tokens.dtype),
+        scratch_shapes=[
+            pltpu.VMEM(shape, tokens.dtype),
+            pltpu.SemaphoreType.DMA((shares, lengths.shape[0])),
+            pltpu.SemaphoreType.DMA((shares,)),
+        ],
+        compiler_params=FULL,
         name="spread",
     )(lengths, ids, tokens)
 
@@ -134,6 +162,7 @@
         cost_estimate=pl.CostEstimate(
             flops=0, bytes_accessed=0, transcendentals=0
         ),
+        compiler_params=FULL,
         name="base",
     )(side.reshape(1), lengths, tokens, base_key, *after)
 
@@ -145,7 +174,7 @@
     return g * pair + y
 
 
-def rank_kernel(groups, ring, pair, ids, owner, tok, *refs):
+def rank_kernel(groups, ring, pair, rows, owner, tok, *refs):
     shares = groups * pair
     tok_held, held, tok_sems, sems = refs[-4:]
     outs = refs[-4 - shares : -4]
@@ -157,17 +186,21 @@
     mates = [mate_at(k, 1, groups, pair) for k in range(shares)]
     copies = [pltpu.make_async_copy(piece, held.at[pl.ds(j * per, per)], sems.at[j]) for j, piece in enumerate(pieces)]
     tok_copies = [
-        pltpu.make_async_copy(tok.at[mates[k], : blocks * block, :], tok_held.at[k], tok_sems.at[k])
+        pltpu.make_async_copy(tok.at[mates[k]], tok_held.at[k], tok_sems.at[k])
         for k in range(shares)
     ]
     for copy in copies + tok_copies:
         copy.start()
     for copy in copies:
         copy.wait()
+    lane = lax.broadcasted_iota(jnp.int32, (16, LANES), 1)
+    row = lax.broadcasted_iota(jnp.int32, (16, LANES), 0)
     for k in range(shares):
         tok_copies[k].wait()
+        named = tok_held[k, rows:, :LANES].astype(jnp.float32)
+        ids = [jnp.sum(jnp.where((lane == b) & (row == 0), named, 0.0)).astype(jnp.int32) for b in range(blocks)]
         for b in range(blocks):
-            slot = owner[ids[mates[k] * blocks + b]]
+            slot = owner[ids[b]]
             chip = slot // per
             away = lax.rem(chip // pair - z + ring, ring)
             way = lax.rem(lax.rem(chip, pair) - y + pair, pair)
@@ -182,24 +215,25 @@
             outs[k][b, rank:, :] = held[at, :, feats:]
 
 
-def rank_parts(ids, owner, tok, pieces, groups, ring, pair, blocks):
+def rank_parts(owner, tok, pieces, groups, ring, pair, rows, blocks):
     shares, tall, feats = tok.shape
-    block = tall // blocks // LANES * LANES
+    block = rows // blocks
     per, rank, wide = pieces[0].shape
     return pl.pallas_call(
-        functools.partial(rank_kernel, groups, ring, pair),
-        in_specs=[SMEM, SMEM, ANY] + [ANY] * len(pieces),
+        functools.partial(rank_kernel, groups, ring, pair, rows),
+        in_specs=[SMEM, ANY] + [ANY] * len(pieces),
         out_specs=[VMEM] * shares,
         out_shape=[jax.ShapeDtypeStruct((blocks, 2 * rank, block), tok.dtype)] * shares,
         scratch_shapes=[
-            pltpu.VMEM((shares, blocks * block, feats), tok.dtype),
+            pltpu.VMEM(tok.shape, tok.dtype),
             pltpu.VMEM((len(pieces) * per, rank, wide), tok.dtype),
             pltpu.SemaphoreType.DMA((shares,)),
             pltpu.SemaphoreType.DMA((len(pieces),)),
         ],
         cost_estimate=pl.CostEstimate(flops=2 * tok.size * rank, bytes_accessed=2 * tok.size, transcendentals=0),
+        compiler_params=FULL,
         name="rank",
-    )(ids, owner, tok, *pieces)
+    )(owner, tok, *pieces)
 
 
 def final_kernel(groups, pair, base_a, base_b, *refs):
@@ -230,7 +264,7 @@
         out_specs=VMEM,
         out_shape=jax.ShapeDtypeStruct(base[0].shape, dtype),
         scratch_shapes=[pltpu.VMEM((blocks, tall // 2, base[0].shape[1]), mine[0].dtype)],
-        compiler_params=BIG,
+        compiler_params=ROOM,
         name="final",
     )(*base, *mine, *theirs)
 
@@ -280,18 +314,17 @@
         lax.ppermute(packed[pair - w], "pair", [(a, (a - w) % pair) for a in range(pair)]) for w in range(1, pair)
     ]
     firsts = [first_hops(piece) for piece in [packed[0]] + swapped]
-    tok = to_plane(hand_on(slabs, *swapped))
-    ids = tok[:, rows, :blocks].astype(jnp.int32).reshape(-1)
-
-    base_out = base_half(tokens, base_key, (t + 1) % sides, sides, lengths, *swapped)
-    base_mine = base_half(tokens, base_key, t, sides, lengths, *swapped)
+    tok = to_plane(hand_on(slabs, *swapped, firsts[0][ring - 1]))
+
+    base_out = base_half(tokens, base_key, (t + 1) % sides, sides, lengths)
+    base_mine = base_half(tokens, base_key, t, sides, lengths)
     pieces = [
         more_hops(held, way, base_out, base_mine)
         for way, held in enumerate(firsts)
     ]
 
     flat = [piece for way in pieces for piece in way]
-    parts = rank_parts(ids, owner_slot, tok, flat, groups, ring, pair, blocks)
+    parts = rank_parts(owner_slot, tok, flat, groups, ring, pair, rows, blocks)
     mine = [parts[0]] + [in_plane(parts[k], k // pair, k % pair) for k in range(1, shares)]
     theirs = [across(part) for part in mine]
     base_in = across(hand_on(base_out, parts[0]))

time: 76.9 us -> 76 us (0.988)
  local copies, waits for them, and re-layouts: 3.87 us -> 3.1 us
    ppermute x6, waiting for transfers between devices: 13.3 us -> 15.4 us  [along(): lax.ppermute(x, 'ring', [(a, (a + step) % ring) for a in range(ring)])]
    ppermute x6, starting transfers between devices: 8.92 us -> 7.79 us  [along(): lax.ppermute(x, 'ring', [(a, (a + step) % ring) for a in range(ring)])]
    ppermute x1, waiting for transfers between devices: 2.93 us -> 1.96 us  [body(): lax.ppermute(packed[pair - w], 'pair', [(a, (a - w) % pair) for a in rang...]
    all_to_all x1, starting transfers between devices: 3.94 us -> 4.81 us  [to_plane(): return lax.all_to_all(x, PLANE, split_axis=0, concat_axis=0, tiled=True)]
    unnamed x8 -> x22, local copies, waits for them, and re-layouts: 3.27 us -> 3.1 us
  transfers between devices with their start and end apart: 16 -> 16, of which waited for: 9 -> 10; matrix products, arithmetic and copies ran while one was open for 1% -> 0% of each run, Pallas kernels for 23% -> 22%
where the time goes in v13:
time: 76 us; the launch traced here: 75.6 us
  waiting for transfers between devices  27.4 us (36%)
  Pallas kernels  25.7 us (34%)
  starting transfers between devices  19.3 us (25%)
  local copies, waits for them, and re-layouts  3.1 us (4%)
    ppermute x6, waiting for transfers between devices, along(): lax.ppermute(x, 'ring', [(a, (a + step) % ring) for a in range(ring)])  15.4 us
    pallas_call x2, Pallas kernels, base_half(): pl.pallas_call(base_kernel, grid_spec=pltpu.PrefetchScalarGridSpec(num_sc...  13.3 us
    ppermute x6, starting transfers between devices, along(): lax.ppermute(x, 'ring', [(a, (a + step) % ring) for a in range(ring)])  7.79 us
    pallas_call x1, Pallas kernels, rank_parts(): pl.pallas_call(functools.partial(rank_kernel, groups, ring, pair, rows),...  5.82 us
    ppermute x3, waiting for transfers between devices, in_plane(): return lax.ppermute(x, PLANE, pairs)  5.15 us
    all_to_all x1, starting transfers between devices, to_plane(): return lax.all_to_all(x, PLANE, split_axis=0, concat_axis=0, tiled=True)  4.81 us
    pallas_call x1, Pallas kernels, spread(): pl.pallas_call(spread_kernel, in_specs=[SMEM, SMEM, ANY], out_specs=ANY,...  3.68 us
    all_to_all x1, waiting for transfers between devices, to_plane(): return lax.all_to_all(x, PLANE, split_axis=0, concat_axis=0, tiled=True)  3.66 us
  transfers between devices with their start and end apart: 16, of which 10 were waited for; matrix products, arithmetic and copies ran while one was open for 0% of the time, Pallas kernels for 22%

profile of v13, /device:TPU:0, one launch (start us, length us, event | category | flops | bytes accessed | tf_op | source)
XLA Modules:
  0.0 75.6 jit_solution(2237930773656715072)
XLA Ops:
  0.0 1.9 %pack.1 = (bf16[2,64,1152]{2,1,0:T(8,128)(2,1)}, bf16[2,64,1152]{2,1,0:T(8,128)(2,1)}) custom-call(bf16[2,64,4096]{2,1,0:T(8,128)(2,1)} %bitcast.4, bf16[2,64,512]{2,1,0:T(8,128)(2,1)} %up.1), custom_call_target="tpu_custom_call" | custom-call | tf_op jit(solution)/shard_map/pack/pallas_call | solution.py:57
  1.9 3.0 %collective-permute-start = (bf16[2,64,1152]{2,1,0:T(8,128)(2,1)}, bf16[2,64,1152]{2,1,0:T(8,128)(2,1)S(1)}, u32[]{:S(2)}, u32[]{:S(2)}) collective-permute-start(bf16[2,64,1152]{2,1,0:T(8,128)(2,1)} %get-tuple-element.11), channel_id=1, source_target_pairs={{0,2},{2,0},{1,3},{3,1},{4,6},{6,4},{5,7},{7,5},{8,10},{10,8},{9,1... | collective-permute-start | bytes 884744 | tf_op jit(solution)/shard_map/ppermute | solution.py:314
  4.9 1.6 %collective-permute-start.1 = (bf16[2,64,1152]{2,1,0:T(8,128)(2,1)}, bf16[2,64,1152]{2,1,0:T(8,128)(2,1)S(1)}, u32[]{:S(2)}, u32[]{:S(2)}) collective-permute-start(bf16[2,64,1152]{2,1,0:T(8,128)(2,1)} %get-tuple-element.12.refs_0_), channel_id=1, source_target_pairs={{0,4},{4,8},{8,12},{12,0},{1,5},{5,9},{9,13},{13,1},{2,6},{6,10},{... | collective-permute-start | bytes 884744 | tf_op jit(solution)/shard_map/ppermute | solution.py:287
  6.5 3.7 %spread.1.refs_0_ = bf16[4,400,1024]{2,1,0:T(8,128)(2,1)} custom-call(s32[3]{0:T(128)} %lengths.5, s32[3]{0:T(128)} %bitcast.5, bf16[384,4096]{1,0:T(8,128)(2,1)} %tok.1), custom_call_target="tpu_custom_call" | custom-call | tf_op jit(solution)/shard_map/spread/pallas_call | solution.py:107
  10.2 2.0 %collective-permute-done.refs_1_.refs_4_ = bf16[2,64,1152]{2,1,0:T(8,128)(2,1)S(1)} collective-permute-done((bf16[2,64,1152]{2,1,0:T(8,128)(2,1)}, bf16[2,64,1152]{2,1,0:T(8,128)(2,1)S(1)}, u32[]{:S(2)}, u32[]{:S(2)}) %collective-permute-start) | collective-permute-done | bytes 294944 | tf_op jit(solution)/shard_map/ppermute | solution.py:314
  12.2 3.3 %collective-permute-done.1.refs_2_.refs_0_ = bf16[2,64,1152]{2,1,0:T(8,128)(2,1)S(1)} collective-permute-done((bf16[2,64,1152]{2,1,0:T(8,128)(2,1)}, bf16[2,64,1152]{2,1,0:T(8,128)(2,1)S(1)}, u32[]{:S(2)}, u32[]{:S(2)}) %collective-permute-start.1) | collective-permute-done | bytes 294944 | tf_op jit(solution)/shard_map/ppermute | solution.py:287
  15.5 0.0 copy-done.3
  15.5 0.7 copy-done.2
  16.2 4.8 %all-to-all-start = ((bf16[4,400,1024]{2,1,0:T(8,128)(2,1)}), bf16[4,400,1024]{2,1,0:T(8,128)(2,1)}, u32[]{:S(2)}, u32[]{:S(2)}) async-start(bf16[4,400,1024]{2,1,0:T(8,128)(2,1)} %hand.4), calls=%async_computation | async-start | bytes 6553600 | tf_op jit(solution)/shard_map/all_to_all | solution.py:284
  21.0 0.0 copy-done.8
  21.0 1.8 %collective-permute-start.2 = (bf16[2,64,1152]{2,1,0:T(8,128)(2,1)S(1)}, bf16[2,64,1152]{2,1,0:T(8,128)(2,1)S(1)}, u32[]{:S(2)}, u32[]{:S(2)}) collective-permute-start(bf16[2,64,1152]{2,1,0:T(8,128)(2,1)S(1)} %copy-done.8), channel_id=1, source_target_pairs={{0,12},{4,0},{8,4},{12,8},{1,13},{5,1},{9,5},{13,9},{2,14},{6,2},{... | collective-permute-start | bytes 884744 | tf_op jit(solution)/shard_map/ppermute | solution.py:287
  22.8 0.0 copy-done.4
  22.8 0.4 collective-permute-start.4
  23.3 1.6 %collective-permute-start.5 = (bf16[2,64,1152]{2,1,0:T(8,128)(2,1)S(1)}, bf16[2,64,1152]{2,1,0:T(8,128)(2,1)S(1)}, u32[]{:S(2)}, u32[]{:S(2)}) collective-permute-start(bf16[2,64,1152]{2,1,0:T(8,128)(2,1)S(1)} %copy-done.4), channel_id=1, source_target_pairs={{0,4},{4,8},{8,12},{12,0},{1,5},{5,9},{9,13},{13,1},{2,6},{6,10},{... | collective-permute-start | bytes 884744 | tf_op jit(solution)/shard_map/ppermute | solution.py:287
  24.9 6.6 %base.2.refs_3_.base_a = f32[384,512]{1,0:T(8,128)} custom-call(s32[1]{0:T(128)} %bitcast.side, s32[3]{0:T(128)} %lengths.5, bf16[384,4096]{1,0:T(8,128)(2,1)} %tok.1, bf16[4096,1024]{1,0:T(8,128)(2,1)} %key_ref.3), custom_call_target="tpu_custom_call" | custom-call | tf_op jit(solution)/shard_map/base/pallas_call | solution.py:149
  31.5 6.7 %base.3.refs_2_.refs_0_ = f32[384,512]{1,0:T(8,128)} custom-call(s32[1]{0:T(128)} %bitcast.1.side, s32[3]{0:T(128)} %lengths.5, bf16[384,4096]{1,0:T(8,128)(2,1)} %tok.1, bf16[4096,1024]{1,0:T(8,128)(2,1)} %key_ref.3), custom_call_target="tpu_custom_call" | custom-call | tf_op jit(solution)/shard_map/base/pallas_call | solution.py:149
  38.1 0.0 collective-permute-done.2.refs_1_
  38.1 0.7 copy-done.5
  38.9 0.3 collective-permute-start.3
  39.2 0.0 collective-permute-done.4.refs_0_
  39.2 3.8 %collective-permute-done.5.refs_1_.refs_7_ = bf16[2,64,1152]{2,1,0:T(8,128)(2,1)S(1)} collective-permute-done((bf16[2,64,1152]{2,1,0:T(8,128)(2,1)S(1)}, bf16[2,64,1152]{2,1,0:T(8,128)(2,1)S(1)}, u32[]{:S(2)}, u32[]{:S(2)}) %collective-permute-start.5) | collective-permute-done | bytes 294944 | tf_op jit(solution)/shard_map/ppermute | solution.py:287
  42.9 0.0 copy-done.7
  42.9 0.7 copy-done.6
  43.7 2.1 %collective-permute-start.6 = (bf16[2,64,1152]{2,1,0:T(8,128)(2,1)}, bf16[2,64,1152]{2,1,0:T(8,128)(2,1)S(1)}, u32[]{:S(2)}, u32[]{:S(2)}) collective-permute-start(bf16[2,64,1152]{2,1,0:T(8,128)(2,1)} %hand.6.refs_5_), channel_id=1, source_target_pairs={{0,12},{4,0},{8,4},{12,8},{1,13},{5,1},{9,5},{13,9},{2,14},{6,2},{... | collective-permute-start | bytes 884744 | tf_op jit(solution)/shard_map/ppermute | solution.py:287
  45.8 3.6 %collective-permute-done.3.refs_2_ = bf16[2,64,1152]{2,1,0:T(8,128)(2,1)S(1)} collective-permute-done((bf16[2,64,1152]{2,1,0:T(8,128)(2,1)}, bf16[2,64,1152]{2,1,0:T(8,128)(2,1)S(1)}, u32[]{:S(2)}, u32[]{:S(2)}) %collective-permute-start.3) | collective-permute-done | bytes 294944 | tf_op jit(solution)/shard_map/ppermute | solution.py:287
  49.4 4.7 %collective-permute-done.6.refs_6_ = bf16[2,64,1152]{2,1,0:T(8,128)(2,1)S(1)} collective-permute-done((bf16[2,64,1152]{2,1,0:T(8,128)(2,1)}, bf16[2,64,1152]{2,1,0:T(8,128)(2,1)S(1)}, u32[]{:S(2)}, u32[]{:S(2)}) %collective-permute-start.6) | collective-permute-done | bytes 294944 | tf_op jit(solution)/shard_map/ppermute | solution.py:287
  54.1 3.7 %all-to-all-done.tok = bf16[4,400,1024]{2,1,0:T(8,128)(2,1)} async-done(((bf16[4,400,1024]{2,1,0:T(8,128)(2,1)}), bf16[4,400,1024]{2,1,0:T(8,128)(2,1)}, u32[]{:S(2)}, u32[]{:S(2)}) %all-to-all-start) | async-done | bytes 3276832 | tf_op jit(solution)/shard_map/all_to_all | solution.py:284
  57.7 0.0 copy-done.9
  57.8 0.0 copy-done.10
  57.8 5.8 %rank.1 = (bf16[3,128,128]{2,1,0:T(8,128)(2,1)}, bf16[3,128,128]{2,1,0:T(8,128)(2,1)}, bf16[3,128,128]{2,1,0:T(8,128)(2,1)}, bf16[3,128,128]{2,1,0:T(8,128)(2,1)}) custom-call(s32[16]{0:T(128)} %owner.1, bf16[4,400,1024]{2,1,0:T(8,128)(2,1)} %all-to-all-done.tok, bf16[2,64,1152]{2,1,0:T(8,128)(2,1)} %get-tuple-element.12.refs_0_, ...), custom_call_target="tpu_custom_call" | custom-call | flops 209715200 | bytes 3276800 | tf_op jit(solution)/shard_map/rank/pallas_call | solution.py:222
  63.6 0.1 collective-permute-start.7
  63.7 1.5 %collective-permute-start.8 = (bf16[3,128,128]{2,1,0:T(8,128)(2,1)}, bf16[3,128,128]{2,1,0:T(8,128)(2,1)S(1)}, u32[]{:S(2)}, u32[]{:S(2)}) collective-permute-start(bf16[3,128,128]{2,1,0:T(8,128)(2,1)} %get-tuple-element.14), channel_id=1, source_target_pairs={{0,2},{2,0},{16,18},{18,16},{1,3},{3,1},{17,19},{19,17},{4,6},{6,4... | collective-permute-start | bytes 294920 | tf_op jit(solution)/shard_map/ppermute | solution.py:297
  65.2 0.6 collective-permute-start.9
  65.8 1.5 %collective-permute-start.10 = (bf16[3,128,128]{2,1,0:T(8,128)(2,1)}, bf16[3,128,128]{2,1,0:T(8,128)(2,1)S(1)}, u32[]{:S(2)}, u32[]{:S(2)}) collective-permute-start(bf16[3,128,128]{2,1,0:T(8,128)(2,1)} %get-tuple-element.16), channel_id=1, source_target_pairs={{0,18},{2,16},{16,2},{18,0},{1,19},{3,17},{17,3},{19,1},{4,22},{6,... | collective-permute-start | bytes 294920 | tf_op jit(solution)/shard_map/ppermute | solution.py:297
  67.2 0.0 collective-permute-start.11
  67.2 1.9 %collective-permute-done.8.refs_1_ = bf16[3,128,128]{2,1,0:T(8,128)(2,1)S(1)} collective-permute-done((bf16[3,128,128]{2,1,0:T(8,128)(2,1)}, bf16[3,128,128]{2,1,0:T(8,128)(2,1)S(1)}, u32[]{:S(2)}, u32[]{:S(2)}) %collective-permute-start.8) | collective-permute-done | bytes 98336 | tf_op jit(solution)/shard_map/ppermute | solution.py:297
  69.1 0.0 collective-permute-start.12
  69.1 1.9 %collective-permute-done.9.refs_2_ = bf16[3,128,128]{2,1,0:T(8,128)(2,1)S(1)} collective-permute-done((bf16[3,128,128]{2,1,0:T(8,128)(2,1)}, bf16[3,128,128]{2,1,0:T(8,128)(2,1)S(1)}, u32[]{:S(2)}, u32[]{:S(2)}) %collective-permute-start.9) | collective-permute-done | bytes 98336 | tf_op jit(solution)/shard_map/ppermute | solution.py:297
  71.0 0.0 collective-permute-start.13
  71.1 1.3 %collective-permute-done.10.refs_3_ = bf16[3,128,128]{2,1,0:T(8,128)(2,1)S(1)} collective-permute-done((bf16[3,128,128]{2,1,0:T(8,128)(2,1)}, bf16[3,128,128]{2,1,0:T(8,128)(2,1)S(1)}, u32[]{:S(2)}, u32[]{:S(2)}) %collective-permute-start.10) | collective-permute-done | bytes 98336 | tf_op jit(solution)/shard_map/ppermute | solution.py:297
  72.4 0.0 collective-permute-start.14
  72.4 0.0 collective-permute-done.11.refs_4_
  72.4 0.0 collective-permute-done.12.refs_5_
  72.4 0.0 collective-permute-done.13.refs_6_
  72.4 1.3 %collective-permute-done.14.refs_7_ = bf16[3,128,128]{2,1,0:T(8,128)(2,1)S(1)} collective-permute-done((bf16[3,128,128]{2,1,0:T(8,128)(2,1)S(1)}, bf16[3,128,128]{2,1,0:T(8,128)(2,1)S(1)}, u32[]{:S(2)}, u32[]{:S(2)}) %collective-permute-start.14) | collective-permute-done | bytes 98336 | tf_op jit(solution)/shard_map/ppermute | solution.py:281
  73.7 0.0 collective-permute-done.7.base_b
  73.7 0.9 %copy-done.1 = bf16[3,128,128]{2,1,0:T(8,128)(2,1)S(1)} copy-done((bf16[3,128,128]{2,1,0:T(8,128)(2,1)S(1)}, bf16[3,128,128]{2,1,0:T(8,128)(2,1)}, u32[]{:S(2)}) %copy-start.1) | copy-done | bytes 98328
  74.6 1.1 %final.1 = bf16[384,512]{1,0:T(8,128)(2,1)} custom-call(f32[384,512]{1,0:T(8,128)S(1)} %copy-done, f32[384,512]{1,0:T(8,128)S(1)} %collective-permute-done.7.base_b, bf16[3,128,128]{2,1,0:T(8,128)(2,1)S(1)} %copy-done.1, bf16[3,128,128]{2,1,0:T(8,128)(2,1)S(1)} %collective-permute-done.8.refs_1_, bf16[3,128,128]{2,1,0:T(8,128)(2,1)S(1)} %collective-permute-done.9.refs_2_, ...), custom_call_target="tpu_custom_call" | custom-call | tf_op jit(solution)/shard_map/final/pallas_call | solution.py:261
  (16 shorter events, 0.0 us)
Async XLA Ops:
  1.9 10.2 %collective-permute-start = (bf16[2,64,1152]{2,1,0:T(8,128)(2,1)}, bf16[2,64,1152]{2,1,0:T(8,128)(2,1)S(1)}, u32[]{:S(2)}, u32[]{:S(2)}) collective-permute-start(bf16[2,64,1152]{2,1,0:T(8,128)(2,1)} %get-tuple-element.11), channel_id=1, source_target_pairs={{0,2},{2,0},{1,3},{3,1},{4,6},{6,4},{5,7},{7,5},{8,10},{10,8},{9,1... | collective-permute-start | bytes 884744 | tf_op jit(solution)/shard_map/ppermute | solution.py:314
  4.9 10.5 %collective-permute-start.1 = (bf16[2,64,1152]{2,1,0:T(8,128)(2,1)}, bf16[2,64,1152]{2,1,0:T(8,128)(2,1)S(1)}, u32[]{:S(2)}, u32[]{:S(2)}) collective-permute-start(bf16[2,64,1152]{2,1,0:T(8,128)(2,1)} %get-tuple-element.12.refs_0_), channel_id=1, source_target_pairs={{0,4},{4,8},{8,12},{12,0},{1,5},{5,9},{9,13},{13,1},{2,6},{6,10},{... | collective-permute-start | bytes 884744 | tf_op jit(solution)/shard_map/ppermute | solution.py:287
  12.2 3.3 %copy-start.3 = (bf16[2,64,1152]{2,1,0:T(8,128)(2,1)}, bf16[2,64,1152]{2,1,0:T(8,128)(2,1)S(1)}, u32[]{:S(2)}) copy-start(bf16[2,64,1152]{2,1,0:T(8,128)(2,1)S(1)} %collective-permute-done.refs_1_.refs_4_) | copy-start | bytes 884740
  15.5 0.7 copy-start.2
  16.2 4.8 %copy-start.8 = (bf16[2,64,1152]{2,1,0:T(8,128)(2,1)S(1)}, bf16[2,64,1152]{2,1,0:T(8,128)(2,1)}, u32[]{:S(2)}) copy-start(bf16[2,64,1152]{2,1,0:T(8,128)(2,1)} %get-tuple-element.12.refs_0_) | copy-start | bytes 884740
  16.2 6.6 %copy-start.4 = (bf16[2,64,1152]{2,1,0:T(8,128)(2,1)S(1)}, bf16[2,64,1152]{2,1,0:T(8,128)(2,1)}, u32[]{:S(2)}) copy-start(bf16[2,64,1152]{2,1,0:T(8,128)(2,1)} %copy-done.3) | copy-start | bytes 884740
  16.2 41.6 %all-to-all-start = ((bf16[4,400,1024]{2,1,0:T(8,128)(2,1)}), bf16[4,400,1024]{2,1,0:T(8,128)(2,1)}, u32[]{:S(2)}, u32[]{:S(2)}) async-start(bf16[4,400,1024]{2,1,0:T(8,128)(2,1)} %hand.4), calls=%async_computation | async-start | bytes 6553600 | tf_op jit(solution)/shard_map/all_to_all | solution.py:284
  21.0 17.1 %collective-permute-start.2 = (bf16[2,64,1152]{2,1,0:T(8,128)(2,1)S(1)}, bf16[2,64,1152]{2,1,0:T(8,128)(2,1)S(1)}, u32[]{:S(2)}, u32[]{:S(2)}) collective-permute-start(bf16[2,64,1152]{2,1,0:T(8,128)(2,1)S(1)} %copy-done.8), channel_id=1, source_target_pairs={{0,12},{4,0},{8,4},{12,8},{1,13},{5,1},{9,5},{13,9},{2,14},{6,2},{... | collective-permute-start | bytes 884744 | tf_op jit(solution)/shard_map/ppermute | solution.py:287
  22.8 16.3 %collective-permute-start.4 = (bf16[2,64,1152]{2,1,0:T(8,128)(2,1)S(1)}, bf16[2,64,1152]{2,1,0:T(8,128)(2,1)S(1)}, u32[]{:S(2)}, u32[]{:S(2)}) collective-permute-start(bf16[2,64,1152]{2,1,0:T(8,128)(2,1)S(1)} %copy-done.4), channel_id=1, source_target_pairs={{0,12},{4,0},{8,4},{12,8},{1,13},{5,1},{9,5},{13,9},{2,14},{6,2},{... | collective-permute-start | bytes 884744 | tf_op jit(solution)/shard_map/ppermute | solution.py:287
  23.3 19.6 %collective-permute-start.5 = (bf16[2,64,1152]{2,1,0:T(8,128)(2,1)S(1)}, bf16[2,64,1152]{2,1,0:T(8,128)(2,1)S(1)}, u32[]{:S(2)}, u32[]{:S(2)}) collective-permute-start(bf16[2,64,1152]{2,1,0:T(8,128)(2,1)S(1)} %copy-done.4), channel_id=1, source_target_pairs={{0,4},{4,8},{8,12},{12,0},{1,5},{5,9},{9,13},{13,1},{2,6},{6,10},{... | collective-permute-start | bytes 884744 | tf_op jit(solution)/shard_map/ppermute | solution.py:287
  38.1 0.7 copy-start.5
  38.9 10.5 %collective-permute-start.3 = (bf16[2,64,1152]{2,1,0:T(8,128)(2,1)}, bf16[2,64,1152]{2,1,0:T(8,128)(2,1)S(1)}, u32[]{:S(2)}, u32[]{:S(2)}) collective-permute-start(bf16[2,64,1152]{2,1,0:T(8,128)(2,1)} %hand.5.refs_3_), channel_id=1, source_target_pairs={{0,4},{4,8},{8,12},{12,0},{1,5},{5,9},{9,13},{13,1},{2,6},{6,10},{... | collective-permute-start | bytes 884744 | tf_op jit(solution)/shard_map/ppermute | solution.py:287
  39.2 3.8 %copy-start.7 = (bf16[2,64,1152]{2,1,0:T(8,128)(2,1)}, bf16[2,64,1152]{2,1,0:T(8,128)(2,1)S(1)}, u32[]{:S(2)}) copy-start(bf16[2,64,1152]{2,1,0:T(8,128)(2,1)S(1)} %collective-permute-done.4.refs_0_) | copy-start | bytes 884740
  42.9 0.7 copy-start.6
  43.7 30.0 %copy-start = (f32[384,512]{1,0:T(8,128)S(1)}, f32[384,512]{1,0:T(8,128)}, u32[]{:S(2)}) copy-start(f32[384,512]{1,0:T(8,128)} %base.2.refs_3_.base_a) | copy-start | bytes 2359300
  43.7 10.4 %collective-permute-start.6 = (bf16[2,64,1152]{2,1,0:T(8,128)(2,1)}, bf16[2,64,1152]{2,1,0:T(8,128)(2,1)S(1)}, u32[]{:S(2)}, u32[]{:S(2)}) collective-permute-start(bf16[2,64,1152]{2,1,0:T(8,128)(2,1)} %hand.6.refs_5_), channel_id=1, source_target_pairs={{0,12},{4,0},{8,4},{12,8},{1,13},{5,1},{9,5},{13,9},{2,14},{6,2},{... | collective-permute-start | bytes 884744 | tf_op jit(solution)/shard_map/ppermute | solution.py:287
  49.4 8.4 %copy-start.9 = (bf16[2,64,1152]{2,1,0:T(8,128)(2,1)}, bf16[2,64,1152]{2,1,0:T(8,128)(2,1)S(1)}, u32[]{:S(2)}) copy-start(bf16[2,64,1152]{2,1,0:T(8,128)(2,1)S(1)} %collective-permute-done.3.refs_2_) | copy-start | bytes 884740
  54.1 3.7 %copy-start.10 = (bf16[2,64,1152]{2,1,0:T(8,128)(2,1)}, bf16[2,64,1152]{2,1,0:T(8,128)(2,1)S(1)}, u32[]{:S(2)}) copy-start(bf16[2,64,1152]{2,1,0:T(8,128)(2,1)S(1)} %collective-permute-done.6.refs_6_) | copy-start | bytes 884740
  63.6 10.1 %collective-permute-start.7 = (f32[384,512]{1,0:T(8,128)}, f32[384,512]{1,0:T(8,128)S(1)}, u32[]{:S(2)}, u32[]{:S(2)}) collective-permute-start(f32[384,512]{1,0:T(8,128)} %hand.7), channel_id=1, source_target_pairs={{0,1},{1,0},{2,3},{3,2},{4,5},{5,4},{6,7},{7,6},{8,9},{9,8},{10,11... | collective-permute-start | bytes 2359304 | tf_op jit(solution)/shard_map/ppermute | solution.py:281
  63.7 5.4 %collective-permute-start.8 = (bf16[3,128,128]{2,1,0:T(8,128)(2,1)}, bf16[3,128,128]{2,1,0:T(8,128)(2,1)S(1)}, u32[]{:S(2)}, u32[]{:S(2)}) collective-permute-start(bf16[3,128,128]{2,1,0:T(8,128)(2,1)} %get-tuple-element.14), channel_id=1, source_target_pairs={{0,2},{2,0},{16,18},{18,16},{1,3},{3,1},{17,19},{19,17},{4,6},{6,4... | collective-permute-start | bytes 294920 | tf_op jit(solution)/shard_map/ppermute | solution.py:297
  65.2 5.9 %collective-permute-start.9 = (bf16[3,128,128]{2,1,0:T(8,128)(2,1)}, bf16[3,128,128]{2,1,0:T(8,128)(2,1)S(1)}, u32[]{:S(2)}, u32[]{:S(2)}) collective-permute-start(bf16[3,128,128]{2,1,0:T(8,128)(2,1)} %get-tuple-element.15), channel_id=1, source_target_pairs={{0,16},{2,18},{16,0},{18,2},{1,17},{3,19},{17,1},{19,3},{4,20},{6,... | collective-permute-start | bytes 294920 | tf_op jit(solution)/shard_map/ppermute | solution.py:297
  65.8 6.6 %collective-permute-start.10 = (bf16[3,128,128]{2,1,0:T(8,128)(2,1)}, bf16[3,128,128]{2,1,0:T(8,128)(2,1)S(1)}, u32[]{:S(2)}, u32[]{:S(2)}) collective-permute-start(bf16[3,128,128]{2,1,0:T(8,128)(2,1)} %get-tuple-element.16), channel_id=1, source_target_pairs={{0,18},{2,16},{16,2},{18,0},{1,19},{3,17},{17,3},{19,1},{4,22},{6,... | collective-permute-start | bytes 294920 | tf_op jit(solution)/shard_map/ppermute | solution.py:297
  67.2 5.2 %collective-permute-start.11 = (bf16[3,128,128]{2,1,0:T(8,128)(2,1)}, bf16[3,128,128]{2,1,0:T(8,128)(2,1)S(1)}, u32[]{:S(2)}, u32[]{:S(2)}) collective-permute-start(bf16[3,128,128]{2,1,0:T(8,128)(2,1)} %get-tuple-element.13.refs_1_.refs_0_), channel_id=1, source_target_pairs={{0,1},{1,0},{2,3},{3,2},{4,5},{5,4},{6,7},{7,6},{8,9},{9,8},{10,11... | collective-permute-start | bytes 294920 | tf_op jit(solution)/shard_map/ppermute | solution.py:281
  69.1 3.3 %collective-permute-start.12 = (bf16[3,128,128]{2,1,0:T(8,128)(2,1)S(1)}, bf16[3,128,128]{2,1,0:T(8,128)(2,1)S(1)}, u32[]{:S(2)}, u32[]{:S(2)}) collective-permute-start(bf16[3,128,128]{2,1,0:T(8,128)(2,1)S(1)} %collective-permute-done.8.refs_1_), channel_id=1, source_target_pairs={{0,1},{1,0},{2,3},{3,2},{4,5},{5,4},{6,7},{7,6},{8,9},{9,8},{10,11... | collective-permute-start | bytes 294920 | tf_op jit(solution)/shard_map/ppermute | solution.py:281
  71.0 1.4 %collective-permute-start.13 = (bf16[3,128,128]{2,1,0:T(8,128)(2,1)S(1)}, bf16[3,128,128]{2,1,0:T(8,128)(2,1)S(1)}, u32[]{:S(2)}, u32[]{:S(2)}) collective-permute-start(bf16[3,128,128]{2,1,0:T(8,128)(2,1)S(1)} %collective-permute-done.9.refs_2_), channel_id=1, source_target_pairs={{0,1},{1,0},{2,3},{3,2},{4,5},{5,4},{6,7},{7,6},{8,9},{9,8},{10,11... | collective-permute-start | bytes 294920 | tf_op jit(solution)/shard_map/ppermute | solution.py:281
  72.4 1.3 %collective-permute-start.14 = (bf16[3,128,128]{2,1,0:T(8,128)(2,1)S(1)}, bf16[3,128,128]{2,1,0:T(8,128)(2,1)S(1)}, u32[]{:S(2)}, u32[]{:S(2)}) collective-permute-start(bf16[3,128,128]{2,1,0:T(8,128)(2,1)S(1)} %collective-permute-done.10.refs_3_), channel_id=1, source_target_pairs={{0,1},{1,0},{2,3},{3,2},{4,5},{5,4},{6,7},{7,6},{8,9},{9,8},{10,11... | collective-permute-start | bytes 294920 | tf_op jit(solution)/shard_map/ppermute | solution.py:281
  73.7 0.9 %copy-start.1 = (bf16[3,128,128]{2,1,0:T(8,128)(2,1)S(1)}, bf16[3,128,128]{2,1,0:T(8,128)(2,1)}, u32[]{:S(2)}) copy-start(bf16[3,128,128]{2,1,0:T(8,128)(2,1)} %get-tuple-element.13.refs_1_.refs_0_) | copy-start | bytes 294916

commit v14 on v13

--- a/solution.py
+++ b/solution.py
@@ -119,52 +119,57 @@
     )(lengths, ids, tokens)
 
 
-def base_kernel(side, lengths, tok_ref, key_ref, *refs):
-    out_ref = refs[-1]
+def base_kernel(sides, lengths, tok_ref, key_ref, mine, other, flag_ref, total):
+    step = pl.program_id(0)
     part = jnp.dot(tok_ref[...], key_ref[...], preferred_element_type=jnp.float32)
-    step = pl.program_id(0)
 
     @pl.when(step == 0)
     def _():
-        out_ref[...] = part
+        total[...] = part
 
     @pl.when(step > 0)
     def _():
-        out_ref[...] += part
+        total[...] += part
 
     @pl.when(step == pl.num_programs(0) - 1)
     def _():
+        flag_ref[...] = jnp.zeros_like(flag_ref)
         blocks = lengths.shape[0]
-        block = out_ref.shape[0] // blocks
-        row = lax.broadcasted_iota(jnp.int32, (block, out_ref.shape[1]), 0)
-        for b in range(blocks):
-            here = slice(b * block, (b + 1) * block)
-            out_ref[here, :] = jnp.where(row < lengths[b], out_ref[here, :], 0.0)
-
-
-def base_half(tokens, base_key, side, sides, lengths, *after):
+        rows, wide = mine.shape
+        block = rows // blocks
+        row = lax.broadcasted_iota(jnp.int32, (block, wide), 0)
+        t = lax.axis_index("tensor")
+        for out, side in ((mine, t), (other, lax.rem(t + 1, sides))):
+            columns = pl.ds(pl.multiple_of(side * wide, LANES), wide)
+            for b in range(blocks):
+                here = slice(b * block, (b + 1) * block)
+                out[here, :] = jnp.where(row < lengths[b], total[here, columns], 0.0)
+
+
+def base_halves(tokens, base_key, sides, lengths):
     rows, depth = tokens.shape
-    wide = base_key.shape[1] // sides
-    step = 1024
-    return pl.pallas_call(
-        base_kernel,
+    features = base_key.shape[1]
+    wide = features // sides
+    step = 512
+    half = pl.BlockSpec((rows, wide), lambda i, n: (0, 0))
+    return pl.pallas_call(
+        functools.partial(base_kernel, sides),
         grid_spec=pltpu.PrefetchScalarGridSpec(
-            num_scalar_prefetch=2,
+            num_scalar_prefetch=1,
             grid=(depth // step,),
             in_specs=[
-                pl.BlockSpec((rows, step), lambda i, s, n: (0, i)),
-                pl.BlockSpec((step, wide), lambda i, s, n: (i, s[0])),
-            ]
-            + [ANY] * len(after),
-            out_specs=pl.BlockSpec((rows, wide), lambda i, s, n: (0, 0)),
+                pl.BlockSpec((rows, step), lambda i, n: (0, i)),
+                pl.BlockSpec((step, features), lambda i, n: (i, 0)),
+            ],
+            out_specs=[half, half, pl.BlockSpec((8, LANES), lambda i, n: (0, 0))],
+            scratch_shapes=[pltpu.VMEM((rows, features), jnp.float32)],
         ),
-        out_shape=jax.ShapeDtypeStruct((rows, wide), jnp.float32),
-        cost_estimate=pl.CostEstimate(
-            flops=0, bytes_accessed=0, transcendentals=0
-        ),
+        out_shape=[jax.ShapeDtypeStruct((rows, wide), jnp.float32)] * 2
+        + [jax.ShapeDtypeStruct((8, LANES), jnp.float32)],
+        cost_estimate=pl.CostEstimate(flops=0, bytes_accessed=0, transcendentals=0),
         compiler_params=FULL,
         name="base",
-    )(side.reshape(1), lengths, tokens, base_key, *after)
+    )(lengths, tokens, base_key)
 
 
 def mate_at(k, sign, groups, pair):
@@ -174,40 +179,54 @@
     return g * pair + y
 
 
-def rank_kernel(groups, ring, pair, rows, owner, tok, *refs):
+def collect_kernel(*refs):
+    sems, held, pieces = refs[-1], refs[-2], refs[:-2]
+    copies, start = [], 0
+    for j, piece in enumerate(pieces):
+        copies.append(pltpu.make_async_copy(piece, held.at[pl.ds(start, piece.shape[0])], sems.at[j]))
+        start += piece.shape[0]
+    for copy in copies:
+        copy.start()
+    for copy in copies:
+        copy.wait()
+
+
+def collect(pieces):
+    count = sum(piece.shape[0] for piece in pieces)
+    return pl.pallas_call(
+        collect_kernel,
+        in_specs=[ANY] * len(pieces),
+        out_specs=VMEM,
+        out_shape=jax.ShapeDtypeStruct((count,) + pieces[0].shape[1:], pieces[0].dtype),
+        scratch_shapes=[pltpu.SemaphoreType.DMA((len(pieces),))],
+        compiler_params=ROOM,
+        name="collect",
+    )(*pieces)
+
+
+def rank_kernel(groups, ring, pair, rows, owner, tok, held, *outs):
     shares = groups * pair
-    tok_held, held, tok_sems, sems = refs[-4:]
-    outs = refs[-4 - shares : -4]
-    pieces = refs[: ring * pair]
-    per, rank = pieces[0].shape[:2]
+    per, rank = held.shape[0] // (ring * pair), held.shape[1]
     blocks, _, block = outs[0].shape
     feats = tok.shape[2]
     z, y = lax.axis_index("ring"), lax.axis_index("pair")
-    mates = [mate_at(k, 1, groups, pair) for k in range(shares)]
-    copies = [pltpu.make_async_copy(piece, held.at[pl.ds(j * per, per)], sems.at[j]) for j, piece in enumerate(pieces)]
-    tok_copies = [
-        pltpu.make_async_copy(tok.at[mates[k]], tok_held.at[k], tok_sems.at[k])
-        for k in range(shares)
-    ]
-    for copy in copies + tok_copies:
-        copy.start()
-    for copy in copies:
-        copy.wait()
     lane = lax.broadcasted_iota(jnp.int32, (16, LANES), 1)
     row = lax.broadcasted_iota(jnp.int32, (16, LANES), 0)
-    for k in range(shares):
-        tok_copies[k].wait()
-        named = tok_held[k, rows:, :LANES].astype(jnp.float32)
-        ids = [jnp.sum(jnp.where((lane == b) & (row == 0), named, 0.0)).astype(jnp.int32) for b in range(blocks)]
+    mates = [mate_at(k, 1, groups, pair) for k in range(shares)]
+    ids = []
+    for mate in mates:
+        named = tok[mate, rows:, :LANES].astype(jnp.float32)
+        ids += [jnp.sum(jnp.where((lane == b) & (row == 0), named, 0.0)).astype(jnp.int32) for b in range(blocks)]
+    for k, mate in enumerate(mates):
         for b in range(blocks):
-            slot = owner[ids[b]]
+            slot = owner[ids[k * blocks + b]]
             chip = slot // per
             away = lax.rem(chip // pair - z + ring, ring)
             way = lax.rem(lax.rem(chip, pair) - y + pair, pair)
             at = (way * ring + away) * per + lax.rem(slot, per)
             part = lax.dot_general(
                 held[at, :, :feats],
-                tok_held[k, b * block : (b + 1) * block, :],
+                tok[mate, b * block : (b + 1) * block, :],
                 (((1,), (1,)), ((), ())),
                 preferred_element_type=jnp.float32,
             )
@@ -215,25 +234,17 @@
             outs[k][b, rank:, :] = held[at, :, feats:]
 
 
-def rank_parts(owner, tok, pieces, groups, ring, pair, rows, blocks):
-    shares, tall, feats = tok.shape
-    block = rows // blocks
-    per, rank, wide = pieces[0].shape
+def rank_parts(owner, tok, held, groups, ring, pair, rows, blocks):
+    shares, rank = tok.shape[0], held.shape[1]
     return pl.pallas_call(
         functools.partial(rank_kernel, groups, ring, pair, rows),
-        in_specs=[SMEM, ANY] + [ANY] * len(pieces),
+        in_specs=[SMEM, VMEM, VMEM],
         out_specs=[VMEM] * shares,
-        out_shape=[jax.ShapeDtypeStruct((blocks, 2 * rank, block), tok.dtype)] * shares,
-        scratch_shapes=[
-            pltpu.VMEM(tok.shape, tok.dtype),
-            pltpu.VMEM((len(pieces) * per, rank, wide), tok.dtype),
-            pltpu.SemaphoreType.DMA((shares,)),
-            pltpu.SemaphoreType.DMA((len(pieces),)),
-        ],
+        out_shape=[jax.ShapeDtypeStruct((blocks, 2 * rank, rows // blocks), tok.dtype)] * shares,
         cost_estimate=pl.CostEstimate(flops=2 * tok.size * rank, bytes_accessed=2 * tok.size, transcendentals=0),
-        compiler_params=FULL,
+        compiler_params=ROOM,
         name="rank",
-    )(owner, tok, *pieces)
+    )(owner, tok, held)
 
 
 def final_kernel(groups, pair, base_a, base_b, *refs):
@@ -273,7 +284,6 @@
     groups, ring, pair = lax.axis_size("groups"), lax.axis_size("ring"), lax.axis_size("pair")
     sides = lax.axis_size("tensor")
     shares = groups * pair
-    t = lax.axis_index("tensor")
     rows = tokens.shape[0]
     blocks = lengths.shape[0]
 
@@ -316,15 +326,14 @@
     firsts = [first_hops(piece) for piece in [packed[0]] + swapped]
     tok = to_plane(hand_on(slabs, *swapped, firsts[0][ring - 1]))
 
-    base_out = base_half(tokens, base_key, (t + 1) % sides, sides, lengths)
-    base_mine = base_half(tokens, base_key, t, sides, lengths)
+    base_mine, base_out, flag = base_halves(tokens, base_key, sides, lengths)
     pieces = [
-        more_hops(held, way, base_out, base_mine)
+        more_hops(held, way, flag)
         for way, held in enumerate(firsts)
     ]
 
     flat = [piece for way in pieces for piece in way]
-    parts = rank_parts(owner_slot, tok, flat, groups, ring, pair, rows, blocks)
+    parts = rank_parts(owner_slot, tok, collect(flat), groups, ring, pair, rows, blocks)
     mine = [parts[0]] + [in_plane(parts[k], k // pair, k % pair) for k in range(1, shares)]
     theirs = [across(part) for part in mine]
     base_in = across(hand_on(base_out, parts[0]))

time: 76 us -> 75.6 us (level)
  local copies, waits for them, and re-layouts: 3.1 us -> 8.41 us
  Pallas kernels: 25.7 us -> 20.9 us
  starting transfers between devices: 19.3 us -> 17.1 us
  waiting for transfers between devices: 27.4 us -> 28.5 us
    unnamed x22, local copies, waits for them, and re-layouts: 3.1 us -> 8.41 us
    ppermute x6, waiting for transfers between devices: 15.4 us -> 20 us  [along(): lax.ppermute(x, 'ring', [(a, (a + step) % ring) for a in range(ring)])]
    pallas_call x1, Pallas kernels: 5.82 us -> 1.64 us  [rank_parts(): pl.pallas_call(functools.partial(rank_kernel, groups, ring, pair, rows),...]
    all_to_all x1, waiting for transfers between devices: 3.66 us -> 0.01 us  [to_plane(): return lax.all_to_all(x, PLANE, split_axis=0, concat_axis=0, tiled=True)]
    all_to_all x1, starting transfers between devices: 4.81 us -> 3.71 us  [to_plane(): return lax.all_to_all(x, PLANE, split_axis=0, concat_axis=0, tiled=True)]
    ppermute x6, starting transfers between devices: 7.79 us -> 6.87 us  [along(): lax.ppermute(x, 'ring', [(a, (a + step) % ring) for a in range(ring)])]
where the time goes in v14:
time: 75.6 us; the launch traced here: 75 us
  waiting for transfers between devices  28.5 us (38%)
  Pallas kernels  20.9 us (28%)
  starting transfers between devices  17.1 us (23%)
  local copies, waits for them, and re-layouts  8.41 us (11%)
    ppermute x6, waiting for transfers between devices, along(): lax.ppermute(x, 'ring', [(a, (a + step) % ring) for a in range(ring)])  20 us
    pallas_call x1, Pallas kernels, base_halves(): pl.pallas_call(functools.partial(base_kernel, sides), grid_spec=pltpu.Pre...  11.3 us
    unnamed x22, local copies, waits for them, and re-layouts  8.41 us
    ppermute x6, starting transfers between devices, along(): lax.ppermute(x, 'ring', [(a, (a + step) % ring) for a in range(ring)])  6.87 us
    ppermute x3, waiting for transfers between devices, in_plane(): return lax.ppermute(x, PLANE, pairs)  5.16 us
    all_to_all x1, starting transfers between devices, to_plane(): return lax.all_to_all(x, PLANE, split_axis=0, concat_axis=0, tiled=True)  3.71 us
    pallas_call x1, Pallas kernels, spread(): pl.pallas_call(spread_kernel, in_specs=[SMEM, SMEM, ANY], out_specs=ANY,...  3.62 us
    ppermute x3, starting transfers between devices, in_plane(): return lax.ppermute(x, PLANE, pairs)  3.49 us
  transfers between devices with their start and end apart: 16, of which 10 were waited for; matrix products, arithmetic and copies ran while one was open for 0% of the time, Pallas kernels for 22%

profile of v14, /device:TPU:0, one launch (start us, length us, event | category | flops | bytes accessed | tf_op | source)
XLA Modules:
  0.0 75.0 jit_solution(989270196688900635)
XLA Ops:
  0.0 1.9 %pack.1 = (bf16[2,64,1152]{2,1,0:T(8,128)(2,1)}, bf16[2,64,1152]{2,1,0:T(8,128)(2,1)}) custom-call(bf16[2,64,4096]{2,1,0:T(8,128)(2,1)} %bitcast.2, bf16[2,64,512]{2,1,0:T(8,128)(2,1)} %up.1), custom_call_target="tpu_custom_call" | custom-call | tf_op jit(solution)/shard_map/pack/pallas_call | solution.py:57
  1.9 3.0 %collective-permute-start = (bf16[2,64,1152]{2,1,0:T(8,128)(2,1)}, bf16[2,64,1152]{2,1,0:T(8,128)(2,1)S(1)}, u32[]{:S(2)}, u32[]{:S(2)}) collective-permute-start(bf16[2,64,1152]{2,1,0:T(8,128)(2,1)} %get-tuple-element.16), channel_id=1, source_target_pairs={{0,2},{2,0},{1,3},{3,1},{4,6},{6,4},{5,7},{7,5},{8,10},{10,8},{9,1... | collective-permute-start | bytes 884744 | tf_op jit(solution)/shard_map/ppermute | solution.py:324
  4.9 1.6 %collective-permute-start.1 = (bf16[2,64,1152]{2,1,0:T(8,128)(2,1)}, bf16[2,64,1152]{2,1,0:T(8,128)(2,1)S(1)}, u32[]{:S(2)}, u32[]{:S(2)}) collective-permute-start(bf16[2,64,1152]{2,1,0:T(8,128)(2,1)} %get-tuple-element.17.refs_0_), channel_id=1, source_target_pairs={{0,4},{4,8},{8,12},{12,0},{1,5},{5,9},{9,13},{13,1},{2,6},{6,10},{... | collective-permute-start | bytes 884744 | tf_op jit(solution)/shard_map/ppermute | solution.py:297
  6.5 3.6 %spread.1.refs_0_ = bf16[4,400,1024]{2,1,0:T(8,128)(2,1)} custom-call(s32[3]{0:T(128)} %lengths.3, s32[3]{0:T(128)} %bitcast.3, bf16[384,4096]{1,0:T(8,128)(2,1)} %tok.1), custom_call_target="tpu_custom_call" | custom-call | tf_op jit(solution)/shard_map/spread/pallas_call | solution.py:107
  10.1 2.0 %collective-permute-done.refs_1_.refs_4_ = bf16[2,64,1152]{2,1,0:T(8,128)(2,1)S(1)} collective-permute-done((bf16[2,64,1152]{2,1,0:T(8,128)(2,1)}, bf16[2,64,1152]{2,1,0:T(8,128)(2,1)S(1)}, u32[]{:S(2)}, u32[]{:S(2)}) %collective-permute-start) | collective-permute-done | bytes 294944 | tf_op jit(solution)/shard_map/ppermute | solution.py:324
  12.1 3.3 %collective-permute-done.1.refs_2_.refs_0_ = bf16[2,64,1152]{2,1,0:T(8,128)(2,1)S(1)} collective-permute-done((bf16[2,64,1152]{2,1,0:T(8,128)(2,1)}, bf16[2,64,1152]{2,1,0:T(8,128)(2,1)S(1)}, u32[]{:S(2)}, u32[]{:S(2)}) %collective-permute-start.1) | collective-permute-done | bytes 294944 | tf_op jit(solution)/shard_map/ppermute | solution.py:297
  15.5 0.7 copy-done.2
  16.2 3.7 %all-to-all-start = ((bf16[4,400,1024]{2,1,0:T(8,128)(2,1)}), bf16[4,400,1024]{2,1,0:T(8,128)(2,1)S(1)}, u32[]{:S(2)}, u32[]{:S(2)}) async-start(bf16[4,400,1024]{2,1,0:T(8,128)(2,1)} %hand.4), calls=%async_computation | async-start | bytes 6553600 | tf_op jit(solution)/shard_map/all_to_all | solution.py:294
  19.9 1.8 %collective-permute-start.2 = (bf16[2,64,1152]{2,1,0:T(8,128)(2,1)}, bf16[2,64,1152]{2,1,0:T(8,128)(2,1)}, u32[]{:S(2)}, u32[]{:S(2)}) collective-permute-start(bf16[2,64,1152]{2,1,0:T(8,128)(2,1)} %get-tuple-element.17.refs_0_), channel_id=1, source_target_pairs={{0,12},{4,0},{8,4},{12,8},{1,13},{5,1},{9,5},{13,9},{2,14},{6,2},{... | collective-permute-start | bytes 884744 | tf_op jit(solution)/shard_map/ppermute | solution.py:297
  21.7 0.4 collective-permute-start.4
  22.2 1.6 %collective-permute-start.5 = (bf16[2,64,1152]{2,1,0:T(8,128)(2,1)}, bf16[2,64,1152]{2,1,0:T(8,128)(2,1)}, u32[]{:S(2)}, u32[]{:S(2)}) collective-permute-start(bf16[2,64,1152]{2,1,0:T(8,128)(2,1)} %copy-done.4), channel_id=1, source_target_pairs={{0,4},{4,8},{8,12},{12,0},{1,5},{5,9},{9,13},{13,1},{2,6},{6,10},{... | collective-permute-start | bytes 884744 | tf_op jit(solution)/shard_map/ppermute | solution.py:297
  23.7 11.3 %base.1 = (f32[384,512]{1,0:T(8,128)}, f32[384,512]{1,0:T(8,128)}, f32[8,128]{1,0:T(8,128)}) custom-call(s32[3]{0:T(128)} %lengths.3, bf16[384,4096]{1,0:T(8,128)(2,1)} %tok.1, bf16[4096,1024]{1,0:T(8,128)(2,1)} %key_ref.1), custom_call_target="tpu_custom_call" | custom-call | tf_op jit(solution)/shard_map/base/pallas_call | solution.py:155
  35.0 0.0 collective-permute-done.2.refs_1_
  35.1 0.3 collective-permute-start.3
  35.4 1.1 %collective-permute-done.4.refs_0_ = bf16[2,64,1152]{2,1,0:T(8,128)(2,1)} collective-permute-done((bf16[2,64,1152]{2,1,0:T(8,128)(2,1)}, bf16[2,64,1152]{2,1,0:T(8,128)(2,1)}, u32[]{:S(2)}, u32[]{:S(2)}) %collective-permute-start.4) | collective-permute-done | bytes 294944 | tf_op jit(solution)/shard_map/ppermute | solution.py:297
  36.5 6.6 %collective-permute-done.5.refs_1_.refs_7_ = bf16[2,64,1152]{2,1,0:T(8,128)(2,1)} collective-permute-done((bf16[2,64,1152]{2,1,0:T(8,128)(2,1)}, bf16[2,64,1152]{2,1,0:T(8,128)(2,1)}, u32[]{:S(2)}, u32[]{:S(2)}) %collective-permute-start.5) | collective-permute-done | bytes 294944 | tf_op jit(solution)/shard_map/ppermute | solution.py:297
  43.1 1.1 %collective-permute-start.6 = (bf16[2,64,1152]{2,1,0:T(8,128)(2,1)}, bf16[2,64,1152]{2,1,0:T(8,128)(2,1)S(1)}, u32[]{:S(2)}, u32[]{:S(2)}) collective-permute-start(bf16[2,64,1152]{2,1,0:T(8,128)(2,1)} %hand.6.refs_5_), channel_id=1, source_target_pairs={{0,12},{4,0},{8,4},{12,8},{1,13},{5,1},{9,5},{13,9},{2,14},{6,2},{... | collective-permute-start | bytes 884744 | tf_op jit(solution)/shard_map/ppermute | solution.py:297
  44.2 4.2 %collective-permute-done.3.refs_2_ = bf16[2,64,1152]{2,1,0:T(8,128)(2,1)} collective-permute-done((bf16[2,64,1152]{2,1,0:T(8,128)(2,1)}, bf16[2,64,1152]{2,1,0:T(8,128)(2,1)}, u32[]{:S(2)}, u32[]{:S(2)}) %collective-permute-start.3) | collective-permute-done | bytes 294944 | tf_op jit(solution)/shard_map/ppermute | solution.py:297
  48.5 4.7 %collective-permute-done.6.refs_6_ = bf16[2,64,1152]{2,1,0:T(8,128)(2,1)S(1)} collective-permute-done((bf16[2,64,1152]{2,1,0:T(8,128)(2,1)}, bf16[2,64,1152]{2,1,0:T(8,128)(2,1)S(1)}, u32[]{:S(2)}, u32[]{:S(2)}) %collective-permute-start.6) | collective-permute-done | bytes 294944 | tf_op jit(solution)/shard_map/ppermute | solution.py:297
  53.2 1.0 %copy-done.3 = bf16[2,64,1152]{2,1,0:T(8,128)(2,1)S(1)} copy-done((bf16[2,64,1152]{2,1,0:T(8,128)(2,1)S(1)}, bf16[2,64,1152]{2,1,0:T(8,128)(2,1)}, u32[]{:S(2)}) %copy-start.3) | copy-done | bytes 294936
  54.2 1.0 %copy-done.9 = bf16[2,64,1152]{2,1,0:T(8,128)(2,1)S(1)} copy-done((bf16[2,64,1152]{2,1,0:T(8,128)(2,1)S(1)}, bf16[2,64,1152]{2,1,0:T(8,128)(2,1)}, u32[]{:S(2)}) %copy-start.9) | copy-done | bytes 294936
  55.1 1.4 %collect.1.held = bf16[16,64,1152]{2,1,0:T(8,128)(2,1)S(1)} custom-call(bf16[2,64,1152]{2,1,0:T(8,128)(2,1)S(1)} %copy-done.9, bf16[2,64,1152]{2,1,0:T(8,128)(2,1)} %collective-permute-done.2.refs_1_, bf16[2,64,1152]{2,1,0:T(8,128)(2,1)} %collective-permute-done.3.refs_2_, bf16[2,64,1152]{2,1,0:T(8,128)(2,1)S(1)} %copy-done.3, ...), custom_call_target="tpu_custom_call" | custom-call | tf_op jit(solution)/shard_map/collect/pallas_call | solution.py:196
  56.5 0.0 copy-start
  56.5 1.4 %copy-done = bf16[16,64,1152]{2,1,0:T(8,128)(2,1)} copy-done((bf16[16,64,1152]{2,1,0:T(8,128)(2,1)}, bf16[16,64,1152]{2,1,0:T(8,128)(2,1)S(1)}, u32[]{:S(2)}) %copy-start) | copy-done | bytes 2359320
  58.0 0.0 all-to-all-done.tok
  58.0 1.7 %copy-done.1 = bf16[16,64,1152]{2,1,0:T(8,128)(2,1)S(1)} copy-done((bf16[16,64,1152]{2,1,0:T(8,128)(2,1)S(1)}, bf16[16,64,1152]{2,1,0:T(8,128)(2,1)}, u32[]{:S(2)}) %copy-start.1) | copy-done | bytes 2359320
  59.6 1.6 %rank.1 = (bf16[3,128,128]{2,1,0:T(8,128)(2,1)S(1)}, bf16[3,128,128]{2,1,0:T(8,128)(2,1)S(1)}, bf16[3,128,128]{2,1,0:T(8,128)(2,1)S(1)}, bf16[3,128,128]{2,1,0:T(8,128)(2,1)S(1)}) custom-call(s32[16]{0:T(128)S(1)} %copy-done.10, bf16[4,400,1024]{2,1,0:T(8,128)(2,1)S(1)} %all-to-all-done.tok, bf16[16,64,1152]{2,1,0:T(8,128)(2,1)S(1)} %copy-done.1), custom_call_target="tpu_custom_call" | custom-call | flops 209715200 | bytes 3276800 | tf_op jit(solution)/shard_map/rank/pallas_call | solution.py:239
  61.3 0.0 copy-start.7
  61.3 0.6 copy-done.7
  61.9 0.0 collective-permute-start.7
  61.9 1.6 %collective-permute-start.8 = (bf16[3,128,128]{2,1,0:T(8,128)(2,1)S(1)}, bf16[3,128,128]{2,1,0:T(8,128)(2,1)S(1)}, u32[]{:S(2)}, u32[]{:S(2)}) collective-permute-start(bf16[3,128,128]{2,1,0:T(8,128)(2,1)S(1)} %get-tuple-element.20), channel_id=1, source_target_pairs={{0,2},{2,0},{16,18},{18,16},{1,3},{3,1},{17,19},{19,17},{4,6},{6,4... | collective-permute-start | bytes 294920 | tf_op jit(solution)/shard_map/ppermute | solution.py:307
  63.6 1.5 %collective-permute-start.9 = (bf16[3,128,128]{2,1,0:T(8,128)(2,1)S(1)}, bf16[3,128,128]{2,1,0:T(8,128)(2,1)S(1)}, u32[]{:S(2)}, u32[]{:S(2)}) collective-permute-start(bf16[3,128,128]{2,1,0:T(8,128)(2,1)S(1)} %get-tuple-element.21), channel_id=1, source_target_pairs={{0,16},{2,18},{16,0},{18,2},{1,17},{3,19},{17,1},{19,3},{4,20},{6,... | collective-permute-start | bytes 294920 | tf_op jit(solution)/shard_map/ppermute | solution.py:307
  65.0 0.4 collective-permute-start.10
  65.4 0.0 collective-permute-start.11
  65.4 1.7 %collective-permute-done.8.refs_1_ = bf16[3,128,128]{2,1,0:T(8,128)(2,1)S(1)} collective-permute-done((bf16[3,128,128]{2,1,0:T(8,128)(2,1)S(1)}, bf16[3,128,128]{2,1,0:T(8,128)(2,1)S(1)}, u32[]{:S(2)}, u32[]{:S(2)}) %collective-permute-start.8) | collective-permute-done | bytes 98336 | tf_op jit(solution)/shard_map/ppermute | solution.py:307
  67.1 0.0 collective-permute-start.12
  67.1 2.1 %collective-permute-done.9.refs_2_ = bf16[3,128,128]{2,1,0:T(8,128)(2,1)S(1)} collective-permute-done((bf16[3,128,128]{2,1,0:T(8,128)(2,1)S(1)}, bf16[3,128,128]{2,1,0:T(8,128)(2,1)S(1)}, u32[]{:S(2)}, u32[]{:S(2)}) %collective-permute-start.9) | collective-permute-done | bytes 98336 | tf_op jit(solution)/shard_map/ppermute | solution.py:307
  69.2 0.0 collective-permute-start.13
  69.2 1.4 %collective-permute-done.10.refs_3_ = bf16[3,128,128]{2,1,0:T(8,128)(2,1)S(1)} collective-permute-done((bf16[3,128,128]{2,1,0:T(8,128)(2,1)S(1)}, bf16[3,128,128]{2,1,0:T(8,128)(2,1)S(1)}, u32[]{:S(2)}, u32[]{:S(2)}) %collective-permute-start.10) | collective-permute-done | bytes 98336 | tf_op jit(solution)/shard_map/ppermute | solution.py:307
  70.6 0.0 collective-permute-start.14
  70.6 0.0 collective-permute-done.11.refs_4_
  70.6 0.0 collective-permute-done.12.refs_5_
  70.6 0.0 collective-permute-done.13.refs_6_
  70.6 1.3 %collective-permute-done.14.refs_7_ = bf16[3,128,128]{2,1,0:T(8,128)(2,1)S(1)} collective-permute-done((bf16[3,128,128]{2,1,0:T(8,128)(2,1)S(1)}, bf16[3,128,128]{2,1,0:T(8,128)(2,1)S(1)}, u32[]{:S(2)}, u32[]{:S(2)}) %collective-permute-start.14) | collective-permute-done | bytes 98336 | tf_op jit(solution)/shard_map/ppermute | solution.py:291
  71.9 0.0 collective-permute-done.7.base_b
  71.9 1.1 %copy-done.6 = f32[384,512]{1,0:T(8,128)S(1)} copy-done((f32[384,512]{1,0:T(8,128)S(1)}, f32[384,512]{1,0:T(8,128)}, u32[]{:S(2)}) %copy-start.6) | copy-done | bytes 786456
  73.0 0.9 %copy-done.8 = bf16[3,128,128]{2,1,0:T(8,128)(2,1)S(1)} copy-done((bf16[3,128,128]{2,1,0:T(8,128)(2,1)S(1)}, bf16[3,128,128]{2,1,0:T(8,128)(2,1)}, u32[]{:S(2)}) %copy-start.8) | copy-done | bytes 98328
  73.9 1.0 %final.1 = bf16[384,512]{1,0:T(8,128)(2,1)} custom-call(f32[384,512]{1,0:T(8,128)S(1)} %copy-done.6, f32[384,512]{1,0:T(8,128)S(1)} %collective-permute-done.7.base_b, bf16[3,128,128]{2,1,0:T(8,128)(2,1)S(1)} %copy-done.8, bf16[3,128,128]{2,1,0:T(8,128)(2,1)S(1)} %collective-permute-done.8.refs_1_, bf16[3,128,128]{2,1,0:T(8,128)(2,1)S(1)} %collective-permute-done.9.refs_2_, ...), custom_call_target="tpu_custom_call" | custom-call | tf_op jit(solution)/shard_map/final/pallas_call | solution.py:272
  (16 shorter events, 0.0 us)
Async XLA Ops:
  1.9 10.2 %collective-permute-start = (bf16[2,64,1152]{2,1,0:T(8,128)(2,1)}, bf16[2,64,1152]{2,1,0:T(8,128)(2,1)S(1)}, u32[]{:S(2)}, u32[]{:S(2)}) collective-permute-start(bf16[2,64,1152]{2,1,0:T(8,128)(2,1)} %get-tuple-element.16), channel_id=1, source_target_pairs={{0,2},{2,0},{1,3},{3,1},{4,6},{6,4},{5,7},{7,5},{8,10},{10,8},{9,1... | collective-permute-start | bytes 884744 | tf_op jit(solution)/shard_map/ppermute | solution.py:324
  4.9 10.5 %collective-permute-start.1 = (bf16[2,64,1152]{2,1,0:T(8,128)(2,1)}, bf16[2,64,1152]{2,1,0:T(8,128)(2,1)S(1)}, u32[]{:S(2)}, u32[]{:S(2)}) collective-permute-start(bf16[2,64,1152]{2,1,0:T(8,128)(2,1)} %get-tuple-element.17.refs_0_), channel_id=1, source_target_pairs={{0,4},{4,8},{8,12},{12,0},{1,5},{5,9},{9,13},{13,1},{2,6},{6,10},{... | collective-permute-start | bytes 884744 | tf_op jit(solution)/shard_map/ppermute | solution.py:297
  12.1 3.3 %copy-start.4 = (bf16[2,64,1152]{2,1,0:T(8,128)(2,1)}, bf16[2,64,1152]{2,1,0:T(8,128)(2,1)S(1)}, u32[]{:S(2)}) copy-start(bf16[2,64,1152]{2,1,0:T(8,128)(2,1)S(1)} %collective-permute-done.refs_1_.refs_4_) | copy-start | bytes 884740
  15.5 0.7 copy-start.2
  16.2 41.8 %all-to-all-start = ((bf16[4,400,1024]{2,1,0:T(8,128)(2,1)}), bf16[4,400,1024]{2,1,0:T(8,128)(2,1)S(1)}, u32[]{:S(2)}, u32[]{:S(2)}) async-start(bf16[4,400,1024]{2,1,0:T(8,128)(2,1)} %hand.4), calls=%async_computation | async-start | bytes 6553600 | tf_op jit(solution)/shard_map/all_to_all | solution.py:294
  19.9 33.3 %copy-start.5 = (bf16[2,64,1152]{2,1,0:T(8,128)(2,1)S(1)}, bf16[2,64,1152]{2,1,0:T(8,128)(2,1)}, u32[]{:S(2)}) copy-start(bf16[2,64,1152]{2,1,0:T(8,128)(2,1)} %copy-done.4) | copy-start | bytes 884740
  19.9 15.1 %collective-permute-start.2 = (bf16[2,64,1152]{2,1,0:T(8,128)(2,1)}, bf16[2,64,1152]{2,1,0:T(8,128)(2,1)}, u32[]{:S(2)}, u32[]{:S(2)}) collective-permute-start(bf16[2,64,1152]{2,1,0:T(8,128)(2,1)} %get-tuple-element.17.refs_0_), channel_id=1, source_target_pairs={{0,12},{4,0},{8,4},{12,8},{1,13},{5,1},{9,5},{13,9},{2,14},{6,2},{... | collective-permute-start | bytes 884744 | tf_op jit(solution)/shard_map/ppermute | solution.py:297
  21.7 14.8 %collective-permute-start.4 = (bf16[2,64,1152]{2,1,0:T(8,128)(2,1)}, bf16[2,64,1152]{2,1,0:T(8,128)(2,1)}, u32[]{:S(2)}, u32[]{:S(2)}) collective-permute-start(bf16[2,64,1152]{2,1,0:T(8,128)(2,1)} %copy-done.4), channel_id=1, source_target_pairs={{0,12},{4,0},{8,4},{12,8},{1,13},{5,1},{9,5},{13,9},{2,14},{6,2},{... | collective-permute-start | bytes 884744 | tf_op jit(solution)/shard_map/ppermute | solution.py:297
  22.2 20.9 %collective-permute-start.5 = (bf16[2,64,1152]{2,1,0:T(8,128)(2,1)}, bf16[2,64,1152]{2,1,0:T(8,128)(2,1)}, u32[]{:S(2)}, u32[]{:S(2)}) collective-permute-start(bf16[2,64,1152]{2,1,0:T(8,128)(2,1)} %copy-done.4), channel_id=1, source_target_pairs={{0,4},{4,8},{8,12},{12,0},{1,5},{5,9},{9,13},{13,1},{2,6},{6,10},{... | collective-permute-start | bytes 884744 | tf_op jit(solution)/shard_map/ppermute | solution.py:297
  35.0 22.9 %copy-start.10 = (s32[16]{0:T(128)S(1)}, s32[16]{0:T(128)}, u32[]{:S(2)}) copy-start(s32[16]{0:T(128)} %owner.1) | copy-start | bytes 196
  35.1 13.4 %collective-permute-start.3 = (bf16[2,64,1152]{2,1,0:T(8,128)(2,1)}, bf16[2,64,1152]{2,1,0:T(8,128)(2,1)}, u32[]{:S(2)}, u32[]{:S(2)}) collective-permute-start(bf16[2,64,1152]{2,1,0:T(8,128)(2,1)} %hand.5.refs_3_), channel_id=1, source_target_pairs={{0,4},{4,8},{8,12},{12,0},{1,5},{5,9},{9,13},{13,1},{2,6},{6,10},{... | collective-permute-start | bytes 884744 | tf_op jit(solution)/shard_map/ppermute | solution.py:297
  43.1 10.1 %collective-permute-start.6 = (bf16[2,64,1152]{2,1,0:T(8,128)(2,1)}, bf16[2,64,1152]{2,1,0:T(8,128)(2,1)S(1)}, u32[]{:S(2)}, u32[]{:S(2)}) collective-permute-start(bf16[2,64,1152]{2,1,0:T(8,128)(2,1)} %hand.6.refs_5_), channel_id=1, source_target_pairs={{0,12},{4,0},{8,4},{12,8},{1,13},{5,1},{9,5},{13,9},{2,14},{6,2},{... | collective-permute-start | bytes 884744 | tf_op jit(solution)/shard_map/ppermute | solution.py:297
  53.2 1.0 %copy-start.3 = (bf16[2,64,1152]{2,1,0:T(8,128)(2,1)S(1)}, bf16[2,64,1152]{2,1,0:T(8,128)(2,1)}, u32[]{:S(2)}) copy-start(bf16[2,64,1152]{2,1,0:T(8,128)(2,1)} %hand.5.refs_3_) | copy-start | bytes 884740
  54.2 1.0 %copy-start.9 = (bf16[2,64,1152]{2,1,0:T(8,128)(2,1)S(1)}, bf16[2,64,1152]{2,1,0:T(8,128)(2,1)}, u32[]{:S(2)}) copy-start(bf16[2,64,1152]{2,1,0:T(8,128)(2,1)} %get-tuple-element.17.refs_0_) | copy-start | bytes 884740
  56.5 1.4 %copy-start = (bf16[16,64,1152]{2,1,0:T(8,128)(2,1)}, bf16[16,64,1152]{2,1,0:T(8,128)(2,1)S(1)}, u32[]{:S(2)}) copy-start(bf16[16,64,1152]{2,1,0:T(8,128)(2,1)S(1)} %collect.1.held) | copy-start | bytes 7077892
  58.0 1.7 %copy-start.1 = (bf16[16,64,1152]{2,1,0:T(8,128)(2,1)S(1)}, bf16[16,64,1152]{2,1,0:T(8,128)(2,1)}, u32[]{:S(2)}) copy-start(bf16[16,64,1152]{2,1,0:T(8,128)(2,1)} %copy-done) | copy-start | bytes 7077892
  61.3 0.6 copy-start.7
  61.9 10.0 %collective-permute-start.7 = (f32[384,512]{1,0:T(8,128)}, f32[384,512]{1,0:T(8,128)S(1)}, u32[]{:S(2)}, u32[]{:S(2)}) collective-permute-start(f32[384,512]{1,0:T(8,128)} %hand.7), channel_id=1, source_target_pairs={{0,1},{1,0},{2,3},{3,2},{4,5},{5,4},{6,7},{7,6},{8,9},{9,8},{10,11... | collective-permute-start | bytes 2359304 | tf_op jit(solution)/shard_map/ppermute | solution.py:291
  61.9 5.2 %collective-permute-start.8 = (bf16[3,128,128]{2,1,0:T(8,128)(2,1)S(1)}, bf16[3,128,128]{2,1,0:T(8,128)(2,1)S(1)}, u32[]{:S(2)}, u32[]{:S(2)}) collective-permute-start(bf16[3,128,128]{2,1,0:T(8,128)(2,1)S(1)} %get-tuple-element.20), channel_id=1, source_target_pairs={{0,2},{2,0},{16,18},{18,16},{1,3},{3,1},{17,19},{19,17},{4,6},{6,4... | collective-permute-start | bytes 294920 | tf_op jit(solution)/shard_map/ppermute | solution.py:307
  63.6 5.6 %collective-permute-start.9 = (bf16[3,128,128]{2,1,0:T(8,128)(2,1)S(1)}, bf16[3,128,128]{2,1,0:T(8,128)(2,1)S(1)}, u32[]{:S(2)}, u32[]{:S(2)}) collective-permute-start(bf16[3,128,128]{2,1,0:T(8,128)(2,1)S(1)} %get-tuple-element.21), channel_id=1, source_target_pairs={{0,16},{2,18},{16,0},{18,2},{1,17},{3,19},{17,1},{19,3},{4,20},{6,... | collective-permute-start | bytes 294920 | tf_op jit(solution)/shard_map/ppermute | solution.py:307
  65.0 5.5 %collective-permute-start.10 = (bf16[3,128,128]{2,1,0:T(8,128)(2,1)S(1)}, bf16[3,128,128]{2,1,0:T(8,128)(2,1)S(1)}, u32[]{:S(2)}, u32[]{:S(2)}) collective-permute-start(bf16[3,128,128]{2,1,0:T(8,128)(2,1)S(1)} %get-tuple-element.22), channel_id=1, source_target_pairs={{0,18},{2,16},{16,2},{18,0},{1,19},{3,17},{17,3},{19,1},{4,22},{6,... | collective-permute-start | bytes 294920 | tf_op jit(solution)/shard_map/ppermute | solution.py:307
  65.4 5.2 %collective-permute-start.11 = (bf16[3,128,128]{2,1,0:T(8,128)(2,1)}, bf16[3,128,128]{2,1,0:T(8,128)(2,1)S(1)}, u32[]{:S(2)}, u32[]{:S(2)}) collective-permute-start(bf16[3,128,128]{2,1,0:T(8,128)(2,1)} %copy-done.7), channel_id=1, source_target_pairs={{0,1},{1,0},{2,3},{3,2},{4,5},{5,4},{6,7},{7,6},{8,9},{9,8},{10,11... | collective-permute-start | bytes 294920 | tf_op jit(solution)/shard_map/ppermute | solution.py:291
  67.1 3.5 %collective-permute-start.12 = (bf16[3,128,128]{2,1,0:T(8,128)(2,1)S(1)}, bf16[3,128,128]{2,1,0:T(8,128)(2,1)S(1)}, u32[]{:S(2)}, u32[]{:S(2)}) collective-permute-start(bf16[3,128,128]{2,1,0:T(8,128)(2,1)S(1)} %collective-permute-done.8.refs_1_), channel_id=1, source_target_pairs={{0,1},{1,0},{2,3},{3,2},{4,5},{5,4},{6,7},{7,6},{8,9},{9,8},{10,11... | collective-permute-start | bytes 294920 | tf_op jit(solution)/shard_map/ppermute | solution.py:291
  69.2 1.4 %collective-permute-start.13 = (bf16[3,128,128]{2,1,0:T(8,128)(2,1)S(1)}, bf16[3,128,128]{2,1,0:T(8,128)(2,1)S(1)}, u32[]{:S(2)}, u32[]{:S(2)}) collective-permute-start(bf16[3,128,128]{2,1,0:T(8,128)(2,1)S(1)} %collective-permute-done.9.refs_2_), channel_id=1, source_target_pairs={{0,1},{1,0},{2,3},{3,2},{4,5},{5,4},{6,7},{7,6},{8,9},{9,8},{10,11... | collective-permute-start | bytes 294920 | tf_op jit(solution)/shard_map/ppermute | solution.py:291
  70.6 1.3 %collective-permute-start.14 = (bf16[3,128,128]{2,1,0:T(8,128)(2,1)S(1)}, bf16[3,128,128]{2,1,0:T(8,128)(2,1)S(1)}, u32[]{:S(2)}, u32[]{:S(2)}) collective-permute-start(bf16[3,128,128]{2,1,0:T(8,128)(2,1)S(1)} %collective-permute-done.10.refs_3_), channel_id=1, source_target_pairs={{0,1},{1,0},{2,3},{3,2},{4,5},{5,4},{6,7},{7,6},{8,9},{9,8},{10,11... | collective-permute-start | bytes 294920 | tf_op jit(solution)/shard_map/ppermute | solution.py:291
  71.9 1.1 %copy-start.6 = (f32[384,512]{1,0:T(8,128)S(1)}, f32[384,512]{1,0:T(8,128)}, u32[]{:S(2)}) copy-start(f32[384,512]{1,0:T(8,128)} %get-tuple-element.14.base_a) | copy-start | bytes 2359300
  73.0 0.9 %copy-start.8 = (bf16[3,128,128]{2,1,0:T(8,128)(2,1)S(1)}, bf16[3,128,128]{2,1,0:T(8,128)(2,1)}, u32[]{:S(2)}) copy-start(bf16[3,128,128]{2,1,0:T(8,128)(2,1)} %copy-done.7) | copy-start | bytes 294916

commit v15 on v14

--- a/solution.py
+++ b/solution.py
@@ -14,6 +14,7 @@
 VMEM = pl.BlockSpec(memory_space=pltpu.VMEM)
 HBM = pl.BlockSpec(memory_space=pltpu.HBM)
 ROOM = pltpu.CompilerParams(vmem_limit_bytes=32 * 1024 * 1024)
+TOKENS_ROOM = pltpu.CompilerParams(vmem_limit_bytes=60 * 1000 * 1000)
 FULL = pltpu.CompilerParams(vmem_limit_bytes=60 * 1024 * 1024)
 PLANE = ("groups", "pair")
 WHOLE = ("groups", "ring", "pair")
@@ -179,33 +180,16 @@
     return g * pair + y
 
 
-def collect_kernel(*refs):
-    sems, held, pieces = refs[-1], refs[-2], refs[:-2]
+def rank_kernel(groups, ring, pair, rows, owner, tok, *refs):
+    shares = groups * pair
+    held, sems = refs[-2:]
+    pieces, outs = refs[: -2 - shares], refs[-2 - shares : -2]
     copies, start = [], 0
     for j, piece in enumerate(pieces):
         copies.append(pltpu.make_async_copy(piece, held.at[pl.ds(start, piece.shape[0])], sems.at[j]))
         start += piece.shape[0]
     for copy in copies:
         copy.start()
-    for copy in copies:
-        copy.wait()
-
-
-def collect(pieces):
-    count = sum(piece.shape[0] for piece in pieces)
-    return pl.pallas_call(
-        collect_kernel,
-        in_specs=[ANY] * len(pieces),
-        out_specs=VMEM,
-        out_shape=jax.ShapeDtypeStruct((count,) + pieces[0].shape[1:], pieces[0].dtype),
-        scratch_shapes=[pltpu.SemaphoreType.DMA((len(pieces),))],
-        compiler_params=ROOM,
-        name="collect",
-    )(*pieces)
-
-
-def rank_kernel(groups, ring, pair, rows, owner, tok, held, *outs):
-    shares = groups * pair
     per, rank = held.shape[0] // (ring * pair), held.shape[1]
     blocks, _, block = outs[0].shape
     feats = tok.shape[2]
@@ -217,6 +201,8 @@
     for mate in mates:
         named = tok[mate, rows:, :LANES].astype(jnp.float32)
         ids += [jnp.sum(jnp.where((lane == b) & (row == 0), named, 0.0)).astype(jnp.int32) for b in range(blocks)]
+    for copy in copies:
+        copy.wait()
     for k, mate in enumerate(mates):
         for b in range(blocks):
             slot = owner[ids[k * blocks + b]]
@@ -234,20 +220,22 @@
             outs[k][b, rank:, :] = held[at, :, feats:]
 
 
-def rank_parts(owner, tok, held, groups, ring, pair, rows, blocks):
-    shares, rank = tok.shape[0], held.shape[1]
+def rank_parts(owner, tok, pieces, groups, ring, pair, rows, blocks):
+    shares, rank = tok.shape[0], pieces[0].shape[1]
+    held = (sum(piece.shape[0] for piece in pieces),) + pieces[0].shape[1:]
     return pl.pallas_call(
         functools.partial(rank_kernel, groups, ring, pair, rows),
-        in_specs=[SMEM, VMEM, VMEM],
+        in_specs=[SMEM, VMEM] + [ANY] * len(pieces),
         out_specs=[VMEM] * shares,
         out_shape=[jax.ShapeDtypeStruct((blocks, 2 * rank, rows // blocks), tok.dtype)] * shares,
+        scratch_shapes=[pltpu.VMEM(held, tok.dtype), pltpu.SemaphoreType.DMA((len(pieces),))],
         cost_estimate=pl.CostEstimate(flops=2 * tok.size * rank, bytes_accessed=2 * tok.size, transcendentals=0),
-        compiler_params=ROOM,
+        compiler_params=TOKENS_ROOM,
         name="rank",
-    )(owner, tok, held)
-
-
-def final_kernel(groups, pair, base_a, base_b, *refs):
+    )(owner, tok, *pieces)
+
+
+def final_kernel(groups, pair, base, *refs):
     shares = groups * pair
     mine, theirs, out_ref, up = refs[:shares], refs[shares : 2 * shares], refs[-2], refs[-1]
     blocks, tall, block = mine[0].shape
@@ -260,24 +248,24 @@
             total += part[b, :rank, :].astype(jnp.float32)
         for k in range(shares):
             tile = lax.rem(mate_at(k, -1, groups, pair), tiles)
-            up[b, :, pl.ds(pl.multiple_of(tile * LANES, LANES), LANES)] = mine[k][b, rank:, :]
+            up[b, :, pl.ds(pl.multiple_of(tile * LANES, LANES), LANES)] = mine[k][b, rank:, :].astype(up.dtype)
         delta = lax.dot_general(
             total.astype(jnp.bfloat16), up[b], (((0,), (0,)), ((), ())), preferred_element_type=jnp.float32
         )
-        out_ref[here, :] = (base_a[here, :] + base_b[here, :] + delta).astype(out_ref.dtype)
+        out_ref[here, :] = (base[here, :] + delta).astype(out_ref.dtype)
 
 
 def final(mine, theirs, base, groups, pair, dtype):
     blocks, tall, _ = mine[0].shape
     return pl.pallas_call(
         functools.partial(final_kernel, groups, pair),
-        in_specs=[VMEM] * (2 + 2 * len(mine)),
+        in_specs=[VMEM] * (1 + 2 * len(mine)),
         out_specs=VMEM,
-        out_shape=jax.ShapeDtypeStruct(base[0].shape, dtype),
-        scratch_shapes=[pltpu.VMEM((blocks, tall // 2, base[0].shape[1]), mine[0].dtype)],
+        out_shape=jax.ShapeDtypeStruct(base.shape, dtype),
+        scratch_shapes=[pltpu.VMEM((blocks, tall // 2, base.shape[1]), theirs[0].dtype)],
         compiler_params=ROOM,
         name="final",
-    )(*base, *mine, *theirs)
+    )(base, *mine, *theirs)
 
 
 def body(tokens, base_key, adapter_down, adapter_up, adapter_ids, owner_slot, lengths):
@@ -324,7 +312,7 @@
         lax.ppermute(packed[pair - w], "pair", [(a, (a - w) % pair) for a in range(pair)]) for w in range(1, pair)
     ]
     firsts = [first_hops(piece) for piece in [packed[0]] + swapped]
-    tok = to_plane(hand_on(slabs, *swapped, firsts[0][ring - 1]))
+    tok = to_plane(hand_on(slabs, *swapped))
 
     base_mine, base_out, flag = base_halves(tokens, base_key, sides, lengths)
     pieces = [
@@ -333,11 +321,12 @@
     ]
 
     flat = [piece for way in pieces for piece in way]
-    parts = rank_parts(owner_slot, tok, collect(flat), groups, ring, pair, rows, blocks)
+    parts = rank_parts(owner_slot, tok, flat, groups, ring, pair, rows, blocks)
     mine = [parts[0]] + [in_plane(parts[k], k // pair, k % pair) for k in range(1, shares)]
     theirs = [across(part) for part in mine]
     base_in = across(hand_on(base_out, parts[0]))
-    return final(mine, theirs, [base_mine, base_in], groups, pair, tokens.dtype)
+    mine[0] = mine[0].astype(jnp.float32)
+    return final(mine, theirs, base_mine + base_in, groups, pair, tokens.dtype)
 
 
 def solution(mesh):

time: 75.6 us -> 78.7 us (1.041)
  local copies, waits for them, and re-layouts: 8.41 us -> 3.8 us
  starting transfers between devices: 17.1 us -> 20.2 us
  Pallas kernels: 20.9 us -> 23.3 us
  other arithmetic: 0 us -> 2.18 us
    unnamed x22 -> x8, local copies, waits for them, and re-layouts: 8.41 us -> 3.8 us
    pallas_call x1, Pallas kernels: 1.64 us -> 5.43 us  [rank_parts(): pl.pallas_call(functools.partial(rank_kernel, groups, ring, pair, rows),...]
    ppermute x6, starting transfers between devices: 6.87 us -> 9.61 us  [along(): lax.ppermute(x, 'ring', [(a, (a + step) % ring) for a in range(ring)])]
    ppermute x1, waiting for transfers between devices: 2.01 us -> 3.58 us  [body(): lax.ppermute(packed[pair - w], 'pair', [(a, (a - w) % pair) for a in rang...]
    pallas_call x1 -> x0, Pallas kernels: 1.4 us -> none  [collect(): pl.pallas_call(collect_kernel, in_specs=[ANY] * len(pieces), out_specs=VM...]
    ppermute x5, waiting for transfers between devices: 1.29 us -> 0.01 us  [across(): lax.ppermute(x, 'tensor', [(i, (i + 1) % sides) for i in range(sides)])]
    add x0 -> x1, other arithmetic: none -> 1.28 us  [body(): return final(mine, theirs, base_mine + base_in, groups, pair, tokens.dtype)]
    convert_element_type x0 -> x1, other arithmetic: none -> 0.91 us  [body(): mine[0] = mine[0].astype(jnp.float32)]
  transfers between devices with their start and end apart: 16 -> 16, of which waited for: 10 -> 8; matrix products, arithmetic and copies ran while one was open for 0% -> 3% of each run, Pallas kernels for 22% -> 19%
where the time goes in v15:
time: 78.7 us; the launch traced here: 78.2 us
  waiting for transfers between devices  28.5 us (36%)
  Pallas kernels  23.3 us (30%)
  starting transfers between devices  20.2 us (26%)
  local copies, waits for them, and re-layouts  3.8 us (5%)
  other arithmetic  2.18 us (3%)
    ppermute x6, waiting for transfers between devices, along(): lax.ppermute(x, 'ring', [(a, (a + step) % ring) for a in range(ring)])  19.6 us
    pallas_call x1, Pallas kernels, base_halves(): pl.pallas_call(functools.partial(base_kernel, sides), grid_spec=pltpu.Pre...  11.3 us
    ppermute x6, starting transfers between devices, along(): lax.ppermute(x, 'ring', [(a, (a + step) % ring) for a in range(ring)])  9.61 us
    pallas_call x1, Pallas kernels, rank_parts(): pl.pallas_call(functools.partial(rank_kernel, groups, ring, pair, rows),...  5.43 us
    ppermute x3, waiting for transfers between devices, in_plane(): return lax.ppermute(x, PLANE, pairs)  5.35 us
    all_to_all x1, starting transfers between devices, to_plane(): return lax.all_to_all(x, PLANE, split_axis=0, concat_axis=0, tiled=True)  3.94 us
    unnamed x8, local copies, waits for them, and re-layouts  3.8 us
    pallas_call x1, Pallas kernels, spread(): pl.pallas_call(spread_kernel, in_specs=[SMEM, SMEM, ANY], out_specs=ANY,...  3.63 us
  transfers between devices with their start and end apart: 16, of which 8 were waited for; matrix products, arithmetic and copies ran while one was open for 3% of the time, Pallas kernels for 19%

profile of v15, /device:TPU:0, one launch (start us, length us, event | category | flops | bytes accessed | tf_op | source)
XLA Modules:
  0.0 78.2 jit_solution(12057997191651503495)
XLA Ops:
  0.0 1.9 %pack.1 = (bf16[2,64,1152]{2,1,0:T(8,128)(2,1)}, bf16[2,64,1152]{2,1,0:T(8,128)(2,1)}) custom-call(bf16[2,64,4096]{2,1,0:T(8,128)(2,1)} %bitcast.2, bf16[2,64,512]{2,1,0:T(8,128)(2,1)} %up.1), custom_call_target="tpu_custom_call" | custom-call | tf_op jit(solution)/shard_map/pack/pallas_call | solution.py:58
  1.9 3.0 %collective-permute-start = (bf16[2,64,1152]{2,1,0:T(8,128)(2,1)}, bf16[2,64,1152]{2,1,0:T(8,128)(2,1)S(1)}, u32[]{:S(2)}, u32[]{:S(2)}) collective-permute-start(bf16[2,64,1152]{2,1,0:T(8,128)(2,1)} %get-tuple-element.16), channel_id=1, source_target_pairs={{0,2},{2,0},{1,3},{3,1},{4,6},{6,4},{5,7},{7,5},{8,10},{10,8},{9,1... | collective-permute-start | bytes 884744 | tf_op jit(solution)/shard_map/ppermute | solution.py:312
  4.9 3.6 %spread.1.refs_0_ = bf16[4,400,1024]{2,1,0:T(8,128)(2,1)} custom-call(s32[3]{0:T(128)} %lengths.3, s32[3]{0:T(128)} %bitcast.3, bf16[384,4096]{1,0:T(8,128)(2,1)} %tok.1), custom_call_target="tpu_custom_call" | custom-call | tf_op jit(solution)/shard_map/spread/pallas_call | solution.py:108
  8.6 3.6 %collective-permute-done.refs_1_.refs_4_ = bf16[2,64,1152]{2,1,0:T(8,128)(2,1)S(1)} collective-permute-done((bf16[2,64,1152]{2,1,0:T(8,128)(2,1)}, bf16[2,64,1152]{2,1,0:T(8,128)(2,1)S(1)}, u32[]{:S(2)}, u32[]{:S(2)}) %collective-permute-start) | collective-permute-done | bytes 294944 | tf_op jit(solution)/shard_map/ppermute | solution.py:312
  12.1 0.0 copy-start.2
  12.1 0.7 copy-done.2
  12.9 3.9 %all-to-all-start = ((bf16[4,400,1024]{2,1,0:T(8,128)(2,1)}), bf16[4,400,1024]{2,1,0:T(8,128)(2,1)S(1)}, u32[]{:S(2)}, u32[]{:S(2)}) async-start(bf16[4,400,1024]{2,1,0:T(8,128)(2,1)} %hand.4), calls=%async_computation | async-start | bytes 6553600 | tf_op jit(solution)/shard_map/all_to_all | solution.py:282
  16.8 3.7 %collective-permute-start.1 = (bf16[2,64,1152]{2,1,0:T(8,128)(2,1)}, bf16[2,64,1152]{2,1,0:T(8,128)(2,1)S(1)}, u32[]{:S(2)}, u32[]{:S(2)}) collective-permute-start(bf16[2,64,1152]{2,1,0:T(8,128)(2,1)} %get-tuple-element.17.refs_0_), channel_id=1, source_target_pairs={{0,12},{4,0},{8,4},{12,8},{1,13},{5,1},{9,5},{13,9},{2,14},{6,2},{... | collective-permute-start | bytes 884744 | tf_op jit(solution)/shard_map/ppermute | solution.py:285
  20.5 0.0 collective-permute-start.2
  20.5 3.8 %collective-permute-start.4 = (bf16[2,64,1152]{2,1,0:T(8,128)(2,1)}, bf16[2,64,1152]{2,1,0:T(8,128)(2,1)}, u32[]{:S(2)}, u32[]{:S(2)}) collective-permute-start(bf16[2,64,1152]{2,1,0:T(8,128)(2,1)} %copy-done.2), channel_id=1, source_target_pairs={{0,12},{4,0},{8,4},{12,8},{1,13},{5,1},{9,5},{13,9},{2,14},{6,2},{... | collective-permute-start | bytes 884744 | tf_op jit(solution)/shard_map/ppermute | solution.py:285
  24.3 0.0 collective-permute-start.5
  24.3 11.3 %base.1 = (f32[384,512]{1,0:T(8,128)}, f32[384,512]{1,0:T(8,128)}, f32[8,128]{1,0:T(8,128)}) custom-call(s32[3]{0:T(128)} %lengths.3, bf16[384,4096]{1,0:T(8,128)(2,1)} %tok.1, bf16[4096,1024]{1,0:T(8,128)(2,1)} %key_ref.1), custom_call_target="tpu_custom_call" | custom-call | tf_op jit(solution)/shard_map/base/pallas_call | solution.py:156
  35.6 0.0 collective-permute-done.1.refs_1_
  35.6 0.0 copy-start.1
  35.6 0.0 collective-permute-done.2.refs_0_
  35.6 0.7 copy-done.1
  36.3 0.7 collective-permute-start.3
  37.1 3.9 %collective-permute-done.4.refs_0_ = bf16[2,64,1152]{2,1,0:T(8,128)(2,1)} collective-permute-done((bf16[2,64,1152]{2,1,0:T(8,128)(2,1)}, bf16[2,64,1152]{2,1,0:T(8,128)(2,1)}, u32[]{:S(2)}, u32[]{:S(2)}) %collective-permute-start.4) | collective-permute-done | bytes 294944 | tf_op jit(solution)/shard_map/ppermute | solution.py:285
  40.9 7.3 %collective-permute-done.5.refs_1_.refs_7_ = bf16[2,64,1152]{2,1,0:T(8,128)(2,1)} collective-permute-done((bf16[2,64,1152]{2,1,0:T(8,128)(2,1)}, bf16[2,64,1152]{2,1,0:T(8,128)(2,1)}, u32[]{:S(2)}, u32[]{:S(2)}) %collective-permute-start.5) | collective-permute-done | bytes 294944 | tf_op jit(solution)/shard_map/ppermute | solution.py:285
  48.3 1.4 %collective-permute-start.6 = (bf16[2,64,1152]{2,1,0:T(8,128)(2,1)}, bf16[2,64,1152]{2,1,0:T(8,128)(2,1)}, u32[]{:S(2)}, u32[]{:S(2)}) collective-permute-start(bf16[2,64,1152]{2,1,0:T(8,128)(2,1)} %hand.6.refs_5_), channel_id=1, source_target_pairs={{0,12},{4,0},{8,4},{12,8},{1,13},{5,1},{9,5},{13,9},{2,14},{6,2},{... | collective-permute-start | bytes 884744 | tf_op jit(solution)/shard_map/ppermute | solution.py:285
  49.6 4.8 %collective-permute-done.3.refs_2_ = bf16[2,64,1152]{2,1,0:T(8,128)(2,1)S(1)} collective-permute-done((bf16[2,64,1152]{2,1,0:T(8,128)(2,1)}, bf16[2,64,1152]{2,1,0:T(8,128)(2,1)S(1)}, u32[]{:S(2)}, u32[]{:S(2)}) %collective-permute-start.3) | collective-permute-done | bytes 294944 | tf_op jit(solution)/shard_map/ppermute | solution.py:285
  54.4 0.0 copy-start.3
  54.4 0.7 copy-done.3
  55.1 3.6 %collective-permute-done.6.refs_6_ = bf16[2,64,1152]{2,1,0:T(8,128)(2,1)} collective-permute-done((bf16[2,64,1152]{2,1,0:T(8,128)(2,1)}, bf16[2,64,1152]{2,1,0:T(8,128)(2,1)}, u32[]{:S(2)}, u32[]{:S(2)}) %collective-permute-start.6) | collective-permute-done | bytes 294944 | tf_op jit(solution)/shard_map/ppermute | solution.py:285
  58.7 0.0 all-to-all-done.tok
  58.7 0.0 copy-start
  58.7 1.7 %copy-done = bf16[4,400,1024]{2,1,0:T(8,128)(2,1)} copy-done((bf16[4,400,1024]{2,1,0:T(8,128)(2,1)}, bf16[4,400,1024]{2,1,0:T(8,128)(2,1)S(1)}, u32[]{:S(2)}) %copy-start) | copy-done | bytes 3276824
  60.4 5.4 %rank.1 = (bf16[3,128,128]{2,1,0:T(8,128)(2,1)}, bf16[3,128,128]{2,1,0:T(8,128)(2,1)}, bf16[3,128,128]{2,1,0:T(8,128)(2,1)}, bf16[3,128,128]{2,1,0:T(8,128)(2,1)}) custom-call(s32[16]{0:T(128)} %owner.1, bf16[4,400,1024]{2,1,0:T(8,128)(2,1)} %copy-done, bf16[2,64,1152]{2,1,0:T(8,128)(2,1)} %get-tuple-element.17.refs_0_, bf16[2,64,1152]{2,1,0:T(8,128)(2,1)} %copy-done.1, ...), custom_call_target="tpu_custom_call" | custom-call | flops 209715200 | bytes 3276800 | tf_op jit(solution)/shard_map/rank/pallas_call | solution.py:226
  65.9 0.1 collective-permute-start.7
  65.9 1.7 %collective-permute-start.8 = (bf16[3,128,128]{2,1,0:T(8,128)(2,1)}, bf16[3,128,128]{2,1,0:T(8,128)(2,1)S(1)}, u32[]{:S(2)}, u32[]{:S(2)}) collective-permute-start(bf16[3,128,128]{2,1,0:T(8,128)(2,1)} %get-tuple-element.20), channel_id=1, source_target_pairs={{0,2},{2,0},{16,18},{18,16},{1,3},{3,1},{17,19},{19,17},{4,6},{6,4... | collective-permute-start | bytes 294920 | tf_op jit(solution)/shard_map/ppermute | solution.py:295
  67.7 1.5 %collective-permute-start.9 = (bf16[3,128,128]{2,1,0:T(8,128)(2,1)}, bf16[3,128,128]{2,1,0:T(8,128)(2,1)S(1)}, u32[]{:S(2)}, u32[]{:S(2)}) collective-permute-start(bf16[3,128,128]{2,1,0:T(8,128)(2,1)} %get-tuple-element.21), channel_id=1, source_target_pairs={{0,16},{2,18},{16,0},{18,2},{1,17},{3,19},{17,1},{19,3},{4,20},{6,... | collective-permute-start | bytes 294920 | tf_op jit(solution)/shard_map/ppermute | solution.py:295
  69.1 0.4 collective-permute-start.10
  69.5 0.0 collective-permute-start.11
  69.5 1.9 %collective-permute-done.8.refs_1_ = bf16[3,128,128]{2,1,0:T(8,128)(2,1)S(1)} collective-permute-done((bf16[3,128,128]{2,1,0:T(8,128)(2,1)}, bf16[3,128,128]{2,1,0:T(8,128)(2,1)S(1)}, u32[]{:S(2)}, u32[]{:S(2)}) %collective-permute-start.8) | collective-permute-done | bytes 98336 | tf_op jit(solution)/shard_map/ppermute | solution.py:295
  71.4 0.0 collective-permute-start.12
  71.4 2.1 %collective-permute-done.9.refs_2_ = bf16[3,128,128]{2,1,0:T(8,128)(2,1)S(1)} collective-permute-done((bf16[3,128,128]{2,1,0:T(8,128)(2,1)}, bf16[3,128,128]{2,1,0:T(8,128)(2,1)S(1)}, u32[]{:S(2)}, u32[]{:S(2)}) %collective-permute-start.9) | collective-permute-done | bytes 98336 | tf_op jit(solution)/shard_map/ppermute | solution.py:295
  73.5 0.0 collective-permute-start.13
  73.5 1.3 %collective-permute-done.10.refs_3_ = bf16[3,128,128]{2,1,0:T(8,128)(2,1)S(1)} collective-permute-done((bf16[3,128,128]{2,1,0:T(8,128)(2,1)}, bf16[3,128,128]{2,1,0:T(8,128)(2,1)S(1)}, u32[]{:S(2)}, u32[]{:S(2)}) %collective-permute-start.10) | collective-permute-done | bytes 98336 | tf_op jit(solution)/shard_map/ppermute | solution.py:295
  74.9 0.0 collective-permute-start.14
  74.9 0.9 %convert_element_type.3.refs_0_ = f32[3,128,128]{2,1,0:T(8,128)S(1)} convert(bf16[3,128,128]{2,1,0:T(8,128)(2,1)} %get-tuple-element.19.refs_1_) | non-fusion elementwise | flops 49152 | bytes 294912 | tf_op jit(solution)/shard_map/convert_element_type | solution.py:328
  75.8 0.0 collective-permute-done.7
  75.8 1.3 %add.3.base = f32[384,512]{1,0:T(8,128)S(1)} add(f32[384,512]{1,0:T(8,128)} %get-tuple-element.14, f32[384,512]{1,0:T(8,128)S(1)} %collective-permute-done.7) | non-fusion elementwise | flops 196608 | bytes 2359296 | tf_op jit(solution)/shard_map/add | solution.py:329
  77.1 0.0 collective-permute-done.11.refs_4_
  77.1 0.0 collective-permute-done.12.refs_5_
  77.1 0.0 collective-permute-done.13.refs_6_
  77.1 0.0 collective-permute-done.14.refs_7_
  77.1 1.1 %final.1 = bf16[384,512]{1,0:T(8,128)(2,1)} custom-call(f32[384,512]{1,0:T(8,128)S(1)} %add.3.base, f32[3,128,128]{2,1,0:T(8,128)S(1)} %convert_element_type.3.refs_0_, bf16[3,128,128]{2,1,0:T(8,128)(2,1)S(1)} %collective-permute-done.8.refs_1_, bf16[3,128,128]{2,1,0:T(8,128)(2,1)S(1)} %collective-permute-done.9.refs_2_, ...), custom_call_target="tpu_custom_call" | custom-call | tf_op jit(solution)/shard_map/final/pallas_call | solution.py:260
  (4 shorter events, 0.0 us)
Async XLA Ops:
  1.9 10.2 %collective-permute-start = (bf16[2,64,1152]{2,1,0:T(8,128)(2,1)}, bf16[2,64,1152]{2,1,0:T(8,128)(2,1)S(1)}, u32[]{:S(2)}, u32[]{:S(2)}) collective-permute-start(bf16[2,64,1152]{2,1,0:T(8,128)(2,1)} %get-tuple-element.16), channel_id=1, source_target_pairs={{0,2},{2,0},{1,3},{3,1},{4,6},{6,4},{5,7},{7,5},{8,10},{10,8},{9,1... | collective-permute-start | bytes 884744 | tf_op jit(solution)/shard_map/ppermute | solution.py:312
  12.1 0.7 copy-start.2
  12.9 45.9 %all-to-all-start = ((bf16[4,400,1024]{2,1,0:T(8,128)(2,1)}), bf16[4,400,1024]{2,1,0:T(8,128)(2,1)S(1)}, u32[]{:S(2)}, u32[]{:S(2)}) async-start(bf16[4,400,1024]{2,1,0:T(8,128)(2,1)} %hand.4), calls=%async_computation | async-start | bytes 6553600 | tf_op jit(solution)/shard_map/all_to_all | solution.py:282
  16.8 18.8 %collective-permute-start.1 = (bf16[2,64,1152]{2,1,0:T(8,128)(2,1)}, bf16[2,64,1152]{2,1,0:T(8,128)(2,1)S(1)}, u32[]{:S(2)}, u32[]{:S(2)}) collective-permute-start(bf16[2,64,1152]{2,1,0:T(8,128)(2,1)} %get-tuple-element.17.refs_0_), channel_id=1, source_target_pairs={{0,12},{4,0},{8,4},{12,8},{1,13},{5,1},{9,5},{13,9},{2,14},{6,2},{... | collective-permute-start | bytes 884744 | tf_op jit(solution)/shard_map/ppermute | solution.py:285
  20.5 15.1 %collective-permute-start.2 = (bf16[2,64,1152]{2,1,0:T(8,128)(2,1)}, bf16[2,64,1152]{2,1,0:T(8,128)(2,1)}, u32[]{:S(2)}, u32[]{:S(2)}) collective-permute-start(bf16[2,64,1152]{2,1,0:T(8,128)(2,1)} %get-tuple-element.17.refs_0_), channel_id=1, source_target_pairs={{0,4},{4,8},{8,12},{12,0},{1,5},{5,9},{9,13},{13,1},{2,6},{6,10},{... | collective-permute-start | bytes 884744 | tf_op jit(solution)/shard_map/ppermute | solution.py:285
  20.5 20.5 %collective-permute-start.4 = (bf16[2,64,1152]{2,1,0:T(8,128)(2,1)}, bf16[2,64,1152]{2,1,0:T(8,128)(2,1)}, u32[]{:S(2)}, u32[]{:S(2)}) collective-permute-start(bf16[2,64,1152]{2,1,0:T(8,128)(2,1)} %copy-done.2), channel_id=1, source_target_pairs={{0,12},{4,0},{8,4},{12,8},{1,13},{5,1},{9,5},{13,9},{2,14},{6,2},{... | collective-permute-start | bytes 884744 | tf_op jit(solution)/shard_map/ppermute | solution.py:285
  24.3 24.0 %collective-permute-start.5 = (bf16[2,64,1152]{2,1,0:T(8,128)(2,1)}, bf16[2,64,1152]{2,1,0:T(8,128)(2,1)}, u32[]{:S(2)}, u32[]{:S(2)}) collective-permute-start(bf16[2,64,1152]{2,1,0:T(8,128)(2,1)} %copy-done.2), channel_id=1, source_target_pairs={{0,4},{4,8},{8,12},{12,0},{1,5},{5,9},{9,13},{13,1},{2,6},{6,10},{... | collective-permute-start | bytes 884744 | tf_op jit(solution)/shard_map/ppermute | solution.py:285
  35.6 0.7 copy-start.1
  36.3 18.1 %collective-permute-start.3 = (bf16[2,64,1152]{2,1,0:T(8,128)(2,1)}, bf16[2,64,1152]{2,1,0:T(8,128)(2,1)S(1)}, u32[]{:S(2)}, u32[]{:S(2)}) collective-permute-start(bf16[2,64,1152]{2,1,0:T(8,128)(2,1)} %hand.5.refs_3_), channel_id=1, source_target_pairs={{0,4},{4,8},{8,12},{12,0},{1,5},{5,9},{9,13},{13,1},{2,6},{6,10},{... | collective-permute-start | bytes 884744 | tf_op jit(solution)/shard_map/ppermute | solution.py:285
  48.3 10.5 %collective-permute-start.6 = (bf16[2,64,1152]{2,1,0:T(8,128)(2,1)}, bf16[2,64,1152]{2,1,0:T(8,128)(2,1)}, u32[]{:S(2)}, u32[]{:S(2)}) collective-permute-start(bf16[2,64,1152]{2,1,0:T(8,128)(2,1)} %hand.6.refs_5_), channel_id=1, source_target_pairs={{0,12},{4,0},{8,4},{12,8},{1,13},{5,1},{9,5},{13,9},{2,14},{6,2},{... | collective-permute-start | bytes 884744 | tf_op jit(solution)/shard_map/ppermute | solution.py:285
  54.4 0.7 copy-start.3
  58.7 1.7 %copy-start = (bf16[4,400,1024]{2,1,0:T(8,128)(2,1)}, bf16[4,400,1024]{2,1,0:T(8,128)(2,1)S(1)}, u32[]{:S(2)}) copy-start(bf16[4,400,1024]{2,1,0:T(8,128)(2,1)S(1)} %all-to-all-done.tok) | copy-start | bytes 9830404
  65.9 9.9 %collective-permute-start.7 = (f32[384,512]{1,0:T(8,128)}, f32[384,512]{1,0:T(8,128)S(1)}, u32[]{:S(2)}, u32[]{:S(2)}) collective-permute-start(f32[384,512]{1,0:T(8,128)} %hand.7), channel_id=1, source_target_pairs={{0,1},{1,0},{2,3},{3,2},{4,5},{5,4},{6,7},{7,6},{8,9},{9,8},{10,11... | collective-permute-start | bytes 2359304 | tf_op jit(solution)/shard_map/ppermute | solution.py:279
  65.9 5.4 %collective-permute-start.8 = (bf16[3,128,128]{2,1,0:T(8,128)(2,1)}, bf16[3,128,128]{2,1,0:T(8,128)(2,1)S(1)}, u32[]{:S(2)}, u32[]{:S(2)}) collective-permute-start(bf16[3,128,128]{2,1,0:T(8,128)(2,1)} %get-tuple-element.20), channel_id=1, source_target_pairs={{0,2},{2,0},{16,18},{18,16},{1,3},{3,1},{17,19},{19,17},{4,6},{6,4... | collective-permute-start | bytes 294920 | tf_op jit(solution)/shard_map/ppermute | solution.py:295
  67.7 5.9 %collective-permute-start.9 = (bf16[3,128,128]{2,1,0:T(8,128)(2,1)}, bf16[3,128,128]{2,1,0:T(8,128)(2,1)S(1)}, u32[]{:S(2)}, u32[]{:S(2)}) collective-permute-start(bf16[3,128,128]{2,1,0:T(8,128)(2,1)} %get-tuple-element.21), channel_id=1, source_target_pairs={{0,16},{2,18},{16,0},{18,2},{1,17},{3,19},{17,1},{19,3},{4,20},{6,... | collective-permute-start | bytes 294920 | tf_op jit(solution)/shard_map/ppermute | solution.py:295
  69.1 5.7 %collective-permute-start.10 = (bf16[3,128,128]{2,1,0:T(8,128)(2,1)}, bf16[3,128,128]{2,1,0:T(8,128)(2,1)S(1)}, u32[]{:S(2)}, u32[]{:S(2)}) collective-permute-start(bf16[3,128,128]{2,1,0:T(8,128)(2,1)} %get-tuple-element.22), channel_id=1, source_target_pairs={{0,18},{2,16},{16,2},{18,0},{1,19},{3,17},{17,3},{19,1},{4,22},{6,... | collective-permute-start | bytes 294920 | tf_op jit(solution)/shard_map/ppermute | solution.py:295
  69.5 7.6 %collective-permute-start.11 = (bf16[3,128,128]{2,1,0:T(8,128)(2,1)}, bf16[3,128,128]{2,1,0:T(8,128)(2,1)S(1)}, u32[]{:S(2)}, u32[]{:S(2)}) collective-permute-start(bf16[3,128,128]{2,1,0:T(8,128)(2,1)} %get-tuple-element.19.refs_1_), channel_id=1, source_target_pairs={{0,1},{1,0},{2,3},{3,2},{4,5},{5,4},{6,7},{7,6},{8,9},{9,8},{10,11... | collective-permute-start | bytes 294920 | tf_op jit(solution)/shard_map/ppermute | solution.py:279
  71.4 5.7 %collective-permute-start.12 = (bf16[3,128,128]{2,1,0:T(8,128)(2,1)S(1)}, bf16[3,128,128]{2,1,0:T(8,128)(2,1)S(1)}, u32[]{:S(2)}, u32[]{:S(2)}) collective-permute-start(bf16[3,128,128]{2,1,0:T(8,128)(2,1)S(1)} %collective-permute-done.8.refs_1_), channel_id=1, source_target_pairs={{0,1},{1,0},{2,3},{3,2},{4,5},{5,4},{6,7},{7,6},{8,9},{9,8},{10,11... | collective-permute-start | bytes 294920 | tf_op jit(solution)/shard_map/ppermute | solution.py:279
  73.5 3.6 %collective-permute-start.13 = (bf16[3,128,128]{2,1,0:T(8,128)(2,1)S(1)}, bf16[3,128,128]{2,1,0:T(8,128)(2,1)S(1)}, u32[]{:S(2)}, u32[]{:S(2)}) collective-permute-start(bf16[3,128,128]{2,1,0:T(8,128)(2,1)S(1)} %collective-permute-done.9.refs_2_), channel_id=1, source_target_pairs={{0,1},{1,0},{2,3},{3,2},{4,5},{5,4},{6,7},{7,6},{8,9},{9,8},{10,11... | collective-permute-start | bytes 294920 | tf_op jit(solution)/shard_map/ppermute | solution.py:279
  74.9 2.2 %collective-permute-start.14 = (bf16[3,128,128]{2,1,0:T(8,128)(2,1)S(1)}, bf16[3,128,128]{2,1,0:T(8,128)(2,1)S(1)}, u32[]{:S(2)}, u32[]{:S(2)}) collective-permute-start(bf16[3,128,128]{2,1,0:T(8,128)(2,1)S(1)} %collective-permute-done.10.refs_3_), channel_id=1, source_target_pairs={{0,1},{1,0},{2,3},{3,2},{4,5},{5,4},{6,7},{7,6},{8,9},{9,8},{10,11... | collective-permute-start | bytes 294920 | tf_op jit(solution)/shard_map/ppermute | solution.py:279

commit v16 on v14

--- a/solution.py
+++ b/solution.py
@@ -14,6 +14,7 @@
 VMEM = pl.BlockSpec(memory_space=pltpu.VMEM)
 HBM = pl.BlockSpec(memory_space=pltpu.HBM)
 ROOM = pltpu.CompilerParams(vmem_limit_bytes=32 * 1024 * 1024)
+TOKENS_ROOM = pltpu.CompilerParams(vmem_limit_bytes=58_200_000)
 FULL = pltpu.CompilerParams(vmem_limit_bytes=60 * 1024 * 1024)
 PLANE = ("groups", "pair")
 WHOLE = ("groups", "ring", "pair")
@@ -199,13 +200,16 @@
         out_specs=VMEM,
         out_shape=jax.ShapeDtypeStruct((count,) + pieces[0].shape[1:], pieces[0].dtype),
         scratch_shapes=[pltpu.SemaphoreType.DMA((len(pieces),))],
-        compiler_params=ROOM,
+        compiler_params=FULL,
         name="collect",
     )(*pieces)
 
 
-def rank_kernel(groups, ring, pair, rows, owner, tok, held, *outs):
+def rank_kernel(groups, ring, pair, rows, owner, tok, pieces, *refs):
     shares = groups * pair
+    outs, held, sem = refs[:-2], refs[-2], refs[-1]
+    copy = pltpu.make_async_copy(pieces, held, sem)
+    copy.start()
     per, rank = held.shape[0] // (ring * pair), held.shape[1]
     blocks, _, block = outs[0].shape
     feats = tok.shape[2]
@@ -217,6 +221,7 @@
     for mate in mates:
         named = tok[mate, rows:, :LANES].astype(jnp.float32)
         ids += [jnp.sum(jnp.where((lane == b) & (row == 0), named, 0.0)).astype(jnp.int32) for b in range(blocks)]
+    copy.wait()
     for k, mate in enumerate(mates):
         for b in range(blocks):
             slot = owner[ids[k * blocks + b]]
@@ -238,11 +243,12 @@
     shares, rank = tok.shape[0], held.shape[1]
     return pl.pallas_call(
         functools.partial(rank_kernel, groups, ring, pair, rows),
-        in_specs=[SMEM, VMEM, VMEM],
+        in_specs=[SMEM, VMEM, ANY],
         out_specs=[VMEM] * shares,
         out_shape=[jax.ShapeDtypeStruct((blocks, 2 * rank, rows // blocks), tok.dtype)] * shares,
+        scratch_shapes=[pltpu.VMEM(held.shape, held.dtype), pltpu.SemaphoreType.DMA],
         cost_estimate=pl.CostEstimate(flops=2 * tok.size * rank, bytes_accessed=2 * tok.size, transcendentals=0),
-        compiler_params=ROOM,
+        compiler_params=TOKENS_ROOM,
         name="rank",
     )(owner, tok, held)
 
@@ -336,7 +342,7 @@
     parts = rank_parts(owner_slot, tok, collect(flat), groups, ring, pair, rows, blocks)
     mine = [parts[0]] + [in_plane(parts[k], k // pair, k % pair) for k in range(1, shares)]
     theirs = [across(part) for part in mine]
-    base_in = across(hand_on(base_out, parts[0]))
+    base_in = across(hand_on(base_out, pieces[-1][ring // 2]))
     return final(mine, theirs, [base_mine, base_in], groups, pair, tokens.dtype)
 
 

time: 75.6 us -> 82.3 us (1.089)
  Pallas kernels: 20.9 us -> 26.5 us
  local copies, waits for them, and re-layouts: 8.41 us -> 4.47 us
  waiting for transfers between devices: 28.5 us -> 31.7 us
  starting transfers between devices: 17.1 us -> 19 us
    unnamed x22, local copies, waits for them, and re-layouts: 8.41 us -> 4.47 us
    pallas_call x1, Pallas kernels: 1.64 us -> 5.54 us  [rank_parts(): pl.pallas_call(functools.partial(rank_kernel, groups, ring, pair, rows),...]
    ppermute x6, waiting for transfers between devices: 20 us -> 22.9 us  [along(): lax.ppermute(x, 'ring', [(a, (a + step) % ring) for a in range(ring)])]
    pallas_call x1, Pallas kernels: 1.4 us -> 3.12 us  [collect(): pl.pallas_call(collect_kernel, in_specs=[ANY] * len(pieces), out_specs=VM...]
    all_to_all x1, starting transfers between devices: 3.71 us -> 4.81 us  [to_plane(): return lax.all_to_all(x, PLANE, split_axis=0, concat_axis=0, tiled=True)]
  transfers between devices with their start and end apart: 16 -> 16, of which waited for: 10 -> 10; matrix products, arithmetic and copies ran while one was open for 0% -> 0% of each run, Pallas kernels for 22% -> 29%
where the time goes in v16:
time: 82.3 us; the launch traced here: 81.8 us
  waiting for transfers between devices  31.7 us (39%)
  Pallas kernels  26.5 us (32%)
  starting transfers between devices  19 us (23%)
  local copies, waits for them, and re-layouts  4.47 us (5%)
    ppermute x6, waiting for transfers between devices, along(): lax.ppermute(x, 'ring', [(a, (a + step) % ring) for a in range(ring)])  22.9 us
    pallas_call x1, Pallas kernels, base_halves(): pl.pallas_call(functools.partial(base_kernel, sides), grid_spec=pltpu.Pre...  11.2 us
    ppermute x6, starting transfers between devices, along(): lax.ppermute(x, 'ring', [(a, (a + step) % ring) for a in range(ring)])  7.58 us
    pallas_call x1, Pallas kernels, rank_parts(): pl.pallas_call(functools.partial(rank_kernel, groups, ring, pair, rows),...  5.54 us
    ppermute x3, waiting for transfers between devices, in_plane(): return lax.ppermute(x, PLANE, pairs)  5.53 us
    all_to_all x1, starting transfers between devices, to_plane(): return lax.all_to_all(x, PLANE, split_axis=0, concat_axis=0, tiled=True)  4.81 us
    unnamed x22, local copies, waits for them, and re-layouts  4.47 us
    pallas_call x1, Pallas kernels, spread(): pl.pallas_call(spread_kernel, in_specs=[SMEM, SMEM, ANY], out_specs=ANY,...  3.67 us
  transfers between devices with their start and end apart: 16, of which 10 were waited for; matrix products, arithmetic and copies ran while one was open for 0% of the time, Pallas kernels for 29%

profile of v16, /device:TPU:0, one launch (start us, length us, event | category | flops | bytes accessed | tf_op | source)
XLA Modules:
  0.0 81.8 jit_solution(3075546342347063217)
XLA Ops:
  0.0 1.9 %pack.1 = (bf16[2,64,1152]{2,1,0:T(8,128)(2,1)}, bf16[2,64,1152]{2,1,0:T(8,128)(2,1)}) custom-call(bf16[2,64,4096]{2,1,0:T(8,128)(2,1)} %bitcast.2, bf16[2,64,512]{2,1,0:T(8,128)(2,1)} %up.1), custom_call_target="tpu_custom_call" | custom-call | tf_op jit(solution)/shard_map/pack/pallas_call | solution.py:58
  1.9 3.0 %collective-permute-start = (bf16[2,64,1152]{2,1,0:T(8,128)(2,1)}, bf16[2,64,1152]{2,1,0:T(8,128)(2,1)S(1)}, u32[]{:S(2)}, u32[]{:S(2)}) collective-permute-start(bf16[2,64,1152]{2,1,0:T(8,128)(2,1)} %get-tuple-element.16), channel_id=1, source_target_pairs={{0,2},{2,0},{1,3},{3,1},{4,6},{6,4},{5,7},{7,5},{8,10},{10,8},{9,1... | collective-permute-start | bytes 884744 | tf_op jit(solution)/shard_map/ppermute | solution.py:330
  4.9 1.6 %collective-permute-start.5 = (bf16[2,64,1152]{2,1,0:T(8,128)(2,1)}, bf16[2,64,1152]{2,1,0:T(8,128)(2,1)S(1)}, u32[]{:S(2)}, u32[]{:S(2)}) collective-permute-start(bf16[2,64,1152]{2,1,0:T(8,128)(2,1)} %get-tuple-element.18.refs_0_), channel_id=1, source_target_pairs={{0,4},{4,8},{8,12},{12,0},{1,5},{5,9},{9,13},{13,1},{2,6},{6,10},{... | collective-permute-start | bytes 884744 | tf_op jit(solution)/shard_map/ppermute | solution.py:303
  6.5 3.7 %spread.1.refs_0_ = bf16[4,400,1024]{2,1,0:T(8,128)(2,1)} custom-call(s32[3]{0:T(128)} %lengths.3, s32[3]{0:T(128)} %bitcast.3, bf16[384,4096]{1,0:T(8,128)(2,1)} %tok.1), custom_call_target="tpu_custom_call" | custom-call | tf_op jit(solution)/shard_map/spread/pallas_call | solution.py:108
  10.2 2.0 %collective-permute-done.refs_1_.refs_4_ = bf16[2,64,1152]{2,1,0:T(8,128)(2,1)S(1)} collective-permute-done((bf16[2,64,1152]{2,1,0:T(8,128)(2,1)}, bf16[2,64,1152]{2,1,0:T(8,128)(2,1)S(1)}, u32[]{:S(2)}, u32[]{:S(2)}) %collective-permute-start) | collective-permute-done | bytes 294944 | tf_op jit(solution)/shard_map/ppermute | solution.py:330
  12.2 3.3 %collective-permute-done.5.refs_2_.refs_0_ = bf16[2,64,1152]{2,1,0:T(8,128)(2,1)S(1)} collective-permute-done((bf16[2,64,1152]{2,1,0:T(8,128)(2,1)}, bf16[2,64,1152]{2,1,0:T(8,128)(2,1)S(1)}, u32[]{:S(2)}, u32[]{:S(2)}) %collective-permute-start.5) | collective-permute-done | bytes 294944 | tf_op jit(solution)/shard_map/ppermute | solution.py:303
  15.5 0.0 copy-done.3
  15.5 0.7 copy-done.2
  16.2 4.8 %all-to-all-start = ((bf16[4,400,1024]{2,1,0:T(8,128)(2,1)}), bf16[4,400,1024]{2,1,0:T(8,128)(2,1)}, u32[]{:S(2)}, u32[]{:S(2)}) async-start(bf16[4,400,1024]{2,1,0:T(8,128)(2,1)} %hand.6), calls=%async_computation | async-start | bytes 6553600 | tf_op jit(solution)/shard_map/all_to_all | solution.py:300
  21.0 0.0 copy-done.4
  21.0 0.0 copy-start.9
  21.0 1.8 %collective-permute-start.1 = (bf16[2,64,1152]{2,1,0:T(8,128)(2,1)S(1)}, bf16[2,64,1152]{2,1,0:T(8,128)(2,1)S(1)}, u32[]{:S(2)}, u32[]{:S(2)}) collective-permute-start(bf16[2,64,1152]{2,1,0:T(8,128)(2,1)S(1)} %copy-done.4), channel_id=1, source_target_pairs={{0,12},{4,0},{8,4},{12,8},{1,13},{5,1},{9,5},{13,9},{2,14},{6,2},{... | collective-permute-start | bytes 884744 | tf_op jit(solution)/shard_map/ppermute | solution.py:303
  22.8 0.3 collective-permute-start.2
  23.1 11.2 %base.1 = (f32[384,512]{1,0:T(8,128)}, f32[384,512]{1,0:T(8,128)}, f32[8,128]{1,0:T(8,128)}) custom-call(s32[3]{0:T(128)} %lengths.3, bf16[384,4096]{1,0:T(8,128)(2,1)} %tok.1, bf16[4096,1024]{1,0:T(8,128)(2,1)} %key_ref.1), custom_call_target="tpu_custom_call" | custom-call | tf_op jit(solution)/shard_map/base/pallas_call | solution.py:156
  34.3 0.0 collective-permute-done.1.refs_0_
  34.3 0.8 collective-permute-done.2.refs_1_.refs_7_
  35.1 0.7 copy-done.5
  35.8 2.9 %collective-permute-start.3 = (bf16[2,64,1152]{2,1,0:T(8,128)(2,1)}, bf16[2,64,1152]{2,1,0:T(8,128)(2,1)S(1)}, u32[]{:S(2)}, u32[]{:S(2)}) collective-permute-start(bf16[2,64,1152]{2,1,0:T(8,128)(2,1)} %hand.4.refs_5_), channel_id=1, source_target_pairs={{0,12},{4,0},{8,4},{12,8},{1,13},{5,1},{9,5},{13,9},{2,14},{6,2},{... | collective-permute-start | bytes 884744 | tf_op jit(solution)/shard_map/ppermute | solution.py:303
  38.7 0.0 copy-done.9
  38.7 0.0 collective-permute-start.6
  38.8 7.7 %collective-permute-done.3.refs_1_.refs_6_ = bf16[2,64,1152]{2,1,0:T(8,128)(2,1)S(1)} collective-permute-done((bf16[2,64,1152]{2,1,0:T(8,128)(2,1)}, bf16[2,64,1152]{2,1,0:T(8,128)(2,1)S(1)}, u32[]{:S(2)}, u32[]{:S(2)}) %collective-permute-start.3) | collective-permute-done | bytes 294944 | tf_op jit(solution)/shard_map/ppermute | solution.py:303
  46.5 0.7 copy-done.6
  47.2 0.0 collective-permute-start.4
  47.2 2.6 %collective-permute-done.6.refs_1_ = bf16[2,64,1152]{2,1,0:T(8,128)(2,1)S(1)} collective-permute-done((bf16[2,64,1152]{2,1,0:T(8,128)(2,1)S(1)}, bf16[2,64,1152]{2,1,0:T(8,128)(2,1)S(1)}, u32[]{:S(2)}, u32[]{:S(2)}) %collective-permute-start.6) | collective-permute-done | bytes 294944 | tf_op jit(solution)/shard_map/ppermute | solution.py:303
  49.8 0.7 copy-done.7
  50.5 1.0 %collective-permute-start.7 = (bf16[2,64,1152]{2,1,0:T(8,128)(2,1)}, bf16[2,64,1152]{2,1,0:T(8,128)(2,1)S(1)}, u32[]{:S(2)}, u32[]{:S(2)}) collective-permute-start(bf16[2,64,1152]{2,1,0:T(8,128)(2,1)} %hand.7.refs_3_), channel_id=1, source_target_pairs={{0,4},{4,8},{8,12},{12,0},{1,5},{5,9},{9,13},{13,1},{2,6},{6,10},{... | collective-permute-start | bytes 884744 | tf_op jit(solution)/shard_map/ppermute | solution.py:303
  51.5 8.5 %collective-permute-done.7.refs_2_ = bf16[2,64,1152]{2,1,0:T(8,128)(2,1)S(1)} collective-permute-done((bf16[2,64,1152]{2,1,0:T(8,128)(2,1)}, bf16[2,64,1152]{2,1,0:T(8,128)(2,1)S(1)}, u32[]{:S(2)}, u32[]{:S(2)}) %collective-permute-start.7) | collective-permute-done | bytes 294944 | tf_op jit(solution)/shard_map/ppermute | solution.py:303
  60.0 0.7 copy-done.10
  60.7 3.1 %collect.1.pieces = bf16[16,64,1152]{2,1,0:T(8,128)(2,1)} custom-call(bf16[2,64,1152]{2,1,0:T(8,128)(2,1)} %get-tuple-element.18.refs_0_, bf16[2,64,1152]{2,1,0:T(8,128)(2,1)} %copy-done.7, bf16[2,64,1152]{2,1,0:T(8,128)(2,1)} %copy-done.10, bf16[2,64,1152]{2,1,0:T(8,128)(2,1)} %hand.7.refs_3_, bf16[2,64,1152]{2,1,0:T(8,128)(2,1)} %copy-done.3, ...), custom_call_target="tpu_custom_call" | custom-call | tf_op jit(solution)/shard_map/collect/pallas_call | solution.py:197
  63.9 0.0 all-to-all-done.tok
  63.9 5.5 %rank.1 = (bf16[3,128,128]{2,1,0:T(8,128)(2,1)}, bf16[3,128,128]{2,1,0:T(8,128)(2,1)}, bf16[3,128,128]{2,1,0:T(8,128)(2,1)}, bf16[3,128,128]{2,1,0:T(8,128)(2,1)}) custom-call(s32[16]{0:T(128)} %owner.1, bf16[4,400,1024]{2,1,0:T(8,128)(2,1)} %all-to-all-done.tok, bf16[16,64,1152]{2,1,0:T(8,128)(2,1)} %collect.1.pieces), custom_call_target="tpu_custom_call" | custom-call | flops 209715200 | bytes 3276800 | tf_op jit(solution)/shard_map/rank/pallas_call | solution.py:244
  69.4 1.9 %collective-permute-start.8 = (bf16[3,128,128]{2,1,0:T(8,128)(2,1)}, bf16[3,128,128]{2,1,0:T(8,128)(2,1)S(1)}, u32[]{:S(2)}, u32[]{:S(2)}) collective-permute-start(bf16[3,128,128]{2,1,0:T(8,128)(2,1)} %get-tuple-element.20), channel_id=1, source_target_pairs={{0,2},{2,0},{16,18},{18,16},{1,3},{3,1},{17,19},{19,17},{4,6},{6,4... | collective-permute-start | bytes 294920 | tf_op jit(solution)/shard_map/ppermute | solution.py:313
  71.3 1.5 %collective-permute-start.9 = (bf16[3,128,128]{2,1,0:T(8,128)(2,1)}, bf16[3,128,128]{2,1,0:T(8,128)(2,1)S(1)}, u32[]{:S(2)}, u32[]{:S(2)}) collective-permute-start(bf16[3,128,128]{2,1,0:T(8,128)(2,1)} %get-tuple-element.21), channel_id=1, source_target_pairs={{0,16},{2,18},{16,0},{18,2},{1,17},{3,19},{17,1},{19,3},{4,20},{6,... | collective-permute-start | bytes 294920 | tf_op jit(solution)/shard_map/ppermute | solution.py:313
  72.8 0.2 collective-permute-start.10
  73.0 0.0 collective-permute-start.11
  73.0 2.4 %collective-permute-done.8.refs_1_ = bf16[3,128,128]{2,1,0:T(8,128)(2,1)S(1)} collective-permute-done((bf16[3,128,128]{2,1,0:T(8,128)(2,1)}, bf16[3,128,128]{2,1,0:T(8,128)(2,1)S(1)}, u32[]{:S(2)}, u32[]{:S(2)}) %collective-permute-start.8) | collective-permute-done | bytes 98336 | tf_op jit(solution)/shard_map/ppermute | solution.py:313
  75.3 0.0 collective-permute-start.12
  75.3 0.8 collective-permute-done.9.refs_2_
  76.1 0.0 collective-permute-start.13
  76.1 2.4 %collective-permute-done.10.refs_3_ = bf16[3,128,128]{2,1,0:T(8,128)(2,1)S(1)} collective-permute-done((bf16[3,128,128]{2,1,0:T(8,128)(2,1)}, bf16[3,128,128]{2,1,0:T(8,128)(2,1)S(1)}, u32[]{:S(2)}, u32[]{:S(2)}) %collective-permute-start.10) | collective-permute-done | bytes 98336 | tf_op jit(solution)/shard_map/ppermute | solution.py:313
  78.5 0.0 collective-permute-start.14
  78.5 0.0 collective-permute-done.4.base_b
  78.5 0.0 collective-permute-done.11.refs_4_
  78.5 0.0 collective-permute-done.12.refs_5_
  78.5 0.0 collective-permute-done.13.refs_6_
  78.5 1.3 %collective-permute-done.14.refs_7_ = bf16[3,128,128]{2,1,0:T(8,128)(2,1)S(1)} collective-permute-done((bf16[3,128,128]{2,1,0:T(8,128)(2,1)S(1)}, bf16[3,128,128]{2,1,0:T(8,128)(2,1)S(1)}, u32[]{:S(2)}, u32[]{:S(2)}) %collective-permute-start.14) | collective-permute-done | bytes 98336 | tf_op jit(solution)/shard_map/ppermute | solution.py:297
  79.8 0.9 %copy-done.1 = bf16[3,128,128]{2,1,0:T(8,128)(2,1)S(1)} copy-done((bf16[3,128,128]{2,1,0:T(8,128)(2,1)S(1)}, bf16[3,128,128]{2,1,0:T(8,128)(2,1)}, u32[]{:S(2)}) %copy-start.1) | copy-done | bytes 98328
  80.7 1.1 %final.1 = bf16[384,512]{1,0:T(8,128)(2,1)} custom-call(f32[384,512]{1,0:T(8,128)S(1)} %copy-done, f32[384,512]{1,0:T(8,128)S(1)} %collective-permute-done.4.base_b, bf16[3,128,128]{2,1,0:T(8,128)(2,1)S(1)} %copy-done.1, bf16[3,128,128]{2,1,0:T(8,128)(2,1)S(1)} %collective-permute-done.8.refs_1_, bf16[3,128,128]{2,1,0:T(8,128)(2,1)S(1)} %collective-permute-done.9.refs_2_, ...), custom_call_target="tpu_custom_call" | custom-call | tf_op jit(solution)/shard_map/final/pallas_call | solution.py:278
  (16 shorter events, 0.0 us)
Async XLA Ops:
  1.9 10.2 %collective-permute-start = (bf16[2,64,1152]{2,1,0:T(8,128)(2,1)}, bf16[2,64,1152]{2,1,0:T(8,128)(2,1)S(1)}, u32[]{:S(2)}, u32[]{:S(2)}) collective-permute-start(bf16[2,64,1152]{2,1,0:T(8,128)(2,1)} %get-tuple-element.16), channel_id=1, source_target_pairs={{0,2},{2,0},{1,3},{3,1},{4,6},{6,4},{5,7},{7,5},{8,10},{10,8},{9,1... | collective-permute-start | bytes 884744 | tf_op jit(solution)/shard_map/ppermute | solution.py:330
  4.9 10.5 %collective-permute-start.5 = (bf16[2,64,1152]{2,1,0:T(8,128)(2,1)}, bf16[2,64,1152]{2,1,0:T(8,128)(2,1)S(1)}, u32[]{:S(2)}, u32[]{:S(2)}) collective-permute-start(bf16[2,64,1152]{2,1,0:T(8,128)(2,1)} %get-tuple-element.18.refs_0_), channel_id=1, source_target_pairs={{0,4},{4,8},{8,12},{12,0},{1,5},{5,9},{9,13},{13,1},{2,6},{6,10},{... | collective-permute-start | bytes 884744 | tf_op jit(solution)/shard_map/ppermute | solution.py:303
  12.1 3.3 %copy-start.3 = (bf16[2,64,1152]{2,1,0:T(8,128)(2,1)}, bf16[2,64,1152]{2,1,0:T(8,128)(2,1)S(1)}, u32[]{:S(2)}) copy-start(bf16[2,64,1152]{2,1,0:T(8,128)(2,1)S(1)} %collective-permute-done.refs_1_.refs_4_) | copy-start | bytes 884740
  15.5 0.7 copy-start.2
  16.2 4.8 %copy-start.4 = (bf16[2,64,1152]{2,1,0:T(8,128)(2,1)S(1)}, bf16[2,64,1152]{2,1,0:T(8,128)(2,1)}, u32[]{:S(2)}) copy-start(bf16[2,64,1152]{2,1,0:T(8,128)(2,1)} %copy-done.3) | copy-start | bytes 884740
  16.2 47.7 %all-to-all-start = ((bf16[4,400,1024]{2,1,0:T(8,128)(2,1)}), bf16[4,400,1024]{2,1,0:T(8,128)(2,1)}, u32[]{:S(2)}, u32[]{:S(2)}) async-start(bf16[4,400,1024]{2,1,0:T(8,128)(2,1)} %hand.6), calls=%async_computation | async-start | bytes 6553600 | tf_op jit(solution)/shard_map/all_to_all | solution.py:300
  21.0 17.7 %copy-start.9 = (bf16[2,64,1152]{2,1,0:T(8,128)(2,1)S(1)}, bf16[2,64,1152]{2,1,0:T(8,128)(2,1)}, u32[]{:S(2)}) copy-start(bf16[2,64,1152]{2,1,0:T(8,128)(2,1)} %get-tuple-element.18.refs_0_) | copy-start | bytes 884740
  21.0 13.3 %collective-permute-start.1 = (bf16[2,64,1152]{2,1,0:T(8,128)(2,1)S(1)}, bf16[2,64,1152]{2,1,0:T(8,128)(2,1)S(1)}, u32[]{:S(2)}, u32[]{:S(2)}) collective-permute-start(bf16[2,64,1152]{2,1,0:T(8,128)(2,1)S(1)} %copy-done.4), channel_id=1, source_target_pairs={{0,12},{4,0},{8,4},{12,8},{1,13},{5,1},{9,5},{13,9},{2,14},{6,2},{... | collective-permute-start | bytes 884744 | tf_op jit(solution)/shard_map/ppermute | solution.py:303
  22.8 12.3 %collective-permute-start.2 = (bf16[2,64,1152]{2,1,0:T(8,128)(2,1)S(1)}, bf16[2,64,1152]{2,1,0:T(8,128)(2,1)S(1)}, u32[]{:S(2)}, u32[]{:S(2)}) collective-permute-start(bf16[2,64,1152]{2,1,0:T(8,128)(2,1)S(1)} %copy-done.4), channel_id=1, source_target_pairs={{0,4},{4,8},{8,12},{12,0},{1,5},{5,9},{9,13},{13,1},{2,6},{6,10},{... | collective-permute-start | bytes 884744 | tf_op jit(solution)/shard_map/ppermute | solution.py:303
  34.3 0.8 copy-start.8
  35.1 0.7 copy-start.5
  35.8 10.7 %collective-permute-start.3 = (bf16[2,64,1152]{2,1,0:T(8,128)(2,1)}, bf16[2,64,1152]{2,1,0:T(8,128)(2,1)S(1)}, u32[]{:S(2)}, u32[]{:S(2)}) collective-permute-start(bf16[2,64,1152]{2,1,0:T(8,128)(2,1)} %hand.4.refs_5_), channel_id=1, source_target_pairs={{0,12},{4,0},{8,4},{12,8},{1,13},{5,1},{9,5},{13,9},{2,14},{6,2},{... | collective-permute-start | bytes 884744 | tf_op jit(solution)/shard_map/ppermute | solution.py:303
  38.7 11.0 %collective-permute-start.6 = (bf16[2,64,1152]{2,1,0:T(8,128)(2,1)S(1)}, bf16[2,64,1152]{2,1,0:T(8,128)(2,1)S(1)}, u32[]{:S(2)}, u32[]{:S(2)}) collective-permute-start(bf16[2,64,1152]{2,1,0:T(8,128)(2,1)S(1)} %copy-done.9), channel_id=1, source_target_pairs={{0,12},{4,0},{8,4},{12,8},{1,13},{5,1},{9,5},{13,9},{2,14},{6,2},{... | collective-permute-start | bytes 884744 | tf_op jit(solution)/shard_map/ppermute | solution.py:303
  46.5 0.7 copy-start.6
  47.2 31.3 %collective-permute-start.4 = (f32[384,512]{1,0:T(8,128)}, f32[384,512]{1,0:T(8,128)S(1)}, u32[]{:S(2)}, u32[]{:S(2)}) collective-permute-start(f32[384,512]{1,0:T(8,128)} %hand.5), channel_id=1, source_target_pairs={{0,1},{1,0},{2,3},{3,2},{4,5},{5,4},{6,7},{7,6},{8,9},{9,8},{10,11... | collective-permute-start | bytes 2359304 | tf_op jit(solution)/shard_map/ppermute | solution.py:297
  49.8 0.7 copy-start.7
  50.5 9.5 %collective-permute-start.7 = (bf16[2,64,1152]{2,1,0:T(8,128)(2,1)}, bf16[2,64,1152]{2,1,0:T(8,128)(2,1)S(1)}, u32[]{:S(2)}, u32[]{:S(2)}) collective-permute-start(bf16[2,64,1152]{2,1,0:T(8,128)(2,1)} %hand.7.refs_3_), channel_id=1, source_target_pairs={{0,4},{4,8},{8,12},{12,0},{1,5},{5,9},{9,13},{13,1},{2,6},{6,10},{... | collective-permute-start | bytes 884744 | tf_op jit(solution)/shard_map/ppermute | solution.py:303
  60.0 0.7 copy-start.10
  63.8 16.0 %copy-start = (f32[384,512]{1,0:T(8,128)S(1)}, f32[384,512]{1,0:T(8,128)}, u32[]{:S(2)}) copy-start(f32[384,512]{1,0:T(8,128)} %get-tuple-element.14.base_a) | copy-start | bytes 2359300
  69.4 5.9 %collective-permute-start.8 = (bf16[3,128,128]{2,1,0:T(8,128)(2,1)}, bf16[3,128,128]{2,1,0:T(8,128)(2,1)S(1)}, u32[]{:S(2)}, u32[]{:S(2)}) collective-permute-start(bf16[3,128,128]{2,1,0:T(8,128)(2,1)} %get-tuple-element.20), channel_id=1, source_target_pairs={{0,2},{2,0},{16,18},{18,16},{1,3},{3,1},{17,19},{19,17},{4,6},{6,4... | collective-permute-start | bytes 294920 | tf_op jit(solution)/shard_map/ppermute | solution.py:313
  71.3 4.8 %collective-permute-start.9 = (bf16[3,128,128]{2,1,0:T(8,128)(2,1)}, bf16[3,128,128]{2,1,0:T(8,128)(2,1)S(1)}, u32[]{:S(2)}, u32[]{:S(2)}) collective-permute-start(bf16[3,128,128]{2,1,0:T(8,128)(2,1)} %get-tuple-element.21), channel_id=1, source_target_pairs={{0,16},{2,18},{16,0},{18,2},{1,17},{3,19},{17,1},{19,3},{4,20},{6,... | collective-permute-start | bytes 294920 | tf_op jit(solution)/shard_map/ppermute | solution.py:313
  72.8 5.7 %collective-permute-start.10 = (bf16[3,128,128]{2,1,0:T(8,128)(2,1)}, bf16[3,128,128]{2,1,0:T(8,128)(2,1)S(1)}, u32[]{:S(2)}, u32[]{:S(2)}) collective-permute-start(bf16[3,128,128]{2,1,0:T(8,128)(2,1)} %get-tuple-element.22), channel_id=1, source_target_pairs={{0,18},{2,16},{16,2},{18,0},{1,19},{3,17},{17,3},{19,1},{4,22},{6,... | collective-permute-start | bytes 294920 | tf_op jit(solution)/shard_map/ppermute | solution.py:313
  73.0 5.6 %collective-permute-start.11 = (bf16[3,128,128]{2,1,0:T(8,128)(2,1)}, bf16[3,128,128]{2,1,0:T(8,128)(2,1)S(1)}, u32[]{:S(2)}, u32[]{:S(2)}) collective-permute-start(bf16[3,128,128]{2,1,0:T(8,128)(2,1)} %get-tuple-element.19.refs_0_), channel_id=1, source_target_pairs={{0,1},{1,0},{2,3},{3,2},{4,5},{5,4},{6,7},{7,6},{8,9},{9,8},{10,11... | collective-permute-start | bytes 294920 | tf_op jit(solution)/shard_map/ppermute | solution.py:297
  75.3 3.2 %collective-permute-start.12 = (bf16[3,128,128]{2,1,0:T(8,128)(2,1)S(1)}, bf16[3,128,128]{2,1,0:T(8,128)(2,1)S(1)}, u32[]{:S(2)}, u32[]{:S(2)}) collective-permute-start(bf16[3,128,128]{2,1,0:T(8,128)(2,1)S(1)} %collective-permute-done.8.refs_1_), channel_id=1, source_target_pairs={{0,1},{1,0},{2,3},{3,2},{4,5},{5,4},{6,7},{7,6},{8,9},{9,8},{10,11... | collective-permute-start | bytes 294920 | tf_op jit(solution)/shard_map/ppermute | solution.py:297
  76.1 2.4 %collective-permute-start.13 = (bf16[3,128,128]{2,1,0:T(8,128)(2,1)S(1)}, bf16[3,128,128]{2,1,0:T(8,128)(2,1)S(1)}, u32[]{:S(2)}, u32[]{:S(2)}) collective-permute-start(bf16[3,128,128]{2,1,0:T(8,128)(2,1)S(1)} %collective-permute-done.9.refs_2_), channel_id=1, source_target_pairs={{0,1},{1,0},{2,3},{3,2},{4,5},{5,4},{6,7},{7,6},{8,9},{9,8},{10,11... | collective-permute-start | bytes 294920 | tf_op jit(solution)/shard_map/ppermute | solution.py:297
  78.5 1.3 %collective-permute-start.14 = (bf16[3,128,128]{2,1,0:T(8,128)(2,1)S(1)}, bf16[3,128,128]{2,1,0:T(8,128)(2,1)S(1)}, u32[]{:S(2)}, u32[]{:S(2)}) collective-permute-start(bf16[3,128,128]{2,1,0:T(8,128)(2,1)S(1)} %collective-permute-done.10.refs_3_), channel_id=1, source_target_pairs={{0,1},{1,0},{2,3},{3,2},{4,5},{5,4},{6,7},{7,6},{8,9},{9,8},{10,11... | collective-permute-start | bytes 294920 | tf_op jit(solution)/shard_map/ppermute | solution.py:297
  79.8 0.9 %copy-start.1 = (bf16[3,128,128]{2,1,0:T(8,128)(2,1)S(1)}, bf16[3,128,128]{2,1,0:T(8,128)(2,1)}, u32[]{:S(2)}) copy-start(bf16[3,128,128]{2,1,0:T(8,128)(2,1)} %get-tuple-element.19.refs_0_) | copy-start | bytes 294916

commit v17 on v14

--- a/solution.py
+++ b/solution.py
@@ -204,8 +204,10 @@
     )(*pieces)
 
 
-def rank_kernel(groups, ring, pair, rows, owner, tok, held, *outs):
+def rank_kernel(groups, ring, pair, rows, owner, tok, held, *refs):
     shares = groups * pair
+    outs, flag = refs[:-1], refs[-1]
+    flag[...] = jnp.zeros_like(flag)
     per, rank = held.shape[0] // (ring * pair), held.shape[1]
     blocks, _, block = outs[0].shape
     feats = tok.shape[2]
@@ -239,24 +241,47 @@
     return pl.pallas_call(
         functools.partial(rank_kernel, groups, ring, pair, rows),
         in_specs=[SMEM, VMEM, VMEM],
-        out_specs=[VMEM] * shares,
-        out_shape=[jax.ShapeDtypeStruct((blocks, 2 * rank, rows // blocks), tok.dtype)] * shares,
+        out_specs=[VMEM] * (shares + 1),
+        out_shape=[jax.ShapeDtypeStruct((blocks, 2 * rank, rows // blocks), tok.dtype)] * shares
+        + [jax.ShapeDtypeStruct((8, LANES), jnp.float32)],
         cost_estimate=pl.CostEstimate(flops=2 * tok.size * rank, bytes_accessed=2 * tok.size, transcendentals=0),
         compiler_params=ROOM,
         name="rank",
     )(owner, tok, held)
 
 
-def final_kernel(groups, pair, base_a, base_b, *refs):
+def sums_kernel(base_a, base_b, one, two, base, total):
+    rank = total.shape[1]
+    base[...] = base_a[...] + base_b[...]
+    for b in range(one.shape[0]):
+        total[b] = one[b, :rank, :].astype(jnp.float32) + two[b, :rank, :].astype(jnp.float32)
+
+
+def first_sums(base_a, base_b, one, two):
+    blocks, tall, block = one.shape
+    return pl.pallas_call(
+        sums_kernel,
+        in_specs=[VMEM] * 4,
+        out_specs=[VMEM] * 2,
+        out_shape=[
+            jax.ShapeDtypeStruct(base_a.shape, base_a.dtype),
+            jax.ShapeDtypeStruct((blocks, tall // 2, block), jnp.float32),
+        ],
+        compiler_params=ROOM,
+        name="sums",
+    )(base_a, base_b, one, two)
+
+
+def final_kernel(groups, pair, base, mine_sum, their_sum, *refs):
     shares = groups * pair
-    mine, theirs, out_ref, up = refs[:shares], refs[shares : 2 * shares], refs[-2], refs[-1]
+    mine, theirs, out_ref, up = refs[:shares], refs[shares:-2], refs[-2], refs[-1]
     blocks, tall, block = mine[0].shape
     rank = tall // 2
     tiles = out_ref.shape[1] // LANES
     for b in range(blocks):
         here = slice(b * block, (b + 1) * block)
-        total = mine[0][b, :rank, :].astype(jnp.float32)
-        for part in mine[1:] + theirs:
+        total = mine_sum[b] + their_sum[b]
+        for part in mine[2:] + theirs:
             total += part[b, :rank, :].astype(jnp.float32)
         for k in range(shares):
             tile = lax.rem(mate_at(k, -1, groups, pair), tiles)
@@ -264,20 +289,20 @@
         delta = lax.dot_general(
             total.astype(jnp.bfloat16), up[b], (((0,), (0,)), ((), ())), preferred_element_type=jnp.float32
         )
-        out_ref[here, :] = (base_a[here, :] + base_b[here, :] + delta).astype(out_ref.dtype)
-
-
-def final(mine, theirs, base, groups, pair, dtype):
+        out_ref[here, :] = (base[here, :] + delta).astype(out_ref.dtype)
+
+
+def final(mine, theirs, sums, base, groups, pair, dtype):
     blocks, tall, _ = mine[0].shape
     return pl.pallas_call(
         functools.partial(final_kernel, groups, pair),
-        in_specs=[VMEM] * (2 + 2 * len(mine)),
+        in_specs=[VMEM] * (3 + len(mine) + len(theirs)),
         out_specs=VMEM,
-        out_shape=jax.ShapeDtypeStruct(base[0].shape, dtype),
-        scratch_shapes=[pltpu.VMEM((blocks, tall // 2, base[0].shape[1]), mine[0].dtype)],
+        out_shape=jax.ShapeDtypeStruct(base.shape, dtype),
+        scratch_shapes=[pltpu.VMEM((blocks, tall // 2, base.shape[1]), mine[0].dtype)],
         compiler_params=ROOM,
         name="final",
-    )(*base, *mine, *theirs)
+    )(base, *sums, *mine, *theirs)
 
 
 def body(tokens, base_key, adapter_down, adapter_up, adapter_ids, owner_slot, lengths):
@@ -333,11 +358,12 @@
     ]
 
     flat = [piece for way in pieces for piece in way]
-    parts = rank_parts(owner_slot, tok, collect(flat), groups, ring, pair, rows, blocks)
+    *parts, flag = rank_parts(owner_slot, tok, collect(flat), groups, ring, pair, rows, blocks)
+    base_in = across(hand_on(base_out, flag))
     mine = [parts[0]] + [in_plane(parts[k], k // pair, k % pair) for k in range(1, shares)]
-    theirs = [across(part) for part in mine]
-    base_in = across(hand_on(base_out, parts[0]))
-    return final(mine, theirs, [base_mine, base_in], groups, pair, tokens.dtype)
+    base, first = first_sums(base_mine, base_in, mine[0], mine[1])
+    theirs = [across(part) for part in mine[2:]]
+    return final(mine, theirs, [first, across(first)], base, groups, pair, tokens.dtype)
 
 
 def solution(mesh):

time: 75.6 us -> 76 us (level)
  waiting for transfers between devices: 28.5 us -> 29.6 us
  local copies, waits for them, and re-layouts: 8.41 us -> 7.46 us
    ppermute x3, waiting for transfers between devices: 5.16 us -> 6.37 us  [in_plane(): return lax.ppermute(x, PLANE, pairs)]
    unnamed x22 -> x20, local copies, waits for them, and re-layouts: 8.41 us -> 7.46 us
  transfers between devices with their start and end apart: 16 -> 15, of which waited for: 10 -> 10; matrix products, arithmetic and copies ran while one was open for 0% -> 0% of each run, Pallas kernels for 22% -> 22%
where the time goes in v17:
time: 76 us; the launch traced here: 75.4 us
  waiting for transfers between devices  29.6 us (39%)
  Pallas kernels  21 us (28%)
  starting transfers between devices  17.2 us (23%)
  local copies, waits for them, and re-layouts  7.46 us (10%)
    ppermute x6, waiting for transfers between devices, along(): lax.ppermute(x, 'ring', [(a, (a + step) % ring) for a in range(ring)])  20 us
    pallas_call x1, Pallas kernels, base_halves(): pl.pallas_call(functools.partial(base_kernel, sides), grid_spec=pltpu.Pre...  11.3 us
    unnamed x20, local copies, waits for them, and re-layouts  7.46 us
    ppermute x6, starting transfers between devices, along(): lax.ppermute(x, 'ring', [(a, (a + step) % ring) for a in range(ring)])  6.86 us
    ppermute x3, waiting for transfers between devices, in_plane(): return lax.ppermute(x, PLANE, pairs)  6.37 us
    all_to_all x1, starting transfers between devices, to_plane(): return lax.all_to_all(x, PLANE, split_axis=0, concat_axis=0, tiled=True)  3.71 us
    pallas_call x1, Pallas kernels, spread(): pl.pallas_call(spread_kernel, in_specs=[SMEM, SMEM, ANY], out_specs=ANY,...  3.62 us
    ppermute x3, starting transfers between devices, in_plane(): return lax.ppermute(x, PLANE, pairs)  3.49 us
  transfers between devices with their start and end apart: 15, of which 10 were waited for; matrix products, arithmetic and copies ran while one was open for 0% of the time, Pallas kernels for 22%

profile of v17, /device:TPU:0, one launch (start us, length us, event | category | flops | bytes accessed | tf_op | source)
XLA Modules:
  0.0 75.4 jit_solution(17573249097664404707)
XLA Ops:
  0.0 1.9 %pack.1 = (bf16[2,64,1152]{2,1,0:T(8,128)(2,1)}, bf16[2,64,1152]{2,1,0:T(8,128)(2,1)}) custom-call(bf16[2,64,4096]{2,1,0:T(8,128)(2,1)} %bitcast.2, bf16[2,64,512]{2,1,0:T(8,128)(2,1)} %up.1), custom_call_target="tpu_custom_call" | custom-call | tf_op jit(solution)/shard_map/pack/pallas_call | solution.py:57
  1.9 3.0 %collective-permute-start = (bf16[2,64,1152]{2,1,0:T(8,128)(2,1)}, bf16[2,64,1152]{2,1,0:T(8,128)(2,1)S(1)}, u32[]{:S(2)}, u32[]{:S(2)}) collective-permute-start(bf16[2,64,1152]{2,1,0:T(8,128)(2,1)} %get-tuple-element.19), channel_id=1, source_target_pairs={{0,2},{2,0},{1,3},{3,1},{4,6},{6,4},{5,7},{7,5},{8,10},{10,8},{9,1... | collective-permute-start | bytes 884744 | tf_op jit(solution)/shard_map/ppermute | solution.py:349
  4.9 1.6 %collective-permute-start.1 = (bf16[2,64,1152]{2,1,0:T(8,128)(2,1)}, bf16[2,64,1152]{2,1,0:T(8,128)(2,1)S(1)}, u32[]{:S(2)}, u32[]{:S(2)}) collective-permute-start(bf16[2,64,1152]{2,1,0:T(8,128)(2,1)} %get-tuple-element.20.refs_0_), channel_id=1, source_target_pairs={{0,4},{4,8},{8,12},{12,0},{1,5},{5,9},{9,13},{13,1},{2,6},{6,10},{... | collective-permute-start | bytes 884744 | tf_op jit(solution)/shard_map/ppermute | solution.py:322
  6.5 3.6 %spread.1.refs_0_ = bf16[4,400,1024]{2,1,0:T(8,128)(2,1)} custom-call(s32[3]{0:T(128)} %lengths.3, s32[3]{0:T(128)} %bitcast.3, bf16[384,4096]{1,0:T(8,128)(2,1)} %tok.1), custom_call_target="tpu_custom_call" | custom-call | tf_op jit(solution)/shard_map/spread/pallas_call | solution.py:107
  10.1 2.0 %collective-permute-done.refs_1_.refs_4_ = bf16[2,64,1152]{2,1,0:T(8,128)(2,1)S(1)} collective-permute-done((bf16[2,64,1152]{2,1,0:T(8,128)(2,1)}, bf16[2,64,1152]{2,1,0:T(8,128)(2,1)S(1)}, u32[]{:S(2)}, u32[]{:S(2)}) %collective-permute-start) | collective-permute-done | bytes 294944 | tf_op jit(solution)/shard_map/ppermute | solution.py:349
  12.2 3.3 %collective-permute-done.1.refs_2_.refs_0_ = bf16[2,64,1152]{2,1,0:T(8,128)(2,1)S(1)} collective-permute-done((bf16[2,64,1152]{2,1,0:T(8,128)(2,1)}, bf16[2,64,1152]{2,1,0:T(8,128)(2,1)S(1)}, u32[]{:S(2)}, u32[]{:S(2)}) %collective-permute-start.1) | collective-permute-done | bytes 294944 | tf_op jit(solution)/shard_map/ppermute | solution.py:322
  15.5 0.0 copy-done.4
  15.5 0.7 copy-done.2
  16.2 3.7 %all-to-all-start = ((bf16[4,400,1024]{2,1,0:T(8,128)(2,1)}), bf16[4,400,1024]{2,1,0:T(8,128)(2,1)S(1)}, u32[]{:S(2)}, u32[]{:S(2)}) async-start(bf16[4,400,1024]{2,1,0:T(8,128)(2,1)} %hand.4), calls=%async_computation | async-start | bytes 6553600 | tf_op jit(solution)/shard_map/all_to_all | solution.py:319
  19.9 0.0 copy-start.5
  19.9 1.8 %collective-permute-start.2 = (bf16[2,64,1152]{2,1,0:T(8,128)(2,1)}, bf16[2,64,1152]{2,1,0:T(8,128)(2,1)}, u32[]{:S(2)}, u32[]{:S(2)}) collective-permute-start(bf16[2,64,1152]{2,1,0:T(8,128)(2,1)} %get-tuple-element.20.refs_0_), channel_id=1, source_target_pairs={{0,12},{4,0},{8,4},{12,8},{1,13},{5,1},{9,5},{13,9},{2,14},{6,2},{... | collective-permute-start | bytes 884744 | tf_op jit(solution)/shard_map/ppermute | solution.py:322
  21.7 0.4 collective-permute-start.4
  22.2 1.6 %collective-permute-start.5 = (bf16[2,64,1152]{2,1,0:T(8,128)(2,1)}, bf16[2,64,1152]{2,1,0:T(8,128)(2,1)}, u32[]{:S(2)}, u32[]{:S(2)}) collective-permute-start(bf16[2,64,1152]{2,1,0:T(8,128)(2,1)} %copy-done.4), channel_id=1, source_target_pairs={{0,4},{4,8},{8,12},{12,0},{1,5},{5,9},{9,13},{13,1},{2,6},{6,10},{... | collective-permute-start | bytes 884744 | tf_op jit(solution)/shard_map/ppermute | solution.py:322
  23.7 11.3 %base.1 = (f32[384,512]{1,0:T(8,128)}, f32[384,512]{1,0:T(8,128)}, f32[8,128]{1,0:T(8,128)}) custom-call(s32[3]{0:T(128)} %lengths.3, bf16[384,4096]{1,0:T(8,128)(2,1)} %tok.1, bf16[4096,1024]{1,0:T(8,128)(2,1)} %key_ref.1), custom_call_target="tpu_custom_call" | custom-call | tf_op jit(solution)/shard_map/base/pallas_call | solution.py:155
  35.0 0.0 collective-permute-done.2.refs_1_
  35.0 0.3 collective-permute-start.3
  35.4 1.1 %collective-permute-done.4.refs_0_ = bf16[2,64,1152]{2,1,0:T(8,128)(2,1)} collective-permute-done((bf16[2,64,1152]{2,1,0:T(8,128)(2,1)}, bf16[2,64,1152]{2,1,0:T(8,128)(2,1)}, u32[]{:S(2)}, u32[]{:S(2)}) %collective-permute-start.4) | collective-permute-done | bytes 294944 | tf_op jit(solution)/shard_map/ppermute | solution.py:322
  36.5 6.6 %collective-permute-done.5.refs_1_.refs_7_ = bf16[2,64,1152]{2,1,0:T(8,128)(2,1)} collective-permute-done((bf16[2,64,1152]{2,1,0:T(8,128)(2,1)}, bf16[2,64,1152]{2,1,0:T(8,128)(2,1)}, u32[]{:S(2)}, u32[]{:S(2)}) %collective-permute-start.5) | collective-permute-done | bytes 294944 | tf_op jit(solution)/shard_map/ppermute | solution.py:322
  43.1 1.1 %collective-permute-start.6 = (bf16[2,64,1152]{2,1,0:T(8,128)(2,1)}, bf16[2,64,1152]{2,1,0:T(8,128)(2,1)S(1)}, u32[]{:S(2)}, u32[]{:S(2)}) collective-permute-start(bf16[2,64,1152]{2,1,0:T(8,128)(2,1)} %hand.6.refs_5_), channel_id=1, source_target_pairs={{0,12},{4,0},{8,4},{12,8},{1,13},{5,1},{9,5},{13,9},{2,14},{6,2},{... | collective-permute-start | bytes 884744 | tf_op jit(solution)/shard_map/ppermute | solution.py:322
  44.2 4.2 %collective-permute-done.3.refs_2_ = bf16[2,64,1152]{2,1,0:T(8,128)(2,1)} collective-permute-done((bf16[2,64,1152]{2,1,0:T(8,128)(2,1)}, bf16[2,64,1152]{2,1,0:T(8,128)(2,1)}, u32[]{:S(2)}, u32[]{:S(2)}) %collective-permute-start.3) | collective-permute-done | bytes 294944 | tf_op jit(solution)/shard_map/ppermute | solution.py:322
  48.4 4.7 %collective-permute-done.6.refs_6_ = bf16[2,64,1152]{2,1,0:T(8,128)(2,1)S(1)} collective-permute-done((bf16[2,64,1152]{2,1,0:T(8,128)(2,1)}, bf16[2,64,1152]{2,1,0:T(8,128)(2,1)S(1)}, u32[]{:S(2)}, u32[]{:S(2)}) %collective-permute-start.6) | collective-permute-done | bytes 294944 | tf_op jit(solution)/shard_map/ppermute | solution.py:322
  53.2 0.0 copy-done.5
  53.2 1.0 %copy-done.3 = bf16[2,64,1152]{2,1,0:T(8,128)(2,1)S(1)} copy-done((bf16[2,64,1152]{2,1,0:T(8,128)(2,1)S(1)}, bf16[2,64,1152]{2,1,0:T(8,128)(2,1)}, u32[]{:S(2)}) %copy-start.3) | copy-done | bytes 294936
  54.1 1.0 %copy-done.7 = bf16[2,64,1152]{2,1,0:T(8,128)(2,1)S(1)} copy-done((bf16[2,64,1152]{2,1,0:T(8,128)(2,1)S(1)}, bf16[2,64,1152]{2,1,0:T(8,128)(2,1)}, u32[]{:S(2)}) %copy-start.7) | copy-done | bytes 294936
  55.1 1.4 %collect.1.held = bf16[16,64,1152]{2,1,0:T(8,128)(2,1)S(1)} custom-call(bf16[2,64,1152]{2,1,0:T(8,128)(2,1)S(1)} %copy-done.7, bf16[2,64,1152]{2,1,0:T(8,128)(2,1)} %collective-permute-done.2.refs_1_, bf16[2,64,1152]{2,1,0:T(8,128)(2,1)} %collective-permute-done.3.refs_2_, bf16[2,64,1152]{2,1,0:T(8,128)(2,1)S(1)} %copy-done.3, ...), custom_call_target="tpu_custom_call" | custom-call | tf_op jit(solution)/shard_map/collect/pallas_call | solution.py:196
  56.5 1.4 %copy-done = bf16[16,64,1152]{2,1,0:T(8,128)(2,1)} copy-done((bf16[16,64,1152]{2,1,0:T(8,128)(2,1)}, bf16[16,64,1152]{2,1,0:T(8,128)(2,1)S(1)}, u32[]{:S(2)}) %copy-start) | copy-done | bytes 2359320
  57.9 0.0 all-to-all-done.tok
  58.0 1.7 %copy-done.1 = bf16[16,64,1152]{2,1,0:T(8,128)(2,1)S(1)} copy-done((bf16[16,64,1152]{2,1,0:T(8,128)(2,1)S(1)}, bf16[16,64,1152]{2,1,0:T(8,128)(2,1)}, u32[]{:S(2)}) %copy-start.1) | copy-done | bytes 2359320
  59.6 1.6 %rank.1 = (bf16[3,128,128]{2,1,0:T(8,128)(2,1)S(1)}, bf16[3,128,128]{2,1,0:T(8,128)(2,1)S(1)}, bf16[3,128,128]{2,1,0:T(8,128)(2,1)S(1)}, bf16[3,128,128]{2,1,0:T(8,128)(2,1)S(1)}, f32[8,128]{1,0:T(8,128)S(1)}) custom-call(s32[16]{0:T(128)S(1)} %copy-done.9, bf16[4,400,1024]{2,1,0:T(8,128)(2,1)S(1)} %all-to-all-done.tok, bf16[16,64,1152]{2,1,0:T(8,128)(2,1)S(1)} %copy-done.1), custom_call_target="tpu_custom_call" | custom-call | flops 209715200 | bytes 3276800 | tf_op jit(solution)/shard_map/rank/pallas_call | solution.py:241
  61.3 0.0 copy-start.8
  61.3 0.6 copy-done.8
  61.9 0.0 collective-permute-start.7
  61.9 1.6 %collective-permute-start.10 = (bf16[3,128,128]{2,1,0:T(8,128)(2,1)S(1)}, bf16[3,128,128]{2,1,0:T(8,128)(2,1)S(1)}, u32[]{:S(2)}, u32[]{:S(2)}) collective-permute-start(bf16[3,128,128]{2,1,0:T(8,128)(2,1)S(1)} %get-tuple-element.27), channel_id=1, source_target_pairs={{0,16},{2,18},{16,0},{18,2},{1,17},{3,19},{17,1},{19,3},{4,20},{6,... | collective-permute-start | bytes 294920 | tf_op jit(solution)/shard_map/ppermute | solution.py:332
  63.5 1.5 %collective-permute-start.11 = (bf16[3,128,128]{2,1,0:T(8,128)(2,1)S(1)}, bf16[3,128,128]{2,1,0:T(8,128)(2,1)S(1)}, u32[]{:S(2)}, u32[]{:S(2)}) collective-permute-start(bf16[3,128,128]{2,1,0:T(8,128)(2,1)S(1)} %get-tuple-element.28), channel_id=1, source_target_pairs={{0,18},{2,16},{16,2},{18,0},{1,19},{3,17},{17,3},{19,1},{4,22},{6,... | collective-permute-start | bytes 294920 | tf_op jit(solution)/shard_map/ppermute | solution.py:332
  65.0 0.4 collective-permute-start.8
  65.4 1.7 %collective-permute-done.10.refs_2_ = bf16[3,128,128]{2,1,0:T(8,128)(2,1)S(1)} collective-permute-done((bf16[3,128,128]{2,1,0:T(8,128)(2,1)S(1)}, bf16[3,128,128]{2,1,0:T(8,128)(2,1)S(1)}, u32[]{:S(2)}, u32[]{:S(2)}) %collective-permute-start.10) | collective-permute-done | bytes 98336 | tf_op jit(solution)/shard_map/ppermute | solution.py:332
  67.1 0.0 collective-permute-start.12
  67.1 3.3 %collective-permute-done.11.refs_3_ = bf16[3,128,128]{2,1,0:T(8,128)(2,1)S(1)} collective-permute-done((bf16[3,128,128]{2,1,0:T(8,128)(2,1)S(1)}, bf16[3,128,128]{2,1,0:T(8,128)(2,1)S(1)}, u32[]{:S(2)}, u32[]{:S(2)}) %collective-permute-start.11) | collective-permute-done | bytes 98336 | tf_op jit(solution)/shard_map/ppermute | solution.py:332
  70.4 0.0 collective-permute-start.13
  70.4 1.4 %collective-permute-done.8.two.refs_1_ = bf16[3,128,128]{2,1,0:T(8,128)(2,1)S(1)} collective-permute-done((bf16[3,128,128]{2,1,0:T(8,128)(2,1)S(1)}, bf16[3,128,128]{2,1,0:T(8,128)(2,1)S(1)}, u32[]{:S(2)}, u32[]{:S(2)}) %collective-permute-start.8) | collective-permute-done | bytes 98336 | tf_op jit(solution)/shard_map/ppermute | solution.py:332
  71.7 0.0 collective-permute-done.7.base_b
  71.7 1.1 %copy-done.6 = f32[384,512]{1,0:T(8,128)S(1)} copy-done((f32[384,512]{1,0:T(8,128)S(1)}, f32[384,512]{1,0:T(8,128)}, u32[]{:S(2)}) %copy-start.6) | copy-done | bytes 786456
  72.9 0.1 sums.1
  73.0 0.1 collective-permute-start.9
  73.0 0.0 collective-permute-done.12.refs_4_
  73.1 0.0 collective-permute-done.13.refs_5_
  73.1 1.3 %collective-permute-done.9.their_sum = f32[3,64,128]{2,1,0:T(8,128)S(1)} collective-permute-done((f32[3,64,128]{2,1,0:T(8,128)S(1)}, f32[3,64,128]{2,1,0:T(8,128)S(1)}, u32[]{:S(2)}, u32[]{:S(2)}) %collective-permute-start.9) | collective-permute-done | bytes 98336 | tf_op jit(solution)/shard_map/ppermute | solution.py:316
  74.3 1.1 %final.1 = bf16[384,512]{1,0:T(8,128)(2,1)} custom-call(f32[384,512]{1,0:T(8,128)S(1)} %get-tuple-element.25.base, f32[3,64,128]{2,1,0:T(8,128)S(1)} %get-tuple-element.26.mine_sum, f32[3,64,128]{2,1,0:T(8,128)S(1)} %collective-permute-done.9.their_sum, bf16[3,128,128]{2,1,0:T(8,128)(2,1)S(1)} %get-tuple-element.23.one.refs_0_, ...), custom_call_target="tpu_custom_call" | custom-call | tf_op jit(solution)/shard_map/final/pallas_call | solution.py:297
  (13 shorter events, 0.0 us)
Async XLA Ops:
  1.9 10.2 %collective-permute-start = (bf16[2,64,1152]{2,1,0:T(8,128)(2,1)}, bf16[2,64,1152]{2,1,0:T(8,128)(2,1)S(1)}, u32[]{:S(2)}, u32[]{:S(2)}) collective-permute-start(bf16[2,64,1152]{2,1,0:T(8,128)(2,1)} %get-tuple-element.19), channel_id=1, source_target_pairs={{0,2},{2,0},{1,3},{3,1},{4,6},{6,4},{5,7},{7,5},{8,10},{10,8},{9,1... | collective-permute-start | bytes 884744 | tf_op jit(solution)/shard_map/ppermute | solution.py:349
  4.9 10.5 %collective-permute-start.1 = (bf16[2,64,1152]{2,1,0:T(8,128)(2,1)}, bf16[2,64,1152]{2,1,0:T(8,128)(2,1)S(1)}, u32[]{:S(2)}, u32[]{:S(2)}) collective-permute-start(bf16[2,64,1152]{2,1,0:T(8,128)(2,1)} %get-tuple-element.20.refs_0_), channel_id=1, source_target_pairs={{0,4},{4,8},{8,12},{12,0},{1,5},{5,9},{9,13},{13,1},{2,6},{6,10},{... | collective-permute-start | bytes 884744 | tf_op jit(solution)/shard_map/ppermute | solution.py:322
  12.1 3.3 %copy-start.4 = (bf16[2,64,1152]{2,1,0:T(8,128)(2,1)}, bf16[2,64,1152]{2,1,0:T(8,128)(2,1)S(1)}, u32[]{:S(2)}) copy-start(bf16[2,64,1152]{2,1,0:T(8,128)(2,1)S(1)} %collective-permute-done.refs_1_.refs_4_) | copy-start | bytes 884740
  15.5 0.7 copy-start.2
  16.2 41.8 %all-to-all-start = ((bf16[4,400,1024]{2,1,0:T(8,128)(2,1)}), bf16[4,400,1024]{2,1,0:T(8,128)(2,1)S(1)}, u32[]{:S(2)}, u32[]{:S(2)}) async-start(bf16[4,400,1024]{2,1,0:T(8,128)(2,1)} %hand.4), calls=%async_computation | async-start | bytes 6553600 | tf_op jit(solution)/shard_map/all_to_all | solution.py:319
  19.9 33.3 %copy-start.5 = (bf16[2,64,1152]{2,1,0:T(8,128)(2,1)S(1)}, bf16[2,64,1152]{2,1,0:T(8,128)(2,1)}, u32[]{:S(2)}) copy-start(bf16[2,64,1152]{2,1,0:T(8,128)(2,1)} %copy-done.4) | copy-start | bytes 884740
  19.9 15.1 %collective-permute-start.2 = (bf16[2,64,1152]{2,1,0:T(8,128)(2,1)}, bf16[2,64,1152]{2,1,0:T(8,128)(2,1)}, u32[]{:S(2)}, u32[]{:S(2)}) collective-permute-start(bf16[2,64,1152]{2,1,0:T(8,128)(2,1)} %get-tuple-element.20.refs_0_), channel_id=1, source_target_pairs={{0,12},{4,0},{8,4},{12,8},{1,13},{5,1},{9,5},{13,9},{2,14},{6,2},{... | collective-permute-start | bytes 884744 | tf_op jit(solution)/shard_map/ppermute | solution.py:322
  21.7 14.8 %collective-permute-start.4 = (bf16[2,64,1152]{2,1,0:T(8,128)(2,1)}, bf16[2,64,1152]{2,1,0:T(8,128)(2,1)}, u32[]{:S(2)}, u32[]{:S(2)}) collective-permute-start(bf16[2,64,1152]{2,1,0:T(8,128)(2,1)} %copy-done.4), channel_id=1, source_target_pairs={{0,12},{4,0},{8,4},{12,8},{1,13},{5,1},{9,5},{13,9},{2,14},{6,2},{... | collective-permute-start | bytes 884744 | tf_op jit(solution)/shard_map/ppermute | solution.py:322
  22.2 20.9 %collective-permute-start.5 = (bf16[2,64,1152]{2,1,0:T(8,128)(2,1)}, bf16[2,64,1152]{2,1,0:T(8,128)(2,1)}, u32[]{:S(2)}, u32[]{:S(2)}) collective-permute-start(bf16[2,64,1152]{2,1,0:T(8,128)(2,1)} %copy-done.4), channel_id=1, source_target_pairs={{0,4},{4,8},{8,12},{12,0},{1,5},{5,9},{9,13},{13,1},{2,6},{6,10},{... | collective-permute-start | bytes 884744 | tf_op jit(solution)/shard_map/ppermute | solution.py:322
  35.0 22.9 %copy-start.9 = (s32[16]{0:T(128)S(1)}, s32[16]{0:T(128)}, u32[]{:S(2)}) copy-start(s32[16]{0:T(128)} %owner.1) | copy-start | bytes 196
  35.0 13.4 %collective-permute-start.3 = (bf16[2,64,1152]{2,1,0:T(8,128)(2,1)}, bf16[2,64,1152]{2,1,0:T(8,128)(2,1)}, u32[]{:S(2)}, u32[]{:S(2)}) collective-permute-start(bf16[2,64,1152]{2,1,0:T(8,128)(2,1)} %hand.5.refs_3_), channel_id=1, source_target_pairs={{0,4},{4,8},{8,12},{12,0},{1,5},{5,9},{9,13},{13,1},{2,6},{6,10},{... | collective-permute-start | bytes 884744 | tf_op jit(solution)/shard_map/ppermute | solution.py:322
  43.1 10.1 %collective-permute-start.6 = (bf16[2,64,1152]{2,1,0:T(8,128)(2,1)}, bf16[2,64,1152]{2,1,0:T(8,128)(2,1)S(1)}, u32[]{:S(2)}, u32[]{:S(2)}) collective-permute-start(bf16[2,64,1152]{2,1,0:T(8,128)(2,1)} %hand.6.refs_5_), channel_id=1, source_target_pairs={{0,12},{4,0},{8,4},{12,8},{1,13},{5,1},{9,5},{13,9},{2,14},{6,2},{... | collective-permute-start | bytes 884744 | tf_op jit(solution)/shard_map/ppermute | solution.py:322
  53.2 1.0 %copy-start.3 = (bf16[2,64,1152]{2,1,0:T(8,128)(2,1)S(1)}, bf16[2,64,1152]{2,1,0:T(8,128)(2,1)}, u32[]{:S(2)}) copy-start(bf16[2,64,1152]{2,1,0:T(8,128)(2,1)} %hand.5.refs_3_) | copy-start | bytes 884740
  54.1 1.0 %copy-start.7 = (bf16[2,64,1152]{2,1,0:T(8,128)(2,1)S(1)}, bf16[2,64,1152]{2,1,0:T(8,128)(2,1)}, u32[]{:S(2)}) copy-start(bf16[2,64,1152]{2,1,0:T(8,128)(2,1)} %get-tuple-element.20.refs_0_) | copy-start | bytes 884740
  56.5 1.4 %copy-start = (bf16[16,64,1152]{2,1,0:T(8,128)(2,1)}, bf16[16,64,1152]{2,1,0:T(8,128)(2,1)S(1)}, u32[]{:S(2)}) copy-start(bf16[16,64,1152]{2,1,0:T(8,128)(2,1)S(1)} %collect.1.held) | copy-start | bytes 7077892
  58.0 1.7 %copy-start.1 = (bf16[16,64,1152]{2,1,0:T(8,128)(2,1)S(1)}, bf16[16,64,1152]{2,1,0:T(8,128)(2,1)}, u32[]{:S(2)}) copy-start(bf16[16,64,1152]{2,1,0:T(8,128)(2,1)} %copy-done) | copy-start | bytes 7077892
  61.3 0.6 copy-start.8
  61.9 9.9 %collective-permute-start.7 = (f32[384,512]{1,0:T(8,128)}, f32[384,512]{1,0:T(8,128)S(1)}, u32[]{:S(2)}, u32[]{:S(2)}) collective-permute-start(f32[384,512]{1,0:T(8,128)} %hand.7), channel_id=1, source_target_pairs={{0,1},{1,0},{2,3},{3,2},{4,5},{5,4},{6,7},{7,6},{8,9},{9,8},{10,11... | collective-permute-start | bytes 2359304 | tf_op jit(solution)/shard_map/ppermute | solution.py:316
  61.9 5.2 %collective-permute-start.10 = (bf16[3,128,128]{2,1,0:T(8,128)(2,1)S(1)}, bf16[3,128,128]{2,1,0:T(8,128)(2,1)S(1)}, u32[]{:S(2)}, u32[]{:S(2)}) collective-permute-start(bf16[3,128,128]{2,1,0:T(8,128)(2,1)S(1)} %get-tuple-element.27), channel_id=1, source_target_pairs={{0,16},{2,18},{16,0},{18,2},{1,17},{3,19},{17,1},{19,3},{4,20},{6,... | collective-permute-start | bytes 294920 | tf_op jit(solution)/shard_map/ppermute | solution.py:332
  63.5 6.9 %collective-permute-start.11 = (bf16[3,128,128]{2,1,0:T(8,128)(2,1)S(1)}, bf16[3,128,128]{2,1,0:T(8,128)(2,1)S(1)}, u32[]{:S(2)}, u32[]{:S(2)}) collective-permute-start(bf16[3,128,128]{2,1,0:T(8,128)(2,1)S(1)} %get-tuple-element.28), channel_id=1, source_target_pairs={{0,18},{2,16},{16,2},{18,0},{1,19},{3,17},{17,3},{19,1},{4,22},{6,... | collective-permute-start | bytes 294920 | tf_op jit(solution)/shard_map/ppermute | solution.py:332
  65.0 6.8 %collective-permute-start.8 = (bf16[3,128,128]{2,1,0:T(8,128)(2,1)S(1)}, bf16[3,128,128]{2,1,0:T(8,128)(2,1)S(1)}, u32[]{:S(2)}, u32[]{:S(2)}) collective-permute-start(bf16[3,128,128]{2,1,0:T(8,128)(2,1)S(1)} %get-tuple-element.24), channel_id=1, source_target_pairs={{0,2},{2,0},{16,18},{18,16},{1,3},{3,1},{17,19},{19,17},{4,6},{6,4... | collective-permute-start | bytes 294920 | tf_op jit(solution)/shard_map/ppermute | solution.py:332
  67.1 6.0 %collective-permute-start.12 = (bf16[3,128,128]{2,1,0:T(8,128)(2,1)S(1)}, bf16[3,128,128]{2,1,0:T(8,128)(2,1)S(1)}, u32[]{:S(2)}, u32[]{:S(2)}) collective-permute-start(bf16[3,128,128]{2,1,0:T(8,128)(2,1)S(1)} %collective-permute-done.10.refs_2_), channel_id=1, source_target_pairs={{0,1},{1,0},{2,3},{3,2},{4,5},{5,4},{6,7},{7,6},{8,9},{9,8},{10,11... | collective-permute-start | bytes 294920 | tf_op jit(solution)/shard_map/ppermute | solution.py:316
  70.4 2.7 %collective-permute-start.13 = (bf16[3,128,128]{2,1,0:T(8,128)(2,1)S(1)}, bf16[3,128,128]{2,1,0:T(8,128)(2,1)S(1)}, u32[]{:S(2)}, u32[]{:S(2)}) collective-permute-start(bf16[3,128,128]{2,1,0:T(8,128)(2,1)S(1)} %collective-permute-done.11.refs_3_), channel_id=1, source_target_pairs={{0,1},{1,0},{2,3},{3,2},{4,5},{5,4},{6,7},{7,6},{8,9},{9,8},{10,11... | collective-permute-start | bytes 294920 | tf_op jit(solution)/shard_map/ppermute | solution.py:316
  71.7 1.1 %copy-start.6 = (f32[384,512]{1,0:T(8,128)S(1)}, f32[384,512]{1,0:T(8,128)}, u32[]{:S(2)}) copy-start(f32[384,512]{1,0:T(8,128)} %get-tuple-element.17.base_a) | copy-start | bytes 2359300
  73.0 1.4 %collective-permute-start.9 = (f32[3,64,128]{2,1,0:T(8,128)S(1)}, f32[3,64,128]{2,1,0:T(8,128)S(1)}, u32[]{:S(2)}, u32[]{:S(2)}) collective-permute-start(f32[3,64,128]{2,1,0:T(8,128)S(1)} %get-tuple-element.26.mine_sum), channel_id=1, source_target_pairs={{0,1},{1,0},{2,3},{3,2},{4,5},{5,4},{6,7},{7,6},{8,9},{9,8},{10,11... | collective-permute-start | bytes 294920 | tf_op jit(solution)/shard_map/ppermute | solution.py:316

commit v18 on v15

--- a/solution.py
+++ b/solution.py
@@ -14,7 +14,7 @@
 VMEM = pl.BlockSpec(memory_space=pltpu.VMEM)
 HBM = pl.BlockSpec(memory_space=pltpu.HBM)
 ROOM = pltpu.CompilerParams(vmem_limit_bytes=32 * 1024 * 1024)
-TOKENS_ROOM = pltpu.CompilerParams(vmem_limit_bytes=60 * 1000 * 1000)
+TOKENS_ROOM = pltpu.CompilerParams(vmem_limit_bytes=59_550_000)
 FULL = pltpu.CompilerParams(vmem_limit_bytes=60 * 1024 * 1024)
 PLANE = ("groups", "pair")
 WHOLE = ("groups", "ring", "pair")
@@ -36,34 +36,39 @@
     )(x, *after)
 
 
-def pack_kernel(down, up, *refs):
+def pack_kernel(ways, down, up, *refs):
     outs, sems = refs[:-1], refs[-1]
     feats = outs[0].shape[2] - LANES
+    adapters = down.shape[0]
     copies = []
-    for way, out in enumerate(outs):
-        share = lax.axis_index("groups") * len(outs) + lax.rem(lax.axis_index("pair") + way, len(outs))
+    for j, out in enumerate(outs):
+        way = j if j < ways else 0
+        share = lax.axis_index("groups") * ways + lax.rem(lax.axis_index("pair") + way, ways)
         start = pl.multiple_of(share * feats, LANES)
         tile = pl.multiple_of(lax.rem(share, up.shape[2] // LANES) * LANES, LANES)
-        copies.append(pltpu.make_async_copy(down.at[:, :, pl.ds(start, feats)], out.at[:, :, :feats], sems.at[way, 0]))
-        copies.append(pltpu.make_async_copy(up.at[:, :, pl.ds(tile, LANES)], out.at[:, :, feats:], sems.at[way, 1]))
+        own = pl.ds(0, adapters) if j < ways else pl.ds(j - ways, 1)
+        copies.append(pltpu.make_async_copy(down.at[own, :, pl.ds(start, feats)], out.at[:, :, :feats], sems.at[j, 0]))
+        copies.append(pltpu.make_async_copy(up.at[own, :, pl.ds(tile, LANES)], out.at[:, :, feats:], sems.at[j, 1]))
     for copy in copies:
         copy.start()
     for copy in copies:
         copy.wait()
 
 
-def pack(down, up, shares, ways):
+def pack(down, up, shares, ways, apart):
     adapters, rank, feats = down.shape
-    shape = jax.ShapeDtypeStruct((adapters, rank, feats // shares + LANES), down.dtype)
-    return pl.pallas_call(
-        pack_kernel,
+    wide = feats // shares + LANES
+    shapes = [(adapters, rank, wide)] * ways + [(1, rank, wide)] * (adapters if apart else 0)
+    outs = pl.pallas_call(
+        functools.partial(pack_kernel, ways),
         in_specs=[HBM, HBM],
-        out_specs=[VMEM] * ways,
-        out_shape=[shape] * ways,
-        scratch_shapes=[pltpu.SemaphoreType.DMA((ways, 2))],
+        out_specs=[VMEM] * len(shapes),
+        out_shape=[jax.ShapeDtypeStruct(shape, down.dtype) for shape in shapes],
+        scratch_shapes=[pltpu.SemaphoreType.DMA((len(shapes), 2))],
         compiler_params=FULL,
         name="pack",
     )(down, up)
+    return outs[:ways], outs[ways:]
 
 
 def spread_kernel(lengths, ids, tok, out, held, in_sems, out_sems):
@@ -183,11 +188,16 @@
 def rank_kernel(groups, ring, pair, rows, owner, tok, *refs):
     shares = groups * pair
     held, sems = refs[-2:]
-    pieces, outs = refs[: -2 - shares], refs[-2 - shares : -2]
-    copies, start = [], 0
-    for j, piece in enumerate(pieces):
-        copies.append(pltpu.make_async_copy(piece, held.at[pl.ds(start, piece.shape[0])], sems.at[j]))
-        start += piece.shape[0]
+    pieces, outs, flag = refs[: -3 - shares], refs[-3 - shares : -3], refs[-3]
+    flag[...] = jnp.zeros_like(flag)
+    half = held.shape[1] // 2
+    copies = []
+    for piece in pieces:
+        for a in range(piece.shape[0]):
+            at = len(copies) // 2
+            for rank_rows in (pl.ds(0, half), pl.ds(half, half)):
+                sem = sems.at[len(copies)]
+                copies.append(pltpu.make_async_copy(piece.at[a, rank_rows, :], held.at[at, rank_rows, :], sem))
     for copy in copies:
         copy.start()
     per, rank = held.shape[0] // (ring * pair), held.shape[1]
@@ -222,20 +232,21 @@
 
 def rank_parts(owner, tok, pieces, groups, ring, pair, rows, blocks):
     shares, rank = tok.shape[0], pieces[0].shape[1]
-    held = (sum(piece.shape[0] for piece in pieces),) + pieces[0].shape[1:]
+    count = sum(piece.shape[0] for piece in pieces)
     return pl.pallas_call(
         functools.partial(rank_kernel, groups, ring, pair, rows),
         in_specs=[SMEM, VMEM] + [ANY] * len(pieces),
-        out_specs=[VMEM] * shares,
-        out_shape=[jax.ShapeDtypeStruct((blocks, 2 * rank, rows // blocks), tok.dtype)] * shares,
-        scratch_shapes=[pltpu.VMEM(held, tok.dtype), pltpu.SemaphoreType.DMA((len(pieces),))],
+        out_specs=[VMEM] * (shares + 1),
+        out_shape=[jax.ShapeDtypeStruct((blocks, 2 * rank, rows // blocks), tok.dtype)] * shares
+        + [jax.ShapeDtypeStruct((8, LANES), jnp.float32)],
+        scratch_shapes=[pltpu.VMEM((count,) + pieces[0].shape[1:], tok.dtype), pltpu.SemaphoreType.DMA((2 * count,))],
         cost_estimate=pl.CostEstimate(flops=2 * tok.size * rank, bytes_accessed=2 * tok.size, transcendentals=0),
         compiler_params=TOKENS_ROOM,
         name="rank",
     )(owner, tok, *pieces)
 
 
-def final_kernel(groups, pair, base, *refs):
+def final_kernel(groups, pair, base_a, base_b, *refs):
     shares = groups * pair
     mine, theirs, out_ref, up = refs[:shares], refs[shares : 2 * shares], refs[-2], refs[-1]
     blocks, tall, block = mine[0].shape
@@ -248,24 +259,24 @@
             total += part[b, :rank, :].astype(jnp.float32)
         for k in range(shares):
             tile = lax.rem(mate_at(k, -1, groups, pair), tiles)
-            up[b, :, pl.ds(pl.multiple_of(tile * LANES, LANES), LANES)] = mine[k][b, rank:, :].astype(up.dtype)
+            up[b, :, pl.ds(pl.multiple_of(tile * LANES, LANES), LANES)] = mine[k][b, rank:, :]
         delta = lax.dot_general(
             total.astype(jnp.bfloat16), up[b], (((0,), (0,)), ((), ())), preferred_element_type=jnp.float32
         )
-        out_ref[here, :] = (base[here, :] + delta).astype(out_ref.dtype)
+        out_ref[here, :] = (base_a[here, :] + base_b[here, :] + delta).astype(out_ref.dtype)
 
 
 def final(mine, theirs, base, groups, pair, dtype):
     blocks, tall, _ = mine[0].shape
     return pl.pallas_call(
         functools.partial(final_kernel, groups, pair),
-        in_specs=[VMEM] * (1 + 2 * len(mine)),
+        in_specs=[VMEM] * (2 + 2 * len(mine)),
         out_specs=VMEM,
-        out_shape=jax.ShapeDtypeStruct(base.shape, dtype),
-        scratch_shapes=[pltpu.VMEM((blocks, tall // 2, base.shape[1]), theirs[0].dtype)],
+        out_shape=jax.ShapeDtypeStruct(base[0].shape, dtype),
+        scratch_shapes=[pltpu.VMEM((blocks, tall // 2, base[0].shape[1]), mine[0].dtype)],
         compiler_params=ROOM,
         name="final",
-    )(base, *mine, *theirs)
+    )(*base, *mine, *theirs)
 
 
 def body(tokens, base_key, adapter_down, adapter_up, adapter_ids, owner_slot, lengths):
@@ -284,8 +295,11 @@
     def along(x, step):
         return lax.ppermute(x, "ring", [(a, (a + step) % ring) for a in range(ring)])
 
-    def first_hops(x):
-        return {0: x, ring - 1: along(x, 1), **({1: along(x, -1)} if ring > 2 else {})}
+    def first_hops(x, apart=()):
+        held = {0: x, ring - 1: along(x, 1)}
+        if ring > 2:
+            held[1] = [along(one, -1) for one in apart] if apart else along(x, -1)
+        return held
 
     def in_plane(x, kg, ky):
         pairs = []
@@ -298,7 +312,7 @@
         for k in range(2, ring // 2 + 1):
             if 2 * k < ring or way % 2 == 0:
                 if k == 2:
-                    held[ring - 1] = hand_on(held[ring - 1], held[1], *after)
+                    held[ring - 1] = hand_on(held[ring - 1], held[1][-1] if way == 0 and apart else held[1], *after)
                 held[ring - k] = along(held[ring - k + 1], 1)
             if 2 * k < ring or way % 2 == 1:
                 if k == 2:
@@ -306,13 +320,13 @@
                 held[k] = along(held[k - 1], -1)
         return [held[k] for k in range(ring)]
 
-    packed = pack(jnp.swapaxes(adapter_down, 1, 2), adapter_up, shares, pair)
+    packed, apart = pack(jnp.swapaxes(adapter_down, 1, 2), adapter_up, shares, pair, ring == 4)
     slabs = spread(tokens, lengths, adapter_ids.reshape(-1), shares)
     swapped = [
         lax.ppermute(packed[pair - w], "pair", [(a, (a - w) % pair) for a in range(pair)]) for w in range(1, pair)
     ]
-    firsts = [first_hops(piece) for piece in [packed[0]] + swapped]
-    tok = to_plane(hand_on(slabs, *swapped))
+    firsts = [first_hops(packed[0], apart)] + [first_hops(piece) for piece in swapped]
+    tok = to_plane(hand_on(slabs, *swapped, *(firsts[0][1][:1] if apart else [])))
 
     base_mine, base_out, flag = base_halves(tokens, base_key, sides, lengths)
     pieces = [
@@ -320,13 +334,14 @@
         for way, held in enumerate(firsts)
     ]
 
-    flat = [piece for way in pieces for piece in way]
-    parts = rank_parts(owner_slot, tok, flat, groups, ring, pair, rows, blocks)
+    flat = []
+    for piece in [piece for way in pieces for piece in way]:
+        flat += piece if isinstance(piece, list) else [piece]
+    *parts, ready = rank_parts(owner_slot, tok, flat, groups, ring, pair, rows, blocks)
     mine = [parts[0]] + [in_plane(parts[k], k // pair, k % pair) for k in range(1, shares)]
     theirs = [across(part) for part in mine]
-    base_in = across(hand_on(base_out, parts[0]))
-    mine[0] = mine[0].astype(jnp.float32)
-    return final(mine, theirs, base_mine + base_in, groups, pair, tokens.dtype)
+    base_in = across(hand_on(base_out, ready))
+    return final(mine, theirs, [base_mine, base_in], groups, pair, tokens.dtype)
 
 
 def solution(mesh):

time: 78.7 us -> 78.2 us (level)
  waiting for transfers between devices: 28.5 us -> 21.9 us
  starting transfers between devices: 20.2 us -> 26.6 us
  other arithmetic: 2.18 us -> 0 us
  local copies, waits for them, and re-layouts: 3.8 us -> 5.18 us
    ppermute x6 -> x7, starting transfers between devices: 9.61 us -> 15.1 us  [along(): lax.ppermute(x, 'ring', [(a, (a + step) % ring) for a in range(ring)])]
    ppermute x6 -> x7, waiting for transfers between devices: 19.6 us -> 15.3 us  [along(): lax.ppermute(x, 'ring', [(a, (a + step) % ring) for a in range(ring)])]
    ppermute x1, waiting for transfers between devices: 3.58 us -> 0.01 us  [body(): lax.ppermute(packed[pair - w], 'pair', [(a, (a - w) % pair) for a in rang...]
    unnamed x8 -> x26, local copies, waits for them, and re-layouts: 3.8 us -> 5.18 us
    ppermute x5, waiting for transfers between devices: 0.01 us -> 1.29 us  [across(): lax.ppermute(x, 'tensor', [(i, (i + 1) % sides) for i in range(sides)])]
    add x1 -> x0, other arithmetic: 1.28 us -> none  [body(): return final(mine, theirs, base_mine + base_in, groups, pair, tokens.dtype)]
    convert_element_type x1 -> x0, other arithmetic: 0.91 us -> none  [body(): mine[0] = mine[0].astype(jnp.float32)]
    all_to_all x1, starting transfers between devices: 3.94 us -> 4.81 us  [to_plane(): return lax.all_to_all(x, PLANE, split_axis=0, concat_axis=0, tiled=True)]
  transfers between devices with their start and end apart: 16 -> 17, of which waited for: 8 -> 7; matrix products, arithmetic and copies ran while one was open for 3% -> 0% of each run, Pallas kernels for 19% -> 19%
where the time goes in v18:
time: 78.2 us; the launch traced here: 77.7 us
  starting transfers between devices  26.6 us (34%)
  Pallas kernels  23.8 us (30%)
  waiting for transfers between devices  21.9 us (28%)
  local copies, waits for them, and re-layouts  5.18 us (7%)
    ppermute x7, waiting for transfers between devices, along(): lax.ppermute(x, 'ring', [(a, (a + step) % ring) for a in range(ring)])  15.3 us
    ppermute x7, starting transfers between devices, along(): lax.ppermute(x, 'ring', [(a, (a + step) % ring) for a in range(ring)])  15.1 us
    pallas_call x1, Pallas kernels, base_halves(): pl.pallas_call(functools.partial(base_kernel, sides), grid_spec=pltpu.Pre...  11.3 us
    pallas_call x1, Pallas kernels, rank_parts(): pl.pallas_call(functools.partial(rank_kernel, groups, ring, pair, rows),...  5.75 us
    ppermute x3, waiting for transfers between devices, in_plane(): return lax.ppermute(x, PLANE, pairs)  5.33 us
    unnamed x26, local copies, waits for them, and re-layouts  5.18 us
    all_to_all x1, starting transfers between devices, to_plane(): return lax.all_to_all(x, PLANE, split_axis=0, concat_axis=0, tiled=True)  4.81 us
    pallas_call x1, Pallas kernels, spread(): pl.pallas_call(spread_kernel, in_specs=[SMEM, SMEM, ANY], out_specs=ANY,...  3.63 us
  transfers between devices with their start and end apart: 17, of which 7 were waited for; matrix products, arithmetic and copies ran while one was open for 0% of the time, Pallas kernels for 19%

profile of v18, /device:TPU:0, one launch (start us, length us, event | category | flops | bytes accessed | tf_op | source)
XLA Modules:
  0.0 77.7 jit_solution(16517906023548170552)
XLA Ops:
  0.0 2.1 %pack.1 = (bf16[2,64,1152]{2,1,0:T(8,128)(2,1)}, bf16[2,64,1152]{2,1,0:T(8,128)(2,1)}, bf16[1,64,1152]{2,1,0:T(8,128)(2,1)}, bf16[1,64,1152]{2,1,0:T(8,128)(2,1)}) custom-call(bf16[2,64,4096]{2,1,0:T(8,128)(2,1)} %bitcast.2, bf16[2,64,512]{2,1,0:T(8,128)(2,1)} %up.1), custom_call_target="tpu_custom_call" | custom-call | tf_op jit(solution)/shard_map/pack/pallas_call | solution.py:62
  2.1 3.0 %collective-permute-start = (bf16[2,64,1152]{2,1,0:T(8,128)(2,1)}, bf16[2,64,1152]{2,1,0:T(8,128)(2,1)S(1)}, u32[]{:S(2)}, u32[]{:S(2)}) collective-permute-start(bf16[2,64,1152]{2,1,0:T(8,128)(2,1)} %get-tuple-element.19), channel_id=1, source_target_pairs={{0,2},{2,0},{1,3},{3,1},{4,6},{6,4},{5,7},{7,5},{8,10},{10,8},{9,1... | collective-permute-start | bytes 884744 | tf_op jit(solution)/shard_map/ppermute | solution.py:326
  5.2 3.6 %collective-permute-start.1 = (bf16[1,64,1152]{2,1,0:T(8,128)(2,1)}, bf16[1,64,1152]{2,1,0:T(8,128)(2,1)S(1)}, u32[]{:S(2)}, u32[]{:S(2)}) collective-permute-start(bf16[1,64,1152]{2,1,0:T(8,128)(2,1)} %get-tuple-element.20), channel_id=1, source_target_pairs={{0,12},{4,0},{8,4},{12,8},{1,13},{5,1},{9,5},{13,9},{2,14},{6,2},{... | collective-permute-start | bytes 442376 | tf_op jit(solution)/shard_map/ppermute | solution.py:296
  8.8 3.6 %spread.1.refs_0_ = bf16[4,400,1024]{2,1,0:T(8,128)(2,1)} custom-call(s32[3]{0:T(128)} %lengths.3, s32[3]{0:T(128)} %bitcast.3, bf16[384,4096]{1,0:T(8,128)(2,1)} %tok.1), custom_call_target="tpu_custom_call" | custom-call | tf_op jit(solution)/shard_map/spread/pallas_call | solution.py:113
  12.4 0.0 collective-permute-done.1.refs_2_.refs_1_
  12.4 0.0 collective-permute-done.refs_1_.refs_5_
  12.5 0.6 copy-done.7
  13.1 0.7 copy-done.5
  13.8 4.8 %all-to-all-start = ((bf16[4,400,1024]{2,1,0:T(8,128)(2,1)}), bf16[4,400,1024]{2,1,0:T(8,128)(2,1)}, u32[]{:S(2)}, u32[]{:S(2)}) async-start(bf16[4,400,1024]{2,1,0:T(8,128)(2,1)} %hand.4), calls=%async_computation | async-start | bytes 6553600 | tf_op jit(solution)/shard_map/all_to_all | solution.py:293
  18.7 1.1 %collective-permute-start.3 = (bf16[2,64,1152]{2,1,0:T(8,128)(2,1)S(1)}, bf16[2,64,1152]{2,1,0:T(8,128)(2,1)S(1)}, u32[]{:S(2)}, u32[]{:S(2)}) collective-permute-start(bf16[2,64,1152]{2,1,0:T(8,128)(2,1)S(1)} %copy-done.9), channel_id=1, source_target_pairs={{0,4},{4,8},{8,12},{12,0},{1,5},{5,9},{9,13},{13,1},{2,6},{6,10},{... | collective-permute-start | bytes 884744 | tf_op jit(solution)/shard_map/ppermute | solution.py:296
  19.8 0.0 copy-done.6
  19.8 2.7 %collective-permute-start.5 = (bf16[2,64,1152]{2,1,0:T(8,128)(2,1)S(1)}, bf16[2,64,1152]{2,1,0:T(8,128)(2,1)S(1)}, u32[]{:S(2)}, u32[]{:S(2)}) collective-permute-start(bf16[2,64,1152]{2,1,0:T(8,128)(2,1)S(1)} %copy-done.6), channel_id=1, source_target_pairs={{0,12},{4,0},{8,4},{12,8},{1,13},{5,1},{9,5},{13,9},{2,14},{6,2},{... | collective-permute-start | bytes 884744 | tf_op jit(solution)/shard_map/ppermute | solution.py:296
  22.5 0.0 collective-permute-start.6
  22.5 3.8 %collective-permute-start.2 = (bf16[1,64,1152]{2,1,0:T(8,128)(2,1)S(1)}, bf16[1,64,1152]{2,1,0:T(8,128)(2,1)S(1)}, u32[]{:S(2)}, u32[]{:S(2)}) collective-permute-start(bf16[1,64,1152]{2,1,0:T(8,128)(2,1)S(1)} %copy-done.12), channel_id=1, source_target_pairs={{0,12},{4,0},{8,4},{12,8},{1,13},{5,1},{9,5},{13,9},{2,14},{6,2},{... | collective-permute-start | bytes 442376 | tf_op jit(solution)/shard_map/ppermute | solution.py:296
  26.4 11.3 %base.1 = (f32[384,512]{1,0:T(8,128)}, f32[384,512]{1,0:T(8,128)}, f32[8,128]{1,0:T(8,128)}) custom-call(s32[3]{0:T(128)} %lengths.3, bf16[384,4096]{1,0:T(8,128)(2,1)} %tok.1, bf16[4096,1024]{1,0:T(8,128)(2,1)} %key_ref.1), custom_call_target="tpu_custom_call" | custom-call | tf_op jit(solution)/shard_map/base/pallas_call | solution.py:161
  37.6 5.6 %collective-permute-done.2.refs_1_.refs_2_ = bf16[1,64,1152]{2,1,0:T(8,128)(2,1)S(1)} collective-permute-done((bf16[1,64,1152]{2,1,0:T(8,128)(2,1)S(1)}, bf16[1,64,1152]{2,1,0:T(8,128)(2,1)S(1)}, u32[]{:S(2)}, u32[]{:S(2)}) %collective-permute-start.2) | collective-permute-done | bytes 147488 | tf_op jit(solution)/shard_map/ppermute | solution.py:296
  43.2 0.0 collective-permute-done.3.refs_0_
  43.2 0.7 copy-done.8
  43.9 0.1 copy-done.4
  44.0 1.6 %collective-permute-start.4 = (bf16[2,64,1152]{2,1,0:T(8,128)(2,1)}, bf16[2,64,1152]{2,1,0:T(8,128)(2,1)S(1)}, u32[]{:S(2)}, u32[]{:S(2)}) collective-permute-start(bf16[2,64,1152]{2,1,0:T(8,128)(2,1)} %hand.5.refs_4_), channel_id=1, source_target_pairs={{0,4},{4,8},{8,12},{12,0},{1,5},{5,9},{9,13},{13,1},{2,6},{6,10},{... | collective-permute-start | bytes 884744 | tf_op jit(solution)/shard_map/ppermute | solution.py:296
  45.6 0.0 collective-permute-done.5.refs_0_
  45.6 0.0 collective-permute-done.6.refs_1_.refs_8_
  45.6 0.7 copy-done.3
  46.3 0.7 copy-done.2
  47.1 2.2 %collective-permute-start.7 = (bf16[2,64,1152]{2,1,0:T(8,128)(2,1)}, bf16[2,64,1152]{2,1,0:T(8,128)(2,1)S(1)}, u32[]{:S(2)}, u32[]{:S(2)}) collective-permute-start(bf16[2,64,1152]{2,1,0:T(8,128)(2,1)} %hand.6.refs_6_), channel_id=1, source_target_pairs={{0,12},{4,0},{8,4},{12,8},{1,13},{5,1},{9,5},{13,9},{2,14},{6,2},{... | collective-permute-start | bytes 884744 | tf_op jit(solution)/shard_map/ppermute | solution.py:296
  49.3 6.2 %collective-permute-done.4.refs_3_ = bf16[2,64,1152]{2,1,0:T(8,128)(2,1)S(1)} collective-permute-done((bf16[2,64,1152]{2,1,0:T(8,128)(2,1)}, bf16[2,64,1152]{2,1,0:T(8,128)(2,1)S(1)}, u32[]{:S(2)}, u32[]{:S(2)}) %collective-permute-start.4) | collective-permute-done | bytes 294944 | tf_op jit(solution)/shard_map/ppermute | solution.py:296
  55.5 3.5 %collective-permute-done.7.refs_7_ = bf16[2,64,1152]{2,1,0:T(8,128)(2,1)S(1)} collective-permute-done((bf16[2,64,1152]{2,1,0:T(8,128)(2,1)}, bf16[2,64,1152]{2,1,0:T(8,128)(2,1)S(1)}, u32[]{:S(2)}, u32[]{:S(2)}) %collective-permute-start.7) | collective-permute-done | bytes 294944 | tf_op jit(solution)/shard_map/ppermute | solution.py:296
  59.0 0.0 all-to-all-done.tok
  59.0 0.7 copy-done.11
  59.7 5.8 %rank.1 = (bf16[3,128,128]{2,1,0:T(8,128)(2,1)}, bf16[3,128,128]{2,1,0:T(8,128)(2,1)}, bf16[3,128,128]{2,1,0:T(8,128)(2,1)}, bf16[3,128,128]{2,1,0:T(8,128)(2,1)}, f32[8,128]{1,0:T(8,128)}) custom-call(s32[16]{0:T(128)} %owner.1, bf16[4,400,1024]{2,1,0:T(8,128)(2,1)} %all-to-all-done.tok, bf16[2,64,1152]{2,1,0:T(8,128)(2,1)} %get-tuple-element.21.refs_0_, ...), custom_call_target="tpu_custom_call" | custom-call | flops 209715200 | bytes 3276800 | tf_op jit(solution)/shard_map/rank/pallas_call | solution.py:236
  65.4 0.1 collective-permute-start.8
  65.5 1.7 %collective-permute-start.9 = (bf16[3,128,128]{2,1,0:T(8,128)(2,1)}, bf16[3,128,128]{2,1,0:T(8,128)(2,1)S(1)}, u32[]{:S(2)}, u32[]{:S(2)}) collective-permute-start(bf16[3,128,128]{2,1,0:T(8,128)(2,1)} %get-tuple-element.26), channel_id=1, source_target_pairs={{0,2},{2,0},{16,18},{18,16},{1,3},{3,1},{17,19},{19,17},{4,6},{6,4... | collective-permute-start | bytes 294920 | tf_op jit(solution)/shard_map/ppermute | solution.py:309
  67.2 1.5 %collective-permute-start.10 = (bf16[3,128,128]{2,1,0:T(8,128)(2,1)}, bf16[3,128,128]{2,1,0:T(8,128)(2,1)S(1)}, u32[]{:S(2)}, u32[]{:S(2)}) collective-permute-start(bf16[3,128,128]{2,1,0:T(8,128)(2,1)} %get-tuple-element.27), channel_id=1, source_target_pairs={{0,16},{2,18},{16,0},{18,2},{1,17},{3,19},{17,1},{19,3},{4,20},{6,... | collective-permute-start | bytes 294920 | tf_op jit(solution)/shard_map/ppermute | solution.py:309
  68.7 0.4 collective-permute-start.11
  69.1 0.0 collective-permute-start.12
  69.1 1.9 %collective-permute-done.9.refs_1_ = bf16[3,128,128]{2,1,0:T(8,128)(2,1)S(1)} collective-permute-done((bf16[3,128,128]{2,1,0:T(8,128)(2,1)}, bf16[3,128,128]{2,1,0:T(8,128)(2,1)S(1)}, u32[]{:S(2)}, u32[]{:S(2)}) %collective-permute-start.9) | collective-permute-done | bytes 98336 | tf_op jit(solution)/shard_map/ppermute | solution.py:309
  70.9 0.0 collective-permute-start.13
  71.0 2.1 %collective-permute-done.10.refs_2_ = bf16[3,128,128]{2,1,0:T(8,128)(2,1)S(1)} collective-permute-done((bf16[3,128,128]{2,1,0:T(8,128)(2,1)}, bf16[3,128,128]{2,1,0:T(8,128)(2,1)S(1)}, u32[]{:S(2)}, u32[]{:S(2)}) %collective-permute-start.10) | collective-permute-done | bytes 98336 | tf_op jit(solution)/shard_map/ppermute | solution.py:309
  73.1 0.0 collective-permute-start.14
  73.1 1.3 %collective-permute-done.11.refs_3_ = bf16[3,128,128]{2,1,0:T(8,128)(2,1)S(1)} collective-permute-done((bf16[3,128,128]{2,1,0:T(8,128)(2,1)}, bf16[3,128,128]{2,1,0:T(8,128)(2,1)S(1)}, u32[]{:S(2)}, u32[]{:S(2)}) %collective-permute-start.11) | collective-permute-done | bytes 98336 | tf_op jit(solution)/shard_map/ppermute | solution.py:309
  74.4 0.0 collective-permute-start.15
  74.4 0.0 collective-permute-done.12.refs_4_
  74.4 0.0 collective-permute-done.13.refs_5_
  74.4 0.0 collective-permute-done.14.refs_6_
  74.4 1.3 %collective-permute-done.15.refs_7_ = bf16[3,128,128]{2,1,0:T(8,128)(2,1)S(1)} collective-permute-done((bf16[3,128,128]{2,1,0:T(8,128)(2,1)S(1)}, bf16[3,128,128]{2,1,0:T(8,128)(2,1)S(1)}, u32[]{:S(2)}, u32[]{:S(2)}) %collective-permute-start.15) | collective-permute-done | bytes 98336 | tf_op jit(solution)/shard_map/ppermute | solution.py:290
  75.7 0.0 collective-permute-done.8.base_b
  75.7 0.9 %copy-done.1 = bf16[3,128,128]{2,1,0:T(8,128)(2,1)S(1)} copy-done((bf16[3,128,128]{2,1,0:T(8,128)(2,1)S(1)}, bf16[3,128,128]{2,1,0:T(8,128)(2,1)}, u32[]{:S(2)}) %copy-start.1) | copy-done | bytes 98328
  76.6 1.0 %final.1 = bf16[384,512]{1,0:T(8,128)(2,1)} custom-call(f32[384,512]{1,0:T(8,128)S(1)} %copy-done, f32[384,512]{1,0:T(8,128)S(1)} %collective-permute-done.8.base_b, bf16[3,128,128]{2,1,0:T(8,128)(2,1)S(1)} %copy-done.1, bf16[3,128,128]{2,1,0:T(8,128)(2,1)S(1)} %collective-permute-done.9.refs_1_, bf16[3,128,128]{2,1,0:T(8,128)(2,1)S(1)} %collective-permute-done.10.refs_2_, ...), custom_call_target="tpu_custom_call" | custom-call | tf_op jit(solution)/shard_map/final/pallas_call | solution.py:271
  (21 shorter events, 0.0 us)
Async XLA Ops:
  2.1 10.3 %collective-permute-start = (bf16[2,64,1152]{2,1,0:T(8,128)(2,1)}, bf16[2,64,1152]{2,1,0:T(8,128)(2,1)S(1)}, u32[]{:S(2)}, u32[]{:S(2)}) collective-permute-start(bf16[2,64,1152]{2,1,0:T(8,128)(2,1)} %get-tuple-element.19), channel_id=1, source_target_pairs={{0,2},{2,0},{1,3},{3,1},{4,6},{6,4},{5,7},{7,5},{8,10},{10,8},{9,1... | collective-permute-start | bytes 884744 | tf_op jit(solution)/shard_map/ppermute | solution.py:326
  5.2 7.2 %collective-permute-start.1 = (bf16[1,64,1152]{2,1,0:T(8,128)(2,1)}, bf16[1,64,1152]{2,1,0:T(8,128)(2,1)S(1)}, u32[]{:S(2)}, u32[]{:S(2)}) collective-permute-start(bf16[1,64,1152]{2,1,0:T(8,128)(2,1)} %get-tuple-element.20), channel_id=1, source_target_pairs={{0,12},{4,0},{8,4},{12,8},{1,13},{5,1},{9,5},{13,9},{2,14},{6,2},{... | collective-permute-start | bytes 442376 | tf_op jit(solution)/shard_map/ppermute | solution.py:296
  12.4 0.7 copy-start.7
  13.1 0.7 copy-start.5
  13.8 4.8 %copy-start.9 = (bf16[2,64,1152]{2,1,0:T(8,128)(2,1)S(1)}, bf16[2,64,1152]{2,1,0:T(8,128)(2,1)}, u32[]{:S(2)}) copy-start(bf16[2,64,1152]{2,1,0:T(8,128)(2,1)} %get-tuple-element.21.refs_0_) | copy-start | bytes 884740
  13.8 6.0 %copy-start.6 = (bf16[2,64,1152]{2,1,0:T(8,128)(2,1)S(1)}, bf16[2,64,1152]{2,1,0:T(8,128)(2,1)}, u32[]{:S(2)}) copy-start(bf16[2,64,1152]{2,1,0:T(8,128)(2,1)} %copy-done.5) | copy-start | bytes 884740
  13.8 8.7 %copy-start.12 = (bf16[1,64,1152]{2,1,0:T(8,128)(2,1)S(1)}, bf16[1,64,1152]{2,1,0:T(8,128)(2,1)}, u32[]{:S(2)}) copy-start(bf16[1,64,1152]{2,1,0:T(8,128)(2,1)} %get-tuple-element.22) | copy-start | bytes 442372
  13.8 45.1 %all-to-all-start = ((bf16[4,400,1024]{2,1,0:T(8,128)(2,1)}), bf16[4,400,1024]{2,1,0:T(8,128)(2,1)}, u32[]{:S(2)}, u32[]{:S(2)}) async-start(bf16[4,400,1024]{2,1,0:T(8,128)(2,1)} %hand.4), calls=%async_computation | async-start | bytes 6553600 | tf_op jit(solution)/shard_map/all_to_all | solution.py:293
  18.7 24.6 %collective-permute-start.3 = (bf16[2,64,1152]{2,1,0:T(8,128)(2,1)S(1)}, bf16[2,64,1152]{2,1,0:T(8,128)(2,1)S(1)}, u32[]{:S(2)}, u32[]{:S(2)}) collective-permute-start(bf16[2,64,1152]{2,1,0:T(8,128)(2,1)S(1)} %copy-done.9), channel_id=1, source_target_pairs={{0,4},{4,8},{8,12},{12,0},{1,5},{5,9},{9,13},{13,1},{2,6},{6,10},{... | collective-permute-start | bytes 884744 | tf_op jit(solution)/shard_map/ppermute | solution.py:296
  19.8 25.8 %collective-permute-start.5 = (bf16[2,64,1152]{2,1,0:T(8,128)(2,1)S(1)}, bf16[2,64,1152]{2,1,0:T(8,128)(2,1)S(1)}, u32[]{:S(2)}, u32[]{:S(2)}) collective-permute-start(bf16[2,64,1152]{2,1,0:T(8,128)(2,1)S(1)} %copy-done.6), channel_id=1, source_target_pairs={{0,12},{4,0},{8,4},{12,8},{1,13},{5,1},{9,5},{13,9},{2,14},{6,2},{... | collective-permute-start | bytes 884744 | tf_op jit(solution)/shard_map/ppermute | solution.py:296
  22.5 23.1 %collective-permute-start.6 = (bf16[2,64,1152]{2,1,0:T(8,128)(2,1)S(1)}, bf16[2,64,1152]{2,1,0:T(8,128)(2,1)S(1)}, u32[]{:S(2)}, u32[]{:S(2)}) collective-permute-start(bf16[2,64,1152]{2,1,0:T(8,128)(2,1)S(1)} %copy-done.6), channel_id=1, source_target_pairs={{0,4},{4,8},{8,12},{12,0},{1,5},{5,9},{9,13},{13,1},{2,6},{6,10},{... | collective-permute-start | bytes 884744 | tf_op jit(solution)/shard_map/ppermute | solution.py:296
  22.5 20.7 %collective-permute-start.2 = (bf16[1,64,1152]{2,1,0:T(8,128)(2,1)S(1)}, bf16[1,64,1152]{2,1,0:T(8,128)(2,1)S(1)}, u32[]{:S(2)}, u32[]{:S(2)}) collective-permute-start(bf16[1,64,1152]{2,1,0:T(8,128)(2,1)S(1)} %copy-done.12), channel_id=1, source_target_pairs={{0,12},{4,0},{8,4},{12,8},{1,13},{5,1},{9,5},{13,9},{2,14},{6,2},{... | collective-permute-start | bytes 442376 | tf_op jit(solution)/shard_map/ppermute | solution.py:296
  43.2 0.7 copy-start.8
  43.2 0.8 copy-start.4
  44.0 11.5 %collective-permute-start.4 = (bf16[2,64,1152]{2,1,0:T(8,128)(2,1)}, bf16[2,64,1152]{2,1,0:T(8,128)(2,1)S(1)}, u32[]{:S(2)}, u32[]{:S(2)}) collective-permute-start(bf16[2,64,1152]{2,1,0:T(8,128)(2,1)} %hand.5.refs_4_), channel_id=1, source_target_pairs={{0,4},{4,8},{8,12},{12,0},{1,5},{5,9},{9,13},{13,1},{2,6},{6,10},{... | collective-permute-start | bytes 884744 | tf_op jit(solution)/shard_map/ppermute | solution.py:296
  45.6 0.7 copy-start.3
  46.3 0.7 copy-start.2
  47.1 28.7 %copy-start = (f32[384,512]{1,0:T(8,128)S(1)}, f32[384,512]{1,0:T(8,128)}, u32[]{:S(2)}) copy-start(f32[384,512]{1,0:T(8,128)} %get-tuple-element.17.base_a) | copy-start | bytes 2359300
  47.1 11.9 %collective-permute-start.7 = (bf16[2,64,1152]{2,1,0:T(8,128)(2,1)}, bf16[2,64,1152]{2,1,0:T(8,128)(2,1)S(1)}, u32[]{:S(2)}, u32[]{:S(2)}) collective-permute-start(bf16[2,64,1152]{2,1,0:T(8,128)(2,1)} %hand.6.refs_6_), channel_id=1, source_target_pairs={{0,12},{4,0},{8,4},{12,8},{1,13},{5,1},{9,5},{13,9},{2,14},{6,2},{... | collective-permute-start | bytes 884744 | tf_op jit(solution)/shard_map/ppermute | solution.py:296
  55.5 3.5 %copy-start.10 = (bf16[2,64,1152]{2,1,0:T(8,128)(2,1)}, bf16[2,64,1152]{2,1,0:T(8,128)(2,1)S(1)}, u32[]{:S(2)}) copy-start(bf16[2,64,1152]{2,1,0:T(8,128)(2,1)S(1)} %collective-permute-done.4.refs_3_) | copy-start | bytes 884740
  59.0 0.7 copy-start.11
  65.4 10.3 %collective-permute-start.8 = (f32[384,512]{1,0:T(8,128)}, f32[384,512]{1,0:T(8,128)S(1)}, u32[]{:S(2)}, u32[]{:S(2)}) collective-permute-start(f32[384,512]{1,0:T(8,128)} %hand.7), channel_id=1, source_target_pairs={{0,1},{1,0},{2,3},{3,2},{4,5},{5,4},{6,7},{7,6},{8,9},{9,8},{10,11... | collective-permute-start | bytes 2359304 | tf_op jit(solution)/shard_map/ppermute | solution.py:290
  65.5 5.4 %collective-permute-start.9 = (bf16[3,128,128]{2,1,0:T(8,128)(2,1)}, bf16[3,128,128]{2,1,0:T(8,128)(2,1)S(1)}, u32[]{:S(2)}, u32[]{:S(2)}) collective-permute-start(bf16[3,128,128]{2,1,0:T(8,128)(2,1)} %get-tuple-element.26), channel_id=1, source_target_pairs={{0,2},{2,0},{16,18},{18,16},{1,3},{3,1},{17,19},{19,17},{4,6},{6,4... | collective-permute-start | bytes 294920 | tf_op jit(solution)/shard_map/ppermute | solution.py:309
  67.2 5.9 %collective-permute-start.10 = (bf16[3,128,128]{2,1,0:T(8,128)(2,1)}, bf16[3,128,128]{2,1,0:T(8,128)(2,1)S(1)}, u32[]{:S(2)}, u32[]{:S(2)}) collective-permute-start(bf16[3,128,128]{2,1,0:T(8,128)(2,1)} %get-tuple-element.27), channel_id=1, source_target_pairs={{0,16},{2,18},{16,0},{18,2},{1,17},{3,19},{17,1},{19,3},{4,20},{6,... | collective-permute-start | bytes 294920 | tf_op jit(solution)/shard_map/ppermute | solution.py:309
  68.7 5.7 %collective-permute-start.11 = (bf16[3,128,128]{2,1,0:T(8,128)(2,1)}, bf16[3,128,128]{2,1,0:T(8,128)(2,1)S(1)}, u32[]{:S(2)}, u32[]{:S(2)}) collective-permute-start(bf16[3,128,128]{2,1,0:T(8,128)(2,1)} %get-tuple-element.28), channel_id=1, source_target_pairs={{0,18},{2,16},{16,2},{18,0},{1,19},{3,17},{17,3},{19,1},{4,22},{6,... | collective-permute-start | bytes 294920 | tf_op jit(solution)/shard_map/ppermute | solution.py:309
  69.1 5.3 %collective-permute-start.12 = (bf16[3,128,128]{2,1,0:T(8,128)(2,1)}, bf16[3,128,128]{2,1,0:T(8,128)(2,1)S(1)}, u32[]{:S(2)}, u32[]{:S(2)}) collective-permute-start(bf16[3,128,128]{2,1,0:T(8,128)(2,1)} %get-tuple-element.25.refs_0_), channel_id=1, source_target_pairs={{0,1},{1,0},{2,3},{3,2},{4,5},{5,4},{6,7},{7,6},{8,9},{9,8},{10,11... | collective-permute-start | bytes 294920 | tf_op jit(solution)/shard_map/ppermute | solution.py:290
  70.9 3.5 %collective-permute-start.13 = (bf16[3,128,128]{2,1,0:T(8,128)(2,1)S(1)}, bf16[3,128,128]{2,1,0:T(8,128)(2,1)S(1)}, u32[]{:S(2)}, u32[]{:S(2)}) collective-permute-start(bf16[3,128,128]{2,1,0:T(8,128)(2,1)S(1)} %collective-permute-done.9.refs_1_), channel_id=1, source_target_pairs={{0,1},{1,0},{2,3},{3,2},{4,5},{5,4},{6,7},{7,6},{8,9},{9,8},{10,11... | collective-permute-start | bytes 294920 | tf_op jit(solution)/shard_map/ppermute | solution.py:290
  73.1 1.4 %collective-permute-start.14 = (bf16[3,128,128]{2,1,0:T(8,128)(2,1)S(1)}, bf16[3,128,128]{2,1,0:T(8,128)(2,1)S(1)}, u32[]{:S(2)}, u32[]{:S(2)}) collective-permute-start(bf16[3,128,128]{2,1,0:T(8,128)(2,1)S(1)} %collective-permute-done.10.refs_2_), channel_id=1, source_target_pairs={{0,1},{1,0},{2,3},{3,2},{4,5},{5,4},{6,7},{7,6},{8,9},{9,8},{10,11... | collective-permute-start | bytes 294920 | tf_op jit(solution)/shard_map/ppermute | solution.py:290
  74.4 1.3 %collective-permute-start.15 = (bf16[3,128,128]{2,1,0:T(8,128)(2,1)S(1)}, bf16[3,128,128]{2,1,0:T(8,128)(2,1)S(1)}, u32[]{:S(2)}, u32[]{:S(2)}) collective-permute-start(bf16[3,128,128]{2,1,0:T(8,128)(2,1)S(1)} %collective-permute-done.11.refs_3_), channel_id=1, source_target_pairs={{0,1},{1,0},{2,3},{3,2},{4,5},{5,4},{6,7},{7,6},{8,9},{9,8},{10,11... | collective-permute-start | bytes 294920 | tf_op jit(solution)/shard_map/ppermute | solution.py:290
  75.7 0.9 %copy-start.1 = (bf16[3,128,128]{2,1,0:T(8,128)(2,1)S(1)}, bf16[3,128,128]{2,1,0:T(8,128)(2,1)}, u32[]{:S(2)}) copy-start(bf16[3,128,128]{2,1,0:T(8,128)(2,1)} %get-tuple-element.25.refs_0_) | copy-start | bytes 294916

commit v19 on v14

--- a/solution.py
+++ b/solution.py
@@ -65,17 +65,28 @@
     )(down, up)
 
 
-def spread_kernel(lengths, ids, tok, out, held, in_sems, out_sems):
+def mate_at(k, sign, groups, pair):
+    kg, ky = k // pair, k % pair
+    g = lax.rem(lax.axis_index("groups") + sign * kg + groups, groups)
+    y = lax.rem(lax.axis_index("pair") + sign * ky + pair, pair)
+    return g * pair + y
+
+
+def spread_kernel(groups, pair, lengths, ids, tok, *refs):
+    held, in_sems, out_sems = refs[-3:]
+    outs = refs[:-3]
     blocks = lengths.shape[0]
     shares, tall, step = held.shape
     rows = tok.shape[0]
     block = rows // blocks
+    mates = [pl.multiple_of(mate_at(k, 1, groups, pair) * step, LANES) for k in range(shares)]
+    order = list(range(1, shares)) + [0]
 
     def read(k, b):
         here = pl.ds(b * block, block)
-        return pltpu.make_async_copy(tok.at[here, pl.ds(k * step, step)], held.at[k, here, :], in_sems.at[k, b])
-
-    for k in range(shares):
+        return pltpu.make_async_copy(tok.at[here, pl.ds(mates[k], step)], held.at[k, here, :], in_sems.at[k, b])
+
+    for k in order:
         for b in range(blocks):
             read(k, b).start()
     lane = lax.broadcasted_iota(jnp.int32, (tall - rows, step), 1)
@@ -83,8 +94,8 @@
     for b in range(blocks):
         named = jnp.where(lane == b, ids[b].astype(jnp.float32), named)
     named = named.astype(held.dtype)
-    writes = [pltpu.make_async_copy(held.at[k], out.at[k], out_sems.at[k]) for k in range(shares)]
-    for k in range(shares):
+    writes = [pltpu.make_async_copy(held.at[k], outs[k], out_sems.at[k]) for k in range(shares)]
+    for k in order:
         held[k, rows:, :] = named
         for b in range(blocks):
             read(k, b).wait()
@@ -101,16 +112,17 @@
         write.wait()
 
 
-def spread(tokens, lengths, ids, shares):
+def spread(tokens, lengths, ids, groups, pair):
     rows, feats = tokens.shape
-    shape = (shares, rows + 16, feats // shares)
-    return pl.pallas_call(
-        spread_kernel,
+    shares = groups * pair
+    shape = (rows + 16, feats // shares)
+    return pl.pallas_call(
+        functools.partial(spread_kernel, groups, pair),
         in_specs=[SMEM, SMEM, ANY],
-        out_specs=ANY,
-        out_shape=jax.ShapeDtypeStruct(shape, tokens.dtype),
+        out_specs=[ANY] * shares,
+        out_shape=[jax.ShapeDtypeStruct(shape, tokens.dtype)] * shares,
         scratch_shapes=[
-            pltpu.VMEM(shape, tokens.dtype),
+            pltpu.VMEM((shares,) + shape, tokens.dtype),
             pltpu.SemaphoreType.DMA((shares, lengths.shape[0])),
             pltpu.SemaphoreType.DMA((shares,)),
         ],
@@ -172,13 +184,6 @@
     )(lengths, tokens, base_key)
 
 
-def mate_at(k, sign, groups, pair):
-    kg, ky = k // pair, k % pair
-    g = lax.rem(lax.axis_index("groups") + sign * kg + groups, groups)
-    y = lax.rem(lax.axis_index("pair") + sign * ky + pair, pair)
-    return g * pair + y
-
-
 def collect_kernel(*refs):
     sems, held, pieces = refs[-1], refs[-2], refs[:-2]
     copies, start = [], 0
@@ -204,20 +209,21 @@
     )(*pieces)
 
 
-def rank_kernel(groups, ring, pair, rows, owner, tok, held, *outs):
-    shares = groups * pair
+def rank_kernel(ring, pair, rows, owner, held, *refs):
+    shares = (len(refs) - 1) // 2
+    toks, outs, flag = refs[:shares], refs[shares:-1], refs[-1]
+    flag[...] = jnp.zeros_like(flag)
     per, rank = held.shape[0] // (ring * pair), held.shape[1]
     blocks, _, block = outs[0].shape
-    feats = tok.shape[2]
+    feats = toks[0].shape[1]
     z, y = lax.axis_index("ring"), lax.axis_index("pair")
     lane = lax.broadcasted_iota(jnp.int32, (16, LANES), 1)
     row = lax.broadcasted_iota(jnp.int32, (16, LANES), 0)
-    mates = [mate_at(k, 1, groups, pair) for k in range(shares)]
     ids = []
-    for mate in mates:
-        named = tok[mate, rows:, :LANES].astype(jnp.float32)
+    for tok in toks:
+        named = tok[rows:, :LANES].astype(jnp.float32)
         ids += [jnp.sum(jnp.where((lane == b) & (row == 0), named, 0.0)).astype(jnp.int32) for b in range(blocks)]
-    for k, mate in enumerate(mates):
+    for k, tok in enumerate(toks):
         for b in range(blocks):
             slot = owner[ids[k * blocks + b]]
             chip = slot // per
@@ -226,7 +232,7 @@
             at = (way * ring + away) * per + lax.rem(slot, per)
             part = lax.dot_general(
                 held[at, :, :feats],
-                tok[mate, b * block : (b + 1) * block, :],
+                tok[b * block : (b + 1) * block, :],
                 (((1,), (1,)), ((), ())),
                 preferred_element_type=jnp.float32,
             )
@@ -234,17 +240,18 @@
             outs[k][b, rank:, :] = held[at, :, feats:]
 
 
-def rank_parts(owner, tok, held, groups, ring, pair, rows, blocks):
-    shares, rank = tok.shape[0], held.shape[1]
-    return pl.pallas_call(
-        functools.partial(rank_kernel, groups, ring, pair, rows),
-        in_specs=[SMEM, VMEM, VMEM],
-        out_specs=[VMEM] * shares,
-        out_shape=[jax.ShapeDtypeStruct((blocks, 2 * rank, rows // blocks), tok.dtype)] * shares,
-        cost_estimate=pl.CostEstimate(flops=2 * tok.size * rank, bytes_accessed=2 * tok.size, transcendentals=0),
+def rank_parts(owner, toks, held, ring, pair, rows, blocks):
+    shares, rank = len(toks), held.shape[1]
+    return pl.pallas_call(
+        functools.partial(rank_kernel, ring, pair, rows),
+        in_specs=[SMEM, VMEM] + [VMEM] * shares,
+        out_specs=[VMEM] * (shares + 1),
+        out_shape=[jax.ShapeDtypeStruct((blocks, 2 * rank, rows // blocks), held.dtype)] * shares
+        + [jax.ShapeDtypeStruct((8, LANES), jnp.float32)],
+        cost_estimate=pl.CostEstimate(flops=0, bytes_accessed=0, transcendentals=0),
         compiler_params=ROOM,
         name="rank",
-    )(owner, tok, held)
+    )(owner, held, *toks)
 
 
 def final_kernel(groups, pair, base_a, base_b, *refs):
@@ -259,7 +266,7 @@
         for part in mine[1:] + theirs:
             total += part[b, :rank, :].astype(jnp.float32)
         for k in range(shares):
-            tile = lax.rem(mate_at(k, -1, groups, pair), tiles)
+            tile = lax.rem(mate_at(k, 1, groups, pair), tiles)
             up[b, :, pl.ds(pl.multiple_of(tile * LANES, LANES), LANES)] = mine[k][b, rank:, :]
         delta = lax.dot_general(
             total.astype(jnp.bfloat16), up[b], (((0,), (0,)), ((), ())), preferred_element_type=jnp.float32
@@ -289,9 +296,6 @@
 
     def across(x):
         return lax.ppermute(x, "tensor", [(i, (i + 1) % sides) for i in range(sides)])
-
-    def to_plane(x):
-        return lax.all_to_all(x, PLANE, split_axis=0, concat_axis=0, tiled=True)
 
     def along(x, step):
         return lax.ppermute(x, "ring", [(a, (a + step) % ring) for a in range(ring)])
@@ -319,12 +323,12 @@
         return [held[k] for k in range(ring)]
 
     packed = pack(jnp.swapaxes(adapter_down, 1, 2), adapter_up, shares, pair)
-    slabs = spread(tokens, lengths, adapter_ids.reshape(-1), shares)
+    slabs = spread(tokens, lengths, adapter_ids.reshape(-1), groups, pair)
     swapped = [
         lax.ppermute(packed[pair - w], "pair", [(a, (a - w) % pair) for a in range(pair)]) for w in range(1, pair)
     ]
     firsts = [first_hops(piece) for piece in [packed[0]] + swapped]
-    tok = to_plane(hand_on(slabs, *swapped, firsts[0][ring - 1]))
+    toks = [slabs[0]] + [in_plane(slabs[k], k // pair, k % pair) for k in range(1, shares)]
 
     base_mine, base_out, flag = base_halves(tokens, base_key, sides, lengths)
     pieces = [
@@ -333,10 +337,10 @@
     ]
 
     flat = [piece for way in pieces for piece in way]
-    parts = rank_parts(owner_slot, tok, collect(flat), groups, ring, pair, rows, blocks)
-    mine = [parts[0]] + [in_plane(parts[k], k // pair, k % pair) for k in range(1, shares)]
+    *parts, ready = rank_parts(owner_slot, toks, collect(flat), ring, pair, rows, blocks)
+    mine = [parts[0]] + [in_plane(parts[k], -(k // pair), -(k % pair)) for k in range(1, shares)]
     theirs = [across(part) for part in mine]
-    base_in = across(hand_on(base_out, parts[0]))
+    base_in = across(hand_on(base_out, ready))
     return final(mine, theirs, [base_mine, base_in], groups, pair, tokens.dtype)
 
 

time: 75.6 us -> 69.9 us (0.925)
  waiting for transfers between devices: 28.5 us -> 21.3 us
  starting transfers between devices: 17.1 us -> 20.6 us
  local copies, waits for them, and re-layouts: 8.41 us -> 5.81 us
    ppermute x6, waiting for transfers between devices: 20 us -> 15.2 us  [along(): lax.ppermute(x, 'ring', [(a, (a + step) % ring) for a in range(ring)])]
    all_to_all x1 -> x0, starting transfers between devices: 3.71 us -> none  [to_plane(): return lax.all_to_all(x, PLANE, split_axis=0, concat_axis=0, tiled=True)]
    ppermute x3 -> x6, starting transfers between devices: 3.49 us -> 7.04 us  [in_plane(): return lax.ppermute(x, PLANE, pairs)]
    ppermute x6, starting transfers between devices: 6.87 us -> 10.2 us  [along(): lax.ppermute(x, 'ring', [(a, (a + step) % ring) for a in range(ring)])]
    unnamed x22 -> x26, local copies, waits for them, and re-layouts: 8.41 us -> 5.81 us
    ppermute x1, waiting for transfers between devices: 2.01 us -> 0.01 us  [body(): lax.ppermute(packed[pair - w], 'pair', [(a, (a - w) % pair) for a in rang...]
    ppermute x3 -> x6, waiting for transfers between devices: 5.16 us -> 4.72 us  [in_plane(): return lax.ppermute(x, PLANE, pairs)]
  transfers between devices with their start and end apart: 16 -> 18, of which waited for: 10 -> 8; matrix products, arithmetic and copies ran while one was open for 0% -> 0% of each run, Pallas kernels for 22% -> 23%
where the time goes in v19:
time: 69.9 us; the launch traced here: 69.3 us
  Pallas kernels  21.5 us (31%)
  waiting for transfers between devices  21.3 us (30%)
  starting transfers between devices  20.6 us (29%)
  local copies, waits for them, and re-layouts  5.81 us (8%)
    ppermute x6, waiting for transfers between devices, along(): lax.ppermute(x, 'ring', [(a, (a + step) % ring) for a in range(ring)])  15.2 us
    pallas_call x1, Pallas kernels, base_halves(): pl.pallas_call(functools.partial(base_kernel, sides), grid_spec=pltpu.Pre...  11.3 us
    ppermute x6, starting transfers between devices, along(): lax.ppermute(x, 'ring', [(a, (a + step) % ring) for a in range(ring)])  10.2 us
    ppermute x6, starting transfers between devices, in_plane(): return lax.ppermute(x, PLANE, pairs)  7.04 us
    unnamed x26, local copies, waits for them, and re-layouts  5.81 us
    ppermute x6, waiting for transfers between devices, in_plane(): return lax.ppermute(x, PLANE, pairs)  4.72 us
    pallas_call x1, Pallas kernels, spread(): pl.pallas_call(functools.partial(spread_kernel, groups, pair), in_specs=[...  3.67 us
    ppermute x1, starting transfers between devices, body(): lax.ppermute(packed[pair - w], 'pair', [(a, (a - w) % pair) for a in rang...  3.03 us
  transfers between devices with their start and end apart: 18, of which 8 were waited for; matrix products, arithmetic and copies ran while one was open for 0% of the time, Pallas kernels for 23%

profile of v19, /device:TPU:0, one launch (start us, length us, event | category | flops | bytes accessed | tf_op | source)
XLA Modules:
  0.0 69.3 jit_solution(6333641898743706063)
XLA Ops:
  0.0 1.9 %pack.1 = (bf16[2,64,1152]{2,1,0:T(8,128)(2,1)}, bf16[2,64,1152]{2,1,0:T(8,128)(2,1)}) custom-call(bf16[2,64,4096]{2,1,0:T(8,128)(2,1)} %bitcast.2, bf16[2,64,512]{2,1,0:T(8,128)(2,1)} %up.1), custom_call_target="tpu_custom_call" | custom-call | tf_op jit(solution)/shard_map/pack/pallas_call | solution.py:57
  1.9 3.0 %collective-permute-start.3 = (bf16[2,64,1152]{2,1,0:T(8,128)(2,1)}, bf16[2,64,1152]{2,1,0:T(8,128)(2,1)}, u32[]{:S(2)}, u32[]{:S(2)}) collective-permute-start(bf16[2,64,1152]{2,1,0:T(8,128)(2,1)} %get-tuple-element.23), channel_id=1, source_target_pairs={{0,2},{2,0},{1,3},{3,1},{4,6},{6,4},{5,7},{7,5},{8,10},{10,8},{9,1... | collective-permute-start | bytes 884744 | tf_op jit(solution)/shard_map/ppermute | solution.py:328
  5.0 1.6 %collective-permute-start.1 = (bf16[2,64,1152]{2,1,0:T(8,128)(2,1)}, bf16[2,64,1152]{2,1,0:T(8,128)(2,1)S(1)}, u32[]{:S(2)}, u32[]{:S(2)}) collective-permute-start(bf16[2,64,1152]{2,1,0:T(8,128)(2,1)} %get-tuple-element.21.refs_0_), channel_id=1, source_target_pairs={{0,4},{4,8},{8,12},{12,0},{1,5},{5,9},{9,13},{13,1},{2,6},{6,10},{... | collective-permute-start | bytes 884744 | tf_op jit(solution)/shard_map/ppermute | solution.py:301
  6.5 2.2 %collective-permute-start = (bf16[2,64,1152]{2,1,0:T(8,128)(2,1)}, bf16[2,64,1152]{2,1,0:T(8,128)(2,1)S(1)}, u32[]{:S(2)}, u32[]{:S(2)}) collective-permute-start(bf16[2,64,1152]{2,1,0:T(8,128)(2,1)} %get-tuple-element.21.refs_0_), channel_id=1, source_target_pairs={{0,12},{4,0},{8,4},{12,8},{1,13},{5,1},{9,5},{13,9},{2,14},{6,2},{... | collective-permute-start | bytes 884744 | tf_op jit(solution)/shard_map/ppermute | solution.py:301
  8.8 3.7 %spread.1 = (bf16[400,1024]{1,0:T(8,128)(2,1)}, bf16[400,1024]{1,0:T(8,128)(2,1)}, bf16[400,1024]{1,0:T(8,128)(2,1)}, bf16[400,1024]{1,0:T(8,128)(2,1)}) custom-call(s32[3]{0:T(128)} %lengths.3, s32[3]{0:T(128)} %bitcast.3, bf16[384,4096]{1,0:T(8,128)(2,1)} %tok.1), custom_call_target="tpu_custom_call" | custom-call | tf_op jit(solution)/shard_map/spread/pallas_call | solution.py:119
  12.5 0.4 collective-permute-start.7
  12.8 1.7 %collective-permute-start.8 = (bf16[400,1024]{1,0:T(8,128)(2,1)}, bf16[400,1024]{1,0:T(8,128)(2,1)S(1)}, u32[]{:S(2)}, u32[]{:S(2)}) collective-permute-start(bf16[400,1024]{1,0:T(8,128)(2,1)} %get-tuple-element.26), channel_id=1, source_target_pairs={{0,16},{2,18},{16,0},{18,2},{1,17},{3,19},{17,1},{19,3},{4,20},{6,... | collective-permute-start | bytes 2457608 | tf_op jit(solution)/shard_map/ppermute | solution.py:311
  14.5 0.0 collective-permute-done.3.refs_4_
  14.5 1.5 %collective-permute-start.9 = (bf16[400,1024]{1,0:T(8,128)(2,1)}, bf16[400,1024]{1,0:T(8,128)(2,1)}, u32[]{:S(2)}, u32[]{:S(2)}) collective-permute-start(bf16[400,1024]{1,0:T(8,128)(2,1)} %get-tuple-element.27), channel_id=1, source_target_pairs={{0,18},{2,16},{16,2},{18,0},{1,19},{3,17},{17,3},{19,1},{4,22},{6,... | collective-permute-start | bytes 2457608 | tf_op jit(solution)/shard_map/ppermute | solution.py:311
  16.0 0.9 %collective-permute-done.1.refs_0_ = bf16[2,64,1152]{2,1,0:T(8,128)(2,1)S(1)} collective-permute-done((bf16[2,64,1152]{2,1,0:T(8,128)(2,1)}, bf16[2,64,1152]{2,1,0:T(8,128)(2,1)S(1)}, u32[]{:S(2)}, u32[]{:S(2)}) %collective-permute-start.1) | collective-permute-done | bytes 294944 | tf_op jit(solution)/shard_map/ppermute | solution.py:301
  16.9 0.4 collective-permute-start.5
  17.3 4.7 %collective-permute-done.refs_1_ = bf16[2,64,1152]{2,1,0:T(8,128)(2,1)S(1)} collective-permute-done((bf16[2,64,1152]{2,1,0:T(8,128)(2,1)}, bf16[2,64,1152]{2,1,0:T(8,128)(2,1)S(1)}, u32[]{:S(2)}, u32[]{:S(2)}) %collective-permute-start) | collective-permute-done | bytes 294944 | tf_op jit(solution)/shard_map/ppermute | solution.py:301
  22.0 2.8 %collective-permute-start.4 = (bf16[2,64,1152]{2,1,0:T(8,128)(2,1)}, bf16[2,64,1152]{2,1,0:T(8,128)(2,1)S(1)}, u32[]{:S(2)}, u32[]{:S(2)}) collective-permute-start(bf16[2,64,1152]{2,1,0:T(8,128)(2,1)} %collective-permute-done.3.refs_4_), channel_id=1, source_target_pairs={{0,12},{4,0},{8,4},{12,8},{1,13},{5,1},{9,5},{13,9},{2,14},{6,2},{... | collective-permute-start | bytes 884744 | tf_op jit(solution)/shard_map/ppermute | solution.py:301
  24.8 11.3 %base.1 = (f32[384,512]{1,0:T(8,128)}, f32[384,512]{1,0:T(8,128)}, f32[8,128]{1,0:T(8,128)}) custom-call(s32[3]{0:T(128)} %lengths.3, bf16[384,4096]{1,0:T(8,128)(2,1)} %tok.1, bf16[4096,1024]{1,0:T(8,128)(2,1)} %key_ref.1), custom_call_target="tpu_custom_call" | custom-call | tf_op jit(solution)/shard_map/base/pallas_call | solution.py:167
  36.1 0.0 copy-start.12
  36.2 0.0 collective-permute-done.5.refs_1_.refs_7_
  36.2 0.1 collective-permute-start.2
  36.2 0.0 collective-permute-done.4.refs_0_
  36.2 0.6 copy-done.4
  36.9 0.7 %copy-done.6 = bf16[2,64,1152]{2,1,0:T(8,128)(2,1)} copy-done((bf16[2,64,1152]{2,1,0:T(8,128)(2,1)}, bf16[2,64,1152]{2,1,0:T(8,128)(2,1)S(1)}, u32[]{:S(2)}) %copy-start.6) | copy-done | bytes 294936
  37.6 3.2 %collective-permute-start.6 = (bf16[2,64,1152]{2,1,0:T(8,128)(2,1)}, bf16[2,64,1152]{2,1,0:T(8,128)(2,1)S(1)}, u32[]{:S(2)}, u32[]{:S(2)}) collective-permute-start(bf16[2,64,1152]{2,1,0:T(8,128)(2,1)} %hand.4.refs_5_), channel_id=1, source_target_pairs={{0,12},{4,0},{8,4},{12,8},{1,13},{5,1},{9,5},{13,9},{2,14},{6,2},{... | collective-permute-start | bytes 884744 | tf_op jit(solution)/shard_map/ppermute | solution.py:301
  40.8 6.6 %collective-permute-done.2.refs_2_ = bf16[2,64,1152]{2,1,0:T(8,128)(2,1)S(1)} collective-permute-done((bf16[2,64,1152]{2,1,0:T(8,128)(2,1)}, bf16[2,64,1152]{2,1,0:T(8,128)(2,1)S(1)}, u32[]{:S(2)}, u32[]{:S(2)}) %collective-permute-start.2) | collective-permute-done | bytes 294944 | tf_op jit(solution)/shard_map/ppermute | solution.py:301
  47.4 3.0 %collective-permute-done.6.refs_6_ = bf16[2,64,1152]{2,1,0:T(8,128)(2,1)S(1)} collective-permute-done((bf16[2,64,1152]{2,1,0:T(8,128)(2,1)}, bf16[2,64,1152]{2,1,0:T(8,128)(2,1)S(1)}, u32[]{:S(2)}, u32[]{:S(2)}) %collective-permute-start.6) | collective-permute-done | bytes 294944 | tf_op jit(solution)/shard_map/ppermute | solution.py:301
  50.4 1.0 %copy-done.1 = bf16[2,64,1152]{2,1,0:T(8,128)(2,1)S(1)} copy-done((bf16[2,64,1152]{2,1,0:T(8,128)(2,1)S(1)}, bf16[2,64,1152]{2,1,0:T(8,128)(2,1)}, u32[]{:S(2)}) %copy-start.1) | copy-done | bytes 294936
  51.3 1.0 %copy-done.3 = bf16[2,64,1152]{2,1,0:T(8,128)(2,1)S(1)} copy-done((bf16[2,64,1152]{2,1,0:T(8,128)(2,1)S(1)}, bf16[2,64,1152]{2,1,0:T(8,128)(2,1)}, u32[]{:S(2)}) %copy-start.3) | copy-done | bytes 294936
  52.3 1.0 %copy-done.5 = bf16[2,64,1152]{2,1,0:T(8,128)(2,1)S(1)} copy-done((bf16[2,64,1152]{2,1,0:T(8,128)(2,1)S(1)}, bf16[2,64,1152]{2,1,0:T(8,128)(2,1)}, u32[]{:S(2)}) %copy-start.5) | copy-done | bytes 294936
  53.3 1.0 %copy-done.7 = bf16[2,64,1152]{2,1,0:T(8,128)(2,1)S(1)} copy-done((bf16[2,64,1152]{2,1,0:T(8,128)(2,1)S(1)}, bf16[2,64,1152]{2,1,0:T(8,128)(2,1)}, u32[]{:S(2)}) %copy-start.7) | copy-done | bytes 294936
  54.2 1.3 %collect.1.held = bf16[16,64,1152]{2,1,0:T(8,128)(2,1)S(1)} custom-call(bf16[2,64,1152]{2,1,0:T(8,128)(2,1)S(1)} %copy-done.10, bf16[2,64,1152]{2,1,0:T(8,128)(2,1)S(1)} %copy-done.1, bf16[2,64,1152]{2,1,0:T(8,128)(2,1)S(1)} %collective-permute-done.2.refs_2_, bf16[2,64,1152]{2,1,0:T(8,128)(2,1)S(1)} %copy-done.3, ...), custom_call_target="tpu_custom_call" | custom-call | tf_op jit(solution)/shard_map/collect/pallas_call | solution.py:201
  55.5 0.0 collective-permute-done.7.refs_1_
  55.5 0.0 collective-permute-done.8.refs_2_
  55.5 0.0 collective-permute-done.9.refs_3_
  55.6 2.3 %rank.1 = (bf16[3,128,128]{2,1,0:T(8,128)(2,1)S(1)}, bf16[3,128,128]{2,1,0:T(8,128)(2,1)S(1)}, bf16[3,128,128]{2,1,0:T(8,128)(2,1)S(1)}, bf16[3,128,128]{2,1,0:T(8,128)(2,1)S(1)}, f32[8,128]{1,0:T(8,128)S(1)}) custom-call(s32[16]{0:T(128)S(1)} %copy-done.12, bf16[16,64,1152]{2,1,0:T(8,128)(2,1)S(1)} %collect.1.held, bf16[400,1024]{1,0:T(8,128)(2,1)S(1)} %copy-done.8, ...), custom_call_target="tpu_custom_call" | custom-call | tf_op jit(solution)/shard_map/rank/pallas_call | solution.py:245
  57.9 0.0 copy-start.11
  57.9 0.6 copy-done.11
  58.5 0.0 collective-permute-start.10
  58.5 0.5 collective-permute-start.11
  59.0 1.5 %collective-permute-start.12 = (bf16[3,128,128]{2,1,0:T(8,128)(2,1)S(1)}, bf16[3,128,128]{2,1,0:T(8,128)(2,1)S(1)}, u32[]{:S(2)}, u32[]{:S(2)}) collective-permute-start(bf16[3,128,128]{2,1,0:T(8,128)(2,1)S(1)} %get-tuple-element.31), channel_id=1, source_target_pairs={{0,16},{2,18},{16,0},{18,2},{1,17},{3,19},{17,1},{19,3},{4,20},{6,... | collective-permute-start | bytes 294920 | tf_op jit(solution)/shard_map/ppermute | solution.py:311
  60.5 1.5 %collective-permute-start.13 = (bf16[3,128,128]{2,1,0:T(8,128)(2,1)S(1)}, bf16[3,128,128]{2,1,0:T(8,128)(2,1)S(1)}, u32[]{:S(2)}, u32[]{:S(2)}) collective-permute-start(bf16[3,128,128]{2,1,0:T(8,128)(2,1)S(1)} %get-tuple-element.32), channel_id=1, source_target_pairs={{0,18},{2,16},{16,2},{18,0},{1,19},{3,17},{17,3},{19,1},{4,22},{6,... | collective-permute-start | bytes 294920 | tf_op jit(solution)/shard_map/ppermute | solution.py:311
  62.0 1.7 %collective-permute-done.11.refs_1_ = bf16[3,128,128]{2,1,0:T(8,128)(2,1)S(1)} collective-permute-done((bf16[3,128,128]{2,1,0:T(8,128)(2,1)S(1)}, bf16[3,128,128]{2,1,0:T(8,128)(2,1)S(1)}, u32[]{:S(2)}, u32[]{:S(2)}) %collective-permute-start.11) | collective-permute-done | bytes 98336 | tf_op jit(solution)/shard_map/ppermute | solution.py:311
  63.7 0.2 collective-permute-done.12.refs_2_
  63.9 0.3 collective-permute-start.16
  64.2 2.8 %collective-permute-done.13.refs_3_ = bf16[3,128,128]{2,1,0:T(8,128)(2,1)S(1)} collective-permute-done((bf16[3,128,128]{2,1,0:T(8,128)(2,1)S(1)}, bf16[3,128,128]{2,1,0:T(8,128)(2,1)S(1)}, u32[]{:S(2)}, u32[]{:S(2)}) %collective-permute-start.13) | collective-permute-done | bytes 98336 | tf_op jit(solution)/shard_map/ppermute | solution.py:311
  67.0 0.0 collective-permute-start.17
  67.0 0.0 collective-permute-done.14.refs_4_
  67.0 0.0 collective-permute-done.15.refs_5_
  67.0 0.0 collective-permute-done.16.refs_6_
  67.0 1.3 %collective-permute-done.17.refs_7_ = bf16[3,128,128]{2,1,0:T(8,128)(2,1)S(1)} collective-permute-done((bf16[3,128,128]{2,1,0:T(8,128)(2,1)S(1)}, bf16[3,128,128]{2,1,0:T(8,128)(2,1)S(1)}, u32[]{:S(2)}, u32[]{:S(2)}) %collective-permute-start.17) | collective-permute-done | bytes 98336 | tf_op jit(solution)/shard_map/ppermute | solution.py:298
  68.3 1.1 %final.1 = bf16[384,512]{1,0:T(8,128)(2,1)} custom-call(f32[384,512]{1,0:T(8,128)S(1)} %copy-done.9, f32[384,512]{1,0:T(8,128)S(1)} %collective-permute-done.10.base_b, bf16[3,128,128]{2,1,0:T(8,128)(2,1)S(1)} %get-tuple-element.29.refs_0_, bf16[3,128,128]{2,1,0:T(8,128)(2,1)S(1)} %collective-permute-done.11.refs_1_, ...), custom_call_target="tpu_custom_call" | custom-call | tf_op jit(solution)/shard_map/final/pallas_call | solution.py:279
  (23 shorter events, 0.0 us)
Async XLA Ops:
  1.9 12.6 %collective-permute-start.3 = (bf16[2,64,1152]{2,1,0:T(8,128)(2,1)}, bf16[2,64,1152]{2,1,0:T(8,128)(2,1)}, u32[]{:S(2)}, u32[]{:S(2)}) collective-permute-start(bf16[2,64,1152]{2,1,0:T(8,128)(2,1)} %get-tuple-element.23), channel_id=1, source_target_pairs={{0,2},{2,0},{1,3},{3,1},{4,6},{6,4},{5,7},{7,5},{8,10},{10,8},{9,1... | collective-permute-start | bytes 884744 | tf_op jit(solution)/shard_map/ppermute | solution.py:328
  5.0 12.0 %collective-permute-start.1 = (bf16[2,64,1152]{2,1,0:T(8,128)(2,1)}, bf16[2,64,1152]{2,1,0:T(8,128)(2,1)S(1)}, u32[]{:S(2)}, u32[]{:S(2)}) collective-permute-start(bf16[2,64,1152]{2,1,0:T(8,128)(2,1)} %get-tuple-element.21.refs_0_), channel_id=1, source_target_pairs={{0,4},{4,8},{8,12},{12,0},{1,5},{5,9},{9,13},{13,1},{2,6},{6,10},{... | collective-permute-start | bytes 884744 | tf_op jit(solution)/shard_map/ppermute | solution.py:301
  6.5 15.5 %collective-permute-start = (bf16[2,64,1152]{2,1,0:T(8,128)(2,1)}, bf16[2,64,1152]{2,1,0:T(8,128)(2,1)S(1)}, u32[]{:S(2)}, u32[]{:S(2)}) collective-permute-start(bf16[2,64,1152]{2,1,0:T(8,128)(2,1)} %get-tuple-element.21.refs_0_), channel_id=1, source_target_pairs={{0,12},{4,0},{8,4},{12,8},{1,13},{5,1},{9,5},{13,9},{2,14},{6,2},{... | collective-permute-start | bytes 884744 | tf_op jit(solution)/shard_map/ppermute | solution.py:301
  12.5 43.0 %collective-permute-start.7 = (bf16[400,1024]{1,0:T(8,128)(2,1)}, bf16[400,1024]{1,0:T(8,128)(2,1)S(1)}, u32[]{:S(2)}, u32[]{:S(2)}) collective-permute-start(bf16[400,1024]{1,0:T(8,128)(2,1)} %get-tuple-element.25), channel_id=1, source_target_pairs={{0,2},{2,0},{16,18},{18,16},{1,3},{3,1},{17,19},{19,17},{4,6},{6,4... | collective-permute-start | bytes 2457608 | tf_op jit(solution)/shard_map/ppermute | solution.py:311
  12.8 42.7 %collective-permute-start.8 = (bf16[400,1024]{1,0:T(8,128)(2,1)}, bf16[400,1024]{1,0:T(8,128)(2,1)S(1)}, u32[]{:S(2)}, u32[]{:S(2)}) collective-permute-start(bf16[400,1024]{1,0:T(8,128)(2,1)} %get-tuple-element.26), channel_id=1, source_target_pairs={{0,16},{2,18},{16,0},{18,2},{1,17},{3,19},{17,1},{19,3},{4,20},{6,... | collective-permute-start | bytes 2457608 | tf_op jit(solution)/shard_map/ppermute | solution.py:311
  14.5 35.8 %copy-start.10 = (bf16[2,64,1152]{2,1,0:T(8,128)(2,1)S(1)}, bf16[2,64,1152]{2,1,0:T(8,128)(2,1)}, u32[]{:S(2)}) copy-start(bf16[2,64,1152]{2,1,0:T(8,128)(2,1)} %get-tuple-element.21.refs_0_) | copy-start | bytes 884740
  14.5 41.0 %collective-permute-start.9 = (bf16[400,1024]{1,0:T(8,128)(2,1)}, bf16[400,1024]{1,0:T(8,128)(2,1)}, u32[]{:S(2)}, u32[]{:S(2)}) collective-permute-start(bf16[400,1024]{1,0:T(8,128)(2,1)} %get-tuple-element.27), channel_id=1, source_target_pairs={{0,18},{2,16},{16,2},{18,0},{1,19},{3,17},{17,3},{19,1},{4,22},{6,... | collective-permute-start | bytes 2457608 | tf_op jit(solution)/shard_map/ppermute | solution.py:311
  16.9 19.2 %copy-start.2 = (bf16[2,64,1152]{2,1,0:T(8,128)(2,1)}, bf16[2,64,1152]{2,1,0:T(8,128)(2,1)S(1)}, u32[]{:S(2)}) copy-start(bf16[2,64,1152]{2,1,0:T(8,128)(2,1)S(1)} %collective-permute-done.1.refs_0_) | copy-start | bytes 884740
  16.9 19.2 %collective-permute-start.5 = (bf16[2,64,1152]{2,1,0:T(8,128)(2,1)}, bf16[2,64,1152]{2,1,0:T(8,128)(2,1)S(1)}, u32[]{:S(2)}, u32[]{:S(2)}) collective-permute-start(bf16[2,64,1152]{2,1,0:T(8,128)(2,1)} %collective-permute-done.3.refs_4_), channel_id=1, source_target_pairs={{0,4},{4,8},{8,12},{12,0},{1,5},{5,9},{9,13},{13,1},{2,6},{6,10},{... | collective-permute-start | bytes 884744 | tf_op jit(solution)/shard_map/ppermute | solution.py:301
  22.0 14.1 %copy-start = (bf16[2,64,1152]{2,1,0:T(8,128)(2,1)}, bf16[2,64,1152]{2,1,0:T(8,128)(2,1)S(1)}, u32[]{:S(2)}) copy-start(bf16[2,64,1152]{2,1,0:T(8,128)(2,1)S(1)} %collective-permute-done.refs_1_) | copy-start | bytes 884740
  22.0 14.2 %collective-permute-start.4 = (bf16[2,64,1152]{2,1,0:T(8,128)(2,1)}, bf16[2,64,1152]{2,1,0:T(8,128)(2,1)S(1)}, u32[]{:S(2)}, u32[]{:S(2)}) collective-permute-start(bf16[2,64,1152]{2,1,0:T(8,128)(2,1)} %collective-permute-done.3.refs_4_), channel_id=1, source_target_pairs={{0,12},{4,0},{8,4},{12,8},{1,13},{5,1},{9,5},{13,9},{2,14},{6,2},{... | collective-permute-start | bytes 884744 | tf_op jit(solution)/shard_map/ppermute | solution.py:301
  36.1 19.4 %copy-start.8 = (bf16[400,1024]{1,0:T(8,128)(2,1)S(1)}, bf16[400,1024]{1,0:T(8,128)(2,1)}, u32[]{:S(2)}) copy-start(bf16[400,1024]{1,0:T(8,128)(2,1)} %get-tuple-element.24.refs_0_) | copy-start | bytes 2457604
  36.1 19.4 %copy-start.12 = (s32[16]{0:T(128)S(1)}, s32[16]{0:T(128)}, u32[]{:S(2)}) copy-start(s32[16]{0:T(128)} %owner.1) | copy-start | bytes 196
  36.2 0.7 %copy-start.4 = (bf16[2,64,1152]{2,1,0:T(8,128)(2,1)}, bf16[2,64,1152]{2,1,0:T(8,128)(2,1)S(1)}, u32[]{:S(2)}) copy-start(bf16[2,64,1152]{2,1,0:T(8,128)(2,1)S(1)} %collective-permute-done.5.refs_1_.refs_7_) | copy-start | bytes 884740
  36.2 11.2 %collective-permute-start.2 = (bf16[2,64,1152]{2,1,0:T(8,128)(2,1)}, bf16[2,64,1152]{2,1,0:T(8,128)(2,1)S(1)}, u32[]{:S(2)}, u32[]{:S(2)}) collective-permute-start(bf16[2,64,1152]{2,1,0:T(8,128)(2,1)} %hand.3.refs_3_), channel_id=1, source_target_pairs={{0,4},{4,8},{8,12},{12,0},{1,5},{5,9},{9,13},{13,1},{2,6},{6,10},{... | collective-permute-start | bytes 884744 | tf_op jit(solution)/shard_map/ppermute | solution.py:301
  36.9 0.7 %copy-start.6 = (bf16[2,64,1152]{2,1,0:T(8,128)(2,1)}, bf16[2,64,1152]{2,1,0:T(8,128)(2,1)S(1)}, u32[]{:S(2)}) copy-start(bf16[2,64,1152]{2,1,0:T(8,128)(2,1)S(1)} %collective-permute-done.4.refs_0_) | copy-start | bytes 884740
  37.6 12.8 %collective-permute-start.6 = (bf16[2,64,1152]{2,1,0:T(8,128)(2,1)}, bf16[2,64,1152]{2,1,0:T(8,128)(2,1)S(1)}, u32[]{:S(2)}, u32[]{:S(2)}) collective-permute-start(bf16[2,64,1152]{2,1,0:T(8,128)(2,1)} %hand.4.refs_5_), channel_id=1, source_target_pairs={{0,12},{4,0},{8,4},{12,8},{1,13},{5,1},{9,5},{13,9},{2,14},{6,2},{... | collective-permute-start | bytes 884744 | tf_op jit(solution)/shard_map/ppermute | solution.py:301
  50.4 1.0 %copy-start.1 = (bf16[2,64,1152]{2,1,0:T(8,128)(2,1)S(1)}, bf16[2,64,1152]{2,1,0:T(8,128)(2,1)}, u32[]{:S(2)}) copy-start(bf16[2,64,1152]{2,1,0:T(8,128)(2,1)} %copy-done) | copy-start | bytes 884740
  51.3 1.0 %copy-start.3 = (bf16[2,64,1152]{2,1,0:T(8,128)(2,1)S(1)}, bf16[2,64,1152]{2,1,0:T(8,128)(2,1)}, u32[]{:S(2)}) copy-start(bf16[2,64,1152]{2,1,0:T(8,128)(2,1)} %hand.3.refs_3_) | copy-start | bytes 884740
  52.3 1.0 %copy-start.5 = (bf16[2,64,1152]{2,1,0:T(8,128)(2,1)S(1)}, bf16[2,64,1152]{2,1,0:T(8,128)(2,1)}, u32[]{:S(2)}) copy-start(bf16[2,64,1152]{2,1,0:T(8,128)(2,1)} %copy-done.4) | copy-start | bytes 884740
  53.3 1.0 %copy-start.7 = (bf16[2,64,1152]{2,1,0:T(8,128)(2,1)S(1)}, bf16[2,64,1152]{2,1,0:T(8,128)(2,1)}, u32[]{:S(2)}) copy-start(bf16[2,64,1152]{2,1,0:T(8,128)(2,1)} %hand.4.refs_5_) | copy-start | bytes 884740
  55.5 12.7 %copy-start.9 = (f32[384,512]{1,0:T(8,128)S(1)}, f32[384,512]{1,0:T(8,128)}, u32[]{:S(2)}) copy-start(f32[384,512]{1,0:T(8,128)} %get-tuple-element.19.base_a) | copy-start | bytes 2359300
  57.9 0.6 copy-start.11
  58.5 9.8 %collective-permute-start.10 = (f32[384,512]{1,0:T(8,128)}, f32[384,512]{1,0:T(8,128)S(1)}, u32[]{:S(2)}, u32[]{:S(2)}) collective-permute-start(f32[384,512]{1,0:T(8,128)} %hand.5), channel_id=1, source_target_pairs={{0,1},{1,0},{2,3},{3,2},{4,5},{5,4},{6,7},{7,6},{8,9},{9,8},{10,11... | collective-permute-start | bytes 2359304 | tf_op jit(solution)/shard_map/ppermute | solution.py:298
  58.5 5.2 %collective-permute-start.11 = (bf16[3,128,128]{2,1,0:T(8,128)(2,1)S(1)}, bf16[3,128,128]{2,1,0:T(8,128)(2,1)S(1)}, u32[]{:S(2)}, u32[]{:S(2)}) collective-permute-start(bf16[3,128,128]{2,1,0:T(8,128)(2,1)S(1)} %get-tuple-element.30), channel_id=1, source_target_pairs={{0,2},{2,0},{16,18},{18,16},{1,3},{3,1},{17,19},{19,17},{4,6},{6,4... | collective-permute-start | bytes 294920 | tf_op jit(solution)/shard_map/ppermute | solution.py:311
  59.0 4.9 %collective-permute-start.12 = (bf16[3,128,128]{2,1,0:T(8,128)(2,1)S(1)}, bf16[3,128,128]{2,1,0:T(8,128)(2,1)S(1)}, u32[]{:S(2)}, u32[]{:S(2)}) collective-permute-start(bf16[3,128,128]{2,1,0:T(8,128)(2,1)S(1)} %get-tuple-element.31), channel_id=1, source_target_pairs={{0,16},{2,18},{16,0},{18,2},{1,17},{3,19},{17,1},{19,3},{4,20},{6,... | collective-permute-start | bytes 294920 | tf_op jit(solution)/shard_map/ppermute | solution.py:311
  60.5 6.5 %collective-permute-start.13 = (bf16[3,128,128]{2,1,0:T(8,128)(2,1)S(1)}, bf16[3,128,128]{2,1,0:T(8,128)(2,1)S(1)}, u32[]{:S(2)}, u32[]{:S(2)}) collective-permute-start(bf16[3,128,128]{2,1,0:T(8,128)(2,1)S(1)} %get-tuple-element.32), channel_id=1, source_target_pairs={{0,18},{2,16},{16,2},{18,0},{1,19},{3,17},{17,3},{19,1},{4,22},{6,... | collective-permute-start | bytes 294920 | tf_op jit(solution)/shard_map/ppermute | solution.py:311
  62.0 5.0 %collective-permute-start.14 = (bf16[3,128,128]{2,1,0:T(8,128)(2,1)S(1)}, bf16[3,128,128]{2,1,0:T(8,128)(2,1)S(1)}, u32[]{:S(2)}, u32[]{:S(2)}) collective-permute-start(bf16[3,128,128]{2,1,0:T(8,128)(2,1)S(1)} %get-tuple-element.29.refs_0_), channel_id=1, source_target_pairs={{0,1},{1,0},{2,3},{3,2},{4,5},{5,4},{6,7},{7,6},{8,9},{9,8},{10,11... | collective-permute-start | bytes 294920 | tf_op jit(solution)/shard_map/ppermute | solution.py:298
  63.7 3.3 %collective-permute-start.15 = (bf16[3,128,128]{2,1,0:T(8,128)(2,1)S(1)}, bf16[3,128,128]{2,1,0:T(8,128)(2,1)S(1)}, u32[]{:S(2)}, u32[]{:S(2)}) collective-permute-start(bf16[3,128,128]{2,1,0:T(8,128)(2,1)S(1)} %collective-permute-done.11.refs_1_), channel_id=1, source_target_pairs={{0,1},{1,0},{2,3},{3,2},{4,5},{5,4},{6,7},{7,6},{8,9},{9,8},{10,11... | collective-permute-start | bytes 294920 | tf_op jit(solution)/shard_map/ppermute | solution.py:298
  63.9 3.1 %collective-permute-start.16 = (bf16[3,128,128]{2,1,0:T(8,128)(2,1)S(1)}, bf16[3,128,128]{2,1,0:T(8,128)(2,1)S(1)}, u32[]{:S(2)}, u32[]{:S(2)}) collective-permute-start(bf16[3,128,128]{2,1,0:T(8,128)(2,1)S(1)} %collective-permute-done.12.refs_2_), channel_id=1, source_target_pairs={{0,1},{1,0},{2,3},{3,2},{4,5},{5,4},{6,7},{7,6},{8,9},{9,8},{10,11... | collective-permute-start | bytes 294920 | tf_op jit(solution)/shard_map/ppermute | solution.py:298
  67.0 1.3 %collective-permute-start.17 = (bf16[3,128,128]{2,1,0:T(8,128)(2,1)S(1)}, bf16[3,128,128]{2,1,0:T(8,128)(2,1)S(1)}, u32[]{:S(2)}, u32[]{:S(2)}) collective-permute-start(bf16[3,128,128]{2,1,0:T(8,128)(2,1)S(1)} %collective-permute-done.13.refs_3_), channel_id=1, source_target_pairs={{0,1},{1,0},{2,3},{3,2},{4,5},{5,4},{6,7},{7,6},{8,9},{9,8},{10,11... | collective-permute-start | bytes 294920 | tf_op jit(solution)/shard_map/ppermute | solution.py:298

commit v20 on v19

--- a/solution.py
+++ b/solution.py
@@ -204,15 +204,15 @@
         out_specs=VMEM,
         out_shape=jax.ShapeDtypeStruct((count,) + pieces[0].shape[1:], pieces[0].dtype),
         scratch_shapes=[pltpu.SemaphoreType.DMA((len(pieces),))],
+        cost_estimate=pl.CostEstimate(flops=0, bytes_accessed=0, transcendentals=0),
         compiler_params=ROOM,
         name="collect",
     )(*pieces)
 
 
 def rank_kernel(ring, pair, rows, owner, held, *refs):
-    shares = (len(refs) - 1) // 2
-    toks, outs, flag = refs[:shares], refs[shares:-1], refs[-1]
-    flag[...] = jnp.zeros_like(flag)
+    shares = len(refs) // 2
+    toks, outs = refs[:shares], refs[shares:]
     per, rank = held.shape[0] // (ring * pair), held.shape[1]
     blocks, _, block = outs[0].shape
     feats = toks[0].shape[1]
@@ -245,9 +245,8 @@
     return pl.pallas_call(
         functools.partial(rank_kernel, ring, pair, rows),
         in_specs=[SMEM, VMEM] + [VMEM] * shares,
-        out_specs=[VMEM] * (shares + 1),
-        out_shape=[jax.ShapeDtypeStruct((blocks, 2 * rank, rows // blocks), held.dtype)] * shares
-        + [jax.ShapeDtypeStruct((8, LANES), jnp.float32)],
+        out_specs=[VMEM] * shares,
+        out_shape=[jax.ShapeDtypeStruct((blocks, 2 * rank, rows // blocks), held.dtype)] * shares,
         cost_estimate=pl.CostEstimate(flops=0, bytes_accessed=0, transcendentals=0),
         compiler_params=ROOM,
         name="rank",
@@ -337,10 +336,13 @@
     ]
 
     flat = [piece for way in pieces for piece in way]
-    *parts, ready = rank_parts(owner_slot, toks, collect(flat), ring, pair, rows, blocks)
-    mine = [parts[0]] + [in_plane(parts[k], -(k // pair), -(k % pair)) for k in range(1, shares)]
-    theirs = [across(part) for part in mine]
-    base_in = across(hand_on(base_out, ready))
+    parts = rank_parts(owner_slot, toks, collect(flat), ring, pair, rows, blocks)
+    mine, theirs = [parts[0]] * shares, [None] * shares
+    for k in reversed(range(1, shares)):
+        mine[k] = in_plane(parts[k], -(k // pair), -(k % pair))
+    for k in reversed(range(shares)):
+        theirs[k] = across(mine[k])
+    base_in = across(hand_on(base_out, pieces[-1][1]))
     return final(mine, theirs, [base_mine, base_in], groups, pair, tokens.dtype)
 
 

time: 69.9 us -> 70.7 us (1.011)
  waiting for transfers between devices: 21.3 us -> 25.1 us
  starting transfers between devices: 20.6 us -> 19.3 us
  local copies, waits for them, and re-layouts: 5.81 us -> 5 us
  Pallas kernels: 21.5 us -> 20.7 us
    ppermute x1, waiting for transfers between devices: 0.01 us -> 3.5 us  [body(): lax.ppermute(packed[pair - w], 'pair', [(a, (a - w) % pair) for a in rang...]
    ppermute x6, starting transfers between devices: 10.2 us -> 7.95 us  [along(): lax.ppermute(x, 'ring', [(a, (a + step) % ring) for a in range(ring)])]
    ppermute x6, starting transfers between devices: 7.04 us -> 8.28 us  [in_plane(): return lax.ppermute(x, PLANE, pairs)]
    unnamed x26 -> x24, local copies, waits for them, and re-layouts: 5.81 us -> 5 us
  transfers between devices with their start and end apart: 18 -> 18, of which waited for: 8 -> 9; matrix products, arithmetic and copies ran while one was open for 0% -> 0% of each run, Pallas kernels for 23% -> 25%
where the time goes in v20:
time: 70.7 us; the launch traced here: 70.2 us
  waiting for transfers between devices  25.1 us (36%)
  Pallas kernels  20.7 us (29%)
  starting transfers between devices  19.3 us (27%)
  local copies, waits for them, and re-layouts  5 us (7%)
    ppermute x6, waiting for transfers between devices, along(): lax.ppermute(x, 'ring', [(a, (a + step) % ring) for a in range(ring)])  14.9 us
    pallas_call x1, Pallas kernels, base_halves(): pl.pallas_call(functools.partial(base_kernel, sides), grid_spec=pltpu.Pre...  11.2 us
    ppermute x6, starting transfers between devices, in_plane(): return lax.ppermute(x, PLANE, pairs)  8.28 us
    ppermute x6, starting transfers between devices, along(): lax.ppermute(x, 'ring', [(a, (a + step) % ring) for a in range(ring)])  7.95 us
    ppermute x6, waiting for transfers between devices, in_plane(): return lax.ppermute(x, PLANE, pairs)  5.34 us
    unnamed x24, local copies, waits for them, and re-layouts  5 us
    pallas_call x1, Pallas kernels, spread(): pl.pallas_call(functools.partial(spread_kernel, groups, pair), in_specs=[...  3.68 us
    ppermute x1, waiting for transfers between devices, body(): lax.ppermute(packed[pair - w], 'pair', [(a, (a - w) % pair) for a in rang...  3.5 us
  transfers between devices with their start and end apart: 18, of which 9 were waited for; matrix products, arithmetic and copies ran while one was open for 0% of the time, Pallas kernels for 25%

profile of v20, /device:TPU:0, one launch (start us, length us, event | category | flops | bytes accessed | tf_op | source)
XLA Modules:
  0.0 70.2 jit_solution(18187004907443511187)
XLA Ops:
  0.0 1.9 %pack.1 = (bf16[2,64,1152]{2,1,0:T(8,128)(2,1)}, bf16[2,64,1152]{2,1,0:T(8,128)(2,1)}) custom-call(bf16[2,64,4096]{2,1,0:T(8,128)(2,1)} %bitcast.2, bf16[2,64,512]{2,1,0:T(8,128)(2,1)} %up.1), custom_call_target="tpu_custom_call" | custom-call | tf_op jit(solution)/shard_map/pack/pallas_call | solution.py:57
  1.9 3.0 %collective-permute-start = (bf16[2,64,1152]{2,1,0:T(8,128)(2,1)}, bf16[2,64,1152]{2,1,0:T(8,128)(2,1)}, u32[]{:S(2)}, u32[]{:S(2)}) collective-permute-start(bf16[2,64,1152]{2,1,0:T(8,128)(2,1)} %get-tuple-element.20), channel_id=1, source_target_pairs={{0,2},{2,0},{1,3},{3,1},{4,6},{6,4},{5,7},{7,5},{8,10},{10,8},{9,1... | collective-permute-start | bytes 884744 | tf_op jit(solution)/shard_map/ppermute | solution.py:327
  4.9 1.6 %collective-permute-start.5 = (bf16[2,64,1152]{2,1,0:T(8,128)(2,1)}, bf16[2,64,1152]{2,1,0:T(8,128)(2,1)S(1)}, u32[]{:S(2)}, u32[]{:S(2)}) collective-permute-start(bf16[2,64,1152]{2,1,0:T(8,128)(2,1)} %get-tuple-element.22.refs_0_), channel_id=1, source_target_pairs={{0,4},{4,8},{8,12},{12,0},{1,5},{5,9},{9,13},{13,1},{2,6},{6,10},{... | collective-permute-start | bytes 884744 | tf_op jit(solution)/shard_map/ppermute | solution.py:300
  6.5 2.2 %collective-permute-start.4 = (bf16[2,64,1152]{2,1,0:T(8,128)(2,1)}, bf16[2,64,1152]{2,1,0:T(8,128)(2,1)S(1)}, u32[]{:S(2)}, u32[]{:S(2)}) collective-permute-start(bf16[2,64,1152]{2,1,0:T(8,128)(2,1)} %get-tuple-element.22.refs_0_), channel_id=1, source_target_pairs={{0,12},{4,0},{8,4},{12,8},{1,13},{5,1},{9,5},{13,9},{2,14},{6,2},{... | collective-permute-start | bytes 884744 | tf_op jit(solution)/shard_map/ppermute | solution.py:300
  8.8 3.5 %collective-permute-done.refs_4_ = bf16[2,64,1152]{2,1,0:T(8,128)(2,1)} collective-permute-done((bf16[2,64,1152]{2,1,0:T(8,128)(2,1)}, bf16[2,64,1152]{2,1,0:T(8,128)(2,1)}, u32[]{:S(2)}, u32[]{:S(2)}) %collective-permute-start) | collective-permute-done | bytes 294944 | tf_op jit(solution)/shard_map/ppermute | solution.py:327
  12.3 1.8 %collective-permute-start.2 = (bf16[2,64,1152]{2,1,0:T(8,128)(2,1)}, bf16[2,64,1152]{2,1,0:T(8,128)(2,1)S(1)}, u32[]{:S(2)}, u32[]{:S(2)}) collective-permute-start(bf16[2,64,1152]{2,1,0:T(8,128)(2,1)} %collective-permute-done.refs_4_), channel_id=1, source_target_pairs={{0,4},{4,8},{8,12},{12,0},{1,5},{5,9},{9,13},{13,1},{2,6},{6,10},{... | collective-permute-start | bytes 884744 | tf_op jit(solution)/shard_map/ppermute | solution.py:300
  14.1 2.0 %collective-permute-start.1 = (bf16[2,64,1152]{2,1,0:T(8,128)(2,1)}, bf16[2,64,1152]{2,1,0:T(8,128)(2,1)S(1)}, u32[]{:S(2)}, u32[]{:S(2)}) collective-permute-start(bf16[2,64,1152]{2,1,0:T(8,128)(2,1)} %collective-permute-done.refs_4_), channel_id=1, source_target_pairs={{0,12},{4,0},{8,4},{12,8},{1,13},{5,1},{9,5},{13,9},{2,14},{6,2},{... | collective-permute-start | bytes 884744 | tf_op jit(solution)/shard_map/ppermute | solution.py:300
  16.1 3.7 %spread.1 = (bf16[400,1024]{1,0:T(8,128)(2,1)}, bf16[400,1024]{1,0:T(8,128)(2,1)}, bf16[400,1024]{1,0:T(8,128)(2,1)}, bf16[400,1024]{1,0:T(8,128)(2,1)}) custom-call(s32[3]{0:T(128)} %lengths.3, s32[3]{0:T(128)} %bitcast.3, bf16[384,4096]{1,0:T(8,128)(2,1)} %tok.1), custom_call_target="tpu_custom_call" | custom-call | tf_op jit(solution)/shard_map/spread/pallas_call | solution.py:119
  19.8 1.8 %collective-permute-start.8 = (bf16[400,1024]{1,0:T(8,128)(2,1)}, bf16[400,1024]{1,0:T(8,128)(2,1)S(1)}, u32[]{:S(2)}, u32[]{:S(2)}) collective-permute-start(bf16[400,1024]{1,0:T(8,128)(2,1)} %get-tuple-element.24), channel_id=1, source_target_pairs={{0,2},{2,0},{16,18},{18,16},{1,3},{3,1},{17,19},{19,17},{4,6},{6,4... | collective-permute-start | bytes 2457608 | tf_op jit(solution)/shard_map/ppermute | solution.py:310
  21.6 0.0 collective-permute-done.5.refs_0_
  21.6 1.5 %collective-permute-start.9 = (bf16[400,1024]{1,0:T(8,128)(2,1)}, bf16[400,1024]{1,0:T(8,128)(2,1)S(1)}, u32[]{:S(2)}, u32[]{:S(2)}) collective-permute-start(bf16[400,1024]{1,0:T(8,128)(2,1)} %get-tuple-element.25), channel_id=1, source_target_pairs={{0,16},{2,18},{16,0},{18,2},{1,17},{3,19},{17,1},{19,3},{4,20},{6,... | collective-permute-start | bytes 2457608 | tf_op jit(solution)/shard_map/ppermute | solution.py:310
  23.1 0.5 collective-permute-done.4.refs_1_
  23.6 1.4 %collective-permute-start.10 = (bf16[400,1024]{1,0:T(8,128)(2,1)}, bf16[400,1024]{1,0:T(8,128)(2,1)S(1)}, u32[]{:S(2)}, u32[]{:S(2)}) collective-permute-start(bf16[400,1024]{1,0:T(8,128)(2,1)} %get-tuple-element.26), channel_id=1, source_target_pairs={{0,18},{2,16},{16,2},{18,0},{1,19},{3,17},{17,3},{19,1},{4,22},{6,... | collective-permute-start | bytes 2457608 | tf_op jit(solution)/shard_map/ppermute | solution.py:310
  25.0 11.2 %base.1 = (f32[384,512]{1,0:T(8,128)}, f32[384,512]{1,0:T(8,128)}, f32[8,128]{1,0:T(8,128)}) custom-call(s32[3]{0:T(128)} %lengths.3, bf16[384,4096]{1,0:T(8,128)(2,1)} %tok.1, bf16[4096,1024]{1,0:T(8,128)(2,1)} %key_ref.1), custom_call_target="tpu_custom_call" | custom-call | tf_op jit(solution)/shard_map/base/pallas_call | solution.py:167
  36.3 0.0 collective-permute-done.2.refs_1_.refs_7_
  36.3 0.3 collective-permute-start.6
  36.6 0.0 collective-permute-done.1.refs_0_
  36.6 0.4 copy-done.4
  37.0 0.7 %copy-done = bf16[2,64,1152]{2,1,0:T(8,128)(2,1)} copy-done((bf16[2,64,1152]{2,1,0:T(8,128)(2,1)}, bf16[2,64,1152]{2,1,0:T(8,128)(2,1)S(1)}, u32[]{:S(2)}) %copy-start) | copy-done | bytes 294936
  37.8 0.0 collective-permute-start.3
  37.8 7.5 %collective-permute-done.6.refs_2_ = bf16[2,64,1152]{2,1,0:T(8,128)(2,1)} collective-permute-done((bf16[2,64,1152]{2,1,0:T(8,128)(2,1)}, bf16[2,64,1152]{2,1,0:T(8,128)(2,1)}, u32[]{:S(2)}, u32[]{:S(2)}) %collective-permute-start.6) | collective-permute-done | bytes 294944 | tf_op jit(solution)/shard_map/ppermute | solution.py:300
  45.2 0.0 collective-permute-start.7
  45.2 6.9 %collective-permute-done.7.refs_6_ = bf16[2,64,1152]{2,1,0:T(8,128)(2,1)S(1)} collective-permute-done((bf16[2,64,1152]{2,1,0:T(8,128)(2,1)}, bf16[2,64,1152]{2,1,0:T(8,128)(2,1)S(1)}, u32[]{:S(2)}, u32[]{:S(2)}) %collective-permute-start.7) | collective-permute-done | bytes 294944 | tf_op jit(solution)/shard_map/ppermute | solution.py:300
  52.2 1.0 %copy-done.1 = bf16[2,64,1152]{2,1,0:T(8,128)(2,1)S(1)} copy-done((bf16[2,64,1152]{2,1,0:T(8,128)(2,1)S(1)}, bf16[2,64,1152]{2,1,0:T(8,128)(2,1)}, u32[]{:S(2)}) %copy-start.1) | copy-done | bytes 294936
  53.1 1.0 %copy-done.5 = bf16[2,64,1152]{2,1,0:T(8,128)(2,1)S(1)} copy-done((bf16[2,64,1152]{2,1,0:T(8,128)(2,1)S(1)}, bf16[2,64,1152]{2,1,0:T(8,128)(2,1)}, u32[]{:S(2)}) %copy-start.5) | copy-done | bytes 294936
  54.1 1.0 %copy-done.7 = bf16[2,64,1152]{2,1,0:T(8,128)(2,1)S(1)} copy-done((bf16[2,64,1152]{2,1,0:T(8,128)(2,1)S(1)}, bf16[2,64,1152]{2,1,0:T(8,128)(2,1)}, u32[]{:S(2)}) %copy-start.7) | copy-done | bytes 294936
  55.1 1.0 %copy-done.10 = bf16[2,64,1152]{2,1,0:T(8,128)(2,1)S(1)} copy-done((bf16[2,64,1152]{2,1,0:T(8,128)(2,1)S(1)}, bf16[2,64,1152]{2,1,0:T(8,128)(2,1)}, u32[]{:S(2)}) %copy-start.10) | copy-done | bytes 294936
  56.0 1.3 %collect.1.held = bf16[16,64,1152]{2,1,0:T(8,128)(2,1)S(1)} custom-call(bf16[2,64,1152]{2,1,0:T(8,128)(2,1)S(1)} %copy-done.10, bf16[2,64,1152]{2,1,0:T(8,128)(2,1)S(1)} %copy-done.3, bf16[2,64,1152]{2,1,0:T(8,128)(2,1)} %collective-permute-done.6.refs_2_, bf16[2,64,1152]{2,1,0:T(8,128)(2,1)S(1)} %copy-done.7, ...), custom_call_target="tpu_custom_call" | custom-call | tf_op jit(solution)/shard_map/collect/pallas_call | solution.py:201
  57.3 0.0 collective-permute-done.8.refs_1_
  57.3 0.0 collective-permute-done.9.refs_2_
  57.3 0.3 collective-permute-done.10.refs_3_
  57.7 1.6 %rank.1 = (bf16[3,128,128]{2,1,0:T(8,128)(2,1)S(1)}, bf16[3,128,128]{2,1,0:T(8,128)(2,1)S(1)}, bf16[3,128,128]{2,1,0:T(8,128)(2,1)S(1)}, bf16[3,128,128]{2,1,0:T(8,128)(2,1)S(1)}) custom-call(s32[16]{0:T(128)S(1)} %copy-done.11, bf16[16,64,1152]{2,1,0:T(8,128)(2,1)S(1)} %collect.1.held, bf16[400,1024]{1,0:T(8,128)(2,1)S(1)} %copy-done.8, ...), custom_call_target="tpu_custom_call" | custom-call | tf_op jit(solution)/shard_map/rank/pallas_call | solution.py:245
  59.3 1.5 %collective-permute-start.11 = (bf16[3,128,128]{2,1,0:T(8,128)(2,1)S(1)}, bf16[3,128,128]{2,1,0:T(8,128)(2,1)S(1)}, u32[]{:S(2)}, u32[]{:S(2)}) collective-permute-start(bf16[3,128,128]{2,1,0:T(8,128)(2,1)S(1)} %get-tuple-element.28), channel_id=1, source_target_pairs={{0,2},{2,0},{16,18},{18,16},{1,3},{3,1},{17,19},{19,17},{4,6},{6,4... | collective-permute-start | bytes 294920 | tf_op jit(solution)/shard_map/ppermute | solution.py:310
  60.9 1.5 %collective-permute-start.12 = (bf16[3,128,128]{2,1,0:T(8,128)(2,1)S(1)}, bf16[3,128,128]{2,1,0:T(8,128)(2,1)S(1)}, u32[]{:S(2)}, u32[]{:S(2)}) collective-permute-start(bf16[3,128,128]{2,1,0:T(8,128)(2,1)S(1)} %get-tuple-element.29), channel_id=1, source_target_pairs={{0,16},{2,18},{16,0},{18,2},{1,17},{3,19},{17,1},{19,3},{4,20},{6,... | collective-permute-start | bytes 294920 | tf_op jit(solution)/shard_map/ppermute | solution.py:310
  62.4 0.5 collective-permute-start.13
  62.9 0.0 collective-permute-start.14
  62.9 1.8 %collective-permute-done.11.refs_1_ = bf16[3,128,128]{2,1,0:T(8,128)(2,1)S(1)} collective-permute-done((bf16[3,128,128]{2,1,0:T(8,128)(2,1)S(1)}, bf16[3,128,128]{2,1,0:T(8,128)(2,1)S(1)}, u32[]{:S(2)}, u32[]{:S(2)}) %collective-permute-start.11) | collective-permute-done | bytes 98336 | tf_op jit(solution)/shard_map/ppermute | solution.py:310
  64.7 0.0 collective-permute-start.15
  64.7 0.8 %collective-permute-done.12.refs_2_ = bf16[3,128,128]{2,1,0:T(8,128)(2,1)S(1)} collective-permute-done((bf16[3,128,128]{2,1,0:T(8,128)(2,1)S(1)}, bf16[3,128,128]{2,1,0:T(8,128)(2,1)S(1)}, u32[]{:S(2)}, u32[]{:S(2)}) %collective-permute-start.12) | collective-permute-done | bytes 98336 | tf_op jit(solution)/shard_map/ppermute | solution.py:310
  65.5 0.0 collective-permute-start.16
  65.5 2.4 %collective-permute-done.13.refs_3_ = bf16[3,128,128]{2,1,0:T(8,128)(2,1)S(1)} collective-permute-done((bf16[3,128,128]{2,1,0:T(8,128)(2,1)S(1)}, bf16[3,128,128]{2,1,0:T(8,128)(2,1)S(1)}, u32[]{:S(2)}, u32[]{:S(2)}) %collective-permute-start.13) | collective-permute-done | bytes 98336 | tf_op jit(solution)/shard_map/ppermute | solution.py:310
  67.9 0.0 collective-permute-start.17
  67.9 0.0 collective-permute-done.14.refs_4_
  67.9 0.0 collective-permute-done.15.refs_5_
  67.9 0.0 collective-permute-done.16.refs_6_
  67.9 1.3 %collective-permute-done.17.refs_7_ = bf16[3,128,128]{2,1,0:T(8,128)(2,1)S(1)} collective-permute-done((bf16[3,128,128]{2,1,0:T(8,128)(2,1)S(1)}, bf16[3,128,128]{2,1,0:T(8,128)(2,1)S(1)}, u32[]{:S(2)}, u32[]{:S(2)}) %collective-permute-start.17) | collective-permute-done | bytes 98336 | tf_op jit(solution)/shard_map/ppermute | solution.py:297
  69.2 0.0 collective-permute-done.3.base_b
  69.2 1.0 %final.1 = bf16[384,512]{1,0:T(8,128)(2,1)} custom-call(f32[384,512]{1,0:T(8,128)S(1)} %copy-done.9, f32[384,512]{1,0:T(8,128)S(1)} %collective-permute-done.3.base_b, bf16[3,128,128]{2,1,0:T(8,128)(2,1)S(1)} %get-tuple-element.27.refs_0_, bf16[3,128,128]{2,1,0:T(8,128)(2,1)S(1)} %collective-permute-done.11.refs_1_, ...), custom_call_target="tpu_custom_call" | custom-call | tf_op jit(solution)/shard_map/final/pallas_call | solution.py:278
  (21 shorter events, 0.0 us)
Async XLA Ops:
  1.9 10.4 %collective-permute-start = (bf16[2,64,1152]{2,1,0:T(8,128)(2,1)}, bf16[2,64,1152]{2,1,0:T(8,128)(2,1)}, u32[]{:S(2)}, u32[]{:S(2)}) collective-permute-start(bf16[2,64,1152]{2,1,0:T(8,128)(2,1)} %get-tuple-element.20), channel_id=1, source_target_pairs={{0,2},{2,0},{1,3},{3,1},{4,6},{6,4},{5,7},{7,5},{8,10},{10,8},{9,1... | collective-permute-start | bytes 884744 | tf_op jit(solution)/shard_map/ppermute | solution.py:327
  4.9 16.6 %collective-permute-start.5 = (bf16[2,64,1152]{2,1,0:T(8,128)(2,1)}, bf16[2,64,1152]{2,1,0:T(8,128)(2,1)S(1)}, u32[]{:S(2)}, u32[]{:S(2)}) collective-permute-start(bf16[2,64,1152]{2,1,0:T(8,128)(2,1)} %get-tuple-element.22.refs_0_), channel_id=1, source_target_pairs={{0,4},{4,8},{8,12},{12,0},{1,5},{5,9},{9,13},{13,1},{2,6},{6,10},{... | collective-permute-start | bytes 884744 | tf_op jit(solution)/shard_map/ppermute | solution.py:300
  6.5 17.1 %collective-permute-start.4 = (bf16[2,64,1152]{2,1,0:T(8,128)(2,1)}, bf16[2,64,1152]{2,1,0:T(8,128)(2,1)S(1)}, u32[]{:S(2)}, u32[]{:S(2)}) collective-permute-start(bf16[2,64,1152]{2,1,0:T(8,128)(2,1)} %get-tuple-element.22.refs_0_), channel_id=1, source_target_pairs={{0,12},{4,0},{8,4},{12,8},{1,13},{5,1},{9,5},{13,9},{2,14},{6,2},{... | collective-permute-start | bytes 884744 | tf_op jit(solution)/shard_map/ppermute | solution.py:300
  12.3 24.1 %collective-permute-start.2 = (bf16[2,64,1152]{2,1,0:T(8,128)(2,1)}, bf16[2,64,1152]{2,1,0:T(8,128)(2,1)S(1)}, u32[]{:S(2)}, u32[]{:S(2)}) collective-permute-start(bf16[2,64,1152]{2,1,0:T(8,128)(2,1)} %collective-permute-done.refs_4_), channel_id=1, source_target_pairs={{0,4},{4,8},{8,12},{12,0},{1,5},{5,9},{9,13},{13,1},{2,6},{6,10},{... | collective-permute-start | bytes 884744 | tf_op jit(solution)/shard_map/ppermute | solution.py:300
  14.1 22.6 %collective-permute-start.1 = (bf16[2,64,1152]{2,1,0:T(8,128)(2,1)}, bf16[2,64,1152]{2,1,0:T(8,128)(2,1)S(1)}, u32[]{:S(2)}, u32[]{:S(2)}) collective-permute-start(bf16[2,64,1152]{2,1,0:T(8,128)(2,1)} %collective-permute-done.refs_4_), channel_id=1, source_target_pairs={{0,12},{4,0},{8,4},{12,8},{1,13},{5,1},{9,5},{13,9},{2,14},{6,2},{... | collective-permute-start | bytes 884744 | tf_op jit(solution)/shard_map/ppermute | solution.py:300
  19.8 37.5 %collective-permute-start.8 = (bf16[400,1024]{1,0:T(8,128)(2,1)}, bf16[400,1024]{1,0:T(8,128)(2,1)S(1)}, u32[]{:S(2)}, u32[]{:S(2)}) collective-permute-start(bf16[400,1024]{1,0:T(8,128)(2,1)} %get-tuple-element.24), channel_id=1, source_target_pairs={{0,2},{2,0},{16,18},{18,16},{1,3},{3,1},{17,19},{19,17},{4,6},{6,4... | collective-permute-start | bytes 2457608 | tf_op jit(solution)/shard_map/ppermute | solution.py:310
  21.6 14.7 %copy-start.6 = (bf16[2,64,1152]{2,1,0:T(8,128)(2,1)}, bf16[2,64,1152]{2,1,0:T(8,128)(2,1)S(1)}, u32[]{:S(2)}) copy-start(bf16[2,64,1152]{2,1,0:T(8,128)(2,1)S(1)} %collective-permute-done.5.refs_0_) | copy-start | bytes 884740
  21.6 35.7 %collective-permute-start.9 = (bf16[400,1024]{1,0:T(8,128)(2,1)}, bf16[400,1024]{1,0:T(8,128)(2,1)S(1)}, u32[]{:S(2)}, u32[]{:S(2)}) collective-permute-start(bf16[400,1024]{1,0:T(8,128)(2,1)} %get-tuple-element.25), channel_id=1, source_target_pairs={{0,16},{2,18},{16,0},{18,2},{1,17},{3,19},{17,1},{19,3},{4,20},{6,... | collective-permute-start | bytes 2457608 | tf_op jit(solution)/shard_map/ppermute | solution.py:310
  23.6 12.7 %copy-start.2 = (bf16[2,64,1152]{2,1,0:T(8,128)(2,1)}, bf16[2,64,1152]{2,1,0:T(8,128)(2,1)S(1)}, u32[]{:S(2)}) copy-start(bf16[2,64,1152]{2,1,0:T(8,128)(2,1)S(1)} %collective-permute-done.4.refs_1_) | copy-start | bytes 884740
  23.6 34.0 %collective-permute-start.10 = (bf16[400,1024]{1,0:T(8,128)(2,1)}, bf16[400,1024]{1,0:T(8,128)(2,1)S(1)}, u32[]{:S(2)}, u32[]{:S(2)}) collective-permute-start(bf16[400,1024]{1,0:T(8,128)(2,1)} %get-tuple-element.26), channel_id=1, source_target_pairs={{0,18},{2,16},{16,2},{18,0},{1,19},{3,17},{17,3},{19,1},{4,22},{6,... | collective-permute-start | bytes 2457608 | tf_op jit(solution)/shard_map/ppermute | solution.py:310
  36.3 15.9 %copy-start.3 = (bf16[2,64,1152]{2,1,0:T(8,128)(2,1)S(1)}, bf16[2,64,1152]{2,1,0:T(8,128)(2,1)}, u32[]{:S(2)}) copy-start(bf16[2,64,1152]{2,1,0:T(8,128)(2,1)} %copy-done.2) | copy-start | bytes 884740
  36.3 0.7 %copy-start.4 = (bf16[2,64,1152]{2,1,0:T(8,128)(2,1)}, bf16[2,64,1152]{2,1,0:T(8,128)(2,1)S(1)}, u32[]{:S(2)}) copy-start(bf16[2,64,1152]{2,1,0:T(8,128)(2,1)S(1)} %collective-permute-done.2.refs_1_.refs_7_) | copy-start | bytes 884740
  36.3 8.9 %collective-permute-start.6 = (bf16[2,64,1152]{2,1,0:T(8,128)(2,1)}, bf16[2,64,1152]{2,1,0:T(8,128)(2,1)}, u32[]{:S(2)}, u32[]{:S(2)}) collective-permute-start(bf16[2,64,1152]{2,1,0:T(8,128)(2,1)} %hand.5.refs_3_), channel_id=1, source_target_pairs={{0,4},{4,8},{8,12},{12,0},{1,5},{5,9},{9,13},{13,1},{2,6},{6,10},{... | collective-permute-start | bytes 884744 | tf_op jit(solution)/shard_map/ppermute | solution.py:300
  37.0 0.7 %copy-start = (bf16[2,64,1152]{2,1,0:T(8,128)(2,1)}, bf16[2,64,1152]{2,1,0:T(8,128)(2,1)S(1)}, u32[]{:S(2)}) copy-start(bf16[2,64,1152]{2,1,0:T(8,128)(2,1)S(1)} %collective-permute-done.1.refs_0_) | copy-start | bytes 884740
  37.8 19.9 %copy-start.8 = (bf16[400,1024]{1,0:T(8,128)(2,1)S(1)}, bf16[400,1024]{1,0:T(8,128)(2,1)}, u32[]{:S(2)}) copy-start(bf16[400,1024]{1,0:T(8,128)(2,1)} %get-tuple-element.23.refs_0_) | copy-start | bytes 2457604
  37.8 19.9 %copy-start.11 = (s32[16]{0:T(128)S(1)}, s32[16]{0:T(128)}, u32[]{:S(2)}) copy-start(s32[16]{0:T(128)} %owner.1) | copy-start | bytes 196
  37.8 31.4 %collective-permute-start.3 = (f32[384,512]{1,0:T(8,128)}, f32[384,512]{1,0:T(8,128)S(1)}, u32[]{:S(2)}, u32[]{:S(2)}) collective-permute-start(f32[384,512]{1,0:T(8,128)} %hand.4), channel_id=1, source_target_pairs={{0,1},{1,0},{2,3},{3,2},{4,5},{5,4},{6,7},{7,6},{8,9},{9,8},{10,11... | collective-permute-start | bytes 2359304 | tf_op jit(solution)/shard_map/ppermute | solution.py:297
  45.2 6.9 %collective-permute-start.7 = (bf16[2,64,1152]{2,1,0:T(8,128)(2,1)}, bf16[2,64,1152]{2,1,0:T(8,128)(2,1)S(1)}, u32[]{:S(2)}, u32[]{:S(2)}) collective-permute-start(bf16[2,64,1152]{2,1,0:T(8,128)(2,1)} %hand.3.refs_1_.refs_5_), channel_id=1, source_target_pairs={{0,12},{4,0},{8,4},{12,8},{1,13},{5,1},{9,5},{13,9},{2,14},{6,2},{... | collective-permute-start | bytes 884744 | tf_op jit(solution)/shard_map/ppermute | solution.py:300
  52.2 1.0 %copy-start.1 = (bf16[2,64,1152]{2,1,0:T(8,128)(2,1)S(1)}, bf16[2,64,1152]{2,1,0:T(8,128)(2,1)}, u32[]{:S(2)}) copy-start(bf16[2,64,1152]{2,1,0:T(8,128)(2,1)} %hand.3.refs_1_.refs_5_) | copy-start | bytes 884740
  53.1 1.0 %copy-start.5 = (bf16[2,64,1152]{2,1,0:T(8,128)(2,1)S(1)}, bf16[2,64,1152]{2,1,0:T(8,128)(2,1)}, u32[]{:S(2)}) copy-start(bf16[2,64,1152]{2,1,0:T(8,128)(2,1)} %copy-done.4) | copy-start | bytes 884740
  54.1 1.0 %copy-start.7 = (bf16[2,64,1152]{2,1,0:T(8,128)(2,1)S(1)}, bf16[2,64,1152]{2,1,0:T(8,128)(2,1)}, u32[]{:S(2)}) copy-start(bf16[2,64,1152]{2,1,0:T(8,128)(2,1)} %hand.5.refs_3_) | copy-start | bytes 884740
  55.1 1.0 %copy-start.10 = (bf16[2,64,1152]{2,1,0:T(8,128)(2,1)S(1)}, bf16[2,64,1152]{2,1,0:T(8,128)(2,1)}, u32[]{:S(2)}) copy-start(bf16[2,64,1152]{2,1,0:T(8,128)(2,1)} %get-tuple-element.22.refs_0_) | copy-start | bytes 884740
  57.3 11.9 %copy-start.9 = (f32[384,512]{1,0:T(8,128)S(1)}, f32[384,512]{1,0:T(8,128)}, u32[]{:S(2)}) copy-start(f32[384,512]{1,0:T(8,128)} %get-tuple-element.18.base_a) | copy-start | bytes 2359300
  59.3 5.3 %collective-permute-start.11 = (bf16[3,128,128]{2,1,0:T(8,128)(2,1)S(1)}, bf16[3,128,128]{2,1,0:T(8,128)(2,1)S(1)}, u32[]{:S(2)}, u32[]{:S(2)}) collective-permute-start(bf16[3,128,128]{2,1,0:T(8,128)(2,1)S(1)} %get-tuple-element.28), channel_id=1, source_target_pairs={{0,2},{2,0},{16,18},{18,16},{1,3},{3,1},{17,19},{19,17},{4,6},{6,4... | collective-permute-start | bytes 294920 | tf_op jit(solution)/shard_map/ppermute | solution.py:310
  60.9 4.6 %collective-permute-start.12 = (bf16[3,128,128]{2,1,0:T(8,128)(2,1)S(1)}, bf16[3,128,128]{2,1,0:T(8,128)(2,1)S(1)}, u32[]{:S(2)}, u32[]{:S(2)}) collective-permute-start(bf16[3,128,128]{2,1,0:T(8,128)(2,1)S(1)} %get-tuple-element.29), channel_id=1, source_target_pairs={{0,16},{2,18},{16,0},{18,2},{1,17},{3,19},{17,1},{19,3},{4,20},{6,... | collective-permute-start | bytes 294920 | tf_op jit(solution)/shard_map/ppermute | solution.py:310
  62.4 5.5 %collective-permute-start.13 = (bf16[3,128,128]{2,1,0:T(8,128)(2,1)S(1)}, bf16[3,128,128]{2,1,0:T(8,128)(2,1)S(1)}, u32[]{:S(2)}, u32[]{:S(2)}) collective-permute-start(bf16[3,128,128]{2,1,0:T(8,128)(2,1)S(1)} %get-tuple-element.30), channel_id=1, source_target_pairs={{0,18},{2,16},{16,2},{18,0},{1,19},{3,17},{17,3},{19,1},{4,22},{6,... | collective-permute-start | bytes 294920 | tf_op jit(solution)/shard_map/ppermute | solution.py:310
  62.9 5.0 %collective-permute-start.14 = (bf16[3,128,128]{2,1,0:T(8,128)(2,1)S(1)}, bf16[3,128,128]{2,1,0:T(8,128)(2,1)S(1)}, u32[]{:S(2)}, u32[]{:S(2)}) collective-permute-start(bf16[3,128,128]{2,1,0:T(8,128)(2,1)S(1)} %get-tuple-element.27.refs_0_), channel_id=1, source_target_pairs={{0,1},{1,0},{2,3},{3,2},{4,5},{5,4},{6,7},{7,6},{8,9},{9,8},{10,11... | collective-permute-start | bytes 294920 | tf_op jit(solution)/shard_map/ppermute | solution.py:297
  64.7 3.2 %collective-permute-start.15 = (bf16[3,128,128]{2,1,0:T(8,128)(2,1)S(1)}, bf16[3,128,128]{2,1,0:T(8,128)(2,1)S(1)}, u32[]{:S(2)}, u32[]{:S(2)}) collective-permute-start(bf16[3,128,128]{2,1,0:T(8,128)(2,1)S(1)} %collective-permute-done.11.refs_1_), channel_id=1, source_target_pairs={{0,1},{1,0},{2,3},{3,2},{4,5},{5,4},{6,7},{7,6},{8,9},{9,8},{10,11... | collective-permute-start | bytes 294920 | tf_op jit(solution)/shard_map/ppermute | solution.py:297
  65.5 2.4 %collective-permute-start.16 = (bf16[3,128,128]{2,1,0:T(8,128)(2,1)S(1)}, bf16[3,128,128]{2,1,0:T(8,128)(2,1)S(1)}, u32[]{:S(2)}, u32[]{:S(2)}) collective-permute-start(bf16[3,128,128]{2,1,0:T(8,128)(2,1)S(1)} %collective-permute-done.12.refs_2_), channel_id=1, source_target_pairs={{0,1},{1,0},{2,3},{3,2},{4,5},{5,4},{6,7},{7,6},{8,9},{9,8},{10,11... | collective-permute-start | bytes 294920 | tf_op jit(solution)/shard_map/ppermute | solution.py:297
  67.9 1.3 %collective-permute-start.17 = (bf16[3,128,128]{2,1,0:T(8,128)(2,1)S(1)}, bf16[3,128,128]{2,1,0:T(8,128)(2,1)S(1)}, u32[]{:S(2)}, u32[]{:S(2)}) collective-permute-start(bf16[3,128,128]{2,1,0:T(8,128)(2,1)S(1)} %collective-permute-done.13.refs_3_), channel_id=1, source_target_pairs={{0,1},{1,0},{2,3},{3,2},{4,5},{5,4},{6,7},{7,6},{8,9},{9,8},{10,11... | collective-permute-start | bytes 294920 | tf_op jit(solution)/shard_map/ppermute | solution.py:297

commit v21 on v19

--- a/solution.py
+++ b/solution.py
@@ -185,7 +185,8 @@
 
 
 def collect_kernel(*refs):
-    sems, held, pieces = refs[-1], refs[-2], refs[:-2]
+    sems, flag, held, pieces = refs[-1], refs[-2], refs[-3], refs[:-3]
+    flag[...] = jnp.zeros_like(flag)
     copies, start = [], 0
     for j, piece in enumerate(pieces):
         copies.append(pltpu.make_async_copy(piece, held.at[pl.ds(start, piece.shape[0])], sems.at[j]))
@@ -201,19 +202,21 @@
     return pl.pallas_call(
         collect_kernel,
         in_specs=[ANY] * len(pieces),
-        out_specs=VMEM,
-        out_shape=jax.ShapeDtypeStruct((count,) + pieces[0].shape[1:], pieces[0].dtype),
+        out_specs=[VMEM] * 2,
+        out_shape=[
+            jax.ShapeDtypeStruct((count,) + pieces[0].shape[1:], pieces[0].dtype),
+            jax.ShapeDtypeStruct((8, LANES), jnp.float32),
+        ],
         scratch_shapes=[pltpu.SemaphoreType.DMA((len(pieces),))],
         compiler_params=ROOM,
         name="collect",
     )(*pieces)
 
 
-def rank_kernel(ring, pair, rows, owner, held, *refs):
-    shares = (len(refs) - 1) // 2
-    toks, outs, flag = refs[:shares], refs[shares:-1], refs[-1]
-    flag[...] = jnp.zeros_like(flag)
-    per, rank = held.shape[0] // (ring * pair), held.shape[1]
+def rank_kernel(ring, pair, rows, shares, owner, held, *refs):
+    late, toks, outs, picked = refs[: -1 - 2 * shares], refs[-1 - 2 * shares : -1 - shares], refs[-1 - shares : -1], refs[-1]
+    rank = held.shape[1]
+    per = owner.shape[0] // (ring * pair)
     blocks, _, block = outs[0].shape
     feats = toks[0].shape[1]
     z, y = lax.axis_index("ring"), lax.axis_index("pair")
@@ -223,35 +226,53 @@
     for tok in toks:
         named = tok[rows:, :LANES].astype(jnp.float32)
         ids += [jnp.sum(jnp.where((lane == b) & (row == 0), named, 0.0)).astype(jnp.int32) for b in range(blocks)]
+    for i, one in enumerate(ids):
+        slot = owner[one]
+        chip = slot // per
+        local = lax.rem(slot, per)
+        away = lax.rem(chip // pair - z + ring, ring)
+        way = lax.rem(lax.rem(chip, pair) - y + pair, pair)
+        if late:
+            half = ring // 2
+            near = away - jnp.where(away > half, 1, 0)
+
+            @pl.when(away != half)
+            def _():
+                picked[i] = held[(way * (ring - 1) + near) * per + local]
+
+            for w in range(pair):
+
+                @pl.when((away == half) & (way == w))
+                def _():
+                    picked[i] = late[w][local]
+
+        else:
+            picked[i] = held[(way * ring + away) * per + local]
     for k, tok in enumerate(toks):
         for b in range(blocks):
-            slot = owner[ids[k * blocks + b]]
-            chip = slot // per
-            away = lax.rem(chip // pair - z + ring, ring)
-            way = lax.rem(lax.rem(chip, pair) - y + pair, pair)
-            at = (way * ring + away) * per + lax.rem(slot, per)
+            i = k * blocks + b
             part = lax.dot_general(
-                held[at, :, :feats],
+                picked[i, :, :feats],
                 tok[b * block : (b + 1) * block, :],
                 (((1,), (1,)), ((), ())),
                 preferred_element_type=jnp.float32,
             )
             outs[k][b, :rank, :] = part.astype(outs[k].dtype)
-            outs[k][b, rank:, :] = held[at, :, feats:]
-
-
-def rank_parts(owner, toks, held, ring, pair, rows, blocks):
+            outs[k][b, rank:, :] = picked[i, :, feats:]
+
+
+def rank_parts(owner, toks, held, late, ring, pair, rows, blocks):
     shares, rank = len(toks), held.shape[1]
     return pl.pallas_call(
-        functools.partial(rank_kernel, ring, pair, rows),
-        in_specs=[SMEM, VMEM] + [VMEM] * shares,
-        out_specs=[VMEM] * (shares + 1),
-        out_shape=[jax.ShapeDtypeStruct((blocks, 2 * rank, rows // blocks), held.dtype)] * shares
-        + [jax.ShapeDtypeStruct((8, LANES), jnp.float32)],
+        functools.partial(rank_kernel, ring, pair, rows, shares),
+        in_specs=[SMEM, VMEM] + [VMEM] * (len(late) + shares),
+        out_specs=[VMEM] * shares,
+        out_shape=[jax.ShapeDtypeStruct((blocks, 2 * rank, rows // blocks), held.dtype)] * shares,
+        scratch_shapes=[pltpu.VMEM((shares * blocks,) + held.shape[1:], held.dtype)],
         cost_estimate=pl.CostEstimate(flops=0, bytes_accessed=0, transcendentals=0),
         compiler_params=ROOM,
         name="rank",
-    )(owner, held, *toks)
+    )(owner, held, *late, *toks)
 
 
 def final_kernel(groups, pair, base_a, base_b, *refs):
@@ -336,8 +357,10 @@
         for way, held in enumerate(firsts)
     ]
 
-    flat = [piece for way in pieces for piece in way]
-    *parts, ready = rank_parts(owner_slot, toks, collect(flat), ring, pair, rows, blocks)
+    halfway = ring // 2 if ring % 2 == 0 else ring
+    held, ready = collect([piece for way in pieces for away, piece in enumerate(way) if away != halfway])
+    late = [way[halfway] for way in pieces] if halfway < ring else []
+    parts = rank_parts(owner_slot, toks, held, late, ring, pair, rows, blocks)
     mine = [parts[0]] + [in_plane(parts[k], -(k // pair), -(k % pair)) for k in range(1, shares)]
     theirs = [across(part) for part in mine]
     base_in = across(hand_on(base_out, ready))

time: 69.9 us -> 72.7 us (1.040)
  local copies, waits for them, and re-layouts: 5.81 us -> 7.57 us
  starting transfers between devices: 20.6 us -> 22 us
    ppermute x6, waiting for transfers between devices: 15.2 us -> 1.18 us  [along(): lax.ppermute(x, 'ring', [(a, (a + step) % ring) for a in range(ring)])]
    ppermute x6, waiting for transfers between devices: 4.72 us -> 14.8 us  [in_plane(): return lax.ppermute(x, PLANE, pairs)]
    ppermute x1, waiting for transfers between devices: 0.01 us -> 3.39 us  [body(): lax.ppermute(packed[pair - w], 'pair', [(a, (a - w) % pair) for a in rang...]
    unnamed x26 -> x32, local copies, waits for them, and re-layouts: 5.81 us -> 7.57 us
    ppermute x6, starting transfers between devices: 7.04 us -> 8.31 us  [in_plane(): return lax.ppermute(x, PLANE, pairs)]
  transfers between devices with their start and end apart: 18 -> 18, of which waited for: 8 -> 8; matrix products, arithmetic and copies ran while one was open for 0% -> 0% of each run, Pallas kernels for 23% -> 26%
where the time goes in v21:
time: 72.7 us; the launch traced here: 72.1 us
  starting transfers between devices  22 us (30%)
  Pallas kernels  21.8 us (30%)
  waiting for transfers between devices  20.6 us (28%)
  local copies, waits for them, and re-layouts  7.57 us (10%)
    ppermute x6, waiting for transfers between devices, in_plane(): return lax.ppermute(x, PLANE, pairs)  14.8 us
    pallas_call x1, Pallas kernels, base_halves(): pl.pallas_call(functools.partial(base_kernel, sides), grid_spec=pltpu.Pre...  11.2 us
    ppermute x6, starting transfers between devices, along(): lax.ppermute(x, 'ring', [(a, (a + step) % ring) for a in range(ring)])  10.7 us
    ppermute x6, starting transfers between devices, in_plane(): return lax.ppermute(x, PLANE, pairs)  8.31 us
    unnamed x32, local copies, waits for them, and re-layouts  7.57 us
    pallas_call x1, Pallas kernels, spread(): pl.pallas_call(functools.partial(spread_kernel, groups, pair), in_specs=[...  3.63 us
    pallas_call x1, Pallas kernels, rank_parts(): pl.pallas_call(functools.partial(rank_kernel, ring, pair, rows, shares),...  3.54 us
    ppermute x1, waiting for transfers between devices, body(): lax.ppermute(packed[pair - w], 'pair', [(a, (a - w) % pair) for a in rang...  3.39 us
  transfers between devices with their start and end apart: 18, of which 8 were waited for; matrix products, arithmetic and copies ran while one was open for 0% of the time, Pallas kernels for 26%

profile of v21, /device:TPU:0, one launch (start us, length us, event | category | flops | bytes accessed | tf_op | source)
XLA Modules:
  0.0 72.1 jit_solution(4387741227561876551)
XLA Ops:
  0.0 1.9 %pack.1 = (bf16[2,64,1152]{2,1,0:T(8,128)(2,1)}, bf16[2,64,1152]{2,1,0:T(8,128)(2,1)}) custom-call(bf16[2,64,4096]{2,1,0:T(8,128)(2,1)} %bitcast.2, bf16[2,64,512]{2,1,0:T(8,128)(2,1)} %up.1), custom_call_target="tpu_custom_call" | custom-call | tf_op jit(solution)/shard_map/pack/pallas_call | solution.py:57
  1.9 3.0 %collective-permute-start.2 = (bf16[2,64,1152]{2,1,0:T(8,128)(2,1)}, bf16[2,64,1152]{2,1,0:T(8,128)(2,1)S(1)}, u32[]{:S(2)}, u32[]{:S(2)}) collective-permute-start(bf16[2,64,1152]{2,1,0:T(8,128)(2,1)} %get-tuple-element.24), channel_id=1, source_target_pairs={{0,2},{2,0},{1,3},{3,1},{4,6},{6,4},{5,7},{7,5},{8,10},{10,8},{9,1... | collective-permute-start | bytes 884744 | tf_op jit(solution)/shard_map/ppermute | solution.py:349
  4.9 1.6 %collective-permute-start.1 = (bf16[2,64,1152]{2,1,0:T(8,128)(2,1)}, bf16[2,64,1152]{2,1,0:T(8,128)(2,1)S(1)}, u32[]{:S(2)}, u32[]{:S(2)}) collective-permute-start(bf16[2,64,1152]{2,1,0:T(8,128)(2,1)} %get-tuple-element.22.refs_0_), channel_id=1, source_target_pairs={{0,4},{4,8},{8,12},{12,0},{1,5},{5,9},{9,13},{13,1},{2,6},{6,10},{... | collective-permute-start | bytes 884744 | tf_op jit(solution)/shard_map/ppermute | solution.py:322
  6.5 2.2 %collective-permute-start = (bf16[2,64,1152]{2,1,0:T(8,128)(2,1)}, bf16[2,64,1152]{2,1,0:T(8,128)(2,1)S(1)}, u32[]{:S(2)}, u32[]{:S(2)}) collective-permute-start(bf16[2,64,1152]{2,1,0:T(8,128)(2,1)} %get-tuple-element.22.refs_0_), channel_id=1, source_target_pairs={{0,12},{4,0},{8,4},{12,8},{1,13},{5,1},{9,5},{13,9},{2,14},{6,2},{... | collective-permute-start | bytes 884744 | tf_op jit(solution)/shard_map/ppermute | solution.py:322
  8.8 3.4 %collective-permute-done.2.refs_3_ = bf16[2,64,1152]{2,1,0:T(8,128)(2,1)S(1)} collective-permute-done((bf16[2,64,1152]{2,1,0:T(8,128)(2,1)}, bf16[2,64,1152]{2,1,0:T(8,128)(2,1)S(1)}, u32[]{:S(2)}, u32[]{:S(2)}) %collective-permute-start.2) | collective-permute-done | bytes 294944 | tf_op jit(solution)/shard_map/ppermute | solution.py:349
  12.2 1.8 %collective-permute-start.4 = (bf16[2,64,1152]{2,1,0:T(8,128)(2,1)S(1)}, bf16[2,64,1152]{2,1,0:T(8,128)(2,1)S(1)}, u32[]{:S(2)}, u32[]{:S(2)}) collective-permute-start(bf16[2,64,1152]{2,1,0:T(8,128)(2,1)S(1)} %collective-permute-done.2.refs_3_), channel_id=1, source_target_pairs={{0,4},{4,8},{8,12},{12,0},{1,5},{5,9},{9,13},{13,1},{2,6},{6,10},{... | collective-permute-start | bytes 884744 | tf_op jit(solution)/shard_map/ppermute | solution.py:322
  14.0 2.0 %collective-permute-start.3 = (bf16[2,64,1152]{2,1,0:T(8,128)(2,1)S(1)}, bf16[2,64,1152]{2,1,0:T(8,128)(2,1)S(1)}, u32[]{:S(2)}, u32[]{:S(2)}) collective-permute-start(bf16[2,64,1152]{2,1,0:T(8,128)(2,1)S(1)} %collective-permute-done.2.refs_3_), channel_id=1, source_target_pairs={{0,12},{4,0},{8,4},{12,8},{1,13},{5,1},{9,5},{13,9},{2,14},{6,2},{... | collective-permute-start | bytes 884744 | tf_op jit(solution)/shard_map/ppermute | solution.py:322
  16.0 3.6 %spread.1 = (bf16[400,1024]{1,0:T(8,128)(2,1)}, bf16[400,1024]{1,0:T(8,128)(2,1)}, bf16[400,1024]{1,0:T(8,128)(2,1)}, bf16[400,1024]{1,0:T(8,128)(2,1)}) custom-call(s32[3]{0:T(128)} %lengths.3, s32[3]{0:T(128)} %bitcast.3, bf16[384,4096]{1,0:T(8,128)(2,1)} %tok.1), custom_call_target="tpu_custom_call" | custom-call | tf_op jit(solution)/shard_map/spread/pallas_call | solution.py:119
  19.6 1.8 %collective-permute-start.8 = (bf16[400,1024]{1,0:T(8,128)(2,1)}, bf16[400,1024]{1,0:T(8,128)(2,1)}, u32[]{:S(2)}, u32[]{:S(2)}) collective-permute-start(bf16[400,1024]{1,0:T(8,128)(2,1)} %get-tuple-element.28), channel_id=1, source_target_pairs={{0,2},{2,0},{16,18},{18,16},{1,3},{3,1},{17,19},{19,17},{4,6},{6,4... | collective-permute-start | bytes 2457608 | tf_op jit(solution)/shard_map/ppermute | solution.py:332
  21.5 0.0 collective-permute-done.1.refs_0_
  21.5 1.5 %collective-permute-start.9 = (bf16[400,1024]{1,0:T(8,128)(2,1)}, bf16[400,1024]{1,0:T(8,128)(2,1)}, u32[]{:S(2)}, u32[]{:S(2)}) collective-permute-start(bf16[400,1024]{1,0:T(8,128)(2,1)} %get-tuple-element.29), channel_id=1, source_target_pairs={{0,16},{2,18},{16,0},{18,2},{1,17},{3,19},{17,1},{19,3},{4,20},{6,... | collective-permute-start | bytes 2457608 | tf_op jit(solution)/shard_map/ppermute | solution.py:332
  23.0 0.7 collective-permute-done.refs_1_
  23.6 1.4 %collective-permute-start.10 = (bf16[400,1024]{1,0:T(8,128)(2,1)}, bf16[400,1024]{1,0:T(8,128)(2,1)}, u32[]{:S(2)}, u32[]{:S(2)}) collective-permute-start(bf16[400,1024]{1,0:T(8,128)(2,1)} %get-tuple-element.30), channel_id=1, source_target_pairs={{0,18},{2,16},{16,2},{18,0},{1,19},{3,17},{17,3},{19,1},{4,22},{6,... | collective-permute-start | bytes 2457608 | tf_op jit(solution)/shard_map/ppermute | solution.py:332
  25.1 11.2 %base.1 = (f32[384,512]{1,0:T(8,128)}, f32[384,512]{1,0:T(8,128)}, f32[8,128]{1,0:T(8,128)}) custom-call(s32[3]{0:T(128)} %lengths.3, bf16[384,4096]{1,0:T(8,128)(2,1)} %tok.1, bf16[4096,1024]{1,0:T(8,128)(2,1)} %key_ref.1), custom_call_target="tpu_custom_call" | custom-call | tf_op jit(solution)/shard_map/base/pallas_call | solution.py:167
  36.3 0.0 copy-start.15
  36.3 0.0 collective-permute-done.4.refs_1_.refs_5_
  36.4 0.3 collective-permute-start.6
  36.7 0.0 collective-permute-done.3.refs_0_
  36.7 0.4 copy-done.2
  37.1 0.7 %copy-done.6 = bf16[2,64,1152]{2,1,0:T(8,128)(2,1)} copy-done((bf16[2,64,1152]{2,1,0:T(8,128)(2,1)}, bf16[2,64,1152]{2,1,0:T(8,128)(2,1)S(1)}, u32[]{:S(2)}) %copy-start.6) | copy-done | bytes 294936
  37.9 1.0 %copy-done.1 = bf16[2,64,1152]{2,1,0:T(8,128)(2,1)S(1)} copy-done((bf16[2,64,1152]{2,1,0:T(8,128)(2,1)S(1)}, bf16[2,64,1152]{2,1,0:T(8,128)(2,1)}, u32[]{:S(2)}) %copy-start.1) | copy-done | bytes 294936
  38.8 1.0 %copy-done.3 = bf16[2,64,1152]{2,1,0:T(8,128)(2,1)S(1)} copy-done((bf16[2,64,1152]{2,1,0:T(8,128)(2,1)S(1)}, bf16[2,64,1152]{2,1,0:T(8,128)(2,1)}, u32[]{:S(2)}) %copy-start.3) | copy-done | bytes 294936
  39.8 1.0 %copy-done.5 = bf16[2,64,1152]{2,1,0:T(8,128)(2,1)S(1)} copy-done((bf16[2,64,1152]{2,1,0:T(8,128)(2,1)S(1)}, bf16[2,64,1152]{2,1,0:T(8,128)(2,1)}, u32[]{:S(2)}) %copy-start.5) | copy-done | bytes 294936
  40.7 1.0 %copy-done.7 = bf16[2,64,1152]{2,1,0:T(8,128)(2,1)S(1)} copy-done((bf16[2,64,1152]{2,1,0:T(8,128)(2,1)S(1)}, bf16[2,64,1152]{2,1,0:T(8,128)(2,1)}, u32[]{:S(2)}) %copy-start.7) | copy-done | bytes 294936
  41.7 1.0 %copy-done.11 = bf16[2,64,1152]{2,1,0:T(8,128)(2,1)S(1)} copy-done((bf16[2,64,1152]{2,1,0:T(8,128)(2,1)S(1)}, bf16[2,64,1152]{2,1,0:T(8,128)(2,1)}, u32[]{:S(2)}) %copy-start.11) | copy-done | bytes 294936
  42.7 1.0 %copy-done.13 = bf16[2,64,1152]{2,1,0:T(8,128)(2,1)S(1)} copy-done((bf16[2,64,1152]{2,1,0:T(8,128)(2,1)S(1)}, bf16[2,64,1152]{2,1,0:T(8,128)(2,1)}, u32[]{:S(2)}) %copy-start.13) | copy-done | bytes 294936
  43.6 0.4 collect.1
  44.1 0.0 copy-start.14
  44.1 0.6 copy-done.14
  44.7 0.5 collective-permute-done.6.refs_0_
  45.2 2.7 %collective-permute-start.7 = (bf16[2,64,1152]{2,1,0:T(8,128)(2,1)S(1)}, bf16[2,64,1152]{2,1,0:T(8,128)(2,1)S(1)}, u32[]{:S(2)}, u32[]{:S(2)}) collective-permute-start(bf16[2,64,1152]{2,1,0:T(8,128)(2,1)S(1)} %copy-done.8), channel_id=1, source_target_pairs={{0,12},{4,0},{8,4},{12,8},{1,13},{5,1},{9,5},{13,9},{2,14},{6,2},{... | collective-permute-start | bytes 884744 | tf_op jit(solution)/shard_map/ppermute | solution.py:322
  47.9 0.0 collective-permute-done.8.refs_3_
  47.9 9.7 %collective-permute-done.10.refs_5_ = bf16[400,1024]{1,0:T(8,128)(2,1)} collective-permute-done((bf16[400,1024]{1,0:T(8,128)(2,1)}, bf16[400,1024]{1,0:T(8,128)(2,1)}, u32[]{:S(2)}, u32[]{:S(2)}) %collective-permute-start.10) | collective-permute-done | bytes 819232 | tf_op jit(solution)/shard_map/ppermute | solution.py:332
  57.6 0.0 collective-permute-done.7.refs_1_
  57.6 3.5 %rank.1 = (bf16[3,128,128]{2,1,0:T(8,128)(2,1)S(1)}, bf16[3,128,128]{2,1,0:T(8,128)(2,1)S(1)}, bf16[3,128,128]{2,1,0:T(8,128)(2,1)S(1)}, bf16[3,128,128]{2,1,0:T(8,128)(2,1)S(1)}) custom-call(s32[16]{0:T(128)S(1)} %copy-done.15, bf16[12,64,1152]{2,1,0:T(8,128)(2,1)S(1)} %get-tuple-element.26.held, bf16[2,64,1152]{2,1,0:T(8,128)(2,1)S(1)} %collective-permute-done.6.refs_0_, ...), custom_call_target="tpu_custom_call" | custom-call | tf_op jit(solution)/shard_map/rank/pallas_call | solution.py:266
  61.2 1.6 %collective-permute-start.11 = (bf16[3,128,128]{2,1,0:T(8,128)(2,1)S(1)}, bf16[3,128,128]{2,1,0:T(8,128)(2,1)S(1)}, u32[]{:S(2)}, u32[]{:S(2)}) collective-permute-start(bf16[3,128,128]{2,1,0:T(8,128)(2,1)S(1)} %get-tuple-element.32), channel_id=1, source_target_pairs={{0,2},{2,0},{16,18},{18,16},{1,3},{3,1},{17,19},{19,17},{4,6},{6,4... | collective-permute-start | bytes 294920 | tf_op jit(solution)/shard_map/ppermute | solution.py:332
  62.8 1.5 %collective-permute-start.12 = (bf16[3,128,128]{2,1,0:T(8,128)(2,1)S(1)}, bf16[3,128,128]{2,1,0:T(8,128)(2,1)S(1)}, u32[]{:S(2)}, u32[]{:S(2)}) collective-permute-start(bf16[3,128,128]{2,1,0:T(8,128)(2,1)S(1)} %get-tuple-element.33), channel_id=1, source_target_pairs={{0,16},{2,18},{16,0},{18,2},{1,17},{3,19},{17,1},{19,3},{4,20},{6,... | collective-permute-start | bytes 294920 | tf_op jit(solution)/shard_map/ppermute | solution.py:332
  64.2 0.5 collective-permute-start.13
  64.7 0.0 collective-permute-start.14
  64.7 1.8 %collective-permute-done.11.refs_1_ = bf16[3,128,128]{2,1,0:T(8,128)(2,1)S(1)} collective-permute-done((bf16[3,128,128]{2,1,0:T(8,128)(2,1)S(1)}, bf16[3,128,128]{2,1,0:T(8,128)(2,1)S(1)}, u32[]{:S(2)}, u32[]{:S(2)}) %collective-permute-start.11) | collective-permute-done | bytes 98336 | tf_op jit(solution)/shard_map/ppermute | solution.py:332
  66.6 0.8 %collective-permute-done.12.refs_2_ = bf16[3,128,128]{2,1,0:T(8,128)(2,1)S(1)} collective-permute-done((bf16[3,128,128]{2,1,0:T(8,128)(2,1)S(1)}, bf16[3,128,128]{2,1,0:T(8,128)(2,1)S(1)}, u32[]{:S(2)}, u32[]{:S(2)}) %collective-permute-start.12) | collective-permute-done | bytes 98336 | tf_op jit(solution)/shard_map/ppermute | solution.py:332
  67.4 0.0 collective-permute-start.16
  67.4 2.4 %collective-permute-done.13.refs_3_ = bf16[3,128,128]{2,1,0:T(8,128)(2,1)S(1)} collective-permute-done((bf16[3,128,128]{2,1,0:T(8,128)(2,1)S(1)}, bf16[3,128,128]{2,1,0:T(8,128)(2,1)S(1)}, u32[]{:S(2)}, u32[]{:S(2)}) %collective-permute-start.13) | collective-permute-done | bytes 98336 | tf_op jit(solution)/shard_map/ppermute | solution.py:332
  69.8 0.0 collective-permute-start.17
  69.8 0.0 collective-permute-done.14.refs_4_
  69.8 1.3 %collective-permute-done.17.refs_7_ = bf16[3,128,128]{2,1,0:T(8,128)(2,1)S(1)} collective-permute-done((bf16[3,128,128]{2,1,0:T(8,128)(2,1)S(1)}, bf16[3,128,128]{2,1,0:T(8,128)(2,1)S(1)}, u32[]{:S(2)}, u32[]{:S(2)}) %collective-permute-start.17) | collective-permute-done | bytes 98336 | tf_op jit(solution)/shard_map/ppermute | solution.py:319
  71.1 0.0 collective-permute-done.5.base_b
  71.1 1.0 %final.1 = bf16[384,512]{1,0:T(8,128)(2,1)} custom-call(f32[384,512]{1,0:T(8,128)S(1)} %copy-done.10, f32[384,512]{1,0:T(8,128)S(1)} %collective-permute-done.5.base_b, bf16[3,128,128]{2,1,0:T(8,128)(2,1)S(1)} %get-tuple-element.31.refs_0_, bf16[3,128,128]{2,1,0:T(8,128)(2,1)S(1)} %collective-permute-done.11.refs_1_, ...), custom_call_target="tpu_custom_call" | custom-call | tf_op jit(solution)/shard_map/final/pallas_call | solution.py:300
  (29 shorter events, 0.1 us)
Async XLA Ops:
  1.9 10.2 %collective-permute-start.2 = (bf16[2,64,1152]{2,1,0:T(8,128)(2,1)}, bf16[2,64,1152]{2,1,0:T(8,128)(2,1)S(1)}, u32[]{:S(2)}, u32[]{:S(2)}) collective-permute-start(bf16[2,64,1152]{2,1,0:T(8,128)(2,1)} %get-tuple-element.24), channel_id=1, source_target_pairs={{0,2},{2,0},{1,3},{3,1},{4,6},{6,4},{5,7},{7,5},{8,10},{10,8},{9,1... | collective-permute-start | bytes 884744 | tf_op jit(solution)/shard_map/ppermute | solution.py:349
  4.9 16.5 %collective-permute-start.1 = (bf16[2,64,1152]{2,1,0:T(8,128)(2,1)}, bf16[2,64,1152]{2,1,0:T(8,128)(2,1)S(1)}, u32[]{:S(2)}, u32[]{:S(2)}) collective-permute-start(bf16[2,64,1152]{2,1,0:T(8,128)(2,1)} %get-tuple-element.22.refs_0_), channel_id=1, source_target_pairs={{0,4},{4,8},{8,12},{12,0},{1,5},{5,9},{9,13},{13,1},{2,6},{6,10},{... | collective-permute-start | bytes 884744 | tf_op jit(solution)/shard_map/ppermute | solution.py:322
  6.5 17.1 %collective-permute-start = (bf16[2,64,1152]{2,1,0:T(8,128)(2,1)}, bf16[2,64,1152]{2,1,0:T(8,128)(2,1)S(1)}, u32[]{:S(2)}, u32[]{:S(2)}) collective-permute-start(bf16[2,64,1152]{2,1,0:T(8,128)(2,1)} %get-tuple-element.22.refs_0_), channel_id=1, source_target_pairs={{0,12},{4,0},{8,4},{12,8},{1,13},{5,1},{9,5},{13,9},{2,14},{6,2},{... | collective-permute-start | bytes 884744 | tf_op jit(solution)/shard_map/ppermute | solution.py:322
  12.2 24.1 %copy-start.12 = (bf16[2,64,1152]{2,1,0:T(8,128)(2,1)}, bf16[2,64,1152]{2,1,0:T(8,128)(2,1)S(1)}, u32[]{:S(2)}) copy-start(bf16[2,64,1152]{2,1,0:T(8,128)(2,1)S(1)} %collective-permute-done.2.refs_3_) | copy-start | bytes 884740
  12.2 24.2 %collective-permute-start.4 = (bf16[2,64,1152]{2,1,0:T(8,128)(2,1)S(1)}, bf16[2,64,1152]{2,1,0:T(8,128)(2,1)S(1)}, u32[]{:S(2)}, u32[]{:S(2)}) collective-permute-start(bf16[2,64,1152]{2,1,0:T(8,128)(2,1)S(1)} %collective-permute-done.2.refs_3_), channel_id=1, source_target_pairs={{0,4},{4,8},{8,12},{12,0},{1,5},{5,9},{9,13},{13,1},{2,6},{6,10},{... | collective-permute-start | bytes 884744 | tf_op jit(solution)/shard_map/ppermute | solution.py:322
  14.0 22.7 %collective-permute-start.3 = (bf16[2,64,1152]{2,1,0:T(8,128)(2,1)S(1)}, bf16[2,64,1152]{2,1,0:T(8,128)(2,1)S(1)}, u32[]{:S(2)}, u32[]{:S(2)}) collective-permute-start(bf16[2,64,1152]{2,1,0:T(8,128)(2,1)S(1)} %collective-permute-done.2.refs_3_), channel_id=1, source_target_pairs={{0,12},{4,0},{8,4},{12,8},{1,13},{5,1},{9,5},{13,9},{2,14},{6,2},{... | collective-permute-start | bytes 884744 | tf_op jit(solution)/shard_map/ppermute | solution.py:322
  19.6 28.2 %collective-permute-start.8 = (bf16[400,1024]{1,0:T(8,128)(2,1)}, bf16[400,1024]{1,0:T(8,128)(2,1)}, u32[]{:S(2)}, u32[]{:S(2)}) collective-permute-start(bf16[400,1024]{1,0:T(8,128)(2,1)} %get-tuple-element.28), channel_id=1, source_target_pairs={{0,2},{2,0},{16,18},{18,16},{1,3},{3,1},{17,19},{19,17},{4,6},{6,4... | collective-permute-start | bytes 2457608 | tf_op jit(solution)/shard_map/ppermute | solution.py:332
  21.5 14.8 %copy-start.4 = (bf16[2,64,1152]{2,1,0:T(8,128)(2,1)}, bf16[2,64,1152]{2,1,0:T(8,128)(2,1)S(1)}, u32[]{:S(2)}) copy-start(bf16[2,64,1152]{2,1,0:T(8,128)(2,1)S(1)} %collective-permute-done.1.refs_0_) | copy-start | bytes 884740
  21.5 26.4 %collective-permute-start.9 = (bf16[400,1024]{1,0:T(8,128)(2,1)}, bf16[400,1024]{1,0:T(8,128)(2,1)}, u32[]{:S(2)}, u32[]{:S(2)}) collective-permute-start(bf16[400,1024]{1,0:T(8,128)(2,1)} %get-tuple-element.29), channel_id=1, source_target_pairs={{0,16},{2,18},{16,0},{18,2},{1,17},{3,19},{17,1},{19,3},{4,20},{6,... | collective-permute-start | bytes 2457608 | tf_op jit(solution)/shard_map/ppermute | solution.py:332
  23.6 12.7 %copy-start = (bf16[2,64,1152]{2,1,0:T(8,128)(2,1)}, bf16[2,64,1152]{2,1,0:T(8,128)(2,1)S(1)}, u32[]{:S(2)}) copy-start(bf16[2,64,1152]{2,1,0:T(8,128)(2,1)S(1)} %collective-permute-done.refs_1_) | copy-start | bytes 884740
  23.6 34.0 %collective-permute-start.10 = (bf16[400,1024]{1,0:T(8,128)(2,1)}, bf16[400,1024]{1,0:T(8,128)(2,1)}, u32[]{:S(2)}, u32[]{:S(2)}) collective-permute-start(bf16[400,1024]{1,0:T(8,128)(2,1)} %get-tuple-element.30), channel_id=1, source_target_pairs={{0,18},{2,16},{16,2},{18,0},{1,19},{3,17},{17,3},{19,1},{4,22},{6,... | collective-permute-start | bytes 2457608 | tf_op jit(solution)/shard_map/ppermute | solution.py:332
  36.3 21.3 %copy-start.9 = (bf16[400,1024]{1,0:T(8,128)(2,1)S(1)}, bf16[400,1024]{1,0:T(8,128)(2,1)}, u32[]{:S(2)}) copy-start(bf16[400,1024]{1,0:T(8,128)(2,1)} %get-tuple-element.27.refs_2_) | copy-start | bytes 2457604
  36.3 21.3 %copy-start.15 = (s32[16]{0:T(128)S(1)}, s32[16]{0:T(128)}, u32[]{:S(2)}) copy-start(s32[16]{0:T(128)} %owner.1) | copy-start | bytes 196
  36.4 0.7 %copy-start.2 = (bf16[2,64,1152]{2,1,0:T(8,128)(2,1)}, bf16[2,64,1152]{2,1,0:T(8,128)(2,1)S(1)}, u32[]{:S(2)}) copy-start(bf16[2,64,1152]{2,1,0:T(8,128)(2,1)S(1)} %collective-permute-done.4.refs_1_.refs_5_) | copy-start | bytes 884740
  36.4 8.8 %collective-permute-start.6 = (bf16[2,64,1152]{2,1,0:T(8,128)(2,1)}, bf16[2,64,1152]{2,1,0:T(8,128)(2,1)S(1)}, u32[]{:S(2)}, u32[]{:S(2)}) collective-permute-start(bf16[2,64,1152]{2,1,0:T(8,128)(2,1)} %hand.3.refs_2_), channel_id=1, source_target_pairs={{0,4},{4,8},{8,12},{12,0},{1,5},{5,9},{9,13},{13,1},{2,6},{6,10},{... | collective-permute-start | bytes 884744 | tf_op jit(solution)/shard_map/ppermute | solution.py:322
  37.1 0.7 %copy-start.6 = (bf16[2,64,1152]{2,1,0:T(8,128)(2,1)}, bf16[2,64,1152]{2,1,0:T(8,128)(2,1)S(1)}, u32[]{:S(2)}) copy-start(bf16[2,64,1152]{2,1,0:T(8,128)(2,1)S(1)} %collective-permute-done.3.refs_0_) | copy-start | bytes 884740
  37.8 1.0 %copy-start.1 = (bf16[2,64,1152]{2,1,0:T(8,128)(2,1)S(1)}, bf16[2,64,1152]{2,1,0:T(8,128)(2,1)}, u32[]{:S(2)}) copy-start(bf16[2,64,1152]{2,1,0:T(8,128)(2,1)} %copy-done) | copy-start | bytes 884740
  38.8 1.0 %copy-start.3 = (bf16[2,64,1152]{2,1,0:T(8,128)(2,1)S(1)}, bf16[2,64,1152]{2,1,0:T(8,128)(2,1)}, u32[]{:S(2)}) copy-start(bf16[2,64,1152]{2,1,0:T(8,128)(2,1)} %copy-done.2) | copy-start | bytes 884740
  39.8 1.0 %copy-start.5 = (bf16[2,64,1152]{2,1,0:T(8,128)(2,1)S(1)}, bf16[2,64,1152]{2,1,0:T(8,128)(2,1)}, u32[]{:S(2)}) copy-start(bf16[2,64,1152]{2,1,0:T(8,128)(2,1)} %hand.3.refs_2_) | copy-start | bytes 884740
  40.7 1.0 %copy-start.7 = (bf16[2,64,1152]{2,1,0:T(8,128)(2,1)S(1)}, bf16[2,64,1152]{2,1,0:T(8,128)(2,1)}, u32[]{:S(2)}) copy-start(bf16[2,64,1152]{2,1,0:T(8,128)(2,1)} %hand.4.refs_4_) | copy-start | bytes 884740
  41.7 1.0 %copy-start.11 = (bf16[2,64,1152]{2,1,0:T(8,128)(2,1)S(1)}, bf16[2,64,1152]{2,1,0:T(8,128)(2,1)}, u32[]{:S(2)}) copy-start(bf16[2,64,1152]{2,1,0:T(8,128)(2,1)} %get-tuple-element.22.refs_0_) | copy-start | bytes 884740
  42.7 1.0 %copy-start.13 = (bf16[2,64,1152]{2,1,0:T(8,128)(2,1)S(1)}, bf16[2,64,1152]{2,1,0:T(8,128)(2,1)}, u32[]{:S(2)}) copy-start(bf16[2,64,1152]{2,1,0:T(8,128)(2,1)} %copy-done.12) | copy-start | bytes 884740
  43.6 1.5 %copy-start.8 = (bf16[2,64,1152]{2,1,0:T(8,128)(2,1)S(1)}, bf16[2,64,1152]{2,1,0:T(8,128)(2,1)}, u32[]{:S(2)}) copy-start(bf16[2,64,1152]{2,1,0:T(8,128)(2,1)} %hand.4.refs_4_) | copy-start | bytes 884740
  44.1 0.6 copy-start.14
  44.6 26.4 %copy-start.10 = (f32[384,512]{1,0:T(8,128)S(1)}, f32[384,512]{1,0:T(8,128)}, u32[]{:S(2)}) copy-start(f32[384,512]{1,0:T(8,128)} %get-tuple-element.20.base_a) | copy-start | bytes 2359300
  44.6 26.4 %collective-permute-start.5 = (f32[384,512]{1,0:T(8,128)}, f32[384,512]{1,0:T(8,128)S(1)}, u32[]{:S(2)}, u32[]{:S(2)}) collective-permute-start(f32[384,512]{1,0:T(8,128)} %hand.5), channel_id=1, source_target_pairs={{0,1},{1,0},{2,3},{3,2},{4,5},{5,4},{6,7},{7,6},{8,9},{9,8},{10,11... | collective-permute-start | bytes 2359304 | tf_op jit(solution)/shard_map/ppermute | solution.py:319
  45.2 12.5 %collective-permute-start.7 = (bf16[2,64,1152]{2,1,0:T(8,128)(2,1)S(1)}, bf16[2,64,1152]{2,1,0:T(8,128)(2,1)S(1)}, u32[]{:S(2)}, u32[]{:S(2)}) collective-permute-start(bf16[2,64,1152]{2,1,0:T(8,128)(2,1)S(1)} %copy-done.8), channel_id=1, source_target_pairs={{0,12},{4,0},{8,4},{12,8},{1,13},{5,1},{9,5},{13,9},{2,14},{6,2},{... | collective-permute-start | bytes 884744 | tf_op jit(solution)/shard_map/ppermute | solution.py:322
  61.2 5.4 %collective-permute-start.11 = (bf16[3,128,128]{2,1,0:T(8,128)(2,1)S(1)}, bf16[3,128,128]{2,1,0:T(8,128)(2,1)S(1)}, u32[]{:S(2)}, u32[]{:S(2)}) collective-permute-start(bf16[3,128,128]{2,1,0:T(8,128)(2,1)S(1)} %get-tuple-element.32), channel_id=1, source_target_pairs={{0,2},{2,0},{16,18},{18,16},{1,3},{3,1},{17,19},{19,17},{4,6},{6,4... | collective-permute-start | bytes 294920 | tf_op jit(solution)/shard_map/ppermute | solution.py:332
  62.8 4.6 %collective-permute-start.12 = (bf16[3,128,128]{2,1,0:T(8,128)(2,1)S(1)}, bf16[3,128,128]{2,1,0:T(8,128)(2,1)S(1)}, u32[]{:S(2)}, u32[]{:S(2)}) collective-permute-start(bf16[3,128,128]{2,1,0:T(8,128)(2,1)S(1)} %get-tuple-element.33), channel_id=1, source_target_pairs={{0,16},{2,18},{16,0},{18,2},{1,17},{3,19},{17,1},{19,3},{4,20},{6,... | collective-permute-start | bytes 294920 | tf_op jit(solution)/shard_map/ppermute | solution.py:332
  64.2 5.5 %collective-permute-start.13 = (bf16[3,128,128]{2,1,0:T(8,128)(2,1)S(1)}, bf16[3,128,128]{2,1,0:T(8,128)(2,1)S(1)}, u32[]{:S(2)}, u32[]{:S(2)}) collective-permute-start(bf16[3,128,128]{2,1,0:T(8,128)(2,1)S(1)} %get-tuple-element.34), channel_id=1, source_target_pairs={{0,18},{2,16},{16,2},{18,0},{1,19},{3,17},{17,3},{19,1},{4,22},{6,... | collective-permute-start | bytes 294920 | tf_op jit(solution)/shard_map/ppermute | solution.py:332
  64.7 5.0 %collective-permute-start.14 = (bf16[3,128,128]{2,1,0:T(8,128)(2,1)S(1)}, bf16[3,128,128]{2,1,0:T(8,128)(2,1)S(1)}, u32[]{:S(2)}, u32[]{:S(2)}) collective-permute-start(bf16[3,128,128]{2,1,0:T(8,128)(2,1)S(1)} %get-tuple-element.31.refs_0_), channel_id=1, source_target_pairs={{0,1},{1,0},{2,3},{3,2},{4,5},{5,4},{6,7},{7,6},{8,9},{9,8},{10,11... | collective-permute-start | bytes 294920 | tf_op jit(solution)/shard_map/ppermute | solution.py:319
  66.5 3.2 %collective-permute-start.15 = (bf16[3,128,128]{2,1,0:T(8,128)(2,1)S(1)}, bf16[3,128,128]{2,1,0:T(8,128)(2,1)S(1)}, u32[]{:S(2)}, u32[]{:S(2)}) collective-permute-start(bf16[3,128,128]{2,1,0:T(8,128)(2,1)S(1)} %collective-permute-done.11.refs_1_), channel_id=1, source_target_pairs={{0,1},{1,0},{2,3},{3,2},{4,5},{5,4},{6,7},{7,6},{8,9},{9,8},{10,11... | collective-permute-start | bytes 294920 | tf_op jit(solution)/shard_map/ppermute | solution.py:319
  67.4 2.4 %collective-permute-start.16 = (bf16[3,128,128]{2,1,0:T(8,128)(2,1)S(1)}, bf16[3,128,128]{2,1,0:T(8,128)(2,1)S(1)}, u32[]{:S(2)}, u32[]{:S(2)}) collective-permute-start(bf16[3,128,128]{2,1,0:T(8,128)(2,1)S(1)} %collective-permute-done.12.refs_2_), channel_id=1, source_target_pairs={{0,1},{1,0},{2,3},{3,2},{4,5},{5,4},{6,7},{7,6},{8,9},{9,8},{10,11... | collective-permute-start | bytes 294920 | tf_op jit(solution)/shard_map/ppermute | solution.py:319
  69.8 1.3 %collective-permute-start.17 = (bf16[3,128,128]{2,1,0:T(8,128)(2,1)S(1)}, bf16[3,128,128]{2,1,0:T(8,128)(2,1)S(1)}, u32[]{:S(2)}, u32[]{:S(2)}) collective-permute-start(bf16[3,128,128]{2,1,0:T(8,128)(2,1)S(1)} %collective-permute-done.13.refs_3_), channel_id=1, source_target_pairs={{0,1},{1,0},{2,3},{3,2},{4,5},{5,4},{6,7},{7,6},{8,9},{9,8},{10,11... | collective-permute-start | bytes 294920 | tf_op jit(solution)/shard_map/ppermute | solution.py:319

commit v22 on v20

--- a/solution.py
+++ b/solution.py
@@ -204,13 +204,12 @@
         out_specs=VMEM,
         out_shape=jax.ShapeDtypeStruct((count,) + pieces[0].shape[1:], pieces[0].dtype),
         scratch_shapes=[pltpu.SemaphoreType.DMA((len(pieces),))],
-        cost_estimate=pl.CostEstimate(flops=0, bytes_accessed=0, transcendentals=0),
         compiler_params=ROOM,
         name="collect",
     )(*pieces)
 
 
-def rank_kernel(ring, pair, rows, owner, held, *refs):
+def rank_kernel(ring, pair, rows, owner, flag, held, *refs):
     shares = len(refs) // 2
     toks, outs = refs[:shares], refs[shares:]
     per, rank = held.shape[0] // (ring * pair), held.shape[1]
@@ -240,17 +239,17 @@
             outs[k][b, rank:, :] = held[at, :, feats:]
 
 
-def rank_parts(owner, toks, held, ring, pair, rows, blocks):
+def rank_parts(owner, flag, toks, held, ring, pair, rows, blocks):
     shares, rank = len(toks), held.shape[1]
     return pl.pallas_call(
         functools.partial(rank_kernel, ring, pair, rows),
-        in_specs=[SMEM, VMEM] + [VMEM] * shares,
+        in_specs=[SMEM, ANY, VMEM] + [VMEM] * shares,
         out_specs=[VMEM] * shares,
         out_shape=[jax.ShapeDtypeStruct((blocks, 2 * rank, rows // blocks), held.dtype)] * shares,
         cost_estimate=pl.CostEstimate(flops=0, bytes_accessed=0, transcendentals=0),
         compiler_params=ROOM,
         name="rank",
-    )(owner, held, *toks)
+    )(owner, flag, held, *toks)
 
 
 def final_kernel(groups, pair, base_a, base_b, *refs):
@@ -331,18 +330,15 @@
 
     base_mine, base_out, flag = base_halves(tokens, base_key, sides, lengths)
     pieces = [
-        more_hops(held, way, flag)
+        more_hops(held, way)
         for way, held in enumerate(firsts)
     ]
 
     flat = [piece for way in pieces for piece in way]
-    parts = rank_parts(owner_slot, toks, collect(flat), ring, pair, rows, blocks)
-    mine, theirs = [parts[0]] * shares, [None] * shares
-    for k in reversed(range(1, shares)):
-        mine[k] = in_plane(parts[k], -(k // pair), -(k % pair))
-    for k in reversed(range(shares)):
-        theirs[k] = across(mine[k])
-    base_in = across(hand_on(base_out, pieces[-1][1]))
+    parts = rank_parts(owner_slot, flag, toks, collect(flat), ring, pair, rows, blocks)
+    mine = [parts[0]] + [in_plane(parts[k], -(k // pair), -(k % pair)) for k in range(1, shares)]
+    theirs = [across(part) for part in mine]
+    base_in = across(base_out)
     return final(mine, theirs, [base_mine, base_in], groups, pair, tokens.dtype)
 
 

time: 70.7 us -> 71.8 us (1.016)
  starting transfers between devices: 19.3 us -> 22.6 us
  local copies, waits for them, and re-layouts: 5 us -> 2.62 us
  Pallas kernels: 20.7 us -> 22.5 us
  waiting for transfers between devices: 25.1 us -> 23.4 us
    ppermute x6, starting transfers between devices: 7.95 us -> 11.3 us  [along(): lax.ppermute(x, 'ring', [(a, (a + step) % ring) for a in range(ring)])]
    ppermute x6, waiting for transfers between devices: 14.9 us -> 11.9 us  [along(): lax.ppermute(x, 'ring', [(a, (a + step) % ring) for a in range(ring)])]
    unnamed x24 -> x26, local copies, waits for them, and re-layouts: 5 us -> 2.62 us
    pallas_call x1, Pallas kernels: 1.05 us -> 2.18 us  [final(): pl.pallas_call(functools.partial(final_kernel, groups, pair), in_specs=[V...]
    ppermute x6, waiting for transfers between devices: 5.34 us -> 6.44 us  [in_plane(): return lax.ppermute(x, PLANE, pairs)]
  transfers between devices with their start and end apart: 18 -> 18, of which waited for: 9 -> 11; matrix products, arithmetic and copies ran while one was open for 0% -> 0% of each run, Pallas kernels for 25% -> 26%
where the time goes in v22:
time: 71.8 us; the launch traced here: 71.3 us
  waiting for transfers between devices  23.4 us (33%)
  starting transfers between devices  22.6 us (31%)
  Pallas kernels  22.5 us (31%)
  local copies, waits for them, and re-layouts  2.62 us (4%)
    ppermute x6, waiting for transfers between devices, along(): lax.ppermute(x, 'ring', [(a, (a + step) % ring) for a in range(ring)])  11.9 us
    pallas_call x1, Pallas kernels, base_halves(): pl.pallas_call(functools.partial(base_kernel, sides), grid_spec=pltpu.Pre...  11.3 us
    ppermute x6, starting transfers between devices, along(): lax.ppermute(x, 'ring', [(a, (a + step) % ring) for a in range(ring)])  11.3 us
    ppermute x6, starting transfers between devices, in_plane(): return lax.ppermute(x, PLANE, pairs)  8.26 us
    ppermute x6, waiting for transfers between devices, in_plane(): return lax.ppermute(x, PLANE, pairs)  6.44 us
    ppermute x1, waiting for transfers between devices, body(): lax.ppermute(packed[pair - w], 'pair', [(a, (a - w) % pair) for a in rang...  3.72 us
    pallas_call x1, Pallas kernels, spread(): pl.pallas_call(functools.partial(spread_kernel, groups, pair), in_specs=[...  3.69 us
    ppermute x1, starting transfers between devices, body(): lax.ppermute(packed[pair - w], 'pair', [(a, (a - w) % pair) for a in rang...  3.03 us
  transfers between devices with their start and end apart: 18, of which 11 were waited for; matrix products, arithmetic and copies ran while one was open for 0% of the time, Pallas kernels for 26%

profile of v22, /device:TPU:0, one launch (start us, length us, event | category | flops | bytes accessed | tf_op | source)
XLA Modules:
  0.0 71.3 jit_solution(13831842679624938906)
XLA Ops:
  0.0 1.9 %pack.1 = (bf16[2,64,1152]{2,1,0:T(8,128)(2,1)}, bf16[2,64,1152]{2,1,0:T(8,128)(2,1)}) custom-call(bf16[2,64,4096]{2,1,0:T(8,128)(2,1)} %bitcast.2, bf16[2,64,512]{2,1,0:T(8,128)(2,1)} %up.1), custom_call_target="tpu_custom_call" | custom-call | tf_op jit(solution)/shard_map/pack/pallas_call | solution.py:57
  1.9 3.0 %collective-permute-start.4 = (bf16[2,64,1152]{2,1,0:T(8,128)(2,1)}, bf16[2,64,1152]{2,1,0:T(8,128)(2,1)}, u32[]{:S(2)}, u32[]{:S(2)}) collective-permute-start(bf16[2,64,1152]{2,1,0:T(8,128)(2,1)} %get-tuple-element.22), channel_id=1, source_target_pairs={{0,2},{2,0},{1,3},{3,1},{4,6},{6,4},{5,7},{7,5},{8,10},{10,8},{9,1... | collective-permute-start | bytes 884744 | tf_op jit(solution)/shard_map/ppermute | solution.py:326
  4.9 3.6 %collective-permute-start.1 = (bf16[2,64,1152]{2,1,0:T(8,128)(2,1)}, bf16[2,64,1152]{2,1,0:T(8,128)(2,1)S(1)}, u32[]{:S(2)}, u32[]{:S(2)}) collective-permute-start(bf16[2,64,1152]{2,1,0:T(8,128)(2,1)} %get-tuple-element.21.refs_0_), channel_id=1, source_target_pairs={{0,12},{4,0},{8,4},{12,8},{1,13},{5,1},{9,5},{13,9},{2,14},{6,2},{... | collective-permute-start | bytes 884744 | tf_op jit(solution)/shard_map/ppermute | solution.py:299
  8.5 0.0 collective-permute-start.2
  8.5 3.7 %collective-permute-done.4.refs_4_ = bf16[2,64,1152]{2,1,0:T(8,128)(2,1)} collective-permute-done((bf16[2,64,1152]{2,1,0:T(8,128)(2,1)}, bf16[2,64,1152]{2,1,0:T(8,128)(2,1)}, u32[]{:S(2)}, u32[]{:S(2)}) %collective-permute-start.4) | collective-permute-done | bytes 294944 | tf_op jit(solution)/shard_map/ppermute | solution.py:326
  12.3 1.8 %collective-permute-start.6 = (bf16[2,64,1152]{2,1,0:T(8,128)(2,1)}, bf16[2,64,1152]{2,1,0:T(8,128)(2,1)S(1)}, u32[]{:S(2)}, u32[]{:S(2)}) collective-permute-start(bf16[2,64,1152]{2,1,0:T(8,128)(2,1)} %collective-permute-done.4.refs_4_), channel_id=1, source_target_pairs={{0,4},{4,8},{8,12},{12,0},{1,5},{5,9},{9,13},{13,1},{2,6},{6,10},{... | collective-permute-start | bytes 884744 | tf_op jit(solution)/shard_map/ppermute | solution.py:299
  14.0 2.0 %collective-permute-start.5 = (bf16[2,64,1152]{2,1,0:T(8,128)(2,1)}, bf16[2,64,1152]{2,1,0:T(8,128)(2,1)S(1)}, u32[]{:S(2)}, u32[]{:S(2)}) collective-permute-start(bf16[2,64,1152]{2,1,0:T(8,128)(2,1)} %collective-permute-done.4.refs_4_), channel_id=1, source_target_pairs={{0,12},{4,0},{8,4},{12,8},{1,13},{5,1},{9,5},{13,9},{2,14},{6,2},{... | collective-permute-start | bytes 884744 | tf_op jit(solution)/shard_map/ppermute | solution.py:299
  16.1 3.7 %spread.1 = (bf16[400,1024]{1,0:T(8,128)(2,1)}, bf16[400,1024]{1,0:T(8,128)(2,1)}, bf16[400,1024]{1,0:T(8,128)(2,1)}, bf16[400,1024]{1,0:T(8,128)(2,1)}) custom-call(s32[3]{0:T(128)} %lengths.3, s32[3]{0:T(128)} %bitcast.3, bf16[384,4096]{1,0:T(8,128)(2,1)} %tok.1), custom_call_target="tpu_custom_call" | custom-call | tf_op jit(solution)/shard_map/spread/pallas_call | solution.py:119
  19.8 2.7 %collective-permute-start.10 = (bf16[400,1024]{1,0:T(8,128)(2,1)}, bf16[400,1024]{1,0:T(8,128)(2,1)S(1)}, u32[]{:S(2)}, u32[]{:S(2)}) collective-permute-start(bf16[400,1024]{1,0:T(8,128)(2,1)} %get-tuple-element.26), channel_id=1, source_target_pairs={{0,18},{2,16},{16,2},{18,0},{1,19},{3,17},{17,3},{19,1},{4,22},{6,... | collective-permute-start | bytes 2457608 | tf_op jit(solution)/shard_map/ppermute | solution.py:309
  22.5 0.0 collective-permute-done.1.refs_1_
  22.5 0.5 collective-permute-start.8
  23.0 0.6 collective-permute-done.2.refs_0_
  23.6 1.5 %collective-permute-start.9 = (bf16[400,1024]{1,0:T(8,128)(2,1)}, bf16[400,1024]{1,0:T(8,128)(2,1)}, u32[]{:S(2)}, u32[]{:S(2)}) collective-permute-start(bf16[400,1024]{1,0:T(8,128)(2,1)} %get-tuple-element.25), channel_id=1, source_target_pairs={{0,16},{2,18},{16,0},{18,2},{1,17},{3,19},{17,1},{19,3},{4,20},{6,... | collective-permute-start | bytes 2457608 | tf_op jit(solution)/shard_map/ppermute | solution.py:309
  25.1 0.0 copy-done.6
  25.1 0.0 copy-start.10
  25.1 4.7 %collective-permute-done.6.refs_1_.refs_7_ = bf16[2,64,1152]{2,1,0:T(8,128)(2,1)S(1)} collective-permute-done((bf16[2,64,1152]{2,1,0:T(8,128)(2,1)}, bf16[2,64,1152]{2,1,0:T(8,128)(2,1)S(1)}, u32[]{:S(2)}, u32[]{:S(2)}) %collective-permute-start.6) | collective-permute-done | bytes 294944 | tf_op jit(solution)/shard_map/ppermute | solution.py:299
  29.8 1.5 %collective-permute-start.3 = (bf16[2,64,1152]{2,1,0:T(8,128)(2,1)}, bf16[2,64,1152]{2,1,0:T(8,128)(2,1)}, u32[]{:S(2)}, u32[]{:S(2)}) collective-permute-start(bf16[2,64,1152]{2,1,0:T(8,128)(2,1)} %hand.2.refs_3_), channel_id=1, source_target_pairs={{0,4},{4,8},{8,12},{12,0},{1,5},{5,9},{9,13},{13,1},{2,6},{6,10},{... | collective-permute-start | bytes 884744 | tf_op jit(solution)/shard_map/ppermute | solution.py:299
  31.3 11.3 %base.1 = (f32[384,512]{1,0:T(8,128)}, f32[384,512]{1,0:T(8,128)}, f32[8,128]{1,0:T(8,128)}) custom-call(s32[3]{0:T(128)} %lengths.3, bf16[384,4096]{1,0:T(8,128)(2,1)} %tok.1, bf16[4096,1024]{1,0:T(8,128)(2,1)} %key_ref.1), custom_call_target="tpu_custom_call" | custom-call | tf_op jit(solution)/shard_map/base/pallas_call | solution.py:167
  42.6 0.0 copy-start.12
  42.6 0.0 collective-permute-done.5.refs_0_
  42.6 0.1 collective-permute-start
  42.7 0.7 copy-done.4
  43.4 0.0 collective-permute-done.3.refs_2_
  43.4 2.3 %collective-permute-start.7 = (bf16[2,64,1152]{2,1,0:T(8,128)(2,1)}, bf16[2,64,1152]{2,1,0:T(8,128)(2,1)S(1)}, u32[]{:S(2)}, u32[]{:S(2)}) collective-permute-start(bf16[2,64,1152]{2,1,0:T(8,128)(2,1)} %hand.3.refs_5_), channel_id=1, source_target_pairs={{0,12},{4,0},{8,4},{12,8},{1,13},{5,1},{9,5},{13,9},{2,14},{6,2},{... | collective-permute-start | bytes 884744 | tf_op jit(solution)/shard_map/ppermute | solution.py:299
  45.7 6.7 %collective-permute-done.7.refs_6_ = bf16[2,64,1152]{2,1,0:T(8,128)(2,1)S(1)} collective-permute-done((bf16[2,64,1152]{2,1,0:T(8,128)(2,1)}, bf16[2,64,1152]{2,1,0:T(8,128)(2,1)S(1)}, u32[]{:S(2)}, u32[]{:S(2)}) %collective-permute-start.7) | collective-permute-done | bytes 294944 | tf_op jit(solution)/shard_map/ppermute | solution.py:299
  52.4 1.0 %copy-done.3 = bf16[2,64,1152]{2,1,0:T(8,128)(2,1)S(1)} copy-done((bf16[2,64,1152]{2,1,0:T(8,128)(2,1)S(1)}, bf16[2,64,1152]{2,1,0:T(8,128)(2,1)}, u32[]{:S(2)}) %copy-start.3) | copy-done | bytes 294936
  53.3 1.0 %copy-done.5 = bf16[2,64,1152]{2,1,0:T(8,128)(2,1)S(1)} copy-done((bf16[2,64,1152]{2,1,0:T(8,128)(2,1)S(1)}, bf16[2,64,1152]{2,1,0:T(8,128)(2,1)}, u32[]{:S(2)}) %copy-start.5) | copy-done | bytes 294936
  54.3 1.3 %collect.1.held = bf16[16,64,1152]{2,1,0:T(8,128)(2,1)S(1)} custom-call(bf16[2,64,1152]{2,1,0:T(8,128)(2,1)S(1)} %copy-done.10, bf16[2,64,1152]{2,1,0:T(8,128)(2,1)S(1)} %copy-done.1, bf16[2,64,1152]{2,1,0:T(8,128)(2,1)} %collective-permute-done.3.refs_2_, bf16[2,64,1152]{2,1,0:T(8,128)(2,1)S(1)} %copy-done.7, ...), custom_call_target="tpu_custom_call" | custom-call | tf_op jit(solution)/shard_map/collect/pallas_call | solution.py:201
  55.5 0.0 collective-permute-done.10.refs_3_
  55.6 1.8 %collective-permute-done.8.refs_1_ = bf16[400,1024]{1,0:T(8,128)(2,1)S(1)} collective-permute-done((bf16[400,1024]{1,0:T(8,128)(2,1)}, bf16[400,1024]{1,0:T(8,128)(2,1)S(1)}, u32[]{:S(2)}, u32[]{:S(2)}) %collective-permute-start.8) | collective-permute-done | bytes 819232 | tf_op jit(solution)/shard_map/ppermute | solution.py:309
  57.4 0.2 collective-permute-done.9.refs_2_
  57.6 2.2 %rank.1 = (bf16[3,128,128]{2,1,0:T(8,128)(2,1)S(1)}, bf16[3,128,128]{2,1,0:T(8,128)(2,1)S(1)}, bf16[3,128,128]{2,1,0:T(8,128)(2,1)S(1)}, bf16[3,128,128]{2,1,0:T(8,128)(2,1)S(1)}) custom-call(s32[16]{0:T(128)S(1)} %copy-done.12, f32[8,128]{1,0:T(8,128)S(1)} %copy-done.11, bf16[16,64,1152]{2,1,0:T(8,128)(2,1)S(1)} %collect.1.held, ...), custom_call_target="tpu_custom_call" | custom-call | tf_op jit(solution)/shard_map/rank/pallas_call | solution.py:244
  59.8 1.4 %collective-permute-start.11 = (bf16[3,128,128]{2,1,0:T(8,128)(2,1)S(1)}, bf16[3,128,128]{2,1,0:T(8,128)(2,1)S(1)}, u32[]{:S(2)}, u32[]{:S(2)}) collective-permute-start(bf16[3,128,128]{2,1,0:T(8,128)(2,1)S(1)} %get-tuple-element.28), channel_id=1, source_target_pairs={{0,2},{2,0},{16,18},{18,16},{1,3},{3,1},{17,19},{19,17},{4,6},{6,4... | collective-permute-start | bytes 294920 | tf_op jit(solution)/shard_map/ppermute | solution.py:309
  61.2 0.8 %collective-permute-start.12 = (bf16[3,128,128]{2,1,0:T(8,128)(2,1)S(1)}, bf16[3,128,128]{2,1,0:T(8,128)(2,1)S(1)}, u32[]{:S(2)}, u32[]{:S(2)}) collective-permute-start(bf16[3,128,128]{2,1,0:T(8,128)(2,1)S(1)} %get-tuple-element.29), channel_id=1, source_target_pairs={{0,16},{2,18},{16,0},{18,2},{1,17},{3,19},{17,1},{19,3},{4,20},{6,... | collective-permute-start | bytes 294920 | tf_op jit(solution)/shard_map/ppermute | solution.py:309
  62.0 1.3 %collective-permute-start.13 = (bf16[3,128,128]{2,1,0:T(8,128)(2,1)S(1)}, bf16[3,128,128]{2,1,0:T(8,128)(2,1)S(1)}, u32[]{:S(2)}, u32[]{:S(2)}) collective-permute-start(bf16[3,128,128]{2,1,0:T(8,128)(2,1)S(1)} %get-tuple-element.30), channel_id=1, source_target_pairs={{0,18},{2,16},{16,2},{18,0},{1,19},{3,17},{17,3},{19,1},{4,22},{6,... | collective-permute-start | bytes 294920 | tf_op jit(solution)/shard_map/ppermute | solution.py:309
  63.4 0.0 collective-permute-start.14
  63.4 1.2 %collective-permute-done.11.refs_1_ = bf16[3,128,128]{2,1,0:T(8,128)(2,1)S(1)} collective-permute-done((bf16[3,128,128]{2,1,0:T(8,128)(2,1)S(1)}, bf16[3,128,128]{2,1,0:T(8,128)(2,1)S(1)}, u32[]{:S(2)}, u32[]{:S(2)}) %collective-permute-start.11) | collective-permute-done | bytes 98336 | tf_op jit(solution)/shard_map/ppermute | solution.py:309
  64.5 0.0 collective-permute-start.15
  64.5 2.3 %collective-permute-done.12.refs_2_ = bf16[3,128,128]{2,1,0:T(8,128)(2,1)S(1)} collective-permute-done((bf16[3,128,128]{2,1,0:T(8,128)(2,1)S(1)}, bf16[3,128,128]{2,1,0:T(8,128)(2,1)S(1)}, u32[]{:S(2)}, u32[]{:S(2)}) %collective-permute-start.12) | collective-permute-done | bytes 98336 | tf_op jit(solution)/shard_map/ppermute | solution.py:309
  66.9 0.0 collective-permute-start.16
  66.9 1.0 %collective-permute-done.13.refs_3_ = bf16[3,128,128]{2,1,0:T(8,128)(2,1)S(1)} collective-permute-done((bf16[3,128,128]{2,1,0:T(8,128)(2,1)S(1)}, bf16[3,128,128]{2,1,0:T(8,128)(2,1)S(1)}, u32[]{:S(2)}, u32[]{:S(2)}) %collective-permute-start.13) | collective-permute-done | bytes 98336 | tf_op jit(solution)/shard_map/ppermute | solution.py:309
  67.8 0.0 collective-permute-start.17
  67.8 0.0 collective-permute-done.base_b
  67.8 0.0 collective-permute-done.14.refs_4_
  67.8 0.0 collective-permute-done.15.refs_5_
  67.9 0.3 collective-permute-done.16.refs_6_
  68.2 1.0 %collective-permute-done.17.refs_7_ = bf16[3,128,128]{2,1,0:T(8,128)(2,1)S(1)} collective-permute-done((bf16[3,128,128]{2,1,0:T(8,128)(2,1)S(1)}, bf16[3,128,128]{2,1,0:T(8,128)(2,1)S(1)}, u32[]{:S(2)}, u32[]{:S(2)}) %collective-permute-start.17) | collective-permute-done | bytes 98336 | tf_op jit(solution)/shard_map/ppermute | solution.py:296
  69.1 2.2 %final.1 = bf16[384,512]{1,0:T(8,128)(2,1)} custom-call(f32[384,512]{1,0:T(8,128)S(1)} %copy-done.9, f32[384,512]{1,0:T(8,128)} %collective-permute-done.base_b, bf16[3,128,128]{2,1,0:T(8,128)(2,1)S(1)} %get-tuple-element.27.refs_0_, bf16[3,128,128]{2,1,0:T(8,128)(2,1)S(1)} %collective-permute-done.11.refs_1_, ...), custom_call_target="tpu_custom_call" | custom-call | tf_op jit(solution)/shard_map/final/pallas_call | solution.py:277
  (22 shorter events, 0.0 us)
Async XLA Ops:
  1.9 10.4 %collective-permute-start.4 = (bf16[2,64,1152]{2,1,0:T(8,128)(2,1)}, bf16[2,64,1152]{2,1,0:T(8,128)(2,1)}, u32[]{:S(2)}, u32[]{:S(2)}) collective-permute-start(bf16[2,64,1152]{2,1,0:T(8,128)(2,1)} %get-tuple-element.22), channel_id=1, source_target_pairs={{0,2},{2,0},{1,3},{3,1},{4,6},{6,4},{5,7},{7,5},{8,10},{10,8},{9,1... | collective-permute-start | bytes 884744 | tf_op jit(solution)/shard_map/ppermute | solution.py:326
  4.9 17.6 %collective-permute-start.1 = (bf16[2,64,1152]{2,1,0:T(8,128)(2,1)}, bf16[2,64,1152]{2,1,0:T(8,128)(2,1)S(1)}, u32[]{:S(2)}, u32[]{:S(2)}) collective-permute-start(bf16[2,64,1152]{2,1,0:T(8,128)(2,1)} %get-tuple-element.21.refs_0_), channel_id=1, source_target_pairs={{0,12},{4,0},{8,4},{12,8},{1,13},{5,1},{9,5},{13,9},{2,14},{6,2},{... | collective-permute-start | bytes 884744 | tf_op jit(solution)/shard_map/ppermute | solution.py:299
  8.5 15.0 %collective-permute-start.2 = (bf16[2,64,1152]{2,1,0:T(8,128)(2,1)}, bf16[2,64,1152]{2,1,0:T(8,128)(2,1)S(1)}, u32[]{:S(2)}, u32[]{:S(2)}) collective-permute-start(bf16[2,64,1152]{2,1,0:T(8,128)(2,1)} %get-tuple-element.21.refs_0_), channel_id=1, source_target_pairs={{0,4},{4,8},{8,12},{12,0},{1,5},{5,9},{9,13},{13,1},{2,6},{6,10},{... | collective-permute-start | bytes 884744 | tf_op jit(solution)/shard_map/ppermute | solution.py:299
  12.3 17.5 %collective-permute-start.6 = (bf16[2,64,1152]{2,1,0:T(8,128)(2,1)}, bf16[2,64,1152]{2,1,0:T(8,128)(2,1)S(1)}, u32[]{:S(2)}, u32[]{:S(2)}) collective-permute-start(bf16[2,64,1152]{2,1,0:T(8,128)(2,1)} %collective-permute-done.4.refs_4_), channel_id=1, source_target_pairs={{0,4},{4,8},{8,12},{12,0},{1,5},{5,9},{9,13},{13,1},{2,6},{6,10},{... | collective-permute-start | bytes 884744 | tf_op jit(solution)/shard_map/ppermute | solution.py:299
  14.0 28.6 %collective-permute-start.5 = (bf16[2,64,1152]{2,1,0:T(8,128)(2,1)}, bf16[2,64,1152]{2,1,0:T(8,128)(2,1)S(1)}, u32[]{:S(2)}, u32[]{:S(2)}) collective-permute-start(bf16[2,64,1152]{2,1,0:T(8,128)(2,1)} %collective-permute-done.4.refs_4_), channel_id=1, source_target_pairs={{0,12},{4,0},{8,4},{12,8},{1,13},{5,1},{9,5},{13,9},{2,14},{6,2},{... | collective-permute-start | bytes 884744 | tf_op jit(solution)/shard_map/ppermute | solution.py:299
  19.8 35.8 %collective-permute-start.10 = (bf16[400,1024]{1,0:T(8,128)(2,1)}, bf16[400,1024]{1,0:T(8,128)(2,1)S(1)}, u32[]{:S(2)}, u32[]{:S(2)}) collective-permute-start(bf16[400,1024]{1,0:T(8,128)(2,1)} %get-tuple-element.26), channel_id=1, source_target_pairs={{0,18},{2,16},{16,2},{18,0},{1,19},{3,17},{17,3},{19,1},{4,22},{6,... | collective-permute-start | bytes 2457608 | tf_op jit(solution)/shard_map/ppermute | solution.py:309
  22.5 2.6 %copy-start = (bf16[2,64,1152]{2,1,0:T(8,128)(2,1)}, bf16[2,64,1152]{2,1,0:T(8,128)(2,1)S(1)}, u32[]{:S(2)}) copy-start(bf16[2,64,1152]{2,1,0:T(8,128)(2,1)S(1)} %collective-permute-done.1.refs_1_) | copy-start | bytes 884740
  22.5 34.9 %collective-permute-start.8 = (bf16[400,1024]{1,0:T(8,128)(2,1)}, bf16[400,1024]{1,0:T(8,128)(2,1)S(1)}, u32[]{:S(2)}, u32[]{:S(2)}) collective-permute-start(bf16[400,1024]{1,0:T(8,128)(2,1)} %get-tuple-element.24), channel_id=1, source_target_pairs={{0,2},{2,0},{16,18},{18,16},{1,3},{3,1},{17,19},{19,17},{4,6},{6,4... | collective-permute-start | bytes 2457608 | tf_op jit(solution)/shard_map/ppermute | solution.py:309
  23.6 1.5 %copy-start.6 = (bf16[2,64,1152]{2,1,0:T(8,128)(2,1)}, bf16[2,64,1152]{2,1,0:T(8,128)(2,1)S(1)}, u32[]{:S(2)}) copy-start(bf16[2,64,1152]{2,1,0:T(8,128)(2,1)S(1)} %collective-permute-done.2.refs_0_) | copy-start | bytes 884740
  23.6 34.0 %collective-permute-start.9 = (bf16[400,1024]{1,0:T(8,128)(2,1)}, bf16[400,1024]{1,0:T(8,128)(2,1)}, u32[]{:S(2)}, u32[]{:S(2)}) collective-permute-start(bf16[400,1024]{1,0:T(8,128)(2,1)} %get-tuple-element.25), channel_id=1, source_target_pairs={{0,16},{2,18},{16,0},{18,2},{1,17},{3,19},{17,1},{19,3},{4,20},{6,... | collective-permute-start | bytes 2457608 | tf_op jit(solution)/shard_map/ppermute | solution.py:309
  25.1 27.3 %copy-start.1 = (bf16[2,64,1152]{2,1,0:T(8,128)(2,1)S(1)}, bf16[2,64,1152]{2,1,0:T(8,128)(2,1)}, u32[]{:S(2)}) copy-start(bf16[2,64,1152]{2,1,0:T(8,128)(2,1)} %copy-done) | copy-start | bytes 884740
  25.1 27.3 %copy-start.7 = (bf16[2,64,1152]{2,1,0:T(8,128)(2,1)S(1)}, bf16[2,64,1152]{2,1,0:T(8,128)(2,1)}, u32[]{:S(2)}) copy-start(bf16[2,64,1152]{2,1,0:T(8,128)(2,1)} %hand.2.refs_3_) | copy-start | bytes 884740
  25.1 27.3 %copy-start.10 = (bf16[2,64,1152]{2,1,0:T(8,128)(2,1)S(1)}, bf16[2,64,1152]{2,1,0:T(8,128)(2,1)}, u32[]{:S(2)}) copy-start(bf16[2,64,1152]{2,1,0:T(8,128)(2,1)} %get-tuple-element.21.refs_0_) | copy-start | bytes 884740
  29.8 12.8 %copy-start.2 = (bf16[2,64,1152]{2,1,0:T(8,128)(2,1)}, bf16[2,64,1152]{2,1,0:T(8,128)(2,1)S(1)}, u32[]{:S(2)}) copy-start(bf16[2,64,1152]{2,1,0:T(8,128)(2,1)S(1)} %collective-permute-done.6.refs_1_.refs_7_) | copy-start | bytes 884740
  29.8 13.6 %collective-permute-start.3 = (bf16[2,64,1152]{2,1,0:T(8,128)(2,1)}, bf16[2,64,1152]{2,1,0:T(8,128)(2,1)}, u32[]{:S(2)}, u32[]{:S(2)}) collective-permute-start(bf16[2,64,1152]{2,1,0:T(8,128)(2,1)} %hand.2.refs_3_), channel_id=1, source_target_pairs={{0,4},{4,8},{8,12},{12,0},{1,5},{5,9},{9,13},{13,1},{2,6},{6,10},{... | collective-permute-start | bytes 884744 | tf_op jit(solution)/shard_map/ppermute | solution.py:299
  42.6 15.0 %copy-start.8 = (bf16[400,1024]{1,0:T(8,128)(2,1)S(1)}, bf16[400,1024]{1,0:T(8,128)(2,1)}, u32[]{:S(2)}) copy-start(bf16[400,1024]{1,0:T(8,128)(2,1)} %get-tuple-element.23.refs_0_) | copy-start | bytes 2457604
  42.6 15.0 %copy-start.11 = (f32[8,128]{1,0:T(8,128)S(1)}, f32[8,128]{1,0:T(8,128)}, u32[]{:S(2)}) copy-start(f32[8,128]{1,0:T(8,128)} %get-tuple-element.20.flag) | copy-start | bytes 12292
  42.6 15.0 %copy-start.12 = (s32[16]{0:T(128)S(1)}, s32[16]{0:T(128)}, u32[]{:S(2)}) copy-start(s32[16]{0:T(128)} %owner.1) | copy-start | bytes 196
  42.6 0.7 %copy-start.4 = (bf16[2,64,1152]{2,1,0:T(8,128)(2,1)}, bf16[2,64,1152]{2,1,0:T(8,128)(2,1)S(1)}, u32[]{:S(2)}) copy-start(bf16[2,64,1152]{2,1,0:T(8,128)(2,1)S(1)} %collective-permute-done.5.refs_0_) | copy-start | bytes 884740
  42.6 25.2 %collective-permute-start = (f32[384,512]{1,0:T(8,128)}, f32[384,512]{1,0:T(8,128)}, u32[]{:S(2)}, u32[]{:S(2)}) collective-permute-start(f32[384,512]{1,0:T(8,128)} %get-tuple-element.19), channel_id=1, source_target_pairs={{0,1},{1,0},{2,3},{3,2},{4,5},{5,4},{6,7},{7,6},{8,9},{9,8},{10,11... | collective-permute-start | bytes 2359304 | tf_op jit(solution)/shard_map/ppermute | solution.py:296
  43.4 9.0 %collective-permute-start.7 = (bf16[2,64,1152]{2,1,0:T(8,128)(2,1)}, bf16[2,64,1152]{2,1,0:T(8,128)(2,1)S(1)}, u32[]{:S(2)}, u32[]{:S(2)}) collective-permute-start(bf16[2,64,1152]{2,1,0:T(8,128)(2,1)} %hand.3.refs_5_), channel_id=1, source_target_pairs={{0,12},{4,0},{8,4},{12,8},{1,13},{5,1},{9,5},{13,9},{2,14},{6,2},{... | collective-permute-start | bytes 884744 | tf_op jit(solution)/shard_map/ppermute | solution.py:299
  52.4 1.0 %copy-start.3 = (bf16[2,64,1152]{2,1,0:T(8,128)(2,1)S(1)}, bf16[2,64,1152]{2,1,0:T(8,128)(2,1)}, u32[]{:S(2)}) copy-start(bf16[2,64,1152]{2,1,0:T(8,128)(2,1)} %copy-done.2) | copy-start | bytes 884740
  53.3 1.0 %copy-start.5 = (bf16[2,64,1152]{2,1,0:T(8,128)(2,1)S(1)}, bf16[2,64,1152]{2,1,0:T(8,128)(2,1)}, u32[]{:S(2)}) copy-start(bf16[2,64,1152]{2,1,0:T(8,128)(2,1)} %hand.3.refs_5_) | copy-start | bytes 884740
  55.5 13.6 %copy-start.9 = (f32[384,512]{1,0:T(8,128)S(1)}, f32[384,512]{1,0:T(8,128)}, u32[]{:S(2)}) copy-start(f32[384,512]{1,0:T(8,128)} %get-tuple-element.18.base_a) | copy-start | bytes 2359300
  59.8 4.7 %collective-permute-start.11 = (bf16[3,128,128]{2,1,0:T(8,128)(2,1)S(1)}, bf16[3,128,128]{2,1,0:T(8,128)(2,1)S(1)}, u32[]{:S(2)}, u32[]{:S(2)}) collective-permute-start(bf16[3,128,128]{2,1,0:T(8,128)(2,1)S(1)} %get-tuple-element.28), channel_id=1, source_target_pairs={{0,2},{2,0},{16,18},{18,16},{1,3},{3,1},{17,19},{19,17},{4,6},{6,4... | collective-permute-start | bytes 294920 | tf_op jit(solution)/shard_map/ppermute | solution.py:309
  61.2 5.7 %collective-permute-start.12 = (bf16[3,128,128]{2,1,0:T(8,128)(2,1)S(1)}, bf16[3,128,128]{2,1,0:T(8,128)(2,1)S(1)}, u32[]{:S(2)}, u32[]{:S(2)}) collective-permute-start(bf16[3,128,128]{2,1,0:T(8,128)(2,1)S(1)} %get-tuple-element.29), channel_id=1, source_target_pairs={{0,16},{2,18},{16,0},{18,2},{1,17},{3,19},{17,1},{19,3},{4,20},{6,... | collective-permute-start | bytes 294920 | tf_op jit(solution)/shard_map/ppermute | solution.py:309
  62.0 5.8 %collective-permute-start.13 = (bf16[3,128,128]{2,1,0:T(8,128)(2,1)S(1)}, bf16[3,128,128]{2,1,0:T(8,128)(2,1)S(1)}, u32[]{:S(2)}, u32[]{:S(2)}) collective-permute-start(bf16[3,128,128]{2,1,0:T(8,128)(2,1)S(1)} %get-tuple-element.30), channel_id=1, source_target_pairs={{0,18},{2,16},{16,2},{18,0},{1,19},{3,17},{17,3},{19,1},{4,22},{6,... | collective-permute-start | bytes 294920 | tf_op jit(solution)/shard_map/ppermute | solution.py:309
  63.4 4.5 %collective-permute-start.14 = (bf16[3,128,128]{2,1,0:T(8,128)(2,1)S(1)}, bf16[3,128,128]{2,1,0:T(8,128)(2,1)S(1)}, u32[]{:S(2)}, u32[]{:S(2)}) collective-permute-start(bf16[3,128,128]{2,1,0:T(8,128)(2,1)S(1)} %get-tuple-element.27.refs_0_), channel_id=1, source_target_pairs={{0,1},{1,0},{2,3},{3,2},{4,5},{5,4},{6,7},{7,6},{8,9},{9,8},{10,11... | collective-permute-start | bytes 294920 | tf_op jit(solution)/shard_map/ppermute | solution.py:296
  64.5 3.3 %collective-permute-start.15 = (bf16[3,128,128]{2,1,0:T(8,128)(2,1)S(1)}, bf16[3,128,128]{2,1,0:T(8,128)(2,1)S(1)}, u32[]{:S(2)}, u32[]{:S(2)}) collective-permute-start(bf16[3,128,128]{2,1,0:T(8,128)(2,1)S(1)} %collective-permute-done.11.refs_1_), channel_id=1, source_target_pairs={{0,1},{1,0},{2,3},{3,2},{4,5},{5,4},{6,7},{7,6},{8,9},{9,8},{10,11... | collective-permute-start | bytes 294920 | tf_op jit(solution)/shard_map/ppermute | solution.py:296
  66.9 1.3 %collective-permute-start.16 = (bf16[3,128,128]{2,1,0:T(8,128)(2,1)S(1)}, bf16[3,128,128]{2,1,0:T(8,128)(2,1)S(1)}, u32[]{:S(2)}, u32[]{:S(2)}) collective-permute-start(bf16[3,128,128]{2,1,0:T(8,128)(2,1)S(1)} %collective-permute-done.12.refs_2_), channel_id=1, source_target_pairs={{0,1},{1,0},{2,3},{3,2},{4,5},{5,4},{6,7},{7,6},{8,9},{9,8},{10,11... | collective-permute-start | bytes 294920 | tf_op jit(solution)/shard_map/ppermute | solution.py:296
  67.8 1.3 %collective-permute-start.17 = (bf16[3,128,128]{2,1,0:T(8,128)(2,1)S(1)}, bf16[3,128,128]{2,1,0:T(8,128)(2,1)S(1)}, u32[]{:S(2)}, u32[]{:S(2)}) collective-permute-start(bf16[3,128,128]{2,1,0:T(8,128)(2,1)S(1)} %collective-permute-done.13.refs_3_), channel_id=1, source_target_pairs={{0,1},{1,0},{2,3},{3,2},{4,5},{5,4},{6,7},{7,6},{8,9},{9,8},{10,11... | collective-permute-start | bytes 294920 | tf_op jit(solution)/shard_map/ppermute | solution.py:296

commit v23 on v22

--- a/solution.py
+++ b/solution.py
@@ -131,7 +131,8 @@
     )(lengths, ids, tokens)
 
 
-def base_kernel(sides, lengths, tok_ref, key_ref, mine, other, flag_ref, total):
+def base_kernel(sides, lengths, tok_ref, key_ref, *refs):
+    mine, other, flag_ref, total = refs[-4:]
     step = pl.program_id(0)
     part = jnp.dot(tok_ref[...], key_ref[...], preferred_element_type=jnp.float32)
 
@@ -158,7 +159,7 @@
                 out[here, :] = jnp.where(row < lengths[b], total[here, columns], 0.0)
 
 
-def base_halves(tokens, base_key, sides, lengths):
+def base_halves(tokens, base_key, sides, lengths, *after):
     rows, depth = tokens.shape
     features = base_key.shape[1]
     wide = features // sides
@@ -172,7 +173,8 @@
             in_specs=[
                 pl.BlockSpec((rows, step), lambda i, n: (0, i)),
                 pl.BlockSpec((step, features), lambda i, n: (i, 0)),
-            ],
+            ]
+            + [ANY] * len(after),
             out_specs=[half, half, pl.BlockSpec((8, LANES), lambda i, n: (0, 0))],
             scratch_shapes=[pltpu.VMEM((rows, features), jnp.float32)],
         ),
@@ -181,7 +183,7 @@
         cost_estimate=pl.CostEstimate(flops=0, bytes_accessed=0, transcendentals=0),
         compiler_params=FULL,
         name="base",
-    )(lengths, tokens, base_key)
+    )(lengths, tokens, base_key, *after)
 
 
 def collect_kernel(*refs):
@@ -325,15 +327,17 @@
     swapped = [
         lax.ppermute(packed[pair - w], "pair", [(a, (a - w) % pair) for a in range(pair)]) for w in range(1, pair)
     ]
+    swapped = [hand_on(piece, slabs[0]) for piece in swapped]
     firsts = [first_hops(piece) for piece in [packed[0]] + swapped]
     toks = [slabs[0]] + [in_plane(slabs[k], k // pair, k % pair) for k in range(1, shares)]
 
-    base_mine, base_out, flag = base_halves(tokens, base_key, sides, lengths)
     pieces = [
         more_hops(held, way)
         for way, held in enumerate(firsts)
     ]
 
+    sent = [pieces[0][ring - 1], pieces[-1][1]]
+    base_mine, base_out, flag = base_halves(tokens, base_key, sides, lengths, *sent)
     flat = [piece for way in pieces for piece in way]
     parts = rank_parts(owner_slot, flag, toks, collect(flat), ring, pair, rows, blocks)
     mine = [parts[0]] + [in_plane(parts[k], -(k // pair), -(k % pair)) for k in range(1, shares)]

time: 71.8 us -> 73 us (1.017)
  starting transfers between devices: 22.6 us -> 24.4 us
  Pallas kernels: 22.5 us -> 20.8 us
  waiting for transfers between devices: 23.4 us -> 24.8 us
    ppermute x6, waiting for transfers between devices: 11.9 us -> 19.3 us  [along(): lax.ppermute(x, 'ring', [(a, (a + step) % ring) for a in range(ring)])]
    ppermute x1, waiting for transfers between devices: 3.72 us -> 0.01 us  [body(): lax.ppermute(packed[pair - w], 'pair', [(a, (a - w) % pair) for a in rang...]
    ppermute x6, waiting for transfers between devices: 6.44 us -> 4.26 us  [in_plane(): return lax.ppermute(x, PLANE, pairs)]
    ppermute x6, starting transfers between devices: 11.3 us -> 13.2 us  [along(): lax.ppermute(x, 'ring', [(a, (a + step) % ring) for a in range(ring)])]
    pallas_call x1, Pallas kernels: 2.18 us -> 1.05 us  [final(): pl.pallas_call(functools.partial(final_kernel, groups, pair), in_specs=[V...]
    unnamed x26 -> x30, local copies, waits for them, and re-layouts: 2.62 us -> 2.46 us
  transfers between devices with their start and end apart: 18 -> 18, of which waited for: 11 -> 8; matrix products, arithmetic and copies ran while one was open for 0% -> 0% of each run, Pallas kernels for 26% -> 25%
where the time goes in v23:
time: 73 us; the launch traced here: 72.7 us
  waiting for transfers between devices  24.8 us (34%)
  starting transfers between devices  24.4 us (33%)
  Pallas kernels  20.8 us (28%)
  local copies, waits for them, and re-layouts  2.46 us (3%)
    ppermute x6, waiting for transfers between devices, along(): lax.ppermute(x, 'ring', [(a, (a + step) % ring) for a in range(ring)])  19.3 us
    ppermute x6, starting transfers between devices, along(): lax.ppermute(x, 'ring', [(a, (a + step) % ring) for a in range(ring)])  13.2 us
    pallas_call x1, Pallas kernels, base_halves(): pl.pallas_call(functools.partial(base_kernel, sides), grid_spec=pltpu.Pre...  11.4 us
    ppermute x6, starting transfers between devices, in_plane(): return lax.ppermute(x, PLANE, pairs)  8.17 us
    ppermute x6, waiting for transfers between devices, in_plane(): return lax.ppermute(x, PLANE, pairs)  4.26 us
    pallas_call x1, Pallas kernels, spread(): pl.pallas_call(functools.partial(spread_kernel, groups, pair), in_specs=[...  3.65 us
    ppermute x1, starting transfers between devices, body(): lax.ppermute(packed[pair - w], 'pair', [(a, (a - w) % pair) for a in rang...  3.03 us
    unnamed x30, local copies, waits for them, and re-layouts  2.46 us
  transfers between devices with their start and end apart: 18, of which 8 were waited for; matrix products, arithmetic and copies ran while one was open for 0% of the time, Pallas kernels for 25%

profile of v23, /device:TPU:0, one launch (start us, length us, event | category | flops | bytes accessed | tf_op | source)
XLA Modules:
  0.0 72.7 jit_solution(14337916467528650125)
XLA Ops:
  0.0 1.9 %pack.1 = (bf16[2,64,1152]{2,1,0:T(8,128)(2,1)}, bf16[2,64,1152]{2,1,0:T(8,128)(2,1)}) custom-call(bf16[2,64,4096]{2,1,0:T(8,128)(2,1)} %bitcast.2, bf16[2,64,512]{2,1,0:T(8,128)(2,1)} %up.1), custom_call_target="tpu_custom_call" | custom-call | tf_op jit(solution)/shard_map/pack/pallas_call | solution.py:57
  1.9 3.0 %collective-permute-start.2 = (bf16[2,64,1152]{2,1,0:T(8,128)(2,1)}, bf16[2,64,1152]{2,1,0:T(8,128)(2,1)S(1)}, u32[]{:S(2)}, u32[]{:S(2)}) collective-permute-start(bf16[2,64,1152]{2,1,0:T(8,128)(2,1)} %get-tuple-element.19), channel_id=1, source_target_pairs={{0,2},{2,0},{1,3},{3,1},{4,6},{6,4},{5,7},{7,5},{8,10},{10,8},{9,1... | collective-permute-start | bytes 884744 | tf_op jit(solution)/shard_map/ppermute | solution.py:328
  5.0 3.6 %collective-permute-start.1 = (bf16[2,64,1152]{2,1,0:T(8,128)(2,1)}, bf16[2,64,1152]{2,1,0:T(8,128)(2,1)S(1)}, u32[]{:S(2)}, u32[]{:S(2)}) collective-permute-start(bf16[2,64,1152]{2,1,0:T(8,128)(2,1)} %get-tuple-element.18.refs_0_), channel_id=1, source_target_pairs={{0,12},{4,0},{8,4},{12,8},{1,13},{5,1},{9,5},{13,9},{2,14},{6,2},{... | collective-permute-start | bytes 884744 | tf_op jit(solution)/shard_map/ppermute | solution.py:301
  8.6 0.0 collective-permute-start
  8.6 3.6 %spread.1 = (bf16[400,1024]{1,0:T(8,128)(2,1)}, bf16[400,1024]{1,0:T(8,128)(2,1)}, bf16[400,1024]{1,0:T(8,128)(2,1)}, bf16[400,1024]{1,0:T(8,128)(2,1)}) custom-call(s32[3]{0:T(128)} %lengths.3, s32[3]{0:T(128)} %bitcast.3, bf16[384,4096]{1,0:T(8,128)(2,1)} %tok_ref.1), custom_call_target="tpu_custom_call" | custom-call | tf_op jit(solution)/shard_map/spread/pallas_call | solution.py:119
  12.2 0.0 collective-permute-done.2.refs_0_
  12.2 0.7 %copy-done.9 = bf16[2,64,1152]{2,1,0:T(8,128)(2,1)} copy-done((bf16[2,64,1152]{2,1,0:T(8,128)(2,1)}, bf16[2,64,1152]{2,1,0:T(8,128)(2,1)S(1)}, u32[]{:S(2)}) %copy-start.9) | copy-done | bytes 294936
  13.0 1.7 %collective-permute-start.4 = (bf16[2,64,1152]{2,1,0:T(8,128)(2,1)}, bf16[2,64,1152]{2,1,0:T(8,128)(2,1)S(1)}, u32[]{:S(2)}, u32[]{:S(2)}) collective-permute-start(bf16[2,64,1152]{2,1,0:T(8,128)(2,1)} %hand.4.refs_4_), channel_id=1, source_target_pairs={{0,4},{4,8},{8,12},{12,0},{1,5},{5,9},{9,13},{13,1},{2,6},{6,10},{... | collective-permute-start | bytes 884744 | tf_op jit(solution)/shard_map/ppermute | solution.py:301
  14.7 2.1 %collective-permute-start.3 = (bf16[2,64,1152]{2,1,0:T(8,128)(2,1)}, bf16[2,64,1152]{2,1,0:T(8,128)(2,1)S(1)}, u32[]{:S(2)}, u32[]{:S(2)}) collective-permute-start(bf16[2,64,1152]{2,1,0:T(8,128)(2,1)} %hand.4.refs_4_), channel_id=1, source_target_pairs={{0,12},{4,0},{8,4},{12,8},{1,13},{5,1},{9,5},{13,9},{2,14},{6,2},{... | collective-permute-start | bytes 884744 | tf_op jit(solution)/shard_map/ppermute | solution.py:301
  16.8 1.7 %collective-permute-start.8 = (bf16[400,1024]{1,0:T(8,128)(2,1)}, bf16[400,1024]{1,0:T(8,128)(2,1)S(1)}, u32[]{:S(2)}, u32[]{:S(2)}) collective-permute-start(bf16[400,1024]{1,0:T(8,128)(2,1)} %get-tuple-element.24), channel_id=1, source_target_pairs={{0,2},{2,0},{16,18},{18,16},{1,3},{3,1},{17,19},{19,17},{4,6},{6,4... | collective-permute-start | bytes 2457608 | tf_op jit(solution)/shard_map/ppermute | solution.py:311
  18.5 0.0 collective-permute-done.1.refs_1_
  18.5 1.5 %collective-permute-start.9 = (bf16[400,1024]{1,0:T(8,128)(2,1)}, bf16[400,1024]{1,0:T(8,128)(2,1)S(1)}, u32[]{:S(2)}, u32[]{:S(2)}) collective-permute-start(bf16[400,1024]{1,0:T(8,128)(2,1)} %get-tuple-element.25), channel_id=1, source_target_pairs={{0,16},{2,18},{16,0},{18,2},{1,17},{3,19},{17,1},{19,3},{4,20},{6,... | collective-permute-start | bytes 2457608 | tf_op jit(solution)/shard_map/ppermute | solution.py:311
  20.0 3.6 %collective-permute-done.refs_0_ = bf16[2,64,1152]{2,1,0:T(8,128)(2,1)S(1)} collective-permute-done((bf16[2,64,1152]{2,1,0:T(8,128)(2,1)}, bf16[2,64,1152]{2,1,0:T(8,128)(2,1)S(1)}, u32[]{:S(2)}, u32[]{:S(2)}) %collective-permute-start) | collective-permute-done | bytes 294944 | tf_op jit(solution)/shard_map/ppermute | solution.py:301
  23.6 1.4 %collective-permute-start.10 = (bf16[400,1024]{1,0:T(8,128)(2,1)}, bf16[400,1024]{1,0:T(8,128)(2,1)S(1)}, u32[]{:S(2)}, u32[]{:S(2)}) collective-permute-start(bf16[400,1024]{1,0:T(8,128)(2,1)} %get-tuple-element.26), channel_id=1, source_target_pairs={{0,18},{2,16},{16,2},{18,0},{1,19},{3,17},{17,3},{19,1},{4,22},{6,... | collective-permute-start | bytes 2457608 | tf_op jit(solution)/shard_map/ppermute | solution.py:311
  25.1 4.8 %collective-permute-done.4.refs_1_.refs_7_ = bf16[2,64,1152]{2,1,0:T(8,128)(2,1)S(1)} collective-permute-done((bf16[2,64,1152]{2,1,0:T(8,128)(2,1)}, bf16[2,64,1152]{2,1,0:T(8,128)(2,1)S(1)}, u32[]{:S(2)}, u32[]{:S(2)}) %collective-permute-start.4) | collective-permute-done | bytes 294944 | tf_op jit(solution)/shard_map/ppermute | solution.py:301
  29.8 1.5 %collective-permute-start.6 = (bf16[2,64,1152]{2,1,0:T(8,128)(2,1)}, bf16[2,64,1152]{2,1,0:T(8,128)(2,1)}, u32[]{:S(2)}, u32[]{:S(2)}) collective-permute-start(bf16[2,64,1152]{2,1,0:T(8,128)(2,1)} %hand.3.refs_0_.refs_3_), channel_id=1, source_target_pairs={{0,4},{4,8},{8,12},{12,0},{1,5},{5,9},{9,13},{13,1},{2,6},{6,10},{... | collective-permute-start | bytes 884744 | tf_op jit(solution)/shard_map/ppermute | solution.py:301
  31.4 4.0 %collective-permute-done.3.refs_0_ = bf16[2,64,1152]{2,1,0:T(8,128)(2,1)S(1)} collective-permute-done((bf16[2,64,1152]{2,1,0:T(8,128)(2,1)}, bf16[2,64,1152]{2,1,0:T(8,128)(2,1)S(1)}, u32[]{:S(2)}, u32[]{:S(2)}) %collective-permute-start.3) | collective-permute-done | bytes 294944 | tf_op jit(solution)/shard_map/ppermute | solution.py:301
  35.3 0.0 copy-done.7
  35.3 0.7 copy-done.3
  36.1 0.0 copy-start.14
  36.1 11.4 %base.1 = (f32[384,512]{1,0:T(8,128)}, f32[384,512]{1,0:T(8,128)}, f32[8,128]{1,0:T(8,128)}) custom-call(s32[3]{0:T(128)} %lengths.3, bf16[384,4096]{1,0:T(8,128)(2,1)} %tok_ref.1, bf16[4096,1024]{1,0:T(8,128)(2,1)} %key_ref.1, bf16[2,64,1152]{2,1,0:T(8,128)(2,1)} %hand.3.refs_0_.refs_3_, bf16[2,64,1152]{2,1,0:T(8,128)(2,1)} %hand.5.refs_1_.refs_5_), custom_call_target="tpu_custom_call" | custom-call | tf_op jit(solution)/shard_map/base/pallas_call | solution.py:168
  47.5 0.0 collective-permute-start.5
  47.5 0.0 collective-permute-done.6.refs_2_
  47.5 4.2 %collective-permute-start.7 = (bf16[2,64,1152]{2,1,0:T(8,128)(2,1)S(1)}, bf16[2,64,1152]{2,1,0:T(8,128)(2,1)S(1)}, u32[]{:S(2)}, u32[]{:S(2)}) collective-permute-start(bf16[2,64,1152]{2,1,0:T(8,128)(2,1)S(1)} %copy-done.4), channel_id=1, source_target_pairs={{0,12},{4,0},{8,4},{12,8},{1,13},{5,1},{9,5},{13,9},{2,14},{6,2},{... | collective-permute-start | bytes 884744 | tf_op jit(solution)/shard_map/ppermute | solution.py:301
  51.7 6.9 %collective-permute-done.7.refs_6_ = bf16[2,64,1152]{2,1,0:T(8,128)(2,1)S(1)} collective-permute-done((bf16[2,64,1152]{2,1,0:T(8,128)(2,1)S(1)}, bf16[2,64,1152]{2,1,0:T(8,128)(2,1)S(1)}, u32[]{:S(2)}, u32[]{:S(2)}) %collective-permute-start.7) | collective-permute-done | bytes 294944 | tf_op jit(solution)/shard_map/ppermute | solution.py:301
  58.6 0.0 copy-start.12
  58.6 1.0 %copy-done.12 = bf16[2,64,1152]{2,1,0:T(8,128)(2,1)S(1)} copy-done((bf16[2,64,1152]{2,1,0:T(8,128)(2,1)S(1)}, bf16[2,64,1152]{2,1,0:T(8,128)(2,1)}, u32[]{:S(2)}) %copy-start.12) | copy-done | bytes 294936
  59.6 1.2 %collect.1.held = bf16[16,64,1152]{2,1,0:T(8,128)(2,1)S(1)} custom-call(bf16[2,64,1152]{2,1,0:T(8,128)(2,1)S(1)} %copy-done.12, bf16[2,64,1152]{2,1,0:T(8,128)(2,1)S(1)} %copy-done.6, bf16[2,64,1152]{2,1,0:T(8,128)(2,1)} %collective-permute-done.6.refs_2_, bf16[2,64,1152]{2,1,0:T(8,128)(2,1)S(1)} %copy-done.2, bf16[2,64,1152]{2,1,0:T(8,128)(2,1)S(1)} %copy-done.10, ...), custom_call_target="tpu_custom_call" | custom-call | tf_op jit(solution)/shard_map/collect/pallas_call | solution.py:203
  60.8 0.0 collective-permute-done.8.refs_1_
  60.8 0.0 collective-permute-done.9.refs_2_
  60.8 0.0 collective-permute-done.10.refs_3_
  60.8 1.6 %rank.1 = (bf16[3,128,128]{2,1,0:T(8,128)(2,1)S(1)}, bf16[3,128,128]{2,1,0:T(8,128)(2,1)S(1)}, bf16[3,128,128]{2,1,0:T(8,128)(2,1)S(1)}, bf16[3,128,128]{2,1,0:T(8,128)(2,1)S(1)}) custom-call(s32[16]{0:T(128)S(1)} %copy-done.14, f32[8,128]{1,0:T(8,128)S(1)} %copy-done.13, bf16[16,64,1152]{2,1,0:T(8,128)(2,1)S(1)} %collect.1.held, ...), custom_call_target="tpu_custom_call" | custom-call | tf_op jit(solution)/shard_map/rank/pallas_call | solution.py:246
  62.5 0.6 collective-permute-start.11
  63.0 1.5 %collective-permute-start.12 = (bf16[3,128,128]{2,1,0:T(8,128)(2,1)S(1)}, bf16[3,128,128]{2,1,0:T(8,128)(2,1)S(1)}, u32[]{:S(2)}, u32[]{:S(2)}) collective-permute-start(bf16[3,128,128]{2,1,0:T(8,128)(2,1)S(1)} %get-tuple-element.29), channel_id=1, source_target_pairs={{0,16},{2,18},{16,0},{18,2},{1,17},{3,19},{17,1},{19,3},{4,20},{6,... | collective-permute-start | bytes 294920 | tf_op jit(solution)/shard_map/ppermute | solution.py:311
  64.5 1.5 %collective-permute-start.13 = (bf16[3,128,128]{2,1,0:T(8,128)(2,1)S(1)}, bf16[3,128,128]{2,1,0:T(8,128)(2,1)S(1)}, u32[]{:S(2)}, u32[]{:S(2)}) collective-permute-start(bf16[3,128,128]{2,1,0:T(8,128)(2,1)S(1)} %get-tuple-element.30), channel_id=1, source_target_pairs={{0,18},{2,16},{16,2},{18,0},{1,19},{3,17},{17,3},{19,1},{4,22},{6,... | collective-permute-start | bytes 294920 | tf_op jit(solution)/shard_map/ppermute | solution.py:311
  66.0 0.0 collective-permute-start.14
  66.0 1.1 %collective-permute-done.11.refs_1_ = bf16[3,128,128]{2,1,0:T(8,128)(2,1)S(1)} collective-permute-done((bf16[3,128,128]{2,1,0:T(8,128)(2,1)S(1)}, bf16[3,128,128]{2,1,0:T(8,128)(2,1)S(1)}, u32[]{:S(2)}, u32[]{:S(2)}) %collective-permute-start.11) | collective-permute-done | bytes 98336 | tf_op jit(solution)/shard_map/ppermute | solution.py:311
  67.2 0.0 collective-permute-start.15
  67.2 1.0 %collective-permute-done.12.refs_2_ = bf16[3,128,128]{2,1,0:T(8,128)(2,1)S(1)} collective-permute-done((bf16[3,128,128]{2,1,0:T(8,128)(2,1)S(1)}, bf16[3,128,128]{2,1,0:T(8,128)(2,1)S(1)}, u32[]{:S(2)}, u32[]{:S(2)}) %collective-permute-start.12) | collective-permute-done | bytes 98336 | tf_op jit(solution)/shard_map/ppermute | solution.py:311
  68.2 0.0 collective-permute-start.16
  68.2 2.1 %collective-permute-done.13.refs_3_ = bf16[3,128,128]{2,1,0:T(8,128)(2,1)S(1)} collective-permute-done((bf16[3,128,128]{2,1,0:T(8,128)(2,1)S(1)}, bf16[3,128,128]{2,1,0:T(8,128)(2,1)S(1)}, u32[]{:S(2)}, u32[]{:S(2)}) %collective-permute-start.13) | collective-permute-done | bytes 98336 | tf_op jit(solution)/shard_map/ppermute | solution.py:311
  70.3 0.0 collective-permute-start.17
  70.3 0.0 collective-permute-done.14.refs_4_
  70.3 0.0 collective-permute-done.15.refs_5_
  70.3 0.0 collective-permute-done.16.refs_6_
  70.3 1.3 %collective-permute-done.17.refs_7_ = bf16[3,128,128]{2,1,0:T(8,128)(2,1)S(1)} collective-permute-done((bf16[3,128,128]{2,1,0:T(8,128)(2,1)S(1)}, bf16[3,128,128]{2,1,0:T(8,128)(2,1)S(1)}, u32[]{:S(2)}, u32[]{:S(2)}) %collective-permute-start.17) | collective-permute-done | bytes 98336 | tf_op jit(solution)/shard_map/ppermute | solution.py:298
  71.6 0.0 collective-permute-done.5.base_b
  71.6 1.1 %final.1 = bf16[384,512]{1,0:T(8,128)(2,1)} custom-call(f32[384,512]{1,0:T(8,128)S(1)} %copy-done.11, f32[384,512]{1,0:T(8,128)S(1)} %collective-permute-done.5.base_b, bf16[3,128,128]{2,1,0:T(8,128)(2,1)S(1)} %get-tuple-element.27.refs_0_, bf16[3,128,128]{2,1,0:T(8,128)(2,1)S(1)} %collective-permute-done.11.refs_1_, ...), custom_call_target="tpu_custom_call" | custom-call | tf_op jit(solution)/shard_map/final/pallas_call | solution.py:279
  (27 shorter events, 0.0 us)
Async XLA Ops:
  1.9 10.3 %collective-permute-start.2 = (bf16[2,64,1152]{2,1,0:T(8,128)(2,1)}, bf16[2,64,1152]{2,1,0:T(8,128)(2,1)S(1)}, u32[]{:S(2)}, u32[]{:S(2)}) collective-permute-start(bf16[2,64,1152]{2,1,0:T(8,128)(2,1)} %get-tuple-element.19), channel_id=1, source_target_pairs={{0,2},{2,0},{1,3},{3,1},{4,6},{6,4},{5,7},{7,5},{8,10},{10,8},{9,1... | collective-permute-start | bytes 884744 | tf_op jit(solution)/shard_map/ppermute | solution.py:328
  5.0 13.5 %collective-permute-start.1 = (bf16[2,64,1152]{2,1,0:T(8,128)(2,1)}, bf16[2,64,1152]{2,1,0:T(8,128)(2,1)S(1)}, u32[]{:S(2)}, u32[]{:S(2)}) collective-permute-start(bf16[2,64,1152]{2,1,0:T(8,128)(2,1)} %get-tuple-element.18.refs_0_), channel_id=1, source_target_pairs={{0,12},{4,0},{8,4},{12,8},{1,13},{5,1},{9,5},{13,9},{2,14},{6,2},{... | collective-permute-start | bytes 884744 | tf_op jit(solution)/shard_map/ppermute | solution.py:301
  8.6 15.0 %collective-permute-start = (bf16[2,64,1152]{2,1,0:T(8,128)(2,1)}, bf16[2,64,1152]{2,1,0:T(8,128)(2,1)S(1)}, u32[]{:S(2)}, u32[]{:S(2)}) collective-permute-start(bf16[2,64,1152]{2,1,0:T(8,128)(2,1)} %get-tuple-element.18.refs_0_), channel_id=1, source_target_pairs={{0,4},{4,8},{8,12},{12,0},{1,5},{5,9},{9,13},{13,1},{2,6},{6,10},{... | collective-permute-start | bytes 884744 | tf_op jit(solution)/shard_map/ppermute | solution.py:301
  12.2 0.7 %copy-start.9 = (bf16[2,64,1152]{2,1,0:T(8,128)(2,1)}, bf16[2,64,1152]{2,1,0:T(8,128)(2,1)S(1)}, u32[]{:S(2)}) copy-start(bf16[2,64,1152]{2,1,0:T(8,128)(2,1)S(1)} %collective-permute-done.2.refs_0_) | copy-start | bytes 884740
  13.0 16.8 %collective-permute-start.4 = (bf16[2,64,1152]{2,1,0:T(8,128)(2,1)}, bf16[2,64,1152]{2,1,0:T(8,128)(2,1)S(1)}, u32[]{:S(2)}, u32[]{:S(2)}) collective-permute-start(bf16[2,64,1152]{2,1,0:T(8,128)(2,1)} %hand.4.refs_4_), channel_id=1, source_target_pairs={{0,4},{4,8},{8,12},{12,0},{1,5},{5,9},{9,13},{13,1},{2,6},{6,10},{... | collective-permute-start | bytes 884744 | tf_op jit(solution)/shard_map/ppermute | solution.py:301
  14.7 20.6 %collective-permute-start.3 = (bf16[2,64,1152]{2,1,0:T(8,128)(2,1)}, bf16[2,64,1152]{2,1,0:T(8,128)(2,1)S(1)}, u32[]{:S(2)}, u32[]{:S(2)}) collective-permute-start(bf16[2,64,1152]{2,1,0:T(8,128)(2,1)} %hand.4.refs_4_), channel_id=1, source_target_pairs={{0,12},{4,0},{8,4},{12,8},{1,13},{5,1},{9,5},{13,9},{2,14},{6,2},{... | collective-permute-start | bytes 884744 | tf_op jit(solution)/shard_map/ppermute | solution.py:301
  16.8 44.0 %collective-permute-start.8 = (bf16[400,1024]{1,0:T(8,128)(2,1)}, bf16[400,1024]{1,0:T(8,128)(2,1)S(1)}, u32[]{:S(2)}, u32[]{:S(2)}) collective-permute-start(bf16[400,1024]{1,0:T(8,128)(2,1)} %get-tuple-element.24), channel_id=1, source_target_pairs={{0,2},{2,0},{16,18},{18,16},{1,3},{3,1},{17,19},{19,17},{4,6},{6,4... | collective-permute-start | bytes 2457608 | tf_op jit(solution)/shard_map/ppermute | solution.py:311
  18.5 6.6 %copy-start.5 = (bf16[2,64,1152]{2,1,0:T(8,128)(2,1)}, bf16[2,64,1152]{2,1,0:T(8,128)(2,1)S(1)}, u32[]{:S(2)}) copy-start(bf16[2,64,1152]{2,1,0:T(8,128)(2,1)S(1)} %collective-permute-done.1.refs_1_) | copy-start | bytes 884740
  18.5 42.3 %collective-permute-start.9 = (bf16[400,1024]{1,0:T(8,128)(2,1)}, bf16[400,1024]{1,0:T(8,128)(2,1)S(1)}, u32[]{:S(2)}, u32[]{:S(2)}) collective-permute-start(bf16[400,1024]{1,0:T(8,128)(2,1)} %get-tuple-element.25), channel_id=1, source_target_pairs={{0,16},{2,18},{16,0},{18,2},{1,17},{3,19},{17,1},{19,3},{4,20},{6,... | collective-permute-start | bytes 2457608 | tf_op jit(solution)/shard_map/ppermute | solution.py:311
  23.6 1.4 %copy-start.1 = (bf16[2,64,1152]{2,1,0:T(8,128)(2,1)}, bf16[2,64,1152]{2,1,0:T(8,128)(2,1)S(1)}, u32[]{:S(2)}) copy-start(bf16[2,64,1152]{2,1,0:T(8,128)(2,1)S(1)} %collective-permute-done.refs_0_) | copy-start | bytes 884740
  23.6 37.2 %collective-permute-start.10 = (bf16[400,1024]{1,0:T(8,128)(2,1)}, bf16[400,1024]{1,0:T(8,128)(2,1)S(1)}, u32[]{:S(2)}, u32[]{:S(2)}) collective-permute-start(bf16[400,1024]{1,0:T(8,128)(2,1)} %get-tuple-element.26), channel_id=1, source_target_pairs={{0,18},{2,16},{16,2},{18,0},{1,19},{3,17},{17,3},{19,1},{4,22},{6,... | collective-permute-start | bytes 2457608 | tf_op jit(solution)/shard_map/ppermute | solution.py:311
  29.8 5.5 %copy-start.7 = (bf16[2,64,1152]{2,1,0:T(8,128)(2,1)}, bf16[2,64,1152]{2,1,0:T(8,128)(2,1)S(1)}, u32[]{:S(2)}) copy-start(bf16[2,64,1152]{2,1,0:T(8,128)(2,1)S(1)} %collective-permute-done.4.refs_1_.refs_7_) | copy-start | bytes 884740
  29.8 17.7 %collective-permute-start.6 = (bf16[2,64,1152]{2,1,0:T(8,128)(2,1)}, bf16[2,64,1152]{2,1,0:T(8,128)(2,1)}, u32[]{:S(2)}, u32[]{:S(2)}) collective-permute-start(bf16[2,64,1152]{2,1,0:T(8,128)(2,1)} %hand.3.refs_0_.refs_3_), channel_id=1, source_target_pairs={{0,4},{4,8},{8,12},{12,0},{1,5},{5,9},{9,13},{13,1},{2,6},{6,10},{... | collective-permute-start | bytes 884744 | tf_op jit(solution)/shard_map/ppermute | solution.py:301
  35.3 0.7 copy-start.3
  36.1 11.4 %copy-start.4 = (bf16[2,64,1152]{2,1,0:T(8,128)(2,1)S(1)}, bf16[2,64,1152]{2,1,0:T(8,128)(2,1)}, u32[]{:S(2)}) copy-start(bf16[2,64,1152]{2,1,0:T(8,128)(2,1)} %hand.5.refs_1_.refs_5_) | copy-start | bytes 884740
  36.1 22.5 %copy-start.2 = (bf16[2,64,1152]{2,1,0:T(8,128)(2,1)S(1)}, bf16[2,64,1152]{2,1,0:T(8,128)(2,1)}, u32[]{:S(2)}) copy-start(bf16[2,64,1152]{2,1,0:T(8,128)(2,1)} %hand.3.refs_0_.refs_3_) | copy-start | bytes 884740
  36.1 22.5 %copy-start.6 = (bf16[2,64,1152]{2,1,0:T(8,128)(2,1)S(1)}, bf16[2,64,1152]{2,1,0:T(8,128)(2,1)}, u32[]{:S(2)}) copy-start(bf16[2,64,1152]{2,1,0:T(8,128)(2,1)} %copy-done.5) | copy-start | bytes 884740
  36.1 22.5 %copy-start.8 = (bf16[2,64,1152]{2,1,0:T(8,128)(2,1)S(1)}, bf16[2,64,1152]{2,1,0:T(8,128)(2,1)}, u32[]{:S(2)}) copy-start(bf16[2,64,1152]{2,1,0:T(8,128)(2,1)} %copy-done.7) | copy-start | bytes 884740
  36.1 22.5 %copy-start.10 = (bf16[2,64,1152]{2,1,0:T(8,128)(2,1)S(1)}, bf16[2,64,1152]{2,1,0:T(8,128)(2,1)}, u32[]{:S(2)}) copy-start(bf16[2,64,1152]{2,1,0:T(8,128)(2,1)} %hand.4.refs_4_) | copy-start | bytes 884740
  36.1 24.7 %copy-start.14 = (s32[16]{0:T(128)S(1)}, s32[16]{0:T(128)}, u32[]{:S(2)}) copy-start(s32[16]{0:T(128)} %owner.1) | copy-start | bytes 196
  47.5 13.3 %copy-start = (bf16[400,1024]{1,0:T(8,128)(2,1)S(1)}, bf16[400,1024]{1,0:T(8,128)(2,1)}, u32[]{:S(2)}) copy-start(bf16[400,1024]{1,0:T(8,128)(2,1)} %get-tuple-element.20.refs_1_.refs_0_) | copy-start | bytes 2457604
  47.5 24.1 %collective-permute-start.5 = (f32[384,512]{1,0:T(8,128)}, f32[384,512]{1,0:T(8,128)S(1)}, u32[]{:S(2)}, u32[]{:S(2)}) collective-permute-start(f32[384,512]{1,0:T(8,128)} %get-tuple-element.22), channel_id=1, source_target_pairs={{0,1},{1,0},{2,3},{3,2},{4,5},{5,4},{6,7},{7,6},{8,9},{9,8},{10,11... | collective-permute-start | bytes 2359304 | tf_op jit(solution)/shard_map/ppermute | solution.py:298
  47.5 11.1 %collective-permute-start.7 = (bf16[2,64,1152]{2,1,0:T(8,128)(2,1)S(1)}, bf16[2,64,1152]{2,1,0:T(8,128)(2,1)S(1)}, u32[]{:S(2)}, u32[]{:S(2)}) collective-permute-start(bf16[2,64,1152]{2,1,0:T(8,128)(2,1)S(1)} %copy-done.4), channel_id=1, source_target_pairs={{0,12},{4,0},{8,4},{12,8},{1,13},{5,1},{9,5},{13,9},{2,14},{6,2},{... | collective-permute-start | bytes 884744 | tf_op jit(solution)/shard_map/ppermute | solution.py:301
  58.6 1.0 %copy-start.12 = (bf16[2,64,1152]{2,1,0:T(8,128)(2,1)S(1)}, bf16[2,64,1152]{2,1,0:T(8,128)(2,1)}, u32[]{:S(2)}) copy-start(bf16[2,64,1152]{2,1,0:T(8,128)(2,1)} %get-tuple-element.18.refs_0_) | copy-start | bytes 884740
  59.6 1.2 %copy-start.13 = (f32[8,128]{1,0:T(8,128)S(1)}, f32[8,128]{1,0:T(8,128)}, u32[]{:S(2)}) copy-start(f32[8,128]{1,0:T(8,128)} %get-tuple-element.23.flag) | copy-start | bytes 12292
  60.8 10.8 %copy-start.11 = (f32[384,512]{1,0:T(8,128)S(1)}, f32[384,512]{1,0:T(8,128)}, u32[]{:S(2)}) copy-start(f32[384,512]{1,0:T(8,128)} %get-tuple-element.21.base_a) | copy-start | bytes 2359300
  62.5 4.7 %collective-permute-start.11 = (bf16[3,128,128]{2,1,0:T(8,128)(2,1)S(1)}, bf16[3,128,128]{2,1,0:T(8,128)(2,1)S(1)}, u32[]{:S(2)}, u32[]{:S(2)}) collective-permute-start(bf16[3,128,128]{2,1,0:T(8,128)(2,1)S(1)} %get-tuple-element.28), channel_id=1, source_target_pairs={{0,2},{2,0},{16,18},{18,16},{1,3},{3,1},{17,19},{19,17},{4,6},{6,4... | collective-permute-start | bytes 294920 | tf_op jit(solution)/shard_map/ppermute | solution.py:311
  63.0 5.1 %collective-permute-start.12 = (bf16[3,128,128]{2,1,0:T(8,128)(2,1)S(1)}, bf16[3,128,128]{2,1,0:T(8,128)(2,1)S(1)}, u32[]{:S(2)}, u32[]{:S(2)}) collective-permute-start(bf16[3,128,128]{2,1,0:T(8,128)(2,1)S(1)} %get-tuple-element.29), channel_id=1, source_target_pairs={{0,16},{2,18},{16,0},{18,2},{1,17},{3,19},{17,1},{19,3},{4,20},{6,... | collective-permute-start | bytes 294920 | tf_op jit(solution)/shard_map/ppermute | solution.py:311
  64.5 5.8 %collective-permute-start.13 = (bf16[3,128,128]{2,1,0:T(8,128)(2,1)S(1)}, bf16[3,128,128]{2,1,0:T(8,128)(2,1)S(1)}, u32[]{:S(2)}, u32[]{:S(2)}) collective-permute-start(bf16[3,128,128]{2,1,0:T(8,128)(2,1)S(1)} %get-tuple-element.30), channel_id=1, source_target_pairs={{0,18},{2,16},{16,2},{18,0},{1,19},{3,17},{17,3},{19,1},{4,22},{6,... | collective-permute-start | bytes 294920 | tf_op jit(solution)/shard_map/ppermute | solution.py:311
  66.0 4.3 %collective-permute-start.14 = (bf16[3,128,128]{2,1,0:T(8,128)(2,1)S(1)}, bf16[3,128,128]{2,1,0:T(8,128)(2,1)S(1)}, u32[]{:S(2)}, u32[]{:S(2)}) collective-permute-start(bf16[3,128,128]{2,1,0:T(8,128)(2,1)S(1)} %get-tuple-element.27.refs_0_), channel_id=1, source_target_pairs={{0,1},{1,0},{2,3},{3,2},{4,5},{5,4},{6,7},{7,6},{8,9},{9,8},{10,11... | collective-permute-start | bytes 294920 | tf_op jit(solution)/shard_map/ppermute | solution.py:298
  67.2 3.1 %collective-permute-start.15 = (bf16[3,128,128]{2,1,0:T(8,128)(2,1)S(1)}, bf16[3,128,128]{2,1,0:T(8,128)(2,1)S(1)}, u32[]{:S(2)}, u32[]{:S(2)}) collective-permute-start(bf16[3,128,128]{2,1,0:T(8,128)(2,1)S(1)} %collective-permute-done.11.refs_1_), channel_id=1, source_target_pairs={{0,1},{1,0},{2,3},{3,2},{4,5},{5,4},{6,7},{7,6},{8,9},{9,8},{10,11... | collective-permute-start | bytes 294920 | tf_op jit(solution)/shard_map/ppermute | solution.py:298
  68.2 2.1 %collective-permute-start.16 = (bf16[3,128,128]{2,1,0:T(8,128)(2,1)S(1)}, bf16[3,128,128]{2,1,0:T(8,128)(2,1)S(1)}, u32[]{:S(2)}, u32[]{:S(2)}) collective-permute-start(bf16[3,128,128]{2,1,0:T(8,128)(2,1)S(1)} %collective-permute-done.12.refs_2_), channel_id=1, source_target_pairs={{0,1},{1,0},{2,3},{3,2},{4,5},{5,4},{6,7},{7,6},{8,9},{9,8},{10,11... | collective-permute-start | bytes 294920 | tf_op jit(solution)/shard_map/ppermute | solution.py:298
  70.3 1.3 %collective-permute-start.17 = (bf16[3,128,128]{2,1,0:T(8,128)(2,1)S(1)}, bf16[3,128,128]{2,1,0:T(8,128)(2,1)S(1)}, u32[]{:S(2)}, u32[]{:S(2)}) collective-permute-start(bf16[3,128,128]{2,1,0:T(8,128)(2,1)S(1)} %collective-permute-done.13.refs_3_), channel_id=1, source_target_pairs={{0,1},{1,0},{2,3},{3,2},{4,5},{5,4},{6,7},{7,6},{8,9},{9,8},{10,11... | collective-permute-start | bytes 294920 | tf_op jit(solution)/shard_map/ppermute | solution.py:298

commit v24 on v19

--- a/solution.py
+++ b/solution.py
@@ -131,53 +131,67 @@
     )(lengths, ids, tokens)
 
 
-def base_kernel(sides, lengths, tok_ref, key_ref, mine, other, flag_ref, total):
-    step = pl.program_id(0)
-    part = jnp.dot(tok_ref[...], key_ref[...], preferred_element_type=jnp.float32)
-
-    @pl.when(step == 0)
-    def _():
-        total[...] = part
-
-    @pl.when(step > 0)
-    def _():
-        total[...] += part
-
-    @pl.when(step == pl.num_programs(0) - 1)
-    def _():
-        flag_ref[...] = jnp.zeros_like(flag_ref)
-        blocks = lengths.shape[0]
-        rows, wide = mine.shape
-        block = rows // blocks
-        row = lax.broadcasted_iota(jnp.int32, (block, wide), 0)
-        t = lax.axis_index("tensor")
-        for out, side in ((mine, t), (other, lax.rem(t + 1, sides))):
-            columns = pl.ds(pl.multiple_of(side * wide, LANES), wide)
-            for b in range(blocks):
-                here = slice(b * block, (b + 1) * block)
-                out[here, :] = jnp.where(row < lengths[b], total[here, columns], 0.0)
+def base_kernel(sides, lengths, tok, key, mine, other, flag_ref, tok_held, key_held, total, tok_sems, key_sems):
+    depth, rows = key.shape[0], tok.shape[0]
+    chunk = depth // key_sems.shape[0]
+    steps = tok_sems.shape[0]
+    step = depth // steps
+
+    def key_copy(i):
+        here = pl.ds(i * chunk, chunk)
+        return pltpu.make_async_copy(key.at[here, :], key_held.at[here, :], key_sems.at[i])
+
+    def tok_copy(i, b):
+        here = pl.ds(i * step, step)
+        some = pl.ds(b * (rows // tok_sems.shape[1]), rows // tok_sems.shape[1])
+        return pltpu.make_async_copy(tok.at[some, here], tok_held.at[some, here], tok_sems.at[i, b])
+
+    flag_ref[...] = jnp.zeros_like(flag_ref)
+    for i in range(steps):
+        for b in range(tok_sems.shape[1]):
+            tok_copy(i, b).start()
+        for j in range(step // chunk):
+            key_copy(i * (step // chunk) + j).start()
+    for i in range(steps):
+        for b in range(tok_sems.shape[1]):
+            tok_copy(i, b).wait()
+        for j in range(step // chunk):
+            key_copy(i * (step // chunk) + j).wait()
+        here = slice(i * step, (i + 1) * step)
+        part = jnp.dot(tok_held[:, here], key_held[here, :], preferred_element_type=jnp.float32)
+        if i == 0:
+            total[...] = part
+        else:
+            total[...] += part
+    blocks = lengths.shape[0]
+    wide = mine.shape[1]
+    block = rows // blocks
+    row = lax.broadcasted_iota(jnp.int32, (block, wide), 0)
+    t = lax.axis_index("tensor")
+    for out, side in ((mine, t), (other, lax.rem(t + 1, sides))):
+        columns = pl.ds(pl.multiple_of(side * wide, LANES), wide)
+        for b in range(blocks):
+            here = slice(b * block, (b + 1) * block)
+            out[here, :] = jnp.where(row < lengths[b], total[here, columns], 0.0)
 
 
 def base_halves(tokens, base_key, sides, lengths):
     rows, depth = tokens.shape
     features = base_key.shape[1]
-    wide = features // sides
-    step = 512
-    half = pl.BlockSpec((rows, wide), lambda i, n: (0, 0))
+    half = jax.ShapeDtypeStruct((rows, features // sides), jnp.float32)
+    steps, chunks = depth // 1024, depth // 256
     return pl.pallas_call(
         functools.partial(base_kernel, sides),
-        grid_spec=pltpu.PrefetchScalarGridSpec(
-            num_scalar_prefetch=1,
-            grid=(depth // step,),
-            in_specs=[
-                pl.BlockSpec((rows, step), lambda i, n: (0, i)),
-                pl.BlockSpec((step, features), lambda i, n: (i, 0)),
-            ],
-            out_specs=[half, half, pl.BlockSpec((8, LANES), lambda i, n: (0, 0))],
-            scratch_shapes=[pltpu.VMEM((rows, features), jnp.float32)],
-        ),
-        out_shape=[jax.ShapeDtypeStruct((rows, wide), jnp.float32)] * 2
-        + [jax.ShapeDtypeStruct((8, LANES), jnp.float32)],
+        in_specs=[SMEM, ANY, ANY],
+        out_specs=[VMEM] * 3,
+        out_shape=[half, half, jax.ShapeDtypeStruct((8, LANES), jnp.float32)],
+        scratch_shapes=[
+            pltpu.VMEM(tokens.shape, tokens.dtype),
+            pltpu.VMEM(base_key.shape, base_key.dtype),
+            pltpu.VMEM((rows, features), jnp.float32),
+            pltpu.SemaphoreType.DMA((steps, lengths.shape[0])),
+            pltpu.SemaphoreType.DMA((chunks,)),
+        ],
         cost_estimate=pl.CostEstimate(flops=0, bytes_accessed=0, transcendentals=0),
         compiler_params=FULL,
         name="base",

time: 69.9 us -> 66.8 us (0.956)
  Pallas kernels: 21.5 us -> 18.1 us
  waiting for transfers between devices: 21.3 us -> 23.2 us
  starting transfers between devices: 20.6 us -> 19.8 us
    pallas_call x1, Pallas kernels: 11.3 us -> 7.85 us  [base_halves(): pl.pallas_call(functools.partial(base_kernel, sides), in_specs=[SMEM, ANY...]
    ppermute x6, waiting for transfers between devices: 15.2 us -> 17.2 us  [along(): lax.ppermute(x, 'ring', [(a, (a + step) % ring) for a in range(ring)])]
    ppermute x6, starting transfers between devices: 10.2 us -> 9.4 us  [along(): lax.ppermute(x, 'ring', [(a, (a + step) % ring) for a in range(ring)])]
  transfers between devices with their start and end apart: 18 -> 18, of which waited for: 8 -> 9; matrix products, arithmetic and copies ran while one was open for 0% -> 0% of each run, Pallas kernels for 23% -> 19%
where the time goes in v24:
time: 66.8 us; the launch traced here: 66.5 us
  waiting for transfers between devices  23.2 us (35%)
  starting transfers between devices  19.8 us (30%)
  Pallas kernels  18.1 us (27%)
  local copies, waits for them, and re-layouts  5.17 us (8%)
    ppermute x6, waiting for transfers between devices, along(): lax.ppermute(x, 'ring', [(a, (a + step) % ring) for a in range(ring)])  17.2 us
    ppermute x6, starting transfers between devices, along(): lax.ppermute(x, 'ring', [(a, (a + step) % ring) for a in range(ring)])  9.4 us
    pallas_call x1, Pallas kernels, base_halves(): pl.pallas_call(functools.partial(base_kernel, sides), in_specs=[SMEM, ANY...  7.85 us
    ppermute x6, starting transfers between devices, in_plane(): return lax.ppermute(x, PLANE, pairs)  7.04 us
    unnamed x26, local copies, waits for them, and re-layouts  5.17 us
    ppermute x6, waiting for transfers between devices, in_plane(): return lax.ppermute(x, PLANE, pairs)  4.72 us
    pallas_call x1, Pallas kernels, spread(): pl.pallas_call(functools.partial(spread_kernel, groups, pair), in_specs=[...  3.69 us
    ppermute x1, starting transfers between devices, body(): lax.ppermute(packed[pair - w], 'pair', [(a, (a - w) % pair) for a in rang...  3.03 us
  transfers between devices with their start and end apart: 18, of which 9 were waited for; matrix products, arithmetic and copies ran while one was open for 0% of the time, Pallas kernels for 19%

profile of v24, /device:TPU:0, one launch (start us, length us, event | category | flops | bytes accessed | tf_op | source)
XLA Modules:
  0.0 66.5 jit_solution(10266259002447900968)
XLA Ops:
  0.0 1.9 %pack.1 = (bf16[2,64,1152]{2,1,0:T(8,128)(2,1)}, bf16[2,64,1152]{2,1,0:T(8,128)(2,1)}) custom-call(bf16[2,64,4096]{2,1,0:T(8,128)(2,1)} %bitcast.2, bf16[2,64,512]{2,1,0:T(8,128)(2,1)} %up.1), custom_call_target="tpu_custom_call" | custom-call | tf_op jit(solution)/shard_map/pack/pallas_call | solution.py:57
  1.9 3.0 %collective-permute-start.3 = (bf16[2,64,1152]{2,1,0:T(8,128)(2,1)}, bf16[2,64,1152]{2,1,0:T(8,128)(2,1)}, u32[]{:S(2)}, u32[]{:S(2)}) collective-permute-start(bf16[2,64,1152]{2,1,0:T(8,128)(2,1)} %get-tuple-element.23), channel_id=1, source_target_pairs={{0,2},{2,0},{1,3},{3,1},{4,6},{6,4},{5,7},{7,5},{8,10},{10,8},{9,1... | collective-permute-start | bytes 884744 | tf_op jit(solution)/shard_map/ppermute | solution.py:342
  5.0 1.6 %collective-permute-start.1 = (bf16[2,64,1152]{2,1,0:T(8,128)(2,1)}, bf16[2,64,1152]{2,1,0:T(8,128)(2,1)S(1)}, u32[]{:S(2)}, u32[]{:S(2)}) collective-permute-start(bf16[2,64,1152]{2,1,0:T(8,128)(2,1)} %get-tuple-element.21.refs_0_), channel_id=1, source_target_pairs={{0,4},{4,8},{8,12},{12,0},{1,5},{5,9},{9,13},{13,1},{2,6},{6,10},{... | collective-permute-start | bytes 884744 | tf_op jit(solution)/shard_map/ppermute | solution.py:315
  6.5 2.2 %collective-permute-start = (bf16[2,64,1152]{2,1,0:T(8,128)(2,1)}, bf16[2,64,1152]{2,1,0:T(8,128)(2,1)S(1)}, u32[]{:S(2)}, u32[]{:S(2)}) collective-permute-start(bf16[2,64,1152]{2,1,0:T(8,128)(2,1)} %get-tuple-element.21.refs_0_), channel_id=1, source_target_pairs={{0,12},{4,0},{8,4},{12,8},{1,13},{5,1},{9,5},{13,9},{2,14},{6,2},{... | collective-permute-start | bytes 884744 | tf_op jit(solution)/shard_map/ppermute | solution.py:315
  8.8 3.7 %spread.1 = (bf16[400,1024]{1,0:T(8,128)(2,1)}, bf16[400,1024]{1,0:T(8,128)(2,1)}, bf16[400,1024]{1,0:T(8,128)(2,1)}, bf16[400,1024]{1,0:T(8,128)(2,1)}) custom-call(s32[3]{0:T(128)} %lengths.3, s32[3]{0:T(128)} %bitcast.3, bf16[384,4096]{1,0:T(8,128)(2,1)} %tok.3), custom_call_target="tpu_custom_call" | custom-call | tf_op jit(solution)/shard_map/spread/pallas_call | solution.py:119
  12.5 0.4 collective-permute-start.7
  12.8 1.7 %collective-permute-start.8 = (bf16[400,1024]{1,0:T(8,128)(2,1)}, bf16[400,1024]{1,0:T(8,128)(2,1)S(1)}, u32[]{:S(2)}, u32[]{:S(2)}) collective-permute-start(bf16[400,1024]{1,0:T(8,128)(2,1)} %get-tuple-element.26), channel_id=1, source_target_pairs={{0,16},{2,18},{16,0},{18,2},{1,17},{3,19},{17,1},{19,3},{4,20},{6,... | collective-permute-start | bytes 2457608 | tf_op jit(solution)/shard_map/ppermute | solution.py:325
  14.5 0.0 collective-permute-done.3.refs_4_
  14.5 1.5 %collective-permute-start.9 = (bf16[400,1024]{1,0:T(8,128)(2,1)}, bf16[400,1024]{1,0:T(8,128)(2,1)}, u32[]{:S(2)}, u32[]{:S(2)}) collective-permute-start(bf16[400,1024]{1,0:T(8,128)(2,1)} %get-tuple-element.27), channel_id=1, source_target_pairs={{0,18},{2,16},{16,2},{18,0},{1,19},{3,17},{17,3},{19,1},{4,22},{6,... | collective-permute-start | bytes 2457608 | tf_op jit(solution)/shard_map/ppermute | solution.py:325
  16.0 0.9 %collective-permute-done.1.refs_0_ = bf16[2,64,1152]{2,1,0:T(8,128)(2,1)S(1)} collective-permute-done((bf16[2,64,1152]{2,1,0:T(8,128)(2,1)}, bf16[2,64,1152]{2,1,0:T(8,128)(2,1)S(1)}, u32[]{:S(2)}, u32[]{:S(2)}) %collective-permute-start.1) | collective-permute-done | bytes 294944 | tf_op jit(solution)/shard_map/ppermute | solution.py:315
  16.9 0.4 collective-permute-start.5
  17.3 4.7 %collective-permute-done.refs_1_ = bf16[2,64,1152]{2,1,0:T(8,128)(2,1)S(1)} collective-permute-done((bf16[2,64,1152]{2,1,0:T(8,128)(2,1)}, bf16[2,64,1152]{2,1,0:T(8,128)(2,1)S(1)}, u32[]{:S(2)}, u32[]{:S(2)}) %collective-permute-start) | collective-permute-done | bytes 294944 | tf_op jit(solution)/shard_map/ppermute | solution.py:315
  22.0 2.8 %collective-permute-start.4 = (bf16[2,64,1152]{2,1,0:T(8,128)(2,1)}, bf16[2,64,1152]{2,1,0:T(8,128)(2,1)S(1)}, u32[]{:S(2)}, u32[]{:S(2)}) collective-permute-start(bf16[2,64,1152]{2,1,0:T(8,128)(2,1)} %collective-permute-done.3.refs_4_), channel_id=1, source_target_pairs={{0,12},{4,0},{8,4},{12,8},{1,13},{5,1},{9,5},{13,9},{2,14},{6,2},{... | collective-permute-start | bytes 884744 | tf_op jit(solution)/shard_map/ppermute | solution.py:315
  24.8 7.8 %base.1 = (f32[384,512]{1,0:T(8,128)}, f32[384,512]{1,0:T(8,128)}, f32[8,128]{1,0:T(8,128)}) custom-call(s32[3]{0:T(128)} %lengths.3, bf16[384,4096]{1,0:T(8,128)(2,1)} %tok.3, bf16[4096,1024]{1,0:T(8,128)(2,1)} %key.1), custom_call_target="tpu_custom_call" | custom-call | tf_op jit(solution)/shard_map/base/pallas_call | solution.py:183
  32.7 0.0 copy-start.12
  32.8 0.0 collective-permute-done.5.refs_1_.refs_7_
  32.8 0.1 collective-permute-start.2
  32.8 1.7 %collective-permute-done.4.refs_0_ = bf16[2,64,1152]{2,1,0:T(8,128)(2,1)S(1)} collective-permute-done((bf16[2,64,1152]{2,1,0:T(8,128)(2,1)}, bf16[2,64,1152]{2,1,0:T(8,128)(2,1)S(1)}, u32[]{:S(2)}, u32[]{:S(2)}) %collective-permute-start.4) | collective-permute-done | bytes 294944 | tf_op jit(solution)/shard_map/ppermute | solution.py:315
  34.6 0.7 %copy-done.6 = bf16[2,64,1152]{2,1,0:T(8,128)(2,1)} copy-done((bf16[2,64,1152]{2,1,0:T(8,128)(2,1)}, bf16[2,64,1152]{2,1,0:T(8,128)(2,1)S(1)}, u32[]{:S(2)}) %copy-start.6) | copy-done | bytes 294936
  35.3 2.3 %collective-permute-start.6 = (bf16[2,64,1152]{2,1,0:T(8,128)(2,1)}, bf16[2,64,1152]{2,1,0:T(8,128)(2,1)S(1)}, u32[]{:S(2)}, u32[]{:S(2)}) collective-permute-start(bf16[2,64,1152]{2,1,0:T(8,128)(2,1)} %hand.4.refs_5_), channel_id=1, source_target_pairs={{0,12},{4,0},{8,4},{12,8},{1,13},{5,1},{9,5},{13,9},{2,14},{6,2},{... | collective-permute-start | bytes 884744 | tf_op jit(solution)/shard_map/ppermute | solution.py:315
  37.6 6.5 %collective-permute-done.2.refs_2_ = bf16[2,64,1152]{2,1,0:T(8,128)(2,1)S(1)} collective-permute-done((bf16[2,64,1152]{2,1,0:T(8,128)(2,1)}, bf16[2,64,1152]{2,1,0:T(8,128)(2,1)S(1)}, u32[]{:S(2)}, u32[]{:S(2)}) %collective-permute-start.2) | collective-permute-done | bytes 294944 | tf_op jit(solution)/shard_map/ppermute | solution.py:315
  44.1 3.4 %collective-permute-done.6.refs_6_ = bf16[2,64,1152]{2,1,0:T(8,128)(2,1)S(1)} collective-permute-done((bf16[2,64,1152]{2,1,0:T(8,128)(2,1)}, bf16[2,64,1152]{2,1,0:T(8,128)(2,1)S(1)}, u32[]{:S(2)}, u32[]{:S(2)}) %collective-permute-start.6) | collective-permute-done | bytes 294944 | tf_op jit(solution)/shard_map/ppermute | solution.py:315
  47.5 1.0 %copy-done.1 = bf16[2,64,1152]{2,1,0:T(8,128)(2,1)S(1)} copy-done((bf16[2,64,1152]{2,1,0:T(8,128)(2,1)S(1)}, bf16[2,64,1152]{2,1,0:T(8,128)(2,1)}, u32[]{:S(2)}) %copy-start.1) | copy-done | bytes 294936
  48.5 1.0 %copy-done.3 = bf16[2,64,1152]{2,1,0:T(8,128)(2,1)S(1)} copy-done((bf16[2,64,1152]{2,1,0:T(8,128)(2,1)S(1)}, bf16[2,64,1152]{2,1,0:T(8,128)(2,1)}, u32[]{:S(2)}) %copy-start.3) | copy-done | bytes 294936
  49.4 1.0 %copy-done.5 = bf16[2,64,1152]{2,1,0:T(8,128)(2,1)S(1)} copy-done((bf16[2,64,1152]{2,1,0:T(8,128)(2,1)S(1)}, bf16[2,64,1152]{2,1,0:T(8,128)(2,1)}, u32[]{:S(2)}) %copy-start.5) | copy-done | bytes 294936
  50.4 1.0 %copy-done.7 = bf16[2,64,1152]{2,1,0:T(8,128)(2,1)S(1)} copy-done((bf16[2,64,1152]{2,1,0:T(8,128)(2,1)S(1)}, bf16[2,64,1152]{2,1,0:T(8,128)(2,1)}, u32[]{:S(2)}) %copy-start.7) | copy-done | bytes 294936
  51.4 1.3 %collect.1.held = bf16[16,64,1152]{2,1,0:T(8,128)(2,1)S(1)} custom-call(bf16[2,64,1152]{2,1,0:T(8,128)(2,1)S(1)} %copy-done.10, bf16[2,64,1152]{2,1,0:T(8,128)(2,1)S(1)} %copy-done.1, bf16[2,64,1152]{2,1,0:T(8,128)(2,1)S(1)} %collective-permute-done.2.refs_2_, bf16[2,64,1152]{2,1,0:T(8,128)(2,1)S(1)} %copy-done.3, ...), custom_call_target="tpu_custom_call" | custom-call | tf_op jit(solution)/shard_map/collect/pallas_call | solution.py:215
  52.6 0.0 collective-permute-done.7.refs_1_
  52.7 0.0 collective-permute-done.8.refs_2_
  52.7 0.0 collective-permute-done.9.refs_3_
  52.7 2.3 %rank.1 = (bf16[3,128,128]{2,1,0:T(8,128)(2,1)S(1)}, bf16[3,128,128]{2,1,0:T(8,128)(2,1)S(1)}, bf16[3,128,128]{2,1,0:T(8,128)(2,1)S(1)}, bf16[3,128,128]{2,1,0:T(8,128)(2,1)S(1)}, f32[8,128]{1,0:T(8,128)S(1)}) custom-call(s32[16]{0:T(128)S(1)} %copy-done.12, bf16[16,64,1152]{2,1,0:T(8,128)(2,1)S(1)} %collect.1.held, bf16[400,1024]{1,0:T(8,128)(2,1)S(1)} %copy-done.8, ...), custom_call_target="tpu_custom_call" | custom-call | tf_op jit(solution)/shard_map/rank/pallas_call | solution.py:259
  55.0 0.0 copy-start.11
  55.0 0.6 copy-done.11
  55.6 0.0 collective-permute-start.10
  55.6 0.5 collective-permute-start.11
  56.1 1.5 %collective-permute-start.12 = (bf16[3,128,128]{2,1,0:T(8,128)(2,1)S(1)}, bf16[3,128,128]{2,1,0:T(8,128)(2,1)S(1)}, u32[]{:S(2)}, u32[]{:S(2)}) collective-permute-start(bf16[3,128,128]{2,1,0:T(8,128)(2,1)S(1)} %get-tuple-element.31), channel_id=1, source_target_pairs={{0,16},{2,18},{16,0},{18,2},{1,17},{3,19},{17,1},{19,3},{4,20},{6,... | collective-permute-start | bytes 294920 | tf_op jit(solution)/shard_map/ppermute | solution.py:325
  57.6 1.5 %collective-permute-start.13 = (bf16[3,128,128]{2,1,0:T(8,128)(2,1)S(1)}, bf16[3,128,128]{2,1,0:T(8,128)(2,1)S(1)}, u32[]{:S(2)}, u32[]{:S(2)}) collective-permute-start(bf16[3,128,128]{2,1,0:T(8,128)(2,1)S(1)} %get-tuple-element.32), channel_id=1, source_target_pairs={{0,18},{2,16},{16,2},{18,0},{1,19},{3,17},{17,3},{19,1},{4,22},{6,... | collective-permute-start | bytes 294920 | tf_op jit(solution)/shard_map/ppermute | solution.py:325
  59.1 0.0 collective-permute-start.14
  59.1 1.7 %collective-permute-done.11.refs_1_ = bf16[3,128,128]{2,1,0:T(8,128)(2,1)S(1)} collective-permute-done((bf16[3,128,128]{2,1,0:T(8,128)(2,1)S(1)}, bf16[3,128,128]{2,1,0:T(8,128)(2,1)S(1)}, u32[]{:S(2)}, u32[]{:S(2)}) %collective-permute-start.11) | collective-permute-done | bytes 98336 | tf_op jit(solution)/shard_map/ppermute | solution.py:325
  60.8 0.2 collective-permute-done.12.refs_2_
  61.1 0.3 collective-permute-start.16
  61.4 2.8 %collective-permute-done.13.refs_3_ = bf16[3,128,128]{2,1,0:T(8,128)(2,1)S(1)} collective-permute-done((bf16[3,128,128]{2,1,0:T(8,128)(2,1)S(1)}, bf16[3,128,128]{2,1,0:T(8,128)(2,1)S(1)}, u32[]{:S(2)}, u32[]{:S(2)}) %collective-permute-start.13) | collective-permute-done | bytes 98336 | tf_op jit(solution)/shard_map/ppermute | solution.py:325
  64.1 0.0 collective-permute-start.17
  64.1 0.0 collective-permute-done.14.refs_4_
  64.1 0.0 collective-permute-done.15.refs_5_
  64.1 0.0 collective-permute-done.16.refs_6_
  64.2 1.3 %collective-permute-done.17.refs_7_ = bf16[3,128,128]{2,1,0:T(8,128)(2,1)S(1)} collective-permute-done((bf16[3,128,128]{2,1,0:T(8,128)(2,1)S(1)}, bf16[3,128,128]{2,1,0:T(8,128)(2,1)S(1)}, u32[]{:S(2)}, u32[]{:S(2)}) %collective-permute-start.17) | collective-permute-done | bytes 98336 | tf_op jit(solution)/shard_map/ppermute | solution.py:312
  65.4 1.0 %final.1 = bf16[384,512]{1,0:T(8,128)(2,1)} custom-call(f32[384,512]{1,0:T(8,128)S(1)} %copy-done.9, f32[384,512]{1,0:T(8,128)S(1)} %collective-permute-done.10.base_b, bf16[3,128,128]{2,1,0:T(8,128)(2,1)S(1)} %get-tuple-element.29.refs_0_, bf16[3,128,128]{2,1,0:T(8,128)(2,1)S(1)} %collective-permute-done.11.refs_1_, ...), custom_call_target="tpu_custom_call" | custom-call | tf_op jit(solution)/shard_map/final/pallas_call | solution.py:293
  (23 shorter events, 0.0 us)
Async XLA Ops:
  1.9 12.6 %collective-permute-start.3 = (bf16[2,64,1152]{2,1,0:T(8,128)(2,1)}, bf16[2,64,1152]{2,1,0:T(8,128)(2,1)}, u32[]{:S(2)}, u32[]{:S(2)}) collective-permute-start(bf16[2,64,1152]{2,1,0:T(8,128)(2,1)} %get-tuple-element.23), channel_id=1, source_target_pairs={{0,2},{2,0},{1,3},{3,1},{4,6},{6,4},{5,7},{7,5},{8,10},{10,8},{9,1... | collective-permute-start | bytes 884744 | tf_op jit(solution)/shard_map/ppermute | solution.py:342
  5.0 12.0 %collective-permute-start.1 = (bf16[2,64,1152]{2,1,0:T(8,128)(2,1)}, bf16[2,64,1152]{2,1,0:T(8,128)(2,1)S(1)}, u32[]{:S(2)}, u32[]{:S(2)}) collective-permute-start(bf16[2,64,1152]{2,1,0:T(8,128)(2,1)} %get-tuple-element.21.refs_0_), channel_id=1, source_target_pairs={{0,4},{4,8},{8,12},{12,0},{1,5},{5,9},{9,13},{13,1},{2,6},{6,10},{... | collective-permute-start | bytes 884744 | tf_op jit(solution)/shard_map/ppermute | solution.py:315
  6.5 15.5 %collective-permute-start = (bf16[2,64,1152]{2,1,0:T(8,128)(2,1)}, bf16[2,64,1152]{2,1,0:T(8,128)(2,1)S(1)}, u32[]{:S(2)}, u32[]{:S(2)}) collective-permute-start(bf16[2,64,1152]{2,1,0:T(8,128)(2,1)} %get-tuple-element.21.refs_0_), channel_id=1, source_target_pairs={{0,12},{4,0},{8,4},{12,8},{1,13},{5,1},{9,5},{13,9},{2,14},{6,2},{... | collective-permute-start | bytes 884744 | tf_op jit(solution)/shard_map/ppermute | solution.py:315
  12.5 40.2 %collective-permute-start.7 = (bf16[400,1024]{1,0:T(8,128)(2,1)}, bf16[400,1024]{1,0:T(8,128)(2,1)S(1)}, u32[]{:S(2)}, u32[]{:S(2)}) collective-permute-start(bf16[400,1024]{1,0:T(8,128)(2,1)} %get-tuple-element.25), channel_id=1, source_target_pairs={{0,2},{2,0},{16,18},{18,16},{1,3},{3,1},{17,19},{19,17},{4,6},{6,4... | collective-permute-start | bytes 2457608 | tf_op jit(solution)/shard_map/ppermute | solution.py:325
  12.8 39.8 %collective-permute-start.8 = (bf16[400,1024]{1,0:T(8,128)(2,1)}, bf16[400,1024]{1,0:T(8,128)(2,1)S(1)}, u32[]{:S(2)}, u32[]{:S(2)}) collective-permute-start(bf16[400,1024]{1,0:T(8,128)(2,1)} %get-tuple-element.26), channel_id=1, source_target_pairs={{0,16},{2,18},{16,0},{18,2},{1,17},{3,19},{17,1},{19,3},{4,20},{6,... | collective-permute-start | bytes 2457608 | tf_op jit(solution)/shard_map/ppermute | solution.py:325
  14.5 33.0 %copy-start.10 = (bf16[2,64,1152]{2,1,0:T(8,128)(2,1)S(1)}, bf16[2,64,1152]{2,1,0:T(8,128)(2,1)}, u32[]{:S(2)}) copy-start(bf16[2,64,1152]{2,1,0:T(8,128)(2,1)} %get-tuple-element.21.refs_0_) | copy-start | bytes 884740
  14.5 38.1 %collective-permute-start.9 = (bf16[400,1024]{1,0:T(8,128)(2,1)}, bf16[400,1024]{1,0:T(8,128)(2,1)}, u32[]{:S(2)}, u32[]{:S(2)}) collective-permute-start(bf16[400,1024]{1,0:T(8,128)(2,1)} %get-tuple-element.27), channel_id=1, source_target_pairs={{0,18},{2,16},{16,2},{18,0},{1,19},{3,17},{17,3},{19,1},{4,22},{6,... | collective-permute-start | bytes 2457608 | tf_op jit(solution)/shard_map/ppermute | solution.py:325
  16.9 15.8 %copy-start.2 = (bf16[2,64,1152]{2,1,0:T(8,128)(2,1)}, bf16[2,64,1152]{2,1,0:T(8,128)(2,1)S(1)}, u32[]{:S(2)}) copy-start(bf16[2,64,1152]{2,1,0:T(8,128)(2,1)S(1)} %collective-permute-done.1.refs_0_) | copy-start | bytes 884740
  16.9 15.8 %collective-permute-start.5 = (bf16[2,64,1152]{2,1,0:T(8,128)(2,1)}, bf16[2,64,1152]{2,1,0:T(8,128)(2,1)S(1)}, u32[]{:S(2)}, u32[]{:S(2)}) collective-permute-start(bf16[2,64,1152]{2,1,0:T(8,128)(2,1)} %collective-permute-done.3.refs_4_), channel_id=1, source_target_pairs={{0,4},{4,8},{8,12},{12,0},{1,5},{5,9},{9,13},{13,1},{2,6},{6,10},{... | collective-permute-start | bytes 884744 | tf_op jit(solution)/shard_map/ppermute | solution.py:315
  22.0 10.7 %copy-start = (bf16[2,64,1152]{2,1,0:T(8,128)(2,1)}, bf16[2,64,1152]{2,1,0:T(8,128)(2,1)S(1)}, u32[]{:S(2)}) copy-start(bf16[2,64,1152]{2,1,0:T(8,128)(2,1)S(1)} %collective-permute-done.refs_1_) | copy-start | bytes 884740
  22.0 12.5 %collective-permute-start.4 = (bf16[2,64,1152]{2,1,0:T(8,128)(2,1)}, bf16[2,64,1152]{2,1,0:T(8,128)(2,1)S(1)}, u32[]{:S(2)}, u32[]{:S(2)}) collective-permute-start(bf16[2,64,1152]{2,1,0:T(8,128)(2,1)} %collective-permute-done.3.refs_4_), channel_id=1, source_target_pairs={{0,12},{4,0},{8,4},{12,8},{1,13},{5,1},{9,5},{13,9},{2,14},{6,2},{... | collective-permute-start | bytes 884744 | tf_op jit(solution)/shard_map/ppermute | solution.py:315
  32.7 19.9 %copy-start.8 = (bf16[400,1024]{1,0:T(8,128)(2,1)S(1)}, bf16[400,1024]{1,0:T(8,128)(2,1)}, u32[]{:S(2)}) copy-start(bf16[400,1024]{1,0:T(8,128)(2,1)} %get-tuple-element.24.refs_0_) | copy-start | bytes 2457604
  32.7 19.9 %copy-start.12 = (s32[16]{0:T(128)S(1)}, s32[16]{0:T(128)}, u32[]{:S(2)}) copy-start(s32[16]{0:T(128)} %owner.1) | copy-start | bytes 196
  32.8 1.8 %copy-start.4 = (bf16[2,64,1152]{2,1,0:T(8,128)(2,1)}, bf16[2,64,1152]{2,1,0:T(8,128)(2,1)S(1)}, u32[]{:S(2)}) copy-start(bf16[2,64,1152]{2,1,0:T(8,128)(2,1)S(1)} %collective-permute-done.5.refs_1_.refs_7_) | copy-start | bytes 884740
  32.8 11.4 %collective-permute-start.2 = (bf16[2,64,1152]{2,1,0:T(8,128)(2,1)}, bf16[2,64,1152]{2,1,0:T(8,128)(2,1)S(1)}, u32[]{:S(2)}, u32[]{:S(2)}) collective-permute-start(bf16[2,64,1152]{2,1,0:T(8,128)(2,1)} %hand.3.refs_3_), channel_id=1, source_target_pairs={{0,4},{4,8},{8,12},{12,0},{1,5},{5,9},{9,13},{13,1},{2,6},{6,10},{... | collective-permute-start | bytes 884744 | tf_op jit(solution)/shard_map/ppermute | solution.py:315
  34.6 0.7 %copy-start.6 = (bf16[2,64,1152]{2,1,0:T(8,128)(2,1)}, bf16[2,64,1152]{2,1,0:T(8,128)(2,1)S(1)}, u32[]{:S(2)}) copy-start(bf16[2,64,1152]{2,1,0:T(8,128)(2,1)S(1)} %collective-permute-done.4.refs_0_) | copy-start | bytes 884740
  35.3 12.2 %collective-permute-start.6 = (bf16[2,64,1152]{2,1,0:T(8,128)(2,1)}, bf16[2,64,1152]{2,1,0:T(8,128)(2,1)S(1)}, u32[]{:S(2)}, u32[]{:S(2)}) collective-permute-start(bf16[2,64,1152]{2,1,0:T(8,128)(2,1)} %hand.4.refs_5_), channel_id=1, source_target_pairs={{0,12},{4,0},{8,4},{12,8},{1,13},{5,1},{9,5},{13,9},{2,14},{6,2},{... | collective-permute-start | bytes 884744 | tf_op jit(solution)/shard_map/ppermute | solution.py:315
  47.5 1.0 %copy-start.1 = (bf16[2,64,1152]{2,1,0:T(8,128)(2,1)S(1)}, bf16[2,64,1152]{2,1,0:T(8,128)(2,1)}, u32[]{:S(2)}) copy-start(bf16[2,64,1152]{2,1,0:T(8,128)(2,1)} %copy-done) | copy-start | bytes 884740
  48.5 1.0 %copy-start.3 = (bf16[2,64,1152]{2,1,0:T(8,128)(2,1)S(1)}, bf16[2,64,1152]{2,1,0:T(8,128)(2,1)}, u32[]{:S(2)}) copy-start(bf16[2,64,1152]{2,1,0:T(8,128)(2,1)} %hand.3.refs_3_) | copy-start | bytes 884740
  49.4 1.0 %copy-start.5 = (bf16[2,64,1152]{2,1,0:T(8,128)(2,1)S(1)}, bf16[2,64,1152]{2,1,0:T(8,128)(2,1)}, u32[]{:S(2)}) copy-start(bf16[2,64,1152]{2,1,0:T(8,128)(2,1)} %copy-done.4) | copy-start | bytes 884740
  50.4 1.0 %copy-start.7 = (bf16[2,64,1152]{2,1,0:T(8,128)(2,1)S(1)}, bf16[2,64,1152]{2,1,0:T(8,128)(2,1)}, u32[]{:S(2)}) copy-start(bf16[2,64,1152]{2,1,0:T(8,128)(2,1)} %hand.4.refs_5_) | copy-start | bytes 884740
  52.7 12.7 %copy-start.9 = (f32[384,512]{1,0:T(8,128)S(1)}, f32[384,512]{1,0:T(8,128)}, u32[]{:S(2)}) copy-start(f32[384,512]{1,0:T(8,128)} %get-tuple-element.19.base_a) | copy-start | bytes 2359300
  55.0 0.6 copy-start.11
  55.6 9.8 %collective-permute-start.10 = (f32[384,512]{1,0:T(8,128)}, f32[384,512]{1,0:T(8,128)S(1)}, u32[]{:S(2)}, u32[]{:S(2)}) collective-permute-start(f32[384,512]{1,0:T(8,128)} %hand.5), channel_id=1, source_target_pairs={{0,1},{1,0},{2,3},{3,2},{4,5},{5,4},{6,7},{7,6},{8,9},{9,8},{10,11... | collective-permute-start | bytes 2359304 | tf_op jit(solution)/shard_map/ppermute | solution.py:312
  55.6 5.2 %collective-permute-start.11 = (bf16[3,128,128]{2,1,0:T(8,128)(2,1)S(1)}, bf16[3,128,128]{2,1,0:T(8,128)(2,1)S(1)}, u32[]{:S(2)}, u32[]{:S(2)}) collective-permute-start(bf16[3,128,128]{2,1,0:T(8,128)(2,1)S(1)} %get-tuple-element.30), channel_id=1, source_target_pairs={{0,2},{2,0},{16,18},{18,16},{1,3},{3,1},{17,19},{19,17},{4,6},{6,4... | collective-permute-start | bytes 294920 | tf_op jit(solution)/shard_map/ppermute | solution.py:325
  56.1 4.9 %collective-permute-start.12 = (bf16[3,128,128]{2,1,0:T(8,128)(2,1)S(1)}, bf16[3,128,128]{2,1,0:T(8,128)(2,1)S(1)}, u32[]{:S(2)}, u32[]{:S(2)}) collective-permute-start(bf16[3,128,128]{2,1,0:T(8,128)(2,1)S(1)} %get-tuple-element.31), channel_id=1, source_target_pairs={{0,16},{2,18},{16,0},{18,2},{1,17},{3,19},{17,1},{19,3},{4,20},{6,... | collective-permute-start | bytes 294920 | tf_op jit(solution)/shard_map/ppermute | solution.py:325
  57.6 6.5 %collective-permute-start.13 = (bf16[3,128,128]{2,1,0:T(8,128)(2,1)S(1)}, bf16[3,128,128]{2,1,0:T(8,128)(2,1)S(1)}, u32[]{:S(2)}, u32[]{:S(2)}) collective-permute-start(bf16[3,128,128]{2,1,0:T(8,128)(2,1)S(1)} %get-tuple-element.32), channel_id=1, source_target_pairs={{0,18},{2,16},{16,2},{18,0},{1,19},{3,17},{17,3},{19,1},{4,22},{6,... | collective-permute-start | bytes 294920 | tf_op jit(solution)/shard_map/ppermute | solution.py:325
  59.1 5.0 %collective-permute-start.14 = (bf16[3,128,128]{2,1,0:T(8,128)(2,1)S(1)}, bf16[3,128,128]{2,1,0:T(8,128)(2,1)S(1)}, u32[]{:S(2)}, u32[]{:S(2)}) collective-permute-start(bf16[3,128,128]{2,1,0:T(8,128)(2,1)S(1)} %get-tuple-element.29.refs_0_), channel_id=1, source_target_pairs={{0,1},{1,0},{2,3},{3,2},{4,5},{5,4},{6,7},{7,6},{8,9},{9,8},{10,11... | collective-permute-start | bytes 294920 | tf_op jit(solution)/shard_map/ppermute | solution.py:312
  60.8 3.3 %collective-permute-start.15 = (bf16[3,128,128]{2,1,0:T(8,128)(2,1)S(1)}, bf16[3,128,128]{2,1,0:T(8,128)(2,1)S(1)}, u32[]{:S(2)}, u32[]{:S(2)}) collective-permute-start(bf16[3,128,128]{2,1,0:T(8,128)(2,1)S(1)} %collective-permute-done.11.refs_1_), channel_id=1, source_target_pairs={{0,1},{1,0},{2,3},{3,2},{4,5},{5,4},{6,7},{7,6},{8,9},{9,8},{10,11... | collective-permute-start | bytes 294920 | tf_op jit(solution)/shard_map/ppermute | solution.py:312
  61.1 3.1 %collective-permute-start.16 = (bf16[3,128,128]{2,1,0:T(8,128)(2,1)S(1)}, bf16[3,128,128]{2,1,0:T(8,128)(2,1)S(1)}, u32[]{:S(2)}, u32[]{:S(2)}) collective-permute-start(bf16[3,128,128]{2,1,0:T(8,128)(2,1)S(1)} %collective-permute-done.12.refs_2_), channel_id=1, source_target_pairs={{0,1},{1,0},{2,3},{3,2},{4,5},{5,4},{6,7},{7,6},{8,9},{9,8},{10,11... | collective-permute-start | bytes 294920 | tf_op jit(solution)/shard_map/ppermute | solution.py:312
  64.1 1.3 %collective-permute-start.17 = (bf16[3,128,128]{2,1,0:T(8,128)(2,1)S(1)}, bf16[3,128,128]{2,1,0:T(8,128)(2,1)S(1)}, u32[]{:S(2)}, u32[]{:S(2)}) collective-permute-start(bf16[3,128,128]{2,1,0:T(8,128)(2,1)S(1)} %collective-permute-done.13.refs_3_), channel_id=1, source_target_pairs={{0,1},{1,0},{2,3},{3,2},{4,5},{5,4},{6,7},{7,6},{8,9},{9,8},{10,11... | collective-permute-start | bytes 294920 | tf_op jit(solution)/shard_map/ppermute | solution.py:312

commit v25 on v24

--- a/solution.py
+++ b/solution.py
@@ -223,11 +223,12 @@
     )(*pieces)
 
 
-def rank_kernel(ring, pair, rows, owner, held, *refs):
-    shares = (len(refs) - 1) // 2
-    toks, outs, flag = refs[:shares], refs[shares:-1], refs[-1]
+def rank_kernel(ring, pair, rows, shares, owner, held, *refs):
+    late, toks, outs = refs[: -2 - 2 * shares], refs[-2 - 2 * shares : -2 - shares], refs[-2 - shares : -2]
+    flag, picked = refs[-2:]
     flag[...] = jnp.zeros_like(flag)
-    per, rank = held.shape[0] // (ring * pair), held.shape[1]
+    rank = held.shape[1]
+    per = owner.shape[0] // (ring * pair)
     blocks, _, block = outs[0].shape
     feats = toks[0].shape[1]
     z, y = lax.axis_index("ring"), lax.axis_index("pair")
@@ -237,35 +238,54 @@
     for tok in toks:
         named = tok[rows:, :LANES].astype(jnp.float32)
         ids += [jnp.sum(jnp.where((lane == b) & (row == 0), named, 0.0)).astype(jnp.int32) for b in range(blocks)]
+    for i, one in enumerate(ids):
+        slot = owner[one]
+        chip = slot // per
+        local = lax.rem(slot, per)
+        away = lax.rem(chip // pair - z + ring, ring)
+        way = lax.rem(lax.rem(chip, pair) - y + pair, pair)
+        if late:
+            half = ring // 2
+            near = away - jnp.where(away > half, 1, 0)
+
+            @pl.when(away != half)
+            def _():
+                picked[i] = held[(way * (ring - 1) + near) * per + local]
+
+            for w in range(pair):
+
+                @pl.when((away == half) & (way == w))
+                def _():
+                    picked[i] = late[w][local]
+
+        else:
+            picked[i] = held[(way * ring + away) * per + local]
     for k, tok in enumerate(toks):
         for b in range(blocks):
-            slot = owner[ids[k * blocks + b]]
-            chip = slot // per
-            away = lax.rem(chip // pair - z + ring, ring)
-            way = lax.rem(lax.rem(chip, pair) - y + pair, pair)
-            at = (way * ring + away) * per + lax.rem(slot, per)
+            i = k * blocks + b
             part = lax.dot_general(
-                held[at, :, :feats],
+                picked[i, :, :feats],
                 tok[b * block : (b + 1) * block, :],
                 (((1,), (1,)), ((), ())),
                 preferred_element_type=jnp.float32,
             )
             outs[k][b, :rank, :] = part.astype(outs[k].dtype)
-            outs[k][b, rank:, :] = held[at, :, feats:]
-
-
-def rank_parts(owner, toks, held, ring, pair, rows, blocks):
+            outs[k][b, rank:, :] = picked[i, :, feats:]
+
+
+def rank_parts(owner, toks, held, late, ring, pair, rows, blocks):
     shares, rank = len(toks), held.shape[1]
     return pl.pallas_call(
-        functools.partial(rank_kernel, ring, pair, rows),
-        in_specs=[SMEM, VMEM] + [VMEM] * shares,
+        functools.partial(rank_kernel, ring, pair, rows, shares),
+        in_specs=[SMEM, VMEM] + [VMEM] * (len(late) + shares),
         out_specs=[VMEM] * (shares + 1),
         out_shape=[jax.ShapeDtypeStruct((blocks, 2 * rank, rows // blocks), held.dtype)] * shares
         + [jax.ShapeDtypeStruct((8, LANES), jnp.float32)],
+        scratch_shapes=[pltpu.VMEM((shares * blocks,) + held.shape[1:], held.dtype)],
         cost_estimate=pl.CostEstimate(flops=0, bytes_accessed=0, transcendentals=0),
         compiler_params=ROOM,
         name="rank",
-    )(owner, held, *toks)
+    )(owner, held, *late, *toks)
 
 
 def final_kernel(groups, pair, base_a, base_b, *refs):
@@ -350,8 +370,10 @@
         for way, held in enumerate(firsts)
     ]
 
-    flat = [piece for way in pieces for piece in way]
-    *parts, ready = rank_parts(owner_slot, toks, collect(flat), ring, pair, rows, blocks)
+    halfway = ring // 2 if ring % 2 == 0 else ring
+    held = collect([piece for way in pieces for away, piece in enumerate(way) if away != halfway])
+    late = [way[halfway] for way in pieces] if halfway < ring else []
+    *parts, ready = rank_parts(owner_slot, toks, held, late, ring, pair, rows, blocks)
     mine = [parts[0]] + [in_plane(parts[k], -(k // pair), -(k % pair)) for k in range(1, shares)]
     theirs = [across(part) for part in mine]
     base_in = across(hand_on(base_out, ready))

time: 66.8 us -> 66.7 us (level)
  waiting for transfers between devices: 23.2 us -> 20.7 us
  local copies, waits for them, and re-layouts: 5.17 us -> 6.84 us
  Pallas kernels: 18.1 us -> 18.8 us
    ppermute x6, waiting for transfers between devices: 17.2 us -> 8.79 us  [along(): lax.ppermute(x, 'ring', [(a, (a + step) % ring) for a in range(ring)])]
    ppermute x6, waiting for transfers between devices: 4.72 us -> 10.6 us  [in_plane(): return lax.ppermute(x, PLANE, pairs)]
    unnamed x26 -> x30, local copies, waits for them, and re-layouts: 5.17 us -> 6.84 us
    pallas_call x1, Pallas kernels: 2.32 us -> 3.12 us  [rank_parts(): pl.pallas_call(functools.partial(rank_kernel, ring, pair, rows, shares),...]
where the time goes in v25:
time: 66.7 us; the launch traced here: 66.3 us
  waiting for transfers between devices  20.7 us (31%)
  starting transfers between devices  19.8 us (30%)
  Pallas kernels  18.8 us (28%)
  local copies, waits for them, and re-layouts  6.84 us (10%)
    ppermute x6, waiting for transfers between devices, in_plane(): return lax.ppermute(x, PLANE, pairs)  10.6 us
    ppermute x6, starting transfers between devices, along(): lax.ppermute(x, 'ring', [(a, (a + step) % ring) for a in range(ring)])  9.46 us
    ppermute x6, waiting for transfers between devices, along(): lax.ppermute(x, 'ring', [(a, (a + step) % ring) for a in range(ring)])  8.79 us
    pallas_call x1, Pallas kernels, base_halves(): pl.pallas_call(functools.partial(base_kernel, sides), in_specs=[SMEM, ANY...  7.86 us
    ppermute x6, starting transfers between devices, in_plane(): return lax.ppermute(x, PLANE, pairs)  7.04 us
    unnamed x30, local copies, waits for them, and re-layouts  6.84 us
    pallas_call x1, Pallas kernels, spread(): pl.pallas_call(functools.partial(spread_kernel, groups, pair), in_specs=[...  3.65 us
    pallas_call x1, Pallas kernels, rank_parts(): pl.pallas_call(functools.partial(rank_kernel, ring, pair, rows, shares),...  3.12 us
  transfers between devices with their start and end apart: 18, of which 9 were waited for; matrix products, arithmetic and copies ran while one was open for 0% of the time, Pallas kernels for 19%

profile of v25, /device:TPU:0, one launch (start us, length us, event | category | flops | bytes accessed | tf_op | source)
XLA Modules:
  0.0 66.3 jit_solution(4501301203360181427)
XLA Ops:
  0.0 1.9 %pack.1 = (bf16[2,64,1152]{2,1,0:T(8,128)(2,1)}, bf16[2,64,1152]{2,1,0:T(8,128)(2,1)}) custom-call(bf16[2,64,4096]{2,1,0:T(8,128)(2,1)} %bitcast.2, bf16[2,64,512]{2,1,0:T(8,128)(2,1)} %up.1), custom_call_target="tpu_custom_call" | custom-call | tf_op jit(solution)/shard_map/pack/pallas_call | solution.py:57
  1.9 3.0 %collective-permute-start.2 = (bf16[2,64,1152]{2,1,0:T(8,128)(2,1)}, bf16[2,64,1152]{2,1,0:T(8,128)(2,1)}, u32[]{:S(2)}, u32[]{:S(2)}) collective-permute-start(bf16[2,64,1152]{2,1,0:T(8,128)(2,1)} %get-tuple-element.23), channel_id=1, source_target_pairs={{0,2},{2,0},{1,3},{3,1},{4,6},{6,4},{5,7},{7,5},{8,10},{10,8},{9,1... | collective-permute-start | bytes 884744 | tf_op jit(solution)/shard_map/ppermute | solution.py:362
  5.0 1.6 %collective-permute-start.1 = (bf16[2,64,1152]{2,1,0:T(8,128)(2,1)}, bf16[2,64,1152]{2,1,0:T(8,128)(2,1)S(1)}, u32[]{:S(2)}, u32[]{:S(2)}) collective-permute-start(bf16[2,64,1152]{2,1,0:T(8,128)(2,1)} %get-tuple-element.21.refs_0_), channel_id=1, source_target_pairs={{0,4},{4,8},{8,12},{12,0},{1,5},{5,9},{9,13},{13,1},{2,6},{6,10},{... | collective-permute-start | bytes 884744 | tf_op jit(solution)/shard_map/ppermute | solution.py:335
  6.5 2.2 %collective-permute-start = (bf16[2,64,1152]{2,1,0:T(8,128)(2,1)}, bf16[2,64,1152]{2,1,0:T(8,128)(2,1)S(1)}, u32[]{:S(2)}, u32[]{:S(2)}) collective-permute-start(bf16[2,64,1152]{2,1,0:T(8,128)(2,1)} %get-tuple-element.21.refs_0_), channel_id=1, source_target_pairs={{0,12},{4,0},{8,4},{12,8},{1,13},{5,1},{9,5},{13,9},{2,14},{6,2},{... | collective-permute-start | bytes 884744 | tf_op jit(solution)/shard_map/ppermute | solution.py:335
  8.8 3.6 %spread.1 = (bf16[400,1024]{1,0:T(8,128)(2,1)}, bf16[400,1024]{1,0:T(8,128)(2,1)}, bf16[400,1024]{1,0:T(8,128)(2,1)}, bf16[400,1024]{1,0:T(8,128)(2,1)}) custom-call(s32[3]{0:T(128)} %lengths.3, s32[3]{0:T(128)} %bitcast.3, bf16[384,4096]{1,0:T(8,128)(2,1)} %tok.3), custom_call_target="tpu_custom_call" | custom-call | tf_op jit(solution)/shard_map/spread/pallas_call | solution.py:119
  12.4 0.4 collective-permute-start.7
  12.8 1.7 %collective-permute-start.8 = (bf16[400,1024]{1,0:T(8,128)(2,1)}, bf16[400,1024]{1,0:T(8,128)(2,1)S(1)}, u32[]{:S(2)}, u32[]{:S(2)}) collective-permute-start(bf16[400,1024]{1,0:T(8,128)(2,1)} %get-tuple-element.26), channel_id=1, source_target_pairs={{0,16},{2,18},{16,0},{18,2},{1,17},{3,19},{17,1},{19,3},{4,20},{6,... | collective-permute-start | bytes 2457608 | tf_op jit(solution)/shard_map/ppermute | solution.py:345
  14.5 0.0 collective-permute-done.2.refs_3_
  14.5 1.5 %collective-permute-start.9 = (bf16[400,1024]{1,0:T(8,128)(2,1)}, bf16[400,1024]{1,0:T(8,128)(2,1)}, u32[]{:S(2)}, u32[]{:S(2)}) collective-permute-start(bf16[400,1024]{1,0:T(8,128)(2,1)} %get-tuple-element.27), channel_id=1, source_target_pairs={{0,18},{2,16},{16,2},{18,0},{1,19},{3,17},{17,3},{19,1},{4,22},{6,... | collective-permute-start | bytes 2457608 | tf_op jit(solution)/shard_map/ppermute | solution.py:345
  16.0 0.9 %collective-permute-done.1.refs_0_ = bf16[2,64,1152]{2,1,0:T(8,128)(2,1)S(1)} collective-permute-done((bf16[2,64,1152]{2,1,0:T(8,128)(2,1)}, bf16[2,64,1152]{2,1,0:T(8,128)(2,1)S(1)}, u32[]{:S(2)}, u32[]{:S(2)}) %collective-permute-start.1) | collective-permute-done | bytes 294944 | tf_op jit(solution)/shard_map/ppermute | solution.py:335
  17.0 0.4 collective-permute-start.4
  17.4 4.7 %collective-permute-done.refs_1_ = bf16[2,64,1152]{2,1,0:T(8,128)(2,1)S(1)} collective-permute-done((bf16[2,64,1152]{2,1,0:T(8,128)(2,1)}, bf16[2,64,1152]{2,1,0:T(8,128)(2,1)S(1)}, u32[]{:S(2)}, u32[]{:S(2)}) %collective-permute-start) | collective-permute-done | bytes 294944 | tf_op jit(solution)/shard_map/ppermute | solution.py:335
  22.1 2.8 %collective-permute-start.3 = (bf16[2,64,1152]{2,1,0:T(8,128)(2,1)}, bf16[2,64,1152]{2,1,0:T(8,128)(2,1)S(1)}, u32[]{:S(2)}, u32[]{:S(2)}) collective-permute-start(bf16[2,64,1152]{2,1,0:T(8,128)(2,1)} %collective-permute-done.2.refs_3_), channel_id=1, source_target_pairs={{0,12},{4,0},{8,4},{12,8},{1,13},{5,1},{9,5},{13,9},{2,14},{6,2},{... | collective-permute-start | bytes 884744 | tf_op jit(solution)/shard_map/ppermute | solution.py:335
  24.9 7.9 %base.1 = (f32[384,512]{1,0:T(8,128)}, f32[384,512]{1,0:T(8,128)}, f32[8,128]{1,0:T(8,128)}) custom-call(s32[3]{0:T(128)} %lengths.3, bf16[384,4096]{1,0:T(8,128)(2,1)} %tok.3, bf16[4096,1024]{1,0:T(8,128)(2,1)} %key.1), custom_call_target="tpu_custom_call" | custom-call | tf_op jit(solution)/shard_map/base/pallas_call | solution.py:183
  32.8 0.0 copy-start.14
  32.8 0.1 collective-permute-start.5
  32.9 1.7 %collective-permute-done.3.refs_0_ = bf16[2,64,1152]{2,1,0:T(8,128)(2,1)S(1)} collective-permute-done((bf16[2,64,1152]{2,1,0:T(8,128)(2,1)}, bf16[2,64,1152]{2,1,0:T(8,128)(2,1)S(1)}, u32[]{:S(2)}, u32[]{:S(2)}) %collective-permute-start.3) | collective-permute-done | bytes 294944 | tf_op jit(solution)/shard_map/ppermute | solution.py:335
  34.6 0.7 %copy-done.6 = bf16[2,64,1152]{2,1,0:T(8,128)(2,1)} copy-done((bf16[2,64,1152]{2,1,0:T(8,128)(2,1)}, bf16[2,64,1152]{2,1,0:T(8,128)(2,1)S(1)}, u32[]{:S(2)}) %copy-start.6) | copy-done | bytes 294936
  35.3 2.3 %collective-permute-start.6 = (bf16[2,64,1152]{2,1,0:T(8,128)(2,1)}, bf16[2,64,1152]{2,1,0:T(8,128)(2,1)S(1)}, u32[]{:S(2)}, u32[]{:S(2)}) collective-permute-start(bf16[2,64,1152]{2,1,0:T(8,128)(2,1)} %hand.4.refs_4_), channel_id=1, source_target_pairs={{0,12},{4,0},{8,4},{12,8},{1,13},{5,1},{9,5},{13,9},{2,14},{6,2},{... | collective-permute-start | bytes 884744 | tf_op jit(solution)/shard_map/ppermute | solution.py:335
  37.6 1.0 %copy-done.1 = bf16[2,64,1152]{2,1,0:T(8,128)(2,1)S(1)} copy-done((bf16[2,64,1152]{2,1,0:T(8,128)(2,1)S(1)}, bf16[2,64,1152]{2,1,0:T(8,128)(2,1)}, u32[]{:S(2)}) %copy-start.1) | copy-done | bytes 294936
  38.6 1.0 %copy-done.3 = bf16[2,64,1152]{2,1,0:T(8,128)(2,1)S(1)} copy-done((bf16[2,64,1152]{2,1,0:T(8,128)(2,1)S(1)}, bf16[2,64,1152]{2,1,0:T(8,128)(2,1)}, u32[]{:S(2)}) %copy-start.3) | copy-done | bytes 294936
  39.6 1.0 %copy-done.5 = bf16[2,64,1152]{2,1,0:T(8,128)(2,1)S(1)} copy-done((bf16[2,64,1152]{2,1,0:T(8,128)(2,1)S(1)}, bf16[2,64,1152]{2,1,0:T(8,128)(2,1)}, u32[]{:S(2)}) %copy-start.5) | copy-done | bytes 294936
  40.5 1.0 %copy-done.7 = bf16[2,64,1152]{2,1,0:T(8,128)(2,1)S(1)} copy-done((bf16[2,64,1152]{2,1,0:T(8,128)(2,1)S(1)}, bf16[2,64,1152]{2,1,0:T(8,128)(2,1)}, u32[]{:S(2)}) %copy-start.7) | copy-done | bytes 294936
  41.5 1.2 %collect.1.held = bf16[12,64,1152]{2,1,0:T(8,128)(2,1)S(1)} custom-call(bf16[2,64,1152]{2,1,0:T(8,128)(2,1)S(1)} %copy-done.10, bf16[2,64,1152]{2,1,0:T(8,128)(2,1)S(1)} %copy-done.1, bf16[2,64,1152]{2,1,0:T(8,128)(2,1)S(1)} %copy-done.3, bf16[2,64,1152]{2,1,0:T(8,128)(2,1)} %collective-permute-done.2.refs_3_, bf16[2,64,1152]{2,1,0:T(8,128)(2,1)S(1)} %copy-done.7, ...), custom_call_target="tpu_custom_call" | custom-call | tf_op jit(solution)/shard_map/collect/pallas_call | solution.py:215
  42.7 1.4 %collective-permute-done.5.refs_0_ = bf16[2,64,1152]{2,1,0:T(8,128)(2,1)S(1)} collective-permute-done((bf16[2,64,1152]{2,1,0:T(8,128)(2,1)}, bf16[2,64,1152]{2,1,0:T(8,128)(2,1)S(1)}, u32[]{:S(2)}, u32[]{:S(2)}) %collective-permute-start.5) | collective-permute-done | bytes 294944 | tf_op jit(solution)/shard_map/ppermute | solution.py:335
  44.1 0.7 %copy-done.11 = bf16[2,64,1152]{2,1,0:T(8,128)(2,1)} copy-done((bf16[2,64,1152]{2,1,0:T(8,128)(2,1)}, bf16[2,64,1152]{2,1,0:T(8,128)(2,1)S(1)}, u32[]{:S(2)}) %copy-start.11) | copy-done | bytes 294936
  44.9 0.0 collective-permute-done.7.refs_3_
  44.9 0.0 collective-permute-done.8.refs_4_
  44.9 5.9 %collective-permute-done.9.refs_5_ = bf16[400,1024]{1,0:T(8,128)(2,1)} collective-permute-done((bf16[400,1024]{1,0:T(8,128)(2,1)}, bf16[400,1024]{1,0:T(8,128)(2,1)}, u32[]{:S(2)}, u32[]{:S(2)}) %collective-permute-start.9) | collective-permute-done | bytes 819232 | tf_op jit(solution)/shard_map/ppermute | solution.py:345
  50.8 0.0 collective-permute-done.6.refs_1_
  50.8 0.0 copy-start.12
  50.8 1.0 %copy-done.12 = bf16[2,64,1152]{2,1,0:T(8,128)(2,1)S(1)} copy-done((bf16[2,64,1152]{2,1,0:T(8,128)(2,1)S(1)}, bf16[2,64,1152]{2,1,0:T(8,128)(2,1)}, u32[]{:S(2)}) %copy-start.12) | copy-done | bytes 294936
  51.7 3.1 %rank.1 = (bf16[3,128,128]{2,1,0:T(8,128)(2,1)S(1)}, bf16[3,128,128]{2,1,0:T(8,128)(2,1)S(1)}, bf16[3,128,128]{2,1,0:T(8,128)(2,1)S(1)}, bf16[3,128,128]{2,1,0:T(8,128)(2,1)S(1)}, f32[8,128]{1,0:T(8,128)S(1)}) custom-call(s32[16]{0:T(128)S(1)} %copy-done.14, bf16[12,64,1152]{2,1,0:T(8,128)(2,1)S(1)} %collect.1.held, bf16[2,64,1152]{2,1,0:T(8,128)(2,1)S(1)} %copy-done.12, ...), custom_call_target="tpu_custom_call" | custom-call | tf_op jit(solution)/shard_map/rank/pallas_call | solution.py:278
  54.9 0.0 copy-start.13
  54.9 0.6 copy-done.13
  55.5 0.5 collective-permute-start.11
  56.0 1.5 %collective-permute-start.12 = (bf16[3,128,128]{2,1,0:T(8,128)(2,1)S(1)}, bf16[3,128,128]{2,1,0:T(8,128)(2,1)S(1)}, u32[]{:S(2)}, u32[]{:S(2)}) collective-permute-start(bf16[3,128,128]{2,1,0:T(8,128)(2,1)S(1)} %get-tuple-element.31), channel_id=1, source_target_pairs={{0,16},{2,18},{16,0},{18,2},{1,17},{3,19},{17,1},{19,3},{4,20},{6,... | collective-permute-start | bytes 294920 | tf_op jit(solution)/shard_map/ppermute | solution.py:345
  57.4 1.5 %collective-permute-start.13 = (bf16[3,128,128]{2,1,0:T(8,128)(2,1)S(1)}, bf16[3,128,128]{2,1,0:T(8,128)(2,1)S(1)}, u32[]{:S(2)}, u32[]{:S(2)}) collective-permute-start(bf16[3,128,128]{2,1,0:T(8,128)(2,1)S(1)} %get-tuple-element.32), channel_id=1, source_target_pairs={{0,18},{2,16},{16,2},{18,0},{1,19},{3,17},{17,3},{19,1},{4,22},{6,... | collective-permute-start | bytes 294920 | tf_op jit(solution)/shard_map/ppermute | solution.py:345
  59.0 0.0 collective-permute-start.14
  59.0 1.7 %collective-permute-done.11.refs_1_ = bf16[3,128,128]{2,1,0:T(8,128)(2,1)S(1)} collective-permute-done((bf16[3,128,128]{2,1,0:T(8,128)(2,1)S(1)}, bf16[3,128,128]{2,1,0:T(8,128)(2,1)S(1)}, u32[]{:S(2)}, u32[]{:S(2)}) %collective-permute-start.11) | collective-permute-done | bytes 98336 | tf_op jit(solution)/shard_map/ppermute | solution.py:345
  60.7 0.0 collective-permute-start.15
  60.7 0.2 collective-permute-done.12.refs_2_
  60.9 0.3 collective-permute-start.16
  61.2 2.8 %collective-permute-done.13.refs_3_ = bf16[3,128,128]{2,1,0:T(8,128)(2,1)S(1)} collective-permute-done((bf16[3,128,128]{2,1,0:T(8,128)(2,1)S(1)}, bf16[3,128,128]{2,1,0:T(8,128)(2,1)S(1)}, u32[]{:S(2)}, u32[]{:S(2)}) %collective-permute-start.13) | collective-permute-done | bytes 98336 | tf_op jit(solution)/shard_map/ppermute | solution.py:345
  64.0 0.0 collective-permute-start.17
  64.0 0.0 collective-permute-done.14.refs_4_
  64.0 1.3 %collective-permute-done.17.refs_7_ = bf16[3,128,128]{2,1,0:T(8,128)(2,1)S(1)} collective-permute-done((bf16[3,128,128]{2,1,0:T(8,128)(2,1)S(1)}, bf16[3,128,128]{2,1,0:T(8,128)(2,1)S(1)}, u32[]{:S(2)}, u32[]{:S(2)}) %collective-permute-start.17) | collective-permute-done | bytes 98336 | tf_op jit(solution)/shard_map/ppermute | solution.py:332
  65.3 1.1 %final.1 = bf16[384,512]{1,0:T(8,128)(2,1)} custom-call(f32[384,512]{1,0:T(8,128)S(1)} %copy-done.9, f32[384,512]{1,0:T(8,128)S(1)} %collective-permute-done.10.base_b, bf16[3,128,128]{2,1,0:T(8,128)(2,1)S(1)} %get-tuple-element.29.refs_0_, bf16[3,128,128]{2,1,0:T(8,128)(2,1)S(1)} %collective-permute-done.11.refs_1_, ...), custom_call_target="tpu_custom_call" | custom-call | tf_op jit(solution)/shard_map/final/pallas_call | solution.py:313
  (27 shorter events, 0.1 us)
Async XLA Ops:
  1.9 12.6 %collective-permute-start.2 = (bf16[2,64,1152]{2,1,0:T(8,128)(2,1)}, bf16[2,64,1152]{2,1,0:T(8,128)(2,1)}, u32[]{:S(2)}, u32[]{:S(2)}) collective-permute-start(bf16[2,64,1152]{2,1,0:T(8,128)(2,1)} %get-tuple-element.23), channel_id=1, source_target_pairs={{0,2},{2,0},{1,3},{3,1},{4,6},{6,4},{5,7},{7,5},{8,10},{10,8},{9,1... | collective-permute-start | bytes 884744 | tf_op jit(solution)/shard_map/ppermute | solution.py:362
  5.0 12.0 %collective-permute-start.1 = (bf16[2,64,1152]{2,1,0:T(8,128)(2,1)}, bf16[2,64,1152]{2,1,0:T(8,128)(2,1)S(1)}, u32[]{:S(2)}, u32[]{:S(2)}) collective-permute-start(bf16[2,64,1152]{2,1,0:T(8,128)(2,1)} %get-tuple-element.21.refs_0_), channel_id=1, source_target_pairs={{0,4},{4,8},{8,12},{12,0},{1,5},{5,9},{9,13},{13,1},{2,6},{6,10},{... | collective-permute-start | bytes 884744 | tf_op jit(solution)/shard_map/ppermute | solution.py:335
  6.5 15.5 %collective-permute-start = (bf16[2,64,1152]{2,1,0:T(8,128)(2,1)}, bf16[2,64,1152]{2,1,0:T(8,128)(2,1)S(1)}, u32[]{:S(2)}, u32[]{:S(2)}) collective-permute-start(bf16[2,64,1152]{2,1,0:T(8,128)(2,1)} %get-tuple-element.21.refs_0_), channel_id=1, source_target_pairs={{0,12},{4,0},{8,4},{12,8},{1,13},{5,1},{9,5},{13,9},{2,14},{6,2},{... | collective-permute-start | bytes 884744 | tf_op jit(solution)/shard_map/ppermute | solution.py:335
  12.4 32.4 %collective-permute-start.7 = (bf16[400,1024]{1,0:T(8,128)(2,1)}, bf16[400,1024]{1,0:T(8,128)(2,1)S(1)}, u32[]{:S(2)}, u32[]{:S(2)}) collective-permute-start(bf16[400,1024]{1,0:T(8,128)(2,1)} %get-tuple-element.25), channel_id=1, source_target_pairs={{0,2},{2,0},{16,18},{18,16},{1,3},{3,1},{17,19},{19,17},{4,6},{6,4... | collective-permute-start | bytes 2457608 | tf_op jit(solution)/shard_map/ppermute | solution.py:345
  12.8 32.1 %collective-permute-start.8 = (bf16[400,1024]{1,0:T(8,128)(2,1)}, bf16[400,1024]{1,0:T(8,128)(2,1)S(1)}, u32[]{:S(2)}, u32[]{:S(2)}) collective-permute-start(bf16[400,1024]{1,0:T(8,128)(2,1)} %get-tuple-element.26), channel_id=1, source_target_pairs={{0,16},{2,18},{16,0},{18,2},{1,17},{3,19},{17,1},{19,3},{4,20},{6,... | collective-permute-start | bytes 2457608 | tf_op jit(solution)/shard_map/ppermute | solution.py:345
  14.5 23.2 %copy-start.10 = (bf16[2,64,1152]{2,1,0:T(8,128)(2,1)S(1)}, bf16[2,64,1152]{2,1,0:T(8,128)(2,1)}, u32[]{:S(2)}) copy-start(bf16[2,64,1152]{2,1,0:T(8,128)(2,1)} %get-tuple-element.21.refs_0_) | copy-start | bytes 884740
  14.5 36.3 %collective-permute-start.9 = (bf16[400,1024]{1,0:T(8,128)(2,1)}, bf16[400,1024]{1,0:T(8,128)(2,1)}, u32[]{:S(2)}, u32[]{:S(2)}) collective-permute-start(bf16[400,1024]{1,0:T(8,128)(2,1)} %get-tuple-element.27), channel_id=1, source_target_pairs={{0,18},{2,16},{16,2},{18,0},{1,19},{3,17},{17,3},{19,1},{4,22},{6,... | collective-permute-start | bytes 2457608 | tf_op jit(solution)/shard_map/ppermute | solution.py:345
  16.9 15.8 %copy-start.2 = (bf16[2,64,1152]{2,1,0:T(8,128)(2,1)}, bf16[2,64,1152]{2,1,0:T(8,128)(2,1)S(1)}, u32[]{:S(2)}) copy-start(bf16[2,64,1152]{2,1,0:T(8,128)(2,1)S(1)} %collective-permute-done.1.refs_0_) | copy-start | bytes 884740
  17.0 15.8 %collective-permute-start.4 = (bf16[2,64,1152]{2,1,0:T(8,128)(2,1)}, bf16[2,64,1152]{2,1,0:T(8,128)(2,1)S(1)}, u32[]{:S(2)}, u32[]{:S(2)}) collective-permute-start(bf16[2,64,1152]{2,1,0:T(8,128)(2,1)} %collective-permute-done.2.refs_3_), channel_id=1, source_target_pairs={{0,4},{4,8},{8,12},{12,0},{1,5},{5,9},{9,13},{13,1},{2,6},{6,10},{... | collective-permute-start | bytes 884744 | tf_op jit(solution)/shard_map/ppermute | solution.py:335
  22.1 10.7 %copy-start = (bf16[2,64,1152]{2,1,0:T(8,128)(2,1)}, bf16[2,64,1152]{2,1,0:T(8,128)(2,1)S(1)}, u32[]{:S(2)}) copy-start(bf16[2,64,1152]{2,1,0:T(8,128)(2,1)S(1)} %collective-permute-done.refs_1_) | copy-start | bytes 884740
  22.1 12.5 %collective-permute-start.3 = (bf16[2,64,1152]{2,1,0:T(8,128)(2,1)}, bf16[2,64,1152]{2,1,0:T(8,128)(2,1)S(1)}, u32[]{:S(2)}, u32[]{:S(2)}) collective-permute-start(bf16[2,64,1152]{2,1,0:T(8,128)(2,1)} %collective-permute-done.2.refs_3_), channel_id=1, source_target_pairs={{0,12},{4,0},{8,4},{12,8},{1,13},{5,1},{9,5},{13,9},{2,14},{6,2},{... | collective-permute-start | bytes 884744 | tf_op jit(solution)/shard_map/ppermute | solution.py:335
  32.7 18.0 %copy-start.8 = (bf16[400,1024]{1,0:T(8,128)(2,1)S(1)}, bf16[400,1024]{1,0:T(8,128)(2,1)}, u32[]{:S(2)}) copy-start(bf16[400,1024]{1,0:T(8,128)(2,1)} %get-tuple-element.24.refs_2_) | copy-start | bytes 2457604
  32.8 18.0 %copy-start.14 = (s32[16]{0:T(128)S(1)}, s32[16]{0:T(128)}, u32[]{:S(2)}) copy-start(s32[16]{0:T(128)} %owner.1) | copy-start | bytes 196
  32.8 1.8 %copy-start.4 = (bf16[2,64,1152]{2,1,0:T(8,128)(2,1)}, bf16[2,64,1152]{2,1,0:T(8,128)(2,1)S(1)}, u32[]{:S(2)}) copy-start(bf16[2,64,1152]{2,1,0:T(8,128)(2,1)S(1)} %collective-permute-done.4.refs_1_.refs_5_) | copy-start | bytes 884740
  32.8 11.3 %collective-permute-start.5 = (bf16[2,64,1152]{2,1,0:T(8,128)(2,1)}, bf16[2,64,1152]{2,1,0:T(8,128)(2,1)S(1)}, u32[]{:S(2)}, u32[]{:S(2)}) collective-permute-start(bf16[2,64,1152]{2,1,0:T(8,128)(2,1)} %hand.3.refs_2_), channel_id=1, source_target_pairs={{0,4},{4,8},{8,12},{12,0},{1,5},{5,9},{9,13},{13,1},{2,6},{6,10},{... | collective-permute-start | bytes 884744 | tf_op jit(solution)/shard_map/ppermute | solution.py:335
  34.6 0.7 %copy-start.6 = (bf16[2,64,1152]{2,1,0:T(8,128)(2,1)}, bf16[2,64,1152]{2,1,0:T(8,128)(2,1)S(1)}, u32[]{:S(2)}) copy-start(bf16[2,64,1152]{2,1,0:T(8,128)(2,1)S(1)} %collective-permute-done.3.refs_0_) | copy-start | bytes 884740
  35.3 15.5 %collective-permute-start.6 = (bf16[2,64,1152]{2,1,0:T(8,128)(2,1)}, bf16[2,64,1152]{2,1,0:T(8,128)(2,1)S(1)}, u32[]{:S(2)}, u32[]{:S(2)}) collective-permute-start(bf16[2,64,1152]{2,1,0:T(8,128)(2,1)} %hand.4.refs_4_), channel_id=1, source_target_pairs={{0,12},{4,0},{8,4},{12,8},{1,13},{5,1},{9,5},{13,9},{2,14},{6,2},{... | collective-permute-start | bytes 884744 | tf_op jit(solution)/shard_map/ppermute | solution.py:335
  37.6 1.0 %copy-start.1 = (bf16[2,64,1152]{2,1,0:T(8,128)(2,1)S(1)}, bf16[2,64,1152]{2,1,0:T(8,128)(2,1)}, u32[]{:S(2)}) copy-start(bf16[2,64,1152]{2,1,0:T(8,128)(2,1)} %copy-done) | copy-start | bytes 884740
  38.6 1.0 %copy-start.3 = (bf16[2,64,1152]{2,1,0:T(8,128)(2,1)S(1)}, bf16[2,64,1152]{2,1,0:T(8,128)(2,1)}, u32[]{:S(2)}) copy-start(bf16[2,64,1152]{2,1,0:T(8,128)(2,1)} %hand.3.refs_2_) | copy-start | bytes 884740
  39.6 1.0 %copy-start.5 = (bf16[2,64,1152]{2,1,0:T(8,128)(2,1)S(1)}, bf16[2,64,1152]{2,1,0:T(8,128)(2,1)}, u32[]{:S(2)}) copy-start(bf16[2,64,1152]{2,1,0:T(8,128)(2,1)} %copy-done.4) | copy-start | bytes 884740
  40.5 1.0 %copy-start.7 = (bf16[2,64,1152]{2,1,0:T(8,128)(2,1)S(1)}, bf16[2,64,1152]{2,1,0:T(8,128)(2,1)}, u32[]{:S(2)}) copy-start(bf16[2,64,1152]{2,1,0:T(8,128)(2,1)} %hand.4.refs_4_) | copy-start | bytes 884740
  44.1 0.7 %copy-start.11 = (bf16[2,64,1152]{2,1,0:T(8,128)(2,1)}, bf16[2,64,1152]{2,1,0:T(8,128)(2,1)S(1)}, u32[]{:S(2)}) copy-start(bf16[2,64,1152]{2,1,0:T(8,128)(2,1)S(1)} %collective-permute-done.5.refs_0_) | copy-start | bytes 884740
  50.8 1.0 %copy-start.12 = (bf16[2,64,1152]{2,1,0:T(8,128)(2,1)S(1)}, bf16[2,64,1152]{2,1,0:T(8,128)(2,1)}, u32[]{:S(2)}) copy-start(bf16[2,64,1152]{2,1,0:T(8,128)(2,1)} %copy-done.11) | copy-start | bytes 884740
  51.7 13.5 %copy-start.9 = (f32[384,512]{1,0:T(8,128)S(1)}, f32[384,512]{1,0:T(8,128)}, u32[]{:S(2)}) copy-start(f32[384,512]{1,0:T(8,128)} %get-tuple-element.19.base_a) | copy-start | bytes 2359300
  54.9 0.6 copy-start.13
  55.5 9.8 %collective-permute-start.10 = (f32[384,512]{1,0:T(8,128)}, f32[384,512]{1,0:T(8,128)S(1)}, u32[]{:S(2)}, u32[]{:S(2)}) collective-permute-start(f32[384,512]{1,0:T(8,128)} %hand.5), channel_id=1, source_target_pairs={{0,1},{1,0},{2,3},{3,2},{4,5},{5,4},{6,7},{7,6},{8,9},{9,8},{10,11... | collective-permute-start | bytes 2359304 | tf_op jit(solution)/shard_map/ppermute | solution.py:332
  55.5 5.2 %collective-permute-start.11 = (bf16[3,128,128]{2,1,0:T(8,128)(2,1)S(1)}, bf16[3,128,128]{2,1,0:T(8,128)(2,1)S(1)}, u32[]{:S(2)}, u32[]{:S(2)}) collective-permute-start(bf16[3,128,128]{2,1,0:T(8,128)(2,1)S(1)} %get-tuple-element.30), channel_id=1, source_target_pairs={{0,2},{2,0},{16,18},{18,16},{1,3},{3,1},{17,19},{19,17},{4,6},{6,4... | collective-permute-start | bytes 294920 | tf_op jit(solution)/shard_map/ppermute | solution.py:345
  56.0 4.9 %collective-permute-start.12 = (bf16[3,128,128]{2,1,0:T(8,128)(2,1)S(1)}, bf16[3,128,128]{2,1,0:T(8,128)(2,1)S(1)}, u32[]{:S(2)}, u32[]{:S(2)}) collective-permute-start(bf16[3,128,128]{2,1,0:T(8,128)(2,1)S(1)} %get-tuple-element.31), channel_id=1, source_target_pairs={{0,16},{2,18},{16,0},{18,2},{1,17},{3,19},{17,1},{19,3},{4,20},{6,... | collective-permute-start | bytes 294920 | tf_op jit(solution)/shard_map/ppermute | solution.py:345
  57.4 6.5 %collective-permute-start.13 = (bf16[3,128,128]{2,1,0:T(8,128)(2,1)S(1)}, bf16[3,128,128]{2,1,0:T(8,128)(2,1)S(1)}, u32[]{:S(2)}, u32[]{:S(2)}) collective-permute-start(bf16[3,128,128]{2,1,0:T(8,128)(2,1)S(1)} %get-tuple-element.32), channel_id=1, source_target_pairs={{0,18},{2,16},{16,2},{18,0},{1,19},{3,17},{17,3},{19,1},{4,22},{6,... | collective-permute-start | bytes 294920 | tf_op jit(solution)/shard_map/ppermute | solution.py:345
  59.0 5.0 %collective-permute-start.14 = (bf16[3,128,128]{2,1,0:T(8,128)(2,1)S(1)}, bf16[3,128,128]{2,1,0:T(8,128)(2,1)S(1)}, u32[]{:S(2)}, u32[]{:S(2)}) collective-permute-start(bf16[3,128,128]{2,1,0:T(8,128)(2,1)S(1)} %get-tuple-element.29.refs_0_), channel_id=1, source_target_pairs={{0,1},{1,0},{2,3},{3,2},{4,5},{5,4},{6,7},{7,6},{8,9},{9,8},{10,11... | collective-permute-start | bytes 294920 | tf_op jit(solution)/shard_map/ppermute | solution.py:332
  60.7 3.3 %collective-permute-start.15 = (bf16[3,128,128]{2,1,0:T(8,128)(2,1)S(1)}, bf16[3,128,128]{2,1,0:T(8,128)(2,1)S(1)}, u32[]{:S(2)}, u32[]{:S(2)}) collective-permute-start(bf16[3,128,128]{2,1,0:T(8,128)(2,1)S(1)} %collective-permute-done.11.refs_1_), channel_id=1, source_target_pairs={{0,1},{1,0},{2,3},{3,2},{4,5},{5,4},{6,7},{7,6},{8,9},{9,8},{10,11... | collective-permute-start | bytes 294920 | tf_op jit(solution)/shard_map/ppermute | solution.py:332
  60.9 3.1 %collective-permute-start.16 = (bf16[3,128,128]{2,1,0:T(8,128)(2,1)S(1)}, bf16[3,128,128]{2,1,0:T(8,128)(2,1)S(1)}, u32[]{:S(2)}, u32[]{:S(2)}) collective-permute-start(bf16[3,128,128]{2,1,0:T(8,128)(2,1)S(1)} %collective-permute-done.12.refs_2_), channel_id=1, source_target_pairs={{0,1},{1,0},{2,3},{3,2},{4,5},{5,4},{6,7},{7,6},{8,9},{9,8},{10,11... | collective-permute-start | bytes 294920 | tf_op jit(solution)/shard_map/ppermute | solution.py:332
  64.0 1.3 %collective-permute-start.17 = (bf16[3,128,128]{2,1,0:T(8,128)(2,1)S(1)}, bf16[3,128,128]{2,1,0:T(8,128)(2,1)S(1)}, u32[]{:S(2)}, u32[]{:S(2)}) collective-permute-start(bf16[3,128,128]{2,1,0:T(8,128)(2,1)S(1)} %collective-permute-done.13.refs_3_), channel_id=1, source_target_pairs={{0,1},{1,0},{2,3},{3,2},{4,5},{5,4},{6,7},{7,6},{8,9},{9,8},{10,11... | collective-permute-start | bytes 294920 | tf_op jit(solution)/shard_map/ppermute | solution.py:332

commit v26 on v25

--- a/solution.py
+++ b/solution.py
@@ -94,9 +94,16 @@
     for b in range(blocks):
         named = jnp.where(lane == b, ids[b].astype(jnp.float32), named)
     named = named.astype(held.dtype)
-    writes = [pltpu.make_async_copy(held.at[k], outs[k], out_sems.at[k]) for k in range(shares)]
+    writes = []
+
+    def write(k, b):
+        here = pl.ds(b * block, block if b < blocks else tall - rows)
+        writes.append(pltpu.make_async_copy(held.at[k, here, :], outs[k].at[here, :], out_sems.at[k, b]))
+        writes[-1].start()
+
     for k in order:
         held[k, rows:, :] = named
+        write(k, blocks)
         for b in range(blocks):
             read(k, b).wait()
 
@@ -107,9 +114,9 @@
                 part = held[k, here, :]
                 held[k, here, :] = jnp.where(row < lengths[b], part, jnp.zeros_like(part))
 
-        writes[k].start()
-    for write in writes:
-        write.wait()
+            write(k, b)
+    for one in writes:
+        one.wait()
 
 
 def spread(tokens, lengths, ids, groups, pair):
@@ -124,7 +131,7 @@
         scratch_shapes=[
             pltpu.VMEM((shares,) + shape, tokens.dtype),
             pltpu.SemaphoreType.DMA((shares, lengths.shape[0])),
-            pltpu.SemaphoreType.DMA((shares,)),
+            pltpu.SemaphoreType.DMA((shares, lengths.shape[0] + 1)),
         ],
         compiler_params=FULL,
         name="spread",
@@ -224,8 +231,8 @@
 
 
 def rank_kernel(ring, pair, rows, shares, owner, held, *refs):
-    late, toks, outs = refs[: -2 - 2 * shares], refs[-2 - 2 * shares : -2 - shares], refs[-2 - shares : -2]
-    flag, picked = refs[-2:]
+    late, toks, outs = refs[: -1 - 2 * shares], refs[-1 - 2 * shares : -1 - shares], refs[-1 - shares : -1]
+    flag = refs[-1]
     flag[...] = jnp.zeros_like(flag)
     rank = held.shape[1]
     per = owner.shape[0] // (ring * pair)
@@ -246,31 +253,21 @@
         way = lax.rem(lax.rem(chip, pair) - y + pair, pair)
         if late:
             half = ring // 2
-            near = away - jnp.where(away > half, 1, 0)
-
-            @pl.when(away != half)
-            def _():
-                picked[i] = held[(way * (ring - 1) + near) * per + local]
-
+            near = jnp.where(away == half, 0, away - jnp.where(away > half, 1, 0))
+            piece = held[(way * (ring - 1) + near) * per + local]
             for w in range(pair):
-
-                @pl.when((away == half) & (way == w))
-                def _():
-                    picked[i] = late[w][local]
-
+                piece = jnp.where((away == half) & (way == w), late[w][local], piece)
         else:
-            picked[i] = held[(way * ring + away) * per + local]
-    for k, tok in enumerate(toks):
-        for b in range(blocks):
-            i = k * blocks + b
-            part = lax.dot_general(
-                picked[i, :, :feats],
-                tok[b * block : (b + 1) * block, :],
-                (((1,), (1,)), ((), ())),
-                preferred_element_type=jnp.float32,
-            )
-            outs[k][b, :rank, :] = part.astype(outs[k].dtype)
-            outs[k][b, rank:, :] = picked[i, :, feats:]
+            piece = held[(way * ring + away) * per + local]
+        k, b = i // blocks, i % blocks
+        part = lax.dot_general(
+            piece[:, :feats],
+            toks[k][b * block : (b + 1) * block, :],
+            (((1,), (1,)), ((), ())),
+            preferred_element_type=jnp.float32,
+        )
+        outs[k][b, :rank, :] = part.astype(outs[k].dtype)
+        outs[k][b, rank:, :] = piece[:, feats:]
 
 
 def rank_parts(owner, toks, held, late, ring, pair, rows, blocks):
@@ -281,7 +278,6 @@
         out_specs=[VMEM] * (shares + 1),
         out_shape=[jax.ShapeDtypeStruct((blocks, 2 * rank, rows // blocks), held.dtype)] * shares
         + [jax.ShapeDtypeStruct((8, LANES), jnp.float32)],
-        scratch_shapes=[pltpu.VMEM((shares * blocks,) + held.shape[1:], held.dtype)],
         cost_estimate=pl.CostEstimate(flops=0, bytes_accessed=0, transcendentals=0),
         compiler_params=ROOM,
         name="rank",

time: 66.7 us -> 65.9 us (0.988)
  Pallas kernels: 18.8 us -> 18 us
    pallas_call x1, Pallas kernels: 3.12 us -> 2.38 us  [rank_parts(): pl.pallas_call(functools.partial(rank_kernel, ring, pair, rows, shares),...]
where the time goes in v26:
time: 65.9 us; the launch traced here: 65.6 us
  waiting for transfers between devices  20.7 us (31%)
  starting transfers between devices  19.9 us (30%)
  Pallas kernels  18 us (27%)
  local copies, waits for them, and re-layouts  6.84 us (10%)
    ppermute x6, waiting for transfers between devices, in_plane(): return lax.ppermute(x, PLANE, pairs)  10.6 us
    ppermute x6, starting transfers between devices, along(): lax.ppermute(x, 'ring', [(a, (a + step) % ring) for a in range(ring)])  9.51 us
    ppermute x6, waiting for transfers between devices, along(): lax.ppermute(x, 'ring', [(a, (a + step) % ring) for a in range(ring)])  8.79 us
    pallas_call x1, Pallas kernels, base_halves(): pl.pallas_call(functools.partial(base_kernel, sides), in_specs=[SMEM, ANY...  7.86 us
    ppermute x6, starting transfers between devices, in_plane(): return lax.ppermute(x, PLANE, pairs)  7.04 us
    unnamed x30, local copies, waits for them, and re-layouts  6.84 us
    pallas_call x1, Pallas kernels, spread(): pl.pallas_call(functools.partial(spread_kernel, groups, pair), in_specs=[...  3.59 us
    ppermute x1, starting transfers between devices, body(): lax.ppermute(packed[pair - w], 'pair', [(a, (a - w) % pair) for a in rang...  3.03 us
  transfers between devices with their start and end apart: 18, of which 9 were waited for; matrix products, arithmetic and copies ran while one was open for 0% of the time, Pallas kernels for 19%

profile of v26, /device:TPU:0, one launch (start us, length us, event | category | flops | bytes accessed | tf_op | source)
XLA Modules:
  0.0 65.6 jit_solution(8742158325357614051)
XLA Ops:
  0.0 1.9 %pack.1 = (bf16[2,64,1152]{2,1,0:T(8,128)(2,1)}, bf16[2,64,1152]{2,1,0:T(8,128)(2,1)}) custom-call(bf16[2,64,4096]{2,1,0:T(8,128)(2,1)} %bitcast.2, bf16[2,64,512]{2,1,0:T(8,128)(2,1)} %up.1), custom_call_target="tpu_custom_call" | custom-call | tf_op jit(solution)/shard_map/pack/pallas_call | solution.py:57
  1.9 3.0 %collective-permute-start.2 = (bf16[2,64,1152]{2,1,0:T(8,128)(2,1)}, bf16[2,64,1152]{2,1,0:T(8,128)(2,1)}, u32[]{:S(2)}, u32[]{:S(2)}) collective-permute-start(bf16[2,64,1152]{2,1,0:T(8,128)(2,1)} %get-tuple-element.23), channel_id=1, source_target_pairs={{0,2},{2,0},{1,3},{3,1},{4,6},{6,4},{5,7},{7,5},{8,10},{10,8},{9,1... | collective-permute-start | bytes 884744 | tf_op jit(solution)/shard_map/ppermute | solution.py:358
  5.0 1.6 %collective-permute-start.1 = (bf16[2,64,1152]{2,1,0:T(8,128)(2,1)}, bf16[2,64,1152]{2,1,0:T(8,128)(2,1)S(1)}, u32[]{:S(2)}, u32[]{:S(2)}) collective-permute-start(bf16[2,64,1152]{2,1,0:T(8,128)(2,1)} %get-tuple-element.21.refs_0_), channel_id=1, source_target_pairs={{0,4},{4,8},{8,12},{12,0},{1,5},{5,9},{9,13},{13,1},{2,6},{6,10},{... | collective-permute-start | bytes 884744 | tf_op jit(solution)/shard_map/ppermute | solution.py:331
  6.5 2.2 %collective-permute-start = (bf16[2,64,1152]{2,1,0:T(8,128)(2,1)}, bf16[2,64,1152]{2,1,0:T(8,128)(2,1)S(1)}, u32[]{:S(2)}, u32[]{:S(2)}) collective-permute-start(bf16[2,64,1152]{2,1,0:T(8,128)(2,1)} %get-tuple-element.21.refs_0_), channel_id=1, source_target_pairs={{0,12},{4,0},{8,4},{12,8},{1,13},{5,1},{9,5},{13,9},{2,14},{6,2},{... | collective-permute-start | bytes 884744 | tf_op jit(solution)/shard_map/ppermute | solution.py:331
  8.8 3.6 %spread.1 = (bf16[400,1024]{1,0:T(8,128)(2,1)}, bf16[400,1024]{1,0:T(8,128)(2,1)}, bf16[400,1024]{1,0:T(8,128)(2,1)}, bf16[400,1024]{1,0:T(8,128)(2,1)}) custom-call(s32[3]{0:T(128)} %lengths.3, s32[3]{0:T(128)} %bitcast.3, bf16[384,4096]{1,0:T(8,128)(2,1)} %tok.3), custom_call_target="tpu_custom_call" | custom-call | tf_op jit(solution)/shard_map/spread/pallas_call | solution.py:126
  12.4 0.4 collective-permute-start.7
  12.7 1.7 %collective-permute-start.8 = (bf16[400,1024]{1,0:T(8,128)(2,1)}, bf16[400,1024]{1,0:T(8,128)(2,1)S(1)}, u32[]{:S(2)}, u32[]{:S(2)}) collective-permute-start(bf16[400,1024]{1,0:T(8,128)(2,1)} %get-tuple-element.26), channel_id=1, source_target_pairs={{0,16},{2,18},{16,0},{18,2},{1,17},{3,19},{17,1},{19,3},{4,20},{6,... | collective-permute-start | bytes 2457608 | tf_op jit(solution)/shard_map/ppermute | solution.py:341
  14.5 0.0 collective-permute-done.2.refs_3_
  14.5 1.5 %collective-permute-start.9 = (bf16[400,1024]{1,0:T(8,128)(2,1)}, bf16[400,1024]{1,0:T(8,128)(2,1)}, u32[]{:S(2)}, u32[]{:S(2)}) collective-permute-start(bf16[400,1024]{1,0:T(8,128)(2,1)} %get-tuple-element.27), channel_id=1, source_target_pairs={{0,18},{2,16},{16,2},{18,0},{1,19},{3,17},{17,3},{19,1},{4,22},{6,... | collective-permute-start | bytes 2457608 | tf_op jit(solution)/shard_map/ppermute | solution.py:341
  16.0 1.0 %collective-permute-done.1.refs_0_ = bf16[2,64,1152]{2,1,0:T(8,128)(2,1)S(1)} collective-permute-done((bf16[2,64,1152]{2,1,0:T(8,128)(2,1)}, bf16[2,64,1152]{2,1,0:T(8,128)(2,1)S(1)}, u32[]{:S(2)}, u32[]{:S(2)}) %collective-permute-start.1) | collective-permute-done | bytes 294944 | tf_op jit(solution)/shard_map/ppermute | solution.py:331
  17.0 0.5 collective-permute-start.4
  17.4 4.6 %collective-permute-done.refs_1_ = bf16[2,64,1152]{2,1,0:T(8,128)(2,1)S(1)} collective-permute-done((bf16[2,64,1152]{2,1,0:T(8,128)(2,1)}, bf16[2,64,1152]{2,1,0:T(8,128)(2,1)S(1)}, u32[]{:S(2)}, u32[]{:S(2)}) %collective-permute-start) | collective-permute-done | bytes 294944 | tf_op jit(solution)/shard_map/ppermute | solution.py:331
  22.1 2.8 %collective-permute-start.3 = (bf16[2,64,1152]{2,1,0:T(8,128)(2,1)}, bf16[2,64,1152]{2,1,0:T(8,128)(2,1)S(1)}, u32[]{:S(2)}, u32[]{:S(2)}) collective-permute-start(bf16[2,64,1152]{2,1,0:T(8,128)(2,1)} %collective-permute-done.2.refs_3_), channel_id=1, source_target_pairs={{0,12},{4,0},{8,4},{12,8},{1,13},{5,1},{9,5},{13,9},{2,14},{6,2},{... | collective-permute-start | bytes 884744 | tf_op jit(solution)/shard_map/ppermute | solution.py:331
  24.9 7.9 %base.1 = (f32[384,512]{1,0:T(8,128)}, f32[384,512]{1,0:T(8,128)}, f32[8,128]{1,0:T(8,128)}) custom-call(s32[3]{0:T(128)} %lengths.3, bf16[384,4096]{1,0:T(8,128)(2,1)} %tok.3, bf16[4096,1024]{1,0:T(8,128)(2,1)} %key.1), custom_call_target="tpu_custom_call" | custom-call | tf_op jit(solution)/shard_map/base/pallas_call | solution.py:190
  32.8 0.0 copy-start.14
  32.8 0.0 collective-permute-done.4.refs_1_.refs_5_
  32.8 0.1 collective-permute-start.5
  32.9 1.7 %collective-permute-done.3.refs_0_ = bf16[2,64,1152]{2,1,0:T(8,128)(2,1)S(1)} collective-permute-done((bf16[2,64,1152]{2,1,0:T(8,128)(2,1)}, bf16[2,64,1152]{2,1,0:T(8,128)(2,1)S(1)}, u32[]{:S(2)}, u32[]{:S(2)}) %collective-permute-start.3) | collective-permute-done | bytes 294944 | tf_op jit(solution)/shard_map/ppermute | solution.py:331
  34.6 0.7 %copy-done.6 = bf16[2,64,1152]{2,1,0:T(8,128)(2,1)} copy-done((bf16[2,64,1152]{2,1,0:T(8,128)(2,1)}, bf16[2,64,1152]{2,1,0:T(8,128)(2,1)S(1)}, u32[]{:S(2)}) %copy-start.6) | copy-done | bytes 294936
  35.3 2.3 %collective-permute-start.6 = (bf16[2,64,1152]{2,1,0:T(8,128)(2,1)}, bf16[2,64,1152]{2,1,0:T(8,128)(2,1)S(1)}, u32[]{:S(2)}, u32[]{:S(2)}) collective-permute-start(bf16[2,64,1152]{2,1,0:T(8,128)(2,1)} %hand.4.refs_4_), channel_id=1, source_target_pairs={{0,12},{4,0},{8,4},{12,8},{1,13},{5,1},{9,5},{13,9},{2,14},{6,2},{... | collective-permute-start | bytes 884744 | tf_op jit(solution)/shard_map/ppermute | solution.py:331
  37.6 1.0 %copy-done.1 = bf16[2,64,1152]{2,1,0:T(8,128)(2,1)S(1)} copy-done((bf16[2,64,1152]{2,1,0:T(8,128)(2,1)S(1)}, bf16[2,64,1152]{2,1,0:T(8,128)(2,1)}, u32[]{:S(2)}) %copy-start.1) | copy-done | bytes 294936
  38.6 1.0 %copy-done.3 = bf16[2,64,1152]{2,1,0:T(8,128)(2,1)S(1)} copy-done((bf16[2,64,1152]{2,1,0:T(8,128)(2,1)S(1)}, bf16[2,64,1152]{2,1,0:T(8,128)(2,1)}, u32[]{:S(2)}) %copy-start.3) | copy-done | bytes 294936
  39.6 1.0 %copy-done.5 = bf16[2,64,1152]{2,1,0:T(8,128)(2,1)S(1)} copy-done((bf16[2,64,1152]{2,1,0:T(8,128)(2,1)S(1)}, bf16[2,64,1152]{2,1,0:T(8,128)(2,1)}, u32[]{:S(2)}) %copy-start.5) | copy-done | bytes 294936
  40.5 1.0 %copy-done.7 = bf16[2,64,1152]{2,1,0:T(8,128)(2,1)S(1)} copy-done((bf16[2,64,1152]{2,1,0:T(8,128)(2,1)S(1)}, bf16[2,64,1152]{2,1,0:T(8,128)(2,1)}, u32[]{:S(2)}) %copy-start.7) | copy-done | bytes 294936
  41.5 1.2 %collect.1.held = bf16[12,64,1152]{2,1,0:T(8,128)(2,1)S(1)} custom-call(bf16[2,64,1152]{2,1,0:T(8,128)(2,1)S(1)} %copy-done.10, bf16[2,64,1152]{2,1,0:T(8,128)(2,1)S(1)} %copy-done.1, bf16[2,64,1152]{2,1,0:T(8,128)(2,1)S(1)} %copy-done.3, bf16[2,64,1152]{2,1,0:T(8,128)(2,1)} %collective-permute-done.2.refs_3_, bf16[2,64,1152]{2,1,0:T(8,128)(2,1)S(1)} %copy-done.7, ...), custom_call_target="tpu_custom_call" | custom-call | tf_op jit(solution)/shard_map/collect/pallas_call | solution.py:222
  42.7 1.4 %collective-permute-done.5.refs_0_ = bf16[2,64,1152]{2,1,0:T(8,128)(2,1)S(1)} collective-permute-done((bf16[2,64,1152]{2,1,0:T(8,128)(2,1)}, bf16[2,64,1152]{2,1,0:T(8,128)(2,1)S(1)}, u32[]{:S(2)}, u32[]{:S(2)}) %collective-permute-start.5) | collective-permute-done | bytes 294944 | tf_op jit(solution)/shard_map/ppermute | solution.py:331
  44.1 0.7 %copy-done.11 = bf16[2,64,1152]{2,1,0:T(8,128)(2,1)} copy-done((bf16[2,64,1152]{2,1,0:T(8,128)(2,1)}, bf16[2,64,1152]{2,1,0:T(8,128)(2,1)S(1)}, u32[]{:S(2)}) %copy-start.11) | copy-done | bytes 294936
  44.9 0.0 collective-permute-done.8.refs_4_
  44.9 5.9 %collective-permute-done.9.refs_5_ = bf16[400,1024]{1,0:T(8,128)(2,1)} collective-permute-done((bf16[400,1024]{1,0:T(8,128)(2,1)}, bf16[400,1024]{1,0:T(8,128)(2,1)}, u32[]{:S(2)}, u32[]{:S(2)}) %collective-permute-start.9) | collective-permute-done | bytes 819232 | tf_op jit(solution)/shard_map/ppermute | solution.py:341
  50.7 0.0 collective-permute-done.6.refs_1_
  50.7 0.0 copy-start.12
  50.7 1.0 %copy-done.12 = bf16[2,64,1152]{2,1,0:T(8,128)(2,1)S(1)} copy-done((bf16[2,64,1152]{2,1,0:T(8,128)(2,1)S(1)}, bf16[2,64,1152]{2,1,0:T(8,128)(2,1)}, u32[]{:S(2)}) %copy-start.12) | copy-done | bytes 294936
  51.7 2.4 %rank.1 = (bf16[3,128,128]{2,1,0:T(8,128)(2,1)S(1)}, bf16[3,128,128]{2,1,0:T(8,128)(2,1)S(1)}, bf16[3,128,128]{2,1,0:T(8,128)(2,1)S(1)}, bf16[3,128,128]{2,1,0:T(8,128)(2,1)S(1)}, f32[8,128]{1,0:T(8,128)S(1)}) custom-call(s32[16]{0:T(128)S(1)} %copy-done.14, bf16[12,64,1152]{2,1,0:T(8,128)(2,1)S(1)} %collect.1.held, bf16[2,64,1152]{2,1,0:T(8,128)(2,1)S(1)} %copy-done.12, ...), custom_call_target="tpu_custom_call" | custom-call | tf_op jit(solution)/shard_map/rank/pallas_call | solution.py:275
  54.1 0.0 copy-start.13
  54.1 0.6 copy-done.13
  54.7 0.0 collective-permute-start.10
  54.7 0.5 collective-permute-start.11
  55.2 1.5 %collective-permute-start.12 = (bf16[3,128,128]{2,1,0:T(8,128)(2,1)S(1)}, bf16[3,128,128]{2,1,0:T(8,128)(2,1)S(1)}, u32[]{:S(2)}, u32[]{:S(2)}) collective-permute-start(bf16[3,128,128]{2,1,0:T(8,128)(2,1)S(1)} %get-tuple-element.31), channel_id=1, source_target_pairs={{0,16},{2,18},{16,0},{18,2},{1,17},{3,19},{17,1},{19,3},{4,20},{6,... | collective-permute-start | bytes 294920 | tf_op jit(solution)/shard_map/ppermute | solution.py:341
  56.7 1.5 %collective-permute-start.13 = (bf16[3,128,128]{2,1,0:T(8,128)(2,1)S(1)}, bf16[3,128,128]{2,1,0:T(8,128)(2,1)S(1)}, u32[]{:S(2)}, u32[]{:S(2)}) collective-permute-start(bf16[3,128,128]{2,1,0:T(8,128)(2,1)S(1)} %get-tuple-element.32), channel_id=1, source_target_pairs={{0,18},{2,16},{16,2},{18,0},{1,19},{3,17},{17,3},{19,1},{4,22},{6,... | collective-permute-start | bytes 294920 | tf_op jit(solution)/shard_map/ppermute | solution.py:341
  58.2 1.7 %collective-permute-done.11.refs_1_ = bf16[3,128,128]{2,1,0:T(8,128)(2,1)S(1)} collective-permute-done((bf16[3,128,128]{2,1,0:T(8,128)(2,1)S(1)}, bf16[3,128,128]{2,1,0:T(8,128)(2,1)S(1)}, u32[]{:S(2)}, u32[]{:S(2)}) %collective-permute-start.11) | collective-permute-done | bytes 98336 | tf_op jit(solution)/shard_map/ppermute | solution.py:341
  59.9 0.2 collective-permute-done.12.refs_2_
  60.1 0.3 collective-permute-start.16
  60.4 2.8 %collective-permute-done.13.refs_3_ = bf16[3,128,128]{2,1,0:T(8,128)(2,1)S(1)} collective-permute-done((bf16[3,128,128]{2,1,0:T(8,128)(2,1)S(1)}, bf16[3,128,128]{2,1,0:T(8,128)(2,1)S(1)}, u32[]{:S(2)}, u32[]{:S(2)}) %collective-permute-start.13) | collective-permute-done | bytes 98336 | tf_op jit(solution)/shard_map/ppermute | solution.py:341
  63.2 0.0 collective-permute-start.17
  63.2 0.0 collective-permute-done.14.refs_4_
  63.2 0.0 collective-permute-done.15.refs_5_
  63.2 1.3 %collective-permute-done.17.refs_7_ = bf16[3,128,128]{2,1,0:T(8,128)(2,1)S(1)} collective-permute-done((bf16[3,128,128]{2,1,0:T(8,128)(2,1)S(1)}, bf16[3,128,128]{2,1,0:T(8,128)(2,1)S(1)}, u32[]{:S(2)}, u32[]{:S(2)}) %collective-permute-start.17) | collective-permute-done | bytes 98336 | tf_op jit(solution)/shard_map/ppermute | solution.py:328
  64.5 1.1 %final.1 = bf16[384,512]{1,0:T(8,128)(2,1)} custom-call(f32[384,512]{1,0:T(8,128)S(1)} %copy-done.9, f32[384,512]{1,0:T(8,128)S(1)} %collective-permute-done.10.base_b, bf16[3,128,128]{2,1,0:T(8,128)(2,1)S(1)} %get-tuple-element.29.refs_0_, bf16[3,128,128]{2,1,0:T(8,128)(2,1)S(1)} %collective-permute-done.11.refs_1_, ...), custom_call_target="tpu_custom_call" | custom-call | tf_op jit(solution)/shard_map/final/pallas_call | solution.py:309
  (27 shorter events, 0.1 us)
Async XLA Ops:
  1.9 12.5 %collective-permute-start.2 = (bf16[2,64,1152]{2,1,0:T(8,128)(2,1)}, bf16[2,64,1152]{2,1,0:T(8,128)(2,1)}, u32[]{:S(2)}, u32[]{:S(2)}) collective-permute-start(bf16[2,64,1152]{2,1,0:T(8,128)(2,1)} %get-tuple-element.23), channel_id=1, source_target_pairs={{0,2},{2,0},{1,3},{3,1},{4,6},{6,4},{5,7},{7,5},{8,10},{10,8},{9,1... | collective-permute-start | bytes 884744 | tf_op jit(solution)/shard_map/ppermute | solution.py:358
  5.0 12.0 %collective-permute-start.1 = (bf16[2,64,1152]{2,1,0:T(8,128)(2,1)}, bf16[2,64,1152]{2,1,0:T(8,128)(2,1)S(1)}, u32[]{:S(2)}, u32[]{:S(2)}) collective-permute-start(bf16[2,64,1152]{2,1,0:T(8,128)(2,1)} %get-tuple-element.21.refs_0_), channel_id=1, source_target_pairs={{0,4},{4,8},{8,12},{12,0},{1,5},{5,9},{9,13},{13,1},{2,6},{6,10},{... | collective-permute-start | bytes 884744 | tf_op jit(solution)/shard_map/ppermute | solution.py:331
  6.5 15.5 %collective-permute-start = (bf16[2,64,1152]{2,1,0:T(8,128)(2,1)}, bf16[2,64,1152]{2,1,0:T(8,128)(2,1)S(1)}, u32[]{:S(2)}, u32[]{:S(2)}) collective-permute-start(bf16[2,64,1152]{2,1,0:T(8,128)(2,1)} %get-tuple-element.21.refs_0_), channel_id=1, source_target_pairs={{0,12},{4,0},{8,4},{12,8},{1,13},{5,1},{9,5},{13,9},{2,14},{6,2},{... | collective-permute-start | bytes 884744 | tf_op jit(solution)/shard_map/ppermute | solution.py:331
  12.4 32.5 %collective-permute-start.7 = (bf16[400,1024]{1,0:T(8,128)(2,1)}, bf16[400,1024]{1,0:T(8,128)(2,1)S(1)}, u32[]{:S(2)}, u32[]{:S(2)}) collective-permute-start(bf16[400,1024]{1,0:T(8,128)(2,1)} %get-tuple-element.25), channel_id=1, source_target_pairs={{0,2},{2,0},{16,18},{18,16},{1,3},{3,1},{17,19},{19,17},{4,6},{6,4... | collective-permute-start | bytes 2457608 | tf_op jit(solution)/shard_map/ppermute | solution.py:341
  12.7 32.1 %collective-permute-start.8 = (bf16[400,1024]{1,0:T(8,128)(2,1)}, bf16[400,1024]{1,0:T(8,128)(2,1)S(1)}, u32[]{:S(2)}, u32[]{:S(2)}) collective-permute-start(bf16[400,1024]{1,0:T(8,128)(2,1)} %get-tuple-element.26), channel_id=1, source_target_pairs={{0,16},{2,18},{16,0},{18,2},{1,17},{3,19},{17,1},{19,3},{4,20},{6,... | collective-permute-start | bytes 2457608 | tf_op jit(solution)/shard_map/ppermute | solution.py:341
  14.5 23.2 %copy-start.10 = (bf16[2,64,1152]{2,1,0:T(8,128)(2,1)S(1)}, bf16[2,64,1152]{2,1,0:T(8,128)(2,1)}, u32[]{:S(2)}) copy-start(bf16[2,64,1152]{2,1,0:T(8,128)(2,1)} %get-tuple-element.21.refs_0_) | copy-start | bytes 884740
  14.5 36.3 %collective-permute-start.9 = (bf16[400,1024]{1,0:T(8,128)(2,1)}, bf16[400,1024]{1,0:T(8,128)(2,1)}, u32[]{:S(2)}, u32[]{:S(2)}) collective-permute-start(bf16[400,1024]{1,0:T(8,128)(2,1)} %get-tuple-element.27), channel_id=1, source_target_pairs={{0,18},{2,16},{16,2},{18,0},{1,19},{3,17},{17,3},{19,1},{4,22},{6,... | collective-permute-start | bytes 2457608 | tf_op jit(solution)/shard_map/ppermute | solution.py:341
  16.9 15.8 %copy-start.2 = (bf16[2,64,1152]{2,1,0:T(8,128)(2,1)}, bf16[2,64,1152]{2,1,0:T(8,128)(2,1)S(1)}, u32[]{:S(2)}) copy-start(bf16[2,64,1152]{2,1,0:T(8,128)(2,1)S(1)} %collective-permute-done.1.refs_0_) | copy-start | bytes 884740
  17.0 15.8 %collective-permute-start.4 = (bf16[2,64,1152]{2,1,0:T(8,128)(2,1)}, bf16[2,64,1152]{2,1,0:T(8,128)(2,1)S(1)}, u32[]{:S(2)}, u32[]{:S(2)}) collective-permute-start(bf16[2,64,1152]{2,1,0:T(8,128)(2,1)} %collective-permute-done.2.refs_3_), channel_id=1, source_target_pairs={{0,4},{4,8},{8,12},{12,0},{1,5},{5,9},{9,13},{13,1},{2,6},{6,10},{... | collective-permute-start | bytes 884744 | tf_op jit(solution)/shard_map/ppermute | solution.py:331
  22.1 10.7 %copy-start = (bf16[2,64,1152]{2,1,0:T(8,128)(2,1)}, bf16[2,64,1152]{2,1,0:T(8,128)(2,1)S(1)}, u32[]{:S(2)}) copy-start(bf16[2,64,1152]{2,1,0:T(8,128)(2,1)S(1)} %collective-permute-done.refs_1_) | copy-start | bytes 884740
  22.1 12.5 %collective-permute-start.3 = (bf16[2,64,1152]{2,1,0:T(8,128)(2,1)}, bf16[2,64,1152]{2,1,0:T(8,128)(2,1)S(1)}, u32[]{:S(2)}, u32[]{:S(2)}) collective-permute-start(bf16[2,64,1152]{2,1,0:T(8,128)(2,1)} %collective-permute-done.2.refs_3_), channel_id=1, source_target_pairs={{0,12},{4,0},{8,4},{12,8},{1,13},{5,1},{9,5},{13,9},{2,14},{6,2},{... | collective-permute-start | bytes 884744 | tf_op jit(solution)/shard_map/ppermute | solution.py:331
  32.7 18.0 %copy-start.8 = (bf16[400,1024]{1,0:T(8,128)(2,1)S(1)}, bf16[400,1024]{1,0:T(8,128)(2,1)}, u32[]{:S(2)}) copy-start(bf16[400,1024]{1,0:T(8,128)(2,1)} %get-tuple-element.24.refs_2_) | copy-start | bytes 2457604
  32.8 18.0 %copy-start.14 = (s32[16]{0:T(128)S(1)}, s32[16]{0:T(128)}, u32[]{:S(2)}) copy-start(s32[16]{0:T(128)} %owner.1) | copy-start | bytes 196
  32.8 1.8 %copy-start.4 = (bf16[2,64,1152]{2,1,0:T(8,128)(2,1)}, bf16[2,64,1152]{2,1,0:T(8,128)(2,1)S(1)}, u32[]{:S(2)}) copy-start(bf16[2,64,1152]{2,1,0:T(8,128)(2,1)S(1)} %collective-permute-done.4.refs_1_.refs_5_) | copy-start | bytes 884740
  32.8 11.3 %collective-permute-start.5 = (bf16[2,64,1152]{2,1,0:T(8,128)(2,1)}, bf16[2,64,1152]{2,1,0:T(8,128)(2,1)S(1)}, u32[]{:S(2)}, u32[]{:S(2)}) collective-permute-start(bf16[2,64,1152]{2,1,0:T(8,128)(2,1)} %hand.3.refs_2_), channel_id=1, source_target_pairs={{0,4},{4,8},{8,12},{12,0},{1,5},{5,9},{9,13},{13,1},{2,6},{6,10},{... | collective-permute-start | bytes 884744 | tf_op jit(solution)/shard_map/ppermute | solution.py:331
  34.6 0.7 %copy-start.6 = (bf16[2,64,1152]{2,1,0:T(8,128)(2,1)}, bf16[2,64,1152]{2,1,0:T(8,128)(2,1)S(1)}, u32[]{:S(2)}) copy-start(bf16[2,64,1152]{2,1,0:T(8,128)(2,1)S(1)} %collective-permute-done.3.refs_0_) | copy-start | bytes 884740
  35.3 15.4 %collective-permute-start.6 = (bf16[2,64,1152]{2,1,0:T(8,128)(2,1)}, bf16[2,64,1152]{2,1,0:T(8,128)(2,1)S(1)}, u32[]{:S(2)}, u32[]{:S(2)}) collective-permute-start(bf16[2,64,1152]{2,1,0:T(8,128)(2,1)} %hand.4.refs_4_), channel_id=1, source_target_pairs={{0,12},{4,0},{8,4},{12,8},{1,13},{5,1},{9,5},{13,9},{2,14},{6,2},{... | collective-permute-start | bytes 884744 | tf_op jit(solution)/shard_map/ppermute | solution.py:331
  37.6 1.0 %copy-start.1 = (bf16[2,64,1152]{2,1,0:T(8,128)(2,1)S(1)}, bf16[2,64,1152]{2,1,0:T(8,128)(2,1)}, u32[]{:S(2)}) copy-start(bf16[2,64,1152]{2,1,0:T(8,128)(2,1)} %copy-done) | copy-start | bytes 884740
  38.6 1.0 %copy-start.3 = (bf16[2,64,1152]{2,1,0:T(8,128)(2,1)S(1)}, bf16[2,64,1152]{2,1,0:T(8,128)(2,1)}, u32[]{:S(2)}) copy-start(bf16[2,64,1152]{2,1,0:T(8,128)(2,1)} %hand.3.refs_2_) | copy-start | bytes 884740
  39.6 1.0 %copy-start.5 = (bf16[2,64,1152]{2,1,0:T(8,128)(2,1)S(1)}, bf16[2,64,1152]{2,1,0:T(8,128)(2,1)}, u32[]{:S(2)}) copy-start(bf16[2,64,1152]{2,1,0:T(8,128)(2,1)} %copy-done.4) | copy-start | bytes 884740
  40.5 1.0 %copy-start.7 = (bf16[2,64,1152]{2,1,0:T(8,128)(2,1)S(1)}, bf16[2,64,1152]{2,1,0:T(8,128)(2,1)}, u32[]{:S(2)}) copy-start(bf16[2,64,1152]{2,1,0:T(8,128)(2,1)} %hand.4.refs_4_) | copy-start | bytes 884740
  44.1 0.7 %copy-start.11 = (bf16[2,64,1152]{2,1,0:T(8,128)(2,1)}, bf16[2,64,1152]{2,1,0:T(8,128)(2,1)S(1)}, u32[]{:S(2)}) copy-start(bf16[2,64,1152]{2,1,0:T(8,128)(2,1)S(1)} %collective-permute-done.5.refs_0_) | copy-start | bytes 884740
  50.7 1.0 %copy-start.12 = (bf16[2,64,1152]{2,1,0:T(8,128)(2,1)S(1)}, bf16[2,64,1152]{2,1,0:T(8,128)(2,1)}, u32[]{:S(2)}) copy-start(bf16[2,64,1152]{2,1,0:T(8,128)(2,1)} %copy-done.11) | copy-start | bytes 884740
  51.7 12.8 %copy-start.9 = (f32[384,512]{1,0:T(8,128)S(1)}, f32[384,512]{1,0:T(8,128)}, u32[]{:S(2)}) copy-start(f32[384,512]{1,0:T(8,128)} %get-tuple-element.19.base_a) | copy-start | bytes 2359300
  54.1 0.6 copy-start.13
  54.7 9.8 %collective-permute-start.10 = (f32[384,512]{1,0:T(8,128)}, f32[384,512]{1,0:T(8,128)S(1)}, u32[]{:S(2)}, u32[]{:S(2)}) collective-permute-start(f32[384,512]{1,0:T(8,128)} %hand.5), channel_id=1, source_target_pairs={{0,1},{1,0},{2,3},{3,2},{4,5},{5,4},{6,7},{7,6},{8,9},{9,8},{10,11... | collective-permute-start | bytes 2359304 | tf_op jit(solution)/shard_map/ppermute | solution.py:328
  54.7 5.2 %collective-permute-start.11 = (bf16[3,128,128]{2,1,0:T(8,128)(2,1)S(1)}, bf16[3,128,128]{2,1,0:T(8,128)(2,1)S(1)}, u32[]{:S(2)}, u32[]{:S(2)}) collective-permute-start(bf16[3,128,128]{2,1,0:T(8,128)(2,1)S(1)} %get-tuple-element.30), channel_id=1, source_target_pairs={{0,2},{2,0},{16,18},{18,16},{1,3},{3,1},{17,19},{19,17},{4,6},{6,4... | collective-permute-start | bytes 294920 | tf_op jit(solution)/shard_map/ppermute | solution.py:341
  55.2 4.9 %collective-permute-start.12 = (bf16[3,128,128]{2,1,0:T(8,128)(2,1)S(1)}, bf16[3,128,128]{2,1,0:T(8,128)(2,1)S(1)}, u32[]{:S(2)}, u32[]{:S(2)}) collective-permute-start(bf16[3,128,128]{2,1,0:T(8,128)(2,1)S(1)} %get-tuple-element.31), channel_id=1, source_target_pairs={{0,16},{2,18},{16,0},{18,2},{1,17},{3,19},{17,1},{19,3},{4,20},{6,... | collective-permute-start | bytes 294920 | tf_op jit(solution)/shard_map/ppermute | solution.py:341
  56.7 6.5 %collective-permute-start.13 = (bf16[3,128,128]{2,1,0:T(8,128)(2,1)S(1)}, bf16[3,128,128]{2,1,0:T(8,128)(2,1)S(1)}, u32[]{:S(2)}, u32[]{:S(2)}) collective-permute-start(bf16[3,128,128]{2,1,0:T(8,128)(2,1)S(1)} %get-tuple-element.32), channel_id=1, source_target_pairs={{0,18},{2,16},{16,2},{18,0},{1,19},{3,17},{17,3},{19,1},{4,22},{6,... | collective-permute-start | bytes 294920 | tf_op jit(solution)/shard_map/ppermute | solution.py:341
  58.2 5.0 %collective-permute-start.14 = (bf16[3,128,128]{2,1,0:T(8,128)(2,1)S(1)}, bf16[3,128,128]{2,1,0:T(8,128)(2,1)S(1)}, u32[]{:S(2)}, u32[]{:S(2)}) collective-permute-start(bf16[3,128,128]{2,1,0:T(8,128)(2,1)S(1)} %get-tuple-element.29.refs_0_), channel_id=1, source_target_pairs={{0,1},{1,0},{2,3},{3,2},{4,5},{5,4},{6,7},{7,6},{8,9},{9,8},{10,11... | collective-permute-start | bytes 294920 | tf_op jit(solution)/shard_map/ppermute | solution.py:328
  59.9 3.3 %collective-permute-start.15 = (bf16[3,128,128]{2,1,0:T(8,128)(2,1)S(1)}, bf16[3,128,128]{2,1,0:T(8,128)(2,1)S(1)}, u32[]{:S(2)}, u32[]{:S(2)}) collective-permute-start(bf16[3,128,128]{2,1,0:T(8,128)(2,1)S(1)} %collective-permute-done.11.refs_1_), channel_id=1, source_target_pairs={{0,1},{1,0},{2,3},{3,2},{4,5},{5,4},{6,7},{7,6},{8,9},{9,8},{10,11... | collective-permute-start | bytes 294920 | tf_op jit(solution)/shard_map/ppermute | solution.py:328
  60.1 3.1 %collective-permute-start.16 = (bf16[3,128,128]{2,1,0:T(8,128)(2,1)S(1)}, bf16[3,128,128]{2,1,0:T(8,128)(2,1)S(1)}, u32[]{:S(2)}, u32[]{:S(2)}) collective-permute-start(bf16[3,128,128]{2,1,0:T(8,128)(2,1)S(1)} %collective-permute-done.12.refs_2_), channel_id=1, source_target_pairs={{0,1},{1,0},{2,3},{3,2},{4,5},{5,4},{6,7},{7,6},{8,9},{9,8},{10,11... | collective-permute-start | bytes 294920 | tf_op jit(solution)/shard_map/ppermute | solution.py:328
  63.2 1.3 %collective-permute-start.17 = (bf16[3,128,128]{2,1,0:T(8,128)(2,1)S(1)}, bf16[3,128,128]{2,1,0:T(8,128)(2,1)S(1)}, u32[]{:S(2)}, u32[]{:S(2)}) collective-permute-start(bf16[3,128,128]{2,1,0:T(8,128)(2,1)S(1)} %collective-permute-done.13.refs_3_), channel_id=1, source_target_pairs={{0,1},{1,0},{2,3},{3,2},{4,5},{5,4},{6,7},{7,6},{8,9},{9,8},{10,11... | collective-permute-start | bytes 294920 | tf_op jit(solution)/shard_map/ppermute | solution.py:328

commit v27 on v26

--- a/solution.py
+++ b/solution.py
@@ -230,8 +230,8 @@
     )(*pieces)
 
 
-def rank_kernel(ring, pair, rows, shares, owner, held, *refs):
-    late, toks, outs = refs[: -1 - 2 * shares], refs[-1 - 2 * shares : -1 - shares], refs[-1 - shares : -1]
+def rank_kernel(ring, pair, rows, count, owner, held, *refs):
+    late, toks, outs = refs[: -1 - 2 * count], refs[-1 - 2 * count : -1 - count], refs[-1 - count : -1]
     flag = refs[-1]
     flag[...] = jnp.zeros_like(flag)
     rank = held.shape[1]
@@ -251,14 +251,13 @@
         local = lax.rem(slot, per)
         away = lax.rem(chip // pair - z + ring, ring)
         way = lax.rem(lax.rem(chip, pair) - y + pair, pair)
+        at = way * ring + away
         if late:
-            half = ring // 2
-            near = jnp.where(away == half, 0, away - jnp.where(away > half, 1, 0))
-            piece = held[(way * (ring - 1) + near) * per + local]
-            for w in range(pair):
-                piece = jnp.where((away == half) & (way == w), late[w][local], piece)
+            missing = (pair - 1) * ring + ring // 2
+            piece = held[jnp.where(at == missing, 0, at - jnp.where(at > missing, 1, 0)) * per + local]
+            piece = jnp.where(at == missing, late[0][local], piece)
         else:
-            piece = held[(way * ring + away) * per + local]
+            piece = held[at * per + local]
         k, b = i // blocks, i % blocks
         part = lax.dot_general(
             piece[:, :feats],
@@ -271,12 +270,12 @@
 
 
 def rank_parts(owner, toks, held, late, ring, pair, rows, blocks):
-    shares, rank = len(toks), held.shape[1]
-    return pl.pallas_call(
-        functools.partial(rank_kernel, ring, pair, rows, shares),
-        in_specs=[SMEM, VMEM] + [VMEM] * (len(late) + shares),
-        out_specs=[VMEM] * (shares + 1),
-        out_shape=[jax.ShapeDtypeStruct((blocks, 2 * rank, rows // blocks), held.dtype)] * shares
+    count, rank = len(toks), held.shape[1]
+    return pl.pallas_call(
+        functools.partial(rank_kernel, ring, pair, rows, count),
+        in_specs=[SMEM, VMEM] + [VMEM] * (len(late) + count),
+        out_specs=[VMEM] * (count + 1),
+        out_shape=[jax.ShapeDtypeStruct((blocks, 2 * rank, rows // blocks), held.dtype)] * count
         + [jax.ShapeDtypeStruct((8, LANES), jnp.float32)],
         cost_estimate=pl.CostEstimate(flops=0, bytes_accessed=0, transcendentals=0),
         compiler_params=ROOM,
@@ -366,11 +365,12 @@
         for way, held in enumerate(firsts)
     ]
 
-    halfway = ring // 2 if ring % 2 == 0 else ring
-    held = collect([piece for way in pieces for away, piece in enumerate(way) if away != halfway])
-    late = [way[halfway] for way in pieces] if halfway < ring else []
-    *parts, ready = rank_parts(owner_slot, toks, held, late, ring, pair, rows, blocks)
-    mine = [parts[0]] + [in_plane(parts[k], -(k // pair), -(k % pair)) for k in range(1, shares)]
+    flat = [piece for way in pieces for piece in way]
+    late = [flat.pop((pair - 1) * ring + ring // 2)] if ring % 2 == 0 else []
+    held = collect(flat)
+    *parts, ready = rank_parts(owner_slot, toks[1:], held, late, ring, pair, rows, blocks)
+    own_part = rank_parts(owner_slot, toks[:1], held, late, ring, pair, rows, blocks)[0]
+    mine = [own_part] + [in_plane(parts[k - 1], -(k // pair), -(k % pair)) for k in range(1, shares)]
     theirs = [across(part) for part in mine]
     base_in = across(hand_on(base_out, ready))
     return final(mine, theirs, [base_mine, base_in], groups, pair, tokens.dtype)

time: 65.9 us -> 68.3 us (1.036); the launches traced: 65.6 us -> 67.2 us
  local copies, waits for them, and re-layouts: 6.84 us -> 11.1 us
  waiting for transfers between devices: 20.7 us -> 17.3 us
    ppermute x6, waiting for transfers between devices: 10.6 us -> 2.02 us  [in_plane(): return lax.ppermute(x, PLANE, pairs)]
    ppermute x6, waiting for transfers between devices: 8.79 us -> 14 us  [along(): lax.ppermute(x, 'ring', [(a, (a + step) % ring) for a in range(ring)])]
    unnamed x30 -> x38, local copies, waits for them, and re-layouts: 6.84 us -> 11.1 us
    pallas_call x1 -> x2, Pallas kernels: 2.38 us -> 3.68 us  [rank_parts(): pl.pallas_call(functools.partial(rank_kernel, ring, pair, rows, count), i...]
    pallas_call x1, Pallas kernels: 1.19 us -> 0.49 us  [collect(): pl.pallas_call(collect_kernel, in_specs=[ANY] * len(pieces), out_specs=VM...]
  transfers between devices with their start and end apart: 18 -> 18, of which waited for: 9 -> 6; matrix products, arithmetic and copies ran while one was open for 0% -> 0% of each run, Pallas kernels for 19% -> 20%
where the time goes in v27:
time: 68.3 us; the launch traced here: 67.2 us
  starting transfers between devices  20 us (29%)
  Pallas kernels  18.5 us (27%)
  waiting for transfers between devices  17.3 us (25%)
  local copies, waits for them, and re-layouts  11.1 us (16%)
    ppermute x6, waiting for transfers between devices, along(): lax.ppermute(x, 'ring', [(a, (a + step) % ring) for a in range(ring)])  14 us
    unnamed x38, local copies, waits for them, and re-layouts  11.1 us
    ppermute x6, starting transfers between devices, along(): lax.ppermute(x, 'ring', [(a, (a + step) % ring) for a in range(ring)])  9.37 us
    pallas_call x1, Pallas kernels, base_halves(): pl.pallas_call(functools.partial(base_kernel, sides), in_specs=[SMEM, ANY...  7.83 us
    ppermute x6, starting transfers between devices, in_plane(): return lax.ppermute(x, PLANE, pairs)  7.04 us
    pallas_call x2, Pallas kernels, rank_parts(): pl.pallas_call(functools.partial(rank_kernel, ring, pair, rows, count), i...  3.68 us
    pallas_call x1, Pallas kernels, spread(): pl.pallas_call(functools.partial(spread_kernel, groups, pair), in_specs=[...  3.6 us
    ppermute x1, starting transfers between devices, body(): lax.ppermute(packed[pair - w], 'pair', [(a, (a - w) % pair) for a in rang...  3.03 us
  transfers between devices with their start and end apart: 18, of which 6 were waited for; matrix products, arithmetic and copies ran while one was open for 0% of the time, Pallas kernels for 20%

profile of v27, /device:TPU:0, one launch (start us, length us, event | category | flops | bytes accessed | tf_op | source)
XLA Modules:
  0.0 67.2 jit_solution(10317419089654562016)
XLA Ops:
  0.0 1.9 %pack.1 = (bf16[2,64,1152]{2,1,0:T(8,128)(2,1)}, bf16[2,64,1152]{2,1,0:T(8,128)(2,1)}) custom-call(bf16[2,64,4096]{2,1,0:T(8,128)(2,1)} %bitcast.2, bf16[2,64,512]{2,1,0:T(8,128)(2,1)} %up.1), custom_call_target="tpu_custom_call" | custom-call | tf_op jit(solution)/shard_map/pack/pallas_call | solution.py:57
  1.9 3.0 %collective-permute-start.3 = (bf16[2,64,1152]{2,1,0:T(8,128)(2,1)}, bf16[2,64,1152]{2,1,0:T(8,128)(2,1)S(1)}, u32[]{:S(2)}, u32[]{:S(2)}) collective-permute-start(bf16[2,64,1152]{2,1,0:T(8,128)(2,1)} %get-tuple-element.23), channel_id=1, source_target_pairs={{0,2},{2,0},{1,3},{3,1},{4,6},{6,4},{5,7},{7,5},{8,10},{10,8},{9,1... | collective-permute-start | bytes 884744 | tf_op jit(solution)/shard_map/ppermute | solution.py:357
  4.9 1.6 %collective-permute-start.1 = (bf16[2,64,1152]{2,1,0:T(8,128)(2,1)}, bf16[2,64,1152]{2,1,0:T(8,128)(2,1)S(1)}, u32[]{:S(2)}, u32[]{:S(2)}) collective-permute-start(bf16[2,64,1152]{2,1,0:T(8,128)(2,1)} %get-tuple-element.21.refs_0_), channel_id=1, source_target_pairs={{0,4},{4,8},{8,12},{12,0},{1,5},{5,9},{9,13},{13,1},{2,6},{6,10},{... | collective-permute-start | bytes 884744 | tf_op jit(solution)/shard_map/ppermute | solution.py:330
  6.5 2.2 %collective-permute-start = (bf16[2,64,1152]{2,1,0:T(8,128)(2,1)}, bf16[2,64,1152]{2,1,0:T(8,128)(2,1)S(1)}, u32[]{:S(2)}, u32[]{:S(2)}) collective-permute-start(bf16[2,64,1152]{2,1,0:T(8,128)(2,1)} %get-tuple-element.21.refs_0_), channel_id=1, source_target_pairs={{0,12},{4,0},{8,4},{12,8},{1,13},{5,1},{9,5},{13,9},{2,14},{6,2},{... | collective-permute-start | bytes 884744 | tf_op jit(solution)/shard_map/ppermute | solution.py:330
  8.8 3.6 %spread.1 = (bf16[400,1024]{1,0:T(8,128)(2,1)}, bf16[400,1024]{1,0:T(8,128)(2,1)}, bf16[400,1024]{1,0:T(8,128)(2,1)}, bf16[400,1024]{1,0:T(8,128)(2,1)}) custom-call(s32[3]{0:T(128)} %lengths.3, s32[3]{0:T(128)} %bitcast.3, bf16[384,4096]{1,0:T(8,128)(2,1)} %tok.3), custom_call_target="tpu_custom_call" | custom-call | tf_op jit(solution)/shard_map/spread/pallas_call | solution.py:126
  12.4 0.3 collective-permute-start.7
  12.7 1.7 %collective-permute-start.8 = (bf16[400,1024]{1,0:T(8,128)(2,1)}, bf16[400,1024]{1,0:T(8,128)(2,1)S(1)}, u32[]{:S(2)}, u32[]{:S(2)}) collective-permute-start(bf16[400,1024]{1,0:T(8,128)(2,1)} %get-tuple-element.25), channel_id=1, source_target_pairs={{0,16},{2,18},{16,0},{18,2},{1,17},{3,19},{17,1},{19,3},{4,20},{6,... | collective-permute-start | bytes 2457608 | tf_op jit(solution)/shard_map/ppermute | solution.py:340
  14.4 0.0 collective-permute-done.3.refs_4_
  14.4 1.5 %collective-permute-start.9 = (bf16[400,1024]{1,0:T(8,128)(2,1)}, bf16[400,1024]{1,0:T(8,128)(2,1)}, u32[]{:S(2)}, u32[]{:S(2)}) collective-permute-start(bf16[400,1024]{1,0:T(8,128)(2,1)} %get-tuple-element.26), channel_id=1, source_target_pairs={{0,18},{2,16},{16,2},{18,0},{1,19},{3,17},{17,3},{19,1},{4,22},{6,... | collective-permute-start | bytes 2457608 | tf_op jit(solution)/shard_map/ppermute | solution.py:340
  15.9 1.0 %collective-permute-done.1.refs_0_ = bf16[2,64,1152]{2,1,0:T(8,128)(2,1)S(1)} collective-permute-done((bf16[2,64,1152]{2,1,0:T(8,128)(2,1)}, bf16[2,64,1152]{2,1,0:T(8,128)(2,1)S(1)}, u32[]{:S(2)}, u32[]{:S(2)}) %collective-permute-start.1) | collective-permute-done | bytes 294944 | tf_op jit(solution)/shard_map/ppermute | solution.py:330
  16.9 0.4 collective-permute-start.5
  17.3 4.7 %collective-permute-done.refs_1_ = bf16[2,64,1152]{2,1,0:T(8,128)(2,1)S(1)} collective-permute-done((bf16[2,64,1152]{2,1,0:T(8,128)(2,1)}, bf16[2,64,1152]{2,1,0:T(8,128)(2,1)S(1)}, u32[]{:S(2)}, u32[]{:S(2)}) %collective-permute-start) | collective-permute-done | bytes 294944 | tf_op jit(solution)/shard_map/ppermute | solution.py:330
  22.0 2.8 %collective-permute-start.4 = (bf16[2,64,1152]{2,1,0:T(8,128)(2,1)S(1)}, bf16[2,64,1152]{2,1,0:T(8,128)(2,1)S(1)}, u32[]{:S(2)}, u32[]{:S(2)}) collective-permute-start(bf16[2,64,1152]{2,1,0:T(8,128)(2,1)S(1)} %collective-permute-done.3.refs_4_), channel_id=1, source_target_pairs={{0,12},{4,0},{8,4},{12,8},{1,13},{5,1},{9,5},{13,9},{2,14},{6,2},{... | collective-permute-start | bytes 884744 | tf_op jit(solution)/shard_map/ppermute | solution.py:330
  24.8 7.8 %base.1 = (f32[384,512]{1,0:T(8,128)}, f32[384,512]{1,0:T(8,128)}, f32[8,128]{1,0:T(8,128)}) custom-call(s32[3]{0:T(128)} %lengths.3, bf16[384,4096]{1,0:T(8,128)(2,1)} %tok.3, bf16[4096,1024]{1,0:T(8,128)(2,1)} %key.1), custom_call_target="tpu_custom_call" | custom-call | tf_op jit(solution)/shard_map/base/pallas_call | solution.py:190
  32.7 0.0 copy-start.16
  32.7 0.0 collective-permute-done.5.refs_1_.refs_6_
  32.7 0.1 collective-permute-start.2
  32.8 1.8 %collective-permute-done.4.refs_0_ = bf16[2,64,1152]{2,1,0:T(8,128)(2,1)S(1)} collective-permute-done((bf16[2,64,1152]{2,1,0:T(8,128)(2,1)S(1)}, bf16[2,64,1152]{2,1,0:T(8,128)(2,1)S(1)}, u32[]{:S(2)}, u32[]{:S(2)}) %collective-permute-start.4) | collective-permute-done | bytes 294944 | tf_op jit(solution)/shard_map/ppermute | solution.py:330
  34.6 0.7 %copy-done.6 = bf16[2,64,1152]{2,1,0:T(8,128)(2,1)} copy-done((bf16[2,64,1152]{2,1,0:T(8,128)(2,1)}, bf16[2,64,1152]{2,1,0:T(8,128)(2,1)S(1)}, u32[]{:S(2)}) %copy-start.6) | copy-done | bytes 294936
  35.3 2.3 %collective-permute-start.6 = (bf16[2,64,1152]{2,1,0:T(8,128)(2,1)}, bf16[2,64,1152]{2,1,0:T(8,128)(2,1)S(1)}, u32[]{:S(2)}, u32[]{:S(2)}) collective-permute-start(bf16[2,64,1152]{2,1,0:T(8,128)(2,1)} %hand.4.refs_5_), channel_id=1, source_target_pairs={{0,12},{4,0},{8,4},{12,8},{1,13},{5,1},{9,5},{13,9},{2,14},{6,2},{... | collective-permute-start | bytes 884744 | tf_op jit(solution)/shard_map/ppermute | solution.py:330
  37.6 6.5 %collective-permute-done.2.refs_2_ = bf16[2,64,1152]{2,1,0:T(8,128)(2,1)S(1)} collective-permute-done((bf16[2,64,1152]{2,1,0:T(8,128)(2,1)}, bf16[2,64,1152]{2,1,0:T(8,128)(2,1)S(1)}, u32[]{:S(2)}, u32[]{:S(2)}) %collective-permute-start.2) | collective-permute-done | bytes 294944 | tf_op jit(solution)/shard_map/ppermute | solution.py:330
  44.1 0.7 %copy-done.13 = bf16[2,64,1152]{2,1,0:T(8,128)(2,1)} copy-done((bf16[2,64,1152]{2,1,0:T(8,128)(2,1)}, bf16[2,64,1152]{2,1,0:T(8,128)(2,1)S(1)}, u32[]{:S(2)}) %copy-start.13) | copy-done | bytes 294936
  44.8 1.0 %copy-done.1 = bf16[2,64,1152]{2,1,0:T(8,128)(2,1)S(1)} copy-done((bf16[2,64,1152]{2,1,0:T(8,128)(2,1)S(1)}, bf16[2,64,1152]{2,1,0:T(8,128)(2,1)}, u32[]{:S(2)}) %copy-start.1) | copy-done | bytes 294936
  45.8 1.0 %copy-done.3 = bf16[2,64,1152]{2,1,0:T(8,128)(2,1)S(1)} copy-done((bf16[2,64,1152]{2,1,0:T(8,128)(2,1)S(1)}, bf16[2,64,1152]{2,1,0:T(8,128)(2,1)}, u32[]{:S(2)}) %copy-start.3) | copy-done | bytes 294936
  46.7 1.0 %copy-done.5 = bf16[2,64,1152]{2,1,0:T(8,128)(2,1)S(1)} copy-done((bf16[2,64,1152]{2,1,0:T(8,128)(2,1)S(1)}, bf16[2,64,1152]{2,1,0:T(8,128)(2,1)}, u32[]{:S(2)}) %copy-start.5) | copy-done | bytes 294936
  47.7 1.0 %copy-done.7 = bf16[2,64,1152]{2,1,0:T(8,128)(2,1)S(1)} copy-done((bf16[2,64,1152]{2,1,0:T(8,128)(2,1)S(1)}, bf16[2,64,1152]{2,1,0:T(8,128)(2,1)}, u32[]{:S(2)}) %copy-start.7) | copy-done | bytes 294936
  48.7 1.0 %copy-done.10 = bf16[2,64,1152]{2,1,0:T(8,128)(2,1)S(1)} copy-done((bf16[2,64,1152]{2,1,0:T(8,128)(2,1)S(1)}, bf16[2,64,1152]{2,1,0:T(8,128)(2,1)}, u32[]{:S(2)}) %copy-start.10) | copy-done | bytes 294936
  49.6 1.0 %copy-done.12 = bf16[2,64,1152]{2,1,0:T(8,128)(2,1)S(1)} copy-done((bf16[2,64,1152]{2,1,0:T(8,128)(2,1)S(1)}, bf16[2,64,1152]{2,1,0:T(8,128)(2,1)}, u32[]{:S(2)}) %copy-start.12) | copy-done | bytes 294936
  50.6 1.0 %copy-done.14 = bf16[2,64,1152]{2,1,0:T(8,128)(2,1)S(1)} copy-done((bf16[2,64,1152]{2,1,0:T(8,128)(2,1)S(1)}, bf16[2,64,1152]{2,1,0:T(8,128)(2,1)}, u32[]{:S(2)}) %copy-start.14) | copy-done | bytes 294936
  51.6 0.5 collect.1.held
  52.1 0.0 collective-permute-done.7.refs_1_
  52.1 0.0 collective-permute-done.8.refs_2_
  52.1 0.0 collective-permute-done.6.refs_0_
  52.1 2.2 %rank.2 = (bf16[3,128,128]{2,1,0:T(8,128)(2,1)S(1)}, bf16[3,128,128]{2,1,0:T(8,128)(2,1)S(1)}, bf16[3,128,128]{2,1,0:T(8,128)(2,1)S(1)}, f32[8,128]{1,0:T(8,128)S(1)}) custom-call(s32[16]{0:T(128)S(1)} %copy-done.16, bf16[14,64,1152]{2,1,0:T(8,128)(2,1)S(1)} %collect.1.held, bf16[2,64,1152]{2,1,0:T(8,128)(2,1)S(1)} %collective-permute-done.6.refs_0_, ...), custom_call_target="tpu_custom_call" | custom-call | tf_op jit(solution)/shard_map/rank/pallas_call | solution.py:274
  54.3 0.6 copy-done.15
  54.9 0.6 copy-done.17
  55.5 0.6 copy-done.18
  56.2 0.5 collective-permute-start.11
  56.7 1.5 %collective-permute-start.12 = (bf16[3,128,128]{2,1,0:T(8,128)(2,1)}, bf16[3,128,128]{2,1,0:T(8,128)(2,1)S(1)}, u32[]{:S(2)}, u32[]{:S(2)}) collective-permute-start(bf16[3,128,128]{2,1,0:T(8,128)(2,1)} %copy-done.17), channel_id=1, source_target_pairs={{0,16},{2,18},{16,0},{18,2},{1,17},{3,19},{17,1},{19,3},{4,20},{6,... | collective-permute-start | bytes 294920 | tf_op jit(solution)/shard_map/ppermute | solution.py:340
  58.2 1.5 %collective-permute-start.13 = (bf16[3,128,128]{2,1,0:T(8,128)(2,1)S(1)}, bf16[3,128,128]{2,1,0:T(8,128)(2,1)S(1)}, u32[]{:S(2)}, u32[]{:S(2)}) collective-permute-start(bf16[3,128,128]{2,1,0:T(8,128)(2,1)S(1)} %get-tuple-element.32), channel_id=1, source_target_pairs={{0,18},{2,16},{16,2},{18,0},{1,19},{3,17},{17,3},{19,1},{4,22},{6,... | collective-permute-start | bytes 294920 | tf_op jit(solution)/shard_map/ppermute | solution.py:340
  59.7 1.1 %copy-done.8 = bf16[400,1024]{1,0:T(8,128)(2,1)S(1)} copy-done((bf16[400,1024]{1,0:T(8,128)(2,1)S(1)}, bf16[400,1024]{1,0:T(8,128)(2,1)}, u32[]{:S(2)}) %copy-start.8) | copy-done | bytes 819224
  60.8 1.5 %rank.3 = (bf16[3,128,128]{2,1,0:T(8,128)(2,1)S(1)}, f32[8,128]{1,0:T(8,128)}) custom-call(s32[16]{0:T(128)S(1)} %copy-done.16, bf16[14,64,1152]{2,1,0:T(8,128)(2,1)S(1)} %collect.1.held, bf16[2,64,1152]{2,1,0:T(8,128)(2,1)S(1)} %collective-permute-done.6.refs_0_, bf16[400,1024]{1,0:T(8,128)(2,1)S(1)} %copy-done.8), custom_call_target="tpu_custom_call" | custom-call | tf_op jit(solution)/shard_map/rank/pallas_call | solution.py:274
  62.3 0.0 collective-permute-start.14
  62.3 0.5 collective-permute-start.15
  62.8 0.1 collective-permute-start.16
  62.9 2.0 %collective-permute-done.13.refs_3_ = bf16[3,128,128]{2,1,0:T(8,128)(2,1)S(1)} collective-permute-done((bf16[3,128,128]{2,1,0:T(8,128)(2,1)S(1)}, bf16[3,128,128]{2,1,0:T(8,128)(2,1)S(1)}, u32[]{:S(2)}, u32[]{:S(2)}) %collective-permute-start.13) | collective-permute-done | bytes 98336 | tf_op jit(solution)/shard_map/ppermute | solution.py:340
  64.9 1.3 %collective-permute-done.17.refs_7_ = bf16[3,128,128]{2,1,0:T(8,128)(2,1)S(1)} collective-permute-done((bf16[3,128,128]{2,1,0:T(8,128)(2,1)S(1)}, bf16[3,128,128]{2,1,0:T(8,128)(2,1)S(1)}, u32[]{:S(2)}, u32[]{:S(2)}) %collective-permute-start.17) | collective-permute-done | bytes 98336 | tf_op jit(solution)/shard_map/ppermute | solution.py:327
  66.2 1.0 %final.1 = bf16[384,512]{1,0:T(8,128)(2,1)} custom-call(f32[384,512]{1,0:T(8,128)S(1)} %copy-done.9, f32[384,512]{1,0:T(8,128)S(1)} %collective-permute-done.10.base_b, bf16[3,128,128]{2,1,0:T(8,128)(2,1)S(1)} %get-tuple-element.29.refs_0_, bf16[3,128,128]{2,1,0:T(8,128)(2,1)S(1)} %collective-permute-done.11.refs_1_, ...), custom_call_target="tpu_custom_call" | custom-call | tf_op jit(solution)/shard_map/final/pallas_call | solution.py:308
  (36 shorter events, 0.1 us)
Async XLA Ops:
  1.9 12.5 %collective-permute-start.3 = (bf16[2,64,1152]{2,1,0:T(8,128)(2,1)}, bf16[2,64,1152]{2,1,0:T(8,128)(2,1)S(1)}, u32[]{:S(2)}, u32[]{:S(2)}) collective-permute-start(bf16[2,64,1152]{2,1,0:T(8,128)(2,1)} %get-tuple-element.23), channel_id=1, source_target_pairs={{0,2},{2,0},{1,3},{3,1},{4,6},{6,4},{5,7},{7,5},{8,10},{10,8},{9,1... | collective-permute-start | bytes 884744 | tf_op jit(solution)/shard_map/ppermute | solution.py:357
  4.9 12.0 %collective-permute-start.1 = (bf16[2,64,1152]{2,1,0:T(8,128)(2,1)}, bf16[2,64,1152]{2,1,0:T(8,128)(2,1)S(1)}, u32[]{:S(2)}, u32[]{:S(2)}) collective-permute-start(bf16[2,64,1152]{2,1,0:T(8,128)(2,1)} %get-tuple-element.21.refs_0_), channel_id=1, source_target_pairs={{0,4},{4,8},{8,12},{12,0},{1,5},{5,9},{9,13},{13,1},{2,6},{6,10},{... | collective-permute-start | bytes 884744 | tf_op jit(solution)/shard_map/ppermute | solution.py:330
  6.5 15.5 %collective-permute-start = (bf16[2,64,1152]{2,1,0:T(8,128)(2,1)}, bf16[2,64,1152]{2,1,0:T(8,128)(2,1)S(1)}, u32[]{:S(2)}, u32[]{:S(2)}) collective-permute-start(bf16[2,64,1152]{2,1,0:T(8,128)(2,1)} %get-tuple-element.21.refs_0_), channel_id=1, source_target_pairs={{0,12},{4,0},{8,4},{12,8},{1,13},{5,1},{9,5},{13,9},{2,14},{6,2},{... | collective-permute-start | bytes 884744 | tf_op jit(solution)/shard_map/ppermute | solution.py:330
  12.4 39.7 %collective-permute-start.7 = (bf16[400,1024]{1,0:T(8,128)(2,1)}, bf16[400,1024]{1,0:T(8,128)(2,1)S(1)}, u32[]{:S(2)}, u32[]{:S(2)}) collective-permute-start(bf16[400,1024]{1,0:T(8,128)(2,1)} %get-tuple-element.24), channel_id=1, source_target_pairs={{0,2},{2,0},{16,18},{18,16},{1,3},{3,1},{17,19},{19,17},{4,6},{6,4... | collective-permute-start | bytes 2457608 | tf_op jit(solution)/shard_map/ppermute | solution.py:340
  12.7 39.3 %collective-permute-start.8 = (bf16[400,1024]{1,0:T(8,128)(2,1)}, bf16[400,1024]{1,0:T(8,128)(2,1)S(1)}, u32[]{:S(2)}, u32[]{:S(2)}) collective-permute-start(bf16[400,1024]{1,0:T(8,128)(2,1)} %get-tuple-element.25), channel_id=1, source_target_pairs={{0,16},{2,18},{16,0},{18,2},{1,17},{3,19},{17,1},{19,3},{4,20},{6,... | collective-permute-start | bytes 2457608 | tf_op jit(solution)/shard_map/ppermute | solution.py:340
  14.4 18.2 %copy-start.11 = (bf16[2,64,1152]{2,1,0:T(8,128)(2,1)}, bf16[2,64,1152]{2,1,0:T(8,128)(2,1)S(1)}, u32[]{:S(2)}) copy-start(bf16[2,64,1152]{2,1,0:T(8,128)(2,1)S(1)} %collective-permute-done.3.refs_4_) | copy-start | bytes 884740
  14.4 37.6 %collective-permute-start.9 = (bf16[400,1024]{1,0:T(8,128)(2,1)}, bf16[400,1024]{1,0:T(8,128)(2,1)}, u32[]{:S(2)}, u32[]{:S(2)}) collective-permute-start(bf16[400,1024]{1,0:T(8,128)(2,1)} %get-tuple-element.26), channel_id=1, source_target_pairs={{0,18},{2,16},{16,2},{18,0},{1,19},{3,17},{17,3},{19,1},{4,22},{6,... | collective-permute-start | bytes 2457608 | tf_op jit(solution)/shard_map/ppermute | solution.py:340
  16.9 15.8 %copy-start.2 = (bf16[2,64,1152]{2,1,0:T(8,128)(2,1)}, bf16[2,64,1152]{2,1,0:T(8,128)(2,1)S(1)}, u32[]{:S(2)}) copy-start(bf16[2,64,1152]{2,1,0:T(8,128)(2,1)S(1)} %collective-permute-done.1.refs_0_) | copy-start | bytes 884740
  16.9 15.8 %collective-permute-start.5 = (bf16[2,64,1152]{2,1,0:T(8,128)(2,1)S(1)}, bf16[2,64,1152]{2,1,0:T(8,128)(2,1)S(1)}, u32[]{:S(2)}, u32[]{:S(2)}) collective-permute-start(bf16[2,64,1152]{2,1,0:T(8,128)(2,1)S(1)} %collective-permute-done.3.refs_4_), channel_id=1, source_target_pairs={{0,4},{4,8},{8,12},{12,0},{1,5},{5,9},{9,13},{13,1},{2,6},{6,10},{... | collective-permute-start | bytes 884744 | tf_op jit(solution)/shard_map/ppermute | solution.py:330
  22.0 10.7 %copy-start = (bf16[2,64,1152]{2,1,0:T(8,128)(2,1)}, bf16[2,64,1152]{2,1,0:T(8,128)(2,1)S(1)}, u32[]{:S(2)}) copy-start(bf16[2,64,1152]{2,1,0:T(8,128)(2,1)S(1)} %collective-permute-done.refs_1_) | copy-start | bytes 884740
  22.0 12.6 %collective-permute-start.4 = (bf16[2,64,1152]{2,1,0:T(8,128)(2,1)S(1)}, bf16[2,64,1152]{2,1,0:T(8,128)(2,1)S(1)}, u32[]{:S(2)}, u32[]{:S(2)}) collective-permute-start(bf16[2,64,1152]{2,1,0:T(8,128)(2,1)S(1)} %collective-permute-done.3.refs_4_), channel_id=1, source_target_pairs={{0,12},{4,0},{8,4},{12,8},{1,13},{5,1},{9,5},{13,9},{2,14},{6,2},{... | collective-permute-start | bytes 884744 | tf_op jit(solution)/shard_map/ppermute | solution.py:330
  32.7 19.4 %copy-start.16 = (s32[16]{0:T(128)S(1)}, s32[16]{0:T(128)}, u32[]{:S(2)}) copy-start(s32[16]{0:T(128)} %owner.3) | copy-start | bytes 196
  32.7 1.9 %copy-start.4 = (bf16[2,64,1152]{2,1,0:T(8,128)(2,1)}, bf16[2,64,1152]{2,1,0:T(8,128)(2,1)S(1)}, u32[]{:S(2)}) copy-start(bf16[2,64,1152]{2,1,0:T(8,128)(2,1)S(1)} %collective-permute-done.5.refs_1_.refs_6_) | copy-start | bytes 884740
  32.7 11.4 %collective-permute-start.2 = (bf16[2,64,1152]{2,1,0:T(8,128)(2,1)}, bf16[2,64,1152]{2,1,0:T(8,128)(2,1)S(1)}, u32[]{:S(2)}, u32[]{:S(2)}) collective-permute-start(bf16[2,64,1152]{2,1,0:T(8,128)(2,1)} %hand.3.refs_3_), channel_id=1, source_target_pairs={{0,4},{4,8},{8,12},{12,0},{1,5},{5,9},{9,13},{13,1},{2,6},{6,10},{... | collective-permute-start | bytes 884744 | tf_op jit(solution)/shard_map/ppermute | solution.py:330
  34.6 0.7 %copy-start.6 = (bf16[2,64,1152]{2,1,0:T(8,128)(2,1)}, bf16[2,64,1152]{2,1,0:T(8,128)(2,1)S(1)}, u32[]{:S(2)}) copy-start(bf16[2,64,1152]{2,1,0:T(8,128)(2,1)S(1)} %collective-permute-done.4.refs_0_) | copy-start | bytes 884740
  35.3 16.8 %collective-permute-start.6 = (bf16[2,64,1152]{2,1,0:T(8,128)(2,1)}, bf16[2,64,1152]{2,1,0:T(8,128)(2,1)S(1)}, u32[]{:S(2)}, u32[]{:S(2)}) collective-permute-start(bf16[2,64,1152]{2,1,0:T(8,128)(2,1)} %hand.4.refs_5_), channel_id=1, source_target_pairs={{0,12},{4,0},{8,4},{12,8},{1,13},{5,1},{9,5},{13,9},{2,14},{6,2},{... | collective-permute-start | bytes 884744 | tf_op jit(solution)/shard_map/ppermute | solution.py:330
  44.1 0.7 %copy-start.13 = (bf16[2,64,1152]{2,1,0:T(8,128)(2,1)}, bf16[2,64,1152]{2,1,0:T(8,128)(2,1)S(1)}, u32[]{:S(2)}) copy-start(bf16[2,64,1152]{2,1,0:T(8,128)(2,1)S(1)} %collective-permute-done.2.refs_2_) | copy-start | bytes 884740
  44.8 1.0 %copy-start.1 = (bf16[2,64,1152]{2,1,0:T(8,128)(2,1)S(1)}, bf16[2,64,1152]{2,1,0:T(8,128)(2,1)}, u32[]{:S(2)}) copy-start(bf16[2,64,1152]{2,1,0:T(8,128)(2,1)} %copy-done) | copy-start | bytes 884740
  45.8 1.0 %copy-start.3 = (bf16[2,64,1152]{2,1,0:T(8,128)(2,1)S(1)}, bf16[2,64,1152]{2,1,0:T(8,128)(2,1)}, u32[]{:S(2)}) copy-start(bf16[2,64,1152]{2,1,0:T(8,128)(2,1)} %hand.3.refs_3_) | copy-start | bytes 884740
  46.7 1.0 %copy-start.5 = (bf16[2,64,1152]{2,1,0:T(8,128)(2,1)S(1)}, bf16[2,64,1152]{2,1,0:T(8,128)(2,1)}, u32[]{:S(2)}) copy-start(bf16[2,64,1152]{2,1,0:T(8,128)(2,1)} %copy-done.4) | copy-start | bytes 884740
  47.7 1.0 %copy-start.7 = (bf16[2,64,1152]{2,1,0:T(8,128)(2,1)S(1)}, bf16[2,64,1152]{2,1,0:T(8,128)(2,1)}, u32[]{:S(2)}) copy-start(bf16[2,64,1152]{2,1,0:T(8,128)(2,1)} %hand.4.refs_5_) | copy-start | bytes 884740
  48.7 1.0 %copy-start.10 = (bf16[2,64,1152]{2,1,0:T(8,128)(2,1)S(1)}, bf16[2,64,1152]{2,1,0:T(8,128)(2,1)}, u32[]{:S(2)}) copy-start(bf16[2,64,1152]{2,1,0:T(8,128)(2,1)} %get-tuple-element.21.refs_0_) | copy-start | bytes 884740
  49.6 1.0 %copy-start.12 = (bf16[2,64,1152]{2,1,0:T(8,128)(2,1)S(1)}, bf16[2,64,1152]{2,1,0:T(8,128)(2,1)}, u32[]{:S(2)}) copy-start(bf16[2,64,1152]{2,1,0:T(8,128)(2,1)} %copy-done.11) | copy-start | bytes 884740
  50.6 1.0 %copy-start.14 = (bf16[2,64,1152]{2,1,0:T(8,128)(2,1)S(1)}, bf16[2,64,1152]{2,1,0:T(8,128)(2,1)}, u32[]{:S(2)}) copy-start(bf16[2,64,1152]{2,1,0:T(8,128)(2,1)} %copy-done.13) | copy-start | bytes 884740
  54.3 0.6 copy-start.15
  54.9 0.6 copy-start.17
  55.5 0.6 copy-start.18
  56.2 10.0 %copy-start.9 = (f32[384,512]{1,0:T(8,128)S(1)}, f32[384,512]{1,0:T(8,128)}, u32[]{:S(2)}) copy-start(f32[384,512]{1,0:T(8,128)} %get-tuple-element.19.base_a) | copy-start | bytes 2359300
  56.2 10.0 %collective-permute-start.10 = (f32[384,512]{1,0:T(8,128)}, f32[384,512]{1,0:T(8,128)S(1)}, u32[]{:S(2)}, u32[]{:S(2)}) collective-permute-start(f32[384,512]{1,0:T(8,128)} %hand.5), channel_id=1, source_target_pairs={{0,1},{1,0},{2,3},{3,2},{4,5},{5,4},{6,7},{7,6},{8,9},{9,8},{10,11... | collective-permute-start | bytes 2359304 | tf_op jit(solution)/shard_map/ppermute | solution.py:327
  56.2 6.1 %collective-permute-start.11 = (bf16[3,128,128]{2,1,0:T(8,128)(2,1)}, bf16[3,128,128]{2,1,0:T(8,128)(2,1)S(1)}, u32[]{:S(2)}, u32[]{:S(2)}) collective-permute-start(bf16[3,128,128]{2,1,0:T(8,128)(2,1)} %copy-done.18), channel_id=1, source_target_pairs={{0,2},{2,0},{16,18},{18,16},{1,3},{3,1},{17,19},{19,17},{4,6},{6,4... | collective-permute-start | bytes 294920 | tf_op jit(solution)/shard_map/ppermute | solution.py:340
  56.7 6.1 %collective-permute-start.12 = (bf16[3,128,128]{2,1,0:T(8,128)(2,1)}, bf16[3,128,128]{2,1,0:T(8,128)(2,1)S(1)}, u32[]{:S(2)}, u32[]{:S(2)}) collective-permute-start(bf16[3,128,128]{2,1,0:T(8,128)(2,1)} %copy-done.17), channel_id=1, source_target_pairs={{0,16},{2,18},{16,0},{18,2},{1,17},{3,19},{17,1},{19,3},{4,20},{6,... | collective-permute-start | bytes 294920 | tf_op jit(solution)/shard_map/ppermute | solution.py:340
  58.2 6.7 %collective-permute-start.13 = (bf16[3,128,128]{2,1,0:T(8,128)(2,1)S(1)}, bf16[3,128,128]{2,1,0:T(8,128)(2,1)S(1)}, u32[]{:S(2)}, u32[]{:S(2)}) collective-permute-start(bf16[3,128,128]{2,1,0:T(8,128)(2,1)S(1)} %get-tuple-element.32), channel_id=1, source_target_pairs={{0,18},{2,16},{16,2},{18,0},{1,19},{3,17},{17,3},{19,1},{4,22},{6,... | collective-permute-start | bytes 294920 | tf_op jit(solution)/shard_map/ppermute | solution.py:340
  59.7 1.1 %copy-start.8 = (bf16[400,1024]{1,0:T(8,128)(2,1)S(1)}, bf16[400,1024]{1,0:T(8,128)(2,1)}, u32[]{:S(2)}) copy-start(bf16[400,1024]{1,0:T(8,128)(2,1)} %get-tuple-element.28.refs_1_) | copy-start | bytes 2457604
  62.3 2.6 %collective-permute-start.14 = (bf16[3,128,128]{2,1,0:T(8,128)(2,1)S(1)}, bf16[3,128,128]{2,1,0:T(8,128)(2,1)S(1)}, u32[]{:S(2)}, u32[]{:S(2)}) collective-permute-start(bf16[3,128,128]{2,1,0:T(8,128)(2,1)S(1)} %get-tuple-element.29.refs_0_), channel_id=1, source_target_pairs={{0,1},{1,0},{2,3},{3,2},{4,5},{5,4},{6,7},{7,6},{8,9},{9,8},{10,11... | collective-permute-start | bytes 294920 | tf_op jit(solution)/shard_map/ppermute | solution.py:327
  62.3 2.6 %collective-permute-start.15 = (bf16[3,128,128]{2,1,0:T(8,128)(2,1)S(1)}, bf16[3,128,128]{2,1,0:T(8,128)(2,1)S(1)}, u32[]{:S(2)}, u32[]{:S(2)}) collective-permute-start(bf16[3,128,128]{2,1,0:T(8,128)(2,1)S(1)} %collective-permute-done.11.refs_1_), channel_id=1, source_target_pairs={{0,1},{1,0},{2,3},{3,2},{4,5},{5,4},{6,7},{7,6},{8,9},{9,8},{10,11... | collective-permute-start | bytes 294920 | tf_op jit(solution)/shard_map/ppermute | solution.py:327
  62.8 2.1 %collective-permute-start.16 = (bf16[3,128,128]{2,1,0:T(8,128)(2,1)S(1)}, bf16[3,128,128]{2,1,0:T(8,128)(2,1)S(1)}, u32[]{:S(2)}, u32[]{:S(2)}) collective-permute-start(bf16[3,128,128]{2,1,0:T(8,128)(2,1)S(1)} %collective-permute-done.12.refs_2_), channel_id=1, source_target_pairs={{0,1},{1,0},{2,3},{3,2},{4,5},{5,4},{6,7},{7,6},{8,9},{9,8},{10,11... | collective-permute-start | bytes 294920 | tf_op jit(solution)/shard_map/ppermute | solution.py:327
  64.9 1.3 %collective-permute-start.17 = (bf16[3,128,128]{2,1,0:T(8,128)(2,1)S(1)}, bf16[3,128,128]{2,1,0:T(8,128)(2,1)S(1)}, u32[]{:S(2)}, u32[]{:S(2)}) collective-permute-start(bf16[3,128,128]{2,1,0:T(8,128)(2,1)S(1)} %collective-permute-done.13.refs_3_), channel_id=1, source_target_pairs={{0,1},{1,0},{2,3},{3,2},{4,5},{5,4},{6,7},{7,6},{8,9},{9,8},{10,11... | collective-permute-start | bytes 294920 | tf_op jit(solution)/shard_map/ppermute | solution.py:327

commit v28 on v26

--- a/solution.py
+++ b/solution.py
@@ -230,9 +230,8 @@
     )(*pieces)
 
 
-def rank_kernel(ring, pair, rows, shares, owner, held, *refs):
-    late, toks, outs = refs[: -1 - 2 * shares], refs[-1 - 2 * shares : -1 - shares], refs[-1 - shares : -1]
-    flag = refs[-1]
+def rank_kernel(ring, pair, rows, count, lates, owner, held, *refs):
+    late, toks, outs, flag = refs[:lates], refs[lates : lates + count], refs[-1 - count : -1], refs[-1]
     flag[...] = jnp.zeros_like(flag)
     rank = held.shape[1]
     per = owner.shape[0] // (ring * pair)
@@ -270,18 +269,18 @@
         outs[k][b, rank:, :] = piece[:, feats:]
 
 
-def rank_parts(owner, toks, held, late, ring, pair, rows, blocks):
-    shares, rank = len(toks), held.shape[1]
-    return pl.pallas_call(
-        functools.partial(rank_kernel, ring, pair, rows, shares),
-        in_specs=[SMEM, VMEM] + [VMEM] * (len(late) + shares),
-        out_specs=[VMEM] * (shares + 1),
-        out_shape=[jax.ShapeDtypeStruct((blocks, 2 * rank, rows // blocks), held.dtype)] * shares
+def rank_parts(owner, toks, held, late, ring, pair, rows, blocks, after=()):
+    count, rank = len(toks), held.shape[1]
+    return pl.pallas_call(
+        functools.partial(rank_kernel, ring, pair, rows, count, len(late)),
+        in_specs=[SMEM, VMEM] + [VMEM] * (len(late) + count) + [ANY] * len(after),
+        out_specs=[VMEM] * (count + 1),
+        out_shape=[jax.ShapeDtypeStruct((blocks, 2 * rank, rows // blocks), held.dtype)] * count
         + [jax.ShapeDtypeStruct((8, LANES), jnp.float32)],
         cost_estimate=pl.CostEstimate(flops=0, bytes_accessed=0, transcendentals=0),
         compiler_params=ROOM,
         name="rank",
-    )(owner, held, *late, *toks)
+    )(owner, held, *late, *toks, *after)
 
 
 def final_kernel(groups, pair, base_a, base_b, *refs):
@@ -358,7 +357,9 @@
         lax.ppermute(packed[pair - w], "pair", [(a, (a - w) % pair) for a in range(pair)]) for w in range(1, pair)
     ]
     firsts = [first_hops(piece) for piece in [packed[0]] + swapped]
-    toks = [slabs[0]] + [in_plane(slabs[k], k // pair, k % pair) for k in range(1, shares)]
+    toks = [slabs[0]] * shares
+    for k in reversed(range(1, shares)):
+        toks[k] = in_plane(slabs[k], k // pair, k % pair)
 
     base_mine, base_out, flag = base_halves(tokens, base_key, sides, lengths)
     pieces = [
@@ -369,8 +370,13 @@
     halfway = ring // 2 if ring % 2 == 0 else ring
     held = collect([piece for way in pieces for away, piece in enumerate(way) if away != halfway])
     late = [way[halfway] for way in pieces] if halfway < ring else []
-    *parts, ready = rank_parts(owner_slot, toks, held, late, ring, pair, rows, blocks)
-    mine = [parts[0]] + [in_plane(parts[k], -(k // pair), -(k % pair)) for k in range(1, shares)]
+    first = [0] + list(reversed(range(2, shares)))
+    *parts, ready = rank_parts(owner_slot, [toks[k] for k in first], held, late, ring, pair, rows, blocks)
+    mine = [parts[0]] * shares
+    for k, part in zip(first[1:], parts[1:]):
+        mine[k] = in_plane(part, -(k // pair), -(k % pair))
+    last = rank_parts(owner_slot, toks[1:2], held, late, ring, pair, rows, blocks, mine[2:])[0]
+    mine[1] = in_plane(last, 0, -1)
     theirs = [across(part) for part in mine]
     base_in = across(hand_on(base_out, ready))
     return final(mine, theirs, [base_mine, base_in], groups, pair, tokens.dtype)

time: 65.9 us -> 79.8 us (1.21)
  starting transfers between devices: 19.9 us -> 38.4 us
  waiting for transfers between devices: 20.7 us -> 11.8 us
  local copies, waits for them, and re-layouts: 6.84 us -> 9.8 us
  Pallas kernels: 18 us -> 19.2 us
    ppermute x6, starting transfers between devices: 9.51 us -> 25 us  [along(): lax.ppermute(x, 'ring', [(a, (a + step) % ring) for a in range(ring)])]
    ppermute x6, waiting for transfers between devices: 8.79 us -> 1.47 us  [along(): lax.ppermute(x, 'ring', [(a, (a + step) % ring) for a in range(ring)])]
    unnamed x30 -> x36, local copies, waits for them, and re-layouts: 6.84 us -> 9.8 us
    ppermute x6, starting transfers between devices: 7.04 us -> 9.84 us  [in_plane(): return lax.ppermute(x, PLANE, pairs)]
    pallas_call x1 -> x2, Pallas kernels: 2.38 us -> 4.35 us  [rank_parts(): pl.pallas_call(functools.partial(rank_kernel, ring, pair, rows, count, le...]
    ppermute x6, waiting for transfers between devices: 10.6 us -> 9 us  [in_plane(): return lax.ppermute(x, PLANE, pairs)]
  transfers between devices with their start and end apart: 18 -> 18, of which waited for: 9 -> 5; matrix products, arithmetic and copies ran while one was open for 0% -> 0% of each run, Pallas kernels for 19% -> 20%
where the time goes in v28:
time: 79.8 us; the launch traced here: 79.3 us
  starting transfers between devices  38.4 us (48%)
  Pallas kernels  19.2 us (24%)
  waiting for transfers between devices  11.8 us (15%)
  local copies, waits for them, and re-layouts  9.8 us (12%)
    ppermute x6, starting transfers between devices, along(): lax.ppermute(x, 'ring', [(a, (a + step) % ring) for a in range(ring)])  25 us
    ppermute x6, starting transfers between devices, in_plane(): return lax.ppermute(x, PLANE, pairs)  9.84 us
    unnamed x36, local copies, waits for them, and re-layouts  9.8 us
    ppermute x6, waiting for transfers between devices, in_plane(): return lax.ppermute(x, PLANE, pairs)  9 us
    pallas_call x1, Pallas kernels, base_halves(): pl.pallas_call(functools.partial(base_kernel, sides), in_specs=[SMEM, ANY...  7.86 us
    pallas_call x2, Pallas kernels, rank_parts(): pl.pallas_call(functools.partial(rank_kernel, ring, pair, rows, count, le...  4.35 us
    pallas_call x1, Pallas kernels, spread(): pl.pallas_call(functools.partial(spread_kernel, groups, pair), in_specs=[...  3.58 us
    ppermute x1, starting transfers between devices, body(): lax.ppermute(packed[pair - w], 'pair', [(a, (a - w) % pair) for a in rang...  3.03 us
  transfers between devices with their start and end apart: 18, of which 5 were waited for; matrix products, arithmetic and copies ran while one was open for 0% of the time, Pallas kernels for 20%

profile of v28, /device:TPU:0, one launch (start us, length us, event | category | flops | bytes accessed | tf_op | source)
XLA Modules:
  0.0 79.3 jit_solution(17847658380322991460)
XLA Ops:
  0.0 1.9 %pack.1 = (bf16[2,64,1152]{2,1,0:T(8,128)(2,1)}, bf16[2,64,1152]{2,1,0:T(8,128)(2,1)}) custom-call(bf16[2,64,4096]{2,1,0:T(8,128)(2,1)} %bitcast.2, bf16[2,64,512]{2,1,0:T(8,128)(2,1)} %up.1), custom_call_target="tpu_custom_call" | custom-call | tf_op jit(solution)/shard_map/pack/pallas_call | solution.py:57
  1.9 0.0 copy-start.10
  1.9 3.0 %collective-permute-start.2 = (bf16[2,64,1152]{2,1,0:T(8,128)(2,1)}, bf16[2,64,1152]{2,1,0:T(8,128)(2,1)S(1)}, u32[]{:S(2)}, u32[]{:S(2)}) collective-permute-start(bf16[2,64,1152]{2,1,0:T(8,128)(2,1)} %get-tuple-element.23), channel_id=1, source_target_pairs={{0,2},{2,0},{1,3},{3,1},{4,6},{6,4},{5,7},{7,5},{8,10},{10,8},{9,1... | collective-permute-start | bytes 884744 | tf_op jit(solution)/shard_map/ppermute | solution.py:357
  5.0 1.6 %collective-permute-start.1 = (bf16[2,64,1152]{2,1,0:T(8,128)(2,1)}, bf16[2,64,1152]{2,1,0:T(8,128)(2,1)S(1)}, u32[]{:S(2)}, u32[]{:S(2)}) collective-permute-start(bf16[2,64,1152]{2,1,0:T(8,128)(2,1)} %get-tuple-element.21.refs_0_), channel_id=1, source_target_pairs={{0,4},{4,8},{8,12},{12,0},{1,5},{5,9},{9,13},{13,1},{2,6},{6,10},{... | collective-permute-start | bytes 884744 | tf_op jit(solution)/shard_map/ppermute | solution.py:330
  6.5 3.6 %spread.1 = (bf16[400,1024]{1,0:T(8,128)(2,1)}, bf16[400,1024]{1,0:T(8,128)(2,1)}, bf16[400,1024]{1,0:T(8,128)(2,1)}, bf16[400,1024]{1,0:T(8,128)(2,1)}) custom-call(s32[3]{0:T(128)} %lengths.3, s32[3]{0:T(128)} %bitcast.3, bf16[384,4096]{1,0:T(8,128)(2,1)} %tok.3), custom_call_target="tpu_custom_call" | custom-call | tf_op jit(solution)/shard_map/spread/pallas_call | solution.py:126
  10.1 1.5 %collective-permute-start.7 = (bf16[400,1024]{1,0:T(8,128)(2,1)}, bf16[400,1024]{1,0:T(8,128)(2,1)S(1)}, u32[]{:S(2)}, u32[]{:S(2)}) collective-permute-start(bf16[400,1024]{1,0:T(8,128)(2,1)} %get-tuple-element.25), channel_id=1, source_target_pairs={{0,18},{2,16},{16,2},{18,0},{1,19},{3,17},{17,3},{19,1},{4,22},{6,... | collective-permute-start | bytes 2457608 | tf_op jit(solution)/shard_map/ppermute | solution.py:340
  11.6 0.5 collective-permute-start.8
  12.2 2.0 %collective-permute-start = (bf16[2,64,1152]{2,1,0:T(8,128)(2,1)S(1)}, bf16[2,64,1152]{2,1,0:T(8,128)(2,1)S(1)}, u32[]{:S(2)}, u32[]{:S(2)}) collective-permute-start(bf16[2,64,1152]{2,1,0:T(8,128)(2,1)S(1)} %copy-done.10), channel_id=1, source_target_pairs={{0,12},{4,0},{8,4},{12,8},{1,13},{5,1},{9,5},{13,9},{2,14},{6,2},{... | collective-permute-start | bytes 884744 | tf_op jit(solution)/shard_map/ppermute | solution.py:330
  14.2 0.0 collective-permute-done.2.refs_3_
  14.2 0.0 collective-permute-start.4
  14.2 1.5 %collective-permute-done.1.refs_0_ = bf16[2,64,1152]{2,1,0:T(8,128)(2,1)S(1)} collective-permute-done((bf16[2,64,1152]{2,1,0:T(8,128)(2,1)}, bf16[2,64,1152]{2,1,0:T(8,128)(2,1)S(1)}, u32[]{:S(2)}, u32[]{:S(2)}) %collective-permute-start.1) | collective-permute-done | bytes 294944 | tf_op jit(solution)/shard_map/ppermute | solution.py:330
  15.7 17.0 %collective-permute-start.3 = (bf16[2,64,1152]{2,1,0:T(8,128)(2,1)S(1)}, bf16[2,64,1152]{2,1,0:T(8,128)(2,1)S(1)}, u32[]{:S(2)}, u32[]{:S(2)}) collective-permute-start(bf16[2,64,1152]{2,1,0:T(8,128)(2,1)S(1)} %collective-permute-done.2.refs_3_), channel_id=1, source_target_pairs={{0,12},{4,0},{8,4},{12,8},{1,13},{5,1},{9,5},{13,9},{2,14},{6,2},{... | collective-permute-start | bytes 884744 | tf_op jit(solution)/shard_map/ppermute | solution.py:330
  32.7 7.9 %base.1 = (f32[384,512]{1,0:T(8,128)}, f32[384,512]{1,0:T(8,128)}, f32[8,128]{1,0:T(8,128)}) custom-call(s32[3]{0:T(128)} %lengths.3, bf16[384,4096]{1,0:T(8,128)(2,1)} %tok.3, bf16[4096,1024]{1,0:T(8,128)(2,1)} %key.1), custom_call_target="tpu_custom_call" | custom-call | tf_op jit(solution)/shard_map/base/pallas_call | solution.py:190
  40.6 0.0 copy-start.15
  40.6 0.0 collective-permute-done.refs_1_
  40.6 0.7 copy-done
  41.3 0.0 collective-permute-start.5
  41.3 0.0 collective-permute-done.4.refs_1_.refs_5_
  41.3 0.0 collective-permute-done.3.refs_0_
  41.3 0.7 copy-done.2
  42.1 0.7 copy-done.6
  42.8 4.3 %collective-permute-start.6 = (bf16[2,64,1152]{2,1,0:T(8,128)(2,1)}, bf16[2,64,1152]{2,1,0:T(8,128)(2,1)S(1)}, u32[]{:S(2)}, u32[]{:S(2)}) collective-permute-start(bf16[2,64,1152]{2,1,0:T(8,128)(2,1)} %hand.4.refs_4_), channel_id=1, source_target_pairs={{0,12},{4,0},{8,4},{12,8},{1,13},{5,1},{9,5},{13,9},{2,14},{6,2},{... | collective-permute-start | bytes 884744 | tf_op jit(solution)/shard_map/ppermute | solution.py:330
  47.1 4.2 %collective-permute-start.10 = (bf16[400,1024]{1,0:T(8,128)(2,1)}, bf16[400,1024]{1,0:T(8,128)(2,1)}, u32[]{:S(2)}, u32[]{:S(2)}) collective-permute-start(bf16[400,1024]{1,0:T(8,128)(2,1)} %get-tuple-element.29), channel_id=1, source_target_pairs={{0,2},{2,0},{16,18},{18,16},{1,3},{3,1},{17,19},{19,17},{4,6},{6,4... | collective-permute-start | bytes 2457608 | tf_op jit(solution)/shard_map/ppermute | solution.py:340
  51.3 1.0 %copy-done.1 = bf16[2,64,1152]{2,1,0:T(8,128)(2,1)S(1)} copy-done((bf16[2,64,1152]{2,1,0:T(8,128)(2,1)S(1)}, bf16[2,64,1152]{2,1,0:T(8,128)(2,1)}, u32[]{:S(2)}) %copy-start.1) | copy-done | bytes 294936
  52.3 1.0 %copy-done.3 = bf16[2,64,1152]{2,1,0:T(8,128)(2,1)S(1)} copy-done((bf16[2,64,1152]{2,1,0:T(8,128)(2,1)S(1)}, bf16[2,64,1152]{2,1,0:T(8,128)(2,1)}, u32[]{:S(2)}) %copy-start.3) | copy-done | bytes 294936
  53.2 1.0 %copy-done.5 = bf16[2,64,1152]{2,1,0:T(8,128)(2,1)S(1)} copy-done((bf16[2,64,1152]{2,1,0:T(8,128)(2,1)S(1)}, bf16[2,64,1152]{2,1,0:T(8,128)(2,1)}, u32[]{:S(2)}) %copy-start.5) | copy-done | bytes 294936
  54.2 1.0 %copy-done.7 = bf16[2,64,1152]{2,1,0:T(8,128)(2,1)S(1)} copy-done((bf16[2,64,1152]{2,1,0:T(8,128)(2,1)S(1)}, bf16[2,64,1152]{2,1,0:T(8,128)(2,1)}, u32[]{:S(2)}) %copy-start.7) | copy-done | bytes 294936
  55.1 1.0 %copy-done.11 = bf16[2,64,1152]{2,1,0:T(8,128)(2,1)S(1)} copy-done((bf16[2,64,1152]{2,1,0:T(8,128)(2,1)S(1)}, bf16[2,64,1152]{2,1,0:T(8,128)(2,1)}, u32[]{:S(2)}) %copy-start.11) | copy-done | bytes 294936
  56.1 1.0 %copy-done.13 = bf16[2,64,1152]{2,1,0:T(8,128)(2,1)S(1)} copy-done((bf16[2,64,1152]{2,1,0:T(8,128)(2,1)S(1)}, bf16[2,64,1152]{2,1,0:T(8,128)(2,1)}, u32[]{:S(2)}) %copy-start.13) | copy-done | bytes 294936
  57.1 0.4 collect.1.held
  57.5 0.0 collective-permute-done.5.refs_0_
  57.5 0.0 collective-permute-done.6.refs_1_
  57.6 2.2 %rank.2 = (bf16[3,128,128]{2,1,0:T(8,128)(2,1)S(1)}, bf16[3,128,128]{2,1,0:T(8,128)(2,1)S(1)}, bf16[3,128,128]{2,1,0:T(8,128)(2,1)S(1)}, f32[8,128]{1,0:T(8,128)S(1)}) custom-call(s32[16]{0:T(128)S(1)} %copy-done.15, bf16[12,64,1152]{2,1,0:T(8,128)(2,1)S(1)} %collect.1.held, bf16[2,64,1152]{2,1,0:T(8,128)(2,1)S(1)} %collective-permute-done.5.refs_0_, ...), custom_call_target="tpu_custom_call" | custom-call | tf_op jit(solution)/shard_map/rank/pallas_call | solution.py:274
  59.8 0.6 copy-done.14
  60.4 0.6 copy-done.16
  61.0 0.6 copy-done.17
  61.7 1.0 %collective-permute-start.11 = (bf16[3,128,128]{2,1,0:T(8,128)(2,1)}, bf16[3,128,128]{2,1,0:T(8,128)(2,1)S(1)}, u32[]{:S(2)}, u32[]{:S(2)}) collective-permute-start(bf16[3,128,128]{2,1,0:T(8,128)(2,1)} %copy-done.17), channel_id=1, source_target_pairs={{0,16},{2,18},{16,0},{18,2},{1,17},{3,19},{17,1},{19,3},{4,20},{6,... | collective-permute-start | bytes 294920 | tf_op jit(solution)/shard_map/ppermute | solution.py:340
  62.6 2.2 %collective-permute-start.12 = (bf16[3,128,128]{2,1,0:T(8,128)(2,1)}, bf16[3,128,128]{2,1,0:T(8,128)(2,1)S(1)}, u32[]{:S(2)}, u32[]{:S(2)}) collective-permute-start(bf16[3,128,128]{2,1,0:T(8,128)(2,1)} %copy-done.16), channel_id=1, source_target_pairs={{0,18},{2,16},{16,2},{18,0},{1,19},{3,17},{17,3},{19,1},{4,22},{6,... | collective-permute-start | bytes 294920 | tf_op jit(solution)/shard_map/ppermute | solution.py:340
  64.9 2.2 %collective-permute-done.11.refs_3_.refs_2_ = bf16[3,128,128]{2,1,0:T(8,128)(2,1)S(1)} collective-permute-done((bf16[3,128,128]{2,1,0:T(8,128)(2,1)}, bf16[3,128,128]{2,1,0:T(8,128)(2,1)S(1)}, u32[]{:S(2)}, u32[]{:S(2)}) %collective-permute-start.11) | collective-permute-done | bytes 98336 | tf_op jit(solution)/shard_map/ppermute | solution.py:340
  67.1 3.1 %collective-permute-done.12.refs_4_.refs_3_ = bf16[3,128,128]{2,1,0:T(8,128)(2,1)S(1)} collective-permute-done((bf16[3,128,128]{2,1,0:T(8,128)(2,1)}, bf16[3,128,128]{2,1,0:T(8,128)(2,1)S(1)}, u32[]{:S(2)}, u32[]{:S(2)}) %collective-permute-start.12) | collective-permute-done | bytes 98336 | tf_op jit(solution)/shard_map/ppermute | solution.py:340
  70.2 2.1 %rank.3 = (bf16[3,128,128]{2,1,0:T(8,128)(2,1)S(1)}, f32[8,128]{1,0:T(8,128)}) custom-call(s32[16]{0:T(128)S(1)} %copy-done.15, bf16[12,64,1152]{2,1,0:T(8,128)(2,1)S(1)} %collect.1.held, bf16[2,64,1152]{2,1,0:T(8,128)(2,1)S(1)} %collective-permute-done.5.refs_0_, bf16[2,64,1152]{2,1,0:T(8,128)(2,1)S(1)} %collective-permute-done.6.refs_1_, ...), custom_call_target="tpu_custom_call" | custom-call | tf_op jit(solution)/shard_map/rank/pallas_call | solution.py:274
  72.3 0.4 collective-permute-start.13
  72.8 0.0 collective-permute-start.14
  72.8 0.5 collective-permute-start.16
  73.3 0.0 collective-permute-start.17
  73.3 3.7 %collective-permute-done.13.refs_1_ = bf16[3,128,128]{2,1,0:T(8,128)(2,1)S(1)} collective-permute-done((bf16[3,128,128]{2,1,0:T(8,128)(2,1)S(1)}, bf16[3,128,128]{2,1,0:T(8,128)(2,1)S(1)}, u32[]{:S(2)}, u32[]{:S(2)}) %collective-permute-start.13) | collective-permute-done | bytes 98336 | tf_op jit(solution)/shard_map/ppermute | solution.py:340
  77.0 1.3 %collective-permute-done.15.refs_5_ = bf16[3,128,128]{2,1,0:T(8,128)(2,1)S(1)} collective-permute-done((bf16[3,128,128]{2,1,0:T(8,128)(2,1)S(1)}, bf16[3,128,128]{2,1,0:T(8,128)(2,1)S(1)}, u32[]{:S(2)}, u32[]{:S(2)}) %collective-permute-start.15) | collective-permute-done | bytes 98336 | tf_op jit(solution)/shard_map/ppermute | solution.py:327
  78.3 1.1 %final.1 = bf16[384,512]{1,0:T(8,128)(2,1)} custom-call(f32[384,512]{1,0:T(8,128)S(1)} %copy-done.9, f32[384,512]{1,0:T(8,128)S(1)} %collective-permute-done.9.base_b, bf16[3,128,128]{2,1,0:T(8,128)(2,1)S(1)} %get-tuple-element.28.refs_0_, bf16[3,128,128]{2,1,0:T(8,128)(2,1)S(1)} %collective-permute-done.13.refs_1_, ...), custom_call_target="tpu_custom_call" | custom-call | tf_op jit(solution)/shard_map/final/pallas_call | solution.py:308
  (34 shorter events, 0.1 us)
Async XLA Ops:
  1.9 10.2 %copy-start.10 = (bf16[2,64,1152]{2,1,0:T(8,128)(2,1)S(1)}, bf16[2,64,1152]{2,1,0:T(8,128)(2,1)}, u32[]{:S(2)}) copy-start(bf16[2,64,1152]{2,1,0:T(8,128)(2,1)} %get-tuple-element.21.refs_0_) | copy-start | bytes 884740
  1.9 12.3 %collective-permute-start.2 = (bf16[2,64,1152]{2,1,0:T(8,128)(2,1)}, bf16[2,64,1152]{2,1,0:T(8,128)(2,1)S(1)}, u32[]{:S(2)}, u32[]{:S(2)}) collective-permute-start(bf16[2,64,1152]{2,1,0:T(8,128)(2,1)} %get-tuple-element.23), channel_id=1, source_target_pairs={{0,2},{2,0},{1,3},{3,1},{4,6},{6,4},{5,7},{7,5},{8,10},{10,8},{9,1... | collective-permute-start | bytes 884744 | tf_op jit(solution)/shard_map/ppermute | solution.py:357
  5.0 10.7 %collective-permute-start.1 = (bf16[2,64,1152]{2,1,0:T(8,128)(2,1)}, bf16[2,64,1152]{2,1,0:T(8,128)(2,1)S(1)}, u32[]{:S(2)}, u32[]{:S(2)}) collective-permute-start(bf16[2,64,1152]{2,1,0:T(8,128)(2,1)} %get-tuple-element.21.refs_0_), channel_id=1, source_target_pairs={{0,4},{4,8},{8,12},{12,0},{1,5},{5,9},{9,13},{13,1},{2,6},{6,10},{... | collective-permute-start | bytes 884744 | tf_op jit(solution)/shard_map/ppermute | solution.py:330
  10.1 47.4 %collective-permute-start.7 = (bf16[400,1024]{1,0:T(8,128)(2,1)}, bf16[400,1024]{1,0:T(8,128)(2,1)S(1)}, u32[]{:S(2)}, u32[]{:S(2)}) collective-permute-start(bf16[400,1024]{1,0:T(8,128)(2,1)} %get-tuple-element.25), channel_id=1, source_target_pairs={{0,18},{2,16},{16,2},{18,0},{1,19},{3,17},{17,3},{19,1},{4,22},{6,... | collective-permute-start | bytes 2457608 | tf_op jit(solution)/shard_map/ppermute | solution.py:340
  11.6 45.9 %collective-permute-start.8 = (bf16[400,1024]{1,0:T(8,128)(2,1)}, bf16[400,1024]{1,0:T(8,128)(2,1)}, u32[]{:S(2)}, u32[]{:S(2)}) collective-permute-start(bf16[400,1024]{1,0:T(8,128)(2,1)} %get-tuple-element.26), channel_id=1, source_target_pairs={{0,16},{2,18},{16,0},{18,2},{1,17},{3,19},{17,1},{19,3},{4,20},{6,... | collective-permute-start | bytes 2457608 | tf_op jit(solution)/shard_map/ppermute | solution.py:340
  12.2 28.4 %collective-permute-start = (bf16[2,64,1152]{2,1,0:T(8,128)(2,1)S(1)}, bf16[2,64,1152]{2,1,0:T(8,128)(2,1)S(1)}, u32[]{:S(2)}, u32[]{:S(2)}) collective-permute-start(bf16[2,64,1152]{2,1,0:T(8,128)(2,1)S(1)} %copy-done.10), channel_id=1, source_target_pairs={{0,12},{4,0},{8,4},{12,8},{1,13},{5,1},{9,5},{13,9},{2,14},{6,2},{... | collective-permute-start | bytes 884744 | tf_op jit(solution)/shard_map/ppermute | solution.py:330
  14.2 26.4 %copy-start.12 = (bf16[2,64,1152]{2,1,0:T(8,128)(2,1)}, bf16[2,64,1152]{2,1,0:T(8,128)(2,1)S(1)}, u32[]{:S(2)}) copy-start(bf16[2,64,1152]{2,1,0:T(8,128)(2,1)S(1)} %collective-permute-done.2.refs_3_) | copy-start | bytes 884740
  14.2 27.1 %collective-permute-start.4 = (bf16[2,64,1152]{2,1,0:T(8,128)(2,1)S(1)}, bf16[2,64,1152]{2,1,0:T(8,128)(2,1)S(1)}, u32[]{:S(2)}, u32[]{:S(2)}) collective-permute-start(bf16[2,64,1152]{2,1,0:T(8,128)(2,1)S(1)} %collective-permute-done.2.refs_3_), channel_id=1, source_target_pairs={{0,4},{4,8},{8,12},{12,0},{1,5},{5,9},{9,13},{13,1},{2,6},{6,10},{... | collective-permute-start | bytes 884744 | tf_op jit(solution)/shard_map/ppermute | solution.py:330
  15.7 24.9 %copy-start.4 = (bf16[2,64,1152]{2,1,0:T(8,128)(2,1)}, bf16[2,64,1152]{2,1,0:T(8,128)(2,1)S(1)}, u32[]{:S(2)}) copy-start(bf16[2,64,1152]{2,1,0:T(8,128)(2,1)S(1)} %collective-permute-done.1.refs_0_) | copy-start | bytes 884740
  15.7 25.7 %collective-permute-start.3 = (bf16[2,64,1152]{2,1,0:T(8,128)(2,1)S(1)}, bf16[2,64,1152]{2,1,0:T(8,128)(2,1)S(1)}, u32[]{:S(2)}, u32[]{:S(2)}) collective-permute-start(bf16[2,64,1152]{2,1,0:T(8,128)(2,1)S(1)} %collective-permute-done.2.refs_3_), channel_id=1, source_target_pairs={{0,12},{4,0},{8,4},{12,8},{1,13},{5,1},{9,5},{13,9},{2,14},{6,2},{... | collective-permute-start | bytes 884744 | tf_op jit(solution)/shard_map/ppermute | solution.py:330
  40.6 17.0 %copy-start.8 = (bf16[400,1024]{1,0:T(8,128)(2,1)S(1)}, bf16[400,1024]{1,0:T(8,128)(2,1)}, u32[]{:S(2)}) copy-start(bf16[400,1024]{1,0:T(8,128)(2,1)} %get-tuple-element.24.refs_2_) | copy-start | bytes 2457604
  40.6 17.0 %copy-start.15 = (s32[16]{0:T(128)S(1)}, s32[16]{0:T(128)}, u32[]{:S(2)}) copy-start(s32[16]{0:T(128)} %owner.3) | copy-start | bytes 196
  40.6 0.7 copy-start
  41.3 16.2 %collective-permute-start.5 = (bf16[2,64,1152]{2,1,0:T(8,128)(2,1)}, bf16[2,64,1152]{2,1,0:T(8,128)(2,1)S(1)}, u32[]{:S(2)}, u32[]{:S(2)}) collective-permute-start(bf16[2,64,1152]{2,1,0:T(8,128)(2,1)} %hand.3.refs_2_), channel_id=1, source_target_pairs={{0,4},{4,8},{8,12},{12,0},{1,5},{5,9},{9,13},{13,1},{2,6},{6,10},{... | collective-permute-start | bytes 884744 | tf_op jit(solution)/shard_map/ppermute | solution.py:330
  41.3 0.7 copy-start.2
  42.0 0.7 copy-start.6
  42.8 14.7 %collective-permute-start.6 = (bf16[2,64,1152]{2,1,0:T(8,128)(2,1)}, bf16[2,64,1152]{2,1,0:T(8,128)(2,1)S(1)}, u32[]{:S(2)}, u32[]{:S(2)}) collective-permute-start(bf16[2,64,1152]{2,1,0:T(8,128)(2,1)} %hand.4.refs_4_), channel_id=1, source_target_pairs={{0,12},{4,0},{8,4},{12,8},{1,13},{5,1},{9,5},{13,9},{2,14},{6,2},{... | collective-permute-start | bytes 884744 | tf_op jit(solution)/shard_map/ppermute | solution.py:330
  47.1 17.7 %collective-permute-start.10 = (bf16[400,1024]{1,0:T(8,128)(2,1)}, bf16[400,1024]{1,0:T(8,128)(2,1)}, u32[]{:S(2)}, u32[]{:S(2)}) collective-permute-start(bf16[400,1024]{1,0:T(8,128)(2,1)} %get-tuple-element.29), channel_id=1, source_target_pairs={{0,2},{2,0},{16,18},{18,16},{1,3},{3,1},{17,19},{19,17},{4,6},{6,4... | collective-permute-start | bytes 2457608 | tf_op jit(solution)/shard_map/ppermute | solution.py:340
  51.3 1.0 %copy-start.1 = (bf16[2,64,1152]{2,1,0:T(8,128)(2,1)S(1)}, bf16[2,64,1152]{2,1,0:T(8,128)(2,1)}, u32[]{:S(2)}) copy-start(bf16[2,64,1152]{2,1,0:T(8,128)(2,1)} %copy-done) | copy-start | bytes 884740
  52.3 1.0 %copy-start.3 = (bf16[2,64,1152]{2,1,0:T(8,128)(2,1)S(1)}, bf16[2,64,1152]{2,1,0:T(8,128)(2,1)}, u32[]{:S(2)}) copy-start(bf16[2,64,1152]{2,1,0:T(8,128)(2,1)} %copy-done.2) | copy-start | bytes 884740
  53.2 1.0 %copy-start.5 = (bf16[2,64,1152]{2,1,0:T(8,128)(2,1)S(1)}, bf16[2,64,1152]{2,1,0:T(8,128)(2,1)}, u32[]{:S(2)}) copy-start(bf16[2,64,1152]{2,1,0:T(8,128)(2,1)} %hand.3.refs_2_) | copy-start | bytes 884740
  54.2 1.0 %copy-start.7 = (bf16[2,64,1152]{2,1,0:T(8,128)(2,1)S(1)}, bf16[2,64,1152]{2,1,0:T(8,128)(2,1)}, u32[]{:S(2)}) copy-start(bf16[2,64,1152]{2,1,0:T(8,128)(2,1)} %hand.4.refs_4_) | copy-start | bytes 884740
  55.1 1.0 %copy-start.11 = (bf16[2,64,1152]{2,1,0:T(8,128)(2,1)S(1)}, bf16[2,64,1152]{2,1,0:T(8,128)(2,1)}, u32[]{:S(2)}) copy-start(bf16[2,64,1152]{2,1,0:T(8,128)(2,1)} %get-tuple-element.21.refs_0_) | copy-start | bytes 884740
  56.1 1.0 %copy-start.13 = (bf16[2,64,1152]{2,1,0:T(8,128)(2,1)S(1)}, bf16[2,64,1152]{2,1,0:T(8,128)(2,1)}, u32[]{:S(2)}) copy-start(bf16[2,64,1152]{2,1,0:T(8,128)(2,1)} %copy-done.12) | copy-start | bytes 884740
  59.8 0.6 copy-start.14
  60.4 0.6 copy-start.16
  61.0 0.6 copy-start.17
  61.7 16.6 %copy-start.9 = (f32[384,512]{1,0:T(8,128)S(1)}, f32[384,512]{1,0:T(8,128)}, u32[]{:S(2)}) copy-start(f32[384,512]{1,0:T(8,128)} %get-tuple-element.19.base_a) | copy-start | bytes 2359300
  61.7 16.6 %collective-permute-start.9 = (f32[384,512]{1,0:T(8,128)}, f32[384,512]{1,0:T(8,128)S(1)}, u32[]{:S(2)}, u32[]{:S(2)}) collective-permute-start(f32[384,512]{1,0:T(8,128)} %hand.5), channel_id=1, source_target_pairs={{0,1},{1,0},{2,3},{3,2},{4,5},{5,4},{6,7},{7,6},{8,9},{9,8},{10,11... | collective-permute-start | bytes 2359304 | tf_op jit(solution)/shard_map/ppermute | solution.py:327
  61.7 5.5 %collective-permute-start.11 = (bf16[3,128,128]{2,1,0:T(8,128)(2,1)}, bf16[3,128,128]{2,1,0:T(8,128)(2,1)S(1)}, u32[]{:S(2)}, u32[]{:S(2)}) collective-permute-start(bf16[3,128,128]{2,1,0:T(8,128)(2,1)} %copy-done.17), channel_id=1, source_target_pairs={{0,16},{2,18},{16,0},{18,2},{1,17},{3,19},{17,1},{19,3},{4,20},{6,... | collective-permute-start | bytes 294920 | tf_op jit(solution)/shard_map/ppermute | solution.py:340
  62.6 7.6 %collective-permute-start.12 = (bf16[3,128,128]{2,1,0:T(8,128)(2,1)}, bf16[3,128,128]{2,1,0:T(8,128)(2,1)S(1)}, u32[]{:S(2)}, u32[]{:S(2)}) collective-permute-start(bf16[3,128,128]{2,1,0:T(8,128)(2,1)} %copy-done.16), channel_id=1, source_target_pairs={{0,18},{2,16},{16,2},{18,0},{1,19},{3,17},{17,3},{19,1},{4,22},{6,... | collective-permute-start | bytes 294920 | tf_op jit(solution)/shard_map/ppermute | solution.py:340
  72.3 4.6 %collective-permute-start.13 = (bf16[3,128,128]{2,1,0:T(8,128)(2,1)S(1)}, bf16[3,128,128]{2,1,0:T(8,128)(2,1)S(1)}, u32[]{:S(2)}, u32[]{:S(2)}) collective-permute-start(bf16[3,128,128]{2,1,0:T(8,128)(2,1)S(1)} %get-tuple-element.32), channel_id=1, source_target_pairs={{0,2},{2,0},{16,18},{18,16},{1,3},{3,1},{17,19},{19,17},{4,6},{6,4... | collective-permute-start | bytes 294920 | tf_op jit(solution)/shard_map/ppermute | solution.py:340
  72.8 4.2 %collective-permute-start.14 = (bf16[3,128,128]{2,1,0:T(8,128)(2,1)S(1)}, bf16[3,128,128]{2,1,0:T(8,128)(2,1)S(1)}, u32[]{:S(2)}, u32[]{:S(2)}) collective-permute-start(bf16[3,128,128]{2,1,0:T(8,128)(2,1)S(1)} %get-tuple-element.28.refs_0_), channel_id=1, source_target_pairs={{0,1},{1,0},{2,3},{3,2},{4,5},{5,4},{6,7},{7,6},{8,9},{9,8},{10,11... | collective-permute-start | bytes 294920 | tf_op jit(solution)/shard_map/ppermute | solution.py:327
  72.8 4.2 %collective-permute-start.16 = (bf16[3,128,128]{2,1,0:T(8,128)(2,1)S(1)}, bf16[3,128,128]{2,1,0:T(8,128)(2,1)S(1)}, u32[]{:S(2)}, u32[]{:S(2)}) collective-permute-start(bf16[3,128,128]{2,1,0:T(8,128)(2,1)S(1)} %collective-permute-done.11.refs_3_.refs_2_), channel_id=1, source_target_pairs={{0,1},{1,0},{2,3},{3,2},{4,5},{5,4},{6,7},{7,6},{8,9},{9,8},{10,11... | collective-permute-start | bytes 294920 | tf_op jit(solution)/shard_map/ppermute | solution.py:327
  73.3 3.7 %collective-permute-start.17 = (bf16[3,128,128]{2,1,0:T(8,128)(2,1)S(1)}, bf16[3,128,128]{2,1,0:T(8,128)(2,1)S(1)}, u32[]{:S(2)}, u32[]{:S(2)}) collective-permute-start(bf16[3,128,128]{2,1,0:T(8,128)(2,1)S(1)} %collective-permute-done.12.refs_4_.refs_3_), channel_id=1, source_target_pairs={{0,1},{1,0},{2,3},{3,2},{4,5},{5,4},{6,7},{7,6},{8,9},{9,8},{10,11... | collective-permute-start | bytes 294920 | tf_op jit(solution)/shard_map/ppermute | solution.py:327
  77.0 1.3 %collective-permute-start.15 = (bf16[3,128,128]{2,1,0:T(8,128)(2,1)S(1)}, bf16[3,128,128]{2,1,0:T(8,128)(2,1)S(1)}, u32[]{:S(2)}, u32[]{:S(2)}) collective-permute-start(bf16[3,128,128]{2,1,0:T(8,128)(2,1)S(1)} %collective-permute-done.13.refs_1_), channel_id=1, source_target_pairs={{0,1},{1,0},{2,3},{3,2},{4,5},{5,4},{6,7},{7,6},{8,9},{9,8},{10,11... | collective-permute-start | bytes 294920 | tf_op jit(solution)/shard_map/ppermute | solution.py:327

commit v29 on v26

--- a/solution.py
+++ b/solution.py
@@ -231,9 +231,7 @@
 
 
 def rank_kernel(ring, pair, rows, shares, owner, held, *refs):
-    late, toks, outs = refs[: -1 - 2 * shares], refs[-1 - 2 * shares : -1 - shares], refs[-1 - shares : -1]
-    flag = refs[-1]
-    flag[...] = jnp.zeros_like(flag)
+    late, toks, outs = refs[: -2 * shares], refs[-2 * shares : -shares], refs[-shares:]
     rank = held.shape[1]
     per = owner.shape[0] // (ring * pair)
     blocks, _, block = outs[0].shape
@@ -275,9 +273,8 @@
     return pl.pallas_call(
         functools.partial(rank_kernel, ring, pair, rows, shares),
         in_specs=[SMEM, VMEM] + [VMEM] * (len(late) + shares),
-        out_specs=[VMEM] * (shares + 1),
-        out_shape=[jax.ShapeDtypeStruct((blocks, 2 * rank, rows // blocks), held.dtype)] * shares
-        + [jax.ShapeDtypeStruct((8, LANES), jnp.float32)],
+        out_specs=[VMEM] * shares,
+        out_shape=[jax.ShapeDtypeStruct((blocks, 2 * rank, rows // blocks), held.dtype)] * shares,
         cost_estimate=pl.CostEstimate(flops=0, bytes_accessed=0, transcendentals=0),
         compiler_params=ROOM,
         name="rank",
@@ -369,10 +366,10 @@
     halfway = ring // 2 if ring % 2 == 0 else ring
     held = collect([piece for way in pieces for away, piece in enumerate(way) if away != halfway])
     late = [way[halfway] for way in pieces] if halfway < ring else []
-    *parts, ready = rank_parts(owner_slot, toks, held, late, ring, pair, rows, blocks)
+    parts = rank_parts(owner_slot, toks, held, late, ring, pair, rows, blocks)
     mine = [parts[0]] + [in_plane(parts[k], -(k // pair), -(k % pair)) for k in range(1, shares)]
     theirs = [across(part) for part in mine]
-    base_in = across(hand_on(base_out, ready))
+    base_in = across(base_out)
     return final(mine, theirs, [base_mine, base_in], groups, pair, tokens.dtype)
 
 

time: 65.9 us -> 72.5 us (1.10)
  waiting for transfers between devices: 20.7 us -> 27.6 us
  local copies, waits for them, and re-layouts: 6.84 us -> 4.63 us
  Pallas kernels: 18 us -> 19.1 us
    ppermute x6, waiting for transfers between devices: 10.6 us -> 14.5 us  [in_plane(): return lax.ppermute(x, PLANE, pairs)]
    ppermute x1, waiting for transfers between devices: 0.01 us -> 3.5 us  [body(): lax.ppermute(packed[pair - w], 'pair', [(a, (a - w) % pair) for a in rang...]
    unnamed x30 -> x24, local copies, waits for them, and re-layouts: 6.84 us -> 4.63 us
    ppermute x6, starting transfers between devices: 7.04 us -> 8.28 us  [in_plane(): return lax.ppermute(x, PLANE, pairs)]
    pallas_call x1, Pallas kernels: 1.06 us -> 2.18 us  [final(): pl.pallas_call(functools.partial(final_kernel, groups, pair), in_specs=[V...]
  transfers between devices with their start and end apart: 18 -> 18, of which waited for: 9 -> 9; matrix products, arithmetic and copies ran while one was open for 0% -> 0% of each run, Pallas kernels for 19% -> 21%
where the time goes in v29:
time: 72.5 us; the launch traced here: 72.1 us
  waiting for transfers between devices  27.6 us (38%)
  starting transfers between devices  20.6 us (28%)
  Pallas kernels  19.1 us (26%)
  local copies, waits for them, and re-layouts  4.63 us (6%)
    ppermute x6, waiting for transfers between devices, in_plane(): return lax.ppermute(x, PLANE, pairs)  14.5 us
    ppermute x6, starting transfers between devices, along(): lax.ppermute(x, 'ring', [(a, (a + step) % ring) for a in range(ring)])  9.24 us
    ppermute x6, waiting for transfers between devices, along(): lax.ppermute(x, 'ring', [(a, (a + step) % ring) for a in range(ring)])  8.33 us
    ppermute x6, starting transfers between devices, in_plane(): return lax.ppermute(x, PLANE, pairs)  8.28 us
    pallas_call x1, Pallas kernels, base_halves(): pl.pallas_call(functools.partial(base_kernel, sides), in_specs=[SMEM, ANY...  7.87 us
    unnamed x24, local copies, waits for them, and re-layouts  4.63 us
    pallas_call x1, Pallas kernels, spread(): pl.pallas_call(functools.partial(spread_kernel, groups, pair), in_specs=[...  3.64 us
    ppermute x1, waiting for transfers between devices, body(): lax.ppermute(packed[pair - w], 'pair', [(a, (a - w) % pair) for a in rang...  3.5 us
  transfers between devices with their start and end apart: 18, of which 9 were waited for; matrix products, arithmetic and copies ran while one was open for 0% of the time, Pallas kernels for 21%

profile of v29, /device:TPU:0, one launch (start us, length us, event | category | flops | bytes accessed | tf_op | source)
XLA Modules:
  0.0 72.1 jit_solution(14773038087478348511)
XLA Ops:
  0.0 1.9 %pack.1 = (bf16[2,64,1152]{2,1,0:T(8,128)(2,1)}, bf16[2,64,1152]{2,1,0:T(8,128)(2,1)}) custom-call(bf16[2,64,4096]{2,1,0:T(8,128)(2,1)} %bitcast.2, bf16[2,64,512]{2,1,0:T(8,128)(2,1)} %up.1), custom_call_target="tpu_custom_call" | custom-call | tf_op jit(solution)/shard_map/pack/pallas_call | solution.py:57
  1.9 3.0 %collective-permute-start.3 = (bf16[2,64,1152]{2,1,0:T(8,128)(2,1)}, bf16[2,64,1152]{2,1,0:T(8,128)(2,1)}, u32[]{:S(2)}, u32[]{:S(2)}) collective-permute-start(bf16[2,64,1152]{2,1,0:T(8,128)(2,1)} %get-tuple-element.22), channel_id=1, source_target_pairs={{0,2},{2,0},{1,3},{3,1},{4,6},{6,4},{5,7},{7,5},{8,10},{10,8},{9,1... | collective-permute-start | bytes 884744 | tf_op jit(solution)/shard_map/ppermute | solution.py:355
  4.9 1.6 %collective-permute-start.2 = (bf16[2,64,1152]{2,1,0:T(8,128)(2,1)}, bf16[2,64,1152]{2,1,0:T(8,128)(2,1)S(1)}, u32[]{:S(2)}, u32[]{:S(2)}) collective-permute-start(bf16[2,64,1152]{2,1,0:T(8,128)(2,1)} %get-tuple-element.20.refs_0_), channel_id=1, source_target_pairs={{0,4},{4,8},{8,12},{12,0},{1,5},{5,9},{9,13},{13,1},{2,6},{6,10},{... | collective-permute-start | bytes 884744 | tf_op jit(solution)/shard_map/ppermute | solution.py:328
  6.5 2.2 %collective-permute-start.1 = (bf16[2,64,1152]{2,1,0:T(8,128)(2,1)}, bf16[2,64,1152]{2,1,0:T(8,128)(2,1)S(1)}, u32[]{:S(2)}, u32[]{:S(2)}) collective-permute-start(bf16[2,64,1152]{2,1,0:T(8,128)(2,1)} %get-tuple-element.20.refs_0_), channel_id=1, source_target_pairs={{0,12},{4,0},{8,4},{12,8},{1,13},{5,1},{9,5},{13,9},{2,14},{6,2},{... | collective-permute-start | bytes 884744 | tf_op jit(solution)/shard_map/ppermute | solution.py:328
  8.8 3.5 %collective-permute-done.3.refs_3_ = bf16[2,64,1152]{2,1,0:T(8,128)(2,1)} collective-permute-done((bf16[2,64,1152]{2,1,0:T(8,128)(2,1)}, bf16[2,64,1152]{2,1,0:T(8,128)(2,1)}, u32[]{:S(2)}, u32[]{:S(2)}) %collective-permute-start.3) | collective-permute-done | bytes 294944 | tf_op jit(solution)/shard_map/ppermute | solution.py:355
  12.3 1.8 %collective-permute-start.5 = (bf16[2,64,1152]{2,1,0:T(8,128)(2,1)}, bf16[2,64,1152]{2,1,0:T(8,128)(2,1)S(1)}, u32[]{:S(2)}, u32[]{:S(2)}) collective-permute-start(bf16[2,64,1152]{2,1,0:T(8,128)(2,1)} %collective-permute-done.3.refs_3_), channel_id=1, source_target_pairs={{0,4},{4,8},{8,12},{12,0},{1,5},{5,9},{9,13},{13,1},{2,6},{6,10},{... | collective-permute-start | bytes 884744 | tf_op jit(solution)/shard_map/ppermute | solution.py:328
  14.1 2.0 %collective-permute-start.4 = (bf16[2,64,1152]{2,1,0:T(8,128)(2,1)}, bf16[2,64,1152]{2,1,0:T(8,128)(2,1)S(1)}, u32[]{:S(2)}, u32[]{:S(2)}) collective-permute-start(bf16[2,64,1152]{2,1,0:T(8,128)(2,1)} %collective-permute-done.3.refs_3_), channel_id=1, source_target_pairs={{0,12},{4,0},{8,4},{12,8},{1,13},{5,1},{9,5},{13,9},{2,14},{6,2},{... | collective-permute-start | bytes 884744 | tf_op jit(solution)/shard_map/ppermute | solution.py:328
  16.1 3.6 %spread.1 = (bf16[400,1024]{1,0:T(8,128)(2,1)}, bf16[400,1024]{1,0:T(8,128)(2,1)}, bf16[400,1024]{1,0:T(8,128)(2,1)}, bf16[400,1024]{1,0:T(8,128)(2,1)}) custom-call(s32[3]{0:T(128)} %lengths.3, s32[3]{0:T(128)} %bitcast.3, bf16[384,4096]{1,0:T(8,128)(2,1)} %tok.3), custom_call_target="tpu_custom_call" | custom-call | tf_op jit(solution)/shard_map/spread/pallas_call | solution.py:126
  19.7 1.8 %collective-permute-start.8 = (bf16[400,1024]{1,0:T(8,128)(2,1)}, bf16[400,1024]{1,0:T(8,128)(2,1)S(1)}, u32[]{:S(2)}, u32[]{:S(2)}) collective-permute-start(bf16[400,1024]{1,0:T(8,128)(2,1)} %get-tuple-element.24), channel_id=1, source_target_pairs={{0,2},{2,0},{16,18},{18,16},{1,3},{3,1},{17,19},{19,17},{4,6},{6,4... | collective-permute-start | bytes 2457608 | tf_op jit(solution)/shard_map/ppermute | solution.py:338
  21.5 0.0 collective-permute-done.2.refs_0_
  21.5 1.5 %collective-permute-start.9 = (bf16[400,1024]{1,0:T(8,128)(2,1)}, bf16[400,1024]{1,0:T(8,128)(2,1)S(1)}, u32[]{:S(2)}, u32[]{:S(2)}) collective-permute-start(bf16[400,1024]{1,0:T(8,128)(2,1)} %get-tuple-element.25), channel_id=1, source_target_pairs={{0,16},{2,18},{16,0},{18,2},{1,17},{3,19},{17,1},{19,3},{4,20},{6,... | collective-permute-start | bytes 2457608 | tf_op jit(solution)/shard_map/ppermute | solution.py:338
  23.0 0.6 collective-permute-done.1.refs_1_
  23.6 1.4 %collective-permute-start.10 = (bf16[400,1024]{1,0:T(8,128)(2,1)}, bf16[400,1024]{1,0:T(8,128)(2,1)}, u32[]{:S(2)}, u32[]{:S(2)}) collective-permute-start(bf16[400,1024]{1,0:T(8,128)(2,1)} %get-tuple-element.26), channel_id=1, source_target_pairs={{0,18},{2,16},{16,2},{18,0},{1,19},{3,17},{17,3},{19,1},{4,22},{6,... | collective-permute-start | bytes 2457608 | tf_op jit(solution)/shard_map/ppermute | solution.py:338
  25.1 7.9 %base.1 = (f32[384,512]{1,0:T(8,128)}, f32[384,512]{1,0:T(8,128)}, f32[8,128]{1,0:T(8,128)}) custom-call(s32[3]{0:T(128)} %lengths.3, bf16[384,4096]{1,0:T(8,128)(2,1)} %tok.3, bf16[4096,1024]{1,0:T(8,128)(2,1)} %key.1), custom_call_target="tpu_custom_call" | custom-call | tf_op jit(solution)/shard_map/base/pallas_call | solution.py:190
  33.0 0.0 copy-start.11
  33.0 0.0 collective-permute-done.5.refs_1_.refs_5_
  33.0 0.3 collective-permute-start.6
  33.3 0.6 collective-permute-done.4.refs_0_
  33.9 0.0 collective-permute-start
  33.9 0.8 %copy-done.6 = bf16[2,64,1152]{2,1,0:T(8,128)(2,1)} copy-done((bf16[2,64,1152]{2,1,0:T(8,128)(2,1)}, bf16[2,64,1152]{2,1,0:T(8,128)(2,1)S(1)}, u32[]{:S(2)}) %copy-start.6) | copy-done | bytes 294936
  34.6 7.2 %collective-permute-done.6.refs_0_ = bf16[2,64,1152]{2,1,0:T(8,128)(2,1)S(1)} collective-permute-done((bf16[2,64,1152]{2,1,0:T(8,128)(2,1)}, bf16[2,64,1152]{2,1,0:T(8,128)(2,1)S(1)}, u32[]{:S(2)}, u32[]{:S(2)}) %collective-permute-start.6) | collective-permute-done | bytes 294944 | tf_op jit(solution)/shard_map/ppermute | solution.py:328
  41.8 1.3 %collective-permute-start.7 = (bf16[2,64,1152]{2,1,0:T(8,128)(2,1)}, bf16[2,64,1152]{2,1,0:T(8,128)(2,1)S(1)}, u32[]{:S(2)}, u32[]{:S(2)}) collective-permute-start(bf16[2,64,1152]{2,1,0:T(8,128)(2,1)} %hand.3.refs_4_), channel_id=1, source_target_pairs={{0,12},{4,0},{8,4},{12,8},{1,13},{5,1},{9,5},{13,9},{2,14},{6,2},{... | collective-permute-start | bytes 884744 | tf_op jit(solution)/shard_map/ppermute | solution.py:328
  43.1 1.0 %copy-done.1 = bf16[2,64,1152]{2,1,0:T(8,128)(2,1)S(1)} copy-done((bf16[2,64,1152]{2,1,0:T(8,128)(2,1)S(1)}, bf16[2,64,1152]{2,1,0:T(8,128)(2,1)}, u32[]{:S(2)}) %copy-start.1) | copy-done | bytes 294936
  44.1 1.0 %copy-done.3 = bf16[2,64,1152]{2,1,0:T(8,128)(2,1)S(1)} copy-done((bf16[2,64,1152]{2,1,0:T(8,128)(2,1)S(1)}, bf16[2,64,1152]{2,1,0:T(8,128)(2,1)}, u32[]{:S(2)}) %copy-start.3) | copy-done | bytes 294936
  45.0 1.0 %copy-done.5 = bf16[2,64,1152]{2,1,0:T(8,128)(2,1)S(1)} copy-done((bf16[2,64,1152]{2,1,0:T(8,128)(2,1)S(1)}, bf16[2,64,1152]{2,1,0:T(8,128)(2,1)}, u32[]{:S(2)}) %copy-start.5) | copy-done | bytes 294936
  46.0 1.0 %copy-done.7 = bf16[2,64,1152]{2,1,0:T(8,128)(2,1)S(1)} copy-done((bf16[2,64,1152]{2,1,0:T(8,128)(2,1)S(1)}, bf16[2,64,1152]{2,1,0:T(8,128)(2,1)}, u32[]{:S(2)}) %copy-start.7) | copy-done | bytes 294936
  47.0 1.2 %collect.1.held = bf16[12,64,1152]{2,1,0:T(8,128)(2,1)S(1)} custom-call(bf16[2,64,1152]{2,1,0:T(8,128)(2,1)S(1)} %copy-done.10, bf16[2,64,1152]{2,1,0:T(8,128)(2,1)S(1)} %copy-done.1, bf16[2,64,1152]{2,1,0:T(8,128)(2,1)S(1)} %copy-done.5, bf16[2,64,1152]{2,1,0:T(8,128)(2,1)} %collective-permute-done.3.refs_3_, bf16[2,64,1152]{2,1,0:T(8,128)(2,1)S(1)} %copy-done.7, ...), custom_call_target="tpu_custom_call" | custom-call | tf_op jit(solution)/shard_map/collect/pallas_call | solution.py:222
  48.2 0.0 collective-permute-done.8.refs_3_
  48.2 0.0 collective-permute-done.9.refs_4_
  48.2 9.5 %collective-permute-done.10.refs_5_ = bf16[400,1024]{1,0:T(8,128)(2,1)} collective-permute-done((bf16[400,1024]{1,0:T(8,128)(2,1)}, bf16[400,1024]{1,0:T(8,128)(2,1)}, u32[]{:S(2)}, u32[]{:S(2)}) %collective-permute-start.10) | collective-permute-done | bytes 819232 | tf_op jit(solution)/shard_map/ppermute | solution.py:338
  57.7 0.0 collective-permute-done.7.refs_1_
  57.7 2.3 %rank.1 = (bf16[3,128,128]{2,1,0:T(8,128)(2,1)S(1)}, bf16[3,128,128]{2,1,0:T(8,128)(2,1)S(1)}, bf16[3,128,128]{2,1,0:T(8,128)(2,1)S(1)}, bf16[3,128,128]{2,1,0:T(8,128)(2,1)S(1)}) custom-call(s32[16]{0:T(128)S(1)} %copy-done.11, bf16[12,64,1152]{2,1,0:T(8,128)(2,1)S(1)} %collect.1.held, bf16[2,64,1152]{2,1,0:T(8,128)(2,1)S(1)} %collective-permute-done.6.refs_0_, ...), custom_call_target="tpu_custom_call" | custom-call | tf_op jit(solution)/shard_map/rank/pallas_call | solution.py:273
  60.1 1.5 %collective-permute-start.11 = (bf16[3,128,128]{2,1,0:T(8,128)(2,1)S(1)}, bf16[3,128,128]{2,1,0:T(8,128)(2,1)S(1)}, u32[]{:S(2)}, u32[]{:S(2)}) collective-permute-start(bf16[3,128,128]{2,1,0:T(8,128)(2,1)S(1)} %get-tuple-element.28), channel_id=1, source_target_pairs={{0,2},{2,0},{16,18},{18,16},{1,3},{3,1},{17,19},{19,17},{4,6},{6,4... | collective-permute-start | bytes 294920 | tf_op jit(solution)/shard_map/ppermute | solution.py:338
  61.6 1.5 %collective-permute-start.12 = (bf16[3,128,128]{2,1,0:T(8,128)(2,1)S(1)}, bf16[3,128,128]{2,1,0:T(8,128)(2,1)S(1)}, u32[]{:S(2)}, u32[]{:S(2)}) collective-permute-start(bf16[3,128,128]{2,1,0:T(8,128)(2,1)S(1)} %get-tuple-element.29), channel_id=1, source_target_pairs={{0,16},{2,18},{16,0},{18,2},{1,17},{3,19},{17,1},{19,3},{4,20},{6,... | collective-permute-start | bytes 294920 | tf_op jit(solution)/shard_map/ppermute | solution.py:338
  63.1 0.5 collective-permute-start.13
  63.6 0.0 collective-permute-start.14
  63.6 1.8 %collective-permute-done.11.refs_1_ = bf16[3,128,128]{2,1,0:T(8,128)(2,1)S(1)} collective-permute-done((bf16[3,128,128]{2,1,0:T(8,128)(2,1)S(1)}, bf16[3,128,128]{2,1,0:T(8,128)(2,1)S(1)}, u32[]{:S(2)}, u32[]{:S(2)}) %collective-permute-start.11) | collective-permute-done | bytes 98336 | tf_op jit(solution)/shard_map/ppermute | solution.py:338
  65.4 0.0 collective-permute-start.15
  65.4 0.8 %collective-permute-done.12.refs_2_ = bf16[3,128,128]{2,1,0:T(8,128)(2,1)S(1)} collective-permute-done((bf16[3,128,128]{2,1,0:T(8,128)(2,1)S(1)}, bf16[3,128,128]{2,1,0:T(8,128)(2,1)S(1)}, u32[]{:S(2)}, u32[]{:S(2)}) %collective-permute-start.12) | collective-permute-done | bytes 98336 | tf_op jit(solution)/shard_map/ppermute | solution.py:338
  66.2 0.0 collective-permute-start.16
  66.2 2.4 %collective-permute-done.13.refs_3_ = bf16[3,128,128]{2,1,0:T(8,128)(2,1)S(1)} collective-permute-done((bf16[3,128,128]{2,1,0:T(8,128)(2,1)S(1)}, bf16[3,128,128]{2,1,0:T(8,128)(2,1)S(1)}, u32[]{:S(2)}, u32[]{:S(2)}) %collective-permute-start.13) | collective-permute-done | bytes 98336 | tf_op jit(solution)/shard_map/ppermute | solution.py:338
  68.6 0.0 collective-permute-start.17
  68.6 0.0 collective-permute-done.base_b
  68.6 0.0 collective-permute-done.14.refs_4_
  68.6 0.0 collective-permute-done.15.refs_5_
  68.6 0.0 collective-permute-done.16.refs_6_
  68.6 1.3 %collective-permute-done.17.refs_7_ = bf16[3,128,128]{2,1,0:T(8,128)(2,1)S(1)} collective-permute-done((bf16[3,128,128]{2,1,0:T(8,128)(2,1)S(1)}, bf16[3,128,128]{2,1,0:T(8,128)(2,1)S(1)}, u32[]{:S(2)}, u32[]{:S(2)}) %collective-permute-start.17) | collective-permute-done | bytes 98336 | tf_op jit(solution)/shard_map/ppermute | solution.py:325
  69.9 2.2 %final.1 = bf16[384,512]{1,0:T(8,128)(2,1)} custom-call(f32[384,512]{1,0:T(8,128)S(1)} %copy-done.9, f32[384,512]{1,0:T(8,128)} %collective-permute-done.base_b, bf16[3,128,128]{2,1,0:T(8,128)(2,1)S(1)} %get-tuple-element.27.refs_0_, bf16[3,128,128]{2,1,0:T(8,128)(2,1)S(1)} %collective-permute-done.11.refs_1_, ...), custom_call_target="tpu_custom_call" | custom-call | tf_op jit(solution)/shard_map/final/pallas_call | solution.py:306
  (20 shorter events, 0.0 us)
Async XLA Ops:
  1.9 10.4 %collective-permute-start.3 = (bf16[2,64,1152]{2,1,0:T(8,128)(2,1)}, bf16[2,64,1152]{2,1,0:T(8,128)(2,1)}, u32[]{:S(2)}, u32[]{:S(2)}) collective-permute-start(bf16[2,64,1152]{2,1,0:T(8,128)(2,1)} %get-tuple-element.22), channel_id=1, source_target_pairs={{0,2},{2,0},{1,3},{3,1},{4,6},{6,4},{5,7},{7,5},{8,10},{10,8},{9,1... | collective-permute-start | bytes 884744 | tf_op jit(solution)/shard_map/ppermute | solution.py:355
  4.9 16.6 %collective-permute-start.2 = (bf16[2,64,1152]{2,1,0:T(8,128)(2,1)}, bf16[2,64,1152]{2,1,0:T(8,128)(2,1)S(1)}, u32[]{:S(2)}, u32[]{:S(2)}) collective-permute-start(bf16[2,64,1152]{2,1,0:T(8,128)(2,1)} %get-tuple-element.20.refs_0_), channel_id=1, source_target_pairs={{0,4},{4,8},{8,12},{12,0},{1,5},{5,9},{9,13},{13,1},{2,6},{6,10},{... | collective-permute-start | bytes 884744 | tf_op jit(solution)/shard_map/ppermute | solution.py:328
  6.5 17.1 %collective-permute-start.1 = (bf16[2,64,1152]{2,1,0:T(8,128)(2,1)}, bf16[2,64,1152]{2,1,0:T(8,128)(2,1)S(1)}, u32[]{:S(2)}, u32[]{:S(2)}) collective-permute-start(bf16[2,64,1152]{2,1,0:T(8,128)(2,1)} %get-tuple-element.20.refs_0_), channel_id=1, source_target_pairs={{0,12},{4,0},{8,4},{12,8},{1,13},{5,1},{9,5},{13,9},{2,14},{6,2},{... | collective-permute-start | bytes 884744 | tf_op jit(solution)/shard_map/ppermute | solution.py:328
  12.3 20.7 %collective-permute-start.5 = (bf16[2,64,1152]{2,1,0:T(8,128)(2,1)}, bf16[2,64,1152]{2,1,0:T(8,128)(2,1)S(1)}, u32[]{:S(2)}, u32[]{:S(2)}) collective-permute-start(bf16[2,64,1152]{2,1,0:T(8,128)(2,1)} %collective-permute-done.3.refs_3_), channel_id=1, source_target_pairs={{0,4},{4,8},{8,12},{12,0},{1,5},{5,9},{9,13},{13,1},{2,6},{6,10},{... | collective-permute-start | bytes 884744 | tf_op jit(solution)/shard_map/ppermute | solution.py:328
  14.1 19.8 %collective-permute-start.4 = (bf16[2,64,1152]{2,1,0:T(8,128)(2,1)}, bf16[2,64,1152]{2,1,0:T(8,128)(2,1)S(1)}, u32[]{:S(2)}, u32[]{:S(2)}) collective-permute-start(bf16[2,64,1152]{2,1,0:T(8,128)(2,1)} %collective-permute-done.3.refs_3_), channel_id=1, source_target_pairs={{0,12},{4,0},{8,4},{12,8},{1,13},{5,1},{9,5},{13,9},{2,14},{6,2},{... | collective-permute-start | bytes 884744 | tf_op jit(solution)/shard_map/ppermute | solution.py:328
  19.7 28.4 %collective-permute-start.8 = (bf16[400,1024]{1,0:T(8,128)(2,1)}, bf16[400,1024]{1,0:T(8,128)(2,1)S(1)}, u32[]{:S(2)}, u32[]{:S(2)}) collective-permute-start(bf16[400,1024]{1,0:T(8,128)(2,1)} %get-tuple-element.24), channel_id=1, source_target_pairs={{0,2},{2,0},{16,18},{18,16},{1,3},{3,1},{17,19},{19,17},{4,6},{6,4... | collective-permute-start | bytes 2457608 | tf_op jit(solution)/shard_map/ppermute | solution.py:338
  21.5 11.4 %copy-start.4 = (bf16[2,64,1152]{2,1,0:T(8,128)(2,1)}, bf16[2,64,1152]{2,1,0:T(8,128)(2,1)S(1)}, u32[]{:S(2)}) copy-start(bf16[2,64,1152]{2,1,0:T(8,128)(2,1)S(1)} %collective-permute-done.2.refs_0_) | copy-start | bytes 884740
  21.5 26.6 %collective-permute-start.9 = (bf16[400,1024]{1,0:T(8,128)(2,1)}, bf16[400,1024]{1,0:T(8,128)(2,1)S(1)}, u32[]{:S(2)}, u32[]{:S(2)}) collective-permute-start(bf16[400,1024]{1,0:T(8,128)(2,1)} %get-tuple-element.25), channel_id=1, source_target_pairs={{0,16},{2,18},{16,0},{18,2},{1,17},{3,19},{17,1},{19,3},{4,20},{6,... | collective-permute-start | bytes 2457608 | tf_op jit(solution)/shard_map/ppermute | solution.py:338
  23.6 9.3 %copy-start = (bf16[2,64,1152]{2,1,0:T(8,128)(2,1)}, bf16[2,64,1152]{2,1,0:T(8,128)(2,1)S(1)}, u32[]{:S(2)}) copy-start(bf16[2,64,1152]{2,1,0:T(8,128)(2,1)S(1)} %collective-permute-done.1.refs_1_) | copy-start | bytes 884740
  23.6 19.5 %copy-start.10 = (bf16[2,64,1152]{2,1,0:T(8,128)(2,1)S(1)}, bf16[2,64,1152]{2,1,0:T(8,128)(2,1)}, u32[]{:S(2)}) copy-start(bf16[2,64,1152]{2,1,0:T(8,128)(2,1)} %get-tuple-element.20.refs_0_) | copy-start | bytes 884740
  23.6 34.1 %collective-permute-start.10 = (bf16[400,1024]{1,0:T(8,128)(2,1)}, bf16[400,1024]{1,0:T(8,128)(2,1)}, u32[]{:S(2)}, u32[]{:S(2)}) collective-permute-start(bf16[400,1024]{1,0:T(8,128)(2,1)} %get-tuple-element.26), channel_id=1, source_target_pairs={{0,18},{2,16},{16,2},{18,0},{1,19},{3,17},{17,3},{19,1},{4,22},{6,... | collective-permute-start | bytes 2457608 | tf_op jit(solution)/shard_map/ppermute | solution.py:338
  32.9 24.8 %copy-start.8 = (bf16[400,1024]{1,0:T(8,128)(2,1)S(1)}, bf16[400,1024]{1,0:T(8,128)(2,1)}, u32[]{:S(2)}) copy-start(bf16[400,1024]{1,0:T(8,128)(2,1)} %get-tuple-element.23.refs_2_) | copy-start | bytes 2457604
  33.0 24.8 %copy-start.11 = (s32[16]{0:T(128)S(1)}, s32[16]{0:T(128)}, u32[]{:S(2)}) copy-start(s32[16]{0:T(128)} %owner.1) | copy-start | bytes 196
  33.0 0.9 %copy-start.2 = (bf16[2,64,1152]{2,1,0:T(8,128)(2,1)}, bf16[2,64,1152]{2,1,0:T(8,128)(2,1)S(1)}, u32[]{:S(2)}) copy-start(bf16[2,64,1152]{2,1,0:T(8,128)(2,1)S(1)} %collective-permute-done.5.refs_1_.refs_5_) | copy-start | bytes 884740
  33.0 8.8 %collective-permute-start.6 = (bf16[2,64,1152]{2,1,0:T(8,128)(2,1)}, bf16[2,64,1152]{2,1,0:T(8,128)(2,1)S(1)}, u32[]{:S(2)}, u32[]{:S(2)}) collective-permute-start(bf16[2,64,1152]{2,1,0:T(8,128)(2,1)} %hand.2.refs_2_), channel_id=1, source_target_pairs={{0,4},{4,8},{8,12},{12,0},{1,5},{5,9},{9,13},{13,1},{2,6},{6,10},{... | collective-permute-start | bytes 884744 | tf_op jit(solution)/shard_map/ppermute | solution.py:328
  33.9 0.8 %copy-start.6 = (bf16[2,64,1152]{2,1,0:T(8,128)(2,1)}, bf16[2,64,1152]{2,1,0:T(8,128)(2,1)S(1)}, u32[]{:S(2)}) copy-start(bf16[2,64,1152]{2,1,0:T(8,128)(2,1)S(1)} %collective-permute-done.4.refs_0_) | copy-start | bytes 884740
  33.9 34.7 %collective-permute-start = (f32[384,512]{1,0:T(8,128)}, f32[384,512]{1,0:T(8,128)}, u32[]{:S(2)}, u32[]{:S(2)}) collective-permute-start(f32[384,512]{1,0:T(8,128)} %get-tuple-element.19), channel_id=1, source_target_pairs={{0,1},{1,0},{2,3},{3,2},{4,5},{5,4},{6,7},{7,6},{8,9},{9,8},{10,11... | collective-permute-start | bytes 2359304 | tf_op jit(solution)/shard_map/ppermute | solution.py:325
  41.8 15.9 %collective-permute-start.7 = (bf16[2,64,1152]{2,1,0:T(8,128)(2,1)}, bf16[2,64,1152]{2,1,0:T(8,128)(2,1)S(1)}, u32[]{:S(2)}, u32[]{:S(2)}) collective-permute-start(bf16[2,64,1152]{2,1,0:T(8,128)(2,1)} %hand.3.refs_4_), channel_id=1, source_target_pairs={{0,12},{4,0},{8,4},{12,8},{1,13},{5,1},{9,5},{13,9},{2,14},{6,2},{... | collective-permute-start | bytes 884744 | tf_op jit(solution)/shard_map/ppermute | solution.py:328
  43.1 1.0 %copy-start.1 = (bf16[2,64,1152]{2,1,0:T(8,128)(2,1)S(1)}, bf16[2,64,1152]{2,1,0:T(8,128)(2,1)}, u32[]{:S(2)}) copy-start(bf16[2,64,1152]{2,1,0:T(8,128)(2,1)} %copy-done) | copy-start | bytes 884740
  44.1 1.0 %copy-start.3 = (bf16[2,64,1152]{2,1,0:T(8,128)(2,1)S(1)}, bf16[2,64,1152]{2,1,0:T(8,128)(2,1)}, u32[]{:S(2)}) copy-start(bf16[2,64,1152]{2,1,0:T(8,128)(2,1)} %copy-done.2) | copy-start | bytes 884740
  45.0 1.0 %copy-start.5 = (bf16[2,64,1152]{2,1,0:T(8,128)(2,1)S(1)}, bf16[2,64,1152]{2,1,0:T(8,128)(2,1)}, u32[]{:S(2)}) copy-start(bf16[2,64,1152]{2,1,0:T(8,128)(2,1)} %hand.2.refs_2_) | copy-start | bytes 884740
  46.0 1.0 %copy-start.7 = (bf16[2,64,1152]{2,1,0:T(8,128)(2,1)S(1)}, bf16[2,64,1152]{2,1,0:T(8,128)(2,1)}, u32[]{:S(2)}) copy-start(bf16[2,64,1152]{2,1,0:T(8,128)(2,1)} %hand.3.refs_4_) | copy-start | bytes 884740
  48.2 21.8 %copy-start.9 = (f32[384,512]{1,0:T(8,128)S(1)}, f32[384,512]{1,0:T(8,128)}, u32[]{:S(2)}) copy-start(f32[384,512]{1,0:T(8,128)} %get-tuple-element.18.base_a) | copy-start | bytes 2359300
  60.1 5.3 %collective-permute-start.11 = (bf16[3,128,128]{2,1,0:T(8,128)(2,1)S(1)}, bf16[3,128,128]{2,1,0:T(8,128)(2,1)S(1)}, u32[]{:S(2)}, u32[]{:S(2)}) collective-permute-start(bf16[3,128,128]{2,1,0:T(8,128)(2,1)S(1)} %get-tuple-element.28), channel_id=1, source_target_pairs={{0,2},{2,0},{16,18},{18,16},{1,3},{3,1},{17,19},{19,17},{4,6},{6,4... | collective-permute-start | bytes 294920 | tf_op jit(solution)/shard_map/ppermute | solution.py:338
  61.6 4.6 %collective-permute-start.12 = (bf16[3,128,128]{2,1,0:T(8,128)(2,1)S(1)}, bf16[3,128,128]{2,1,0:T(8,128)(2,1)S(1)}, u32[]{:S(2)}, u32[]{:S(2)}) collective-permute-start(bf16[3,128,128]{2,1,0:T(8,128)(2,1)S(1)} %get-tuple-element.29), channel_id=1, source_target_pairs={{0,16},{2,18},{16,0},{18,2},{1,17},{3,19},{17,1},{19,3},{4,20},{6,... | collective-permute-start | bytes 294920 | tf_op jit(solution)/shard_map/ppermute | solution.py:338
  63.1 5.5 %collective-permute-start.13 = (bf16[3,128,128]{2,1,0:T(8,128)(2,1)S(1)}, bf16[3,128,128]{2,1,0:T(8,128)(2,1)S(1)}, u32[]{:S(2)}, u32[]{:S(2)}) collective-permute-start(bf16[3,128,128]{2,1,0:T(8,128)(2,1)S(1)} %get-tuple-element.30), channel_id=1, source_target_pairs={{0,18},{2,16},{16,2},{18,0},{1,19},{3,17},{17,3},{19,1},{4,22},{6,... | collective-permute-start | bytes 294920 | tf_op jit(solution)/shard_map/ppermute | solution.py:338
  63.6 5.0 %collective-permute-start.14 = (bf16[3,128,128]{2,1,0:T(8,128)(2,1)S(1)}, bf16[3,128,128]{2,1,0:T(8,128)(2,1)S(1)}, u32[]{:S(2)}, u32[]{:S(2)}) collective-permute-start(bf16[3,128,128]{2,1,0:T(8,128)(2,1)S(1)} %get-tuple-element.27.refs_0_), channel_id=1, source_target_pairs={{0,1},{1,0},{2,3},{3,2},{4,5},{5,4},{6,7},{7,6},{8,9},{9,8},{10,11... | collective-permute-start | bytes 294920 | tf_op jit(solution)/shard_map/ppermute | solution.py:325
  65.4 3.2 %collective-permute-start.15 = (bf16[3,128,128]{2,1,0:T(8,128)(2,1)S(1)}, bf16[3,128,128]{2,1,0:T(8,128)(2,1)S(1)}, u32[]{:S(2)}, u32[]{:S(2)}) collective-permute-start(bf16[3,128,128]{2,1,0:T(8,128)(2,1)S(1)} %collective-permute-done.11.refs_1_), channel_id=1, source_target_pairs={{0,1},{1,0},{2,3},{3,2},{4,5},{5,4},{6,7},{7,6},{8,9},{9,8},{10,11... | collective-permute-start | bytes 294920 | tf_op jit(solution)/shard_map/ppermute | solution.py:325
  66.2 2.4 %collective-permute-start.16 = (bf16[3,128,128]{2,1,0:T(8,128)(2,1)S(1)}, bf16[3,128,128]{2,1,0:T(8,128)(2,1)S(1)}, u32[]{:S(2)}, u32[]{:S(2)}) collective-permute-start(bf16[3,128,128]{2,1,0:T(8,128)(2,1)S(1)} %collective-permute-done.12.refs_2_), channel_id=1, source_target_pairs={{0,1},{1,0},{2,3},{3,2},{4,5},{5,4},{6,7},{7,6},{8,9},{9,8},{10,11... | collective-permute-start | bytes 294920 | tf_op jit(solution)/shard_map/ppermute | solution.py:325
  68.6 1.3 %collective-permute-start.17 = (bf16[3,128,128]{2,1,0:T(8,128)(2,1)S(1)}, bf16[3,128,128]{2,1,0:T(8,128)(2,1)S(1)}, u32[]{:S(2)}, u32[]{:S(2)}) collective-permute-start(bf16[3,128,128]{2,1,0:T(8,128)(2,1)S(1)} %collective-permute-done.13.refs_3_), channel_id=1, source_target_pairs={{0,1},{1,0},{2,3},{3,2},{4,5},{5,4},{6,7},{7,6},{8,9},{9,8},{10,11... | collective-permute-start | bytes 294920 | tf_op jit(solution)/shard_map/ppermute | solution.py:325

commit v30 on v26

--- a/solution.py
+++ b/solution.py
@@ -23,10 +23,10 @@
     pass
 
 
-def hand_on(x, *after):
+def hand_on(x, *after, spec=ANY):
     return pl.pallas_call(
         hand_kernel,
-        in_specs=[ANY] * (1 + len(after)),
+        in_specs=[ANY] + [spec] * len(after),
         out_specs=ANY,
         out_shape=jax.ShapeDtypeStruct(x.shape, x.dtype),
         input_output_aliases={0: 0},
@@ -72,37 +72,42 @@
     return g * pair + y
 
 
+def named_rows(ids, shape):
+    lane = lax.broadcasted_iota(jnp.int32, shape, 1)
+    named = jnp.zeros(shape, jnp.float32)
+    for b in range(ids.shape[0]):
+        named = jnp.where(lane == b, ids[b].astype(jnp.float32), named)
+    return named
+
+
 def spread_kernel(groups, pair, lengths, ids, tok, *refs):
     held, in_sems, out_sems = refs[-3:]
     outs = refs[:-3]
     blocks = lengths.shape[0]
-    shares, tall, step = held.shape
+    sent, tall, step = held.shape
+    shares = sent + 1
     rows = tok.shape[0]
     block = rows // blocks
     mates = [pl.multiple_of(mate_at(k, 1, groups, pair) * step, LANES) for k in range(shares)]
-    order = list(range(1, shares)) + [0]
+    order = list(range(1, shares))
 
     def read(k, b):
         here = pl.ds(b * block, block)
-        return pltpu.make_async_copy(tok.at[here, pl.ds(mates[k], step)], held.at[k, here, :], in_sems.at[k, b])
+        return pltpu.make_async_copy(tok.at[here, pl.ds(mates[k], step)], held.at[k - 1, here, :], in_sems.at[k - 1, b])
 
     for k in order:
         for b in range(blocks):
             read(k, b).start()
-    lane = lax.broadcasted_iota(jnp.int32, (tall - rows, step), 1)
-    named = jnp.zeros((tall - rows, step), jnp.float32)
-    for b in range(blocks):
-        named = jnp.where(lane == b, ids[b].astype(jnp.float32), named)
-    named = named.astype(held.dtype)
+    named = named_rows(ids, (tall - rows, step)).astype(held.dtype)
     writes = []
 
     def write(k, b):
         here = pl.ds(b * block, block if b < blocks else tall - rows)
-        writes.append(pltpu.make_async_copy(held.at[k, here, :], outs[k].at[here, :], out_sems.at[k, b]))
+        writes.append(pltpu.make_async_copy(held.at[k - 1, here, :], outs[k - 1].at[here, :], out_sems.at[k - 1, b]))
         writes[-1].start()
 
     for k in order:
-        held[k, rows:, :] = named
+        held[k - 1, rows:, :] = named
         write(k, blocks)
         for b in range(blocks):
             read(k, b).wait()
@@ -111,8 +116,8 @@
             def _():
                 here = slice(b * block, (b + 1) * block)
                 row = lax.broadcasted_iota(jnp.int32, (block, step), 0)
-                part = held[k, here, :]
-                held[k, here, :] = jnp.where(row < lengths[b], part, jnp.zeros_like(part))
+                part = held[k - 1, here, :]
+                held[k - 1, here, :] = jnp.where(row < lengths[b], part, jnp.zeros_like(part))
 
             write(k, b)
     for one in writes:
@@ -126,19 +131,19 @@
     return pl.pallas_call(
         functools.partial(spread_kernel, groups, pair),
         in_specs=[SMEM, SMEM, ANY],
-        out_specs=[ANY] * shares,
-        out_shape=[jax.ShapeDtypeStruct(shape, tokens.dtype)] * shares,
+        out_specs=[ANY] * (shares - 1),
+        out_shape=[jax.ShapeDtypeStruct(shape, tokens.dtype)] * (shares - 1),
         scratch_shapes=[
-            pltpu.VMEM((shares,) + shape, tokens.dtype),
-            pltpu.SemaphoreType.DMA((shares, lengths.shape[0])),
-            pltpu.SemaphoreType.DMA((shares, lengths.shape[0] + 1)),
+            pltpu.VMEM((shares - 1,) + shape, tokens.dtype),
+            pltpu.SemaphoreType.DMA((shares - 1, lengths.shape[0])),
+            pltpu.SemaphoreType.DMA((shares - 1, lengths.shape[0] + 1)),
         ],
         compiler_params=FULL,
         name="spread",
     )(lengths, ids, tokens)
 
 
-def base_kernel(sides, lengths, tok, key, mine, other, flag_ref, tok_held, key_held, total, tok_sems, key_sems):
+def base_kernel(sides, groups, pair, lengths, ids, tok, key, mine, other, flag_ref, slab, tok_held, key_held, total, tok_sems, key_sems):
     depth, rows = key.shape[0], tok.shape[0]
     chunk = depth // key_sems.shape[0]
     steps = tok_sems.shape[0]
@@ -173,6 +178,14 @@
     blocks = lengths.shape[0]
     wide = mine.shape[1]
     block = rows // blocks
+    feats = slab.shape[1]
+    own = pl.ds(pl.multiple_of(mate_at(0, 1, groups, pair) * feats, LANES), feats)
+    row = lax.broadcasted_iota(jnp.int32, (block, feats), 0)
+    for b in range(blocks):
+        here = slice(b * block, (b + 1) * block)
+        some = tok_held[here, own]
+        slab[here, :] = jnp.where(row < lengths[b], some, jnp.zeros_like(some))
+    slab[rows:, :] = named_rows(ids, (slab.shape[0] - rows, feats)).astype(slab.dtype)
     row = lax.broadcasted_iota(jnp.int32, (block, wide), 0)
     t = lax.axis_index("tensor")
     for out, side in ((mine, t), (other, lax.rem(t + 1, sides))):
@@ -182,16 +195,21 @@
             out[here, :] = jnp.where(row < lengths[b], total[here, columns], 0.0)
 
 
-def base_halves(tokens, base_key, sides, lengths):
+def base_halves(tokens, base_key, sides, lengths, ids, groups, pair):
     rows, depth = tokens.shape
     features = base_key.shape[1]
     half = jax.ShapeDtypeStruct((rows, features // sides), jnp.float32)
     steps, chunks = depth // 1024, depth // 256
     return pl.pallas_call(
-        functools.partial(base_kernel, sides),
-        in_specs=[SMEM, ANY, ANY],
-        out_specs=[VMEM] * 3,
-        out_shape=[half, half, jax.ShapeDtypeStruct((8, LANES), jnp.float32)],
+        functools.partial(base_kernel, sides, groups, pair),
+        in_specs=[SMEM, SMEM, ANY, ANY],
+        out_specs=[VMEM] * 4,
+        out_shape=[
+            half,
+            half,
+            jax.ShapeDtypeStruct((8, LANES), jnp.float32),
+            jax.ShapeDtypeStruct((rows + 16, depth // (groups * pair)), tokens.dtype),
+        ],
         scratch_shapes=[
             pltpu.VMEM(tokens.shape, tokens.dtype),
             pltpu.VMEM(base_key.shape, base_key.dtype),
@@ -202,7 +220,7 @@
         cost_estimate=pl.CostEstimate(flops=0, bytes_accessed=0, transcendentals=0),
         compiler_params=FULL,
         name="base",
-    )(lengths, tokens, base_key)
+    )(lengths, ids, tokens, base_key)
 
 
 def collect_kernel(*refs):
@@ -353,14 +371,16 @@
         return [held[k] for k in range(ring)]
 
     packed = pack(jnp.swapaxes(adapter_down, 1, 2), adapter_up, shares, pair)
-    slabs = spread(tokens, lengths, adapter_ids.reshape(-1), groups, pair)
+    ids = adapter_ids.reshape(-1)
+    slabs = spread(tokens, lengths, ids, groups, pair)
     swapped = [
         lax.ppermute(packed[pair - w], "pair", [(a, (a - w) % pair) for a in range(pair)]) for w in range(1, pair)
     ]
     firsts = [first_hops(piece) for piece in [packed[0]] + swapped]
-    toks = [slabs[0]] + [in_plane(slabs[k], k // pair, k % pair) for k in range(1, shares)]
-
-    base_mine, base_out, flag = base_halves(tokens, base_key, sides, lengths)
+    toks = [in_plane(slabs[k - 1], k // pair, k % pair) for k in range(1, shares)]
+
+    base_mine, base_out, flag, own_slab = base_halves(tokens, base_key, sides, lengths, ids, groups, pair)
+    toks = [own_slab] + toks
     pieces = [
         more_hops(held, way, flag)
         for way, held in enumerate(firsts)
@@ -372,7 +392,7 @@
     *parts, ready = rank_parts(owner_slot, toks, held, late, ring, pair, rows, blocks)
     mine = [parts[0]] + [in_plane(parts[k], -(k // pair), -(k % pair)) for k in range(1, shares)]
     theirs = [across(part) for part in mine]
-    base_in = across(hand_on(base_out, ready))
+    base_in = across(hand_on(base_out, ready, spec=VMEM))
     return final(mine, theirs, [base_mine, base_in], groups, pair, tokens.dtype)
 
 

time: 65.9 us -> 65.5 us (level)
  waiting for transfers between devices: 20.7 us -> 19.9 us
    pallas_call x4, Pallas kernels: 7.86 us -> 8.74 us  [the longest x1 8.05 us: base_halves(): pl.pallas_call(functools.partial(base_kernel, sides, groups, pair), in_sp...]
    pallas_call x1, Pallas kernels: 2.38 us -> 1.67 us  [rank_parts(): pl.pallas_call(functools.partial(rank_kernel, ring, pair, rows, shares),...]
where the time goes in v30:
time: 65.5 us; the launch traced here: 65.1 us
  starting transfers between devices  20.2 us (31%)
  waiting for transfers between devices  19.9 us (30%)
  Pallas kernels  17.9 us (27%)
  local copies, waits for them, and re-layouts  6.87 us (10%)
    ppermute x6, waiting for transfers between devices, in_plane(): return lax.ppermute(x, PLANE, pairs)  10.1 us
    ppermute x6, starting transfers between devices, along(): lax.ppermute(x, 'ring', [(a, (a + step) % ring) for a in range(ring)])  9.83 us
    ppermute x6, waiting for transfers between devices, along(): lax.ppermute(x, 'ring', [(a, (a + step) % ring) for a in range(ring)])  8.51 us
    pallas_call x1, Pallas kernels, base_halves(): pl.pallas_call(functools.partial(base_kernel, sides, groups, pair), in_sp...  8.05 us
    ppermute x6, starting transfers between devices, in_plane(): return lax.ppermute(x, PLANE, pairs)  7.04 us
    unnamed x30, local copies, waits for them, and re-layouts  6.87 us
    pallas_call x1, Pallas kernels, spread(): pl.pallas_call(functools.partial(spread_kernel, groups, pair), in_specs=[...  3.29 us
    ppermute x1, starting transfers between devices, body(): lax.ppermute(packed[pair - w], 'pair', [(a, (a - w) % pair) for a in rang...  3.03 us
  transfers between devices with their start and end apart: 18, of which 9 were waited for; matrix products, arithmetic and copies ran while one was open for 0% of the time, Pallas kernels for 19%

profile of v30, /device:TPU:0, one launch (start us, length us, event | category | flops | bytes accessed | tf_op | source)
XLA Modules:
  0.0 65.1 jit_solution(17805986788023989413)
XLA Ops:
  0.0 1.9 %pack.1 = (bf16[2,64,1152]{2,1,0:T(8,128)(2,1)}, bf16[2,64,1152]{2,1,0:T(8,128)(2,1)}) custom-call(bf16[2,64,4096]{2,1,0:T(8,128)(2,1)} %bitcast.2, bf16[2,64,512]{2,1,0:T(8,128)(2,1)} %up.1), custom_call_target="tpu_custom_call" | custom-call | tf_op jit(solution)/shard_map/pack/pallas_call | solution.py:57
  1.9 3.0 %collective-permute-start.2 = (bf16[2,64,1152]{2,1,0:T(8,128)(2,1)}, bf16[2,64,1152]{2,1,0:T(8,128)(2,1)}, u32[]{:S(2)}, u32[]{:S(2)}) collective-permute-start(bf16[2,64,1152]{2,1,0:T(8,128)(2,1)} %get-tuple-element.23), channel_id=1, source_target_pairs={{0,2},{2,0},{1,3},{3,1},{4,6},{6,4},{5,7},{7,5},{8,10},{10,8},{9,1... | collective-permute-start | bytes 884744 | tf_op jit(solution)/shard_map/ppermute | solution.py:377
  5.0 1.6 %collective-permute-start.1 = (bf16[2,64,1152]{2,1,0:T(8,128)(2,1)}, bf16[2,64,1152]{2,1,0:T(8,128)(2,1)S(1)}, u32[]{:S(2)}, u32[]{:S(2)}) collective-permute-start(bf16[2,64,1152]{2,1,0:T(8,128)(2,1)} %get-tuple-element.21.refs_0_), channel_id=1, source_target_pairs={{0,4},{4,8},{8,12},{12,0},{1,5},{5,9},{9,13},{13,1},{2,6},{6,10},{... | collective-permute-start | bytes 884744 | tf_op jit(solution)/shard_map/ppermute | solution.py:349
  6.5 2.2 %collective-permute-start = (bf16[2,64,1152]{2,1,0:T(8,128)(2,1)}, bf16[2,64,1152]{2,1,0:T(8,128)(2,1)S(1)}, u32[]{:S(2)}, u32[]{:S(2)}) collective-permute-start(bf16[2,64,1152]{2,1,0:T(8,128)(2,1)} %get-tuple-element.21.refs_0_), channel_id=1, source_target_pairs={{0,12},{4,0},{8,4},{12,8},{1,13},{5,1},{9,5},{13,9},{2,14},{6,2},{... | collective-permute-start | bytes 884744 | tf_op jit(solution)/shard_map/ppermute | solution.py:349
  8.8 3.3 %spread.1 = (bf16[400,1024]{1,0:T(8,128)(2,1)}, bf16[400,1024]{1,0:T(8,128)(2,1)}, bf16[400,1024]{1,0:T(8,128)(2,1)}) custom-call(s32[3]{0:T(128)} %lengths.3, s32[3]{0:T(128)} %bitcast.3, bf16[384,4096]{1,0:T(8,128)(2,1)} %tok.3), custom_call_target="tpu_custom_call" | custom-call | tf_op jit(solution)/shard_map/spread/pallas_call | solution.py:131
  12.1 0.4 collective-permute-start.7
  12.4 1.7 %collective-permute-start.8 = (bf16[400,1024]{1,0:T(8,128)(2,1)}, bf16[400,1024]{1,0:T(8,128)(2,1)S(1)}, u32[]{:S(2)}, u32[]{:S(2)}) collective-permute-start(bf16[400,1024]{1,0:T(8,128)(2,1)} %get-tuple-element.26), channel_id=1, source_target_pairs={{0,16},{2,18},{16,0},{18,2},{1,17},{3,19},{17,1},{19,3},{4,20},{6,... | collective-permute-start | bytes 2457608 | tf_op jit(solution)/shard_map/ppermute | solution.py:359
  14.2 0.0 collective-permute-done.2.refs_3_
  14.2 1.5 %collective-permute-start.9 = (bf16[400,1024]{1,0:T(8,128)(2,1)}, bf16[400,1024]{1,0:T(8,128)(2,1)S(1)}, u32[]{:S(2)}, u32[]{:S(2)}) collective-permute-start(bf16[400,1024]{1,0:T(8,128)(2,1)} %get-tuple-element.27), channel_id=1, source_target_pairs={{0,18},{2,16},{16,2},{18,0},{1,19},{3,17},{17,3},{19,1},{4,22},{6,... | collective-permute-start | bytes 2457608 | tf_op jit(solution)/shard_map/ppermute | solution.py:359
  15.7 1.3 %collective-permute-done.1.refs_0_ = bf16[2,64,1152]{2,1,0:T(8,128)(2,1)S(1)} collective-permute-done((bf16[2,64,1152]{2,1,0:T(8,128)(2,1)}, bf16[2,64,1152]{2,1,0:T(8,128)(2,1)S(1)}, u32[]{:S(2)}, u32[]{:S(2)}) %collective-permute-start.1) | collective-permute-done | bytes 294944 | tf_op jit(solution)/shard_map/ppermute | solution.py:349
  17.0 0.7 %collective-permute-start.4 = (bf16[2,64,1152]{2,1,0:T(8,128)(2,1)}, bf16[2,64,1152]{2,1,0:T(8,128)(2,1)S(1)}, u32[]{:S(2)}, u32[]{:S(2)}) collective-permute-start(bf16[2,64,1152]{2,1,0:T(8,128)(2,1)} %collective-permute-done.2.refs_3_), channel_id=1, source_target_pairs={{0,4},{4,8},{8,12},{12,0},{1,5},{5,9},{9,13},{13,1},{2,6},{6,10},{... | collective-permute-start | bytes 884744 | tf_op jit(solution)/shard_map/ppermute | solution.py:349
  17.7 4.4 %collective-permute-done.refs_1_ = bf16[2,64,1152]{2,1,0:T(8,128)(2,1)S(1)} collective-permute-done((bf16[2,64,1152]{2,1,0:T(8,128)(2,1)}, bf16[2,64,1152]{2,1,0:T(8,128)(2,1)S(1)}, u32[]{:S(2)}, u32[]{:S(2)}) %collective-permute-start) | collective-permute-done | bytes 294944 | tf_op jit(solution)/shard_map/ppermute | solution.py:349
  22.1 2.8 %collective-permute-start.3 = (bf16[2,64,1152]{2,1,0:T(8,128)(2,1)}, bf16[2,64,1152]{2,1,0:T(8,128)(2,1)S(1)}, u32[]{:S(2)}, u32[]{:S(2)}) collective-permute-start(bf16[2,64,1152]{2,1,0:T(8,128)(2,1)} %collective-permute-done.2.refs_3_), channel_id=1, source_target_pairs={{0,12},{4,0},{8,4},{12,8},{1,13},{5,1},{9,5},{13,9},{2,14},{6,2},{... | collective-permute-start | bytes 884744 | tf_op jit(solution)/shard_map/ppermute | solution.py:349
  24.9 8.0 %base.1 = (f32[384,512]{1,0:T(8,128)}, f32[384,512]{1,0:T(8,128)}, f32[8,128]{1,0:T(8,128)}, bf16[400,1024]{1,0:T(8,128)(2,1)}) custom-call(s32[3]{0:T(128)} %lengths.3, s32[3]{0:T(128)} %bitcast.4, bf16[384,4096]{1,0:T(8,128)(2,1)} %tok.3, bf16[4096,1024]{1,0:T(8,128)(2,1)} %key.1), custom_call_target="tpu_custom_call" | custom-call | tf_op jit(solution)/shard_map/base/pallas_call | solution.py:203
  32.9 0.0 copy-start.14
  33.0 0.1 collective-permute-start.5
  33.0 1.5 %collective-permute-done.3.refs_0_ = bf16[2,64,1152]{2,1,0:T(8,128)(2,1)S(1)} collective-permute-done((bf16[2,64,1152]{2,1,0:T(8,128)(2,1)}, bf16[2,64,1152]{2,1,0:T(8,128)(2,1)S(1)}, u32[]{:S(2)}, u32[]{:S(2)}) %collective-permute-start.3) | collective-permute-done | bytes 294944 | tf_op jit(solution)/shard_map/ppermute | solution.py:349
  34.5 0.7 %copy-done.6 = bf16[2,64,1152]{2,1,0:T(8,128)(2,1)} copy-done((bf16[2,64,1152]{2,1,0:T(8,128)(2,1)}, bf16[2,64,1152]{2,1,0:T(8,128)(2,1)S(1)}, u32[]{:S(2)}) %copy-start.6) | copy-done | bytes 294936
  35.2 2.4 %collective-permute-start.6 = (bf16[2,64,1152]{2,1,0:T(8,128)(2,1)}, bf16[2,64,1152]{2,1,0:T(8,128)(2,1)S(1)}, u32[]{:S(2)}, u32[]{:S(2)}) collective-permute-start(bf16[2,64,1152]{2,1,0:T(8,128)(2,1)} %hand.4.refs_4_), channel_id=1, source_target_pairs={{0,12},{4,0},{8,4},{12,8},{1,13},{5,1},{9,5},{13,9},{2,14},{6,2},{... | collective-permute-start | bytes 884744 | tf_op jit(solution)/shard_map/ppermute | solution.py:349
  37.7 1.0 %copy-done.1 = bf16[2,64,1152]{2,1,0:T(8,128)(2,1)S(1)} copy-done((bf16[2,64,1152]{2,1,0:T(8,128)(2,1)S(1)}, bf16[2,64,1152]{2,1,0:T(8,128)(2,1)}, u32[]{:S(2)}) %copy-start.1) | copy-done | bytes 294936
  38.6 1.0 %copy-done.3 = bf16[2,64,1152]{2,1,0:T(8,128)(2,1)S(1)} copy-done((bf16[2,64,1152]{2,1,0:T(8,128)(2,1)S(1)}, bf16[2,64,1152]{2,1,0:T(8,128)(2,1)}, u32[]{:S(2)}) %copy-start.3) | copy-done | bytes 294936
  39.6 1.0 %copy-done.5 = bf16[2,64,1152]{2,1,0:T(8,128)(2,1)S(1)} copy-done((bf16[2,64,1152]{2,1,0:T(8,128)(2,1)S(1)}, bf16[2,64,1152]{2,1,0:T(8,128)(2,1)}, u32[]{:S(2)}) %copy-start.5) | copy-done | bytes 294936
  40.6 1.0 %copy-done.7 = bf16[2,64,1152]{2,1,0:T(8,128)(2,1)S(1)} copy-done((bf16[2,64,1152]{2,1,0:T(8,128)(2,1)S(1)}, bf16[2,64,1152]{2,1,0:T(8,128)(2,1)}, u32[]{:S(2)}) %copy-start.7) | copy-done | bytes 294936
  41.5 1.3 %collect.1.held = bf16[12,64,1152]{2,1,0:T(8,128)(2,1)S(1)} custom-call(bf16[2,64,1152]{2,1,0:T(8,128)(2,1)S(1)} %copy-done.10, bf16[2,64,1152]{2,1,0:T(8,128)(2,1)S(1)} %copy-done.1, bf16[2,64,1152]{2,1,0:T(8,128)(2,1)S(1)} %copy-done.3, bf16[2,64,1152]{2,1,0:T(8,128)(2,1)} %collective-permute-done.2.refs_3_, bf16[2,64,1152]{2,1,0:T(8,128)(2,1)S(1)} %copy-done.7, ...), custom_call_target="tpu_custom_call" | custom-call | tf_op jit(solution)/shard_map/collect/pallas_call | solution.py:240
  42.8 1.4 %collective-permute-done.5.refs_0_ = bf16[2,64,1152]{2,1,0:T(8,128)(2,1)S(1)} collective-permute-done((bf16[2,64,1152]{2,1,0:T(8,128)(2,1)}, bf16[2,64,1152]{2,1,0:T(8,128)(2,1)S(1)}, u32[]{:S(2)}, u32[]{:S(2)}) %collective-permute-start.5) | collective-permute-done | bytes 294944 | tf_op jit(solution)/shard_map/ppermute | solution.py:349
  44.2 0.7 %copy-done.11 = bf16[2,64,1152]{2,1,0:T(8,128)(2,1)} copy-done((bf16[2,64,1152]{2,1,0:T(8,128)(2,1)}, bf16[2,64,1152]{2,1,0:T(8,128)(2,1)S(1)}, u32[]{:S(2)}) %copy-start.11) | copy-done | bytes 294936
  44.9 0.0 collective-permute-done.7.refs_3_
  44.9 0.0 collective-permute-done.8.refs_4_
  44.9 5.4 %collective-permute-done.9.refs_5_ = bf16[400,1024]{1,0:T(8,128)(2,1)S(1)} collective-permute-done((bf16[400,1024]{1,0:T(8,128)(2,1)}, bf16[400,1024]{1,0:T(8,128)(2,1)S(1)}, u32[]{:S(2)}, u32[]{:S(2)}) %collective-permute-start.9) | collective-permute-done | bytes 819232 | tf_op jit(solution)/shard_map/ppermute | solution.py:359
  50.3 0.0 collective-permute-done.6.refs_1_
  50.3 0.0 copy-start.12
  50.3 1.0 %copy-done.12 = bf16[2,64,1152]{2,1,0:T(8,128)(2,1)S(1)} copy-done((bf16[2,64,1152]{2,1,0:T(8,128)(2,1)S(1)}, bf16[2,64,1152]{2,1,0:T(8,128)(2,1)}, u32[]{:S(2)}) %copy-start.12) | copy-done | bytes 294936
  51.3 1.7 %rank.1 = (bf16[3,128,128]{2,1,0:T(8,128)(2,1)S(1)}, bf16[3,128,128]{2,1,0:T(8,128)(2,1)S(1)}, bf16[3,128,128]{2,1,0:T(8,128)(2,1)S(1)}, bf16[3,128,128]{2,1,0:T(8,128)(2,1)S(1)}, f32[8,128]{1,0:T(8,128)S(1)}) custom-call(s32[16]{0:T(128)S(1)} %copy-done.14, bf16[12,64,1152]{2,1,0:T(8,128)(2,1)S(1)} %collect.1.held, bf16[2,64,1152]{2,1,0:T(8,128)(2,1)S(1)} %copy-done.12, ...), custom_call_target="tpu_custom_call" | custom-call | tf_op jit(solution)/shard_map/rank/pallas_call | solution.py:293
  53.0 0.0 copy-start.13
  53.0 0.6 copy-done.13
  53.6 0.7 %hand.5 = f32[384,512]{1,0:T(8,128)} custom-call(f32[384,512]{1,0:T(8,128)} %get-tuple-element.20.refs_0_, f32[8,128]{1,0:T(8,128)} %copy-done.13), custom_call_target="tpu_custom_call", output_to_operand_aliasing={{}: (0, {})} | custom-call | tf_op jit(solution)/shard_map/hand/pallas_call | solution.py:27
  54.3 0.0 collective-permute-start.10
  54.3 0.5 collective-permute-start.11
  54.8 1.5 %collective-permute-start.12 = (bf16[3,128,128]{2,1,0:T(8,128)(2,1)S(1)}, bf16[3,128,128]{2,1,0:T(8,128)(2,1)S(1)}, u32[]{:S(2)}, u32[]{:S(2)}) collective-permute-start(bf16[3,128,128]{2,1,0:T(8,128)(2,1)S(1)} %get-tuple-element.31), channel_id=1, source_target_pairs={{0,16},{2,18},{16,0},{18,2},{1,17},{3,19},{17,1},{19,3},{4,20},{6,... | collective-permute-start | bytes 294920 | tf_op jit(solution)/shard_map/ppermute | solution.py:359
  56.3 1.5 %collective-permute-start.13 = (bf16[3,128,128]{2,1,0:T(8,128)(2,1)S(1)}, bf16[3,128,128]{2,1,0:T(8,128)(2,1)S(1)}, u32[]{:S(2)}, u32[]{:S(2)}) collective-permute-start(bf16[3,128,128]{2,1,0:T(8,128)(2,1)S(1)} %get-tuple-element.32), channel_id=1, source_target_pairs={{0,18},{2,16},{16,2},{18,0},{1,19},{3,17},{17,3},{19,1},{4,22},{6,... | collective-permute-start | bytes 294920 | tf_op jit(solution)/shard_map/ppermute | solution.py:359
  57.7 1.7 %collective-permute-done.11.refs_1_ = bf16[3,128,128]{2,1,0:T(8,128)(2,1)S(1)} collective-permute-done((bf16[3,128,128]{2,1,0:T(8,128)(2,1)S(1)}, bf16[3,128,128]{2,1,0:T(8,128)(2,1)S(1)}, u32[]{:S(2)}, u32[]{:S(2)}) %collective-permute-start.11) | collective-permute-done | bytes 98336 | tf_op jit(solution)/shard_map/ppermute | solution.py:359
  59.5 0.0 collective-permute-start.15
  59.5 0.2 collective-permute-done.12.refs_2_
  59.7 0.3 collective-permute-start.16
  60.0 2.8 %collective-permute-done.13.refs_3_ = bf16[3,128,128]{2,1,0:T(8,128)(2,1)S(1)} collective-permute-done((bf16[3,128,128]{2,1,0:T(8,128)(2,1)S(1)}, bf16[3,128,128]{2,1,0:T(8,128)(2,1)S(1)}, u32[]{:S(2)}, u32[]{:S(2)}) %collective-permute-start.13) | collective-permute-done | bytes 98336 | tf_op jit(solution)/shard_map/ppermute | solution.py:359
  62.8 0.0 collective-permute-done.15.refs_5_
  62.8 1.3 %collective-permute-done.17.refs_7_ = bf16[3,128,128]{2,1,0:T(8,128)(2,1)S(1)} collective-permute-done((bf16[3,128,128]{2,1,0:T(8,128)(2,1)S(1)}, bf16[3,128,128]{2,1,0:T(8,128)(2,1)S(1)}, u32[]{:S(2)}, u32[]{:S(2)}) %collective-permute-start.17) | collective-permute-done | bytes 98336 | tf_op jit(solution)/shard_map/ppermute | solution.py:346
  64.1 1.1 %final.1 = bf16[384,512]{1,0:T(8,128)(2,1)} custom-call(f32[384,512]{1,0:T(8,128)S(1)} %copy-done.9, f32[384,512]{1,0:T(8,128)S(1)} %collective-permute-done.10.base_b, bf16[3,128,128]{2,1,0:T(8,128)(2,1)S(1)} %get-tuple-element.29.refs_0_, bf16[3,128,128]{2,1,0:T(8,128)(2,1)S(1)} %collective-permute-done.11.refs_1_, ...), custom_call_target="tpu_custom_call" | custom-call | tf_op jit(solution)/shard_map/final/pallas_call | solution.py:327
  (27 shorter events, 0.1 us)
Async XLA Ops:
  1.9 12.2 %collective-permute-start.2 = (bf16[2,64,1152]{2,1,0:T(8,128)(2,1)}, bf16[2,64,1152]{2,1,0:T(8,128)(2,1)}, u32[]{:S(2)}, u32[]{:S(2)}) collective-permute-start(bf16[2,64,1152]{2,1,0:T(8,128)(2,1)} %get-tuple-element.23), channel_id=1, source_target_pairs={{0,2},{2,0},{1,3},{3,1},{4,6},{6,4},{5,7},{7,5},{8,10},{10,8},{9,1... | collective-permute-start | bytes 884744 | tf_op jit(solution)/shard_map/ppermute | solution.py:377
  5.0 12.0 %collective-permute-start.1 = (bf16[2,64,1152]{2,1,0:T(8,128)(2,1)}, bf16[2,64,1152]{2,1,0:T(8,128)(2,1)S(1)}, u32[]{:S(2)}, u32[]{:S(2)}) collective-permute-start(bf16[2,64,1152]{2,1,0:T(8,128)(2,1)} %get-tuple-element.21.refs_0_), channel_id=1, source_target_pairs={{0,4},{4,8},{8,12},{12,0},{1,5},{5,9},{9,13},{13,1},{2,6},{6,10},{... | collective-permute-start | bytes 884744 | tf_op jit(solution)/shard_map/ppermute | solution.py:349
  6.5 15.5 %collective-permute-start = (bf16[2,64,1152]{2,1,0:T(8,128)(2,1)}, bf16[2,64,1152]{2,1,0:T(8,128)(2,1)S(1)}, u32[]{:S(2)}, u32[]{:S(2)}) collective-permute-start(bf16[2,64,1152]{2,1,0:T(8,128)(2,1)} %get-tuple-element.21.refs_0_), channel_id=1, source_target_pairs={{0,12},{4,0},{8,4},{12,8},{1,13},{5,1},{9,5},{13,9},{2,14},{6,2},{... | collective-permute-start | bytes 884744 | tf_op jit(solution)/shard_map/ppermute | solution.py:349
  12.1 32.8 %collective-permute-start.7 = (bf16[400,1024]{1,0:T(8,128)(2,1)}, bf16[400,1024]{1,0:T(8,128)(2,1)S(1)}, u32[]{:S(2)}, u32[]{:S(2)}) collective-permute-start(bf16[400,1024]{1,0:T(8,128)(2,1)} %get-tuple-element.25), channel_id=1, source_target_pairs={{0,2},{2,0},{16,18},{18,16},{1,3},{3,1},{17,19},{19,17},{4,6},{6,4... | collective-permute-start | bytes 2457608 | tf_op jit(solution)/shard_map/ppermute | solution.py:359
  12.4 32.4 %collective-permute-start.8 = (bf16[400,1024]{1,0:T(8,128)(2,1)}, bf16[400,1024]{1,0:T(8,128)(2,1)S(1)}, u32[]{:S(2)}, u32[]{:S(2)}) collective-permute-start(bf16[400,1024]{1,0:T(8,128)(2,1)} %get-tuple-element.26), channel_id=1, source_target_pairs={{0,16},{2,18},{16,0},{18,2},{1,17},{3,19},{17,1},{19,3},{4,20},{6,... | collective-permute-start | bytes 2457608 | tf_op jit(solution)/shard_map/ppermute | solution.py:359
  14.2 23.5 %copy-start.10 = (bf16[2,64,1152]{2,1,0:T(8,128)(2,1)S(1)}, bf16[2,64,1152]{2,1,0:T(8,128)(2,1)}, u32[]{:S(2)}) copy-start(bf16[2,64,1152]{2,1,0:T(8,128)(2,1)} %get-tuple-element.21.refs_0_) | copy-start | bytes 884740
  14.2 36.1 %collective-permute-start.9 = (bf16[400,1024]{1,0:T(8,128)(2,1)}, bf16[400,1024]{1,0:T(8,128)(2,1)S(1)}, u32[]{:S(2)}, u32[]{:S(2)}) collective-permute-start(bf16[400,1024]{1,0:T(8,128)(2,1)} %get-tuple-element.27), channel_id=1, source_target_pairs={{0,18},{2,16},{16,2},{18,0},{1,19},{3,17},{17,3},{19,1},{4,22},{6,... | collective-permute-start | bytes 2457608 | tf_op jit(solution)/shard_map/ppermute | solution.py:359
  16.9 16.0 %copy-start.2 = (bf16[2,64,1152]{2,1,0:T(8,128)(2,1)}, bf16[2,64,1152]{2,1,0:T(8,128)(2,1)S(1)}, u32[]{:S(2)}) copy-start(bf16[2,64,1152]{2,1,0:T(8,128)(2,1)S(1)} %collective-permute-done.1.refs_0_) | copy-start | bytes 884740
  17.0 16.0 %collective-permute-start.4 = (bf16[2,64,1152]{2,1,0:T(8,128)(2,1)}, bf16[2,64,1152]{2,1,0:T(8,128)(2,1)S(1)}, u32[]{:S(2)}, u32[]{:S(2)}) collective-permute-start(bf16[2,64,1152]{2,1,0:T(8,128)(2,1)} %collective-permute-done.2.refs_3_), channel_id=1, source_target_pairs={{0,4},{4,8},{8,12},{12,0},{1,5},{5,9},{9,13},{13,1},{2,6},{6,10},{... | collective-permute-start | bytes 884744 | tf_op jit(solution)/shard_map/ppermute | solution.py:349
  22.1 10.9 %copy-start = (bf16[2,64,1152]{2,1,0:T(8,128)(2,1)}, bf16[2,64,1152]{2,1,0:T(8,128)(2,1)S(1)}, u32[]{:S(2)}) copy-start(bf16[2,64,1152]{2,1,0:T(8,128)(2,1)S(1)} %collective-permute-done.refs_1_) | copy-start | bytes 884740
  22.1 12.5 %collective-permute-start.3 = (bf16[2,64,1152]{2,1,0:T(8,128)(2,1)}, bf16[2,64,1152]{2,1,0:T(8,128)(2,1)S(1)}, u32[]{:S(2)}, u32[]{:S(2)}) collective-permute-start(bf16[2,64,1152]{2,1,0:T(8,128)(2,1)} %collective-permute-done.2.refs_3_), channel_id=1, source_target_pairs={{0,12},{4,0},{8,4},{12,8},{1,13},{5,1},{9,5},{13,9},{2,14},{6,2},{... | collective-permute-start | bytes 884744 | tf_op jit(solution)/shard_map/ppermute | solution.py:349
  32.9 17.4 %copy-start.14 = (s32[16]{0:T(128)S(1)}, s32[16]{0:T(128)}, u32[]{:S(2)}) copy-start(s32[16]{0:T(128)} %owner.1) | copy-start | bytes 196
  33.0 1.5 %copy-start.4 = (bf16[2,64,1152]{2,1,0:T(8,128)(2,1)}, bf16[2,64,1152]{2,1,0:T(8,128)(2,1)S(1)}, u32[]{:S(2)}) copy-start(bf16[2,64,1152]{2,1,0:T(8,128)(2,1)S(1)} %collective-permute-done.4.refs_1_.refs_5_) | copy-start | bytes 884740
  33.0 11.2 %collective-permute-start.5 = (bf16[2,64,1152]{2,1,0:T(8,128)(2,1)}, bf16[2,64,1152]{2,1,0:T(8,128)(2,1)S(1)}, u32[]{:S(2)}, u32[]{:S(2)}) collective-permute-start(bf16[2,64,1152]{2,1,0:T(8,128)(2,1)} %hand.3.refs_2_), channel_id=1, source_target_pairs={{0,4},{4,8},{8,12},{12,0},{1,5},{5,9},{9,13},{13,1},{2,6},{6,10},{... | collective-permute-start | bytes 884744 | tf_op jit(solution)/shard_map/ppermute | solution.py:349
  34.5 0.7 %copy-start.6 = (bf16[2,64,1152]{2,1,0:T(8,128)(2,1)}, bf16[2,64,1152]{2,1,0:T(8,128)(2,1)S(1)}, u32[]{:S(2)}) copy-start(bf16[2,64,1152]{2,1,0:T(8,128)(2,1)S(1)} %collective-permute-done.3.refs_0_) | copy-start | bytes 884740
  35.2 15.1 %collective-permute-start.6 = (bf16[2,64,1152]{2,1,0:T(8,128)(2,1)}, bf16[2,64,1152]{2,1,0:T(8,128)(2,1)S(1)}, u32[]{:S(2)}, u32[]{:S(2)}) collective-permute-start(bf16[2,64,1152]{2,1,0:T(8,128)(2,1)} %hand.4.refs_4_), channel_id=1, source_target_pairs={{0,12},{4,0},{8,4},{12,8},{1,13},{5,1},{9,5},{13,9},{2,14},{6,2},{... | collective-permute-start | bytes 884744 | tf_op jit(solution)/shard_map/ppermute | solution.py:349
  37.7 1.0 %copy-start.1 = (bf16[2,64,1152]{2,1,0:T(8,128)(2,1)S(1)}, bf16[2,64,1152]{2,1,0:T(8,128)(2,1)}, u32[]{:S(2)}) copy-start(bf16[2,64,1152]{2,1,0:T(8,128)(2,1)} %copy-done) | copy-start | bytes 884740
  38.6 1.0 %copy-start.3 = (bf16[2,64,1152]{2,1,0:T(8,128)(2,1)S(1)}, bf16[2,64,1152]{2,1,0:T(8,128)(2,1)}, u32[]{:S(2)}) copy-start(bf16[2,64,1152]{2,1,0:T(8,128)(2,1)} %hand.3.refs_2_) | copy-start | bytes 884740
  39.6 1.0 %copy-start.5 = (bf16[2,64,1152]{2,1,0:T(8,128)(2,1)S(1)}, bf16[2,64,1152]{2,1,0:T(8,128)(2,1)}, u32[]{:S(2)}) copy-start(bf16[2,64,1152]{2,1,0:T(8,128)(2,1)} %copy-done.4) | copy-start | bytes 884740
  40.5 1.0 %copy-start.7 = (bf16[2,64,1152]{2,1,0:T(8,128)(2,1)S(1)}, bf16[2,64,1152]{2,1,0:T(8,128)(2,1)}, u32[]{:S(2)}) copy-start(bf16[2,64,1152]{2,1,0:T(8,128)(2,1)} %hand.4.refs_4_) | copy-start | bytes 884740
  41.5 8.8 %copy-start.8 = (bf16[400,1024]{1,0:T(8,128)(2,1)S(1)}, bf16[400,1024]{1,0:T(8,128)(2,1)}, u32[]{:S(2)}) copy-start(bf16[400,1024]{1,0:T(8,128)(2,1)} %get-tuple-element.24.refs_2_) | copy-start | bytes 2457604
  44.2 0.7 %copy-start.11 = (bf16[2,64,1152]{2,1,0:T(8,128)(2,1)}, bf16[2,64,1152]{2,1,0:T(8,128)(2,1)S(1)}, u32[]{:S(2)}) copy-start(bf16[2,64,1152]{2,1,0:T(8,128)(2,1)S(1)} %collective-permute-done.5.refs_0_) | copy-start | bytes 884740
  50.3 1.0 %copy-start.12 = (bf16[2,64,1152]{2,1,0:T(8,128)(2,1)S(1)}, bf16[2,64,1152]{2,1,0:T(8,128)(2,1)}, u32[]{:S(2)}) copy-start(bf16[2,64,1152]{2,1,0:T(8,128)(2,1)} %copy-done.11) | copy-start | bytes 884740
  51.3 12.8 %copy-start.9 = (f32[384,512]{1,0:T(8,128)S(1)}, f32[384,512]{1,0:T(8,128)}, u32[]{:S(2)}) copy-start(f32[384,512]{1,0:T(8,128)} %get-tuple-element.19.base_a) | copy-start | bytes 2359300
  53.0 0.6 copy-start.13
  54.3 9.8 %collective-permute-start.10 = (f32[384,512]{1,0:T(8,128)}, f32[384,512]{1,0:T(8,128)S(1)}, u32[]{:S(2)}, u32[]{:S(2)}) collective-permute-start(f32[384,512]{1,0:T(8,128)} %hand.5), channel_id=1, source_target_pairs={{0,1},{1,0},{2,3},{3,2},{4,5},{5,4},{6,7},{7,6},{8,9},{9,8},{10,11... | collective-permute-start | bytes 2359304 | tf_op jit(solution)/shard_map/ppermute | solution.py:346
  54.3 5.2 %collective-permute-start.11 = (bf16[3,128,128]{2,1,0:T(8,128)(2,1)S(1)}, bf16[3,128,128]{2,1,0:T(8,128)(2,1)S(1)}, u32[]{:S(2)}, u32[]{:S(2)}) collective-permute-start(bf16[3,128,128]{2,1,0:T(8,128)(2,1)S(1)} %get-tuple-element.30), channel_id=1, source_target_pairs={{0,2},{2,0},{16,18},{18,16},{1,3},{3,1},{17,19},{19,17},{4,6},{6,4... | collective-permute-start | bytes 294920 | tf_op jit(solution)/shard_map/ppermute | solution.py:359
  54.8 4.9 %collective-permute-start.12 = (bf16[3,128,128]{2,1,0:T(8,128)(2,1)S(1)}, bf16[3,128,128]{2,1,0:T(8,128)(2,1)S(1)}, u32[]{:S(2)}, u32[]{:S(2)}) collective-permute-start(bf16[3,128,128]{2,1,0:T(8,128)(2,1)S(1)} %get-tuple-element.31), channel_id=1, source_target_pairs={{0,16},{2,18},{16,0},{18,2},{1,17},{3,19},{17,1},{19,3},{4,20},{6,... | collective-permute-start | bytes 294920 | tf_op jit(solution)/shard_map/ppermute | solution.py:359
  56.3 6.5 %collective-permute-start.13 = (bf16[3,128,128]{2,1,0:T(8,128)(2,1)S(1)}, bf16[3,128,128]{2,1,0:T(8,128)(2,1)S(1)}, u32[]{:S(2)}, u32[]{:S(2)}) collective-permute-start(bf16[3,128,128]{2,1,0:T(8,128)(2,1)S(1)} %get-tuple-element.32), channel_id=1, source_target_pairs={{0,18},{2,16},{16,2},{18,0},{1,19},{3,17},{17,3},{19,1},{4,22},{6,... | collective-permute-start | bytes 294920 | tf_op jit(solution)/shard_map/ppermute | solution.py:359
  57.7 5.0 %collective-permute-start.14 = (bf16[3,128,128]{2,1,0:T(8,128)(2,1)S(1)}, bf16[3,128,128]{2,1,0:T(8,128)(2,1)S(1)}, u32[]{:S(2)}, u32[]{:S(2)}) collective-permute-start(bf16[3,128,128]{2,1,0:T(8,128)(2,1)S(1)} %get-tuple-element.29.refs_0_), channel_id=1, source_target_pairs={{0,1},{1,0},{2,3},{3,2},{4,5},{5,4},{6,7},{7,6},{8,9},{9,8},{10,11... | collective-permute-start | bytes 294920 | tf_op jit(solution)/shard_map/ppermute | solution.py:346
  59.5 3.3 %collective-permute-start.15 = (bf16[3,128,128]{2,1,0:T(8,128)(2,1)S(1)}, bf16[3,128,128]{2,1,0:T(8,128)(2,1)S(1)}, u32[]{:S(2)}, u32[]{:S(2)}) collective-permute-start(bf16[3,128,128]{2,1,0:T(8,128)(2,1)S(1)} %collective-permute-done.11.refs_1_), channel_id=1, source_target_pairs={{0,1},{1,0},{2,3},{3,2},{4,5},{5,4},{6,7},{7,6},{8,9},{9,8},{10,11... | collective-permute-start | bytes 294920 | tf_op jit(solution)/shard_map/ppermute | solution.py:346
  59.7 3.1 %collective-permute-start.16 = (bf16[3,128,128]{2,1,0:T(8,128)(2,1)S(1)}, bf16[3,128,128]{2,1,0:T(8,128)(2,1)S(1)}, u32[]{:S(2)}, u32[]{:S(2)}) collective-permute-start(bf16[3,128,128]{2,1,0:T(8,128)(2,1)S(1)} %collective-permute-done.12.refs_2_), channel_id=1, source_target_pairs={{0,1},{1,0},{2,3},{3,2},{4,5},{5,4},{6,7},{7,6},{8,9},{9,8},{10,11... | collective-permute-start | bytes 294920 | tf_op jit(solution)/shard_map/ppermute | solution.py:346
  62.8 1.3 %collective-permute-start.17 = (bf16[3,128,128]{2,1,0:T(8,128)(2,1)S(1)}, bf16[3,128,128]{2,1,0:T(8,128)(2,1)S(1)}, u32[]{:S(2)}, u32[]{:S(2)}) collective-permute-start(bf16[3,128,128]{2,1,0:T(8,128)(2,1)S(1)} %collective-permute-done.13.refs_3_), channel_id=1, source_target_pairs={{0,1},{1,0},{2,3},{3,2},{4,5},{5,4},{6,7},{7,6},{8,9},{9,8},{10,11... | collective-permute-start | bytes 294920 | tf_op jit(solution)/shard_map/ppermute | solution.py:346

commit v31 on v30

--- a/solution.py
+++ b/solution.py
@@ -23,10 +23,10 @@
     pass
 
 
-def hand_on(x, *after, spec=ANY):
+def hand_on(x, *after):
     return pl.pallas_call(
         hand_kernel,
-        in_specs=[ANY] + [spec] * len(after),
+        in_specs=[ANY] * (1 + len(after)),
         out_specs=ANY,
         out_shape=jax.ShapeDtypeStruct(x.shape, x.dtype),
         input_output_aliases={0: 0},
@@ -392,7 +392,7 @@
     *parts, ready = rank_parts(owner_slot, toks, held, late, ring, pair, rows, blocks)
     mine = [parts[0]] + [in_plane(parts[k], -(k // pair), -(k % pair)) for k in range(1, shares)]
     theirs = [across(part) for part in mine]
-    base_in = across(hand_on(base_out, ready, spec=VMEM))
+    base_in = across(hand_on(base_out, ready))
     return final(mine, theirs, [base_mine, base_in], groups, pair, tokens.dtype)
 
 

time: 65.5 us -> 64.8 us (0.989)
    pallas_call x3, Pallas kernels: 0.69 us -> 0.01 us  [hand_on(): pl.pallas_call(hand_kernel, in_specs=[ANY] * (1 + len(after)), out_specs=...]
  transfers between devices with their start and end apart: 18 -> 18, of which waited for: 9 -> 9; matrix products, arithmetic and copies ran while one was open for 0% -> 0% of each run, Pallas kernels for 19% -> 20%
where the time goes in v31:
time: 64.8 us; the launch traced here: 64.4 us
  starting transfers between devices  20.2 us (31%)
  waiting for transfers between devices  19.9 us (31%)
  Pallas kernels  17.3 us (27%)
  local copies, waits for them, and re-layouts  6.87 us (11%)
    ppermute x6, waiting for transfers between devices, in_plane(): return lax.ppermute(x, PLANE, pairs)  10.1 us
    ppermute x6, starting transfers between devices, along(): lax.ppermute(x, 'ring', [(a, (a + step) % ring) for a in range(ring)])  9.83 us
    ppermute x6, waiting for transfers between devices, along(): lax.ppermute(x, 'ring', [(a, (a + step) % ring) for a in range(ring)])  8.51 us
    pallas_call x1, Pallas kernels, base_halves(): pl.pallas_call(functools.partial(base_kernel, sides, groups, pair), in_sp...  8.05 us
    ppermute x6, starting transfers between devices, in_plane(): return lax.ppermute(x, PLANE, pairs)  7.04 us
    unnamed x30, local copies, waits for them, and re-layouts  6.87 us
    pallas_call x1, Pallas kernels, spread(): pl.pallas_call(functools.partial(spread_kernel, groups, pair), in_specs=[...  3.29 us
    ppermute x1, starting transfers between devices, body(): lax.ppermute(packed[pair - w], 'pair', [(a, (a - w) % pair) for a in rang...  3.03 us
  transfers between devices with their start and end apart: 18, of which 9 were waited for; matrix products, arithmetic and copies ran while one was open for 0% of the time, Pallas kernels for 20%

profile of v31, /device:TPU:0, one launch (start us, length us, event | category | flops | bytes accessed | tf_op | source)
XLA Modules:
  0.0 64.4 jit_solution(1326275340141789685)
XLA Ops:
  0.0 1.9 %pack.1 = (bf16[2,64,1152]{2,1,0:T(8,128)(2,1)}, bf16[2,64,1152]{2,1,0:T(8,128)(2,1)}) custom-call(bf16[2,64,4096]{2,1,0:T(8,128)(2,1)} %bitcast.2, bf16[2,64,512]{2,1,0:T(8,128)(2,1)} %up.1), custom_call_target="tpu_custom_call" | custom-call | tf_op jit(solution)/shard_map/pack/pallas_call | solution.py:57
  1.9 3.0 %collective-permute-start.2 = (bf16[2,64,1152]{2,1,0:T(8,128)(2,1)}, bf16[2,64,1152]{2,1,0:T(8,128)(2,1)}, u32[]{:S(2)}, u32[]{:S(2)}) collective-permute-start(bf16[2,64,1152]{2,1,0:T(8,128)(2,1)} %get-tuple-element.23), channel_id=1, source_target_pairs={{0,2},{2,0},{1,3},{3,1},{4,6},{6,4},{5,7},{7,5},{8,10},{10,8},{9,1... | collective-permute-start | bytes 884744 | tf_op jit(solution)/shard_map/ppermute | solution.py:377
  5.0 1.6 %collective-permute-start.1 = (bf16[2,64,1152]{2,1,0:T(8,128)(2,1)}, bf16[2,64,1152]{2,1,0:T(8,128)(2,1)S(1)}, u32[]{:S(2)}, u32[]{:S(2)}) collective-permute-start(bf16[2,64,1152]{2,1,0:T(8,128)(2,1)} %get-tuple-element.21.refs_0_), channel_id=1, source_target_pairs={{0,4},{4,8},{8,12},{12,0},{1,5},{5,9},{9,13},{13,1},{2,6},{6,10},{... | collective-permute-start | bytes 884744 | tf_op jit(solution)/shard_map/ppermute | solution.py:349
  6.5 2.2 %collective-permute-start = (bf16[2,64,1152]{2,1,0:T(8,128)(2,1)}, bf16[2,64,1152]{2,1,0:T(8,128)(2,1)S(1)}, u32[]{:S(2)}, u32[]{:S(2)}) collective-permute-start(bf16[2,64,1152]{2,1,0:T(8,128)(2,1)} %get-tuple-element.21.refs_0_), channel_id=1, source_target_pairs={{0,12},{4,0},{8,4},{12,8},{1,13},{5,1},{9,5},{13,9},{2,14},{6,2},{... | collective-permute-start | bytes 884744 | tf_op jit(solution)/shard_map/ppermute | solution.py:349
  8.8 3.3 %spread.1 = (bf16[400,1024]{1,0:T(8,128)(2,1)}, bf16[400,1024]{1,0:T(8,128)(2,1)}, bf16[400,1024]{1,0:T(8,128)(2,1)}) custom-call(s32[3]{0:T(128)} %lengths.3, s32[3]{0:T(128)} %bitcast.3, bf16[384,4096]{1,0:T(8,128)(2,1)} %tok.3), custom_call_target="tpu_custom_call" | custom-call | tf_op jit(solution)/shard_map/spread/pallas_call | solution.py:131
  12.1 0.4 collective-permute-start.7
  12.4 1.7 %collective-permute-start.8 = (bf16[400,1024]{1,0:T(8,128)(2,1)}, bf16[400,1024]{1,0:T(8,128)(2,1)S(1)}, u32[]{:S(2)}, u32[]{:S(2)}) collective-permute-start(bf16[400,1024]{1,0:T(8,128)(2,1)} %get-tuple-element.26), channel_id=1, source_target_pairs={{0,16},{2,18},{16,0},{18,2},{1,17},{3,19},{17,1},{19,3},{4,20},{6,... | collective-permute-start | bytes 2457608 | tf_op jit(solution)/shard_map/ppermute | solution.py:359
  14.2 0.0 collective-permute-done.2.refs_3_
  14.2 1.5 %collective-permute-start.9 = (bf16[400,1024]{1,0:T(8,128)(2,1)}, bf16[400,1024]{1,0:T(8,128)(2,1)S(1)}, u32[]{:S(2)}, u32[]{:S(2)}) collective-permute-start(bf16[400,1024]{1,0:T(8,128)(2,1)} %get-tuple-element.27), channel_id=1, source_target_pairs={{0,18},{2,16},{16,2},{18,0},{1,19},{3,17},{17,3},{19,1},{4,22},{6,... | collective-permute-start | bytes 2457608 | tf_op jit(solution)/shard_map/ppermute | solution.py:359
  15.7 1.3 %collective-permute-done.1.refs_0_ = bf16[2,64,1152]{2,1,0:T(8,128)(2,1)S(1)} collective-permute-done((bf16[2,64,1152]{2,1,0:T(8,128)(2,1)}, bf16[2,64,1152]{2,1,0:T(8,128)(2,1)S(1)}, u32[]{:S(2)}, u32[]{:S(2)}) %collective-permute-start.1) | collective-permute-done | bytes 294944 | tf_op jit(solution)/shard_map/ppermute | solution.py:349
  17.0 0.7 %collective-permute-start.4 = (bf16[2,64,1152]{2,1,0:T(8,128)(2,1)}, bf16[2,64,1152]{2,1,0:T(8,128)(2,1)S(1)}, u32[]{:S(2)}, u32[]{:S(2)}) collective-permute-start(bf16[2,64,1152]{2,1,0:T(8,128)(2,1)} %collective-permute-done.2.refs_3_), channel_id=1, source_target_pairs={{0,4},{4,8},{8,12},{12,0},{1,5},{5,9},{9,13},{13,1},{2,6},{6,10},{... | collective-permute-start | bytes 884744 | tf_op jit(solution)/shard_map/ppermute | solution.py:349
  17.7 4.4 %collective-permute-done.refs_1_ = bf16[2,64,1152]{2,1,0:T(8,128)(2,1)S(1)} collective-permute-done((bf16[2,64,1152]{2,1,0:T(8,128)(2,1)}, bf16[2,64,1152]{2,1,0:T(8,128)(2,1)S(1)}, u32[]{:S(2)}, u32[]{:S(2)}) %collective-permute-start) | collective-permute-done | bytes 294944 | tf_op jit(solution)/shard_map/ppermute | solution.py:349
  22.1 2.8 %collective-permute-start.3 = (bf16[2,64,1152]{2,1,0:T(8,128)(2,1)}, bf16[2,64,1152]{2,1,0:T(8,128)(2,1)S(1)}, u32[]{:S(2)}, u32[]{:S(2)}) collective-permute-start(bf16[2,64,1152]{2,1,0:T(8,128)(2,1)} %collective-permute-done.2.refs_3_), channel_id=1, source_target_pairs={{0,12},{4,0},{8,4},{12,8},{1,13},{5,1},{9,5},{13,9},{2,14},{6,2},{... | collective-permute-start | bytes 884744 | tf_op jit(solution)/shard_map/ppermute | solution.py:349
  24.9 8.0 %base.1 = (f32[384,512]{1,0:T(8,128)}, f32[384,512]{1,0:T(8,128)}, f32[8,128]{1,0:T(8,128)}, bf16[400,1024]{1,0:T(8,128)(2,1)}) custom-call(s32[3]{0:T(128)} %lengths.3, s32[3]{0:T(128)} %bitcast.4, bf16[384,4096]{1,0:T(8,128)(2,1)} %tok.3, bf16[4096,1024]{1,0:T(8,128)(2,1)} %key.1), custom_call_target="tpu_custom_call" | custom-call | tf_op jit(solution)/shard_map/base/pallas_call | solution.py:203
  32.9 0.0 copy-start.14
  33.0 0.0 collective-permute-done.4.refs_1_.refs_5_
  33.0 0.1 collective-permute-start.5
  33.0 1.5 %collective-permute-done.3.refs_0_ = bf16[2,64,1152]{2,1,0:T(8,128)(2,1)S(1)} collective-permute-done((bf16[2,64,1152]{2,1,0:T(8,128)(2,1)}, bf16[2,64,1152]{2,1,0:T(8,128)(2,1)S(1)}, u32[]{:S(2)}, u32[]{:S(2)}) %collective-permute-start.3) | collective-permute-done | bytes 294944 | tf_op jit(solution)/shard_map/ppermute | solution.py:349
  34.5 0.7 %copy-done.6 = bf16[2,64,1152]{2,1,0:T(8,128)(2,1)} copy-done((bf16[2,64,1152]{2,1,0:T(8,128)(2,1)}, bf16[2,64,1152]{2,1,0:T(8,128)(2,1)S(1)}, u32[]{:S(2)}) %copy-start.6) | copy-done | bytes 294936
  35.2 2.4 %collective-permute-start.6 = (bf16[2,64,1152]{2,1,0:T(8,128)(2,1)}, bf16[2,64,1152]{2,1,0:T(8,128)(2,1)S(1)}, u32[]{:S(2)}, u32[]{:S(2)}) collective-permute-start(bf16[2,64,1152]{2,1,0:T(8,128)(2,1)} %hand.4.refs_4_), channel_id=1, source_target_pairs={{0,12},{4,0},{8,4},{12,8},{1,13},{5,1},{9,5},{13,9},{2,14},{6,2},{... | collective-permute-start | bytes 884744 | tf_op jit(solution)/shard_map/ppermute | solution.py:349
  37.7 1.0 %copy-done.1 = bf16[2,64,1152]{2,1,0:T(8,128)(2,1)S(1)} copy-done((bf16[2,64,1152]{2,1,0:T(8,128)(2,1)S(1)}, bf16[2,64,1152]{2,1,0:T(8,128)(2,1)}, u32[]{:S(2)}) %copy-start.1) | copy-done | bytes 294936
  38.6 1.0 %copy-done.3 = bf16[2,64,1152]{2,1,0:T(8,128)(2,1)S(1)} copy-done((bf16[2,64,1152]{2,1,0:T(8,128)(2,1)S(1)}, bf16[2,64,1152]{2,1,0:T(8,128)(2,1)}, u32[]{:S(2)}) %copy-start.3) | copy-done | bytes 294936
  39.6 1.0 %copy-done.5 = bf16[2,64,1152]{2,1,0:T(8,128)(2,1)S(1)} copy-done((bf16[2,64,1152]{2,1,0:T(8,128)(2,1)S(1)}, bf16[2,64,1152]{2,1,0:T(8,128)(2,1)}, u32[]{:S(2)}) %copy-start.5) | copy-done | bytes 294936
  40.6 1.0 %copy-done.7 = bf16[2,64,1152]{2,1,0:T(8,128)(2,1)S(1)} copy-done((bf16[2,64,1152]{2,1,0:T(8,128)(2,1)S(1)}, bf16[2,64,1152]{2,1,0:T(8,128)(2,1)}, u32[]{:S(2)}) %copy-start.7) | copy-done | bytes 294936
  41.5 1.3 %collect.1.held = bf16[12,64,1152]{2,1,0:T(8,128)(2,1)S(1)} custom-call(bf16[2,64,1152]{2,1,0:T(8,128)(2,1)S(1)} %copy-done.10, bf16[2,64,1152]{2,1,0:T(8,128)(2,1)S(1)} %copy-done.1, bf16[2,64,1152]{2,1,0:T(8,128)(2,1)S(1)} %copy-done.3, bf16[2,64,1152]{2,1,0:T(8,128)(2,1)} %collective-permute-done.2.refs_3_, bf16[2,64,1152]{2,1,0:T(8,128)(2,1)S(1)} %copy-done.7, ...), custom_call_target="tpu_custom_call" | custom-call | tf_op jit(solution)/shard_map/collect/pallas_call | solution.py:240
  42.8 1.4 %collective-permute-done.5.refs_0_ = bf16[2,64,1152]{2,1,0:T(8,128)(2,1)S(1)} collective-permute-done((bf16[2,64,1152]{2,1,0:T(8,128)(2,1)}, bf16[2,64,1152]{2,1,0:T(8,128)(2,1)S(1)}, u32[]{:S(2)}, u32[]{:S(2)}) %collective-permute-start.5) | collective-permute-done | bytes 294944 | tf_op jit(solution)/shard_map/ppermute | solution.py:349
  44.2 0.7 %copy-done.11 = bf16[2,64,1152]{2,1,0:T(8,128)(2,1)} copy-done((bf16[2,64,1152]{2,1,0:T(8,128)(2,1)}, bf16[2,64,1152]{2,1,0:T(8,128)(2,1)S(1)}, u32[]{:S(2)}) %copy-start.11) | copy-done | bytes 294936
  44.9 0.0 collective-permute-done.7.refs_3_
  44.9 5.4 %collective-permute-done.9.refs_5_ = bf16[400,1024]{1,0:T(8,128)(2,1)S(1)} collective-permute-done((bf16[400,1024]{1,0:T(8,128)(2,1)}, bf16[400,1024]{1,0:T(8,128)(2,1)S(1)}, u32[]{:S(2)}, u32[]{:S(2)}) %collective-permute-start.9) | collective-permute-done | bytes 819232 | tf_op jit(solution)/shard_map/ppermute | solution.py:359
  50.3 0.0 copy-start.12
  50.3 1.0 %copy-done.12 = bf16[2,64,1152]{2,1,0:T(8,128)(2,1)S(1)} copy-done((bf16[2,64,1152]{2,1,0:T(8,128)(2,1)S(1)}, bf16[2,64,1152]{2,1,0:T(8,128)(2,1)}, u32[]{:S(2)}) %copy-start.12) | copy-done | bytes 294936
  51.3 1.7 %rank.1 = (bf16[3,128,128]{2,1,0:T(8,128)(2,1)S(1)}, bf16[3,128,128]{2,1,0:T(8,128)(2,1)S(1)}, bf16[3,128,128]{2,1,0:T(8,128)(2,1)S(1)}, bf16[3,128,128]{2,1,0:T(8,128)(2,1)S(1)}, f32[8,128]{1,0:T(8,128)S(1)}) custom-call(s32[16]{0:T(128)S(1)} %copy-done.14, bf16[12,64,1152]{2,1,0:T(8,128)(2,1)S(1)} %collect.1.held, bf16[2,64,1152]{2,1,0:T(8,128)(2,1)S(1)} %copy-done.12, ...), custom_call_target="tpu_custom_call" | custom-call | tf_op jit(solution)/shard_map/rank/pallas_call | solution.py:293
  53.0 0.0 copy-start.13
  53.0 0.6 copy-done.13
  53.6 0.0 collective-permute-start.10
  53.6 0.5 collective-permute-start.11
  54.1 1.5 %collective-permute-start.12 = (bf16[3,128,128]{2,1,0:T(8,128)(2,1)S(1)}, bf16[3,128,128]{2,1,0:T(8,128)(2,1)S(1)}, u32[]{:S(2)}, u32[]{:S(2)}) collective-permute-start(bf16[3,128,128]{2,1,0:T(8,128)(2,1)S(1)} %get-tuple-element.31), channel_id=1, source_target_pairs={{0,16},{2,18},{16,0},{18,2},{1,17},{3,19},{17,1},{19,3},{4,20},{6,... | collective-permute-start | bytes 294920 | tf_op jit(solution)/shard_map/ppermute | solution.py:359
  55.6 1.5 %collective-permute-start.13 = (bf16[3,128,128]{2,1,0:T(8,128)(2,1)S(1)}, bf16[3,128,128]{2,1,0:T(8,128)(2,1)S(1)}, u32[]{:S(2)}, u32[]{:S(2)}) collective-permute-start(bf16[3,128,128]{2,1,0:T(8,128)(2,1)S(1)} %get-tuple-element.32), channel_id=1, source_target_pairs={{0,18},{2,16},{16,2},{18,0},{1,19},{3,17},{17,3},{19,1},{4,22},{6,... | collective-permute-start | bytes 294920 | tf_op jit(solution)/shard_map/ppermute | solution.py:359
  57.1 1.7 %collective-permute-done.11.refs_1_ = bf16[3,128,128]{2,1,0:T(8,128)(2,1)S(1)} collective-permute-done((bf16[3,128,128]{2,1,0:T(8,128)(2,1)S(1)}, bf16[3,128,128]{2,1,0:T(8,128)(2,1)S(1)}, u32[]{:S(2)}, u32[]{:S(2)}) %collective-permute-start.11) | collective-permute-done | bytes 98336 | tf_op jit(solution)/shard_map/ppermute | solution.py:359
  58.8 0.2 collective-permute-done.12.refs_2_
  59.0 0.3 collective-permute-start.16
  59.3 2.8 %collective-permute-done.13.refs_3_ = bf16[3,128,128]{2,1,0:T(8,128)(2,1)S(1)} collective-permute-done((bf16[3,128,128]{2,1,0:T(8,128)(2,1)S(1)}, bf16[3,128,128]{2,1,0:T(8,128)(2,1)S(1)}, u32[]{:S(2)}, u32[]{:S(2)}) %collective-permute-start.13) | collective-permute-done | bytes 98336 | tf_op jit(solution)/shard_map/ppermute | solution.py:359
  62.1 0.0 collective-permute-start.17
  62.1 0.0 collective-permute-done.14.refs_4_
  62.1 0.0 collective-permute-done.15.refs_5_
  62.1 0.0 collective-permute-done.16.refs_6_
  62.1 1.3 %collective-permute-done.17.refs_7_ = bf16[3,128,128]{2,1,0:T(8,128)(2,1)S(1)} collective-permute-done((bf16[3,128,128]{2,1,0:T(8,128)(2,1)S(1)}, bf16[3,128,128]{2,1,0:T(8,128)(2,1)S(1)}, u32[]{:S(2)}, u32[]{:S(2)}) %collective-permute-start.17) | collective-permute-done | bytes 98336 | tf_op jit(solution)/shard_map/ppermute | solution.py:346
  63.4 1.0 %final.1 = bf16[384,512]{1,0:T(8,128)(2,1)} custom-call(f32[384,512]{1,0:T(8,128)S(1)} %copy-done.9, f32[384,512]{1,0:T(8,128)S(1)} %collective-permute-done.10.base_b, bf16[3,128,128]{2,1,0:T(8,128)(2,1)S(1)} %get-tuple-element.29.refs_0_, bf16[3,128,128]{2,1,0:T(8,128)(2,1)S(1)} %collective-permute-done.11.refs_1_, ...), custom_call_target="tpu_custom_call" | custom-call | tf_op jit(solution)/shard_map/final/pallas_call | solution.py:327
  (27 shorter events, 0.1 us)
Async XLA Ops:
  1.9 12.2 %collective-permute-start.2 = (bf16[2,64,1152]{2,1,0:T(8,128)(2,1)}, bf16[2,64,1152]{2,1,0:T(8,128)(2,1)}, u32[]{:S(2)}, u32[]{:S(2)}) collective-permute-start(bf16[2,64,1152]{2,1,0:T(8,128)(2,1)} %get-tuple-element.23), channel_id=1, source_target_pairs={{0,2},{2,0},{1,3},{3,1},{4,6},{6,4},{5,7},{7,5},{8,10},{10,8},{9,1... | collective-permute-start | bytes 884744 | tf_op jit(solution)/shard_map/ppermute | solution.py:377
  5.0 12.0 %collective-permute-start.1 = (bf16[2,64,1152]{2,1,0:T(8,128)(2,1)}, bf16[2,64,1152]{2,1,0:T(8,128)(2,1)S(1)}, u32[]{:S(2)}, u32[]{:S(2)}) collective-permute-start(bf16[2,64,1152]{2,1,0:T(8,128)(2,1)} %get-tuple-element.21.refs_0_), channel_id=1, source_target_pairs={{0,4},{4,8},{8,12},{12,0},{1,5},{5,9},{9,13},{13,1},{2,6},{6,10},{... | collective-permute-start | bytes 884744 | tf_op jit(solution)/shard_map/ppermute | solution.py:349
  6.5 15.5 %collective-permute-start = (bf16[2,64,1152]{2,1,0:T(8,128)(2,1)}, bf16[2,64,1152]{2,1,0:T(8,128)(2,1)S(1)}, u32[]{:S(2)}, u32[]{:S(2)}) collective-permute-start(bf16[2,64,1152]{2,1,0:T(8,128)(2,1)} %get-tuple-element.21.refs_0_), channel_id=1, source_target_pairs={{0,12},{4,0},{8,4},{12,8},{1,13},{5,1},{9,5},{13,9},{2,14},{6,2},{... | collective-permute-start | bytes 884744 | tf_op jit(solution)/shard_map/ppermute | solution.py:349
  12.1 32.8 %collective-permute-start.7 = (bf16[400,1024]{1,0:T(8,128)(2,1)}, bf16[400,1024]{1,0:T(8,128)(2,1)S(1)}, u32[]{:S(2)}, u32[]{:S(2)}) collective-permute-start(bf16[400,1024]{1,0:T(8,128)(2,1)} %get-tuple-element.25), channel_id=1, source_target_pairs={{0,2},{2,0},{16,18},{18,16},{1,3},{3,1},{17,19},{19,17},{4,6},{6,4... | collective-permute-start | bytes 2457608 | tf_op jit(solution)/shard_map/ppermute | solution.py:359
  12.4 32.4 %collective-permute-start.8 = (bf16[400,1024]{1,0:T(8,128)(2,1)}, bf16[400,1024]{1,0:T(8,128)(2,1)S(1)}, u32[]{:S(2)}, u32[]{:S(2)}) collective-permute-start(bf16[400,1024]{1,0:T(8,128)(2,1)} %get-tuple-element.26), channel_id=1, source_target_pairs={{0,16},{2,18},{16,0},{18,2},{1,17},{3,19},{17,1},{19,3},{4,20},{6,... | collective-permute-start | bytes 2457608 | tf_op jit(solution)/shard_map/ppermute | solution.py:359
  14.2 23.5 %copy-start.10 = (bf16[2,64,1152]{2,1,0:T(8,128)(2,1)S(1)}, bf16[2,64,1152]{2,1,0:T(8,128)(2,1)}, u32[]{:S(2)}) copy-start(bf16[2,64,1152]{2,1,0:T(8,128)(2,1)} %get-tuple-element.21.refs_0_) | copy-start | bytes 884740
  14.2 36.1 %collective-permute-start.9 = (bf16[400,1024]{1,0:T(8,128)(2,1)}, bf16[400,1024]{1,0:T(8,128)(2,1)S(1)}, u32[]{:S(2)}, u32[]{:S(2)}) collective-permute-start(bf16[400,1024]{1,0:T(8,128)(2,1)} %get-tuple-element.27), channel_id=1, source_target_pairs={{0,18},{2,16},{16,2},{18,0},{1,19},{3,17},{17,3},{19,1},{4,22},{6,... | collective-permute-start | bytes 2457608 | tf_op jit(solution)/shard_map/ppermute | solution.py:359
  16.9 16.0 %copy-start.2 = (bf16[2,64,1152]{2,1,0:T(8,128)(2,1)}, bf16[2,64,1152]{2,1,0:T(8,128)(2,1)S(1)}, u32[]{:S(2)}) copy-start(bf16[2,64,1152]{2,1,0:T(8,128)(2,1)S(1)} %collective-permute-done.1.refs_0_) | copy-start | bytes 884740
  17.0 16.0 %collective-permute-start.4 = (bf16[2,64,1152]{2,1,0:T(8,128)(2,1)}, bf16[2,64,1152]{2,1,0:T(8,128)(2,1)S(1)}, u32[]{:S(2)}, u32[]{:S(2)}) collective-permute-start(bf16[2,64,1152]{2,1,0:T(8,128)(2,1)} %collective-permute-done.2.refs_3_), channel_id=1, source_target_pairs={{0,4},{4,8},{8,12},{12,0},{1,5},{5,9},{9,13},{13,1},{2,6},{6,10},{... | collective-permute-start | bytes 884744 | tf_op jit(solution)/shard_map/ppermute | solution.py:349
  22.1 10.9 %copy-start = (bf16[2,64,1152]{2,1,0:T(8,128)(2,1)}, bf16[2,64,1152]{2,1,0:T(8,128)(2,1)S(1)}, u32[]{:S(2)}) copy-start(bf16[2,64,1152]{2,1,0:T(8,128)(2,1)S(1)} %collective-permute-done.refs_1_) | copy-start | bytes 884740
  22.1 12.5 %collective-permute-start.3 = (bf16[2,64,1152]{2,1,0:T(8,128)(2,1)}, bf16[2,64,1152]{2,1,0:T(8,128)(2,1)S(1)}, u32[]{:S(2)}, u32[]{:S(2)}) collective-permute-start(bf16[2,64,1152]{2,1,0:T(8,128)(2,1)} %collective-permute-done.2.refs_3_), channel_id=1, source_target_pairs={{0,12},{4,0},{8,4},{12,8},{1,13},{5,1},{9,5},{13,9},{2,14},{6,2},{... | collective-permute-start | bytes 884744 | tf_op jit(solution)/shard_map/ppermute | solution.py:349
  32.9 17.4 %copy-start.14 = (s32[16]{0:T(128)S(1)}, s32[16]{0:T(128)}, u32[]{:S(2)}) copy-start(s32[16]{0:T(128)} %owner.1) | copy-start | bytes 196
  33.0 1.5 %copy-start.4 = (bf16[2,64,1152]{2,1,0:T(8,128)(2,1)}, bf16[2,64,1152]{2,1,0:T(8,128)(2,1)S(1)}, u32[]{:S(2)}) copy-start(bf16[2,64,1152]{2,1,0:T(8,128)(2,1)S(1)} %collective-permute-done.4.refs_1_.refs_5_) | copy-start | bytes 884740
  33.0 11.2 %collective-permute-start.5 = (bf16[2,64,1152]{2,1,0:T(8,128)(2,1)}, bf16[2,64,1152]{2,1,0:T(8,128)(2,1)S(1)}, u32[]{:S(2)}, u32[]{:S(2)}) collective-permute-start(bf16[2,64,1152]{2,1,0:T(8,128)(2,1)} %hand.3.refs_2_), channel_id=1, source_target_pairs={{0,4},{4,8},{8,12},{12,0},{1,5},{5,9},{9,13},{13,1},{2,6},{6,10},{... | collective-permute-start | bytes 884744 | tf_op jit(solution)/shard_map/ppermute | solution.py:349
  34.5 0.7 %copy-start.6 = (bf16[2,64,1152]{2,1,0:T(8,128)(2,1)}, bf16[2,64,1152]{2,1,0:T(8,128)(2,1)S(1)}, u32[]{:S(2)}) copy-start(bf16[2,64,1152]{2,1,0:T(8,128)(2,1)S(1)} %collective-permute-done.3.refs_0_) | copy-start | bytes 884740
  35.2 15.1 %collective-permute-start.6 = (bf16[2,64,1152]{2,1,0:T(8,128)(2,1)}, bf16[2,64,1152]{2,1,0:T(8,128)(2,1)S(1)}, u32[]{:S(2)}, u32[]{:S(2)}) collective-permute-start(bf16[2,64,1152]{2,1,0:T(8,128)(2,1)} %hand.4.refs_4_), channel_id=1, source_target_pairs={{0,12},{4,0},{8,4},{12,8},{1,13},{5,1},{9,5},{13,9},{2,14},{6,2},{... | collective-permute-start | bytes 884744 | tf_op jit(solution)/shard_map/ppermute | solution.py:349
  37.7 1.0 %copy-start.1 = (bf16[2,64,1152]{2,1,0:T(8,128)(2,1)S(1)}, bf16[2,64,1152]{2,1,0:T(8,128)(2,1)}, u32[]{:S(2)}) copy-start(bf16[2,64,1152]{2,1,0:T(8,128)(2,1)} %copy-done) | copy-start | bytes 884740
  38.6 1.0 %copy-start.3 = (bf16[2,64,1152]{2,1,0:T(8,128)(2,1)S(1)}, bf16[2,64,1152]{2,1,0:T(8,128)(2,1)}, u32[]{:S(2)}) copy-start(bf16[2,64,1152]{2,1,0:T(8,128)(2,1)} %hand.3.refs_2_) | copy-start | bytes 884740
  39.6 1.0 %copy-start.5 = (bf16[2,64,1152]{2,1,0:T(8,128)(2,1)S(1)}, bf16[2,64,1152]{2,1,0:T(8,128)(2,1)}, u32[]{:S(2)}) copy-start(bf16[2,64,1152]{2,1,0:T(8,128)(2,1)} %copy-done.4) | copy-start | bytes 884740
  40.5 1.0 %copy-start.7 = (bf16[2,64,1152]{2,1,0:T(8,128)(2,1)S(1)}, bf16[2,64,1152]{2,1,0:T(8,128)(2,1)}, u32[]{:S(2)}) copy-start(bf16[2,64,1152]{2,1,0:T(8,128)(2,1)} %hand.4.refs_4_) | copy-start | bytes 884740
  41.5 8.8 %copy-start.8 = (bf16[400,1024]{1,0:T(8,128)(2,1)S(1)}, bf16[400,1024]{1,0:T(8,128)(2,1)}, u32[]{:S(2)}) copy-start(bf16[400,1024]{1,0:T(8,128)(2,1)} %get-tuple-element.24.refs_2_) | copy-start | bytes 2457604
  44.2 0.7 %copy-start.11 = (bf16[2,64,1152]{2,1,0:T(8,128)(2,1)}, bf16[2,64,1152]{2,1,0:T(8,128)(2,1)S(1)}, u32[]{:S(2)}) copy-start(bf16[2,64,1152]{2,1,0:T(8,128)(2,1)S(1)} %collective-permute-done.5.refs_0_) | copy-start | bytes 884740
  50.3 1.0 %copy-start.12 = (bf16[2,64,1152]{2,1,0:T(8,128)(2,1)S(1)}, bf16[2,64,1152]{2,1,0:T(8,128)(2,1)}, u32[]{:S(2)}) copy-start(bf16[2,64,1152]{2,1,0:T(8,128)(2,1)} %copy-done.11) | copy-start | bytes 884740
  51.3 12.1 %copy-start.9 = (f32[384,512]{1,0:T(8,128)S(1)}, f32[384,512]{1,0:T(8,128)}, u32[]{:S(2)}) copy-start(f32[384,512]{1,0:T(8,128)} %get-tuple-element.19.base_a) | copy-start | bytes 2359300
  53.0 0.6 copy-start.13
  53.6 9.8 %collective-permute-start.10 = (f32[384,512]{1,0:T(8,128)}, f32[384,512]{1,0:T(8,128)S(1)}, u32[]{:S(2)}, u32[]{:S(2)}) collective-permute-start(f32[384,512]{1,0:T(8,128)} %hand.5), channel_id=1, source_target_pairs={{0,1},{1,0},{2,3},{3,2},{4,5},{5,4},{6,7},{7,6},{8,9},{9,8},{10,11... | collective-permute-start | bytes 2359304 | tf_op jit(solution)/shard_map/ppermute | solution.py:346
  53.6 5.2 %collective-permute-start.11 = (bf16[3,128,128]{2,1,0:T(8,128)(2,1)S(1)}, bf16[3,128,128]{2,1,0:T(8,128)(2,1)S(1)}, u32[]{:S(2)}, u32[]{:S(2)}) collective-permute-start(bf16[3,128,128]{2,1,0:T(8,128)(2,1)S(1)} %get-tuple-element.30), channel_id=1, source_target_pairs={{0,2},{2,0},{16,18},{18,16},{1,3},{3,1},{17,19},{19,17},{4,6},{6,4... | collective-permute-start | bytes 294920 | tf_op jit(solution)/shard_map/ppermute | solution.py:359
  54.1 4.9 %collective-permute-start.12 = (bf16[3,128,128]{2,1,0:T(8,128)(2,1)S(1)}, bf16[3,128,128]{2,1,0:T(8,128)(2,1)S(1)}, u32[]{:S(2)}, u32[]{:S(2)}) collective-permute-start(bf16[3,128,128]{2,1,0:T(8,128)(2,1)S(1)} %get-tuple-element.31), channel_id=1, source_target_pairs={{0,16},{2,18},{16,0},{18,2},{1,17},{3,19},{17,1},{19,3},{4,20},{6,... | collective-permute-start | bytes 294920 | tf_op jit(solution)/shard_map/ppermute | solution.py:359
  55.6 6.5 %collective-permute-start.13 = (bf16[3,128,128]{2,1,0:T(8,128)(2,1)S(1)}, bf16[3,128,128]{2,1,0:T(8,128)(2,1)S(1)}, u32[]{:S(2)}, u32[]{:S(2)}) collective-permute-start(bf16[3,128,128]{2,1,0:T(8,128)(2,1)S(1)} %get-tuple-element.32), channel_id=1, source_target_pairs={{0,18},{2,16},{16,2},{18,0},{1,19},{3,17},{17,3},{19,1},{4,22},{6,... | collective-permute-start | bytes 294920 | tf_op jit(solution)/shard_map/ppermute | solution.py:359
  57.1 5.0 %collective-permute-start.14 = (bf16[3,128,128]{2,1,0:T(8,128)(2,1)S(1)}, bf16[3,128,128]{2,1,0:T(8,128)(2,1)S(1)}, u32[]{:S(2)}, u32[]{:S(2)}) collective-permute-start(bf16[3,128,128]{2,1,0:T(8,128)(2,1)S(1)} %get-tuple-element.29.refs_0_), channel_id=1, source_target_pairs={{0,1},{1,0},{2,3},{3,2},{4,5},{5,4},{6,7},{7,6},{8,9},{9,8},{10,11... | collective-permute-start | bytes 294920 | tf_op jit(solution)/shard_map/ppermute | solution.py:346
  58.8 3.3 %collective-permute-start.15 = (bf16[3,128,128]{2,1,0:T(8,128)(2,1)S(1)}, bf16[3,128,128]{2,1,0:T(8,128)(2,1)S(1)}, u32[]{:S(2)}, u32[]{:S(2)}) collective-permute-start(bf16[3,128,128]{2,1,0:T(8,128)(2,1)S(1)} %collective-permute-done.11.refs_1_), channel_id=1, source_target_pairs={{0,1},{1,0},{2,3},{3,2},{4,5},{5,4},{6,7},{7,6},{8,9},{9,8},{10,11... | collective-permute-start | bytes 294920 | tf_op jit(solution)/shard_map/ppermute | solution.py:346
  59.0 3.1 %collective-permute-start.16 = (bf16[3,128,128]{2,1,0:T(8,128)(2,1)S(1)}, bf16[3,128,128]{2,1,0:T(8,128)(2,1)S(1)}, u32[]{:S(2)}, u32[]{:S(2)}) collective-permute-start(bf16[3,128,128]{2,1,0:T(8,128)(2,1)S(1)} %collective-permute-done.12.refs_2_), channel_id=1, source_target_pairs={{0,1},{1,0},{2,3},{3,2},{4,5},{5,4},{6,7},{7,6},{8,9},{9,8},{10,11... | collective-permute-start | bytes 294920 | tf_op jit(solution)/shard_map/ppermute | solution.py:346
  62.1 1.3 %collective-permute-start.17 = (bf16[3,128,128]{2,1,0:T(8,128)(2,1)S(1)}, bf16[3,128,128]{2,1,0:T(8,128)(2,1)S(1)}, u32[]{:S(2)}, u32[]{:S(2)}) collective-permute-start(bf16[3,128,128]{2,1,0:T(8,128)(2,1)S(1)} %collective-permute-done.13.refs_3_), channel_id=1, source_target_pairs={{0,1},{1,0},{2,3},{3,2},{4,5},{5,4},{6,7},{7,6},{8,9},{9,8},{10,11... | collective-permute-start | bytes 294920 | tf_op jit(solution)/shard_map/ppermute | solution.py:346

commit v32 on v31

--- a/solution.py
+++ b/solution.py
@@ -377,7 +377,7 @@
         lax.ppermute(packed[pair - w], "pair", [(a, (a - w) % pair) for a in range(pair)]) for w in range(1, pair)
     ]
     firsts = [first_hops(piece) for piece in [packed[0]] + swapped]
-    toks = [in_plane(slabs[k - 1], k // pair, k % pair) for k in range(1, shares)]
+    toks = [in_plane(slabs[k - 1], k // pair, k % pair) for k in reversed(range(1, shares))][::-1]
 
     base_mine, base_out, flag, own_slab = base_halves(tokens, base_key, sides, lengths, ids, groups, pair)
     toks = [own_slab] + toks

time: 64.8 us -> 64.8 us (level)
  no operation moved by 1% of the time
where the time goes in v32:
time: 64.8 us; the launch traced here: 64.4 us
  starting transfers between devices  20.2 us (31%)
  waiting for transfers between devices  19.9 us (31%)
  Pallas kernels  17.3 us (27%)
  local copies, waits for them, and re-layouts  6.87 us (11%)
    ppermute x6, waiting for transfers between devices, in_plane(): return lax.ppermute(x, PLANE, pairs)  10.1 us
    ppermute x6, starting transfers between devices, along(): lax.ppermute(x, 'ring', [(a, (a + step) % ring) for a in range(ring)])  9.83 us
    ppermute x6, waiting for transfers between devices, along(): lax.ppermute(x, 'ring', [(a, (a + step) % ring) for a in range(ring)])  8.51 us
    pallas_call x1, Pallas kernels, base_halves(): pl.pallas_call(functools.partial(base_kernel, sides, groups, pair), in_sp...  8.05 us
    ppermute x6, starting transfers between devices, in_plane(): return lax.ppermute(x, PLANE, pairs)  7.04 us
    unnamed x30, local copies, waits for them, and re-layouts  6.87 us
    pallas_call x1, Pallas kernels, spread(): pl.pallas_call(functools.partial(spread_kernel, groups, pair), in_specs=[...  3.29 us
    ppermute x1, starting transfers between devices, body(): lax.ppermute(packed[pair - w], 'pair', [(a, (a - w) % pair) for a in rang...  3.03 us
  transfers between devices with their start and end apart: 18, of which 9 were waited for; matrix products, arithmetic and copies ran while one was open for 0% of the time, Pallas kernels for 20%

profile of v32, /device:TPU:0, one launch (start us, length us, event | category | flops | bytes accessed | tf_op | source)
XLA Modules:
  0.0 64.4 jit_solution(1326275340141789685)
XLA Ops:
  0.0 1.9 %pack.1 = (bf16[2,64,1152]{2,1,0:T(8,128)(2,1)}, bf16[2,64,1152]{2,1,0:T(8,128)(2,1)}) custom-call(bf16[2,64,4096]{2,1,0:T(8,128)(2,1)} %bitcast.2, bf16[2,64,512]{2,1,0:T(8,128)(2,1)} %up.1), custom_call_target="tpu_custom_call" | custom-call | tf_op jit(solution)/shard_map/pack/pallas_call | solution.py:57
  1.9 3.0 %collective-permute-start.2 = (bf16[2,64,1152]{2,1,0:T(8,128)(2,1)}, bf16[2,64,1152]{2,1,0:T(8,128)(2,1)}, u32[]{:S(2)}, u32[]{:S(2)}) collective-permute-start(bf16[2,64,1152]{2,1,0:T(8,128)(2,1)} %get-tuple-element.23), channel_id=1, source_target_pairs={{0,2},{2,0},{1,3},{3,1},{4,6},{6,4},{5,7},{7,5},{8,10},{10,8},{9,1... | collective-permute-start | bytes 884744 | tf_op jit(solution)/shard_map/ppermute | solution.py:377
  5.0 1.6 %collective-permute-start.1 = (bf16[2,64,1152]{2,1,0:T(8,128)(2,1)}, bf16[2,64,1152]{2,1,0:T(8,128)(2,1)S(1)}, u32[]{:S(2)}, u32[]{:S(2)}) collective-permute-start(bf16[2,64,1152]{2,1,0:T(8,128)(2,1)} %get-tuple-element.21.refs_0_), channel_id=1, source_target_pairs={{0,4},{4,8},{8,12},{12,0},{1,5},{5,9},{9,13},{13,1},{2,6},{6,10},{... | collective-permute-start | bytes 884744 | tf_op jit(solution)/shard_map/ppermute | solution.py:349
  6.5 2.2 %collective-permute-start = (bf16[2,64,1152]{2,1,0:T(8,128)(2,1)}, bf16[2,64,1152]{2,1,0:T(8,128)(2,1)S(1)}, u32[]{:S(2)}, u32[]{:S(2)}) collective-permute-start(bf16[2,64,1152]{2,1,0:T(8,128)(2,1)} %get-tuple-element.21.refs_0_), channel_id=1, source_target_pairs={{0,12},{4,0},{8,4},{12,8},{1,13},{5,1},{9,5},{13,9},{2,14},{6,2},{... | collective-permute-start | bytes 884744 | tf_op jit(solution)/shard_map/ppermute | solution.py:349
  8.8 3.3 %spread.1 = (bf16[400,1024]{1,0:T(8,128)(2,1)}, bf16[400,1024]{1,0:T(8,128)(2,1)}, bf16[400,1024]{1,0:T(8,128)(2,1)}) custom-call(s32[3]{0:T(128)} %lengths.3, s32[3]{0:T(128)} %bitcast.3, bf16[384,4096]{1,0:T(8,128)(2,1)} %tok.3), custom_call_target="tpu_custom_call" | custom-call | tf_op jit(solution)/shard_map/spread/pallas_call | solution.py:131
  12.1 0.4 collective-permute-start.7
  12.4 1.7 %collective-permute-start.8 = (bf16[400,1024]{1,0:T(8,128)(2,1)}, bf16[400,1024]{1,0:T(8,128)(2,1)S(1)}, u32[]{:S(2)}, u32[]{:S(2)}) collective-permute-start(bf16[400,1024]{1,0:T(8,128)(2,1)} %get-tuple-element.26), channel_id=1, source_target_pairs={{0,16},{2,18},{16,0},{18,2},{1,17},{3,19},{17,1},{19,3},{4,20},{6,... | collective-permute-start | bytes 2457608 | tf_op jit(solution)/shard_map/ppermute | solution.py:359
  14.2 1.5 %collective-permute-start.9 = (bf16[400,1024]{1,0:T(8,128)(2,1)}, bf16[400,1024]{1,0:T(8,128)(2,1)S(1)}, u32[]{:S(2)}, u32[]{:S(2)}) collective-permute-start(bf16[400,1024]{1,0:T(8,128)(2,1)} %get-tuple-element.27), channel_id=1, source_target_pairs={{0,18},{2,16},{16,2},{18,0},{1,19},{3,17},{17,3},{19,1},{4,22},{6,... | collective-permute-start | bytes 2457608 | tf_op jit(solution)/shard_map/ppermute | solution.py:359
  15.7 1.3 %collective-permute-done.1.refs_0_ = bf16[2,64,1152]{2,1,0:T(8,128)(2,1)S(1)} collective-permute-done((bf16[2,64,1152]{2,1,0:T(8,128)(2,1)}, bf16[2,64,1152]{2,1,0:T(8,128)(2,1)S(1)}, u32[]{:S(2)}, u32[]{:S(2)}) %collective-permute-start.1) | collective-permute-done | bytes 294944 | tf_op jit(solution)/shard_map/ppermute | solution.py:349
  17.0 0.7 %collective-permute-start.4 = (bf16[2,64,1152]{2,1,0:T(8,128)(2,1)}, bf16[2,64,1152]{2,1,0:T(8,128)(2,1)S(1)}, u32[]{:S(2)}, u32[]{:S(2)}) collective-permute-start(bf16[2,64,1152]{2,1,0:T(8,128)(2,1)} %collective-permute-done.2.refs_3_), channel_id=1, source_target_pairs={{0,4},{4,8},{8,12},{12,0},{1,5},{5,9},{9,13},{13,1},{2,6},{6,10},{... | collective-permute-start | bytes 884744 | tf_op jit(solution)/shard_map/ppermute | solution.py:349
  17.7 4.4 %collective-permute-done.refs_1_ = bf16[2,64,1152]{2,1,0:T(8,128)(2,1)S(1)} collective-permute-done((bf16[2,64,1152]{2,1,0:T(8,128)(2,1)}, bf16[2,64,1152]{2,1,0:T(8,128)(2,1)S(1)}, u32[]{:S(2)}, u32[]{:S(2)}) %collective-permute-start) | collective-permute-done | bytes 294944 | tf_op jit(solution)/shard_map/ppermute | solution.py:349
  22.1 2.8 %collective-permute-start.3 = (bf16[2,64,1152]{2,1,0:T(8,128)(2,1)}, bf16[2,64,1152]{2,1,0:T(8,128)(2,1)S(1)}, u32[]{:S(2)}, u32[]{:S(2)}) collective-permute-start(bf16[2,64,1152]{2,1,0:T(8,128)(2,1)} %collective-permute-done.2.refs_3_), channel_id=1, source_target_pairs={{0,12},{4,0},{8,4},{12,8},{1,13},{5,1},{9,5},{13,9},{2,14},{6,2},{... | collective-permute-start | bytes 884744 | tf_op jit(solution)/shard_map/ppermute | solution.py:349
  24.9 8.0 %base.1 = (f32[384,512]{1,0:T(8,128)}, f32[384,512]{1,0:T(8,128)}, f32[8,128]{1,0:T(8,128)}, bf16[400,1024]{1,0:T(8,128)(2,1)}) custom-call(s32[3]{0:T(128)} %lengths.3, s32[3]{0:T(128)} %bitcast.4, bf16[384,4096]{1,0:T(8,128)(2,1)} %tok.3, bf16[4096,1024]{1,0:T(8,128)(2,1)} %key.1), custom_call_target="tpu_custom_call" | custom-call | tf_op jit(solution)/shard_map/base/pallas_call | solution.py:203
  32.9 0.0 copy-start.14
  33.0 0.1 collective-permute-start.5
  33.0 1.5 %collective-permute-done.3.refs_0_ = bf16[2,64,1152]{2,1,0:T(8,128)(2,1)S(1)} collective-permute-done((bf16[2,64,1152]{2,1,0:T(8,128)(2,1)}, bf16[2,64,1152]{2,1,0:T(8,128)(2,1)S(1)}, u32[]{:S(2)}, u32[]{:S(2)}) %collective-permute-start.3) | collective-permute-done | bytes 294944 | tf_op jit(solution)/shard_map/ppermute | solution.py:349
  34.5 0.7 %copy-done.6 = bf16[2,64,1152]{2,1,0:T(8,128)(2,1)} copy-done((bf16[2,64,1152]{2,1,0:T(8,128)(2,1)}, bf16[2,64,1152]{2,1,0:T(8,128)(2,1)S(1)}, u32[]{:S(2)}) %copy-start.6) | copy-done | bytes 294936
  35.2 2.4 %collective-permute-start.6 = (bf16[2,64,1152]{2,1,0:T(8,128)(2,1)}, bf16[2,64,1152]{2,1,0:T(8,128)(2,1)S(1)}, u32[]{:S(2)}, u32[]{:S(2)}) collective-permute-start(bf16[2,64,1152]{2,1,0:T(8,128)(2,1)} %hand.4.refs_4_), channel_id=1, source_target_pairs={{0,12},{4,0},{8,4},{12,8},{1,13},{5,1},{9,5},{13,9},{2,14},{6,2},{... | collective-permute-start | bytes 884744 | tf_op jit(solution)/shard_map/ppermute | solution.py:349
  37.7 1.0 %copy-done.1 = bf16[2,64,1152]{2,1,0:T(8,128)(2,1)S(1)} copy-done((bf16[2,64,1152]{2,1,0:T(8,128)(2,1)S(1)}, bf16[2,64,1152]{2,1,0:T(8,128)(2,1)}, u32[]{:S(2)}) %copy-start.1) | copy-done | bytes 294936
  38.6 1.0 %copy-done.3 = bf16[2,64,1152]{2,1,0:T(8,128)(2,1)S(1)} copy-done((bf16[2,64,1152]{2,1,0:T(8,128)(2,1)S(1)}, bf16[2,64,1152]{2,1,0:T(8,128)(2,1)}, u32[]{:S(2)}) %copy-start.3) | copy-done | bytes 294936
  39.6 1.0 %copy-done.5 = bf16[2,64,1152]{2,1,0:T(8,128)(2,1)S(1)} copy-done((bf16[2,64,1152]{2,1,0:T(8,128)(2,1)S(1)}, bf16[2,64,1152]{2,1,0:T(8,128)(2,1)}, u32[]{:S(2)}) %copy-start.5) | copy-done | bytes 294936
  40.6 1.0 %copy-done.7 = bf16[2,64,1152]{2,1,0:T(8,128)(2,1)S(1)} copy-done((bf16[2,64,1152]{2,1,0:T(8,128)(2,1)S(1)}, bf16[2,64,1152]{2,1,0:T(8,128)(2,1)}, u32[]{:S(2)}) %copy-start.7) | copy-done | bytes 294936
  41.5 1.3 %collect.1.held = bf16[12,64,1152]{2,1,0:T(8,128)(2,1)S(1)} custom-call(bf16[2,64,1152]{2,1,0:T(8,128)(2,1)S(1)} %copy-done.10, bf16[2,64,1152]{2,1,0:T(8,128)(2,1)S(1)} %copy-done.1, bf16[2,64,1152]{2,1,0:T(8,128)(2,1)S(1)} %copy-done.3, bf16[2,64,1152]{2,1,0:T(8,128)(2,1)} %collective-permute-done.2.refs_3_, bf16[2,64,1152]{2,1,0:T(8,128)(2,1)S(1)} %copy-done.7, ...), custom_call_target="tpu_custom_call" | custom-call | tf_op jit(solution)/shard_map/collect/pallas_call | solution.py:240
  42.8 1.4 %collective-permute-done.5.refs_0_ = bf16[2,64,1152]{2,1,0:T(8,128)(2,1)S(1)} collective-permute-done((bf16[2,64,1152]{2,1,0:T(8,128)(2,1)}, bf16[2,64,1152]{2,1,0:T(8,128)(2,1)S(1)}, u32[]{:S(2)}, u32[]{:S(2)}) %collective-permute-start.5) | collective-permute-done | bytes 294944 | tf_op jit(solution)/shard_map/ppermute | solution.py:349
  44.2 0.7 %copy-done.11 = bf16[2,64,1152]{2,1,0:T(8,128)(2,1)} copy-done((bf16[2,64,1152]{2,1,0:T(8,128)(2,1)}, bf16[2,64,1152]{2,1,0:T(8,128)(2,1)S(1)}, u32[]{:S(2)}) %copy-start.11) | copy-done | bytes 294936
  44.9 0.0 collective-permute-done.7.refs_3_
  44.9 0.0 collective-permute-done.8.refs_4_
  44.9 5.4 %collective-permute-done.9.refs_5_ = bf16[400,1024]{1,0:T(8,128)(2,1)S(1)} collective-permute-done((bf16[400,1024]{1,0:T(8,128)(2,1)}, bf16[400,1024]{1,0:T(8,128)(2,1)S(1)}, u32[]{:S(2)}, u32[]{:S(2)}) %collective-permute-start.9) | collective-permute-done | bytes 819232 | tf_op jit(solution)/shard_map/ppermute | solution.py:359
  50.3 0.0 collective-permute-done.6.refs_1_
  50.3 0.0 copy-start.12
  50.3 1.0 %copy-done.12 = bf16[2,64,1152]{2,1,0:T(8,128)(2,1)S(1)} copy-done((bf16[2,64,1152]{2,1,0:T(8,128)(2,1)S(1)}, bf16[2,64,1152]{2,1,0:T(8,128)(2,1)}, u32[]{:S(2)}) %copy-start.12) | copy-done | bytes 294936
  51.3 1.7 %rank.1 = (bf16[3,128,128]{2,1,0:T(8,128)(2,1)S(1)}, bf16[3,128,128]{2,1,0:T(8,128)(2,1)S(1)}, bf16[3,128,128]{2,1,0:T(8,128)(2,1)S(1)}, bf16[3,128,128]{2,1,0:T(8,128)(2,1)S(1)}, f32[8,128]{1,0:T(8,128)S(1)}) custom-call(s32[16]{0:T(128)S(1)} %copy-done.14, bf16[12,64,1152]{2,1,0:T(8,128)(2,1)S(1)} %collect.1.held, bf16[2,64,1152]{2,1,0:T(8,128)(2,1)S(1)} %copy-done.12, ...), custom_call_target="tpu_custom_call" | custom-call | tf_op jit(solution)/shard_map/rank/pallas_call | solution.py:293
  53.0 0.0 copy-start.13
  53.0 0.6 copy-done.13
  53.6 0.5 collective-permute-start.11
  54.1 1.5 %collective-permute-start.12 = (bf16[3,128,128]{2,1,0:T(8,128)(2,1)S(1)}, bf16[3,128,128]{2,1,0:T(8,128)(2,1)S(1)}, u32[]{:S(2)}, u32[]{:S(2)}) collective-permute-start(bf16[3,128,128]{2,1,0:T(8,128)(2,1)S(1)} %get-tuple-element.31), channel_id=1, source_target_pairs={{0,16},{2,18},{16,0},{18,2},{1,17},{3,19},{17,1},{19,3},{4,20},{6,... | collective-permute-start | bytes 294920 | tf_op jit(solution)/shard_map/ppermute | solution.py:359
  55.6 1.5 %collective-permute-start.13 = (bf16[3,128,128]{2,1,0:T(8,128)(2,1)S(1)}, bf16[3,128,128]{2,1,0:T(8,128)(2,1)S(1)}, u32[]{:S(2)}, u32[]{:S(2)}) collective-permute-start(bf16[3,128,128]{2,1,0:T(8,128)(2,1)S(1)} %get-tuple-element.32), channel_id=1, source_target_pairs={{0,18},{2,16},{16,2},{18,0},{1,19},{3,17},{17,3},{19,1},{4,22},{6,... | collective-permute-start | bytes 294920 | tf_op jit(solution)/shard_map/ppermute | solution.py:359
  57.1 0.0 collective-permute-start.14
  57.1 1.7 %collective-permute-done.11.refs_1_ = bf16[3,128,128]{2,1,0:T(8,128)(2,1)S(1)} collective-permute-done((bf16[3,128,128]{2,1,0:T(8,128)(2,1)S(1)}, bf16[3,128,128]{2,1,0:T(8,128)(2,1)S(1)}, u32[]{:S(2)}, u32[]{:S(2)}) %collective-permute-start.11) | collective-permute-done | bytes 98336 | tf_op jit(solution)/shard_map/ppermute | solution.py:359
  58.8 0.0 collective-permute-start.15
  58.8 0.2 collective-permute-done.12.refs_2_
  59.0 0.3 collective-permute-start.16
  59.3 2.8 %collective-permute-done.13.refs_3_ = bf16[3,128,128]{2,1,0:T(8,128)(2,1)S(1)} collective-permute-done((bf16[3,128,128]{2,1,0:T(8,128)(2,1)S(1)}, bf16[3,128,128]{2,1,0:T(8,128)(2,1)S(1)}, u32[]{:S(2)}, u32[]{:S(2)}) %collective-permute-start.13) | collective-permute-done | bytes 98336 | tf_op jit(solution)/shard_map/ppermute | solution.py:359
  62.1 0.0 collective-permute-start.17
  62.1 0.0 collective-permute-done.14.refs_4_
  62.1 0.0 collective-permute-done.15.refs_5_
  62.1 1.3 %collective-permute-done.17.refs_7_ = bf16[3,128,128]{2,1,0:T(8,128)(2,1)S(1)} collective-permute-done((bf16[3,128,128]{2,1,0:T(8,128)(2,1)S(1)}, bf16[3,128,128]{2,1,0:T(8,128)(2,1)S(1)}, u32[]{:S(2)}, u32[]{:S(2)}) %collective-permute-start.17) | collective-permute-done | bytes 98336 | tf_op jit(solution)/shard_map/ppermute | solution.py:346
  63.4 1.1 %final.1 = bf16[384,512]{1,0:T(8,128)(2,1)} custom-call(f32[384,512]{1,0:T(8,128)S(1)} %copy-done.9, f32[384,512]{1,0:T(8,128)S(1)} %collective-permute-done.10.base_b, bf16[3,128,128]{2,1,0:T(8,128)(2,1)S(1)} %get-tuple-element.29.refs_0_, bf16[3,128,128]{2,1,0:T(8,128)(2,1)S(1)} %collective-permute-done.11.refs_1_, ...), custom_call_target="tpu_custom_call" | custom-call | tf_op jit(solution)/shard_map/final/pallas_call | solution.py:327
  (27 shorter events, 0.1 us)
Async XLA Ops:
  1.9 12.2 %collective-permute-start.2 = (bf16[2,64,1152]{2,1,0:T(8,128)(2,1)}, bf16[2,64,1152]{2,1,0:T(8,128)(2,1)}, u32[]{:S(2)}, u32[]{:S(2)}) collective-permute-start(bf16[2,64,1152]{2,1,0:T(8,128)(2,1)} %get-tuple-element.23), channel_id=1, source_target_pairs={{0,2},{2,0},{1,3},{3,1},{4,6},{6,4},{5,7},{7,5},{8,10},{10,8},{9,1... | collective-permute-start | bytes 884744 | tf_op jit(solution)/shard_map/ppermute | solution.py:377
  5.0 12.0 %collective-permute-start.1 = (bf16[2,64,1152]{2,1,0:T(8,128)(2,1)}, bf16[2,64,1152]{2,1,0:T(8,128)(2,1)S(1)}, u32[]{:S(2)}, u32[]{:S(2)}) collective-permute-start(bf16[2,64,1152]{2,1,0:T(8,128)(2,1)} %get-tuple-element.21.refs_0_), channel_id=1, source_target_pairs={{0,4},{4,8},{8,12},{12,0},{1,5},{5,9},{9,13},{13,1},{2,6},{6,10},{... | collective-permute-start | bytes 884744 | tf_op jit(solution)/shard_map/ppermute | solution.py:349
  6.5 15.5 %collective-permute-start = (bf16[2,64,1152]{2,1,0:T(8,128)(2,1)}, bf16[2,64,1152]{2,1,0:T(8,128)(2,1)S(1)}, u32[]{:S(2)}, u32[]{:S(2)}) collective-permute-start(bf16[2,64,1152]{2,1,0:T(8,128)(2,1)} %get-tuple-element.21.refs_0_), channel_id=1, source_target_pairs={{0,12},{4,0},{8,4},{12,8},{1,13},{5,1},{9,5},{13,9},{2,14},{6,2},{... | collective-permute-start | bytes 884744 | tf_op jit(solution)/shard_map/ppermute | solution.py:349
  12.1 32.8 %collective-permute-start.7 = (bf16[400,1024]{1,0:T(8,128)(2,1)}, bf16[400,1024]{1,0:T(8,128)(2,1)S(1)}, u32[]{:S(2)}, u32[]{:S(2)}) collective-permute-start(bf16[400,1024]{1,0:T(8,128)(2,1)} %get-tuple-element.25), channel_id=1, source_target_pairs={{0,2},{2,0},{16,18},{18,16},{1,3},{3,1},{17,19},{19,17},{4,6},{6,4... | collective-permute-start | bytes 2457608 | tf_op jit(solution)/shard_map/ppermute | solution.py:359
  12.4 32.4 %collective-permute-start.8 = (bf16[400,1024]{1,0:T(8,128)(2,1)}, bf16[400,1024]{1,0:T(8,128)(2,1)S(1)}, u32[]{:S(2)}, u32[]{:S(2)}) collective-permute-start(bf16[400,1024]{1,0:T(8,128)(2,1)} %get-tuple-element.26), channel_id=1, source_target_pairs={{0,16},{2,18},{16,0},{18,2},{1,17},{3,19},{17,1},{19,3},{4,20},{6,... | collective-permute-start | bytes 2457608 | tf_op jit(solution)/shard_map/ppermute | solution.py:359
  14.2 23.5 %copy-start.10 = (bf16[2,64,1152]{2,1,0:T(8,128)(2,1)S(1)}, bf16[2,64,1152]{2,1,0:T(8,128)(2,1)}, u32[]{:S(2)}) copy-start(bf16[2,64,1152]{2,1,0:T(8,128)(2,1)} %get-tuple-element.21.refs_0_) | copy-start | bytes 884740
  14.2 36.1 %collective-permute-start.9 = (bf16[400,1024]{1,0:T(8,128)(2,1)}, bf16[400,1024]{1,0:T(8,128)(2,1)S(1)}, u32[]{:S(2)}, u32[]{:S(2)}) collective-permute-start(bf16[400,1024]{1,0:T(8,128)(2,1)} %get-tuple-element.27), channel_id=1, source_target_pairs={{0,18},{2,16},{16,2},{18,0},{1,19},{3,17},{17,3},{19,1},{4,22},{6,... | collective-permute-start | bytes 2457608 | tf_op jit(solution)/shard_map/ppermute | solution.py:359
  16.9 16.0 %copy-start.2 = (bf16[2,64,1152]{2,1,0:T(8,128)(2,1)}, bf16[2,64,1152]{2,1,0:T(8,128)(2,1)S(1)}, u32[]{:S(2)}) copy-start(bf16[2,64,1152]{2,1,0:T(8,128)(2,1)S(1)} %collective-permute-done.1.refs_0_) | copy-start | bytes 884740
  17.0 16.0 %collective-permute-start.4 = (bf16[2,64,1152]{2,1,0:T(8,128)(2,1)}, bf16[2,64,1152]{2,1,0:T(8,128)(2,1)S(1)}, u32[]{:S(2)}, u32[]{:S(2)}) collective-permute-start(bf16[2,64,1152]{2,1,0:T(8,128)(2,1)} %collective-permute-done.2.refs_3_), channel_id=1, source_target_pairs={{0,4},{4,8},{8,12},{12,0},{1,5},{5,9},{9,13},{13,1},{2,6},{6,10},{... | collective-permute-start | bytes 884744 | tf_op jit(solution)/shard_map/ppermute | solution.py:349
  22.1 10.9 %copy-start = (bf16[2,64,1152]{2,1,0:T(8,128)(2,1)}, bf16[2,64,1152]{2,1,0:T(8,128)(2,1)S(1)}, u32[]{:S(2)}) copy-start(bf16[2,64,1152]{2,1,0:T(8,128)(2,1)S(1)} %collective-permute-done.refs_1_) | copy-start | bytes 884740
  22.1 12.5 %collective-permute-start.3 = (bf16[2,64,1152]{2,1,0:T(8,128)(2,1)}, bf16[2,64,1152]{2,1,0:T(8,128)(2,1)S(1)}, u32[]{:S(2)}, u32[]{:S(2)}) collective-permute-start(bf16[2,64,1152]{2,1,0:T(8,128)(2,1)} %collective-permute-done.2.refs_3_), channel_id=1, source_target_pairs={{0,12},{4,0},{8,4},{12,8},{1,13},{5,1},{9,5},{13,9},{2,14},{6,2},{... | collective-permute-start | bytes 884744 | tf_op jit(solution)/shard_map/ppermute | solution.py:349
  32.9 17.4 %copy-start.14 = (s32[16]{0:T(128)S(1)}, s32[16]{0:T(128)}, u32[]{:S(2)}) copy-start(s32[16]{0:T(128)} %owner.1) | copy-start | bytes 196
  33.0 1.5 %copy-start.4 = (bf16[2,64,1152]{2,1,0:T(8,128)(2,1)}, bf16[2,64,1152]{2,1,0:T(8,128)(2,1)S(1)}, u32[]{:S(2)}) copy-start(bf16[2,64,1152]{2,1,0:T(8,128)(2,1)S(1)} %collective-permute-done.4.refs_1_.refs_5_) | copy-start | bytes 884740
  33.0 11.2 %collective-permute-start.5 = (bf16[2,64,1152]{2,1,0:T(8,128)(2,1)}, bf16[2,64,1152]{2,1,0:T(8,128)(2,1)S(1)}, u32[]{:S(2)}, u32[]{:S(2)}) collective-permute-start(bf16[2,64,1152]{2,1,0:T(8,128)(2,1)} %hand.3.refs_2_), channel_id=1, source_target_pairs={{0,4},{4,8},{8,12},{12,0},{1,5},{5,9},{9,13},{13,1},{2,6},{6,10},{... | collective-permute-start | bytes 884744 | tf_op jit(solution)/shard_map/ppermute | solution.py:349
  34.5 0.7 %copy-start.6 = (bf16[2,64,1152]{2,1,0:T(8,128)(2,1)}, bf16[2,64,1152]{2,1,0:T(8,128)(2,1)S(1)}, u32[]{:S(2)}) copy-start(bf16[2,64,1152]{2,1,0:T(8,128)(2,1)S(1)} %collective-permute-done.3.refs_0_) | copy-start | bytes 884740
  35.2 15.1 %collective-permute-start.6 = (bf16[2,64,1152]{2,1,0:T(8,128)(2,1)}, bf16[2,64,1152]{2,1,0:T(8,128)(2,1)S(1)}, u32[]{:S(2)}, u32[]{:S(2)}) collective-permute-start(bf16[2,64,1152]{2,1,0:T(8,128)(2,1)} %hand.4.refs_4_), channel_id=1, source_target_pairs={{0,12},{4,0},{8,4},{12,8},{1,13},{5,1},{9,5},{13,9},{2,14},{6,2},{... | collective-permute-start | bytes 884744 | tf_op jit(solution)/shard_map/ppermute | solution.py:349
  37.7 1.0 %copy-start.1 = (bf16[2,64,1152]{2,1,0:T(8,128)(2,1)S(1)}, bf16[2,64,1152]{2,1,0:T(8,128)(2,1)}, u32[]{:S(2)}) copy-start(bf16[2,64,1152]{2,1,0:T(8,128)(2,1)} %copy-done) | copy-start | bytes 884740
  38.6 1.0 %copy-start.3 = (bf16[2,64,1152]{2,1,0:T(8,128)(2,1)S(1)}, bf16[2,64,1152]{2,1,0:T(8,128)(2,1)}, u32[]{:S(2)}) copy-start(bf16[2,64,1152]{2,1,0:T(8,128)(2,1)} %hand.3.refs_2_) | copy-start | bytes 884740
  39.6 1.0 %copy-start.5 = (bf16[2,64,1152]{2,1,0:T(8,128)(2,1)S(1)}, bf16[2,64,1152]{2,1,0:T(8,128)(2,1)}, u32[]{:S(2)}) copy-start(bf16[2,64,1152]{2,1,0:T(8,128)(2,1)} %copy-done.4) | copy-start | bytes 884740
  40.5 1.0 %copy-start.7 = (bf16[2,64,1152]{2,1,0:T(8,128)(2,1)S(1)}, bf16[2,64,1152]{2,1,0:T(8,128)(2,1)}, u32[]{:S(2)}) copy-start(bf16[2,64,1152]{2,1,0:T(8,128)(2,1)} %hand.4.refs_4_) | copy-start | bytes 884740
  41.5 8.8 %copy-start.8 = (bf16[400,1024]{1,0:T(8,128)(2,1)S(1)}, bf16[400,1024]{1,0:T(8,128)(2,1)}, u32[]{:S(2)}) copy-start(bf16[400,1024]{1,0:T(8,128)(2,1)} %get-tuple-element.24.refs_2_) | copy-start | bytes 2457604
  44.2 0.7 %copy-start.11 = (bf16[2,64,1152]{2,1,0:T(8,128)(2,1)}, bf16[2,64,1152]{2,1,0:T(8,128)(2,1)S(1)}, u32[]{:S(2)}) copy-start(bf16[2,64,1152]{2,1,0:T(8,128)(2,1)S(1)} %collective-permute-done.5.refs_0_) | copy-start | bytes 884740
  50.3 1.0 %copy-start.12 = (bf16[2,64,1152]{2,1,0:T(8,128)(2,1)S(1)}, bf16[2,64,1152]{2,1,0:T(8,128)(2,1)}, u32[]{:S(2)}) copy-start(bf16[2,64,1152]{2,1,0:T(8,128)(2,1)} %copy-done.11) | copy-start | bytes 884740
  51.3 12.1 %copy-start.9 = (f32[384,512]{1,0:T(8,128)S(1)}, f32[384,512]{1,0:T(8,128)}, u32[]{:S(2)}) copy-start(f32[384,512]{1,0:T(8,128)} %get-tuple-element.19.base_a) | copy-start | bytes 2359300
  53.0 0.6 copy-start.13
  53.6 9.8 %collective-permute-start.10 = (f32[384,512]{1,0:T(8,128)}, f32[384,512]{1,0:T(8,128)S(1)}, u32[]{:S(2)}, u32[]{:S(2)}) collective-permute-start(f32[384,512]{1,0:T(8,128)} %hand.5), channel_id=1, source_target_pairs={{0,1},{1,0},{2,3},{3,2},{4,5},{5,4},{6,7},{7,6},{8,9},{9,8},{10,11... | collective-permute-start | bytes 2359304 | tf_op jit(solution)/shard_map/ppermute | solution.py:346
  53.6 5.2 %collective-permute-start.11 = (bf16[3,128,128]{2,1,0:T(8,128)(2,1)S(1)}, bf16[3,128,128]{2,1,0:T(8,128)(2,1)S(1)}, u32[]{:S(2)}, u32[]{:S(2)}) collective-permute-start(bf16[3,128,128]{2,1,0:T(8,128)(2,1)S(1)} %get-tuple-element.30), channel_id=1, source_target_pairs={{0,2},{2,0},{16,18},{18,16},{1,3},{3,1},{17,19},{19,17},{4,6},{6,4... | collective-permute-start | bytes 294920 | tf_op jit(solution)/shard_map/ppermute | solution.py:359
  54.1 4.9 %collective-permute-start.12 = (bf16[3,128,128]{2,1,0:T(8,128)(2,1)S(1)}, bf16[3,128,128]{2,1,0:T(8,128)(2,1)S(1)}, u32[]{:S(2)}, u32[]{:S(2)}) collective-permute-start(bf16[3,128,128]{2,1,0:T(8,128)(2,1)S(1)} %get-tuple-element.31), channel_id=1, source_target_pairs={{0,16},{2,18},{16,0},{18,2},{1,17},{3,19},{17,1},{19,3},{4,20},{6,... | collective-permute-start | bytes 294920 | tf_op jit(solution)/shard_map/ppermute | solution.py:359
  55.6 6.5 %collective-permute-start.13 = (bf16[3,128,128]{2,1,0:T(8,128)(2,1)S(1)}, bf16[3,128,128]{2,1,0:T(8,128)(2,1)S(1)}, u32[]{:S(2)}, u32[]{:S(2)}) collective-permute-start(bf16[3,128,128]{2,1,0:T(8,128)(2,1)S(1)} %get-tuple-element.32), channel_id=1, source_target_pairs={{0,18},{2,16},{16,2},{18,0},{1,19},{3,17},{17,3},{19,1},{4,22},{6,... | collective-permute-start | bytes 294920 | tf_op jit(solution)/shard_map/ppermute | solution.py:359
  57.1 5.0 %collective-permute-start.14 = (bf16[3,128,128]{2,1,0:T(8,128)(2,1)S(1)}, bf16[3,128,128]{2,1,0:T(8,128)(2,1)S(1)}, u32[]{:S(2)}, u32[]{:S(2)}) collective-permute-start(bf16[3,128,128]{2,1,0:T(8,128)(2,1)S(1)} %get-tuple-element.29.refs_0_), channel_id=1, source_target_pairs={{0,1},{1,0},{2,3},{3,2},{4,5},{5,4},{6,7},{7,6},{8,9},{9,8},{10,11... | collective-permute-start | bytes 294920 | tf_op jit(solution)/shard_map/ppermute | solution.py:346
  58.8 3.3 %collective-permute-start.15 = (bf16[3,128,128]{2,1,0:T(8,128)(2,1)S(1)}, bf16[3,128,128]{2,1,0:T(8,128)(2,1)S(1)}, u32[]{:S(2)}, u32[]{:S(2)}) collective-permute-start(bf16[3,128,128]{2,1,0:T(8,128)(2,1)S(1)} %collective-permute-done.11.refs_1_), channel_id=1, source_target_pairs={{0,1},{1,0},{2,3},{3,2},{4,5},{5,4},{6,7},{7,6},{8,9},{9,8},{10,11... | collective-permute-start | bytes 294920 | tf_op jit(solution)/shard_map/ppermute | solution.py:346
  59.0 3.1 %collective-permute-start.16 = (bf16[3,128,128]{2,1,0:T(8,128)(2,1)S(1)}, bf16[3,128,128]{2,1,0:T(8,128)(2,1)S(1)}, u32[]{:S(2)}, u32[]{:S(2)}) collective-permute-start(bf16[3,128,128]{2,1,0:T(8,128)(2,1)S(1)} %collective-permute-done.12.refs_2_), channel_id=1, source_target_pairs={{0,1},{1,0},{2,3},{3,2},{4,5},{5,4},{6,7},{7,6},{8,9},{9,8},{10,11... | collective-permute-start | bytes 294920 | tf_op jit(solution)/shard_map/ppermute | solution.py:346
  62.1 1.3 %collective-permute-start.17 = (bf16[3,128,128]{2,1,0:T(8,128)(2,1)S(1)}, bf16[3,128,128]{2,1,0:T(8,128)(2,1)S(1)}, u32[]{:S(2)}, u32[]{:S(2)}) collective-permute-start(bf16[3,128,128]{2,1,0:T(8,128)(2,1)S(1)} %collective-permute-done.13.refs_3_), channel_id=1, source_target_pairs={{0,1},{1,0},{2,3},{3,2},{4,5},{5,4},{6,7},{7,6},{8,9},{9,8},{10,11... | collective-permute-start | bytes 294920 | tf_op jit(solution)/shard_map/ppermute | solution.py:346

commit v33 on v31

--- a/solution.py
+++ b/solution.py
@@ -273,8 +273,7 @@
             half = ring // 2
             near = jnp.where(away == half, 0, away - jnp.where(away > half, 1, 0))
             piece = held[(way * (ring - 1) + near) * per + local]
-            for w in range(pair):
-                piece = jnp.where((away == half) & (way == w), late[w][local], piece)
+            piece = jnp.where(away == half, late[0][way * per + local], piece)
         else:
             piece = held[(way * ring + away) * per + local]
         k, b = i // blocks, i % blocks
@@ -388,7 +387,7 @@
 
     halfway = ring // 2 if ring % 2 == 0 else ring
     held = collect([piece for way in pieces for away, piece in enumerate(way) if away != halfway])
-    late = [way[halfway] for way in pieces] if halfway < ring else []
+    late = [collect([way[halfway] for way in pieces])] if halfway < ring else []
     *parts, ready = rank_parts(owner_slot, toks, held, late, ring, pair, rows, blocks)
     mine = [parts[0]] + [in_plane(parts[k], -(k // pair), -(k % pair)) for k in range(1, shares)]
     theirs = [across(part) for part in mine]

time: 64.8 us -> 65 us (level)
  waiting for transfers between devices: 19.9 us -> 20.6 us
    ppermute x6, waiting for transfers between devices: 8.51 us -> 12 us  [along(): lax.ppermute(x, 'ring', [(a, (a + step) % ring) for a in range(ring)])]
    ppermute x6, waiting for transfers between devices: 10.1 us -> 7.31 us  [in_plane(): return lax.ppermute(x, PLANE, pairs)]
    unnamed x30 -> x26, local copies, waits for them, and re-layouts: 6.87 us -> 6.33 us
    pallas_call x1 -> x2, Pallas kernels: 1.26 us -> 1.33 us  [collect(): pl.pallas_call(collect_kernel, in_specs=[ANY] * len(pieces), out_specs=VM...]
  transfers between devices with their start and end apart: 18 -> 18, of which waited for: 9 -> 10; matrix products, arithmetic and copies ran while one was open for 0% -> 0% of each run, Pallas kernels for 20% -> 20%
where the time goes in v33:
time: 65 us; the launch traced here: 64.6 us
  waiting for transfers between devices  20.6 us (32%)
  starting transfers between devices  20.2 us (31%)
  Pallas kernels  17.3 us (27%)
  local copies, waits for them, and re-layouts  6.33 us (10%)
    ppermute x6, waiting for transfers between devices, along(): lax.ppermute(x, 'ring', [(a, (a + step) % ring) for a in range(ring)])  12 us
    ppermute x6, starting transfers between devices, along(): lax.ppermute(x, 'ring', [(a, (a + step) % ring) for a in range(ring)])  9.85 us
    pallas_call x1, Pallas kernels, base_halves(): pl.pallas_call(functools.partial(base_kernel, sides, groups, pair), in_sp...  8.04 us
    ppermute x6, waiting for transfers between devices, in_plane(): return lax.ppermute(x, PLANE, pairs)  7.31 us
    ppermute x6, starting transfers between devices, in_plane(): return lax.ppermute(x, PLANE, pairs)  7.04 us
    unnamed x26, local copies, waits for them, and re-layouts  6.33 us
    pallas_call x1, Pallas kernels, spread(): pl.pallas_call(functools.partial(spread_kernel, groups, pair), in_specs=[...  3.29 us
    ppermute x1, starting transfers between devices, body(): lax.ppermute(packed[pair - w], 'pair', [(a, (a - w) % pair) for a in rang...  3.03 us
  transfers between devices with their start and end apart: 18, of which 10 were waited for; matrix products, arithmetic and copies ran while one was open for 0% of the time, Pallas kernels for 20%

profile of v33, /device:TPU:0, one launch (start us, length us, event | category | flops | bytes accessed | tf_op | source)
XLA Modules:
  0.0 64.6 jit_solution(912240689024016876)
XLA Ops:
  0.0 1.9 %pack.1 = (bf16[2,64,1152]{2,1,0:T(8,128)(2,1)}, bf16[2,64,1152]{2,1,0:T(8,128)(2,1)}) custom-call(bf16[2,64,4096]{2,1,0:T(8,128)(2,1)} %bitcast.2, bf16[2,64,512]{2,1,0:T(8,128)(2,1)} %up.1), custom_call_target="tpu_custom_call" | custom-call | tf_op jit(solution)/shard_map/pack/pallas_call | solution.py:57
  1.9 3.0 %collective-permute-start.2 = (bf16[2,64,1152]{2,1,0:T(8,128)(2,1)}, bf16[2,64,1152]{2,1,0:T(8,128)(2,1)}, u32[]{:S(2)}, u32[]{:S(2)}) collective-permute-start(bf16[2,64,1152]{2,1,0:T(8,128)(2,1)} %get-tuple-element.23), channel_id=1, source_target_pairs={{0,2},{2,0},{1,3},{3,1},{4,6},{6,4},{5,7},{7,5},{8,10},{10,8},{9,1... | collective-permute-start | bytes 884744 | tf_op jit(solution)/shard_map/ppermute | solution.py:376
  4.9 1.6 %collective-permute-start.1 = (bf16[2,64,1152]{2,1,0:T(8,128)(2,1)}, bf16[2,64,1152]{2,1,0:T(8,128)(2,1)S(1)}, u32[]{:S(2)}, u32[]{:S(2)}) collective-permute-start(bf16[2,64,1152]{2,1,0:T(8,128)(2,1)} %get-tuple-element.21.refs_0_), channel_id=1, source_target_pairs={{0,4},{4,8},{8,12},{12,0},{1,5},{5,9},{9,13},{13,1},{2,6},{6,10},{... | collective-permute-start | bytes 884744 | tf_op jit(solution)/shard_map/ppermute | solution.py:348
  6.5 2.2 %collective-permute-start = (bf16[2,64,1152]{2,1,0:T(8,128)(2,1)}, bf16[2,64,1152]{2,1,0:T(8,128)(2,1)S(1)}, u32[]{:S(2)}, u32[]{:S(2)}) collective-permute-start(bf16[2,64,1152]{2,1,0:T(8,128)(2,1)} %get-tuple-element.21.refs_0_), channel_id=1, source_target_pairs={{0,12},{4,0},{8,4},{12,8},{1,13},{5,1},{9,5},{13,9},{2,14},{6,2},{... | collective-permute-start | bytes 884744 | tf_op jit(solution)/shard_map/ppermute | solution.py:348
  8.8 3.3 %spread.1 = (bf16[400,1024]{1,0:T(8,128)(2,1)}, bf16[400,1024]{1,0:T(8,128)(2,1)}, bf16[400,1024]{1,0:T(8,128)(2,1)}) custom-call(s32[3]{0:T(128)} %lengths.3, s32[3]{0:T(128)} %bitcast.3, bf16[384,4096]{1,0:T(8,128)(2,1)} %tok.3), custom_call_target="tpu_custom_call" | custom-call | tf_op jit(solution)/shard_map/spread/pallas_call | solution.py:131
  12.1 0.4 collective-permute-start.7
  12.4 1.7 %collective-permute-start.8 = (bf16[400,1024]{1,0:T(8,128)(2,1)}, bf16[400,1024]{1,0:T(8,128)(2,1)S(1)}, u32[]{:S(2)}, u32[]{:S(2)}) collective-permute-start(bf16[400,1024]{1,0:T(8,128)(2,1)} %get-tuple-element.26), channel_id=1, source_target_pairs={{0,16},{2,18},{16,0},{18,2},{1,17},{3,19},{17,1},{19,3},{4,20},{6,... | collective-permute-start | bytes 2457608 | tf_op jit(solution)/shard_map/ppermute | solution.py:358
  14.1 0.0 collective-permute-done.2.refs_3_
  14.1 1.5 %collective-permute-start.9 = (bf16[400,1024]{1,0:T(8,128)(2,1)}, bf16[400,1024]{1,0:T(8,128)(2,1)S(1)}, u32[]{:S(2)}, u32[]{:S(2)}) collective-permute-start(bf16[400,1024]{1,0:T(8,128)(2,1)} %get-tuple-element.27), channel_id=1, source_target_pairs={{0,18},{2,16},{16,2},{18,0},{1,19},{3,17},{17,3},{19,1},{4,22},{6,... | collective-permute-start | bytes 2457608 | tf_op jit(solution)/shard_map/ppermute | solution.py:358
  15.6 1.3 %collective-permute-done.1.refs_0_ = bf16[2,64,1152]{2,1,0:T(8,128)(2,1)S(1)} collective-permute-done((bf16[2,64,1152]{2,1,0:T(8,128)(2,1)}, bf16[2,64,1152]{2,1,0:T(8,128)(2,1)S(1)}, u32[]{:S(2)}, u32[]{:S(2)}) %collective-permute-start.1) | collective-permute-done | bytes 294944 | tf_op jit(solution)/shard_map/ppermute | solution.py:348
  16.9 0.7 %collective-permute-start.4 = (bf16[2,64,1152]{2,1,0:T(8,128)(2,1)}, bf16[2,64,1152]{2,1,0:T(8,128)(2,1)S(1)}, u32[]{:S(2)}, u32[]{:S(2)}) collective-permute-start(bf16[2,64,1152]{2,1,0:T(8,128)(2,1)} %collective-permute-done.2.refs_3_), channel_id=1, source_target_pairs={{0,4},{4,8},{8,12},{12,0},{1,5},{5,9},{9,13},{13,1},{2,6},{6,10},{... | collective-permute-start | bytes 884744 | tf_op jit(solution)/shard_map/ppermute | solution.py:348
  17.7 4.4 %collective-permute-done.refs_1_ = bf16[2,64,1152]{2,1,0:T(8,128)(2,1)S(1)} collective-permute-done((bf16[2,64,1152]{2,1,0:T(8,128)(2,1)}, bf16[2,64,1152]{2,1,0:T(8,128)(2,1)S(1)}, u32[]{:S(2)}, u32[]{:S(2)}) %collective-permute-start) | collective-permute-done | bytes 294944 | tf_op jit(solution)/shard_map/ppermute | solution.py:348
  22.0 2.8 %collective-permute-start.3 = (bf16[2,64,1152]{2,1,0:T(8,128)(2,1)}, bf16[2,64,1152]{2,1,0:T(8,128)(2,1)S(1)}, u32[]{:S(2)}, u32[]{:S(2)}) collective-permute-start(bf16[2,64,1152]{2,1,0:T(8,128)(2,1)} %collective-permute-done.2.refs_3_), channel_id=1, source_target_pairs={{0,12},{4,0},{8,4},{12,8},{1,13},{5,1},{9,5},{13,9},{2,14},{6,2},{... | collective-permute-start | bytes 884744 | tf_op jit(solution)/shard_map/ppermute | solution.py:348
  24.8 8.0 %base.1 = (f32[384,512]{1,0:T(8,128)}, f32[384,512]{1,0:T(8,128)}, f32[8,128]{1,0:T(8,128)}, bf16[400,1024]{1,0:T(8,128)(2,1)}) custom-call(s32[3]{0:T(128)} %lengths.3, s32[3]{0:T(128)} %bitcast.4, bf16[384,4096]{1,0:T(8,128)(2,1)} %tok.3, bf16[4096,1024]{1,0:T(8,128)(2,1)} %key.1), custom_call_target="tpu_custom_call" | custom-call | tf_op jit(solution)/shard_map/base/pallas_call | solution.py:203
  32.9 0.0 copy-start.12
  32.9 0.0 collective-permute-done.4.refs_1_.refs_5_
  32.9 0.1 collective-permute-start.5
  33.0 1.5 %collective-permute-done.3.refs_0_ = bf16[2,64,1152]{2,1,0:T(8,128)(2,1)S(1)} collective-permute-done((bf16[2,64,1152]{2,1,0:T(8,128)(2,1)}, bf16[2,64,1152]{2,1,0:T(8,128)(2,1)S(1)}, u32[]{:S(2)}, u32[]{:S(2)}) %collective-permute-start.3) | collective-permute-done | bytes 294944 | tf_op jit(solution)/shard_map/ppermute | solution.py:348
  34.5 0.7 %copy-done.6 = bf16[2,64,1152]{2,1,0:T(8,128)(2,1)} copy-done((bf16[2,64,1152]{2,1,0:T(8,128)(2,1)}, bf16[2,64,1152]{2,1,0:T(8,128)(2,1)S(1)}, u32[]{:S(2)}) %copy-start.6) | copy-done | bytes 294936
  35.2 2.4 %collective-permute-start.6 = (bf16[2,64,1152]{2,1,0:T(8,128)(2,1)}, bf16[2,64,1152]{2,1,0:T(8,128)(2,1)S(1)}, u32[]{:S(2)}, u32[]{:S(2)}) collective-permute-start(bf16[2,64,1152]{2,1,0:T(8,128)(2,1)} %hand.4.refs_4_), channel_id=1, source_target_pairs={{0,12},{4,0},{8,4},{12,8},{1,13},{5,1},{9,5},{13,9},{2,14},{6,2},{... | collective-permute-start | bytes 884744 | tf_op jit(solution)/shard_map/ppermute | solution.py:348
  37.6 1.0 %copy-done.1 = bf16[2,64,1152]{2,1,0:T(8,128)(2,1)S(1)} copy-done((bf16[2,64,1152]{2,1,0:T(8,128)(2,1)S(1)}, bf16[2,64,1152]{2,1,0:T(8,128)(2,1)}, u32[]{:S(2)}) %copy-start.1) | copy-done | bytes 294936
  38.6 1.0 %copy-done.3 = bf16[2,64,1152]{2,1,0:T(8,128)(2,1)S(1)} copy-done((bf16[2,64,1152]{2,1,0:T(8,128)(2,1)S(1)}, bf16[2,64,1152]{2,1,0:T(8,128)(2,1)}, u32[]{:S(2)}) %copy-start.3) | copy-done | bytes 294936
  39.6 1.0 %copy-done.5 = bf16[2,64,1152]{2,1,0:T(8,128)(2,1)S(1)} copy-done((bf16[2,64,1152]{2,1,0:T(8,128)(2,1)S(1)}, bf16[2,64,1152]{2,1,0:T(8,128)(2,1)}, u32[]{:S(2)}) %copy-start.5) | copy-done | bytes 294936
  40.5 1.0 %copy-done.7 = bf16[2,64,1152]{2,1,0:T(8,128)(2,1)S(1)} copy-done((bf16[2,64,1152]{2,1,0:T(8,128)(2,1)S(1)}, bf16[2,64,1152]{2,1,0:T(8,128)(2,1)}, u32[]{:S(2)}) %copy-start.7) | copy-done | bytes 294936
  41.5 1.2 %collect.2.held = bf16[12,64,1152]{2,1,0:T(8,128)(2,1)S(1)} custom-call(bf16[2,64,1152]{2,1,0:T(8,128)(2,1)S(1)} %copy-done.10, bf16[2,64,1152]{2,1,0:T(8,128)(2,1)S(1)} %copy-done.1, bf16[2,64,1152]{2,1,0:T(8,128)(2,1)S(1)} %copy-done.3, bf16[2,64,1152]{2,1,0:T(8,128)(2,1)} %collective-permute-done.2.refs_3_, bf16[2,64,1152]{2,1,0:T(8,128)(2,1)S(1)} %copy-done.7, ...), custom_call_target="tpu_custom_call" | custom-call | tf_op jit(solution)/shard_map/collect/pallas_call | solution.py:240
  42.7 1.4 %collective-permute-done.5.refs_0_ = bf16[2,64,1152]{2,1,0:T(8,128)(2,1)S(1)} collective-permute-done((bf16[2,64,1152]{2,1,0:T(8,128)(2,1)}, bf16[2,64,1152]{2,1,0:T(8,128)(2,1)S(1)}, u32[]{:S(2)}, u32[]{:S(2)}) %collective-permute-start.5) | collective-permute-done | bytes 294944 | tf_op jit(solution)/shard_map/ppermute | solution.py:348
  44.1 3.4 %collective-permute-done.6.refs_1_ = bf16[2,64,1152]{2,1,0:T(8,128)(2,1)S(1)} collective-permute-done((bf16[2,64,1152]{2,1,0:T(8,128)(2,1)}, bf16[2,64,1152]{2,1,0:T(8,128)(2,1)S(1)}, u32[]{:S(2)}, u32[]{:S(2)}) %collective-permute-start.6) | collective-permute-done | bytes 294944 | tf_op jit(solution)/shard_map/ppermute | solution.py:348
  47.5 0.1 collect.3.refs_0_
  47.7 0.0 collective-permute-done.7.refs_2_
  47.7 2.6 %collective-permute-done.9.refs_4_ = bf16[400,1024]{1,0:T(8,128)(2,1)S(1)} collective-permute-done((bf16[400,1024]{1,0:T(8,128)(2,1)}, bf16[400,1024]{1,0:T(8,128)(2,1)S(1)}, u32[]{:S(2)}, u32[]{:S(2)}) %collective-permute-start.9) | collective-permute-done | bytes 819232 | tf_op jit(solution)/shard_map/ppermute | solution.py:358
  50.3 1.1 %copy-done.8 = bf16[400,1024]{1,0:T(8,128)(2,1)S(1)} copy-done((bf16[400,1024]{1,0:T(8,128)(2,1)S(1)}, bf16[400,1024]{1,0:T(8,128)(2,1)}, u32[]{:S(2)}) %copy-start.8) | copy-done | bytes 819224
  51.4 1.7 %rank.1 = (bf16[3,128,128]{2,1,0:T(8,128)(2,1)S(1)}, bf16[3,128,128]{2,1,0:T(8,128)(2,1)S(1)}, bf16[3,128,128]{2,1,0:T(8,128)(2,1)S(1)}, bf16[3,128,128]{2,1,0:T(8,128)(2,1)S(1)}, f32[8,128]{1,0:T(8,128)S(1)}) custom-call(s32[16]{0:T(128)S(1)} %copy-done.12, bf16[12,64,1152]{2,1,0:T(8,128)(2,1)S(1)} %collect.2.held, ...), custom_call_target="tpu_custom_call" | custom-call | tf_op jit(solution)/shard_map/rank/pallas_call | solution.py:292
  53.1 0.0 copy-start.11
  53.1 0.6 copy-done.11
  53.7 0.0 collective-permute-start.10
  53.7 0.5 collective-permute-start.11
  54.2 1.5 %collective-permute-start.12 = (bf16[3,128,128]{2,1,0:T(8,128)(2,1)S(1)}, bf16[3,128,128]{2,1,0:T(8,128)(2,1)S(1)}, u32[]{:S(2)}, u32[]{:S(2)}) collective-permute-start(bf16[3,128,128]{2,1,0:T(8,128)(2,1)S(1)} %get-tuple-element.31), channel_id=1, source_target_pairs={{0,16},{2,18},{16,0},{18,2},{1,17},{3,19},{17,1},{19,3},{4,20},{6,... | collective-permute-start | bytes 294920 | tf_op jit(solution)/shard_map/ppermute | solution.py:358
  55.7 1.5 %collective-permute-start.13 = (bf16[3,128,128]{2,1,0:T(8,128)(2,1)S(1)}, bf16[3,128,128]{2,1,0:T(8,128)(2,1)S(1)}, u32[]{:S(2)}, u32[]{:S(2)}) collective-permute-start(bf16[3,128,128]{2,1,0:T(8,128)(2,1)S(1)} %get-tuple-element.32), channel_id=1, source_target_pairs={{0,18},{2,16},{16,2},{18,0},{1,19},{3,17},{17,3},{19,1},{4,22},{6,... | collective-permute-start | bytes 294920 | tf_op jit(solution)/shard_map/ppermute | solution.py:358
  57.2 1.7 %collective-permute-done.11.refs_1_ = bf16[3,128,128]{2,1,0:T(8,128)(2,1)S(1)} collective-permute-done((bf16[3,128,128]{2,1,0:T(8,128)(2,1)S(1)}, bf16[3,128,128]{2,1,0:T(8,128)(2,1)S(1)}, u32[]{:S(2)}, u32[]{:S(2)}) %collective-permute-start.11) | collective-permute-done | bytes 98336 | tf_op jit(solution)/shard_map/ppermute | solution.py:358
  58.9 0.2 collective-permute-done.12.refs_2_
  59.2 0.3 collective-permute-start.16
  59.5 2.8 %collective-permute-done.13.refs_3_ = bf16[3,128,128]{2,1,0:T(8,128)(2,1)S(1)} collective-permute-done((bf16[3,128,128]{2,1,0:T(8,128)(2,1)S(1)}, bf16[3,128,128]{2,1,0:T(8,128)(2,1)S(1)}, u32[]{:S(2)}, u32[]{:S(2)}) %collective-permute-start.13) | collective-permute-done | bytes 98336 | tf_op jit(solution)/shard_map/ppermute | solution.py:358
  62.2 0.0 collective-permute-start.17
  62.2 0.0 collective-permute-done.14.refs_4_
  62.2 0.0 collective-permute-done.15.refs_5_
  62.2 0.0 collective-permute-done.16.refs_6_
  62.3 1.3 %collective-permute-done.17.refs_7_ = bf16[3,128,128]{2,1,0:T(8,128)(2,1)S(1)} collective-permute-done((bf16[3,128,128]{2,1,0:T(8,128)(2,1)S(1)}, bf16[3,128,128]{2,1,0:T(8,128)(2,1)S(1)}, u32[]{:S(2)}, u32[]{:S(2)}) %collective-permute-start.17) | collective-permute-done | bytes 98336 | tf_op jit(solution)/shard_map/ppermute | solution.py:345
  63.5 1.1 %final.1 = bf16[384,512]{1,0:T(8,128)(2,1)} custom-call(f32[384,512]{1,0:T(8,128)S(1)} %copy-done.9, f32[384,512]{1,0:T(8,128)S(1)} %collective-permute-done.10.base_b, bf16[3,128,128]{2,1,0:T(8,128)(2,1)S(1)} %get-tuple-element.29.refs_0_, bf16[3,128,128]{2,1,0:T(8,128)(2,1)S(1)} %collective-permute-done.11.refs_1_, ...), custom_call_target="tpu_custom_call" | custom-call | tf_op jit(solution)/shard_map/final/pallas_call | solution.py:326
  (24 shorter events, 0.0 us)
Async XLA Ops:
  1.9 12.2 %collective-permute-start.2 = (bf16[2,64,1152]{2,1,0:T(8,128)(2,1)}, bf16[2,64,1152]{2,1,0:T(8,128)(2,1)}, u32[]{:S(2)}, u32[]{:S(2)}) collective-permute-start(bf16[2,64,1152]{2,1,0:T(8,128)(2,1)} %get-tuple-element.23), channel_id=1, source_target_pairs={{0,2},{2,0},{1,3},{3,1},{4,6},{6,4},{5,7},{7,5},{8,10},{10,8},{9,1... | collective-permute-start | bytes 884744 | tf_op jit(solution)/shard_map/ppermute | solution.py:376
  4.9 12.0 %collective-permute-start.1 = (bf16[2,64,1152]{2,1,0:T(8,128)(2,1)}, bf16[2,64,1152]{2,1,0:T(8,128)(2,1)S(1)}, u32[]{:S(2)}, u32[]{:S(2)}) collective-permute-start(bf16[2,64,1152]{2,1,0:T(8,128)(2,1)} %get-tuple-element.21.refs_0_), channel_id=1, source_target_pairs={{0,4},{4,8},{8,12},{12,0},{1,5},{5,9},{9,13},{13,1},{2,6},{6,10},{... | collective-permute-start | bytes 884744 | tf_op jit(solution)/shard_map/ppermute | solution.py:348
  6.5 15.5 %collective-permute-start = (bf16[2,64,1152]{2,1,0:T(8,128)(2,1)}, bf16[2,64,1152]{2,1,0:T(8,128)(2,1)S(1)}, u32[]{:S(2)}, u32[]{:S(2)}) collective-permute-start(bf16[2,64,1152]{2,1,0:T(8,128)(2,1)} %get-tuple-element.21.refs_0_), channel_id=1, source_target_pairs={{0,12},{4,0},{8,4},{12,8},{1,13},{5,1},{9,5},{13,9},{2,14},{6,2},{... | collective-permute-start | bytes 884744 | tf_op jit(solution)/shard_map/ppermute | solution.py:348
  12.1 35.6 %collective-permute-start.7 = (bf16[400,1024]{1,0:T(8,128)(2,1)}, bf16[400,1024]{1,0:T(8,128)(2,1)S(1)}, u32[]{:S(2)}, u32[]{:S(2)}) collective-permute-start(bf16[400,1024]{1,0:T(8,128)(2,1)} %get-tuple-element.25), channel_id=1, source_target_pairs={{0,2},{2,0},{16,18},{18,16},{1,3},{3,1},{17,19},{19,17},{4,6},{6,4... | collective-permute-start | bytes 2457608 | tf_op jit(solution)/shard_map/ppermute | solution.py:358
  12.4 35.3 %collective-permute-start.8 = (bf16[400,1024]{1,0:T(8,128)(2,1)}, bf16[400,1024]{1,0:T(8,128)(2,1)S(1)}, u32[]{:S(2)}, u32[]{:S(2)}) collective-permute-start(bf16[400,1024]{1,0:T(8,128)(2,1)} %get-tuple-element.26), channel_id=1, source_target_pairs={{0,16},{2,18},{16,0},{18,2},{1,17},{3,19},{17,1},{19,3},{4,20},{6,... | collective-permute-start | bytes 2457608 | tf_op jit(solution)/shard_map/ppermute | solution.py:358
  14.1 23.5 %copy-start.10 = (bf16[2,64,1152]{2,1,0:T(8,128)(2,1)S(1)}, bf16[2,64,1152]{2,1,0:T(8,128)(2,1)}, u32[]{:S(2)}) copy-start(bf16[2,64,1152]{2,1,0:T(8,128)(2,1)} %get-tuple-element.21.refs_0_) | copy-start | bytes 884740
  14.1 36.1 %collective-permute-start.9 = (bf16[400,1024]{1,0:T(8,128)(2,1)}, bf16[400,1024]{1,0:T(8,128)(2,1)S(1)}, u32[]{:S(2)}, u32[]{:S(2)}) collective-permute-start(bf16[400,1024]{1,0:T(8,128)(2,1)} %get-tuple-element.27), channel_id=1, source_target_pairs={{0,18},{2,16},{16,2},{18,0},{1,19},{3,17},{17,3},{19,1},{4,22},{6,... | collective-permute-start | bytes 2457608 | tf_op jit(solution)/shard_map/ppermute | solution.py:358
  16.9 16.0 %copy-start.2 = (bf16[2,64,1152]{2,1,0:T(8,128)(2,1)}, bf16[2,64,1152]{2,1,0:T(8,128)(2,1)S(1)}, u32[]{:S(2)}) copy-start(bf16[2,64,1152]{2,1,0:T(8,128)(2,1)S(1)} %collective-permute-done.1.refs_0_) | copy-start | bytes 884740
  16.9 16.0 %collective-permute-start.4 = (bf16[2,64,1152]{2,1,0:T(8,128)(2,1)}, bf16[2,64,1152]{2,1,0:T(8,128)(2,1)S(1)}, u32[]{:S(2)}, u32[]{:S(2)}) collective-permute-start(bf16[2,64,1152]{2,1,0:T(8,128)(2,1)} %collective-permute-done.2.refs_3_), channel_id=1, source_target_pairs={{0,4},{4,8},{8,12},{12,0},{1,5},{5,9},{9,13},{13,1},{2,6},{6,10},{... | collective-permute-start | bytes 884744 | tf_op jit(solution)/shard_map/ppermute | solution.py:348
  22.0 10.9 %copy-start = (bf16[2,64,1152]{2,1,0:T(8,128)(2,1)}, bf16[2,64,1152]{2,1,0:T(8,128)(2,1)S(1)}, u32[]{:S(2)}) copy-start(bf16[2,64,1152]{2,1,0:T(8,128)(2,1)S(1)} %collective-permute-done.refs_1_) | copy-start | bytes 884740
  22.0 12.5 %collective-permute-start.3 = (bf16[2,64,1152]{2,1,0:T(8,128)(2,1)}, bf16[2,64,1152]{2,1,0:T(8,128)(2,1)S(1)}, u32[]{:S(2)}, u32[]{:S(2)}) collective-permute-start(bf16[2,64,1152]{2,1,0:T(8,128)(2,1)} %collective-permute-done.2.refs_3_), channel_id=1, source_target_pairs={{0,12},{4,0},{8,4},{12,8},{1,13},{5,1},{9,5},{13,9},{2,14},{6,2},{... | collective-permute-start | bytes 884744 | tf_op jit(solution)/shard_map/ppermute | solution.py:348
  32.9 17.4 %copy-start.12 = (s32[16]{0:T(128)S(1)}, s32[16]{0:T(128)}, u32[]{:S(2)}) copy-start(s32[16]{0:T(128)} %owner.1) | copy-start | bytes 196
  32.9 1.5 %copy-start.4 = (bf16[2,64,1152]{2,1,0:T(8,128)(2,1)}, bf16[2,64,1152]{2,1,0:T(8,128)(2,1)S(1)}, u32[]{:S(2)}) copy-start(bf16[2,64,1152]{2,1,0:T(8,128)(2,1)S(1)} %collective-permute-done.4.refs_1_.refs_5_) | copy-start | bytes 884740
  32.9 11.2 %collective-permute-start.5 = (bf16[2,64,1152]{2,1,0:T(8,128)(2,1)}, bf16[2,64,1152]{2,1,0:T(8,128)(2,1)S(1)}, u32[]{:S(2)}, u32[]{:S(2)}) collective-permute-start(bf16[2,64,1152]{2,1,0:T(8,128)(2,1)} %hand.3.refs_2_), channel_id=1, source_target_pairs={{0,4},{4,8},{8,12},{12,0},{1,5},{5,9},{9,13},{13,1},{2,6},{6,10},{... | collective-permute-start | bytes 884744 | tf_op jit(solution)/shard_map/ppermute | solution.py:348
  34.5 0.7 %copy-start.6 = (bf16[2,64,1152]{2,1,0:T(8,128)(2,1)}, bf16[2,64,1152]{2,1,0:T(8,128)(2,1)S(1)}, u32[]{:S(2)}) copy-start(bf16[2,64,1152]{2,1,0:T(8,128)(2,1)S(1)} %collective-permute-done.3.refs_0_) | copy-start | bytes 884740
  35.2 12.3 %collective-permute-start.6 = (bf16[2,64,1152]{2,1,0:T(8,128)(2,1)}, bf16[2,64,1152]{2,1,0:T(8,128)(2,1)S(1)}, u32[]{:S(2)}, u32[]{:S(2)}) collective-permute-start(bf16[2,64,1152]{2,1,0:T(8,128)(2,1)} %hand.4.refs_4_), channel_id=1, source_target_pairs={{0,12},{4,0},{8,4},{12,8},{1,13},{5,1},{9,5},{13,9},{2,14},{6,2},{... | collective-permute-start | bytes 884744 | tf_op jit(solution)/shard_map/ppermute | solution.py:348
  37.6 1.0 %copy-start.1 = (bf16[2,64,1152]{2,1,0:T(8,128)(2,1)S(1)}, bf16[2,64,1152]{2,1,0:T(8,128)(2,1)}, u32[]{:S(2)}) copy-start(bf16[2,64,1152]{2,1,0:T(8,128)(2,1)} %copy-done) | copy-start | bytes 884740
  38.6 1.0 %copy-start.3 = (bf16[2,64,1152]{2,1,0:T(8,128)(2,1)S(1)}, bf16[2,64,1152]{2,1,0:T(8,128)(2,1)}, u32[]{:S(2)}) copy-start(bf16[2,64,1152]{2,1,0:T(8,128)(2,1)} %hand.3.refs_2_) | copy-start | bytes 884740
  39.6 1.0 %copy-start.5 = (bf16[2,64,1152]{2,1,0:T(8,128)(2,1)S(1)}, bf16[2,64,1152]{2,1,0:T(8,128)(2,1)}, u32[]{:S(2)}) copy-start(bf16[2,64,1152]{2,1,0:T(8,128)(2,1)} %copy-done.4) | copy-start | bytes 884740
  40.5 1.0 %copy-start.7 = (bf16[2,64,1152]{2,1,0:T(8,128)(2,1)S(1)}, bf16[2,64,1152]{2,1,0:T(8,128)(2,1)}, u32[]{:S(2)}) copy-start(bf16[2,64,1152]{2,1,0:T(8,128)(2,1)} %hand.4.refs_4_) | copy-start | bytes 884740
  50.3 1.1 %copy-start.8 = (bf16[400,1024]{1,0:T(8,128)(2,1)S(1)}, bf16[400,1024]{1,0:T(8,128)(2,1)}, u32[]{:S(2)}) copy-start(bf16[400,1024]{1,0:T(8,128)(2,1)} %get-tuple-element.24.refs_1_) | copy-start | bytes 2457604
  51.4 12.1 %copy-start.9 = (f32[384,512]{1,0:T(8,128)S(1)}, f32[384,512]{1,0:T(8,128)}, u32[]{:S(2)}) copy-start(f32[384,512]{1,0:T(8,128)} %get-tuple-element.19.base_a) | copy-start | bytes 2359300
  53.1 0.6 copy-start.11
  53.7 9.8 %collective-permute-start.10 = (f32[384,512]{1,0:T(8,128)}, f32[384,512]{1,0:T(8,128)S(1)}, u32[]{:S(2)}, u32[]{:S(2)}) collective-permute-start(f32[384,512]{1,0:T(8,128)} %hand.5), channel_id=1, source_target_pairs={{0,1},{1,0},{2,3},{3,2},{4,5},{5,4},{6,7},{7,6},{8,9},{9,8},{10,11... | collective-permute-start | bytes 2359304 | tf_op jit(solution)/shard_map/ppermute | solution.py:345
  53.7 5.2 %collective-permute-start.11 = (bf16[3,128,128]{2,1,0:T(8,128)(2,1)S(1)}, bf16[3,128,128]{2,1,0:T(8,128)(2,1)S(1)}, u32[]{:S(2)}, u32[]{:S(2)}) collective-permute-start(bf16[3,128,128]{2,1,0:T(8,128)(2,1)S(1)} %get-tuple-element.30), channel_id=1, source_target_pairs={{0,2},{2,0},{16,18},{18,16},{1,3},{3,1},{17,19},{19,17},{4,6},{6,4... | collective-permute-start | bytes 294920 | tf_op jit(solution)/shard_map/ppermute | solution.py:358
  54.2 4.9 %collective-permute-start.12 = (bf16[3,128,128]{2,1,0:T(8,128)(2,1)S(1)}, bf16[3,128,128]{2,1,0:T(8,128)(2,1)S(1)}, u32[]{:S(2)}, u32[]{:S(2)}) collective-permute-start(bf16[3,128,128]{2,1,0:T(8,128)(2,1)S(1)} %get-tuple-element.31), channel_id=1, source_target_pairs={{0,16},{2,18},{16,0},{18,2},{1,17},{3,19},{17,1},{19,3},{4,20},{6,... | collective-permute-start | bytes 294920 | tf_op jit(solution)/shard_map/ppermute | solution.py:358
  55.7 6.5 %collective-permute-start.13 = (bf16[3,128,128]{2,1,0:T(8,128)(2,1)S(1)}, bf16[3,128,128]{2,1,0:T(8,128)(2,1)S(1)}, u32[]{:S(2)}, u32[]{:S(2)}) collective-permute-start(bf16[3,128,128]{2,1,0:T(8,128)(2,1)S(1)} %get-tuple-element.32), channel_id=1, source_target_pairs={{0,18},{2,16},{16,2},{18,0},{1,19},{3,17},{17,3},{19,1},{4,22},{6,... | collective-permute-start | bytes 294920 | tf_op jit(solution)/shard_map/ppermute | solution.py:358
  57.2 5.0 %collective-permute-start.14 = (bf16[3,128,128]{2,1,0:T(8,128)(2,1)S(1)}, bf16[3,128,128]{2,1,0:T(8,128)(2,1)S(1)}, u32[]{:S(2)}, u32[]{:S(2)}) collective-permute-start(bf16[3,128,128]{2,1,0:T(8,128)(2,1)S(1)} %get-tuple-element.29.refs_0_), channel_id=1, source_target_pairs={{0,1},{1,0},{2,3},{3,2},{4,5},{5,4},{6,7},{7,6},{8,9},{9,8},{10,11... | collective-permute-start | bytes 294920 | tf_op jit(solution)/shard_map/ppermute | solution.py:345
  58.9 3.3 %collective-permute-start.15 = (bf16[3,128,128]{2,1,0:T(8,128)(2,1)S(1)}, bf16[3,128,128]{2,1,0:T(8,128)(2,1)S(1)}, u32[]{:S(2)}, u32[]{:S(2)}) collective-permute-start(bf16[3,128,128]{2,1,0:T(8,128)(2,1)S(1)} %collective-permute-done.11.refs_1_), channel_id=1, source_target_pairs={{0,1},{1,0},{2,3},{3,2},{4,5},{5,4},{6,7},{7,6},{8,9},{9,8},{10,11... | collective-permute-start | bytes 294920 | tf_op jit(solution)/shard_map/ppermute | solution.py:345
  59.2 3.1 %collective-permute-start.16 = (bf16[3,128,128]{2,1,0:T(8,128)(2,1)S(1)}, bf16[3,128,128]{2,1,0:T(8,128)(2,1)S(1)}, u32[]{:S(2)}, u32[]{:S(2)}) collective-permute-start(bf16[3,128,128]{2,1,0:T(8,128)(2,1)S(1)} %collective-permute-done.12.refs_2_), channel_id=1, source_target_pairs={{0,1},{1,0},{2,3},{3,2},{4,5},{5,4},{6,7},{7,6},{8,9},{9,8},{10,11... | collective-permute-start | bytes 294920 | tf_op jit(solution)/shard_map/ppermute | solution.py:345
  62.2 1.3 %collective-permute-start.17 = (bf16[3,128,128]{2,1,0:T(8,128)(2,1)S(1)}, bf16[3,128,128]{2,1,0:T(8,128)(2,1)S(1)}, u32[]{:S(2)}, u32[]{:S(2)}) collective-permute-start(bf16[3,128,128]{2,1,0:T(8,128)(2,1)S(1)} %collective-permute-done.13.refs_3_), channel_id=1, source_target_pairs={{0,1},{1,0},{2,3},{3,2},{4,5},{5,4},{6,7},{7,6},{8,9},{9,8},{10,11... | collective-permute-start | bytes 294920 | tf_op jit(solution)/shard_map/ppermute | solution.py:345

commit v34 on v31

--- a/solution.py
+++ b/solution.py
@@ -43,8 +43,13 @@
         share = lax.axis_index("groups") * len(outs) + lax.rem(lax.axis_index("pair") + way, len(outs))
         start = pl.multiple_of(share * feats, LANES)
         tile = pl.multiple_of(lax.rem(share, up.shape[2] // LANES) * LANES, LANES)
-        copies.append(pltpu.make_async_copy(down.at[:, :, pl.ds(start, feats)], out.at[:, :, :feats], sems.at[way, 0]))
-        copies.append(pltpu.make_async_copy(up.at[:, :, pl.ds(tile, LANES)], out.at[:, :, feats:], sems.at[way, 1]))
+        half = down.shape[1] // 2
+        for a in range(down.shape[0]):
+            for h in range(2):
+                rows, sem = pl.ds(h * half, half), sems.at[way, a, h]
+                to = out.at[a, rows, :]
+                copies.append(pltpu.make_async_copy(down.at[a, rows, pl.ds(start, feats)], to.at[:, :feats], sem.at[0]))
+                copies.append(pltpu.make_async_copy(up.at[a, rows, pl.ds(tile, LANES)], to.at[:, feats:], sem.at[1]))
     for copy in copies:
         copy.start()
     for copy in copies:
@@ -59,7 +64,7 @@
         in_specs=[HBM, HBM],
         out_specs=[VMEM] * ways,
         out_shape=[shape] * ways,
-        scratch_shapes=[pltpu.SemaphoreType.DMA((ways, 2))],
+        scratch_shapes=[pltpu.SemaphoreType.DMA((ways, adapters, 2, 2))],
         compiler_params=FULL,
         name="pack",
     )(down, up)

time: 64.8 us -> 65 us (level)
  transfers between devices with their start and end apart: 18 -> 18, of which waited for: 9 -> 9; matrix products, arithmetic and copies ran while one was open for 0% -> 0% of each run, Pallas kernels for 20% -> 19%
where the time goes in v34:
time: 65 us; the launch traced here: 64.6 us
  starting transfers between devices  20.2 us (31%)
  waiting for transfers between devices  20 us (31%)
  Pallas kernels  17.4 us (27%)
  local copies, waits for them, and re-layouts  6.87 us (11%)
    ppermute x6, waiting for transfers between devices, in_plane(): return lax.ppermute(x, PLANE, pairs)  10.1 us
    ppermute x6, starting transfers between devices, along(): lax.ppermute(x, 'ring', [(a, (a + step) % ring) for a in range(ring)])  9.83 us
    ppermute x6, waiting for transfers between devices, along(): lax.ppermute(x, 'ring', [(a, (a + step) % ring) for a in range(ring)])  8.54 us
    pallas_call x1, Pallas kernels, base_halves(): pl.pallas_call(functools.partial(base_kernel, sides, groups, pair), in_sp...  8.05 us
    ppermute x6, starting transfers between devices, in_plane(): return lax.ppermute(x, PLANE, pairs)  7.04 us
    unnamed x30, local copies, waits for them, and re-layouts  6.87 us
    pallas_call x1, Pallas kernels, spread(): pl.pallas_call(functools.partial(spread_kernel, groups, pair), in_specs=[...  3.27 us
    ppermute x1, starting transfers between devices, body(): lax.ppermute(packed[pair - w], 'pair', [(a, (a - w) % pair) for a in rang...  3.03 us
  transfers between devices with their start and end apart: 18, of which 9 were waited for; matrix products, arithmetic and copies ran while one was open for 0% of the time, Pallas kernels for 19%

profile of v34, /device:TPU:0, one launch (start us, length us, event | category | flops | bytes accessed | tf_op | source)
XLA Modules:
  0.0 64.6 jit_solution(5661449485982229871)
XLA Ops:
  0.0 2.1 %pack.1 = (bf16[2,64,1152]{2,1,0:T(8,128)(2,1)}, bf16[2,64,1152]{2,1,0:T(8,128)(2,1)}) custom-call(bf16[2,64,4096]{2,1,0:T(8,128)(2,1)} %bitcast.2, bf16[2,64,512]{2,1,0:T(8,128)(2,1)} %up.1), custom_call_target="tpu_custom_call" | custom-call | tf_op jit(solution)/shard_map/pack/pallas_call | solution.py:62
  2.1 3.0 %collective-permute-start.2 = (bf16[2,64,1152]{2,1,0:T(8,128)(2,1)}, bf16[2,64,1152]{2,1,0:T(8,128)(2,1)}, u32[]{:S(2)}, u32[]{:S(2)}) collective-permute-start(bf16[2,64,1152]{2,1,0:T(8,128)(2,1)} %get-tuple-element.23), channel_id=1, source_target_pairs={{0,2},{2,0},{1,3},{3,1},{4,6},{6,4},{5,7},{7,5},{8,10},{10,8},{9,1... | collective-permute-start | bytes 884744 | tf_op jit(solution)/shard_map/ppermute | solution.py:382
  5.2 1.6 %collective-permute-start.1 = (bf16[2,64,1152]{2,1,0:T(8,128)(2,1)}, bf16[2,64,1152]{2,1,0:T(8,128)(2,1)S(1)}, u32[]{:S(2)}, u32[]{:S(2)}) collective-permute-start(bf16[2,64,1152]{2,1,0:T(8,128)(2,1)} %get-tuple-element.21.refs_0_), channel_id=1, source_target_pairs={{0,4},{4,8},{8,12},{12,0},{1,5},{5,9},{9,13},{13,1},{2,6},{6,10},{... | collective-permute-start | bytes 884744 | tf_op jit(solution)/shard_map/ppermute | solution.py:354
  6.7 2.2 %collective-permute-start = (bf16[2,64,1152]{2,1,0:T(8,128)(2,1)}, bf16[2,64,1152]{2,1,0:T(8,128)(2,1)S(1)}, u32[]{:S(2)}, u32[]{:S(2)}) collective-permute-start(bf16[2,64,1152]{2,1,0:T(8,128)(2,1)} %get-tuple-element.21.refs_0_), channel_id=1, source_target_pairs={{0,12},{4,0},{8,4},{12,8},{1,13},{5,1},{9,5},{13,9},{2,14},{6,2},{... | collective-permute-start | bytes 884744 | tf_op jit(solution)/shard_map/ppermute | solution.py:354
  9.0 3.3 %spread.1 = (bf16[400,1024]{1,0:T(8,128)(2,1)}, bf16[400,1024]{1,0:T(8,128)(2,1)}, bf16[400,1024]{1,0:T(8,128)(2,1)}) custom-call(s32[3]{0:T(128)} %lengths.3, s32[3]{0:T(128)} %bitcast.3, bf16[384,4096]{1,0:T(8,128)(2,1)} %tok.3), custom_call_target="tpu_custom_call" | custom-call | tf_op jit(solution)/shard_map/spread/pallas_call | solution.py:136
  12.3 0.4 collective-permute-start.7
  12.6 1.7 %collective-permute-start.8 = (bf16[400,1024]{1,0:T(8,128)(2,1)}, bf16[400,1024]{1,0:T(8,128)(2,1)S(1)}, u32[]{:S(2)}, u32[]{:S(2)}) collective-permute-start(bf16[400,1024]{1,0:T(8,128)(2,1)} %get-tuple-element.26), channel_id=1, source_target_pairs={{0,16},{2,18},{16,0},{18,2},{1,17},{3,19},{17,1},{19,3},{4,20},{6,... | collective-permute-start | bytes 2457608 | tf_op jit(solution)/shard_map/ppermute | solution.py:364
  14.4 0.0 collective-permute-done.2.refs_3_
  14.4 1.5 %collective-permute-start.9 = (bf16[400,1024]{1,0:T(8,128)(2,1)}, bf16[400,1024]{1,0:T(8,128)(2,1)S(1)}, u32[]{:S(2)}, u32[]{:S(2)}) collective-permute-start(bf16[400,1024]{1,0:T(8,128)(2,1)} %get-tuple-element.27), channel_id=1, source_target_pairs={{0,18},{2,16},{16,2},{18,0},{1,19},{3,17},{17,3},{19,1},{4,22},{6,... | collective-permute-start | bytes 2457608 | tf_op jit(solution)/shard_map/ppermute | solution.py:364
  15.8 1.3 %collective-permute-done.1.refs_0_ = bf16[2,64,1152]{2,1,0:T(8,128)(2,1)S(1)} collective-permute-done((bf16[2,64,1152]{2,1,0:T(8,128)(2,1)}, bf16[2,64,1152]{2,1,0:T(8,128)(2,1)S(1)}, u32[]{:S(2)}, u32[]{:S(2)}) %collective-permute-start.1) | collective-permute-done | bytes 294944 | tf_op jit(solution)/shard_map/ppermute | solution.py:354
  17.1 0.7 %collective-permute-start.4 = (bf16[2,64,1152]{2,1,0:T(8,128)(2,1)}, bf16[2,64,1152]{2,1,0:T(8,128)(2,1)S(1)}, u32[]{:S(2)}, u32[]{:S(2)}) collective-permute-start(bf16[2,64,1152]{2,1,0:T(8,128)(2,1)} %collective-permute-done.2.refs_3_), channel_id=1, source_target_pairs={{0,4},{4,8},{8,12},{12,0},{1,5},{5,9},{9,13},{13,1},{2,6},{6,10},{... | collective-permute-start | bytes 884744 | tf_op jit(solution)/shard_map/ppermute | solution.py:354
  17.9 4.4 %collective-permute-done.refs_1_ = bf16[2,64,1152]{2,1,0:T(8,128)(2,1)S(1)} collective-permute-done((bf16[2,64,1152]{2,1,0:T(8,128)(2,1)}, bf16[2,64,1152]{2,1,0:T(8,128)(2,1)S(1)}, u32[]{:S(2)}, u32[]{:S(2)}) %collective-permute-start) | collective-permute-done | bytes 294944 | tf_op jit(solution)/shard_map/ppermute | solution.py:354
  22.3 2.8 %collective-permute-start.3 = (bf16[2,64,1152]{2,1,0:T(8,128)(2,1)}, bf16[2,64,1152]{2,1,0:T(8,128)(2,1)S(1)}, u32[]{:S(2)}, u32[]{:S(2)}) collective-permute-start(bf16[2,64,1152]{2,1,0:T(8,128)(2,1)} %collective-permute-done.2.refs_3_), channel_id=1, source_target_pairs={{0,12},{4,0},{8,4},{12,8},{1,13},{5,1},{9,5},{13,9},{2,14},{6,2},{... | collective-permute-start | bytes 884744 | tf_op jit(solution)/shard_map/ppermute | solution.py:354
  25.1 8.0 %base.1 = (f32[384,512]{1,0:T(8,128)}, f32[384,512]{1,0:T(8,128)}, f32[8,128]{1,0:T(8,128)}, bf16[400,1024]{1,0:T(8,128)(2,1)}) custom-call(s32[3]{0:T(128)} %lengths.3, s32[3]{0:T(128)} %bitcast.4, bf16[384,4096]{1,0:T(8,128)(2,1)} %tok.3, bf16[4096,1024]{1,0:T(8,128)(2,1)} %key.1), custom_call_target="tpu_custom_call" | custom-call | tf_op jit(solution)/shard_map/base/pallas_call | solution.py:208
  33.1 0.0 copy-start.14
  33.2 0.1 collective-permute-start.5
  33.2 1.5 %collective-permute-done.3.refs_0_ = bf16[2,64,1152]{2,1,0:T(8,128)(2,1)S(1)} collective-permute-done((bf16[2,64,1152]{2,1,0:T(8,128)(2,1)}, bf16[2,64,1152]{2,1,0:T(8,128)(2,1)S(1)}, u32[]{:S(2)}, u32[]{:S(2)}) %collective-permute-start.3) | collective-permute-done | bytes 294944 | tf_op jit(solution)/shard_map/ppermute | solution.py:354
  34.7 0.7 %copy-done.6 = bf16[2,64,1152]{2,1,0:T(8,128)(2,1)} copy-done((bf16[2,64,1152]{2,1,0:T(8,128)(2,1)}, bf16[2,64,1152]{2,1,0:T(8,128)(2,1)S(1)}, u32[]{:S(2)}) %copy-start.6) | copy-done | bytes 294936
  35.4 2.4 %collective-permute-start.6 = (bf16[2,64,1152]{2,1,0:T(8,128)(2,1)}, bf16[2,64,1152]{2,1,0:T(8,128)(2,1)S(1)}, u32[]{:S(2)}, u32[]{:S(2)}) collective-permute-start(bf16[2,64,1152]{2,1,0:T(8,128)(2,1)} %hand.4.refs_4_), channel_id=1, source_target_pairs={{0,12},{4,0},{8,4},{12,8},{1,13},{5,1},{9,5},{13,9},{2,14},{6,2},{... | collective-permute-start | bytes 884744 | tf_op jit(solution)/shard_map/ppermute | solution.py:354
  37.9 1.0 %copy-done.1 = bf16[2,64,1152]{2,1,0:T(8,128)(2,1)S(1)} copy-done((bf16[2,64,1152]{2,1,0:T(8,128)(2,1)S(1)}, bf16[2,64,1152]{2,1,0:T(8,128)(2,1)}, u32[]{:S(2)}) %copy-start.1) | copy-done | bytes 294936
  38.8 1.0 %copy-done.3 = bf16[2,64,1152]{2,1,0:T(8,128)(2,1)S(1)} copy-done((bf16[2,64,1152]{2,1,0:T(8,128)(2,1)S(1)}, bf16[2,64,1152]{2,1,0:T(8,128)(2,1)}, u32[]{:S(2)}) %copy-start.3) | copy-done | bytes 294936
  39.8 1.0 %copy-done.5 = bf16[2,64,1152]{2,1,0:T(8,128)(2,1)S(1)} copy-done((bf16[2,64,1152]{2,1,0:T(8,128)(2,1)S(1)}, bf16[2,64,1152]{2,1,0:T(8,128)(2,1)}, u32[]{:S(2)}) %copy-start.5) | copy-done | bytes 294936
  40.7 1.0 %copy-done.7 = bf16[2,64,1152]{2,1,0:T(8,128)(2,1)S(1)} copy-done((bf16[2,64,1152]{2,1,0:T(8,128)(2,1)S(1)}, bf16[2,64,1152]{2,1,0:T(8,128)(2,1)}, u32[]{:S(2)}) %copy-start.7) | copy-done | bytes 294936
  41.7 1.3 %collect.1.held = bf16[12,64,1152]{2,1,0:T(8,128)(2,1)S(1)} custom-call(bf16[2,64,1152]{2,1,0:T(8,128)(2,1)S(1)} %copy-done.10, bf16[2,64,1152]{2,1,0:T(8,128)(2,1)S(1)} %copy-done.1, bf16[2,64,1152]{2,1,0:T(8,128)(2,1)S(1)} %copy-done.3, bf16[2,64,1152]{2,1,0:T(8,128)(2,1)} %collective-permute-done.2.refs_3_, bf16[2,64,1152]{2,1,0:T(8,128)(2,1)S(1)} %copy-done.7, ...), custom_call_target="tpu_custom_call" | custom-call | tf_op jit(solution)/shard_map/collect/pallas_call | solution.py:245
  43.0 1.4 %collective-permute-done.5.refs_0_ = bf16[2,64,1152]{2,1,0:T(8,128)(2,1)S(1)} collective-permute-done((bf16[2,64,1152]{2,1,0:T(8,128)(2,1)}, bf16[2,64,1152]{2,1,0:T(8,128)(2,1)S(1)}, u32[]{:S(2)}, u32[]{:S(2)}) %collective-permute-start.5) | collective-permute-done | bytes 294944 | tf_op jit(solution)/shard_map/ppermute | solution.py:354
  44.4 0.7 %copy-done.11 = bf16[2,64,1152]{2,1,0:T(8,128)(2,1)} copy-done((bf16[2,64,1152]{2,1,0:T(8,128)(2,1)}, bf16[2,64,1152]{2,1,0:T(8,128)(2,1)S(1)}, u32[]{:S(2)}) %copy-start.11) | copy-done | bytes 294936
  45.1 0.0 collective-permute-done.7.refs_3_
  45.1 0.0 collective-permute-done.8.refs_4_
  45.1 5.4 %collective-permute-done.9.refs_5_ = bf16[400,1024]{1,0:T(8,128)(2,1)S(1)} collective-permute-done((bf16[400,1024]{1,0:T(8,128)(2,1)}, bf16[400,1024]{1,0:T(8,128)(2,1)S(1)}, u32[]{:S(2)}, u32[]{:S(2)}) %collective-permute-start.9) | collective-permute-done | bytes 819232 | tf_op jit(solution)/shard_map/ppermute | solution.py:364
  50.5 0.0 collective-permute-done.6.refs_1_
  50.5 0.0 copy-start.12
  50.5 1.0 %copy-done.12 = bf16[2,64,1152]{2,1,0:T(8,128)(2,1)S(1)} copy-done((bf16[2,64,1152]{2,1,0:T(8,128)(2,1)S(1)}, bf16[2,64,1152]{2,1,0:T(8,128)(2,1)}, u32[]{:S(2)}) %copy-start.12) | copy-done | bytes 294936
  51.5 1.7 %rank.1 = (bf16[3,128,128]{2,1,0:T(8,128)(2,1)S(1)}, bf16[3,128,128]{2,1,0:T(8,128)(2,1)S(1)}, bf16[3,128,128]{2,1,0:T(8,128)(2,1)S(1)}, bf16[3,128,128]{2,1,0:T(8,128)(2,1)S(1)}, f32[8,128]{1,0:T(8,128)S(1)}) custom-call(s32[16]{0:T(128)S(1)} %copy-done.14, bf16[12,64,1152]{2,1,0:T(8,128)(2,1)S(1)} %collect.1.held, bf16[2,64,1152]{2,1,0:T(8,128)(2,1)S(1)} %copy-done.12, ...), custom_call_target="tpu_custom_call" | custom-call | tf_op jit(solution)/shard_map/rank/pallas_call | solution.py:298
  53.1 0.0 copy-start.13
  53.2 0.6 copy-done.13
  53.7 0.0 collective-permute-start.10
  53.7 0.5 collective-permute-start.11
  54.3 1.5 %collective-permute-start.12 = (bf16[3,128,128]{2,1,0:T(8,128)(2,1)S(1)}, bf16[3,128,128]{2,1,0:T(8,128)(2,1)S(1)}, u32[]{:S(2)}, u32[]{:S(2)}) collective-permute-start(bf16[3,128,128]{2,1,0:T(8,128)(2,1)S(1)} %get-tuple-element.31), channel_id=1, source_target_pairs={{0,16},{2,18},{16,0},{18,2},{1,17},{3,19},{17,1},{19,3},{4,20},{6,... | collective-permute-start | bytes 294920 | tf_op jit(solution)/shard_map/ppermute | solution.py:364
  55.8 1.5 %collective-permute-start.13 = (bf16[3,128,128]{2,1,0:T(8,128)(2,1)S(1)}, bf16[3,128,128]{2,1,0:T(8,128)(2,1)S(1)}, u32[]{:S(2)}, u32[]{:S(2)}) collective-permute-start(bf16[3,128,128]{2,1,0:T(8,128)(2,1)S(1)} %get-tuple-element.32), channel_id=1, source_target_pairs={{0,18},{2,16},{16,2},{18,0},{1,19},{3,17},{17,3},{19,1},{4,22},{6,... | collective-permute-start | bytes 294920 | tf_op jit(solution)/shard_map/ppermute | solution.py:364
  57.2 1.7 %collective-permute-done.11.refs_1_ = bf16[3,128,128]{2,1,0:T(8,128)(2,1)S(1)} collective-permute-done((bf16[3,128,128]{2,1,0:T(8,128)(2,1)S(1)}, bf16[3,128,128]{2,1,0:T(8,128)(2,1)S(1)}, u32[]{:S(2)}, u32[]{:S(2)}) %collective-permute-start.11) | collective-permute-done | bytes 98336 | tf_op jit(solution)/shard_map/ppermute | solution.py:364
  59.0 0.0 collective-permute-start.15
  59.0 0.2 collective-permute-done.12.refs_2_
  59.2 0.3 collective-permute-start.16
  59.5 2.8 %collective-permute-done.13.refs_3_ = bf16[3,128,128]{2,1,0:T(8,128)(2,1)S(1)} collective-permute-done((bf16[3,128,128]{2,1,0:T(8,128)(2,1)S(1)}, bf16[3,128,128]{2,1,0:T(8,128)(2,1)S(1)}, u32[]{:S(2)}, u32[]{:S(2)}) %collective-permute-start.13) | collective-permute-done | bytes 98336 | tf_op jit(solution)/shard_map/ppermute | solution.py:364
  62.2 0.0 collective-permute-done.15.refs_5_
  62.3 0.0 collective-permute-done.16.refs_6_
  62.3 1.3 %collective-permute-done.17.refs_7_ = bf16[3,128,128]{2,1,0:T(8,128)(2,1)S(1)} collective-permute-done((bf16[3,128,128]{2,1,0:T(8,128)(2,1)S(1)}, bf16[3,128,128]{2,1,0:T(8,128)(2,1)S(1)}, u32[]{:S(2)}, u32[]{:S(2)}) %collective-permute-start.17) | collective-permute-done | bytes 98336 | tf_op jit(solution)/shard_map/ppermute | solution.py:351
  63.5 1.1 %final.1 = bf16[384,512]{1,0:T(8,128)(2,1)} custom-call(f32[384,512]{1,0:T(8,128)S(1)} %copy-done.9, f32[384,512]{1,0:T(8,128)S(1)} %collective-permute-done.10.base_b, bf16[3,128,128]{2,1,0:T(8,128)(2,1)S(1)} %get-tuple-element.29.refs_0_, bf16[3,128,128]{2,1,0:T(8,128)(2,1)S(1)} %collective-permute-done.11.refs_1_, ...), custom_call_target="tpu_custom_call" | custom-call | tf_op jit(solution)/shard_map/final/pallas_call | solution.py:332
  (27 shorter events, 0.1 us)
Async XLA Ops:
  2.1 12.2 %collective-permute-start.2 = (bf16[2,64,1152]{2,1,0:T(8,128)(2,1)}, bf16[2,64,1152]{2,1,0:T(8,128)(2,1)}, u32[]{:S(2)}, u32[]{:S(2)}) collective-permute-start(bf16[2,64,1152]{2,1,0:T(8,128)(2,1)} %get-tuple-element.23), channel_id=1, source_target_pairs={{0,2},{2,0},{1,3},{3,1},{4,6},{6,4},{5,7},{7,5},{8,10},{10,8},{9,1... | collective-permute-start | bytes 884744 | tf_op jit(solution)/shard_map/ppermute | solution.py:382
  5.2 12.0 %collective-permute-start.1 = (bf16[2,64,1152]{2,1,0:T(8,128)(2,1)}, bf16[2,64,1152]{2,1,0:T(8,128)(2,1)S(1)}, u32[]{:S(2)}, u32[]{:S(2)}) collective-permute-start(bf16[2,64,1152]{2,1,0:T(8,128)(2,1)} %get-tuple-element.21.refs_0_), channel_id=1, source_target_pairs={{0,4},{4,8},{8,12},{12,0},{1,5},{5,9},{9,13},{13,1},{2,6},{6,10},{... | collective-permute-start | bytes 884744 | tf_op jit(solution)/shard_map/ppermute | solution.py:354
  6.7 15.5 %collective-permute-start = (bf16[2,64,1152]{2,1,0:T(8,128)(2,1)}, bf16[2,64,1152]{2,1,0:T(8,128)(2,1)S(1)}, u32[]{:S(2)}, u32[]{:S(2)}) collective-permute-start(bf16[2,64,1152]{2,1,0:T(8,128)(2,1)} %get-tuple-element.21.refs_0_), channel_id=1, source_target_pairs={{0,12},{4,0},{8,4},{12,8},{1,13},{5,1},{9,5},{13,9},{2,14},{6,2},{... | collective-permute-start | bytes 884744 | tf_op jit(solution)/shard_map/ppermute | solution.py:354
  12.3 32.8 %collective-permute-start.7 = (bf16[400,1024]{1,0:T(8,128)(2,1)}, bf16[400,1024]{1,0:T(8,128)(2,1)S(1)}, u32[]{:S(2)}, u32[]{:S(2)}) collective-permute-start(bf16[400,1024]{1,0:T(8,128)(2,1)} %get-tuple-element.25), channel_id=1, source_target_pairs={{0,2},{2,0},{16,18},{18,16},{1,3},{3,1},{17,19},{19,17},{4,6},{6,4... | collective-permute-start | bytes 2457608 | tf_op jit(solution)/shard_map/ppermute | solution.py:364
  12.6 32.4 %collective-permute-start.8 = (bf16[400,1024]{1,0:T(8,128)(2,1)}, bf16[400,1024]{1,0:T(8,128)(2,1)S(1)}, u32[]{:S(2)}, u32[]{:S(2)}) collective-permute-start(bf16[400,1024]{1,0:T(8,128)(2,1)} %get-tuple-element.26), channel_id=1, source_target_pairs={{0,16},{2,18},{16,0},{18,2},{1,17},{3,19},{17,1},{19,3},{4,20},{6,... | collective-permute-start | bytes 2457608 | tf_op jit(solution)/shard_map/ppermute | solution.py:364
  14.4 23.5 %copy-start.10 = (bf16[2,64,1152]{2,1,0:T(8,128)(2,1)S(1)}, bf16[2,64,1152]{2,1,0:T(8,128)(2,1)}, u32[]{:S(2)}) copy-start(bf16[2,64,1152]{2,1,0:T(8,128)(2,1)} %get-tuple-element.21.refs_0_) | copy-start | bytes 884740
  14.4 36.1 %collective-permute-start.9 = (bf16[400,1024]{1,0:T(8,128)(2,1)}, bf16[400,1024]{1,0:T(8,128)(2,1)S(1)}, u32[]{:S(2)}, u32[]{:S(2)}) collective-permute-start(bf16[400,1024]{1,0:T(8,128)(2,1)} %get-tuple-element.27), channel_id=1, source_target_pairs={{0,18},{2,16},{16,2},{18,0},{1,19},{3,17},{17,3},{19,1},{4,22},{6,... | collective-permute-start | bytes 2457608 | tf_op jit(solution)/shard_map/ppermute | solution.py:364
  17.1 16.0 %copy-start.2 = (bf16[2,64,1152]{2,1,0:T(8,128)(2,1)}, bf16[2,64,1152]{2,1,0:T(8,128)(2,1)S(1)}, u32[]{:S(2)}) copy-start(bf16[2,64,1152]{2,1,0:T(8,128)(2,1)S(1)} %collective-permute-done.1.refs_0_) | copy-start | bytes 884740
  17.1 16.0 %collective-permute-start.4 = (bf16[2,64,1152]{2,1,0:T(8,128)(2,1)}, bf16[2,64,1152]{2,1,0:T(8,128)(2,1)S(1)}, u32[]{:S(2)}, u32[]{:S(2)}) collective-permute-start(bf16[2,64,1152]{2,1,0:T(8,128)(2,1)} %collective-permute-done.2.refs_3_), channel_id=1, source_target_pairs={{0,4},{4,8},{8,12},{12,0},{1,5},{5,9},{9,13},{13,1},{2,6},{6,10},{... | collective-permute-start | bytes 884744 | tf_op jit(solution)/shard_map/ppermute | solution.py:354
  22.2 10.9 %copy-start = (bf16[2,64,1152]{2,1,0:T(8,128)(2,1)}, bf16[2,64,1152]{2,1,0:T(8,128)(2,1)S(1)}, u32[]{:S(2)}) copy-start(bf16[2,64,1152]{2,1,0:T(8,128)(2,1)S(1)} %collective-permute-done.refs_1_) | copy-start | bytes 884740
  22.3 12.5 %collective-permute-start.3 = (bf16[2,64,1152]{2,1,0:T(8,128)(2,1)}, bf16[2,64,1152]{2,1,0:T(8,128)(2,1)S(1)}, u32[]{:S(2)}, u32[]{:S(2)}) collective-permute-start(bf16[2,64,1152]{2,1,0:T(8,128)(2,1)} %collective-permute-done.2.refs_3_), channel_id=1, source_target_pairs={{0,12},{4,0},{8,4},{12,8},{1,13},{5,1},{9,5},{13,9},{2,14},{6,2},{... | collective-permute-start | bytes 884744 | tf_op jit(solution)/shard_map/ppermute | solution.py:354
  33.1 17.4 %copy-start.14 = (s32[16]{0:T(128)S(1)}, s32[16]{0:T(128)}, u32[]{:S(2)}) copy-start(s32[16]{0:T(128)} %owner.1) | copy-start | bytes 196
  33.2 1.5 %copy-start.4 = (bf16[2,64,1152]{2,1,0:T(8,128)(2,1)}, bf16[2,64,1152]{2,1,0:T(8,128)(2,1)S(1)}, u32[]{:S(2)}) copy-start(bf16[2,64,1152]{2,1,0:T(8,128)(2,1)S(1)} %collective-permute-done.4.refs_1_.refs_5_) | copy-start | bytes 884740
  33.2 11.2 %collective-permute-start.5 = (bf16[2,64,1152]{2,1,0:T(8,128)(2,1)}, bf16[2,64,1152]{2,1,0:T(8,128)(2,1)S(1)}, u32[]{:S(2)}, u32[]{:S(2)}) collective-permute-start(bf16[2,64,1152]{2,1,0:T(8,128)(2,1)} %hand.3.refs_2_), channel_id=1, source_target_pairs={{0,4},{4,8},{8,12},{12,0},{1,5},{5,9},{9,13},{13,1},{2,6},{6,10},{... | collective-permute-start | bytes 884744 | tf_op jit(solution)/shard_map/ppermute | solution.py:354
  34.7 0.7 %copy-start.6 = (bf16[2,64,1152]{2,1,0:T(8,128)(2,1)}, bf16[2,64,1152]{2,1,0:T(8,128)(2,1)S(1)}, u32[]{:S(2)}) copy-start(bf16[2,64,1152]{2,1,0:T(8,128)(2,1)S(1)} %collective-permute-done.3.refs_0_) | copy-start | bytes 884740
  35.4 15.0 %collective-permute-start.6 = (bf16[2,64,1152]{2,1,0:T(8,128)(2,1)}, bf16[2,64,1152]{2,1,0:T(8,128)(2,1)S(1)}, u32[]{:S(2)}, u32[]{:S(2)}) collective-permute-start(bf16[2,64,1152]{2,1,0:T(8,128)(2,1)} %hand.4.refs_4_), channel_id=1, source_target_pairs={{0,12},{4,0},{8,4},{12,8},{1,13},{5,1},{9,5},{13,9},{2,14},{6,2},{... | collective-permute-start | bytes 884744 | tf_op jit(solution)/shard_map/ppermute | solution.py:354
  37.9 1.0 %copy-start.1 = (bf16[2,64,1152]{2,1,0:T(8,128)(2,1)S(1)}, bf16[2,64,1152]{2,1,0:T(8,128)(2,1)}, u32[]{:S(2)}) copy-start(bf16[2,64,1152]{2,1,0:T(8,128)(2,1)} %copy-done) | copy-start | bytes 884740
  38.8 1.0 %copy-start.3 = (bf16[2,64,1152]{2,1,0:T(8,128)(2,1)S(1)}, bf16[2,64,1152]{2,1,0:T(8,128)(2,1)}, u32[]{:S(2)}) copy-start(bf16[2,64,1152]{2,1,0:T(8,128)(2,1)} %hand.3.refs_2_) | copy-start | bytes 884740
  39.8 1.0 %copy-start.5 = (bf16[2,64,1152]{2,1,0:T(8,128)(2,1)S(1)}, bf16[2,64,1152]{2,1,0:T(8,128)(2,1)}, u32[]{:S(2)}) copy-start(bf16[2,64,1152]{2,1,0:T(8,128)(2,1)} %copy-done.4) | copy-start | bytes 884740
  40.7 1.0 %copy-start.7 = (bf16[2,64,1152]{2,1,0:T(8,128)(2,1)S(1)}, bf16[2,64,1152]{2,1,0:T(8,128)(2,1)}, u32[]{:S(2)}) copy-start(bf16[2,64,1152]{2,1,0:T(8,128)(2,1)} %hand.4.refs_4_) | copy-start | bytes 884740
  41.7 8.8 %copy-start.8 = (bf16[400,1024]{1,0:T(8,128)(2,1)S(1)}, bf16[400,1024]{1,0:T(8,128)(2,1)}, u32[]{:S(2)}) copy-start(bf16[400,1024]{1,0:T(8,128)(2,1)} %get-tuple-element.24.refs_2_) | copy-start | bytes 2457604
  44.4 0.7 %copy-start.11 = (bf16[2,64,1152]{2,1,0:T(8,128)(2,1)}, bf16[2,64,1152]{2,1,0:T(8,128)(2,1)S(1)}, u32[]{:S(2)}) copy-start(bf16[2,64,1152]{2,1,0:T(8,128)(2,1)S(1)} %collective-permute-done.5.refs_0_) | copy-start | bytes 884740
  50.5 1.0 %copy-start.12 = (bf16[2,64,1152]{2,1,0:T(8,128)(2,1)S(1)}, bf16[2,64,1152]{2,1,0:T(8,128)(2,1)}, u32[]{:S(2)}) copy-start(bf16[2,64,1152]{2,1,0:T(8,128)(2,1)} %copy-done.11) | copy-start | bytes 884740
  51.5 12.1 %copy-start.9 = (f32[384,512]{1,0:T(8,128)S(1)}, f32[384,512]{1,0:T(8,128)}, u32[]{:S(2)}) copy-start(f32[384,512]{1,0:T(8,128)} %get-tuple-element.19.base_a) | copy-start | bytes 2359300
  53.1 0.6 copy-start.13
  53.7 9.8 %collective-permute-start.10 = (f32[384,512]{1,0:T(8,128)}, f32[384,512]{1,0:T(8,128)S(1)}, u32[]{:S(2)}, u32[]{:S(2)}) collective-permute-start(f32[384,512]{1,0:T(8,128)} %hand.5), channel_id=1, source_target_pairs={{0,1},{1,0},{2,3},{3,2},{4,5},{5,4},{6,7},{7,6},{8,9},{9,8},{10,11... | collective-permute-start | bytes 2359304 | tf_op jit(solution)/shard_map/ppermute | solution.py:351
  53.7 5.2 %collective-permute-start.11 = (bf16[3,128,128]{2,1,0:T(8,128)(2,1)S(1)}, bf16[3,128,128]{2,1,0:T(8,128)(2,1)S(1)}, u32[]{:S(2)}, u32[]{:S(2)}) collective-permute-start(bf16[3,128,128]{2,1,0:T(8,128)(2,1)S(1)} %get-tuple-element.30), channel_id=1, source_target_pairs={{0,2},{2,0},{16,18},{18,16},{1,3},{3,1},{17,19},{19,17},{4,6},{6,4... | collective-permute-start | bytes 294920 | tf_op jit(solution)/shard_map/ppermute | solution.py:364
  54.3 4.9 %collective-permute-start.12 = (bf16[3,128,128]{2,1,0:T(8,128)(2,1)S(1)}, bf16[3,128,128]{2,1,0:T(8,128)(2,1)S(1)}, u32[]{:S(2)}, u32[]{:S(2)}) collective-permute-start(bf16[3,128,128]{2,1,0:T(8,128)(2,1)S(1)} %get-tuple-element.31), channel_id=1, source_target_pairs={{0,16},{2,18},{16,0},{18,2},{1,17},{3,19},{17,1},{19,3},{4,20},{6,... | collective-permute-start | bytes 294920 | tf_op jit(solution)/shard_map/ppermute | solution.py:364
  55.8 6.5 %collective-permute-start.13 = (bf16[3,128,128]{2,1,0:T(8,128)(2,1)S(1)}, bf16[3,128,128]{2,1,0:T(8,128)(2,1)S(1)}, u32[]{:S(2)}, u32[]{:S(2)}) collective-permute-start(bf16[3,128,128]{2,1,0:T(8,128)(2,1)S(1)} %get-tuple-element.32), channel_id=1, source_target_pairs={{0,18},{2,16},{16,2},{18,0},{1,19},{3,17},{17,3},{19,1},{4,22},{6,... | collective-permute-start | bytes 294920 | tf_op jit(solution)/shard_map/ppermute | solution.py:364
  57.2 5.0 %collective-permute-start.14 = (bf16[3,128,128]{2,1,0:T(8,128)(2,1)S(1)}, bf16[3,128,128]{2,1,0:T(8,128)(2,1)S(1)}, u32[]{:S(2)}, u32[]{:S(2)}) collective-permute-start(bf16[3,128,128]{2,1,0:T(8,128)(2,1)S(1)} %get-tuple-element.29.refs_0_), channel_id=1, source_target_pairs={{0,1},{1,0},{2,3},{3,2},{4,5},{5,4},{6,7},{7,6},{8,9},{9,8},{10,11... | collective-permute-start | bytes 294920 | tf_op jit(solution)/shard_map/ppermute | solution.py:351
  59.0 3.3 %collective-permute-start.15 = (bf16[3,128,128]{2,1,0:T(8,128)(2,1)S(1)}, bf16[3,128,128]{2,1,0:T(8,128)(2,1)S(1)}, u32[]{:S(2)}, u32[]{:S(2)}) collective-permute-start(bf16[3,128,128]{2,1,0:T(8,128)(2,1)S(1)} %collective-permute-done.11.refs_1_), channel_id=1, source_target_pairs={{0,1},{1,0},{2,3},{3,2},{4,5},{5,4},{6,7},{7,6},{8,9},{9,8},{10,11... | collective-permute-start | bytes 294920 | tf_op jit(solution)/shard_map/ppermute | solution.py:351
  59.2 3.1 %collective-permute-start.16 = (bf16[3,128,128]{2,1,0:T(8,128)(2,1)S(1)}, bf16[3,128,128]{2,1,0:T(8,128)(2,1)S(1)}, u32[]{:S(2)}, u32[]{:S(2)}) collective-permute-start(bf16[3,128,128]{2,1,0:T(8,128)(2,1)S(1)} %collective-permute-done.12.refs_2_), channel_id=1, source_target_pairs={{0,1},{1,0},{2,3},{3,2},{4,5},{5,4},{6,7},{7,6},{8,9},{9,8},{10,11... | collective-permute-start | bytes 294920 | tf_op jit(solution)/shard_map/ppermute | solution.py:351
  62.2 1.3 %collective-permute-start.17 = (bf16[3,128,128]{2,1,0:T(8,128)(2,1)S(1)}, bf16[3,128,128]{2,1,0:T(8,128)(2,1)S(1)}, u32[]{:S(2)}, u32[]{:S(2)}) collective-permute-start(bf16[3,128,128]{2,1,0:T(8,128)(2,1)S(1)} %collective-permute-done.13.refs_3_), channel_id=1, source_target_pairs={{0,1},{1,0},{2,3},{3,2},{4,5},{5,4},{6,7},{7,6},{8,9},{9,8},{10,11... | collective-permute-start | bytes 294920 | tf_op jit(solution)/shard_map/ppermute | solution.py:351
